TPU v7x, 32 devices: a whole 2x2x4 slice. The times are simulated.
32 devices in a mesh: dp: 8 (over y, x, core), tensor: 4 (over z).
Axes of the slice: x: 2, y: 2, z: 4, core: 2. Of those that a mesh axis runs over, the one named last changes fastest.
Arguments:
- tokens: bfloat16 [16384, 2048], P('dp'), may hold values from -6 to 6
- lengths: int32 [8], P('dp'), may hold values from 512 to 2048, as said below
- gains: float32 [2, 2048], P(None, 'dp'), may hold values from 0.5 to 1.5
- w_gelu: float32 [2048, 2560], P('dp', 'tensor'), may hold values from -0.125 to 0.125
- w_rec: float32 [2048, 2560], P('dp', 'tensor'), may hold values from -0.125 to 0.125
- chan: float32 [8, 16, 160], P(None, 'tensor', 'dp'), may hold values from -2 to 9, as said below
- w_lru: float32 [2, 16, 160, 160], P(None, 'tensor', 'dp'), may hold values from -0.5 to 0.5
- w_out: float32 [2560, 2048], P('tensor', 'dp'), may hold values from -0.3125 to 0.3125
- w_mlp_in: float32 [2, 2048, 6144], P(None, 'dp', 'tensor'), may hold values from -0.125 to 0.125
- w_down: float32 [6144, 2048], P('tensor', 'dp'), may hold values from -0.15625 to 0.15625
- cotangent: bfloat16 [16384, 2048], P('dp'), may hold values from -6 to 6
Outputs:
- output: bfloat16 [16384, 2048], P('dp')
- grad_tokens: bfloat16 [16384, 2048], P('dp')
- grad_gain_one: float32 [2048], P('dp')
- grad_gain_two: float32 [2048], P('dp')
- grad_w_gelu: float32 [2048, 2560], P('dp', 'tensor')
- grad_w_rec: float32 [2048, 2560], P('dp', 'tensor')
- grad_chan: float32 [8, 16, 160], P(None, 'tensor', 'dp')
- grad_w_lru: float32 [2, 16, 160, 160], P(None, 'tensor', 'dp')
- grad_w_out: float32 [2560, 2048], P('tensor', 'dp')
- grad_w_mlp_in: float32 [2, 2048, 6144], P(None, 'dp', 'tensor')
- grad_w_down: float32 [6144, 2048], P('tensor', 'dp')
Inputs may be any that keep to these rules, and one draw needn't show every extreme that they name: `lengths`: slots at or past a sequence's length are padding; at least one sequence has all 2048 slots live. `chan`: row 7 (the decay parameter) lies from 1 to 9; the other rows lie from -2 to 2.
All inputs are finite; a program needn't handle non-finite values.
Results may differ from a plain program's by a relative error of at most 0.025.
Values may be sent and summed in bfloat16 or wider, within the bound.
No kernel may reach another device: no remote copies, remote signals or barrier semaphores. Data moves between devices by JAX's collectives and lax.ppermute only.
A program may use at most 384 MiB of HBM per device.

v0:
```python
import jax
import jax.numpy as jnp
from jax import lax
from jax.sharding import PartitionSpec as P

NORM_EPS = 1e-06
DECAY_FLOOR = 0.05


def norm_scale(values, gain_row):
    return (
        values * lax.rsqrt(jnp.mean(values * values, axis=-1, keepdims=True) + NORM_EPS) * gain_row
    )


def shifted(values, offset):
    padded = jnp.pad(values, ((0, 0), (offset, 0), (0, 0)))
    return padded[:, : values.shape[1], :]


def combine(earlier, later):
    return (earlier[0] * later[0], later[0] * earlier[1] + later[1])


def recurrence(inputs, params, gate_mats, live_mask):
    convolved = (
        params[0] * inputs
        + params[1] * shifted(inputs, 1)
        + params[2] * shifted(inputs, 2)
        + params[3] * shifted(inputs, 3)
    )
    convolved = (convolved + params[4]) * live_mask
    head_count = gate_mats.shape[1]
    head_size = gate_mats.shape[2]
    per_head = convolved.reshape(convolved.shape[0], convolved.shape[1], head_count, head_size)
    input_gate = jnp.einsum(
        "slhj,hjk->slhk", per_head, gate_mats[0], precision=lax.Precision.HIGHEST
    ).reshape(convolved.shape)
    decay_gate = jnp.einsum(
        "slhj,hjk->slhk", per_head, gate_mats[1], precision=lax.Precision.HIGHEST
    ).reshape(convolved.shape)
    input_gate = jax.nn.sigmoid(input_gate + params[5])
    decay_gate = jax.nn.sigmoid(decay_gate + params[6])
    decays = jnp.exp(-8.0 * decay_gate * jax.nn.softplus(-params[7]))
    normalizer = jnp.sqrt(jnp.maximum(1.0 - decays * decays, DECAY_FLOOR))
    driven = normalizer * input_gate * convolved
    _, states = lax.associative_scan(combine, (decays, driven), axis=1)
    return states * live_mask


def matmul(left, right):
    return jnp.dot(left, right, preferred_element_type=jnp.float32)


def gelu_product(gate_arg, up_arg):
    return jax.nn.gelu(gate_arg) * up_arg


def on_device(
    tokens, lengths, gains, w_gelu, w_rec, chan, w_lru, w_out, w_mlp_in, w_down, cotangent
):
    gain_rows, gelu_w, rec_w, chan_w, lru_w, out_w = (
        lax.all_gather(gains.astype(jnp.bfloat16), "dp", axis=1, tiled=True),
        lax.all_gather(w_gelu.astype(jnp.bfloat16), "dp", axis=0, tiled=True),
        lax.all_gather(w_rec.astype(jnp.bfloat16), "dp", axis=0, tiled=True),
        lax.all_gather(chan.astype(jnp.bfloat16), "dp", axis=2, tiled=True),
        lax.all_gather(w_lru.astype(jnp.bfloat16), "dp", axis=2, tiled=True),
        lax.all_gather(w_out.astype(jnp.bfloat16), "dp", axis=1, tiled=True),
    )
    mlp_w, down_w = (
        lax.all_gather(w_mlp_in.astype(jnp.bfloat16), "dp", axis=1, tiled=True),
        lax.all_gather(w_down.astype(jnp.bfloat16), "dp", axis=1, tiled=True),
    )
    seq_count = lengths.shape[0]
    row_count = tokens.shape[0]
    seq_len = row_count // seq_count
    width_dev = gelu_w.shape[1]
    positions = lax.iota(jnp.int32, seq_len)
    live_mask = (positions[None, :] < lengths[:, None]).astype(jnp.float32)[..., None]
    row_mask = live_mask.reshape(row_count, 1)
    inputs = tokens.astype(jnp.float32)
    gain_vals = gain_rows.astype(jnp.float32)
    normed_one, norm_one_pull = jax.vjp(norm_scale, inputs, gain_vals[0])
    first_in = normed_one.astype(jnp.bfloat16)
    branch_pre = matmul(first_in, gelu_w)
    rec_in = matmul(first_in, rec_w) * row_mask
    channel = chan_w.astype(jnp.float32).reshape(chan_w.shape[0], width_dev)
    lru_vals = lru_w.astype(jnp.float32)

    def run_rec(rec_arg, chan_arg, lru_arg):
        return recurrence(rec_arg, chan_arg, lru_arg, live_mask)

    recurrent, rec_pull = jax.vjp(
        run_rec, rec_in.reshape(seq_count, seq_len, width_dev), channel, lru_vals
    )
    recurrent = recurrent.reshape(row_count, width_dev)
    activated, gelu_pull = jax.vjp(jax.nn.gelu, branch_pre)
    mixed = (activated * recurrent).astype(jnp.bfloat16)
    branch_sum = lax.psum(matmul(mixed, out_w).astype(jnp.bfloat16), "tensor").astype(jnp.float32)
    hidden_res = inputs + branch_sum
    normed_two, norm_two_pull = jax.vjp(norm_scale, hidden_res, gain_vals[1])
    second_in = normed_two.astype(jnp.bfloat16)
    gate_pre = matmul(second_in, mlp_w[0])
    up_pre = matmul(second_in, mlp_w[1])
    product, product_pull = jax.vjp(gelu_product, gate_pre, up_pre)
    product_low = product.astype(jnp.bfloat16)
    mlp_sum = lax.psum(matmul(product_low, down_w).astype(jnp.bfloat16), "tensor").astype(
        jnp.float32
    )
    output = (hidden_res + mlp_sum).astype(jnp.bfloat16)
    cot_vals = cotangent.astype(jnp.float32)
    grad_down = matmul(product_low.T, cotangent)
    grad_product = matmul(cotangent, down_w.T)
    grad_gate, grad_up = product_pull(grad_product)
    gate_low = grad_gate.astype(jnp.bfloat16)
    up_low = grad_up.astype(jnp.bfloat16)
    grad_mlp = jnp.stack([matmul(second_in.T, gate_low), matmul(second_in.T, up_low)])
    grad_second = lax.psum(
        (matmul(gate_low, mlp_w[0].T) + matmul(up_low, mlp_w[1].T)).astype(jnp.bfloat16), "tensor"
    ).astype(jnp.float32)
    grad_hidden, grad_gain_two = norm_two_pull(grad_second)
    grad_hidden = cot_vals + grad_hidden
    hidden_low = grad_hidden.astype(jnp.bfloat16)
    grad_out = matmul(mixed.T, hidden_low)
    grad_mixed = matmul(hidden_low, out_w.T)
    (grad_pre,) = gelu_pull(grad_mixed * recurrent)
    pre_low = grad_pre.astype(jnp.bfloat16)
    grad_rec_in, grad_channel, grad_lru = rec_pull(
        (grad_mixed * activated).reshape(seq_count, seq_len, width_dev)
    )
    rec_low = (grad_rec_in.reshape(row_count, width_dev) * row_mask).astype(jnp.bfloat16)
    grad_gelu_w = matmul(first_in.T, pre_low)
    grad_rec_w = matmul(first_in.T, rec_low)
    grad_first = lax.psum(
        (matmul(pre_low, gelu_w.T) + matmul(rec_low, rec_w.T)).astype(jnp.bfloat16), "tensor"
    ).astype(jnp.float32)
    grad_inputs, grad_gain_one = norm_one_pull(grad_first)
    grad_tokens = (grad_hidden + grad_inputs).astype(jnp.bfloat16)
    grad_gain_rows = jnp.stack([grad_gain_one, grad_gain_two])
    grad_chan = grad_channel.reshape(chan_w.shape)
    sum_gains, sum_gelu, sum_rec, sum_chan, sum_lru, sum_out, sum_mlp, sum_down = (
        lax.psum_scatter(
            grad_gain_rows.astype(jnp.bfloat16), "dp", scatter_dimension=1, tiled=True
        ).astype(jnp.float32),
        lax.psum_scatter(
            grad_gelu_w.astype(jnp.bfloat16), "dp", scatter_dimension=0, tiled=True
        ).astype(jnp.float32),
        lax.psum_scatter(
            grad_rec_w.astype(jnp.bfloat16), "dp", scatter_dimension=0, tiled=True
        ).astype(jnp.float32),
        lax.psum_scatter(
            grad_chan.astype(jnp.bfloat16), "dp", scatter_dimension=2, tiled=True
        ).astype(jnp.float32),
        lax.psum_scatter(
            grad_lru.astype(jnp.bfloat16), "dp", scatter_dimension=2, tiled=True
        ).astype(jnp.float32),
        lax.psum_scatter(
            grad_out.astype(jnp.bfloat16), "dp", scatter_dimension=1, tiled=True
        ).astype(jnp.float32),
        lax.psum_scatter(
            grad_mlp.astype(jnp.bfloat16), "dp", scatter_dimension=1, tiled=True
        ).astype(jnp.float32),
        lax.psum_scatter(
            grad_down.astype(jnp.bfloat16), "dp", scatter_dimension=1, tiled=True
        ).astype(jnp.float32),
    )
    return (
        output,
        grad_tokens,
        sum_gains[0],
        sum_gains[1],
        sum_gelu,
        sum_rec,
        sum_chan,
        sum_lru,
        sum_out,
        sum_mlp,
        sum_down,
    )


def solution(mesh):
    in_specs = (
        P("dp", None),
        P("dp"),
        P(None, "dp"),
        P("dp", "tensor"),
        P("dp", "tensor"),
        P(None, "tensor", "dp"),
        P(None, "tensor", "dp", None),
        P("tensor", "dp"),
        P(None, "dp", "tensor"),
        P("tensor", "dp"),
        P("dp", None),
    )
    out_specs = (
        P("dp", None),
        P("dp", None),
        P("dp"),
        P("dp"),
        P("dp", "tensor"),
        P("dp", "tensor"),
        P(None, "tensor", "dp"),
        P(None, "tensor", "dp", None),
        P("tensor", "dp"),
        P(None, "dp", "tensor"),
        P("tensor", "dp"),
    )
    return jax.shard_map(
        on_device, mesh=mesh, in_specs=in_specs, out_specs=out_specs, check_vma=False
    )
```

profile of v0, /device:TPU:0, one launch (start us, length us, event | category | flops | bytes accessed | tf_op | source)
XLA Modules:
  0.0 2522.9 jit_solution(9105795040358181678)
XLA Ops:
  15.6 11.1 all_gather.26
  27.6 8.9 all_gather.24
  44.8 9.1 all_gather.28
  54.7 10.2 fusion.94
  106.8 10.7 fusion.56
  117.5 11.3 slice.424
  128.8 13.4 slice.428
  142.3 13.0 slice.425
  155.2 13.0 slice.426
  205.4 13.2 slice.423
  218.6 13.1 slice.504
  289.5 9.3 pad.496
  304.9 9.7 pad.497
  314.6 17.7 pad.498
  332.2 14.7 fusion.41
  347.0 11.5 convolution_convert_fusion.1
  361.8 20.3 fusion.152
  382.2 267.9 %all-reduce.129.cloned.1.call-done = bf16[2048,2048]{1,0:T(8,128)(2,1)} async-done(((bf16[2048,2048]{1,0:T(8,128)(2,1)}), bf16[2048,2048]{1,0:T(8,128)(2,1)}) %all-reduce.129.cloned.1.call-update) | async-done | bytes 8388624 | tf_op jit(solution)/shard_map/psum | solution.py:99
  658.6 11.7 multiply_convert_fusion
  670.4 53.2 %all-gather.12.cloned.1.call-done = bf16[2,2048,1536]{2,1,0:T(8,128)(2,1)} async-done(((bf16[2,256,1536]{2,1,0:T(8,128)(2,1)}), bf16[2,2048,1536]{2,1,0:T(8,128)(2,1)}) %all-gather.12.cloned.1.call-update) | async-done | bytes 12582928 | tf_op jit(solution)/shard_map/all_gather | solution.py:71
  723.6 19.2 fusion.23
  742.8 34.0 %multiply_convert_fusion.2 = (bf16[2048,1536]{1,0:T(8,128)(2,1)}, bf16[2048,1536]{1,0:T(8,128)(2,1)}, bf16[2048,1536]{1,0:T(8,128)(2,1)}) fusion(f32[2048,1536]{1,0:T(8,128)} %fusion.23, f32[2048,1536]{1,0:T(8,128)} %fusion.152, bf16[2048,2048]{1,0:T(8,128)(2,1)} %multiply_convert_fusion, bf16[2,2048,1536]{2,1,0:T(8,128)(2,1)} %all-gather.12.cloned.1.call-done), kind=kOutput, calls=%fused_computation.40 | convolution fusion | flops 12966690816 | bytes 58720256 | tf_op jit(solution)/shard_map/dot_general | solution.py:52
  776.8 19.5 fusion.22
  796.3 21.7 add_convert_fusion.1
  818.0 290.9 %all-reduce.131.cloned.1.call-done = bf16[2048,2048]{1,0:T(8,128)(2,1)} async-done(((bf16[2048,2048]{1,0:T(8,128)(2,1)}), bf16[2048,2048]{1,0:T(8,128)(2,1)}) %all-reduce.131.cloned.1.call-update) | async-done | bytes 8388624 | tf_op jit(solution)/shard_map/psum | solution.py:118
  1108.9 12.8 fusion.6
  1121.8 18.0 fusion.8
  1139.8 19.0 multiply_bitcast_fusion
  1158.7 8.6 fusion.115
  1167.3 13.1 slice.508
  1188.7 13.0 slice.509
  1260.5 10.0 pad.501
  1270.7 9.2 pad.506
  1329.7 9.1 pad.570
  1357.5 9.2 pad.600
  1372.9 17.7 pad.572
  1390.6 9.0 pad.601
  1399.6 9.2 pad.574
  1408.8 17.6 pad.571
  1426.4 8.8 multiply_add_fusion
  1435.2 17.9 pad.602
  1453.0 9.7 pad.603
  1462.7 17.7 pad.573
  1480.4 21.5 multiply_reduce_fusion.5
  1501.9 10.2 fusion.101
  1518.3 9.1 convolution_bitcast_fusion
  1537.4 8.9 convolution_bitcast_fusion.1
  1548.1 19.1 convolution_convert_fusion.2
  1569.0 11.1 fusion.53
  1600.6 10.8 convolution_convert_fusion.6
  1611.7 18.1 multiply_reduce_fusion.4
  1643.2 9.3 convolution_convert_fusion.5
  1652.6 17.8 fusion.20
  1670.5 17.3 fusion.21
  1693.6 19.4 convolution_convert_fusion
  1713.0 9.6 fusion.153
  1722.6 12.8 add_convert_fusion
  1737.7 24.8 all-reduce.121
  1770.9 37.1 %reduce-scatter.12.cloned.1.call-done = bf16[256,640]{1,0:T(8,128)(2,1)} async-done(((bf16[2048,640]{1,0:T(8,128)(2,1)}), bf16[256,640]{1,0:T(8,128)(2,1)}) %reduce-scatter.12.cloned.1.call-update) | async-done | bytes 327696 | tf_op jit(solution)/shard_map/reduce_scatter | solution.py:148
  1809.8 94.1 %reduce-scatter.16.cloned.1.call-done = bf16[2,256,1536]{2,1,0:T(8,128)(2,1)} async-done(((bf16[2,2048,1536]{2,1,0:T(8,128)(2,1)}), bf16[2,256,1536]{2,1,0:T(8,128)(2,1)}) %reduce-scatter.16.cloned.1.call-update) | async-done | bytes 1572880 | tf_op jit(solution)/shard_map/reduce_scatter | solution.py:160
  1907.3 562.9 %all-reduce.135.cloned.1.call-done = (bf16[2048,2048]{1,0:T(8,128)(2,1)}, bf16[2048,2048]{1,0:T(8,128)(2,1)}) async-done(((bf16[2048,2048]{1,0:T(8,128)(2,1)}, bf16[2048,2048]{1,0:T(8,128)(2,1)}), (bf16[2048,2048]{1,0:T(8,128)(2,1)}, bf16[2048,2048]{1,0:T(8,128)(2,1)})) %all-reduce.135.cloned.1.call-update) | async-done | bytes 16777232 | tf_op jit(solution)/shard_map/psum | solution.py:134
  2470.2 10.0 fusion.7
  2481.4 23.6 fusion.10
  2504.9 9.7 reduce-scatter.20.cloned.1.call-done
  (690 shorter events, 389.6 us)
Async XLA Ops:
  7.2 20.4 copy-start.152
  7.2 47.5 %all-gather.8.cloned.1.call-start = ((), (), s32[]{:S(2)}) async-start(), calls=%async_computation.7 | async-start | bytes 2949120 | tf_op jit(solution)/shard_map/all_gather | solution.py:65
  9.1 323.1 %all-gather.6.cloned.1.call-start = ((), (), s32[]{:S(2)}) async-start(), calls=%async_computation.6 | async-start | bytes 2949120 | tf_op jit(solution)/shard_map/all_gather | solution.py:64
  11.1 335.9 %all-gather.10.cloned.1.call-start = ((), (), s32[]{:S(2)}) async-start(), calls=%async_computation.8 | async-start | bytes 2949120 | tf_op jit(solution)/shard_map/all_gather | solution.py:68
  13.0 348.8 %all-gather.14.cloned.1.call-start = ((), (), s32[]{:S(2)}) async-start(), calls=%async_computation.11 | async-start | bytes 7077888 | tf_op jit(solution)/shard_map/all_gather | solution.py:72
  15.4 28.1 %copy-start.100 = (f32[2,4,20,160]{3,1,2,0:T(4,128)S(1)}, f32[2,4,20,160]{3,1,2,0:T(4,128)}, u32[]{:S(2)}) copy-start(f32[2,4,20,160]{3,1,2,0:T(4,128)} %param.17) | copy-start | bytes 307204
  15.5 634.6 %all-reduce.129.cloned.1.call-start = ((), (), s32[]{:S(2)}) async-start(), calls=%async_computation.9 | async-start | bytes 16777216 | tf_op jit(solution)/shard_map/psum | solution.py:99
  43.6 63.2 %copy-start.118 = (f32[640]{0:T(1024)}, f32[640]{0:T(1024)S(1)}, u32[]{:S(2)}) copy-start(f32[640]{0:T(1024)S(1)} %add.581) | copy-start | bytes 7684
  43.7 63.1 %copy-start.107 = (f32[640]{0:T(1024)}, f32[640]{0:T(1024)S(1)}, u32[]{:S(2)}) copy-start(f32[640]{0:T(1024)S(1)} %add.586) | copy-start | bytes 7684
  43.8 22.3 copy-start.125
  43.9 22.2 copy-start.129
  43.9 22.1 copy-start.131
  44.0 22.1 copy-start.133
  54.4 38.8 %copy-start.49 = (bf16[1,4,160,160]{2,3,1,0:T(8,128)(2,1)}, bf16[1,4,160,160]{2,3,1,0:T(8,128)(2,1)S(1)}, u32[]{:S(2)}) copy-start(bf16[1,4,160,160]{2,3,1,0:T(8,128)(2,1)S(1)} %copy.104) | copy-start | bytes 614404
  54.7 25.0 copy-start.51
  128.8 39.4 %copy-start.5 = (f32[1,1024,640]{2,1,0:T(8,128)}, f32[1,1024,640]{2,1,0:T(8,128)S(1)}, u32[]{:S(2)}) copy-start(f32[1,1024,640]{2,1,0:T(8,128)S(1)} %slice.424) | copy-start | bytes 7864324
  180.5 24.2 copy-start.14
  187.0 17.7 copy-start.18
  205.4 26.3 %copy-start.16 = (f32[1,1024,640]{2,1,0:T(8,128)S(1)}, f32[1,1024,640]{2,1,0:T(8,128)}, u32[]{:S(2)}) copy-start(f32[1,1024,640]{2,1,0:T(8,128)} %get-tuple-element.129) | copy-start | bytes 7864324
  243.0 15.0 copy-start.31
  246.2 17.5 copy-start.27
  249.5 14.9 copy-start.34
  252.9 26.4 %copy-start.32 = (f32[1,255,640]{2,1,0:T(8,128)}, f32[1,255,640]{2,1,0:T(8,128)S(1)}, u32[]{:S(2)}) copy-start(f32[1,255,640]{2,1,0:T(8,128)S(1)} %slice.435) | copy-start | bytes 1958404
  358.6 365.0 %all-gather.12.cloned.1.call-start = ((), (), s32[]{:S(2)}) async-start(), calls=%async_computation.10 | async-start | bytes 14155776 | tf_op jit(solution)/shard_map/all_gather | solution.py:71
  361.8 747.2 %all-reduce.131.cloned.1.call-start = ((), (), s32[]{:S(2)}) async-start(), calls=%async_computation.12 | async-start | bytes 16777216 | tf_op jit(solution)/shard_map/psum | solution.py:118
  382.2 276.5 %copy-start.106 = (f32[1,2048]{1,0:T(1,128)S(1)}, f32[1,2048]{1,0:T(1,128)}, u32[]{:S(2)}) copy-start(f32[1,2048]{1,0:T(1,128)} %get-tuple-element.211) | copy-start | bytes 24580
  818.0 945.2 %all-reduce.133.cloned.1.call-start = ((), (), s32[]{:S(2)}) async-start(), calls=%async_computation.19 | async-start | bytes 1310720
  1121.8 18.0 copy-start.155
  1239.0 16.5 copy-start.102
  1239.0 21.5 copy-start.19
  1260.5 19.4 copy-start.54
  1270.7 14.8 copy-start.72
  1270.7 14.8 copy-start.148
  1270.7 15.0 copy-start.75
  1270.7 15.0 copy-start.77
  1270.7 16.3 copy-start.60
  1270.7 16.3 copy-start.145
  1300.9 17.5 copy-start.35
  1300.9 17.5 copy-start.36
  1310.7 15.4 copy-start.15
  1310.7 15.4 copy-start.146
  1326.2 17.5 copy-start.53
  1329.7 17.0 copy-start.17
  1351.8 14.9 copy-start.6
  1351.8 14.9 copy-start.143
  1435.2 17.9 copy-start.26
  1462.7 17.7 copy-start.108
  1462.7 17.7 copy-start.119
  1462.7 17.7 copy-start.142
  1462.7 39.2 %slice-start.2 = ((s8[5242880]{0:T(1024)(128)(4,1)}), s8[1048576]{0:T(1024)(128)(4,1)S(1)}, s32[]{:S(2)}) async-start(s8[5242880]{0:T(1024)(128)(4,1)} %bitcast.132), calls=%async_computation.23 | async-start | bytes 2097152
  1480.4 21.5 slice-start.3
  1512.1 15.3 slice-start.4
  1547.8 216.9 %reduce-scatter.18.cloned.1.call-start = ((), (), s32[]{:S(2)}) async-start(), calls=%async_computation.17 | async-start | bytes 7077888 | tf_op jit(solution)/shard_map/reduce_scatter | solution.py:163
  1567.3 199.9 %reduce-scatter.14.cloned.1.call-start = ((), (), s32[]{:S(2)}) async-start(), calls=%async_computation.15 | async-start | bytes 2949120 | tf_op jit(solution)/shard_map/reduce_scatter | solution.py:157
  1580.2 188.8 %reduce-scatter.10.cloned.1.call-start = ((), (), s32[]{:S(2)}) async-start(), calls=%async_computation.13 | async-start | bytes 2949120 | tf_op jit(solution)/shard_map/reduce_scatter | solution.py:145
  1611.4 18.3 copy-start.130
  1611.4 18.3 copy-start.132
  1611.5 18.3 copy-start.134
  1611.5 196.5 %reduce-scatter.12.cloned.1.call-start = ((), (), s32[]{:S(2)}) async-start(), calls=%async_computation.14 | async-start | bytes 2949120 | tf_op jit(solution)/shard_map/reduce_scatter | solution.py:148
  1652.6 251.3 %reduce-scatter.16.cloned.1.call-start = ((), (), s32[]{:S(2)}) async-start(), calls=%async_computation.16 | async-start | bytes 14155776 | tf_op jit(solution)/shard_map/reduce_scatter | solution.py:160
  1693.3 776.9 %all-reduce.135.cloned.1.call-start = ((), (), s32[]{:S(2)}) async-start(), calls=%async_computation.20 | async-start | bytes 33554432 | tf_op jit(solution)/shard_map/psum | solution.py:134
  1693.6 19.4 copy-start.154
  1693.6 19.4 copy-start.158
  1735.4 779.2 %reduce-scatter.20.cloned.1.call-start = ((), (), s32[]{:S(2)}) async-start(), calls=%async_computation.18 | async-start | bytes 589824
  (116 other events, 798.3 us)
Sparse Core Ops, SparseCore 0:
  10.5 33.2 all-gather.7
  45.6 30.0 all-gather.5
  77.6 30.4 all-gather.9
  109.9 46.6 all-gather.13
  358.7 291.3 all-reduce.128
  652.4 71.1 all-gather.11
  818.1 290.8 all-reduce.130
  1548.0 54.0 all-reduce.132
  1605.9 61.0 reduce-scatter.17
  1670.1 43.6 reduce-scatter.13
  1717.1 43.9 reduce-scatter.9
  1764.3 43.6 reduce-scatter.11
  1811.4 92.3 reduce-scatter.15
  1906.9 563.2 all-reduce.134
  2481.5 33.0 reduce-scatter.19
where the time goes:
time: 2540 us; the launch traced here: 2520 us
  waiting for transfers between devices  1320 us (52%)
  local copies, waits for them, and re-layouts  496 us (20%)
  matrix products  345 us (14%)
  other arithmetic  292 us (11%)
  blocking collectives  53.9 us (2%)
    psum x1, waiting for transfers between devices, on_device(): lax.psum((matmul(pre_low, gelu_w.T) + matmul(rec_low, rec_w.T)).astype(jn...  563 us
    dot_general x18, matrix products, matmul(): return jnp.dot(left, right, preferred_element_type=jnp.float32)  297 us
    psum x1, waiting for transfers between devices, on_device(): lax.psum((matmul(gate_low, mlp_w[0].T) + matmul(up_low, mlp_w[1].T)).asty...  291 us
    psum x1, waiting for transfers between devices, on_device(): lax.psum(matmul(mixed, out_w).astype(jnp.bfloat16), 'tensor')  268 us
    pad x88, local copies, waits for them, and re-layouts, recurrence(): _, states = lax.associative_scan(combine, (decays, driven), axis=1)  241 us
    slice x87, local copies, waits for them, and re-layouts, recurrence(): _, states = lax.associative_scan(combine, (decays, driven), axis=1)  192 us
    reduce_scatter x1, waiting for transfers between devices, on_device(): lax.psum_scatter(grad_mlp.astype(jnp.bfloat16), 'dp', scatter_dimension=1...  94.1 us
    all_gather x1, waiting for transfers between devices, on_device(): lax.all_gather(w_mlp_in.astype(jnp.bfloat16), 'dp', axis=1, tiled=True)  53.2 us
  transfers between devices with their start and end apart: 15, of which 7 were waited for; matrix products, arithmetic and copies ran while one was open for 23% of the time, Pallas kernels for 0%

commit v1 on v0

v1 whole, which is shorter than its diff:
```python
import functools

import jax
import jax.numpy as jnp
import numpy as np
from jax import lax
from jax.experimental import pallas as pl
from jax.experimental.pallas import tpu as pltpu
from jax.sharding import PartitionSpec as P

NORM_EPS = 1e-06
DECAY_FLOOR = 0.05
HALO = 16
GROUP = 640
ROWS = 128
SLAB = 8
VMEM = 58 * 1024 * 1024
BF = jnp.bfloat16
F32 = jnp.float32


def dot(left, right, dims=((1,), (0,))):
    return lax.dot_general(left, right, (dims, ((), ())), preferred_element_type=F32)


def exchange(values, bit, size):
    return lax.ppermute(values, "dp", [(k, k ^ (1 << bit)) for k in range(size)])


def orders(size, parts):
    high = list(range(1, size.bit_length() - 1))
    return [high, high[::-1]][:parts]


def parts_of(rows):
    return 2 if rows % 256 == 0 else 1


def spread(own, size):
    parts = parts_of(own.shape[0])
    pieces = jnp.split(own, parts)
    for turn in range(size.bit_length() - 2):
        got = [exchange(p, o[turn], size) for p, o in zip(pieces, orders(size, parts))]
        pieces = [jnp.concatenate([p, g]) for p, g in zip(pieces, got)]
    half = jnp.concatenate(pieces)
    return jnp.concatenate([half, exchange(half, 0, size)])


def add_low(one, two):
    return (one.astype(F32) + two.astype(F32)).astype(BF)


def collect(full, size):
    half = full.shape[0] // 2
    parts = parts_of(full.shape[0] // size)
    kept = add_low(full[:half], exchange(full[half:], 0, size))
    pieces = jnp.split(kept, parts)
    for turn in reversed(range(size.bit_length() - 2)):
        cut = pieces[0].shape[0] // 2
        got = [exchange(p[cut:], o[turn], size) for p, o in zip(pieces, orders(size, parts))]
        pieces = [add_low(p[:cut], g) for p, g in zip(pieces, got)]
    return jnp.concatenate(pieces)


def basis(size, rows, place):
    parts = parts_of(rows)
    count = size // 2
    masks, which = [], []
    for core in range(2):
        for part, order in enumerate(orders(size, parts)):
            for q in range(count):
                masks.append(core | sum(((q >> t) & 1) << b for t, b in enumerate(order)))
                which.append(part)
    table = (place ^ jnp.asarray(np.array(masks, np.int32))) * parts
    table = table + jnp.asarray(np.array(which, np.int32))
    spots = jnp.arange(len(masks), dtype=jnp.int32)
    inverse = jnp.sum(jnp.where(table[None, :] == spots[:, None], spots[None, :], 0), axis=1)
    return table, inverse.astype(jnp.int32)


def copy_kernel(table_ref, in_ref, out_ref):
    out_ref[...] = in_ref[...]


def permute(values, table):
    a, b, r, d = values.shape
    width = d // table.shape[0]
    return pl.pallas_call(
        copy_kernel,
        grid_spec=pltpu.PrefetchScalarGridSpec(
            num_scalar_prefetch=1,
            grid=(b, table.shape[0]),
            in_specs=[
                pl.BlockSpec((a, pl.squeezed, r, width), lambda h, p, tab: (0, h, 0, tab[p]))
            ],
            out_specs=pl.BlockSpec((pl.squeezed, a, r, width), lambda h, p, tab: (h, 0, 0, p)),
        ),
        out_shape=jax.ShapeDtypeStruct((b, a, r, d), values.dtype),
        compiler_params=pltpu.CompilerParams(vmem_limit_bytes=VMEM),
        name="permute",
    )(table, values)


def permute_rows(values, table):
    return permute(values[None, None], table)[0, 0]


def permute_gain(values, table):
    lead = values.shape[0]
    return jnp.take(values.reshape(lead, table.shape[0], -1), table, axis=1).reshape(lead, -1)


def row_ids(count, width, first):
    return lax.broadcasted_iota(jnp.int32, (count, width), 0) + first


def scan_slab(decay, value, back):
    rows = row_ids(SLAB, decay.shape[1], 0)
    for step in (1, 2, 4):
        keep = rows < SLAB - step if back else rows >= step
        shift = SLAB - step if back else step
        moved_decay = pltpu.roll(decay, shift, 0)
        moved_value = pltpu.roll(value, shift, 0)
        value = jnp.where(keep, value + decay * moved_value, value)
        decay = jnp.where(keep, decay * moved_decay, decay)
    return decay, value


def gelu_parts(v):
    c = np.float32(np.sqrt(2 / np.pi))
    return jnp.tanh(c * (v + 0.044715 * v * v * v))


def forward_kernel(live_ref, pre_ref, par_ref, w_ref, conv_ref, decay_ref, ig_ref, dg_ref, state_ref, prod_ref, rec_ref):
    rows, width = conv_ref.shape
    live = live_ref[0]
    rec_ref[...] = jnp.where(row_ids(rows + HALO, width, -HALO) < live, pre_ref[...], 0.0)
    par = [par_ref[k : k + 1, :] for k in range(8)]
    for at in range(0, rows, ROWS):
        span = pl.ds(at, ROWS)
        near = rec_ref[pl.ds(at, ROWS + HALO), :]
        conv = par[4] + par[0] * near[HALO : HALO + ROWS]
        for k in range(1, 4):
            conv = conv + par[k] * near[HALO - k : HALO - k + ROWS]
        conv = jnp.where(row_ids(ROWS, width, at) < live, conv, 0.0)
        conv_ref[span, :] = conv
        gates = dot(conv.astype(BF), w_ref[...])
        ig = lax.logistic(gates[:, :width] + par[5])
        dg = lax.logistic(gates[:, width:] + par[6])
        decay = jnp.exp(dg * par[7])
        ig_ref[span, :] = ig
        dg_ref[span, :] = dg
        decay_ref[span, :] = decay
        state_ref[span, :] = jnp.sqrt(jnp.maximum(1.0 - decay * decay, DECAY_FLOOR)) * ig * conv

    def slab(k, carry):
        state, prod = carry
        for inner in range(4):
            span = pl.ds(pl.multiple_of(k * 4 * SLAB + inner * SLAB, SLAB), SLAB)
            decay, value = scan_slab(decay_ref[span, :], state_ref[span, :], False)
            value = value + decay * state
            decay = decay * prod
            state_ref[span, :] = value
            prod_ref[span, :] = decay
            state = jnp.broadcast_to(value[SLAB - 1 :, :], (SLAB, width))
            prod = jnp.broadcast_to(decay[SLAB - 1 :, :], (SLAB, width))
        return state, prod

    lax.fori_loop(0, rows // (4 * SLAB), slab, (jnp.zeros((SLAB, width), F32), jnp.ones((SLAB, width), F32)))


def back_scan_kernel(live_ref, pre_ref, grad_ref, decay_ref, lam_ref, reach_ref, edge_ref):
    rows, width = grad_ref.shape
    live = live_ref[0]
    for at in range(0, rows, ROWS):
        span = pl.ds(at, ROWS)
        v = pre_ref[pl.ds(at + HALO, ROWS), :]
        act = 0.5 * v * (1.0 + gelu_parts(v))
        lam_ref[span, :] = jnp.where(row_ids(ROWS, width, at) < live, grad_ref[span, :] * act, 0.0)
    last = row_ids(SLAB, width, 0) == SLAB - 1

    def slab(k, carry):
        lam, reach, following, _ = carry
        for inner in range(4):
            span = pl.ds(pl.multiple_of(rows - (k * 4 + inner + 1) * SLAB, SLAB), SLAB)
            own = decay_ref[span, :]
            ahead = jnp.where(last, following, pltpu.roll(own, SLAB - 1, 0))
            decay, value = scan_slab(ahead, lam_ref[span, :], True)
            value = value + decay * lam
            decay = decay * reach
            lam_ref[span, :] = value
            reach_ref[span, :] = decay
            lam = jnp.broadcast_to(value[:1, :], (SLAB, width))
            reach = jnp.broadcast_to(decay[:1, :], (SLAB, width))
            following = jnp.broadcast_to(own[:1, :], (SLAB, width))
        return lam, reach, following, own

    one = jnp.ones((SLAB, width), F32)
    zero = jnp.zeros((SLAB, width), F32)
    lam, _, following, _ = lax.fori_loop(0, rows // (4 * SLAB), slab, (zero, one, one, one))
    edge_ref[...] = lam * following


def backward_kernel(
    live_ref, pre_ref, par_ref, w_ref, lam_ref, reach_ref, edge_ref, decay_ref, conv_ref, ig_ref, dg_ref, state_ref, prod_ref, cin_ref,
    drec_ref, dpar_ref, dw_ref, rec_ref, dconv_ref, full_ref, dw_acc,
):
    rows, width = conv_ref.shape
    live = live_ref[0]
    rec_ref[...] = jnp.where(row_ids(rows + HALO, width, -HALO) < live, pre_ref[...], 0.0)
    par = [par_ref[k : k + 1, :] for k in range(8)]
    cin = cin_ref[:1, :]
    edge = edge_ref[:1, :]
    full_ref[:SLAB, :] = jnp.broadcast_to(cin, (SLAB, width))
    dconv_ref[:HALO, :] = jnp.zeros((HALO, width), F32)
    dconv_ref[rows + HALO :, :] = jnp.zeros((HALO, width), F32)
    sums = [jnp.zeros((1, width), F32) for _ in range(8)]
    for at in range(0, rows, ROWS):
        span = pl.ds(at, ROWS)
        full_ref[pl.ds(at + SLAB, ROWS), :] = state_ref[span, :] + prod_ref[span, :] * cin
        lam = lam_ref[span, :] + reach_ref[span, :] * edge
        decay, conv, ig, dg = decay_ref[span, :], conv_ref[span, :], ig_ref[span, :], dg_ref[span, :]
        before = full_ref[pl.ds(at, ROWS + SLAB), :][SLAB - 1 : SLAB - 1 + ROWS]
        room = 1.0 - decay * decay
        scale = jnp.sqrt(jnp.maximum(room, DECAY_FLOOR))
        lam_conv = lam * conv
        d_decay = lam * before - jnp.where(room > DECAY_FLOOR, lam_conv * ig * decay / scale, 0.0)
        moved = d_decay * decay
        sums[7] = sums[7] + jnp.sum(moved * dg, axis=0, keepdims=True)
        d_ig = lam_conv * scale * ig * (1.0 - ig)
        d_dg = moved * par[7] * dg * (1.0 - dg)
        sums[5] = sums[5] + jnp.sum(d_ig, axis=0, keepdims=True)
        sums[6] = sums[6] + jnp.sum(d_dg, axis=0, keepdims=True)
        both = jnp.concatenate([d_ig.astype(BF), d_dg.astype(BF)], axis=1)
        d_conv = lam * scale * ig + dot(both, w_ref[...], ((1,), (1,)))
        d_conv = jnp.where(row_ids(ROWS, width, at) < live, d_conv, 0.0)
        dconv_ref[pl.ds(at + HALO, ROWS), :] = d_conv
        part = dot(conv.astype(BF), both, ((0,), (0,)))
        dw_acc[...] = part if at == 0 else dw_acc[...] + part
        near = rec_ref[pl.ds(at, ROWS + HALO), :]
        for k in range(4):
            sums[k] = sums[k] + jnp.sum(d_conv * near[HALO - k : HALO - k + ROWS], axis=0, keepdims=True)
        sums[4] = sums[4] + jnp.sum(d_conv, axis=0, keepdims=True)
    for k in range(8):
        dpar_ref[k : k + 1, :] = sums[k]
    dw_ref[...] = dw_acc[...].astype(BF)
    for at in list(range(0, rows, ROWS)) + [rows]:
        count = ROWS if at < rows else HALO
        near = dconv_ref[pl.ds(at, count + SLAB), :]
        total = par[0] * near[:count]
        for k in range(1, 4):
            total = total + par[k] * near[k : k + count]
        drec_ref[pl.ds(at, count), :] = total


def kernel_call(body, live, arrays, offsets, outs, scratch, name):
    width = outs[0][1]
    steps = width // GROUP
    specs = []
    for array, off in zip(arrays, offsets):
        if array.ndim == 3:
            specs.append(pl.BlockSpec((pl.squeezed,) + array.shape[1:], lambda j, s: (j, 0, 0)))
        else:
            specs.append(pl.BlockSpec((array.shape[0], GROUP), lambda j, s, off=off: (0, j + off)))
    out_specs, out_shapes = [], []
    for rows, cols, kind in outs:
        if cols == width:
            out_specs.append(pl.BlockSpec((rows, GROUP), lambda j, s: (0, j)))
            out_shapes.append(jax.ShapeDtypeStruct((rows, cols), kind))
        else:
            out_specs.append(pl.BlockSpec((pl.squeezed, rows, cols), lambda j, s: (j, 0, 0)))
            out_shapes.append(jax.ShapeDtypeStruct((steps, rows, cols), kind))
    return pl.pallas_call(
        body,
        grid_spec=pltpu.PrefetchScalarGridSpec(
            num_scalar_prefetch=1, grid=(steps,), in_specs=specs, out_specs=out_specs,
            scratch_shapes=[pltpu.VMEM(shape, F32) for shape in scratch],
        ),
        out_shape=out_shapes,
        compiler_params=pltpu.CompilerParams(vmem_limit_bytes=VMEM),
        name=name,
    )(live, *arrays)


def norm_rate(values):
    return lax.rsqrt(jnp.mean(values * values, axis=-1, keepdims=True) + NORM_EPS)


def norm_back(grad, unit, rate, gain):
    moved = grad * gain
    return rate * (moved - unit * jnp.mean(moved * unit, axis=-1, keepdims=True))


def gelu_product(gate, up):
    return jax.nn.gelu(gate) * up


def on_device(size, n, tokens, lengths, gains, w_gelu, w_rec, chan, w_lru, w_out, w_mlp_in, w_down, cotangent):
    place = lax.axis_index("dp")
    turn = lax.axis_index("tensor")
    d_model = tokens.shape[1]
    seq_len = tokens.shape[0]
    rows = seq_len // n
    half = rows // 2
    d_own = w_gelu.shape[0]
    heads_own, head = chan.shape[1], w_lru.shape[3]
    heads = heads_own * n
    width = heads * head
    table, inverse = basis(size, d_own, place)
    live_count = (lengths - turn * rows).astype(jnp.int32)
    live = (lax.iota(jnp.int32, rows)[:, None] < live_count).astype(F32)

    gain_rows = lax.all_gather(gains.astype(BF), "dp", axis=1, tiled=True)
    gain = permute_gain(gain_rows, table).astype(F32)

    def wide(parts):
        own = lax.all_gather(jnp.stack(parts).astype(BF), "tensor", axis=0)
        return own.transpose(2, 1, 0, 3).reshape(d_own, -1)

    w_in = spread(wide([w_gelu, w_rec]), size)
    flat = jnp.concatenate([w_lru.reshape(-1), chan.reshape(-1)]).astype(BF)
    flat = lax.all_gather(flat, ("tensor", "dp"), axis=0).reshape(n, size, -1)
    lru = flat[..., : w_lru.size].reshape((n, size) + w_lru.shape)
    lru = lru.transpose(2, 0, 3, 1, 4, 5).reshape(2, heads, head, head)
    chans = flat[..., w_lru.size :].reshape((n, size) + chan.shape)
    chans = chans.transpose(2, 0, 3, 1, 4).reshape(8, width).astype(F32)
    par = jnp.concatenate([chans[:7], -8.0 * jax.nn.softplus(-chans[7:])])
    per = GROUP // head
    groups = width // GROUP
    eye = jnp.eye(per, dtype=BF)[None, None, :, None, :, None]
    dense = lru.reshape(2, groups, per, head, 1, head) * eye
    dense = dense.reshape(2, groups, GROUP, GROUP)
    dense = jnp.concatenate([dense[0], dense[1]], axis=-1)
    w_back = spread(wide([w_out.T]), size)
    w_gu = spread(jnp.concatenate([w_mlp_in[0], w_mlp_in[1]], axis=1).astype(BF), size)
    w_dn = spread(w_down.T.astype(BF), size)

    main = lax.dynamic_slice_in_dim(tokens, turn * rows, rows)
    before = lax.dynamic_slice_in_dim(tokens, jnp.maximum(turn * rows - HALO, 0), HALO)
    before = jnp.where(turn > 0, before, jnp.zeros_like(before))
    extended = permute_rows(jnp.concatenate([before, main]), table).astype(F32)
    first_rate = norm_rate(extended)
    first = (extended * first_rate * gain[0]).astype(BF)
    inputs, first_own, first_rate = extended[HALO:], first[HALO:], first_rate[HALO:]
    cot = permute(cotangent.reshape(n, 2, half, d_model), table)

    pre = dot(first, w_in)
    keep = (rows, width, F32)
    conv, decay, ig, dg, state, prod = kernel_call(
        forward_kernel, live_count, [pre, par, dense], [groups, 0, 0], [keep] * 6,
        [(rows + HALO, GROUP)], "recurrence",
    )
    ends = lax.all_gather(jnp.concatenate([prod[-1:], state[-1:]]), "tensor", axis=0)
    carry = jnp.zeros((1, width), F32)
    for k in range(n - 1):
        carry = jnp.where(k < turn, ends[k, 1:] + ends[k, :1] * carry, carry)
    branch_pre = pre[HALO:, :width]
    recurrent = (state + prod * carry) * live
    activated, gelu_pull = jax.vjp(jax.nn.gelu, branch_pre)
    mixed = (activated * recurrent).astype(BF)
    hidden = inputs + dot(mixed, w_back, ((1,), (1,)))
    second_rate = norm_rate(hidden)
    second_unit = hidden * second_rate
    second_own = (second_unit * gain[1]).astype(BF)

    hidden_units = w_dn.shape[1]
    mlp_sum, grad_second, seconds, products, grads = [], [], [], [], []
    for h in range(2):
        second = lax.all_gather(second_own[h * half : (h + 1) * half], "tensor", axis=0, tiled=True)
        cot_rows = cot[h].reshape(n * half, d_model)
        both = dot(second, w_gu)
        product, pull = jax.vjp(gelu_product, both[:, :hidden_units], both[:, hidden_units:])
        product = product.astype(BF)
        grad_gate, grad_up = pull(dot(cot_rows, w_dn))
        grad = jnp.concatenate([grad_gate.astype(BF), grad_up.astype(BF)], axis=1)
        share = dot(grad, w_gu, ((1,), (1,))).astype(BF)
        grad_second.append(lax.psum_scatter(share, "tensor", scatter_dimension=0, tiled=True))
        share = dot(product, w_dn, ((1,), (1,))).astype(BF)
        mlp_sum.append(lax.psum_scatter(share, "tensor", scatter_dimension=0, tiled=True))
        seconds.append(second)
        products.append(product)
        grads.append(grad)

    def by_rows(lefts, rights):
        part = dot(lefts[0], rights[0], ((0,), (0,))).astype(BF)
        return (part.astype(F32) + dot(lefts[1], rights[1], ((0,), (0,)))).astype(BF)

    cots = [cot[h].reshape(n * half, d_model) for h in range(2)]
    g_gu = collect(by_rows(seconds, grads), size).astype(F32)
    g_dn = collect(by_rows(cots, products), size).astype(F32)
    result = hidden + jnp.concatenate(mlp_sum).astype(F32)
    result = permute_rows(result.astype(BF), inverse)
    output = lax.all_gather(result, "tensor", axis=0, tiled=True)

    grad_second = jnp.concatenate(grad_second).astype(F32)
    cot_own = lax.dynamic_slice_in_dim(cot, turn, 1, axis=1).reshape(rows, d_model).astype(F32)
    gain_two = jnp.sum(grad_second * second_unit, axis=0)
    grad_hidden = cot_own + norm_back(grad_second, second_unit, second_rate, gain[1])
    hidden_low = grad_hidden.astype(BF)

    def to_owner(grad, parts):
        own = collect(grad.astype(BF), size).reshape(d_own, parts, n, -1).transpose(2, 1, 0, 3)
        return lax.psum_scatter(own, "tensor", scatter_dimension=0).astype(F32)

    grad_mixed = dot(hidden_low, w_back)
    lam, reach, edge = kernel_call(
        back_scan_kernel, live_count, [pre, grad_mixed, decay], [0, 0, 0],
        [keep, keep, (SLAB, width, F32)], [], "back_scan",
    )
    edges = lax.all_gather(edge[:1], "tensor", axis=0)
    arriving = jnp.zeros((1, width), F32)
    for k in range(n - 1, 0, -1):
        arriving = jnp.where(k > turn, edges[k] + ends[k, :1] * arriving, arriving)
    (grad_pre,) = gelu_pull(grad_mixed * recurrent)
    g_back = to_owner(dot(hidden_low, mixed, ((0,), (0,))), 1)
    tall = jnp.broadcast_to
    drec, dpar, d_dense = kernel_call(
        backward_kernel, live_count,
        [pre, par, dense, lam, reach, tall(arriving, (SLAB, width)), decay, conv, ig, dg, state, prod, tall(carry, (SLAB, width))],
        [groups] + [0] * 12,
        [(rows + HALO, width, F32), (8, width, F32), (GROUP, 2 * GROUP, BF)],
        [(rows + HALO, GROUP), (rows + 2 * HALO, GROUP), (rows + SLAB, GROUP), (GROUP, 2 * GROUP)], "recurrence_back",
    )
    edge_rows = lax.ppermute(drec[:HALO], "tensor", [(k, k - 1) for k in range(1, n)])
    rec_low = (drec[HALO:] + jnp.pad(edge_rows, ((rows - HALO, 0), (0, 0)))) * live
    grad_in = jnp.concatenate([grad_pre.astype(BF), rec_low.astype(BF)], axis=1)
    g_in = to_owner(dot(first_own, grad_in, ((0,), (0,))), 2)
    grad_first = dot(grad_in, w_in, ((1,), (1,)))
    first_unit = inputs * first_rate
    gain_one = jnp.sum(grad_first * first_unit, axis=0)
    grad_tokens = grad_hidden + norm_back(grad_first, first_unit, first_rate, gain[0])
    grad_tokens = permute_rows(grad_tokens.astype(BF), inverse)
    grad_tokens = lax.all_gather(grad_tokens, "tensor", axis=0, tiled=True)

    d_gain = permute_gain(jnp.stack([gain_one, gain_two]), inverse)
    d_chan = jnp.concatenate([dpar[:7], dpar[7:] * 8.0 * jax.nn.sigmoid(-chans[7:])])
    small = lax.psum(jnp.concatenate([d_gain.reshape(-1), d_chan.reshape(-1)]), ("tensor", "dp"))
    d_gain = small[: d_gain.size].reshape(2, d_model)
    d_gain = lax.dynamic_slice_in_dim(d_gain, place * d_own, d_own, axis=1)
    d_chan = small[d_gain.size * size :].reshape(8, heads, head)
    d_chan = lax.dynamic_slice(d_chan, (0, turn * heads_own, place * chan.shape[2]), chan.shape)
    blocks = [
        d_dense[:, k * head : (k + 1) * head, m * GROUP + k * head : m * GROUP + (k + 1) * head]
        for m in range(2)
        for k in range(per)
    ]
    d_lru = jnp.stack(blocks).reshape(2, per, groups, head, head).transpose(0, 2, 1, 3, 4)
    d_lru = d_lru.reshape(2, n, heads_own, size, head // size, head).transpose(1, 3, 0, 2, 4, 5)
    d_lru = lax.psum_scatter(d_lru.reshape(n * size, -1), ("tensor", "dp"), scatter_dimension=0)
    d_lru = d_lru.reshape(w_lru.shape).astype(F32)
    g_gate, g_up = g_gu[:, :hidden_units], g_gu[:, hidden_units:]
    return (
        output, grad_tokens, d_gain[0], d_gain[1], g_in[0], g_in[1], d_chan, d_lru,
        g_back[0].T, jnp.stack([g_gate, g_up]), g_dn.T,
    )


def solution(mesh):
    in_specs = (
        P("dp", None),
        P("dp"),
        P(None, "dp"),
        P("dp", "tensor"),
        P("dp", "tensor"),
        P(None, "tensor", "dp"),
        P(None, "tensor", "dp", None),
        P("tensor", "dp"),
        P(None, "dp", "tensor"),
        P("tensor", "dp"),
        P("dp", None),
    )
    out_specs = (
        P("dp", None),
        P("dp", None),
        P("dp"),
        P("dp"),
        P("dp", "tensor"),
        P("dp", "tensor"),
        P(None, "tensor", "dp"),
        P(None, "tensor", "dp", None),
        P("tensor", "dp"),
        P(None, "dp", "tensor"),
        P("tensor", "dp"),
    )
    body = functools.partial(on_device, mesh.shape["dp"], mesh.shape["tensor"])
    return jax.shard_map(body, mesh=mesh, in_specs=in_specs, out_specs=out_specs, check_vma=False)
```

time: 2540 us -> 1740 us (0.69)
  waiting for transfers between devices: 1320 us -> 894 us
  local copies, waits for them, and re-layouts: 496 us -> 240 us
  other arithmetic: 292 us -> 126 us
  Pallas kernels: 0 us -> 112 us
  matrix products: 345 us -> 271 us
  starting transfers between devices: 1.63 us -> 41.7 us
    psum x3 -> x1, waiting for transfers between devices: 1120 us -> 0.01 us  [on_device(): lax.psum(jnp.concatenate([d_gain.reshape(-1), d_chan.reshape(-1)]), ('ten...]
    ppermute x0 -> x41, waiting for transfers between devices: none -> 320 us  [the longest x40 320 us: exchange(): return lax.ppermute(values, 'dp', [(k, k ^ 1 << bit) for k in range(size)])]
    pad x88 -> x0, local copies, waits for them, and re-layouts: 241 us -> none  [recurrence(): _, states = lax.associative_scan(combine, (decays, driven), axis=1)]
    all_gather x5 -> x7, waiting for transfers between devices: 53.3 us -> 288 us  [the longest x1 149 us: on_device(): grad_tokens = lax.all_gather(grad_tokens, 'tensor', axis=0, tiled=True)]
    reduce_scatter x5 -> x6, waiting for transfers between devices: 131 us -> 285 us  [the longest x4 232 us: on_device(): lax.psum_scatter(share, 'tensor', scatter_dimension=0, tiled=True)]
    slice x91 -> x31, local copies, waits for them, and re-layouts: 194 us -> 57 us  [the longest x4 18.1 us: collect(): kept = add_low(full[:half], exchange(full[half:], 0, size))]
    pallas_call x0 -> x7, Pallas kernels: none -> 112 us  [the longest x3 60.5 us: kernel_call(): pl.pallas_call(body, grid_spec=pltpu.PrefetchScalarGridSpec(num_scalar_pr...]
    reduce_sum x8 -> x3, other arithmetic: 90.2 us -> 6.19 us  [the longest x1 3.96 us: on_device(): gain_two = jnp.sum(grad_second * second_unit, axis=0)]
  transfers between devices with their start and end apart: 15 -> 56, of which waited for: 7 -> 31; matrix products, arithmetic and copies ran while one was open for 23% -> 31% of each run, Pallas kernels for 0% -> 6%
where the time goes in v1:
time: 1740 us
  waiting for transfers between devices  894 us (51%)
  matrix products  271 us (16%)
  local copies, waits for them, and re-layouts  240 us (14%)
  other arithmetic  126 us (7%)
  Pallas kernels  112 us (6%)
  starting transfers between devices  41.7 us (2%)
  blocking collectives  36.1 us (2%)
    ppermute x40, waiting for transfers between devices, exchange(): return lax.ppermute(values, 'dp', [(k, k ^ 1 << bit) for k in range(size)])  320 us
    dot_general x18, matrix products, dot(): lax.dot_general(left, right, (dims, ((), ())), preferred_element_type=F32)  271 us
    reduce_scatter x4, waiting for transfers between devices, on_device(): lax.psum_scatter(share, 'tensor', scatter_dimension=0, tiled=True)  232 us
    all_gather x1, waiting for transfers between devices, on_device(): grad_tokens = lax.all_gather(grad_tokens, 'tensor', axis=0, tiled=True)  149 us
    unnamed x207, local copies, waits for them, and re-layouts  98.3 us
    all_gather x1, waiting for transfers between devices, on_device(): output = lax.all_gather(result, 'tensor', axis=0, tiled=True)  85.5 us
    pallas_call x3, Pallas kernels, kernel_call(): pl.pallas_call(body, grid_spec=pltpu.PrefetchScalarGridSpec(num_scalar_pr...  60.5 us
    reduce_scatter x2, waiting for transfers between devices, to_owner(): return lax.psum_scatter(own, 'tensor', scatter_dimension=0).astype(F32)  53.2 us
  transfers between devices with their start and end apart: 56, of which 31 were waited for; matrix products, arithmetic and copies ran while one was open for 31% of the time, Pallas kernels for 6%

profile of v1, /device:TPU:0, one launch (start us, length us, event | category | flops | bytes accessed | tf_op | source)
XLA Modules:
  0.0 1737.3 jit_solution(13682047731156665778)
XLA Ops:
  26.8 10.2 permute.4
  43.4 9.3 all_gather.41
  54.0 16.1 all-gather.16.cloned.1.call-done
  79.2 23.4 %collective-permute-done = bf16[128,5120]{0,1:T(8,128)(2,1)S(1)} collective-permute-done((bf16[128,5120]{0,1:T(8,128)(2,1)S(1)}, bf16[128,5120]{0,1:T(8,128)(2,1)S(1)}, u32[]{:S(2)}, u32[]{:S(2)}) %collective-permute-start) | collective-permute-done | bytes 1310752 | tf_op jit(solution)/shard_map/ppermute | solution.py:27
  116.8 57.1 %collective-permute-done.1 = bf16[256,5120]{0,1:T(8,128)(2,1)S(1)} collective-permute-done((bf16[256,5120]{0,1:T(8,128)(2,1)S(1)}, bf16[256,5120]{0,1:T(8,128)(2,1)S(1)}, u32[]{:S(2)}, u32[]{:S(2)}) %collective-permute-start.1) | collective-permute-done | bytes 2621472 | tf_op jit(solution)/shard_map/ppermute | solution.py:27
  181.0 7.0 copy-done.53
  198.8 9.1 collective-permute-done.5
  210.2 14.3 collective-permute-done.11
  230.5 8.0 collective-permute-done.7
  241.4 25.2 %collective-permute-done.6 = bf16[256,2560]{0,1:T(8,128)(2,1)S(1)} collective-permute-done((bf16[256,2560]{0,1:T(8,128)(2,1)S(1)}, bf16[256,2560]{0,1:T(8,128)(2,1)S(1)}, u32[]{:S(2)}, u32[]{:S(2)}) %collective-permute-start.6) | collective-permute-done | bytes 1310752 | tf_op jit(solution)/shard_map/ppermute | solution.py:27
  272.5 9.4 collective-permute-done.12
  319.1 8.2 squeeze.59
  342.0 9.3 constant_dynamic-update-slice_fusion.6
  351.3 18.3 %fusion.73.pre_ref = f32[528,5120]{1,0:T(8,128)} fusion(bf16[528,2048]{1,0:T(8,128)(2,1)S(1)} %copy-done.37, bf16[2048,5120]{0,1:T(8,128)(2,1)} %constant_dynamic-update-slice_fusion.6), kind=kOutput, calls=%fused_computation.275 | convolution fusion | flops 11072962560 | bytes 33947648 | tf_op jit(solution)/shard_map/dot_general | solution.py:23
  369.6 19.7 %recurrence.1 = (f32[512,2560]{1,0:T(8,128)}, f32[512,2560]{1,0:T(8,128)}, f32[512,2560]{1,0:T(8,128)}, f32[512,2560]{1,0:T(8,128)}, f32[512,2560]{1,0:T(8,128)}, /*index=5*/f32[512,2560]{1,0:T(8,128)}) custom-call(s32[1]{0:T(128)} %sub.26.live_ref, f32[528,5120]{1,0:T(8,128)} %fusion.73.pre_ref, f32[8,2560]{1,0:T(8,128)} %pad_maximum_fusion.28.par_ref, ...), custom_call_target="tpu_custom_call" | custom-call | tf_op jit(solution)/shard_map/recurrence/pallas_call | solution.py:273
  391.1 13.2 all-gather.6
  412.6 9.4 multiply_reduce_fusion.2
  427.3 7.1 collective-permute-done.17
  437.0 13.7 collective-permute-done.18
  454.4 20.0 %permute.6 = bf16[2,4,256,2048]{3,2,1,0:T(8,128)(2,1)} custom-call(s32[16]{0:T(128)} %multiply_add_fusion.table_ref, bf16[4,2,256,2048]{3,2,1,0:T(8,128)(2,1)} %bitcast.188), custom_call_target="tpu_custom_call" | custom-call | tf_op jit(solution)/shard_map/permute/pallas_call | solution.py:88
  474.4 7.1 fusion.64
  491.7 12.9 all-gather.20.cloned.1.call-done
  504.6 19.1 %fusion.75 = f32[1024,3072]{1,0:T(8,128)} fusion(bf16[1024,2048]{1,0:T(8,128)(2,1)} %all-gather.20.cloned.1.call-done, bf16[2048,3072]{1,0:T(8,128)(2,1)} %constant_dynamic-update-slice_fusion.34), kind=kOutput, calls=%fused_computation.277 | convolution fusion | flops 12884901888 | bytes 29360128 | tf_op jit(solution)/shard_map/dot_general | solution.py:23
  523.7 16.6 fusion.13
  541.9 19.0 %fusion.36 = bf16[1024,2048]{1,0:T(8,128)(2,1)} fusion(bf16[2048,3072]{1,0:T(8,128)(2,1)} %constant_dynamic-update-slice_fusion.34, bf16[1024,1536]{1,0:T(8,128)(2,1)} %get-tuple-element.122, bf16[1024,1536]{1,0:T(8,128)(2,1)S(1)} %get-tuple-element.121), kind=kOutput, calls=%fused_computation.81 | convolution fusion | flops 12899581952 | bytes 23068672 | tf_op jit(solution)/shard_map/dot_general | solution.py:23
  561.4 24.5 %all-gather.18.cloned.1.call-done = bf16[1024,2048]{1,0:T(8,128)(2,1)} async-done(((bf16[256,2048]{1,0:T(8,128)(2,1)}), bf16[1024,2048]{1,0:T(8,128)(2,1)}) %all-gather.18.cloned.1.call-update) | async-done | bytes 4194320 | tf_op jit(solution)/shard_map/all_gather | solution.py:369
  585.9 19.1 %fusion.74 = f32[1024,3072]{1,0:T(8,128)} fusion(bf16[1024,2048]{1,0:T(8,128)(2,1)} %all-gather.18.cloned.1.call-done, bf16[2048,3072]{1,0:T(8,128)(2,1)} %constant_dynamic-update-slice_fusion.34), kind=kOutput, calls=%fused_computation.276 | convolution fusion | flops 12884901888 | bytes 29360128 | tf_op jit(solution)/shard_map/dot_general | solution.py:23
  605.0 17.0 fusion.6
  623.6 18.5 %fusion.35 = bf16[1024,2048]{1,0:T(8,128)(2,1)} fusion(bf16[2048,3072]{1,0:T(8,128)(2,1)} %constant_dynamic-update-slice_fusion.34, bf16[1024,1536]{1,0:T(8,128)(2,1)} %get-tuple-element.120, bf16[1024,1536]{1,0:T(8,128)(2,1)S(1)} %get-tuple-element.119), kind=kOutput, calls=%fused_computation.80 | convolution fusion | flops 12899581952 | bytes 23068672 | tf_op jit(solution)/shard_map/dot_general | solution.py:23
  642.4 11.0 convolution_convert_fusion.3
  653.5 11.1 convolution_convert_fusion.4
  666.8 76.3 %reduce-scatter.11.cloned.1.call-done = bf16[256,2048]{1,0:T(8,128)(2,1)} async-done(((bf16[1024,2048]{1,0:T(8,128)(2,1)}), bf16[256,2048]{1,0:T(8,128)(2,1)}) %reduce-scatter.11.cloned.1.call-update) | async-done | bytes 1048592 | tf_op jit(solution)/shard_map/reduce_scatter | solution.py:377
  747.1 75.6 %reduce-scatter.9.cloned.1.call-done = bf16[256,2048]{1,0:T(8,128)(2,1)} async-done(((bf16[1024,2048]{1,0:T(8,128)(2,1)}), bf16[256,2048]{1,0:T(8,128)(2,1)}) %reduce-scatter.9.cloned.1.call-update) | async-done | bytes 1048592 | tf_op jit(solution)/shard_map/reduce_scatter | solution.py:379
  822.7 79.7 %reduce-scatter.7.cloned.1.call-done = bf16[256,2048]{1,0:T(8,128)(2,1)} async-done(((bf16[1024,2048]{1,0:T(8,128)(2,1)}), bf16[256,2048]{1,0:T(8,128)(2,1)}) %reduce-scatter.7.cloned.1.call-update) | async-done | bytes 1048592 | tf_op jit(solution)/shard_map/reduce_scatter | solution.py:379
  907.3 11.5 fusion.42.grad_ref
  930.1 13.0 back_scan.1
  944.1 13.7 all-gather.7
  959.9 27.7 %recurrence_back.1 = (f32[528,2560]{1,0:T(8,128)}, f32[8,2560]{1,0:T(8,128)}, bf16[4,640,1280]{2,1,0:T(8,128)(2,1)}) custom-call(s32[1]{0:T(128)} %sub.26.live_ref, f32[528,5120]{1,0:T(8,128)} %fusion.73.pre_ref, f32[8,2560]{1,0:T(8,128)} %pad_maximum_fusion.28.par_ref, bf16[4,640,1280]{2,1,0:T(8,128)(2,1)} %constant_dynamic-update-slice_fusion.13.w_ref, ...), custom_call_target="tpu_custom_call" | custom-call | tf_op jit(solution)/shard_map/recurrence_back/pallas_call | solution.py:273
  1000.3 11.2 fusion.20
  1011.5 7.3 add_convert_fusion.4
  1025.8 17.5 %multiply_reduce_fusion = (f32[2048]{0:T(1024)S(1)}, f32[512]{0:T(512)S(1)}, f32[512,2048]{1,0:T(8,128)}) fusion(f32[1,1,528,2048]{3,2,1,0:T(8,128)} %convert_element_type.360, f32[512]{0:T(512)S(1)} %slice.366, f32[2048]{0:T(1024)S(1)} %bitcast.217, bf16[2048,5120]{0,1:T(8,128)(2,1)} %constant_dynamic-update-slice_fusion.6, ...), kind=kOutput, calls=%fused_computation.67 | convolution fusion | flops 10754193408 | bytes 34623488 | tf_op jit(solution)/shard_map/dot_general | solution.py:23
  1043.9 7.6 collective-permute-done.27
  1073.8 9.0 collective-permute-done.28
  1084.6 10.4 permute.5
  1095.1 17.1 convolution_convert_fusion
  1112.2 8.9 slice.477
  1121.0 18.8 %fusion.31 = bf16[2048,3072]{1,0:T(8,128)(2,1)} fusion(bf16[1024,2048]{1,0:T(8,128)(2,1)} %all-gather.18.cloned.1.call-done, bf16[1024,1536]{1,0:T(8,128)(2,1)} %get-tuple-element.120, bf16[1024,1536]{1,0:T(8,128)(2,1)S(1)} %copy-done.77), kind=kOutput, calls=%fused_computation.74 | convolution fusion | flops 12897484800 | bytes 23068672 | tf_op jit(solution)/shard_map/dot_general | solution.py:23
  1139.8 21.8 %add_convert_fusion = bf16[2048,3072]{1,0:T(8,128)(2,1)} fusion(bf16[1024,2048]{1,0:T(8,128)(2,1)} %all-gather.20.cloned.1.call-done, bf16[2048,3072]{1,0:T(8,128)(2,1)} %fusion.31, bf16[1024,1536]{1,0:T(8,128)(2,1)} %get-tuple-element.122, bf16[1024,1536]{1,0:T(8,128)(2,1)} %copy-done.78), kind=kOutput, calls=%fused_computation.2 | convolution fusion | flops 12916359168 | bytes 35651584 | tf_op jit(solution)/shard_map/dot_general | solution.py:23
  1168.3 8.8 convolution_convert_fusion.2
  1179.6 10.6 permute.7
  1190.3 10.5 add_convert_fusion.2
  1201.1 9.9 add_convert_fusion.1
  1223.4 73.0 %collective-permute-done.37 = bf16[256,1536]{1,0:T(8,128)(2,1)} collective-permute-done((bf16[256,1536]{1,0:T(8,128)(2,1)}, bf16[256,1536]{1,0:T(8,128)(2,1)}, u32[]{:S(2)}, u32[]{:S(2)}) %collective-permute-start.37) | collective-permute-done | bytes 786464 | tf_op jit(solution)/shard_map/ppermute | solution.py:27
  1302.0 7.4 add_convert_fusion.7
  1311.9 7.5 add_convert_fusion.3
  1325.4 17.4 collective-permute-done.25
  1345.6 8.1 collective-permute-done.23
  1362.4 12.9 collective-permute-done.32
  1375.3 9.7 collective-permute-done.34
  1423.2 85.5 %all-gather.24.cloned.1.call-done = bf16[1,1,2048,2048]{3,2,1,0:T(8,128)(2,1)} async-done(((bf16[1,1,512,2048]{3,2,1,0:T(8,128)(2,1)}), bf16[1,1,2048,2048]{3,2,1,0:T(8,128)(2,1)}) %all-gather.24.cloned.1.call-update) | async-done | bytes 8388624 | tf_op jit(solution)/shard_map/all_gather | solution.py:393
  1508.7 149.4 %all-gather.26.cloned.1.call-done = bf16[1,1,2048,2048]{3,2,1,0:T(8,128)(2,1)} async-done(((bf16[1,1,512,2048]{3,2,1,0:T(8,128)(2,1)}), bf16[1,1,2048,2048]{3,2,1,0:T(8,128)(2,1)}) %all-gather.26.cloned.1.call-update) | async-done | bytes 8388624 | tf_op jit(solution)/shard_map/all_gather | solution.py:433
  1658.1 53.2 %reduce-scatter.15.cloned.1.call-done = bf16[1,2,256,640]{3,2,1,0:T(8,128)(2,1)} async-done(((bf16[4,2,256,640]{3,2,1,0:T(8,128)(2,1)}), bf16[1,2,256,640]{3,2,1,0:T(8,128)(2,1)}) %reduce-scatter.15.cloned.1.call-update) | async-done | bytes 655376 | tf_op jit(solution)/shard_map/reduce_scatter | solution.py:403
  1713.6 8.4 copy.177
  1722.1 8.4 copy.178
  (459 shorter events, 329.6 us)
Async XLA Ops:
  7.2 63.0 %all-gather.16.cloned.1.call-start = ((), (), s32[]{:S(2)}) async-start(), calls=%async_computation.6 | async-start | bytes 3276800 | tf_op jit(solution)/shard_map/all_gather | solution.py:317
  12.5 175.5 %all-gather.22.cloned.1.call-start = ((), (), s32[]{:S(2)}) async-start(), calls=%async_computation.16 | async-start | bytes 1638400 | tf_op jit(solution)/shard_map/all_gather | solution.py:317
  14.3 93.6 %collective-permute-start.10 = (bf16[128,3072]{1,0:T(8,128)(2,1)}, bf16[128,3072]{1,0:T(8,128)(2,1)}, u32[]{:S(2)}, u32[]{:S(2)}) collective-permute-start(bf16[128,3072]{1,0:T(8,128)(2,1)} %get-tuple-element.116), channel_id=1, source_target_pairs={{0,8},{4,12},{8,0},{12,4},{16,24},{20,28},{24,16},{28,20},{1,9},{5... | collective-permute-start | bytes 2359304 | tf_op jit(solution)/shard_map/ppermute | solution.py:27
  19.2 85.3 %collective-permute-start.15 = (bf16[128,1536]{0,1:T(8,128)(2,1)}, bf16[128,1536]{0,1:T(8,128)(2,1)S(1)}, u32[]{:S(2)}, u32[]{:S(2)}) collective-permute-start(bf16[128,1536]{0,1:T(8,128)(2,1)} %get-tuple-element.185), channel_id=1, source_target_pairs={{0,8},{4,12},{8,0},{12,4},{16,24},{20,28},{24,16},{28,20},{1,9},{5... | collective-permute-start | bytes 1179656 | tf_op jit(solution)/shard_map/ppermute | solution.py:27
  20.8 264.3 %all-gather.28.cloned.1.call-start = ((), (), s32[]{:S(2)}) async-start(), calls=%async_computation.19 | async-start | bytes 3463680 | tf_op jit(solution)/shard_map/all_gather | solution.py:322
  22.0 482.7 %all-gather.20.cloned.1.call-start = ((), (), s32[]{:S(2)}) async-start(), calls=%async_computation.9 | async-start | bytes 5242880 | tf_op jit(solution)/shard_map/all_gather | solution.py:369
  53.4 351.6 %copy-start.64 = (f32[512]{0:T(512)}, f32[512]{0:T(512)S(1)}, u32[]{:S(2)}) copy-start(f32[512]{0:T(512)S(1)} %fusion.53) | copy-start | bytes 6148
  72.1 30.6 %collective-permute-start = (bf16[128,5120]{0,1:T(8,128)(2,1)S(1)}, bf16[128,5120]{0,1:T(8,128)(2,1)S(1)}, u32[]{:S(2)}, u32[]{:S(2)}) collective-permute-start(bf16[128,5120]{0,1:T(8,128)(2,1)S(1)} %bitcast.182), channel_id=1, source_target_pairs={{0,8},{4,12},{8,0},{12,4},{16,24},{20,28},{24,16},{28,20},{1,9},{5... | collective-permute-start | bytes 3932168 | tf_op jit(solution)/shard_map/ppermute | solution.py:27
  75.7 346.3 %copy-start.47 = (f32[1,2048]{1,0:T(1,128)}, f32[1,2048]{1,0:T(1,128)S(1)}, u32[]{:S(2)}) copy-start(f32[1,2048]{1,0:T(1,128)S(1)} %get-tuple-element.204) | copy-start | bytes 24580
  77.7 34.2 %collective-permute-start.2 = (bf16[128,5120]{0,1:T(8,128)(2,1)S(1)}, bf16[128,5120]{0,1:T(8,128)(2,1)S(1)}, u32[]{:S(2)}, u32[]{:S(2)}) collective-permute-start(bf16[128,5120]{0,1:T(8,128)(2,1)S(1)} %bitcast.179), channel_id=1, source_target_pairs={{0,16},{4,20},{8,24},{12,28},{16,0},{20,4},{24,8},{28,12},{1,17},{... | collective-permute-start | bytes 3932168 | tf_op jit(solution)/shard_map/ppermute | solution.py:27
  102.9 70.9 %collective-permute-start.1 = (bf16[256,5120]{0,1:T(8,128)(2,1)S(1)}, bf16[256,5120]{0,1:T(8,128)(2,1)S(1)}, u32[]{:S(2)}, u32[]{:S(2)}) collective-permute-start(bf16[256,5120]{0,1:T(8,128)(2,1)S(1)} %pad_maximum_fusion.14), channel_id=1, source_target_pairs={{0,16},{4,20},{8,24},{12,28},{16,0},{20,4},{24,8},{28,12},{1,17},{... | collective-permute-start | bytes 7864328 | tf_op jit(solution)/shard_map/ppermute | solution.py:27
  106.6 88.1 %collective-permute-start.16 = (bf16[256,1536]{0,1:T(8,128)(2,1)}, bf16[256,1536]{0,1:T(8,128)(2,1)S(1)}, u32[]{:S(2)}, u32[]{:S(2)}) collective-permute-start(bf16[256,1536]{0,1:T(8,128)(2,1)} %pad_maximum_fusion.24), channel_id=1, source_target_pairs={{0,16},{4,20},{8,24},{12,28},{16,0},{20,4},{24,8},{28,12},{1,17},{... | collective-permute-start | bytes 2359304 | tf_op jit(solution)/shard_map/ppermute | solution.py:27
  110.5 114.0 %collective-permute-start.11 = (bf16[256,3072]{1,0:T(8,128)(2,1)}, bf16[256,3072]{1,0:T(8,128)(2,1)}, u32[]{:S(2)}, u32[]{:S(2)}) collective-permute-start(bf16[256,3072]{1,0:T(8,128)(2,1)} %pad_maximum_fusion.18), channel_id=1, source_target_pairs={{0,16},{4,20},{8,24},{12,28},{16,0},{20,4},{24,8},{28,12},{1,17},{... | collective-permute-start | bytes 4718600 | tf_op jit(solution)/shard_map/ppermute | solution.py:27
  112.3 66.7 %collective-permute-start.3 = (bf16[256,5120]{0,1:T(8,128)(2,1)S(1)}, bf16[256,5120]{0,1:T(8,128)(2,1)S(1)}, u32[]{:S(2)}, u32[]{:S(2)}) collective-permute-start(bf16[256,5120]{0,1:T(8,128)(2,1)S(1)} %pad_maximum_fusion.15), channel_id=1, source_target_pairs={{0,8},{4,12},{8,0},{12,4},{16,24},{20,28},{24,16},{28,20},{1,9},{5... | collective-permute-start | bytes 7864328 | tf_op jit(solution)/shard_map/ppermute | solution.py:27
  188.0 154.0 %collective-permute-start.4 = (bf16[1024,5120]{0,1:T(8,128)(2,1)}, bf16[1024,5120]{0,1:T(8,128)(2,1)}, u32[]{:S(2)}, u32[]{:S(2)}) collective-permute-start(bf16[1024,5120]{0,1:T(8,128)(2,1)} %get-tuple-element.149), channel_id=1, source_target_pairs={{0,4},{4,0},{8,12},{12,8},{16,20},{20,16},{24,28},{28,24},{1,5},{5... | collective-permute-start | bytes 31457288 | tf_op jit(solution)/shard_map/ppermute | solution.py:27
  190.6 17.3 collective-permute-start.5
  197.0 41.4 %collective-permute-start.7 = (bf16[128,2560]{0,1:T(8,128)(2,1)S(1)}, bf16[128,2560]{0,1:T(8,128)(2,1)S(1)}, u32[]{:S(2)}, u32[]{:S(2)}) collective-permute-start(bf16[128,2560]{0,1:T(8,128)(2,1)S(1)} %bitcast.193), channel_id=1, source_target_pairs={{0,16},{4,20},{8,24},{12,28},{16,0},{20,4},{24,8},{28,12},{1,17},{... | collective-permute-start | bytes 1966088 | tf_op jit(solution)/shard_map/ppermute | solution.py:27
  209.1 57.4 %collective-permute-start.6 = (bf16[256,2560]{0,1:T(8,128)(2,1)S(1)}, bf16[256,2560]{0,1:T(8,128)(2,1)S(1)}, u32[]{:S(2)}, u32[]{:S(2)}) collective-permute-start(bf16[256,2560]{0,1:T(8,128)(2,1)S(1)} %pad_maximum_fusion.20), channel_id=1, source_target_pairs={{0,16},{4,20},{8,24},{12,28},{16,0},{20,4},{24,8},{28,12},{1,17},{... | collective-permute-start | bytes 3932168 | tf_op jit(solution)/shard_map/ppermute | solution.py:27
  229.0 52.9 %collective-permute-start.12 = (bf16[128,3072]{1,0:T(8,128)(2,1)S(1)}, bf16[128,3072]{1,0:T(8,128)(2,1)S(1)}, u32[]{:S(2)}, u32[]{:S(2)}) collective-permute-start(bf16[128,3072]{1,0:T(8,128)(2,1)S(1)} %get-tuple-element.114), channel_id=1, source_target_pairs={{0,16},{4,20},{8,24},{12,28},{16,0},{20,4},{24,8},{28,12},{1,17},{... | collective-permute-start | bytes 2359304 | tf_op jit(solution)/shard_map/ppermute | solution.py:27
  238.6 31.4 %collective-permute-start.8 = (bf16[256,2560]{0,1:T(8,128)(2,1)S(1)}, bf16[256,2560]{0,1:T(8,128)(2,1)S(1)}, u32[]{:S(2)}, u32[]{:S(2)}) collective-permute-start(bf16[256,2560]{0,1:T(8,128)(2,1)S(1)} %pad_maximum_fusion.21), channel_id=1, source_target_pairs={{0,8},{4,12},{8,0},{12,4},{16,24},{20,28},{24,16},{28,20},{1,9},{5... | collective-permute-start | bytes 3932168 | tf_op jit(solution)/shard_map/ppermute | solution.py:27
  271.5 65.1 %collective-permute-start.9 = (bf16[1024,2560]{0,1:T(8,128)(2,1)}, bf16[1024,2560]{0,1:T(8,128)(2,1)}, u32[]{:S(2)}, u32[]{:S(2)}) collective-permute-start(bf16[1024,2560]{0,1:T(8,128)(2,1)} %get-tuple-element.165), channel_id=1, source_target_pairs={{0,4},{4,0},{8,12},{12,8},{16,20},{20,16},{24,28},{28,24},{1,5},{5... | collective-permute-start | bytes 15728648 | tf_op jit(solution)/shard_map/ppermute | solution.py:27
  283.1 50.0 %collective-permute-start.13 = (bf16[256,3072]{1,0:T(8,128)(2,1)}, bf16[256,3072]{1,0:T(8,128)(2,1)}, u32[]{:S(2)}, u32[]{:S(2)}) collective-permute-start(bf16[256,3072]{1,0:T(8,128)(2,1)} %pad_maximum_fusion.19), channel_id=1, source_target_pairs={{0,8},{4,12},{8,0},{12,4},{16,24},{20,28},{24,16},{28,20},{1,9},{5... | collective-permute-start | bytes 4718600 | tf_op jit(solution)/shard_map/ppermute | solution.py:27
  336.6 149.0 %collective-permute-start.14 = (bf16[1024,3072]{1,0:T(8,128)(2,1)}, bf16[1024,3072]{1,0:T(8,128)(2,1)}, u32[]{:S(2)}, u32[]{:S(2)}) collective-permute-start(bf16[1024,3072]{1,0:T(8,128)(2,1)} %get-tuple-element.157), channel_id=1, source_target_pairs={{0,4},{4,0},{8,12},{12,8},{16,20},{20,16},{24,28},{28,24},{1,5},{5... | collective-permute-start | bytes 18874376 | tf_op jit(solution)/shard_map/ppermute | solution.py:27
  369.6 43.0 %slice-start = ((s8[4325376]{0:T(1024)(128)(4,1)}), s8[131072]{0:T(1024)(128)(4,1)S(1)}, s32[]{:S(2)}) async-start(s8[4325376]{0:T(1024)(128)(4,1)} %bitcast.174), calls=%async_computation.21 | async-start | bytes 262144
  424.8 161.2 %all-gather.18.cloned.1.call-start = ((), (), s32[]{:S(2)}) async-start(), calls=%async_computation.7 | async-start | bytes 5242880 | tf_op jit(solution)/shard_map/all_gather | solution.py:369
  425.8 8.7 collective-permute-start.17
  434.5 16.2 collective-permute-start.18
  454.4 27.1 %collective-permute-start.19 = (bf16[1024,1536]{0,1:T(8,128)(2,1)}, bf16[1024,1536]{0,1:T(8,128)(2,1)S(1)}, u32[]{:S(2)}, u32[]{:S(2)}) collective-permute-start(bf16[1024,1536]{0,1:T(8,128)(2,1)} %get-tuple-element.179), channel_id=1, source_target_pairs={{0,4},{4,0},{8,12},{12,8},{16,20},{20,16},{24,28},{28,24},{1,5},{5... | collective-permute-start | bytes 9437192 | tf_op jit(solution)/shard_map/ppermute | solution.py:27
  491.5 175.4 %reduce-scatter.13.cloned.1.call-start = ((), (), s32[]{:S(2)}) async-start(), calls=%async_computation.12 | async-start | bytes 5242880 | tf_op jit(solution)/shard_map/reduce_scatter | solution.py:377
  540.3 102.1 %copy-start.73 = (bf16[1024,1536]{1,0:T(8,128)(2,1)}, bf16[1024,1536]{1,0:T(8,128)(2,1)S(1)}, u32[]{:S(2)}) copy-start(bf16[1024,1536]{1,0:T(8,128)(2,1)S(1)} %get-tuple-element.124) | copy-start | bytes 9437188
  561.0 182.1 %reduce-scatter.11.cloned.1.call-start = ((), (), s32[]{:S(2)}) async-start(), calls=%async_computation.11 | async-start | bytes 5242880 | tf_op jit(solution)/shard_map/reduce_scatter | solution.py:377
  642.1 180.6 %reduce-scatter.9.cloned.1.call-start = ((), (), s32[]{:S(2)}) async-start(), calls=%async_computation.10 | async-start | bytes 5242880 | tf_op jit(solution)/shard_map/reduce_scatter | solution.py:379
  653.4 249.0 %reduce-scatter.7.cloned.1.call-start = ((), (), s32[]{:S(2)}) async-start(), calls=%async_computation.8 | async-start | bytes 5242880 | tf_op jit(solution)/shard_map/reduce_scatter | solution.py:379
  664.6 78.5 %copy-start.48 = (f32[1,2048]{1,0:T(1,128)S(1)}, f32[1,2048]{1,0:T(1,128)}, u32[]{:S(2)}) copy-start(f32[1,2048]{1,0:T(1,128)} %copy-done.47) | copy-start | bytes 24580
  664.6 78.5 %copy-start.58 = (f32[512]{0:T(512)S(1)}, f32[512]{0:T(512)}, u32[]{:S(2)}) copy-start(f32[512]{0:T(512)} %copy-done.57) | copy-start | bytes 6148
  664.6 733.5 %all-reduce.5.cloned.1.call-start = ((), (), s32[]{:S(2)}) async-start(), calls=%async_computation.13 | async-start | bytes 196608 | tf_op jit(solution)/shard_map/psum | solution.py:437
  664.9 82.2 %copy-start.68 = (s32[16]{0:T(128)}, s32[16]{0:T(128)S(1)}, u32[]{:S(2)}) copy-start(s32[16]{0:T(128)S(1)} %select_reduce_fusion.table_ref) | copy-start | bytes 196
  666.8 235.6 %copy-start.18 = (bf16[256,2048]{1,0:T(8,128)(2,1)S(1)}, bf16[256,2048]{1,0:T(8,128)(2,1)}, u32[]{:S(2)}) copy-start(bf16[256,2048]{1,0:T(8,128)(2,1)} %reduce-scatter.13.cloned.1.call-done) | copy-start | bytes 3145732
  930.1 81.3 %collective-permute-start.26 = (bf16[1024,2560]{1,0:T(8,128)(2,1)}, bf16[1024,2560]{1,0:T(8,128)(2,1)}, u32[]{:S(2)}, u32[]{:S(2)}) collective-permute-start(bf16[1024,2560]{1,0:T(8,128)(2,1)} %slice.490), channel_id=1, source_target_pairs={{0,4},{4,0},{8,12},{12,8},{16,20},{20,16},{24,28},{28,24},{1,5},{5... | collective-permute-start | bytes 15728648 | tf_op jit(solution)/shard_map/ppermute | solution.py:27
  988.6 11.7 collective-permute-start.20
  1022.9 28.6 %collective-permute-start.27 = (bf16[256,2560]{1,0:T(8,128)(2,1)}, bf16[256,2560]{1,0:T(8,128)(2,1)}, u32[]{:S(2)}, u32[]{:S(2)}) collective-permute-start(bf16[256,2560]{1,0:T(8,128)(2,1)} %get-tuple-element.139), channel_id=1, source_target_pairs={{0,16},{4,20},{8,24},{12,28},{16,0},{20,4},{24,8},{28,12},{1,17},{... | collective-permute-start | bytes 3932168 | tf_op jit(solution)/shard_map/ppermute | solution.py:27
  1024.4 28.3 %collective-permute-start.29 = (bf16[256,2560]{1,0:T(8,128)(2,1)}, bf16[256,2560]{1,0:T(8,128)(2,1)}, u32[]{:S(2)}, u32[]{:S(2)}) collective-permute-start(bf16[256,2560]{1,0:T(8,128)(2,1)} %get-tuple-element.140), channel_id=1, source_target_pairs={{0,8},{4,12},{8,0},{12,4},{16,24},{20,28},{24,16},{28,20},{1,9},{5... | collective-permute-start | bytes 3932168 | tf_op jit(solution)/shard_map/ppermute | solution.py:27
  1058.8 13.5 collective-permute-start.30
  1060.1 358.4 %all-reduce.7.cloned.1.call-start = ((), (), s32[]{:S(2)}) async-start(), calls=%async_computation.20 | async-start | bytes 3276800
  1068.5 352.8 %reduce-scatter.17.cloned.1.call-start = ((), (), s32[]{:S(2)}) async-start(), calls=%async_computation.15 | async-start | bytes 1638400 | tf_op jit(solution)/shard_map/reduce_scatter | solution.py:403
  1069.8 13.0 collective-permute-start.28
  1084.5 424.2 %all-gather.24.cloned.1.call-start = ((), (), s32[]{:S(2)}) async-start(), calls=%async_computation.17 | async-start | bytes 10485760 | tf_op jit(solution)/shard_map/all_gather | solution.py:393
  1095.0 563.1 %all-gather.26.cloned.1.call-start = ((), (), s32[]{:S(2)}) async-start(), calls=%async_computation.18 | async-start | bytes 10485760 | tf_op jit(solution)/shard_map/all_gather | solution.py:433
  1121.0 80.1 %collective-permute-start.21 = (bf16[1024,5120]{1,0:T(8,128)(2,1)}, bf16[1024,5120]{1,0:T(8,128)(2,1)}, u32[]{:S(2)}, u32[]{:S(2)}) collective-permute-start(bf16[1024,5120]{1,0:T(8,128)(2,1)} %slice.477), channel_id=1, source_target_pairs={{0,4},{4,0},{8,12},{12,8},{16,20},{20,16},{24,28},{28,24},{1,5},{5... | collective-permute-start | bytes 31457288 | tf_op jit(solution)/shard_map/ppermute | solution.py:27
  1167.8 144.1 %collective-permute-start.31 = (bf16[1024,3072]{1,0:T(8,128)(2,1)}, bf16[1024,3072]{1,0:T(8,128)(2,1)}, u32[]{:S(2)}, u32[]{:S(2)}) collective-permute-start(bf16[1024,3072]{1,0:T(8,128)(2,1)} %slice.500), channel_id=1, source_target_pairs={{0,4},{4,0},{8,12},{12,8},{16,20},{20,16},{24,28},{28,24},{1,5},{5... | collective-permute-start | bytes 18874376 | tf_op jit(solution)/shard_map/ppermute | solution.py:27
  1190.2 521.1 %reduce-scatter.15.cloned.1.call-start = ((), (), s32[]{:S(2)}) async-start(), calls=%async_computation.14 | async-start | bytes 3276800 | tf_op jit(solution)/shard_map/reduce_scatter | solution.py:403
  1201.0 18.5 %collective-permute-start.36 = (bf16[1024,1536]{1,0:T(8,128)(2,1)S(1)}, bf16[1024,1536]{1,0:T(8,128)(2,1)S(1)}, u32[]{:S(2)}, u32[]{:S(2)}) collective-permute-start(bf16[1024,1536]{1,0:T(8,128)(2,1)S(1)} %slice.512), channel_id=1, source_target_pairs={{0,4},{4,0},{8,12},{12,8},{16,20},{20,16},{24,28},{28,24},{1,5},{5... | collective-permute-start | bytes 9437192 | tf_op jit(solution)/shard_map/ppermute | solution.py:27
  1216.5 85.5 %collective-permute-start.22 = (bf16[256,5120]{1,0:T(8,128)(2,1)}, bf16[256,5120]{1,0:T(8,128)(2,1)}, u32[]{:S(2)}, u32[]{:S(2)}) collective-permute-start(bf16[256,5120]{1,0:T(8,128)(2,1)} %get-tuple-element.127), channel_id=1, source_target_pairs={{0,16},{4,20},{8,24},{12,28},{16,0},{20,4},{24,8},{28,12},{1,17},{... | collective-permute-start | bytes 7864328 | tf_op jit(solution)/shard_map/ppermute | solution.py:27
  1218.0 84.0 %collective-permute-start.24 = (bf16[256,5120]{1,0:T(8,128)(2,1)}, bf16[256,5120]{1,0:T(8,128)(2,1)}, u32[]{:S(2)}, u32[]{:S(2)}) collective-permute-start(bf16[256,5120]{1,0:T(8,128)(2,1)} %get-tuple-element.128), channel_id=1, source_target_pairs={{0,8},{4,12},{8,0},{12,4},{16,24},{20,28},{24,16},{28,20},{1,9},{5... | collective-permute-start | bytes 7864328 | tf_op jit(solution)/shard_map/ppermute | solution.py:27
  1221.6 74.7 %collective-permute-start.37 = (bf16[256,1536]{1,0:T(8,128)(2,1)}, bf16[256,1536]{1,0:T(8,128)(2,1)}, u32[]{:S(2)}, u32[]{:S(2)}) collective-permute-start(bf16[256,1536]{1,0:T(8,128)(2,1)} %get-tuple-element.145), channel_id=1, source_target_pairs={{0,16},{4,20},{8,24},{12,28},{16,0},{20,4},{24,8},{28,12},{1,17},{... | collective-permute-start | bytes 2359304 | tf_op jit(solution)/shard_map/ppermute | solution.py:27
  1222.2 74.8 %collective-permute-start.39 = (bf16[256,1536]{1,0:T(8,128)(2,1)}, bf16[256,1536]{1,0:T(8,128)(2,1)}, u32[]{:S(2)}, u32[]{:S(2)}) collective-permute-start(bf16[256,1536]{1,0:T(8,128)(2,1)} %get-tuple-element.146), channel_id=1, source_target_pairs={{0,8},{4,12},{8,0},{12,4},{16,24},{20,28},{24,16},{28,20},{1,9},{5... | collective-permute-start | bytes 2359304 | tf_op jit(solution)/shard_map/ppermute | solution.py:27
  1299.6 61.7 %collective-permute-start.40 = (bf16[128,1536]{1,0:T(8,128)(2,1)}, bf16[128,1536]{1,0:T(8,128)(2,1)}, u32[]{:S(2)}, u32[]{:S(2)}) collective-permute-start(bf16[128,1536]{1,0:T(8,128)(2,1)} %slice.520), channel_id=1, source_target_pairs={{0,16},{4,20},{8,24},{12,28},{16,0},{20,4},{24,8},{28,12},{1,17},{... | collective-permute-start | bytes 1179656 | tf_op jit(solution)/shard_map/ppermute | solution.py:27
  1300.5 90.6 %collective-permute-start.38 = (bf16[128,1536]{1,0:T(8,128)(2,1)S(1)}, bf16[128,1536]{1,0:T(8,128)(2,1)}, u32[]{:S(2)}, u32[]{:S(2)}) collective-permute-start(bf16[128,1536]{1,0:T(8,128)(2,1)S(1)} %slice.516), channel_id=1, source_target_pairs={{0,8},{4,12},{8,0},{12,4},{16,24},{20,28},{24,16},{28,20},{1,9},{5... | collective-permute-start | bytes 1179656 | tf_op jit(solution)/shard_map/ppermute | solution.py:27
  1310.7 32.1 %collective-permute-start.25 = (bf16[128,5120]{1,0:T(8,128)(2,1)}, bf16[128,5120]{1,0:T(8,128)(2,1)}, u32[]{:S(2)}, u32[]{:S(2)}) collective-permute-start(bf16[128,5120]{1,0:T(8,128)(2,1)} %slice.485), channel_id=1, source_target_pairs={{0,16},{4,20},{8,24},{12,28},{16,0},{20,4},{24,8},{28,12},{1,17},{... | collective-permute-start | bytes 3932168 | tf_op jit(solution)/shard_map/ppermute | solution.py:27
  1321.9 31.8 %collective-permute-start.23 = (bf16[128,5120]{1,0:T(8,128)(2,1)S(1)}, bf16[128,5120]{1,0:T(8,128)(2,1)S(1)}, u32[]{:S(2)}, u32[]{:S(2)}) collective-permute-start(bf16[128,5120]{1,0:T(8,128)(2,1)S(1)} %slice.481), channel_id=1, source_target_pairs={{0,8},{4,12},{8,0},{12,4},{16,24},{20,28},{24,16},{28,20},{1,9},{5... | collective-permute-start | bytes 3932168 | tf_op jit(solution)/shard_map/ppermute | solution.py:27
  1324.6 50.7 %collective-permute-start.32 = (bf16[256,3072]{1,0:T(8,128)(2,1)}, bf16[256,3072]{1,0:T(8,128)(2,1)}, u32[]{:S(2)}, u32[]{:S(2)}) collective-permute-start(bf16[256,3072]{1,0:T(8,128)(2,1)} %get-tuple-element.135), channel_id=1, source_target_pairs={{0,16},{4,20},{8,24},{12,28},{16,0},{20,4},{24,8},{28,12},{1,17},{... | collective-permute-start | bytes 4718600 | tf_op jit(solution)/shard_map/ppermute | solution.py:27
  1342.8 42.3 %collective-permute-start.34 = (bf16[256,3072]{1,0:T(8,128)(2,1)}, bf16[256,3072]{1,0:T(8,128)(2,1)}, u32[]{:S(2)}, u32[]{:S(2)}) collective-permute-start(bf16[256,3072]{1,0:T(8,128)(2,1)} %get-tuple-element.136), channel_id=1, source_target_pairs={{0,8},{4,12},{8,0},{12,4},{16,24},{20,28},{24,16},{28,20},{1,9},{5... | collective-permute-start | bytes 4718600 | tf_op jit(solution)/shard_map/ppermute | solution.py:27
  1390.0 17.3 collective-permute-start.35
  1397.4 17.3 collective-permute-start.33
  (75 other events, 775.6 us)
Sparse Core Ops, SparseCore 0:
  12.6 57.4 all-gather.15
  71.7 31.4 all-gather.21
  106.7 66.0 all-gather.27
  424.9 79.6 all-gather.19
  506.6 79.2 all-gather.17
  588.1 75.2 reduce-scatter.12
  665.8 77.2 reduce-scatter.10
  745.4 77.2 reduce-scatter.8
  825.1 77.2 reduce-scatter.6
  1060.2 124.4 all-reduce.4
  1190.1 134.9 all-reduce.6
  1327.4 31.1 reduce-scatter.16
  1360.2 148.4 all-gather.23
  1510.2 147.8 all-gather.25
  1660.9 50.3 reduce-scatter.14

commit v2 on v1

--- a/solution.py
+++ b/solution.py
@@ -23,6 +23,10 @@
     return lax.dot_general(left, right, (dims, ((), ())), preferred_element_type=F32)
 
 
+def tie(values, *others):
+    return lax.optimization_barrier((values,) + others)[0]
+
+
 def exchange(values, bit, size):
     return lax.ppermute(values, "dp", [(k, k ^ (1 << bit)) for k in range(size)])
 
@@ -43,7 +47,7 @@
         got = [exchange(p, o[turn], size) for p, o in zip(pieces, orders(size, parts))]
         pieces = [jnp.concatenate([p, g]) for p, g in zip(pieces, got)]
     half = jnp.concatenate(pieces)
-    return jnp.concatenate([half, exchange(half, 0, size)])
+    return [half, exchange(half, 0, size)], got[-1][:16, :128]
 
 
 def add_low(one, two):
@@ -60,6 +64,52 @@
         got = [exchange(p[cut:], o[turn], size) for p, o in zip(pieces, orders(size, parts))]
         pieces = [add_low(p[:cut], g) for p, g in zip(pieces, got)]
     return jnp.concatenate(pieces)
+
+
+def z_shift(values, by, n, around=True):
+    pairs = [(k, (k + by) % n) for k in range(n) if around or 0 <= k + by < n]
+    return lax.ppermute(values, "tensor", pairs)
+
+
+def z_scatter(values, n):
+    turn = lax.axis_index("tensor")
+    total = lax.dynamic_index_in_dim(values, turn, 0, keepdims=False).astype(F32)
+    for k in range(1, n):
+        block = lax.dynamic_index_in_dim(values, (turn + k) % n, 0, keepdims=False)
+        total = total + z_shift(block, k, n).astype(F32)
+    return total
+
+
+def z_line(own, n):
+    turn = lax.axis_index("tensor")
+    right, left = [own], [own]
+    for k in range(1, n):
+        right.append(lax.ppermute(right[-1], "tensor", [(s, s + 1) for s in range(k - 1, n - 1)]))
+        left.append(lax.ppermute(left[-1], "tensor", [(s, s - 1) for s in range(1, n - k + 1)]))
+    rows = own.shape[0]
+    out = jnp.zeros((n * rows, own.shape[1]), own.dtype)
+    out = lax.dynamic_update_slice_in_dim(out, own, turn * rows, 0)
+    for k in range(1, n):
+        out = lax.dynamic_update_slice_in_dim(out, left[k] + right[n - k], (turn + k) % n * rows, 0)
+    return out
+
+
+def small_gather(own, size, n):
+    turn, place = lax.axis_index("tensor"), lax.axis_index("dp")
+    rows = jnp.stack([own] + [z_shift(own, -k, n) for k in range(1, n)])
+    rows = jnp.take(rows, (jnp.arange(n) - turn) % n, axis=0)[None]
+    for bit in range(size.bit_length() - 1):
+        rows = jnp.concatenate([rows, exchange(rows, bit, size)])
+    return jnp.take(rows, jnp.arange(size) ^ place, axis=0).transpose(1, 0, 2)
+
+
+def small_scatter(values, size, n):
+    place = lax.axis_index("dp")
+    values = jnp.take(values, jnp.arange(size) ^ place, axis=0)
+    for bit in reversed(range(size.bit_length() - 1)):
+        half = values.shape[0] // 2
+        values = add_low(values[:half], exchange(values[half:], bit, size))
+    return z_scatter(values[0], n)
 
 
 def basis(size, rows, place):
@@ -78,31 +128,27 @@
     return table, inverse.astype(jnp.int32)
 
 
-def copy_kernel(table_ref, in_ref, out_ref):
-    out_ref[...] = in_ref[...]
-
-
-def permute(values, table):
-    a, b, r, d = values.shape
-    width = d // table.shape[0]
+def copy_kernel(blocks, table_ref, in_ref, out_ref):
+    width = in_ref.shape[1] // blocks
+    for p in range(blocks):
+        start = pl.multiple_of(table_ref[p] * width, width)
+        out_ref[:, p * width : (p + 1) * width] = in_ref[:, pl.ds(start, width)]
+
+
+def permute_rows(values, table):
+    rows, d_model = values.shape
+    step = max(k for k in range(16, 289, 16) if rows % k == 0)
+    spec = pl.BlockSpec((step, d_model), lambda r, tab: (r, 0))
     return pl.pallas_call(
-        copy_kernel,
+        functools.partial(copy_kernel, table.shape[0]),
         grid_spec=pltpu.PrefetchScalarGridSpec(
-            num_scalar_prefetch=1,
-            grid=(b, table.shape[0]),
-            in_specs=[
-                pl.BlockSpec((a, pl.squeezed, r, width), lambda h, p, tab: (0, h, 0, tab[p]))
-            ],
-            out_specs=pl.BlockSpec((pl.squeezed, a, r, width), lambda h, p, tab: (h, 0, 0, p)),
+            num_scalar_prefetch=1, grid=(rows // step,), in_specs=[spec], out_specs=spec
         ),
-        out_shape=jax.ShapeDtypeStruct((b, a, r, d), values.dtype),
+        out_shape=jax.ShapeDtypeStruct(values.shape, values.dtype),
         compiler_params=pltpu.CompilerParams(vmem_limit_bytes=VMEM),
+        cost_estimate=pl.CostEstimate(flops=0, bytes_accessed=2 * values.nbytes, transcendentals=0),
         name="permute",
     )(table, values)
-
-
-def permute_rows(values, table):
-    return permute(values[None, None], table)[0, 0]
 
 
 def permute_gain(values, table):
@@ -131,8 +177,25 @@
     return jnp.tanh(c * (v + 0.044715 * v * v * v))
 
 
-def forward_kernel(live_ref, pre_ref, par_ref, w_ref, conv_ref, decay_ref, ig_ref, dg_ref, state_ref, prod_ref, rec_ref):
+def head_mask(head, at, width):
+    lanes = lax.broadcasted_iota(jnp.int32, (head, 2 * width), 1)
+    lanes = jnp.where(lanes >= width, lanes - width, lanes)
+    return (lanes >= at * head) & (lanes < (at + 1) * head)
+
+
+def fill_dense(w_ref, dense_ref):
+    head = w_ref.shape[0]
+    blocks = w_ref[...].astype(F32)
+    for k in range(dense_ref.shape[0] // head):
+        block = jnp.where(head_mask(head, k, dense_ref.shape[0]), blocks, 0.0)
+        dense_ref[k * head : (k + 1) * head, :] = block.astype(BF)
+
+
+def forward_kernel(
+    live_ref, pre_ref, par_ref, w_ref, conv_ref, decay_ref, ig_ref, dg_ref, state_ref, prod_ref, rec_ref, dense_ref
+):
     rows, width = conv_ref.shape
+    fill_dense(w_ref, dense_ref)
     live = live_ref[0]
     rec_ref[...] = jnp.where(row_ids(rows + HALO, width, -HALO) < live, pre_ref[...], 0.0)
     par = [par_ref[k : k + 1, :] for k in range(8)]
@@ -144,7 +207,7 @@
             conv = conv + par[k] * near[HALO - k : HALO - k + ROWS]
         conv = jnp.where(row_ids(ROWS, width, at) < live, conv, 0.0)
         conv_ref[span, :] = conv
-        gates = dot(conv.astype(BF), w_ref[...])
+        gates = dot(conv.astype(BF), dense_ref[...])
         ig = lax.logistic(gates[:, :width] + par[5])
         dg = lax.logistic(gates[:, width:] + par[6])
         decay = jnp.exp(dg * par[7])
@@ -174,7 +237,7 @@
     live = live_ref[0]
     for at in range(0, rows, ROWS):
         span = pl.ds(at, ROWS)
-        v = pre_ref[pl.ds(at + HALO, ROWS), :]
+        v = pre_ref[span, :]
         act = 0.5 * v * (1.0 + gelu_parts(v))
         lam_ref[span, :] = jnp.where(row_ids(ROWS, width, at) < live, grad_ref[span, :] * act, 0.0)
     last = row_ids(SLAB, width, 0) == SLAB - 1
@@ -203,12 +266,13 @@
 
 def backward_kernel(
     live_ref, pre_ref, par_ref, w_ref, lam_ref, reach_ref, edge_ref, decay_ref, conv_ref, ig_ref, dg_ref, state_ref, prod_ref, cin_ref,
-    drec_ref, dpar_ref, dw_ref, rec_ref, dconv_ref, full_ref, dw_acc,
+    drec_ref, dpar_ref, dw_ref, rec_ref, dconv_ref, full_ref, dw_acc, dense_ref,
 ):
     rows, width = conv_ref.shape
     live = live_ref[0]
     rec_ref[...] = jnp.where(row_ids(rows + HALO, width, -HALO) < live, pre_ref[...], 0.0)
     par = [par_ref[k : k + 1, :] for k in range(8)]
+    fill_dense(w_ref, dense_ref)
     cin = cin_ref[:1, :]
     edge = edge_ref[:1, :]
     full_ref[:SLAB, :] = jnp.broadcast_to(cin, (SLAB, width))
@@ -232,7 +296,7 @@
         sums[5] = sums[5] + jnp.sum(d_ig, axis=0, keepdims=True)
         sums[6] = sums[6] + jnp.sum(d_dg, axis=0, keepdims=True)
         both = jnp.concatenate([d_ig.astype(BF), d_dg.astype(BF)], axis=1)
-        d_conv = lam * scale * ig + dot(both, w_ref[...], ((1,), (1,)))
+        d_conv = lam * scale * ig + dot(both, dense_ref[...], ((1,), (1,)))
         d_conv = jnp.where(row_ids(ROWS, width, at) < live, d_conv, 0.0)
         dconv_ref[pl.ds(at + HALO, ROWS), :] = d_conv
         part = dot(conv.astype(BF), both, ((0,), (0,)))
@@ -243,7 +307,11 @@
         sums[4] = sums[4] + jnp.sum(d_conv, axis=0, keepdims=True)
     for k in range(8):
         dpar_ref[k : k + 1, :] = sums[k]
-    dw_ref[...] = dw_acc[...].astype(BF)
+    head = dw_ref.shape[0]
+    total = jnp.zeros((head, 2 * width), F32)
+    for k in range(width // head):
+        total = total + jnp.where(head_mask(head, k, width), dw_acc[k * head : (k + 1) * head, :], 0.0)
+    dw_ref[...] = total.astype(BF)
     for at in list(range(0, rows, ROWS)) + [rows]:
         count = ROWS if at < rows else HALO
         near = dconv_ref[pl.ds(at, count + SLAB), :]
@@ -253,15 +321,15 @@
         drec_ref[pl.ds(at, count), :] = total
 
 
-def kernel_call(body, live, arrays, offsets, outs, scratch, name):
+def kernel_call(body, live, arrays, outs, scratch, name, work):
     width = outs[0][1]
     steps = width // GROUP
     specs = []
-    for array, off in zip(arrays, offsets):
+    for array in arrays:
         if array.ndim == 3:
             specs.append(pl.BlockSpec((pl.squeezed,) + array.shape[1:], lambda j, s: (j, 0, 0)))
         else:
-            specs.append(pl.BlockSpec((array.shape[0], GROUP), lambda j, s, off=off: (0, j + off)))
+            specs.append(pl.BlockSpec((array.shape[0], GROUP), lambda j, s: (0, j)))
     out_specs, out_shapes = [], []
     for rows, cols, kind in outs:
         if cols == width:
@@ -270,14 +338,16 @@
         else:
             out_specs.append(pl.BlockSpec((pl.squeezed, rows, cols), lambda j, s: (j, 0, 0)))
             out_shapes.append(jax.ShapeDtypeStruct((steps, rows, cols), kind))
+    moved = sum(a.nbytes for a in arrays) + sum(int(np.prod(o.shape)) * o.dtype.itemsize for o in out_shapes)
     return pl.pallas_call(
         body,
         grid_spec=pltpu.PrefetchScalarGridSpec(
             num_scalar_prefetch=1, grid=(steps,), in_specs=specs, out_specs=out_specs,
-            scratch_shapes=[pltpu.VMEM(shape, F32) for shape in scratch],
+            scratch_shapes=[pltpu.VMEM(shape, kind) for shape, kind in scratch],
         ),
         out_shape=out_shapes,
         compiler_params=pltpu.CompilerParams(vmem_limit_bytes=VMEM),
+        cost_estimate=pl.CostEstimate(flops=work * outs[0][0] * width, bytes_accessed=moved, transcendentals=0),
         name=name,
     )(live, *arrays)
 
@@ -293,47 +363,57 @@
 
 def gelu_product(gate, up):
     return jax.nn.gelu(gate) * up
+
+
+def wide_dot(left, halves):
+    cut = halves[0].shape[0]
+    return dot(left[:, :cut], halves[0]) + dot(left[:, cut:], halves[1])
+
+
+def wide_back(left, halves):
+    return jnp.concatenate([dot(left, h, ((1,), (1,))) for h in halves], axis=1)
 
 
 def on_device(size, n, tokens, lengths, gains, w_gelu, w_rec, chan, w_lru, w_out, w_mlp_in, w_down, cotangent):
     place = lax.axis_index("dp")
     turn = lax.axis_index("tensor")
     d_model = tokens.shape[1]
-    seq_len = tokens.shape[0]
-    rows = seq_len // n
+    rows = tokens.shape[0] // n
     half = rows // 2
     d_own = w_gelu.shape[0]
-    heads_own, head = chan.shape[1], w_lru.shape[3]
+    heads_own, part, head = chan.shape[1], chan.shape[2], w_lru.shape[3]
     heads = heads_own * n
     width = heads * head
+    groups = width // GROUP
     table, inverse = basis(size, d_own, place)
     live_count = (lengths - turn * rows).astype(jnp.int32)
     live = (lax.iota(jnp.int32, rows)[:, None] < live_count).astype(F32)
 
-    gain_rows = lax.all_gather(gains.astype(BF), "dp", axis=1, tiled=True)
-    gain = permute_gain(gain_rows, table).astype(F32)
-
-    def wide(parts):
-        own = lax.all_gather(jnp.stack(parts).astype(BF), "tensor", axis=0)
-        return own.transpose(2, 1, 0, 3).reshape(d_own, -1)
-
-    w_in = spread(wide([w_gelu, w_rec]), size)
-    flat = jnp.concatenate([w_lru.reshape(-1), chan.reshape(-1)]).astype(BF)
-    flat = lax.all_gather(flat, ("tensor", "dp"), axis=0).reshape(n, size, -1)
-    lru = flat[..., : w_lru.size].reshape((n, size) + w_lru.shape)
-    lru = lru.transpose(2, 0, 3, 1, 4, 5).reshape(2, heads, head, head)
-    chans = flat[..., w_lru.size :].reshape((n, size) + chan.shape)
+    def wide(own):
+        own = lax.all_gather(own, "tensor", axis=0)
+        return own.transpose(1, 0, 2).reshape(d_own, width)
+
+    z_rec = wide(w_rec.astype(BF))
+    small = [w_lru.transpose(2, 0, 1, 3).reshape(-1), chan.reshape(-1), gains.reshape(-1)]
+    small = small_gather(jnp.concatenate(small).astype(BF), size, n)
+    w_r, token = spread(tie(z_rec, small[0, 0, :128]), size)
+    z_gelu = tie(wide(tie(w_gelu.astype(BF), z_rec[:16, :128])), token)
+    w_g, token = spread(z_gelu, size)
+    z_out = tie(wide(tie(w_out.T.astype(BF), z_gelu[:16, :128])), token)
+    w_o, token = spread(z_out, size)
+    w_gu = jnp.concatenate([w_mlp_in[0], w_mlp_in[1]], axis=1).astype(BF)
+    w_gu, token = spread(tie(w_gu, token), size)
+    w_gu = jnp.concatenate(w_gu)
+    w_dn = jnp.concatenate(spread(tie(w_down.T.astype(BF), token), size)[0])
+
+    gain = small[0, :, -gains.size :].reshape(size, 2, d_own).transpose(1, 0, 2).reshape(2, d_model)
+    gain = permute_gain(gain, table).astype(F32)
+    chans = small[..., w_lru.size : w_lru.size + chan.size].reshape((n, size) + chan.shape)
     chans = chans.transpose(2, 0, 3, 1, 4).reshape(8, width).astype(F32)
     par = jnp.concatenate([chans[:7], -8.0 * jax.nn.softplus(-chans[7:])])
-    per = GROUP // head
-    groups = width // GROUP
-    eye = jnp.eye(per, dtype=BF)[None, None, :, None, :, None]
-    dense = lru.reshape(2, groups, per, head, 1, head) * eye
-    dense = dense.reshape(2, groups, GROUP, GROUP)
-    dense = jnp.concatenate([dense[0], dense[1]], axis=-1)
-    w_back = spread(wide([w_out.T]), size)
-    w_gu = spread(jnp.concatenate([w_mlp_in[0], w_mlp_in[1]], axis=1).astype(BF), size)
-    w_dn = spread(w_down.T.astype(BF), size)
+    each = n // groups
+    lru = small[..., : w_lru.size].reshape(groups, each, head, 2, heads_own * head)
+    lru = lru.transpose(0, 2, 3, 1, 4).reshape(groups, head, 2 * GROUP)
 
     main = lax.dynamic_slice_in_dim(tokens, turn * rows, rows)
     before = lax.dynamic_slice_in_dim(tokens, jnp.maximum(turn * rows - HALO, 0), HALO)
@@ -342,41 +422,43 @@
     first_rate = norm_rate(extended)
     first = (extended * first_rate * gain[0]).astype(BF)
     inputs, first_own, first_rate = extended[HALO:], first[HALO:], first_rate[HALO:]
-    cot = permute(cotangent.reshape(n, 2, half, d_model), table)
-
-    pre = dot(first, w_in)
+    cot = permute_rows(cotangent, table).reshape(n, 2, half, d_model)
+    cots = [cot[:, h].reshape(n * half, d_model) for h in range(2)]
+
     keep = (rows, width, F32)
+    dense = ((GROUP, 2 * GROUP), BF)
+    rec_pre = wide_dot(first, w_r)
     conv, decay, ig, dg, state, prod = kernel_call(
-        forward_kernel, live_count, [pre, par, dense], [groups, 0, 0], [keep] * 6,
-        [(rows + HALO, GROUP)], "recurrence",
-    )
-    ends = lax.all_gather(jnp.concatenate([prod[-1:], state[-1:]]), "tensor", axis=0)
+        forward_kernel, live_count, [rec_pre, par, lru], [keep] * 6,
+        [((rows + HALO, GROUP), F32), dense], "recurrence", 18000,
+    )
+    ends = jnp.concatenate([prod[-1:], state[-1:]])
+    came = [z_shift(ends, k, n, False) for k in range(1, n)]
     carry = jnp.zeros((1, width), F32)
-    for k in range(n - 1):
-        carry = jnp.where(k < turn, ends[k, 1:] + ends[k, :1] * carry, carry)
-    branch_pre = pre[HALO:, :width]
+    for end in came[::-1]:
+        carry = end[1:] + end[:1] * carry
+    branch_pre = wide_dot(first_own, w_g)
     recurrent = (state + prod * carry) * live
     activated, gelu_pull = jax.vjp(jax.nn.gelu, branch_pre)
     mixed = (activated * recurrent).astype(BF)
-    hidden = inputs + dot(mixed, w_back, ((1,), (1,)))
+    hidden = inputs + wide_back(mixed, w_o)
     second_rate = norm_rate(hidden)
     second_unit = hidden * second_rate
     second_own = (second_unit * gain[1]).astype(BF)
 
     hidden_units = w_dn.shape[1]
-    mlp_sum, grad_second, seconds, products, grads = [], [], [], [], []
+    grad_products = [dot(c, w_dn) for c in cots]
+    shares, grad_second, seconds, products, grads = [], [], [], [], []
     for h in range(2):
         second = lax.all_gather(second_own[h * half : (h + 1) * half], "tensor", axis=0, tiled=True)
-        cot_rows = cot[h].reshape(n * half, d_model)
         both = dot(second, w_gu)
         product, pull = jax.vjp(gelu_product, both[:, :hidden_units], both[:, hidden_units:])
+        grad_gate, grad_up = pull(grad_products[h])
         product = product.astype(BF)
-        grad_gate, grad_up = pull(dot(cot_rows, w_dn))
         grad = jnp.concatenate([grad_gate.astype(BF), grad_up.astype(BF)], axis=1)
         share = dot(grad, w_gu, ((1,), (1,))).astype(BF)
         grad_second.append(lax.psum_scatter(share, "tensor", scatter_dimension=0, tiled=True))
-        share = dot(product, w_dn, ((1,), (1,))).astype(BF)
-        mlp_sum.append(lax.psum_scatter(share, "tensor", scatter_dimension=0, tiled=True))
+        shares.append(dot(tie(product, share), w_dn, ((1,), (1,))).astype(BF))
         seconds.append(second)
         products.append(product)
         grads.append(grad)
@@ -385,73 +467,80 @@
         part = dot(lefts[0], rights[0], ((0,), (0,))).astype(BF)
         return (part.astype(F32) + dot(lefts[1], rights[1], ((0,), (0,)))).astype(BF)
 
-    cots = [cot[h].reshape(n * half, d_model) for h in range(2)]
-    g_gu = collect(by_rows(seconds, grads), size).astype(F32)
-    g_dn = collect(by_rows(cots, products), size).astype(F32)
-    result = hidden + jnp.concatenate(mlp_sum).astype(F32)
-    result = permute_rows(result.astype(BF), inverse)
-    output = lax.all_gather(result, "tensor", axis=0, tiled=True)
+    part_gu = by_rows(seconds, grads)
+    part_dn = by_rows(cots, products)
+    *grad_second, part_gu, part_dn, share_0, share_1 = lax.optimization_barrier(
+        (*grad_second, part_gu, part_dn, *shares)
+    )
+    g_gu = collect(part_gu, size).astype(F32)
+    g_dn = collect(part_dn, size).astype(F32)
+    output = jnp.zeros((n, 2, half, d_model), BF)
+    for h, share in enumerate([share_0, share_1]):
+        mlp_sum = lax.psum_scatter(share, "tensor", scatter_dimension=0, tiled=True).astype(F32)
+        result = permute_rows((hidden[h * half : (h + 1) * half] + mlp_sum).astype(BF), inverse)
+        result = lax.all_gather(result, "tensor", axis=0)
+        output = lax.dynamic_update_slice(output, result[:, None], (0, h, 0, 0))
+    output = output.reshape(n * rows, d_model)
 
     grad_second = jnp.concatenate(grad_second).astype(F32)
-    cot_own = lax.dynamic_slice_in_dim(cot, turn, 1, axis=1).reshape(rows, d_model).astype(F32)
+    cot_own = lax.dynamic_index_in_dim(cot, turn, 0).reshape(rows, d_model).astype(F32)
     gain_two = jnp.sum(grad_second * second_unit, axis=0)
     grad_hidden = cot_own + norm_back(grad_second, second_unit, second_rate, gain[1])
     hidden_low = grad_hidden.astype(BF)
 
-    def to_owner(grad, parts):
-        own = collect(grad.astype(BF), size).reshape(d_own, parts, n, -1).transpose(2, 1, 0, 3)
-        return lax.psum_scatter(own, "tensor", scatter_dimension=0).astype(F32)
-
-    grad_mixed = dot(hidden_low, w_back)
+    def to_owner(left, right):
+        own = collect(dot(left, right, ((0,), (0,))).astype(BF), size)
+        return z_scatter(own.reshape(d_own, n, width // n).transpose(1, 0, 2), n)
+
+    grad_mixed = wide_dot(hidden_low, w_o)
     lam, reach, edge = kernel_call(
-        back_scan_kernel, live_count, [pre, grad_mixed, decay], [0, 0, 0],
-        [keep, keep, (SLAB, width, F32)], [], "back_scan",
-    )
-    edges = lax.all_gather(edge[:1], "tensor", axis=0)
+        back_scan_kernel, live_count, [branch_pre, grad_mixed, decay],
+        [keep, keep, (SLAB, width, F32)], [], "back_scan", 10000,
+    )
+    edges = jnp.concatenate([prod[-1:], edge[:1]])
+    came = [z_shift(edges, -k, n, False) for k in range(1, n)]
     arriving = jnp.zeros((1, width), F32)
-    for k in range(n - 1, 0, -1):
-        arriving = jnp.where(k > turn, edges[k] + ends[k, :1] * arriving, arriving)
+    for end in came[::-1]:
+        arriving = end[1:] + end[:1] * arriving
     (grad_pre,) = gelu_pull(grad_mixed * recurrent)
-    g_back = to_owner(dot(hidden_low, mixed, ((0,), (0,))), 1)
+    pre_low = grad_pre.astype(BF)
+    first_part = wide_back(pre_low, w_g)
     tall = jnp.broadcast_to
-    drec, dpar, d_dense = kernel_call(
+    drec, dpar, d_lru = kernel_call(
         backward_kernel, live_count,
-        [pre, par, dense, lam, reach, tall(arriving, (SLAB, width)), decay, conv, ig, dg, state, prod, tall(carry, (SLAB, width))],
-        [groups] + [0] * 12,
-        [(rows + HALO, width, F32), (8, width, F32), (GROUP, 2 * GROUP, BF)],
-        [(rows + HALO, GROUP), (rows + 2 * HALO, GROUP), (rows + SLAB, GROUP), (GROUP, 2 * GROUP)], "recurrence_back",
-    )
-    edge_rows = lax.ppermute(drec[:HALO], "tensor", [(k, k - 1) for k in range(1, n)])
+        [rec_pre, par, lru, lam, reach, tall(arriving, (SLAB, width)), decay, conv, ig, dg, state, prod, tall(carry, (SLAB, width))],
+        [(rows + HALO, width, F32), (8, width, F32), (head, 2 * GROUP, BF)],
+        [((rows + HALO, GROUP), F32), ((rows + 2 * HALO, GROUP), F32), ((rows + SLAB, GROUP), F32), ((GROUP, 2 * GROUP), F32), dense],
+        "recurrence_back", 24000,
+    )
+    edge_rows = z_shift(drec[:HALO], -1, n, False)
     rec_low = (drec[HALO:] + jnp.pad(edge_rows, ((rows - HALO, 0), (0, 0)))) * live
-    grad_in = jnp.concatenate([grad_pre.astype(BF), rec_low.astype(BF)], axis=1)
-    g_in = to_owner(dot(first_own, grad_in, ((0,), (0,))), 2)
-    grad_first = dot(grad_in, w_in, ((1,), (1,)))
+    rec_low = rec_low.astype(BF)
+    grad_first = first_part + wide_back(rec_low, w_r)
     first_unit = inputs * first_rate
     gain_one = jnp.sum(grad_first * first_unit, axis=0)
     grad_tokens = grad_hidden + norm_back(grad_first, first_unit, first_rate, gain[0])
     grad_tokens = permute_rows(grad_tokens.astype(BF), inverse)
-    grad_tokens = lax.all_gather(grad_tokens, "tensor", axis=0, tiled=True)
+    g_o = to_owner(hidden_low, mixed)
+    g_g = to_owner(first_own, pre_low)
+    g_r = to_owner(first_own, rec_low)
+    grad_tokens = z_line(grad_tokens, n)
 
     d_gain = permute_gain(jnp.stack([gain_one, gain_two]), inverse)
     d_chan = jnp.concatenate([dpar[:7], dpar[7:] * 8.0 * jax.nn.sigmoid(-chans[7:])])
-    small = lax.psum(jnp.concatenate([d_gain.reshape(-1), d_chan.reshape(-1)]), ("tensor", "dp"))
-    d_gain = small[: d_gain.size].reshape(2, d_model)
-    d_gain = lax.dynamic_slice_in_dim(d_gain, place * d_own, d_own, axis=1)
-    d_chan = small[d_gain.size * size :].reshape(8, heads, head)
-    d_chan = lax.dynamic_slice(d_chan, (0, turn * heads_own, place * chan.shape[2]), chan.shape)
-    blocks = [
-        d_dense[:, k * head : (k + 1) * head, m * GROUP + k * head : m * GROUP + (k + 1) * head]
-        for m in range(2)
-        for k in range(per)
-    ]
-    d_lru = jnp.stack(blocks).reshape(2, per, groups, head, head).transpose(0, 2, 1, 3, 4)
-    d_lru = d_lru.reshape(2, n, heads_own, size, head // size, head).transpose(1, 3, 0, 2, 4, 5)
-    d_lru = lax.psum_scatter(d_lru.reshape(n * size, -1), ("tensor", "dp"), scatter_dimension=0)
-    d_lru = d_lru.reshape(w_lru.shape).astype(F32)
+    d_lru = d_lru.reshape(groups, size, part, 2, each, -1).transpose(1, 0, 4, 2, 3, 5)
+    d_chan = d_chan.reshape(8, n, heads_own, size, part).transpose(3, 1, 0, 2, 4)
+    d_gain = d_gain.reshape(2, size, 1, d_own).transpose(1, 2, 0, 3)
+    d_gain = jnp.broadcast_to(d_gain, (size, n, 2, d_own))
+    small = [v.reshape(size, n, -1).astype(BF) for v in (d_lru, d_chan, d_gain)]
+    small = small_scatter(jnp.concatenate(small, axis=2), size, n)
+    d_lru = small[: w_lru.size].reshape(part, 2, heads_own, head).transpose(1, 2, 0, 3)
+    d_chan = small[w_lru.size : -gains.size].reshape(chan.shape)
+    d_gain = small[-gains.size :].reshape(gains.shape)
     g_gate, g_up = g_gu[:, :hidden_units], g_gu[:, hidden_units:]
     return (
-        output, grad_tokens, d_gain[0], d_gain[1], g_in[0], g_in[1], d_chan, d_lru,
-        g_back[0].T, jnp.stack([g_gate, g_up]), g_dn.T,
+        output, grad_tokens, d_gain[0], d_gain[1], g_g, g_r, d_chan, d_lru,
+        g_o.T, jnp.stack([g_gate, g_up]), g_dn.T,
     )
 
 

time: 1740 us -> 1490 us (0.86)
  waiting for transfers between devices: 894 us -> 582 us
  starting transfers between devices: 41.7 us -> 148 us
  blocking collectives: 36.1 us -> 0 us
  Pallas kernels: 112 us -> 82 us
  other arithmetic: 126 us -> 155 us
  local copies, waits for them, and re-layouts: 240 us -> 213 us
    all_gather x5, waiting for transfers between devices: 251 us -> 0.01 us  [the longest x3 0.01 us: wide(): own = lax.all_gather(own, 'tensor', axis=0)]
    ppermute x1 -> x28, waiting for transfers between devices: 0.01 us -> 221 us  [the longest x22 186 us: z_shift(): return lax.ppermute(values, 'tensor', pairs)]
    reduce_scatter x4, waiting for transfers between devices: 232 us -> 26.7 us  [on_device(): lax.psum_scatter(share, 'tensor', scatter_dimension=0, tiled=True)]
    ppermute x1 -> x28, starting transfers between devices: 1.7 us -> 96.4 us  [the longest x22 81.9 us: z_shift(): return lax.ppermute(values, 'tensor', pairs)]
    reduce_scatter x2 -> x0, waiting for transfers between devices: 53.2 us -> none  [to_owner(): return lax.psum_scatter(own, 'tensor', scatter_dimension=0).astype(F32)]
    all_gather x3 -> x0, blocking collectives: 36.1 us -> none  [the longest x1 13.7 us: on_device(): edges = lax.all_gather(edge[:1], 'tensor', axis=0)]
    unnamed x207 -> x264, local copies, waits for them, and re-layouts: 98.3 us -> 67.3 us
    pallas_call x4 -> x5, Pallas kernels: 51.2 us -> 25.4 us  [permute_rows(): pl.pallas_call(functools.partial(copy_kernel, table.shape[0]), grid_spec=...]
  transfers between devices with their start and end apart: 56 -> 95, of which waited for: 31 -> 38; matrix products, arithmetic and copies ran while one was open for 31% -> 39% of each run, Pallas kernels for 6% -> 5%
where the time goes in v2:
time: 1490 us; the launch traced here: 1480 us
  waiting for transfers between devices  582 us (39%)
  matrix products  286 us (19%)
  local copies, waits for them, and re-layouts  213 us (14%)
  other arithmetic  155 us (10%)
  starting transfers between devices  148 us (10%)
  Pallas kernels  82 us (6%)
  between operations  17.1 us (1%)
    ppermute x56, waiting for transfers between devices, exchange(): return lax.ppermute(values, 'dp', [(k, k ^ 1 << bit) for k in range(size)])  309 us
    dot_general x27, matrix products, dot(): lax.dot_general(left, right, (dims, ((), ())), preferred_element_type=F32)  286 us
    ppermute x22, waiting for transfers between devices, z_shift(): return lax.ppermute(values, 'tensor', pairs)  186 us
    ppermute x22, starting transfers between devices, z_shift(): return lax.ppermute(values, 'tensor', pairs)  81.9 us
    unnamed x264, local copies, waits for them, and re-layouts  67.3 us
    pallas_call x3, Pallas kernels, kernel_call(): pl.pallas_call(body, grid_spec=pltpu.PrefetchScalarGridSpec(num_scalar_pr...  56.6 us
    ppermute x56, starting transfers between devices, exchange(): return lax.ppermute(values, 'dp', [(k, k ^ 1 << bit) for k in range(size)])  50.6 us
    convert_element_type x23, other arithmetic, add_low(): return (one.astype(F32) + two.astype(F32)).astype(BF)  47.9 us
  transfers between devices with their start and end apart: 95, of which 38 were waited for; matrix products, arithmetic and copies ran while one was open for 39% of the time, Pallas kernels for 5%

profile of v2, /device:TPU:0, one launch (start us, length us, event | category | flops | bytes accessed | tf_op | source)
XLA Modules:
  0.0 1483.1 jit_solution(17014594769976545188)
XLA Ops:
  54.1 10.4 collective-permute-done.4
  74.4 12.7 collective-permute-done.5
  126.8 10.9 collective-permute-done.30
  159.9 5.9 collective-permute-done.8
  169.1 38.8 %collective-permute-done.12 = bf16[256,2560]{0,1:T(8,128)(2,1)S(1)} collective-permute-done((bf16[256,2560]{0,1:T(8,128)(2,1)S(1)}, bf16[256,2560]{0,1:T(8,128)(2,1)S(1)}, u32[]{:S(2)}, u32[]{:S(2)}) %collective-permute-start.12) | collective-permute-done | bytes 1310752 | tf_op jit(solution)/shard_map/ppermute | solution.py:31
  213.0 11.7 collective-permute-done.31
  227.4 25.4 %collective-permute-done.7 = bf16[256,2560]{0,1:T(8,128)(2,1)S(1)} collective-permute-done((bf16[256,2560]{0,1:T(8,128)(2,1)S(1)}, bf16[256,2560]{0,1:T(8,128)(2,1)S(1)}, u32[]{:S(2)}, u32[]{:S(2)}) %collective-permute-start.7) | collective-permute-done | bytes 1310752 | tf_op jit(solution)/shard_map/ppermute | solution.py:31
  259.2 20.1 %collective-permute-done.20 = bf16[256,2560]{0,1:T(8,128)(2,1)S(1)} collective-permute-done((bf16[256,2560]{0,1:T(8,128)(2,1)S(1)}, bf16[256,2560]{0,1:T(8,128)(2,1)S(1)}, u32[]{:S(2)}, u32[]{:S(2)}) %collective-permute-start.20) | collective-permute-done | bytes 1310752 | tf_op jit(solution)/shard_map/ppermute | solution.py:31
  285.8 28.3 %collective-permute-done.32 = bf16[256,3072]{1,0:T(8,128)(2,1)S(1)} collective-permute-done((bf16[256,3072]{1,0:T(8,128)(2,1)S(1)}, bf16[256,3072]{1,0:T(8,128)(2,1)S(1)}, u32[]{:S(2)}, u32[]{:S(2)}) %collective-permute-start.32) | collective-permute-done | bytes 1572896 | tf_op jit(solution)/shard_map/ppermute | solution.py:31
  323.3 6.6 convolution_add_fusion.pre_ref
  329.9 18.1 %recurrence.1 = (f32[512,2560]{1,0:T(8,128)}, f32[512,2560]{1,0:T(8,128)}, f32[512,2560]{1,0:T(8,128)}, f32[512,2560]{1,0:T(8,128)}, f32[512,2560]{1,0:T(8,128)}, /*index=5*/f32[512,2560]{1,0:T(8,128)}) custom-call(s32[1]{0:T(128)} %sub.49.live_ref, f32[528,2560]{1,0:T(8,128)} %convolution_add_fusion.pre_ref, f32[8,2560]{1,0:T(8,128)} %pad_maximum_fusion.33.par_ref, ...), custom_call_target="tpu_custom_call" | custom-call | flops 23592960000 | bytes 38584320 | tf_op jit(solution)/shard_map/recurrence/pallas_call | solution.py:342
  356.5 7.5 fusion.42
  364.2 10.4 multiply_convert_fusion.5
  395.9 8.9 collective-permute-done.26
  408.6 15.6 %collective-permute-done.27 = bf16[256,1536]{0,1:T(8,128)(2,1)S(1)} collective-permute-done((bf16[256,1536]{0,1:T(8,128)(2,1)S(1)}, bf16[256,1536]{0,1:T(8,128)(2,1)S(1)}, u32[]{:S(2)}, u32[]{:S(2)}) %collective-permute-start.27) | collective-permute-done | bytes 786464 | tf_op jit(solution)/shard_map/ppermute | solution.py:31
  427.8 10.6 permute.6
  443.2 6.5 fusion.74
  458.7 9.0 all-gather.13.cloned.1.call-done
  467.7 19.4 %fusion.88 = f32[1024,3072]{1,0:T(8,128)} fusion(bf16[1024,2048]{1,0:T(8,128)(2,1)} %all-gather.13.cloned.1.call-done, bf16[2048,3072]{1,0:T(8,128)(2,1)} %constant_dynamic-update-slice_fusion.38), kind=kOutput, calls=%fused_computation.330 | convolution fusion | flops 12884901888 | bytes 29360128 | tf_op jit(solution)/shard_map/dot_general | solution.py:23
  487.1 15.4 %fusion.6 = (bf16[1024,1536]{1,0:T(8,128)(2,1)}, bf16[1024,1536]{1,0:T(8,128)(2,1)}, bf16[1024,1536]{1,0:T(8,128)(2,1)}) fusion(f32[1024,3072]{1,0:T(8,128)} %fusion.88, bf16[1024,2048]{1,0:T(8,128)(2,1)S(1)} %bitcast.207, bf16[2048,1536]{0,1:T(8,128)(2,1)S(1)} %copy-done.69), kind=kOutput, calls=%fused_computation.28 | convolution fusion | flops 6483345408 | bytes 32505856 | tf_op jit(solution)/shard_map/dot_general | solution.py:23
  502.5 19.6 %fusion.30 = bf16[1024,2048]{1,0:T(8,128)(2,1)} fusion(bf16[2048,3072]{1,0:T(8,128)(2,1)} %constant_dynamic-update-slice_fusion.38, bf16[1024,1536]{1,0:T(8,128)(2,1)} %get-tuple-element.110, bf16[1024,1536]{1,0:T(8,128)(2,1)} %get-tuple-element.109), kind=kOutput, calls=%fused_computation.81 | convolution fusion | flops 12899581952 | bytes 23068672 | tf_op jit(solution)/shard_map/dot_general | solution.py:23
  522.1 11.4 convolution_convert_fusion.3
  533.6 15.5 %all-gather.15.cloned.1.call-done = bf16[1024,2048]{1,0:T(8,128)(2,1)} async-done(((bf16[256,2048]{1,0:T(8,128)(2,1)}), bf16[1024,2048]{1,0:T(8,128)(2,1)}) %all-gather.15.cloned.1.call-update) | async-done | bytes 4194320 | tf_op jit(solution)/shard_map/all_gather | solution.py:453
  549.0 19.1 %fusion.89 = f32[1024,3072]{1,0:T(8,128)} fusion(bf16[1024,2048]{1,0:T(8,128)(2,1)} %all-gather.15.cloned.1.call-done, bf16[2048,3072]{1,0:T(8,128)(2,1)} %constant_dynamic-update-slice_fusion.38), kind=kOutput, calls=%fused_computation.331 | convolution fusion | flops 12884901888 | bytes 29360128 | tf_op jit(solution)/shard_map/dot_general | solution.py:23
  568.2 11.0 convolution_convert_fusion.5
  579.1 18.0 %fusion.13 = (bf16[1024,1536]{1,0:T(8,128)(2,1)S(1)}, bf16[1024,1536]{1,0:T(8,128)(2,1)}, bf16[1024,1536]{1,0:T(8,128)(2,1)S(1)}) fusion(f32[1024,3072]{1,0:T(8,128)} %fusion.89, bf16[1024,2048]{1,0:T(8,128)(2,1)} %bitcast.204, bf16[2048,1536]{0,1:T(8,128)(2,1)} %copy-done.68), kind=kOutput, calls=%fused_computation.35 | convolution fusion | flops 6483345408 | bytes 32505856 | tf_op jit(solution)/shard_map/dot_general | solution.py:23
  598.9 18.7 %fusion.31 = bf16[1024,2048]{1,0:T(8,128)(2,1)} fusion(bf16[2048,3072]{1,0:T(8,128)(2,1)} %constant_dynamic-update-slice_fusion.38, bf16[1024,1536]{1,0:T(8,128)(2,1)} %get-tuple-element.108, bf16[1024,1536]{1,0:T(8,128)(2,1)S(1)} %get-tuple-element.107), kind=kOutput, calls=%fused_computation.82 | convolution fusion | flops 12899581952 | bytes 23068672 | tf_op jit(solution)/shard_map/dot_general | solution.py:23
  617.7 11.0 convolution_convert_fusion.4
  628.6 12.1 add_convert_fusion.2
  640.7 17.8 %fusion.28 = bf16[2048,3072]{1,0:T(8,128)(2,1)} fusion(bf16[1024,2048]{1,0:T(8,128)(2,1)S(1)} %copy-done.83, bf16[1024,1536]{1,0:T(8,128)(2,1)} %get-tuple-element.110, bf16[1024,1536]{1,0:T(8,128)(2,1)S(1)} %copy-done.86), kind=kOutput, calls=%fused_computation.76 | convolution fusion | flops 12897484800 | bytes 23068672 | tf_op jit(solution)/shard_map/dot_general | solution.py:23
  658.5 21.0 %add_convert_fusion = bf16[2048,3072]{1,0:T(8,128)(2,1)} fusion(bf16[1024,2048]{1,0:T(8,128)(2,1)} %all-gather.15.cloned.1.call-done, bf16[2048,3072]{1,0:T(8,128)(2,1)} %fusion.28, bf16[1024,1536]{1,0:T(8,128)(2,1)} %get-tuple-element.108, bf16[1024,1536]{1,0:T(8,128)(2,1)S(1)} %copy-done.88), kind=kOutput, calls=%fused_computation.5 | convolution fusion | flops 12916359168 | bytes 35651584 | tf_op jit(solution)/shard_map/dot_general | solution.py:23
  679.5 26.7 %reduce-scatter.7.cloned.1.call-done = bf16[256,2048]{1,0:T(8,128)(2,1)} async-done(((bf16[1024,2048]{1,0:T(8,128)(2,1)}), bf16[256,2048]{1,0:T(8,128)(2,1)}) %reduce-scatter.7.cloned.1.call-update) | async-done | bytes 1048592 | tf_op jit(solution)/shard_map/reduce_scatter | solution.py:460
  719.0 7.8 convolution_add_fusion.1.grad_ref
  726.8 13.0 back_scan.1
  750.4 25.5 %recurrence_back.1 = (f32[528,2560]{1,0:T(8,128)}, f32[8,2560]{1,0:T(8,128)}, bf16[4,160,1280]{2,1,0:T(8,128)(2,1)}) custom-call(s32[1]{0:T(128)} %sub.49.live_ref, f32[528,2560]{1,0:T(8,128)} %convolution_add_fusion.pre_ref, f32[8,2560]{1,0:T(8,128)} %pad_maximum_fusion.33.par_ref, bf16[4,160,1280]{2,1,0:T(8,128)(2,1)} %reshape_transpose_reshape.3.w_ref, ...), custom_call_target="tpu_custom_call" | custom-call | flops 32440320000 | bytes 56360960 | tf_op jit(solution)/shard_map/recurrence_back/pallas_call | solution.py:342
  793.3 11.4 fusion.20
  807.7 5.8 fusion.90
  838.6 17.7 %collective-permute-done.44 = bf16[4,4,26752]{2,1,0:T(4,128)(2,1)S(1)} collective-permute-done((bf16[4,4,26752]{2,1,0:T(4,128)(2,1)}, bf16[4,4,26752]{2,1,0:T(4,128)(2,1)S(1)}, u32[]{:S(2)}, u32[]{:S(2)}) %collective-permute-start.44) | collective-permute-done | bytes 856096 | tf_op jit(solution)/shard_map/ppermute | solution.py:31
  860.4 7.9 convolution_convert_fusion
  874.9 6.1 slice.462
  885.0 9.4 add_convert_fusion.7.in_ref
  897.9 6.6 collective-permute-start.39
  912.0 6.0 convolution_convert_fusion.2
  923.8 72.7 %collective-permute-done.49 = bf16[26752]{0:T(1024)(128)(2,1)S(1)} collective-permute-done((bf16[26752]{0:T(1024)(128)(2,1)S(1)}, bf16[26752]{0:T(1024)(128)(2,1)S(1)}, u32[]{:S(2)}, u32[]{:S(2)}) %collective-permute-start.49) | collective-permute-done | bytes 53536 | tf_op jit(solution)/shard_map/ppermute | solution.py:71
  997.9 6.2 collective-permute-start.47
  1010.6 39.2 %collective-permute-done.47 = bf16[26752]{0:T(1024)(128)(2,1)S(1)} collective-permute-done((bf16[26752]{0:T(1024)(128)(2,1)S(1)}, bf16[26752]{0:T(1024)(128)(2,1)S(1)}, u32[]{:S(2)}, u32[]{:S(2)}) %collective-permute-start.47) | collective-permute-done | bytes 53536 | tf_op jit(solution)/shard_map/ppermute | solution.py:71
  1051.2 6.0 convolution_convert_fusion.1
  1071.7 9.0 collective-permute-done.81
  1085.5 35.4 %collective-permute-done.42 = bf16[512,2048]{1,0:T(8,128)(2,1)} collective-permute-done((bf16[512,2048]{1,0:T(8,128)(2,1)}, bf16[512,2048]{1,0:T(8,128)(2,1)}, u32[]{:S(2)}, u32[]{:S(2)}) %collective-permute-start.42) | collective-permute-done | bytes 2097184 | tf_op jit(solution)/shard_map/ppermute | solution.py:88
  1152.3 7.4 add_convert_fusion.1
  1193.2 8.9 collective-permute-done.53
  1206.9 14.0 collective-permute-done.59
  1221.2 8.9 collective-permute-done.61
  1234.1 34.5 %collective-permute-done.70 = bf16[128,2560]{1,0:T(8,128)(2,1)S(1)} collective-permute-done((bf16[128,2560]{1,0:T(8,128)(2,1)S(1)}, bf16[128,2560]{1,0:T(8,128)(2,1)S(1)}, u32[]{:S(2)}, u32[]{:S(2)}) %collective-permute-start.70) | collective-permute-done | bytes 655392 | tf_op jit(solution)/shard_map/ppermute | solution.py:31
  1269.1 8.8 collective-permute-done.68
  1284.5 7.5 collective-permute-done.52
  1318.9 6.4 constant_dynamic-slice_fusion.3
  1334.8 11.6 collective-permute-start.64
  1350.5 26.8 %collective-permute-done.56 = bf16[256,640]{1,0:T(8,128)(2,1)} collective-permute-done((bf16[256,640]{1,0:T(8,128)(2,1)}, bf16[256,640]{1,0:T(8,128)(2,1)}, u32[]{:S(2)}, u32[]{:S(2)}) %collective-permute-start.56) | collective-permute-done | bytes 327712 | tf_op jit(solution)/shard_map/ppermute | solution.py:71
  1377.4 35.2 %collective-permute-start.71 = (bf16[256,640]{0,1:T(8,128)(2,1)}, bf16[256,640]{0,1:T(8,128)(2,1)S(1)}, u32[]{:S(2)}, u32[]{:S(2)}) collective-permute-start(bf16[256,640]{0,1:T(8,128)(2,1)} %bitcast.54), channel_id=1, source_target_pairs={{0,1},{1,2},{2,3},{3,0},{4,5},{5,6},{6,7},{7,4},{8,9},{9,10},{10,1... | collective-permute-start | bytes 983048 | tf_op jit(solution)/shard_map/ppermute | solution.py:71
  1412.6 26.4 %collective-permute-done.64 = bf16[256,640]{1,0:T(8,128)(2,1)S(1)} collective-permute-done((bf16[256,640]{1,0:T(8,128)(2,1)S(1)}, bf16[256,640]{1,0:T(8,128)(2,1)S(1)}, u32[]{:S(2)}, u32[]{:S(2)}) %collective-permute-start.64) | collective-permute-done | bytes 327712 | tf_op jit(solution)/shard_map/ppermute | solution.py:71
  1443.9 12.6 collective-permute-done.72
  1460.3 7.5 pad_maximum_fusion
  1467.8 8.4 copy.101
  (662 shorter events, 461.6 us)
Async XLA Ops:
  7.2 106.6 %all-gather.19.cloned.1.call-start = ((), (), s32[]{:S(2)}) async-start(), calls=%async_computation.11 | async-start | bytes 1638400 | tf_op jit(solution)/shard_map/all_gather | solution.py:393
  9.3 110.9 %all-gather.17.cloned.1.call-start = ((), (), s32[]{:S(2)}) async-start(), calls=%async_computation.10 | async-start | bytes 1638400 | tf_op jit(solution)/shard_map/all_gather | solution.py:393
  15.5 32.9 %collective-permute-start.2 = (bf16[26752]{0:T(1024)(128)(2,1)}, bf16[26752]{0:T(1024)(128)(2,1)S(1)}, u32[]{:S(2)}, u32[]{:S(2)}) collective-permute-start(bf16[26752]{0:T(1024)(128)(2,1)} %dynamic-update-slice.46), channel_id=1, source_target_pairs={{0,1},{1,2},{2,3},{3,0},{4,5},{5,6},{6,7},{7,4},{8,9},{9,10},{10,1... | collective-permute-start | bytes 160520 | tf_op jit(solution)/shard_map/ppermute | solution.py:71
  24.3 99.7 %all-gather.21.cloned.1.call-start = ((), (), s32[]{:S(2)}) async-start(), calls=%async_computation.12 | async-start | bytes 1638400 | tf_op jit(solution)/shard_map/all_gather | solution.py:393
  27.4 41.9 %collective-permute-start.29 = (bf16[128,3072]{1,0:T(8,128)(2,1)}, bf16[128,3072]{1,0:T(8,128)(2,1)S(1)}, u32[]{:S(2)}, u32[]{:S(2)}) collective-permute-start(bf16[128,3072]{1,0:T(8,128)(2,1)} %get-tuple-element.147), channel_id=1, source_target_pairs={{0,8},{4,12},{8,0},{12,4},{16,24},{20,28},{24,16},{28,20},{1,9},{5... | collective-permute-start | bytes 2359304 | tf_op jit(solution)/shard_map/ppermute | solution.py:31
  30.8 35.8 %collective-permute-start.24 = (bf16[128,1536]{0,1:T(8,128)(2,1)}, bf16[128,1536]{0,1:T(8,128)(2,1)}, u32[]{:S(2)}, u32[]{:S(2)}) collective-permute-start(bf16[128,1536]{0,1:T(8,128)(2,1)} %get-tuple-element.177), channel_id=1, source_target_pairs={{0,8},{4,12},{8,0},{12,4},{16,24},{20,28},{24,16},{28,20},{1,9},{5... | collective-permute-start | bytes 1179656 | tf_op jit(solution)/shard_map/ppermute | solution.py:31
  32.3 435.4 %all-gather.13.cloned.1.call-start = ((), (), s32[]{:S(2)}) async-start(), calls=%async_computation.4 | async-start | bytes 5242880 | tf_op jit(solution)/shard_map/all_gather | solution.py:453
  68.8 321.5 %collective-permute-start.25 = (bf16[256,1536]{0,1:T(8,128)(2,1)}, bf16[256,1536]{0,1:T(8,128)(2,1)}, u32[]{:S(2)}, u32[]{:S(2)}) collective-permute-start(bf16[256,1536]{0,1:T(8,128)(2,1)} %pad_maximum_fusion.29), channel_id=1, source_target_pairs={{0,16},{4,20},{8,24},{12,28},{16,0},{20,4},{24,8},{28,12},{1,17},{... | collective-permute-start | bytes 2359304 | tf_op jit(solution)/shard_map/ppermute | solution.py:31
  71.9 65.8 %collective-permute-start.30 = (bf16[256,3072]{1,0:T(8,128)(2,1)}, bf16[256,3072]{1,0:T(8,128)(2,1)}, u32[]{:S(2)}, u32[]{:S(2)}) collective-permute-start(bf16[256,3072]{1,0:T(8,128)(2,1)} %pad_maximum_fusion.17), channel_id=1, source_target_pairs={{0,16},{4,20},{8,24},{12,28},{16,0},{20,4},{24,8},{28,12},{1,17},{... | collective-permute-start | bytes 4718600 | tf_op jit(solution)/shard_map/ppermute | solution.py:31
  118.6 33.1 %collective-permute-start.13 = (bf16[128,2560]{0,1:T(8,128)(2,1)}, bf16[128,2560]{0,1:T(8,128)(2,1)S(1)}, u32[]{:S(2)}, u32[]{:S(2)}) collective-permute-start(bf16[128,2560]{0,1:T(8,128)(2,1)} %get-tuple-element.165), channel_id=1, source_target_pairs={{0,16},{4,20},{8,24},{12,28},{16,0},{20,4},{24,8},{28,12},{1,17},{... | collective-permute-start | bytes 1966088 | tf_op jit(solution)/shard_map/ppermute | solution.py:31
  123.4 31.0 %collective-permute-start.6 = (bf16[128,2560]{0,1:T(8,128)(2,1)}, bf16[128,2560]{0,1:T(8,128)(2,1)}, u32[]{:S(2)}, u32[]{:S(2)}) collective-permute-start(bf16[128,2560]{0,1:T(8,128)(2,1)} %get-tuple-element.170), channel_id=1, source_target_pairs={{0,8},{4,12},{8,0},{12,4},{16,24},{20,28},{24,16},{28,20},{1,9},{5... | collective-permute-start | bytes 1966088 | tf_op jit(solution)/shard_map/ppermute | solution.py:31
  151.7 59.6 %collective-permute-start.21 = (bf16[128,2560]{0,1:T(8,128)(2,1)S(1)}, bf16[128,2560]{0,1:T(8,128)(2,1)S(1)}, u32[]{:S(2)}, u32[]{:S(2)}) collective-permute-start(bf16[128,2560]{0,1:T(8,128)(2,1)S(1)} %get-tuple-element.162), channel_id=1, source_target_pairs={{0,16},{4,20},{8,24},{12,28},{16,0},{20,4},{24,8},{28,12},{1,17},{... | collective-permute-start | bytes 1966088 | tf_op jit(solution)/shard_map/ppermute | solution.py:31
  154.4 53.4 %collective-permute-start.12 = (bf16[256,2560]{0,1:T(8,128)(2,1)S(1)}, bf16[256,2560]{0,1:T(8,128)(2,1)S(1)}, u32[]{:S(2)}, u32[]{:S(2)}) collective-permute-start(bf16[256,2560]{0,1:T(8,128)(2,1)S(1)} %pad_maximum_fusion.21), channel_id=1, source_target_pairs={{0,16},{4,20},{8,24},{12,28},{16,0},{20,4},{24,8},{28,12},{1,17},{... | collective-permute-start | bytes 3932168 | tf_op jit(solution)/shard_map/ppermute | solution.py:31
  165.8 59.0 %collective-permute-start.31 = (bf16[128,3072]{1,0:T(8,128)(2,1)S(1)}, bf16[128,3072]{1,0:T(8,128)(2,1)S(1)}, u32[]{:S(2)}, u32[]{:S(2)}) collective-permute-start(bf16[128,3072]{1,0:T(8,128)(2,1)S(1)} %get-tuple-element.145), channel_id=1, source_target_pairs={{0,16},{4,20},{8,24},{12,28},{16,0},{20,4},{24,8},{28,12},{1,17},{... | collective-permute-start | bytes 2359304 | tf_op jit(solution)/shard_map/ppermute | solution.py:31
  167.4 42.6 %collective-permute-start.14 = (bf16[256,2560]{0,1:T(8,128)(2,1)S(1)}, bf16[256,2560]{0,1:T(8,128)(2,1)S(1)}, u32[]{:S(2)}, u32[]{:S(2)}) collective-permute-start(bf16[256,2560]{0,1:T(8,128)(2,1)S(1)} %pad_maximum_fusion.22), channel_id=1, source_target_pairs={{0,8},{4,12},{8,0},{12,4},{16,24},{20,28},{24,16},{28,20},{1,9},{5... | collective-permute-start | bytes 3932168 | tf_op jit(solution)/shard_map/ppermute | solution.py:31
  207.9 44.9 %collective-permute-start.7 = (bf16[256,2560]{0,1:T(8,128)(2,1)S(1)}, bf16[256,2560]{0,1:T(8,128)(2,1)S(1)}, u32[]{:S(2)}, u32[]{:S(2)}) collective-permute-start(bf16[256,2560]{0,1:T(8,128)(2,1)S(1)} %pad_maximum_fusion.19), channel_id=1, source_target_pairs={{0,16},{4,20},{8,24},{12,28},{16,0},{20,4},{24,8},{28,12},{1,17},{... | collective-permute-start | bytes 3932168 | tf_op jit(solution)/shard_map/ppermute | solution.py:31
  210.2 105.4 %collective-permute-start.15 = (bf16[1024,2560]{0,1:T(8,128)(2,1)S(1)}, bf16[1024,2560]{0,1:T(8,128)(2,1)S(1)}, u32[]{:S(2)}, u32[]{:S(2)}) collective-permute-start(bf16[1024,2560]{0,1:T(8,128)(2,1)S(1)} %constant_dynamic-update-slice_fusion.7), channel_id=1, source_target_pairs={{0,4},{4,0},{8,12},{12,8},{16,20},{20,16},{24,28},{28,24},{1,5},{5... | collective-permute-start | bytes 15728648 | tf_op jit(solution)/shard_map/ppermute | solution.py:31
  211.4 46.0 %collective-permute-start.9 = (bf16[256,2560]{0,1:T(8,128)(2,1)S(1)}, bf16[256,2560]{0,1:T(8,128)(2,1)S(1)}, u32[]{:S(2)}, u32[]{:S(2)}) collective-permute-start(bf16[256,2560]{0,1:T(8,128)(2,1)S(1)} %pad_maximum_fusion.20), channel_id=1, source_target_pairs={{0,8},{4,12},{8,0},{12,4},{16,24},{20,28},{24,16},{28,20},{1,9},{5... | collective-permute-start | bytes 3932168 | tf_op jit(solution)/shard_map/ppermute | solution.py:31
  224.7 54.6 %collective-permute-start.20 = (bf16[256,2560]{0,1:T(8,128)(2,1)S(1)}, bf16[256,2560]{0,1:T(8,128)(2,1)S(1)}, u32[]{:S(2)}, u32[]{:S(2)}) collective-permute-start(bf16[256,2560]{0,1:T(8,128)(2,1)S(1)} %pad_maximum_fusion.23), channel_id=1, source_target_pairs={{0,16},{4,20},{8,24},{12,28},{16,0},{20,4},{24,8},{28,12},{1,17},{... | collective-permute-start | bytes 3932168 | tf_op jit(solution)/shard_map/ppermute | solution.py:31
  252.8 31.7 %collective-permute-start.22 = (bf16[256,2560]{0,1:T(8,128)(2,1)S(1)}, bf16[256,2560]{0,1:T(8,128)(2,1)S(1)}, u32[]{:S(2)}, u32[]{:S(2)}) collective-permute-start(bf16[256,2560]{0,1:T(8,128)(2,1)S(1)} %pad_maximum_fusion.24), channel_id=1, source_target_pairs={{0,8},{4,12},{8,0},{12,4},{16,24},{20,28},{24,16},{28,20},{1,9},{5... | collective-permute-start | bytes 3932168 | tf_op jit(solution)/shard_map/ppermute | solution.py:31
  257.4 56.7 %collective-permute-start.32 = (bf16[256,3072]{1,0:T(8,128)(2,1)S(1)}, bf16[256,3072]{1,0:T(8,128)(2,1)S(1)}, u32[]{:S(2)}, u32[]{:S(2)}) collective-permute-start(bf16[256,3072]{1,0:T(8,128)(2,1)S(1)} %pad_maximum_fusion.18), channel_id=1, source_target_pairs={{0,8},{4,12},{8,0},{12,4},{16,24},{20,28},{24,16},{28,20},{1,9},{5... | collective-permute-start | bytes 4718600 | tf_op jit(solution)/shard_map/ppermute | solution.py:31
  279.3 74.7 %collective-permute-start.10 = (bf16[1024,2560]{0,1:T(8,128)(2,1)}, bf16[1024,2560]{0,1:T(8,128)(2,1)}, u32[]{:S(2)}, u32[]{:S(2)}) collective-permute-start(bf16[1024,2560]{0,1:T(8,128)(2,1)} %constant_dynamic-update-slice_fusion.1), channel_id=1, source_target_pairs={{0,4},{4,0},{8,12},{12,8},{16,20},{20,16},{24,28},{28,24},{1,5},{5... | collective-permute-start | bytes 15728648 | tf_op jit(solution)/shard_map/ppermute | solution.py:31
  285.8 94.6 %collective-permute-start.23 = (bf16[1024,2560]{0,1:T(8,128)(2,1)}, bf16[1024,2560]{0,1:T(8,128)(2,1)}, u32[]{:S(2)}, u32[]{:S(2)}) collective-permute-start(bf16[1024,2560]{0,1:T(8,128)(2,1)} %constant_dynamic-update-slice_fusion.13), channel_id=1, source_target_pairs={{0,4},{4,0},{8,12},{12,8},{16,20},{20,16},{24,28},{28,24},{1,5},{5... | collective-permute-start | bytes 15728648 | tf_op jit(solution)/shard_map/ppermute | solution.py:31
  364.1 88.8 %collective-permute-start.33 = (bf16[1024,3072]{1,0:T(8,128)(2,1)}, bf16[1024,3072]{1,0:T(8,128)(2,1)}, u32[]{:S(2)}, u32[]{:S(2)}) collective-permute-start(bf16[1024,3072]{1,0:T(8,128)(2,1)} %get-tuple-element.141), channel_id=1, source_target_pairs={{0,4},{4,0},{8,12},{12,8},{16,20},{20,16},{24,28},{28,24},{1,5},{5... | collective-permute-start | bytes 18874376 | tf_op jit(solution)/shard_map/ppermute | solution.py:31
  388.5 160.6 %all-gather.15.cloned.1.call-start = ((), (), s32[]{:S(2)}) async-start(), calls=%async_computation.6 | async-start | bytes 5242880 | tf_op jit(solution)/shard_map/all_gather | solution.py:453
  452.8 226.7 %reduce-scatter.5.cloned.1.call-start = ((), (), s32[]{:S(2)}) async-start(), calls=%async_computation.5 | async-start | bytes 5242880 | tf_op jit(solution)/shard_map/reduce_scatter | solution.py:460
  533.5 172.7 %reduce-scatter.7.cloned.1.call-start = ((), (), s32[]{:S(2)}) async-start(), calls=%async_computation.7 | async-start | bytes 5242880 | tf_op jit(solution)/shard_map/reduce_scatter | solution.py:460
  617.6 559.9 %reduce-scatter.9.cloned.1.call-start = ((), (), s32[]{:S(2)}) async-start(), calls=%async_computation.8 | async-start | bytes 5242880 | tf_op jit(solution)/shard_map/reduce_scatter | solution.py:479
  744.9 432.6 %reduce-scatter.11.cloned.1.call-start = ((), (), s32[]{:S(2)}) async-start(), calls=%async_computation.9 | async-start | bytes 5242880 | tf_op jit(solution)/shard_map/reduce_scatter | solution.py:479
  874.9 248.0 %collective-permute-start.66 = (bf16[1024,2560]{1,0:T(8,128)(2,1)}, bf16[1024,2560]{1,0:T(8,128)(2,1)}, u32[]{:S(2)}, u32[]{:S(2)}) collective-permute-start(bf16[1024,2560]{1,0:T(8,128)(2,1)} %slice.564), channel_id=1, source_target_pairs={{0,4},{4,0},{8,12},{12,8},{16,20},{20,16},{24,28},{28,24},{1,5},{5... | collective-permute-start | bytes 15728648 | tf_op jit(solution)/shard_map/ppermute | solution.py:31
  883.2 577.1 %all-gather.25.cloned.1.call-start = ((), (), s32[]{:S(2)}) async-start(), calls=%async_computation.14 | async-start | bytes 5242880 | tf_op jit(solution)/shard_map/all_gather | solution.py:481
  897.9 110.6 %collective-permute-start.39 = (bf16[512,2048]{1,0:T(8,128)(2,1)}, bf16[512,2048]{1,0:T(8,128)(2,1)}, u32[]{:S(2)}, u32[]{:S(2)}) collective-permute-start(bf16[512,2048]{1,0:T(8,128)(2,1)} %permute.9), channel_id=1, source_target_pairs={{0,1},{1,2},{2,3},{4,5},{5,6},{6,7},{8,9},{9,10},{10,11},{12,13},{... | collective-permute-start | bytes 6291464 | tf_op jit(solution)/shard_map/ppermute | solution.py:87
  905.6 90.9 %collective-permute-start.49 = (bf16[26752]{0:T(1024)(128)(2,1)S(1)}, bf16[26752]{0:T(1024)(128)(2,1)S(1)}, u32[]{:S(2)}, u32[]{:S(2)}) collective-permute-start(bf16[26752]{0:T(1024)(128)(2,1)S(1)} %get-tuple-element.101), channel_id=1, source_target_pairs={{0,3},{1,0},{2,1},{3,2},{4,7},{5,4},{6,5},{7,6},{8,11},{9,8},{10,9... | collective-permute-start | bytes 160520 | tf_op jit(solution)/shard_map/ppermute | solution.py:71
  910.2 87.6 %collective-permute-start.80 = (bf16[256,1536]{1,0:T(8,128)(2,1)S(1)}, bf16[256,1536]{1,0:T(8,128)(2,1)S(1)}, u32[]{:S(2)}, u32[]{:S(2)}) collective-permute-start(bf16[256,1536]{1,0:T(8,128)(2,1)S(1)} %get-tuple-element.135), channel_id=1, source_target_pairs={{0,16},{4,20},{8,24},{12,28},{16,0},{20,4},{24,8},{28,12},{1,17},{... | collective-permute-start | bytes 2359304 | tf_op jit(solution)/shard_map/ppermute | solution.py:31
  911.7 86.2 %collective-permute-start.82 = (bf16[256,1536]{1,0:T(8,128)(2,1)S(1)}, bf16[256,1536]{1,0:T(8,128)(2,1)S(1)}, u32[]{:S(2)}, u32[]{:S(2)}) collective-permute-start(bf16[256,1536]{1,0:T(8,128)(2,1)S(1)} %get-tuple-element.136), channel_id=1, source_target_pairs={{0,8},{4,12},{8,0},{12,4},{16,24},{20,28},{24,16},{28,20},{1,9},{5... | collective-permute-start | bytes 2359304 | tf_op jit(solution)/shard_map/ppermute | solution.py:31
  996.5 73.6 %collective-permute-start.38 = (bf16[512,2048]{1,0:T(8,128)(2,1)S(1)}, bf16[512,2048]{1,0:T(8,128)(2,1)}, u32[]{:S(2)}, u32[]{:S(2)}) collective-permute-start(bf16[512,2048]{1,0:T(8,128)(2,1)S(1)} %copy-done.18), channel_id=1, source_target_pairs={{1,0},{2,1},{3,2},{5,4},{6,5},{7,6},{9,8},{10,9},{11,10},{13,12},{... | collective-permute-start | bytes 6291464 | tf_op jit(solution)/shard_map/ppermute | solution.py:88
  997.9 51.9 %collective-permute-start.47 = (bf16[26752]{0:T(1024)(128)(2,1)S(1)}, bf16[26752]{0:T(1024)(128)(2,1)S(1)}, u32[]{:S(2)}, u32[]{:S(2)}) collective-permute-start(bf16[26752]{0:T(1024)(128)(2,1)S(1)} %get-tuple-element.100), channel_id=1, source_target_pairs={{0,1},{1,2},{2,3},{3,0},{4,5},{5,6},{6,7},{7,4},{8,9},{9,10},{10,1... | collective-permute-start | bytes 160520 | tf_op jit(solution)/shard_map/ppermute | solution.py:71
  1008.6 123.0 %collective-permute-start.50 = (bf16[1024,2560]{1,0:T(8,128)(2,1)}, bf16[1024,2560]{1,0:T(8,128)(2,1)}, u32[]{:S(2)}, u32[]{:S(2)}) collective-permute-start(bf16[1024,2560]{1,0:T(8,128)(2,1)} %slice.542), channel_id=1, source_target_pairs={{0,4},{4,0},{8,12},{12,8},{16,20},{20,16},{24,28},{28,24},{1,5},{5... | collective-permute-start | bytes 15728648 | tf_op jit(solution)/shard_map/ppermute | solution.py:31
  1008.6 74.4 %collective-permute-start.40 = (bf16[512,2048]{1,0:T(8,128)(2,1)}, bf16[512,2048]{1,0:T(8,128)(2,1)}, u32[]{:S(2)}, u32[]{:S(2)}) collective-permute-start(bf16[512,2048]{1,0:T(8,128)(2,1)} %collective-permute-done.39), channel_id=1, source_target_pairs={{1,2},{2,3},{5,6},{6,7},{9,10},{10,11},{13,14},{14,15},{17,18},{18... | collective-permute-start | bytes 6291464 | tf_op jit(solution)/shard_map/ppermute | solution.py:87
  1070.1 50.8 %collective-permute-start.42 = (bf16[512,2048]{1,0:T(8,128)(2,1)}, bf16[512,2048]{1,0:T(8,128)(2,1)}, u32[]{:S(2)}, u32[]{:S(2)}) collective-permute-start(bf16[512,2048]{1,0:T(8,128)(2,1)} %collective-permute-done.38), channel_id=1, source_target_pairs={{1,0},{2,1},{5,4},{6,5},{9,8},{10,9},{13,12},{14,13},{17,16},{18,1... | collective-permute-start | bytes 6291464 | tf_op jit(solution)/shard_map/ppermute | solution.py:88
  1080.8 59.9 %collective-permute-start.58 = (bf16[1024,2560]{1,0:T(8,128)(2,1)}, bf16[1024,2560]{1,0:T(8,128)(2,1)}, u32[]{:S(2)}, u32[]{:S(2)}) collective-permute-start(bf16[1024,2560]{1,0:T(8,128)(2,1)} %slice.552), channel_id=1, source_target_pairs={{0,4},{4,0},{8,12},{12,8},{16,20},{20,16},{24,28},{28,24},{1,5},{5... | collective-permute-start | bytes 15728648 | tf_op jit(solution)/shard_map/ppermute | solution.py:31
  1083.0 66.6 %collective-permute-start.74 = (bf16[1024,3072]{1,0:T(8,128)(2,1)}, bf16[1024,3072]{1,0:T(8,128)(2,1)}, u32[]{:S(2)}, u32[]{:S(2)}) collective-permute-start(bf16[1024,3072]{1,0:T(8,128)(2,1)} %slice.462), channel_id=1, source_target_pairs={{0,4},{4,0},{8,12},{12,8},{16,20},{20,16},{24,28},{28,24},{1,5},{5... | collective-permute-start | bytes 18874376 | tf_op jit(solution)/shard_map/ppermute | solution.py:31
  1120.9 40.9 %collective-permute-start.41 = (bf16[512,2048]{1,0:T(8,128)(2,1)}, bf16[512,2048]{1,0:T(8,128)(2,1)}, u32[]{:S(2)}, u32[]{:S(2)}) collective-permute-start(bf16[512,2048]{1,0:T(8,128)(2,1)} %collective-permute-done.40), channel_id=1, source_target_pairs={{2,3},{6,7},{10,11},{14,15},{18,19},{22,23},{26,27},{30,31}} | collective-permute-start | bytes 6291464 | tf_op jit(solution)/shard_map/ppermute | solution.py:87
  1122.9 49.6 %collective-permute-start.43 = (bf16[512,2048]{1,0:T(8,128)(2,1)}, bf16[512,2048]{1,0:T(8,128)(2,1)}, u32[]{:S(2)}, u32[]{:S(2)}) collective-permute-start(bf16[512,2048]{1,0:T(8,128)(2,1)} %collective-permute-done.42), channel_id=1, source_target_pairs={{1,0},{5,4},{9,8},{13,12},{17,16},{21,20},{25,24},{29,28}} | collective-permute-start | bytes 6291464 | tf_op jit(solution)/shard_map/ppermute | solution.py:88
  1132.8 53.1 %collective-permute-start.67 = (bf16[256,2560]{1,0:T(8,128)(2,1)}, bf16[256,2560]{1,0:T(8,128)(2,1)}, u32[]{:S(2)}, u32[]{:S(2)}) collective-permute-start(bf16[256,2560]{1,0:T(8,128)(2,1)} %get-tuple-element.121), channel_id=1, source_target_pairs={{0,16},{4,20},{8,24},{12,28},{16,0},{20,4},{24,8},{28,12},{1,17},{... | collective-permute-start | bytes 3932168 | tf_op jit(solution)/shard_map/ppermute | solution.py:31
  1142.0 45.0 %collective-permute-start.69 = (bf16[256,2560]{1,0:T(8,128)(2,1)}, bf16[256,2560]{1,0:T(8,128)(2,1)}, u32[]{:S(2)}, u32[]{:S(2)}) collective-permute-start(bf16[256,2560]{1,0:T(8,128)(2,1)} %get-tuple-element.122), channel_id=1, source_target_pairs={{0,8},{4,12},{8,0},{12,4},{16,24},{20,28},{24,16},{28,20},{1,9},{5... | collective-permute-start | bytes 3932168 | tf_op jit(solution)/shard_map/ppermute | solution.py:31
  1150.9 42.1 %collective-permute-start.51 = (bf16[256,2560]{1,0:T(8,128)(2,1)}, bf16[256,2560]{1,0:T(8,128)(2,1)}, u32[]{:S(2)}, u32[]{:S(2)}) collective-permute-start(bf16[256,2560]{1,0:T(8,128)(2,1)} %get-tuple-element.129), channel_id=1, source_target_pairs={{0,16},{4,20},{8,24},{12,28},{16,0},{20,4},{24,8},{28,12},{1,17},{... | collective-permute-start | bytes 3932168 | tf_op jit(solution)/shard_map/ppermute | solution.py:31
  1161.8 40.3 %collective-permute-start.53 = (bf16[256,2560]{1,0:T(8,128)(2,1)}, bf16[256,2560]{1,0:T(8,128)(2,1)}, u32[]{:S(2)}, u32[]{:S(2)}) collective-permute-start(bf16[256,2560]{1,0:T(8,128)(2,1)} %get-tuple-element.130), channel_id=1, source_target_pairs={{0,8},{4,12},{8,0},{12,4},{16,24},{20,28},{24,16},{28,20},{1,9},{5... | collective-permute-start | bytes 3932168 | tf_op jit(solution)/shard_map/ppermute | solution.py:31
  1172.5 48.5 %collective-permute-start.59 = (bf16[256,2560]{1,0:T(8,128)(2,1)}, bf16[256,2560]{1,0:T(8,128)(2,1)S(1)}, u32[]{:S(2)}, u32[]{:S(2)}) collective-permute-start(bf16[256,2560]{1,0:T(8,128)(2,1)} %get-tuple-element.125), channel_id=1, source_target_pairs={{0,16},{4,20},{8,24},{12,28},{16,0},{20,4},{24,8},{28,12},{1,17},{... | collective-permute-start | bytes 3932168 | tf_op jit(solution)/shard_map/ppermute | solution.py:31
  1185.7 274.6 %all-gather.23.cloned.1.call-start = ((), (), s32[]{:S(2)}) async-start(), calls=%async_computation.13 | async-start | bytes 5242880 | tf_op jit(solution)/shard_map/all_gather | solution.py:481
  1186.0 44.2 %collective-permute-start.61 = (bf16[256,2560]{1,0:T(8,128)(2,1)S(1)}, bf16[256,2560]{1,0:T(8,128)(2,1)S(1)}, u32[]{:S(2)}, u32[]{:S(2)}) collective-permute-start(bf16[256,2560]{1,0:T(8,128)(2,1)S(1)} %copy-done.50), channel_id=1, source_target_pairs={{0,8},{4,12},{8,0},{12,4},{16,24},{20,28},{24,16},{28,20},{1,9},{5... | collective-permute-start | bytes 3932168 | tf_op jit(solution)/shard_map/ppermute | solution.py:31
  1187.0 147.8 %collective-permute-start.75 = (bf16[256,3072]{1,0:T(8,128)(2,1)}, bf16[256,3072]{1,0:T(8,128)(2,1)}, u32[]{:S(2)}, u32[]{:S(2)}) collective-permute-start(bf16[256,3072]{1,0:T(8,128)(2,1)} %get-tuple-element.117), channel_id=1, source_target_pairs={{0,16},{4,20},{8,24},{12,28},{16,0},{20,4},{24,8},{28,12},{1,17},{... | collective-permute-start | bytes 4718600 | tf_op jit(solution)/shard_map/ppermute | solution.py:31
  1192.9 153.4 %collective-permute-start.77 = (bf16[256,3072]{1,0:T(8,128)(2,1)}, bf16[256,3072]{1,0:T(8,128)(2,1)}, u32[]{:S(2)}, u32[]{:S(2)}) collective-permute-start(bf16[256,3072]{1,0:T(8,128)(2,1)} %get-tuple-element.118), channel_id=1, source_target_pairs={{0,8},{4,12},{8,0},{12,4},{16,24},{20,28},{24,16},{28,20},{1,9},{5... | collective-permute-start | bytes 4718600 | tf_op jit(solution)/shard_map/ppermute | solution.py:31
  1202.1 66.5 %collective-permute-start.70 = (bf16[128,2560]{1,0:T(8,128)(2,1)S(1)}, bf16[128,2560]{1,0:T(8,128)(2,1)S(1)}, u32[]{:S(2)}, u32[]{:S(2)}) collective-permute-start(bf16[128,2560]{1,0:T(8,128)(2,1)S(1)} %slice.572), channel_id=1, source_target_pairs={{0,16},{4,20},{8,24},{12,28},{16,0},{20,4},{24,8},{28,12},{1,17},{... | collective-permute-start | bytes 1966088 | tf_op jit(solution)/shard_map/ppermute | solution.py:31
  1220.9 57.0 %collective-permute-start.68 = (bf16[128,2560]{1,0:T(8,128)(2,1)S(1)}, bf16[128,2560]{1,0:T(8,128)(2,1)S(1)}, u32[]{:S(2)}, u32[]{:S(2)}) collective-permute-start(bf16[128,2560]{1,0:T(8,128)(2,1)S(1)} %slice.568), channel_id=1, source_target_pairs={{0,8},{4,12},{8,0},{12,4},{16,24},{20,28},{24,16},{28,20},{1,9},{5... | collective-permute-start | bytes 1966088 | tf_op jit(solution)/shard_map/ppermute | solution.py:31
  1230.1 52.7 %collective-permute-start.54 = (bf16[128,2560]{1,0:T(8,128)(2,1)}, bf16[128,2560]{1,0:T(8,128)(2,1)}, u32[]{:S(2)}, u32[]{:S(2)}) collective-permute-start(bf16[128,2560]{1,0:T(8,128)(2,1)} %slice.550), channel_id=1, source_target_pairs={{0,16},{4,20},{8,24},{12,28},{16,0},{20,4},{24,8},{28,12},{1,17},{... | collective-permute-start | bytes 1966088 | tf_op jit(solution)/shard_map/ppermute | solution.py:31
  1305.6 71.7 %collective-permute-start.56 = (bf16[256,640]{1,0:T(8,128)(2,1)}, bf16[256,640]{1,0:T(8,128)(2,1)}, u32[]{:S(2)}, u32[]{:S(2)}) collective-permute-start(bf16[256,640]{1,0:T(8,128)(2,1)} %bitcast.216), channel_id=1, source_target_pairs={{0,2},{1,3},{2,0},{3,1},{4,6},{5,7},{6,4},{7,5},{8,10},{9,11},{10,... | collective-permute-start | bytes 983048 | tf_op jit(solution)/shard_map/ppermute | solution.py:71
  1313.4 64.0 %collective-permute-start.55 = (bf16[256,640]{1,0:T(8,128)(2,1)}, bf16[256,640]{1,0:T(8,128)(2,1)}, u32[]{:S(2)}, u32[]{:S(2)}) collective-permute-start(bf16[256,640]{1,0:T(8,128)(2,1)} %bitcast.176), channel_id=1, source_target_pairs={{0,1},{1,2},{2,3},{3,0},{4,5},{5,6},{6,7},{7,4},{8,9},{9,10},{10,1... | collective-permute-start | bytes 983048 | tf_op jit(solution)/shard_map/ppermute | solution.py:71
  1331.0 46.4 %collective-permute-start.65 = (bf16[256,640]{1,0:T(8,128)(2,1)S(1)}, bf16[256,640]{1,0:T(8,128)(2,1)S(1)}, u32[]{:S(2)}, u32[]{:S(2)}) collective-permute-start(bf16[256,640]{1,0:T(8,128)(2,1)S(1)} %bitcast.218), channel_id=1, source_target_pairs={{0,3},{1,0},{2,1},{3,2},{4,7},{5,4},{6,5},{7,6},{8,11},{9,8},{10,9... | collective-permute-start | bytes 983048 | tf_op jit(solution)/shard_map/ppermute | solution.py:71
  1334.8 104.1 %collective-permute-start.64 = (bf16[256,640]{1,0:T(8,128)(2,1)S(1)}, bf16[256,640]{1,0:T(8,128)(2,1)S(1)}, u32[]{:S(2)}, u32[]{:S(2)}) collective-permute-start(bf16[256,640]{1,0:T(8,128)(2,1)S(1)} %bitcast.217), channel_id=1, source_target_pairs={{0,2},{1,3},{2,0},{3,1},{4,6},{5,7},{6,4},{7,5},{8,10},{9,11},{10,... | collective-permute-start | bytes 983048 | tf_op jit(solution)/shard_map/ppermute | solution.py:71
  1346.4 96.1 %collective-permute-start.63 = (bf16[256,640]{1,0:T(8,128)(2,1)}, bf16[256,640]{1,0:T(8,128)(2,1)S(1)}, u32[]{:S(2)}, u32[]{:S(2)}) collective-permute-start(bf16[256,640]{1,0:T(8,128)(2,1)} %bitcast.173), channel_id=1, source_target_pairs={{0,1},{1,2},{2,3},{3,0},{4,5},{5,6},{6,7},{7,4},{8,9},{9,10},{10,1... | collective-permute-start | bytes 983048 | tf_op jit(solution)/shard_map/ppermute | solution.py:71
  1377.3 66.5 %collective-permute-start.73 = (bf16[256,640]{0,1:T(8,128)(2,1)}, bf16[256,640]{0,1:T(8,128)(2,1)S(1)}, u32[]{:S(2)}, u32[]{:S(2)}) collective-permute-start(bf16[256,640]{0,1:T(8,128)(2,1)} %bitcast.56), channel_id=1, source_target_pairs={{0,3},{1,0},{2,1},{3,2},{4,7},{5,4},{6,5},{7,6},{8,11},{9,8},{10,9... | collective-permute-start | bytes 983048 | tf_op jit(solution)/shard_map/ppermute | solution.py:71
  1377.4 79.1 %collective-permute-start.72 = (bf16[256,640]{0,1:T(8,128)(2,1)}, bf16[256,640]{0,1:T(8,128)(2,1)S(1)}, u32[]{:S(2)}, u32[]{:S(2)}) collective-permute-start(bf16[256,640]{0,1:T(8,128)(2,1)} %bitcast.55), channel_id=1, source_target_pairs={{0,2},{1,3},{2,0},{3,1},{4,6},{5,7},{6,4},{7,5},{8,10},{9,11},{10,... | collective-permute-start | bytes 983048 | tf_op jit(solution)/shard_map/ppermute | solution.py:71
  1377.4 79.1 %collective-permute-start.71 = (bf16[256,640]{0,1:T(8,128)(2,1)}, bf16[256,640]{0,1:T(8,128)(2,1)S(1)}, u32[]{:S(2)}, u32[]{:S(2)}) collective-permute-start(bf16[256,640]{0,1:T(8,128)(2,1)} %bitcast.54), channel_id=1, source_target_pairs={{0,1},{1,2},{2,3},{3,0},{4,5},{5,6},{6,7},{7,4},{8,9},{9,10},{10,1... | collective-permute-start | bytes 983048 | tf_op jit(solution)/shard_map/ppermute | solution.py:71
  (142 other events, 3033.4 us)
Sparse Core Ops, SparseCore 0:
  10.2 37.3 all-gather.18
  49.7 32.3 all-gather.16
  83.7 31.6 all-gather.20
  388.6 79.0 all-gather.12
  469.7 79.2 all-gather.14
  551.2 75.2 reduce-scatter.4
  628.9 77.2 reduce-scatter.6
  745.1 83.4 reduce-scatter.8
  883.3 124.5 reduce-scatter.10
  1185.8 85.0 all-gather.24
  1305.7 147.7 all-gather.22

commit v3 on v2

--- a/solution.py
+++ b/solution.py
@@ -17,14 +17,26 @@
 VMEM = 58 * 1024 * 1024
 BF = jnp.bfloat16
 F32 = jnp.float32
+LITTLE = pl.CostEstimate(flops=1024, bytes_accessed=1024, transcendentals=0)
 
 
 def dot(left, right, dims=((1,), (0,))):
     return lax.dot_general(left, right, (dims, ((), ())), preferred_element_type=F32)
 
 
-def tie(values, *others):
-    return lax.optimization_barrier((values,) + others)[0]
+def fence(values, *others):
+    if not others:
+        return list(values)
+    place = pl.BlockSpec(memory_space=pl.ANY)
+    return pl.pallas_call(
+        lambda *refs: None,
+        in_specs=[place] * (len(values) + len(others)),
+        out_specs=[place] * len(values),
+        out_shape=[jax.ShapeDtypeStruct(v.shape, v.dtype) for v in values],
+        input_output_aliases={k: k for k in range(len(values))},
+        compiler_params=pltpu.CompilerParams(vmem_limit_bytes=VMEM),
+        name="fence",
+    )(*values, *others)
 
 
 def exchange(values, bit, size):
@@ -40,30 +52,54 @@
     return 2 if rows % 256 == 0 else 1
 
 
-def spread(own, size):
-    parts = parts_of(own.shape[0])
-    pieces = jnp.split(own, parts)
-    for turn in range(size.bit_length() - 2):
-        got = [exchange(p, o[turn], size) for p, o in zip(pieces, orders(size, parts))]
-        pieces = [jnp.concatenate([p, g]) for p, g in zip(pieces, got)]
-    half = jnp.concatenate(pieces)
-    return [half, exchange(half, 0, size)], got[-1][:16, :128]
-
-
-def add_low(one, two):
-    return (one.astype(F32) + two.astype(F32)).astype(BF)
-
-
-def collect(full, size):
-    half = full.shape[0] // 2
-    parts = parts_of(full.shape[0] // size)
-    kept = add_low(full[:half], exchange(full[half:], 0, size))
-    pieces = jnp.split(kept, parts)
-    for turn in reversed(range(size.bit_length() - 2)):
-        cut = pieces[0].shape[0] // 2
-        got = [exchange(p[cut:], o[turn], size) for p, o in zip(pieces, orders(size, parts))]
-        pieces = [add_low(p[:cut], g) for p, g in zip(pieces, got)]
-    return jnp.concatenate(pieces)
+def hop(pieces, turn, size):
+    got = [exchange(p, o[turn], size) for p, o in zip(pieces, orders(size, len(pieces)))]
+    return [jnp.concatenate([p, g]) for p, g in zip(pieces, got)], got
+
+
+def spread_begin(own, size, *before):
+    pieces, got = fence(jnp.split(own, parts_of(own.shape[0])), *before), ()
+    for turn in range(size.bit_length() - 3):
+        pieces, got = hop(pieces, turn, size)
+    return pieces, got
+
+
+def spread_end(pieces, size, before_last, before_core):
+    pieces, got = hop(fence(pieces, *before_last), size.bit_length() - 3, size)
+    half = jnp.concatenate(fence(pieces, *before_core))
+    return [half, exchange(half, 0, size)], got
+
+
+def add_all(terms):
+    total = terms[0].astype(F32)
+    for term in terms[1:]:
+        total = total + term.astype(F32)
+    return total.astype(BF)
+
+
+class Collect:
+    def __init__(self, keep, send, size, d_own):
+        self.size = size
+        self.parts = parts_of(d_own)
+        got = exchange(send, 0, size)
+        self.terms = list(zip(jnp.split(keep, self.parts), jnp.split(got, self.parts)))
+        self.turn = size.bit_length() - 2
+
+    def sources(self):
+        cut = self.terms[0][0].shape[0] // 2
+        return [add_all([t[cut:] for t in terms]) for terms in self.terms]
+
+    def hop(self, sources):
+        self.turn -= 1
+        cut = sources[0].shape[0]
+        got = [exchange(v, o[self.turn], self.size) for v, o in zip(sources, orders(self.size, self.parts))]
+        self.terms = [[t[:cut] for t in terms] + [g] for terms, g in zip(self.terms, got)]
+        return got
+
+    def finish(self):
+        while self.turn:
+            self.hop(self.sources())
+        return jnp.concatenate([add_all(terms) for terms in self.terms])
 
 
 def z_shift(values, by, n, around=True):
@@ -80,17 +116,20 @@
     return total
 
 
-def z_line(own, n):
+def line_round(right, left, k, n):
+    right = lax.ppermute(right, "tensor", [(s, s + 1) for s in range(k - 1, n - 1)])
+    left = lax.ppermute(left, "tensor", [(s, s - 1) for s in range(1, n - k + 1)])
+    return right, left
+
+
+def line_result(own, rounds, n):
     turn = lax.axis_index("tensor")
-    right, left = [own], [own]
-    for k in range(1, n):
-        right.append(lax.ppermute(right[-1], "tensor", [(s, s + 1) for s in range(k - 1, n - 1)]))
-        left.append(lax.ppermute(left[-1], "tensor", [(s, s - 1) for s in range(1, n - k + 1)]))
     rows = own.shape[0]
     out = jnp.zeros((n * rows, own.shape[1]), own.dtype)
     out = lax.dynamic_update_slice_in_dim(out, own, turn * rows, 0)
     for k in range(1, n):
-        out = lax.dynamic_update_slice_in_dim(out, left[k] + right[n - k], (turn + k) % n * rows, 0)
+        piece = rounds[k - 1][1] + rounds[n - k - 1][0]
+        out = lax.dynamic_update_slice_in_dim(out, piece, (turn + k) % n * rows, 0)
     return out
 
 
@@ -108,7 +147,7 @@
     values = jnp.take(values, jnp.arange(size) ^ place, axis=0)
     for bit in reversed(range(size.bit_length() - 1)):
         half = values.shape[0] // 2
-        values = add_low(values[:half], exchange(values[half:], bit, size))
+        values = add_all([values[:half], exchange(values[half:], bit, size)])
     return z_scatter(values[0], n)
 
 
@@ -146,7 +185,7 @@
         ),
         out_shape=jax.ShapeDtypeStruct(values.shape, values.dtype),
         compiler_params=pltpu.CompilerParams(vmem_limit_bytes=VMEM),
-        cost_estimate=pl.CostEstimate(flops=0, bytes_accessed=2 * values.nbytes, transcendentals=0),
+        cost_estimate=LITTLE,
         name="permute",
     )(table, values)
 
@@ -321,7 +360,7 @@
         drec_ref[pl.ds(at, count), :] = total
 
 
-def kernel_call(body, live, arrays, outs, scratch, name, work):
+def kernel_call(body, live, arrays, outs, scratch, name):
     width = outs[0][1]
     steps = width // GROUP
     specs = []
@@ -338,7 +377,6 @@
         else:
             out_specs.append(pl.BlockSpec((pl.squeezed, rows, cols), lambda j, s: (j, 0, 0)))
             out_shapes.append(jax.ShapeDtypeStruct((steps, rows, cols), kind))
-    moved = sum(a.nbytes for a in arrays) + sum(int(np.prod(o.shape)) * o.dtype.itemsize for o in out_shapes)
     return pl.pallas_call(
         body,
         grid_spec=pltpu.PrefetchScalarGridSpec(
@@ -347,7 +385,7 @@
         ),
         out_shape=out_shapes,
         compiler_params=pltpu.CompilerParams(vmem_limit_bytes=VMEM),
-        cost_estimate=pl.CostEstimate(flops=work * outs[0][0] * width, bytes_accessed=moved, transcendentals=0),
+        cost_estimate=LITTLE,
         name=name,
     )(live, *arrays)
 
@@ -394,17 +432,15 @@
         return own.transpose(1, 0, 2).reshape(d_own, width)
 
     z_rec = wide(w_rec.astype(BF))
+    own_gu = jnp.concatenate([w_mlp_in[0], w_mlp_in[1]], axis=1).astype(BF)
+    own_dn = w_down.T.astype(BF)
     small = [w_lru.transpose(2, 0, 1, 3).reshape(-1), chan.reshape(-1), gains.reshape(-1)]
     small = small_gather(jnp.concatenate(small).astype(BF), size, n)
-    w_r, token = spread(tie(z_rec, small[0, 0, :128]), size)
-    z_gelu = tie(wide(tie(w_gelu.astype(BF), z_rec[:16, :128])), token)
-    w_g, token = spread(z_gelu, size)
-    z_out = tie(wide(tie(w_out.T.astype(BF), z_gelu[:16, :128])), token)
-    w_o, token = spread(z_out, size)
-    w_gu = jnp.concatenate([w_mlp_in[0], w_mlp_in[1]], axis=1).astype(BF)
-    w_gu, token = spread(tie(w_gu, token), size)
-    w_gu = jnp.concatenate(w_gu)
-    w_dn = jnp.concatenate(spread(tie(w_down.T.astype(BF), token), size)[0])
+    z_gelu = wide(*fence([w_gelu.astype(BF)], z_rec))
+    z_out = wide(*fence([w_out.T.astype(BF)], z_gelu))
+    some_gu, came_gu = spread_begin(own_gu, size)
+    some_dn, came_dn = spread_begin(own_dn, size)
+    some_r, _ = spread_begin(z_rec, size, *came_gu, *came_dn)
 
     gain = small[0, :, -gains.size :].reshape(size, 2, d_own).transpose(1, 0, 2).reshape(2, d_model)
     gain = permute_gain(gain, table).astype(F32)
@@ -424,63 +460,76 @@
     inputs, first_own, first_rate = extended[HALO:], first[HALO:], first_rate[HALO:]
     cot = permute_rows(cotangent, table).reshape(n, 2, half, d_model)
     cots = [cot[:, h].reshape(n * half, d_model) for h in range(2)]
+    cut = d_model // 2
 
     keep = (rows, width, F32)
     dense = ((GROUP, 2 * GROUP), BF)
+    w_r, came_r = spread_end(some_r, size, (), (first, *cots, z_gelu))
+    some_g, _ = spread_begin(z_gelu, size, *came_r)
     rec_pre = wide_dot(first, w_r)
     conv, decay, ig, dg, state, prod = kernel_call(
         forward_kernel, live_count, [rec_pre, par, lru], [keep] * 6,
-        [((rows + HALO, GROUP), F32), dense], "recurrence", 18000,
+        [((rows + HALO, GROUP), F32), dense], "recurrence",
     )
     ends = jnp.concatenate([prod[-1:], state[-1:]])
     came = [z_shift(ends, k, n, False) for k in range(1, n)]
     carry = jnp.zeros((1, width), F32)
     for end in came[::-1]:
         carry = end[1:] + end[:1] * carry
+    w_g, came_g = spread_end(some_g, size, (rec_pre,), (ends,))
+    some_o, _ = spread_begin(z_out, size, *came_g, ends)
     branch_pre = wide_dot(first_own, w_g)
     recurrent = (state + prod * carry) * live
     activated, gelu_pull = jax.vjp(jax.nn.gelu, branch_pre)
     mixed = (activated * recurrent).astype(BF)
+    w_o, came_o = spread_end(some_o, size, (branch_pre,), (mixed,))
     hidden = inputs + wide_back(mixed, w_o)
     second_rate = norm_rate(hidden)
     second_unit = hidden * second_rate
     second_own = (second_unit * gain[1]).astype(BF)
+    w_gu, came_gu = spread_end(some_gu, size, came_o, (second_own,))
+    w_dn, _ = spread_end(some_dn, size, came_gu, ())
+    w_gu, w_dn = jnp.concatenate(w_gu), jnp.concatenate(w_dn)
 
     hidden_units = w_dn.shape[1]
     grad_products = [dot(c, w_dn) for c in cots]
     shares, grad_second, seconds, products, grads = [], [], [], [], []
     for h in range(2):
         second = lax.all_gather(second_own[h * half : (h + 1) * half], "tensor", axis=0, tiled=True)
+        (second,) = fence([second], *shares)
         both = dot(second, w_gu)
         product, pull = jax.vjp(gelu_product, both[:, :hidden_units], both[:, hidden_units:])
         grad_gate, grad_up = pull(grad_products[h])
         product = product.astype(BF)
         grad = jnp.concatenate([grad_gate.astype(BF), grad_up.astype(BF)], axis=1)
         share = dot(grad, w_gu, ((1,), (1,))).astype(BF)
+        shares.append(share)
         grad_second.append(lax.psum_scatter(share, "tensor", scatter_dimension=0, tiled=True))
-        shares.append(dot(tie(product, share), w_dn, ((1,), (1,))).astype(BF))
         seconds.append(second)
         products.append(product)
         grads.append(grad)
 
+    shares = [dot(p, w_dn, ((1,), (1,))).astype(BF) for p in products]
+
     def by_rows(lefts, rights):
-        part = dot(lefts[0], rights[0], ((0,), (0,))).astype(BF)
-        return (part.astype(F32) + dot(lefts[1], rights[1], ((0,), (0,)))).astype(BF)
-
-    part_gu = by_rows(seconds, grads)
-    part_dn = by_rows(cots, products)
-    *grad_second, part_gu, part_dn, share_0, share_1 = lax.optimization_barrier(
-        (*grad_second, part_gu, part_dn, *shares)
-    )
-    g_gu = collect(part_gu, size).astype(F32)
-    g_dn = collect(part_dn, size).astype(F32)
-    output = jnp.zeros((n, 2, half, d_model), BF)
-    for h, share in enumerate([share_0, share_1]):
-        mlp_sum = lax.psum_scatter(share, "tensor", scatter_dimension=0, tiled=True).astype(F32)
-        result = permute_rows((hidden[h * half : (h + 1) * half] + mlp_sum).astype(BF), inverse)
-        result = lax.all_gather(result, "tensor", axis=0)
-        output = lax.dynamic_update_slice(output, result[:, None], (0, h, 0, 0))
-    output = output.reshape(n * rows, d_model)
+        parts = []
+        for span in (slice(cut, None), slice(0, cut)):
+            part = dot(lefts[0][:, span], rights[0], ((0,), (0,)))
+            parts.append((part + dot(lefts[1][:, span], rights[1], ((0,), (0,)))).astype(BF))
+        return Collect(parts[1], parts[0], size, d_own)
+
+    sum_dn = by_rows(cots, products)
+    sum_gu = by_rows(seconds, grads)
+    sent_dn, sent_gu = sum_dn.sources(), sum_gu.sources()
+    grad_second = fence(grad_second, *sent_dn, *sent_gu)
+    sum_dn.hop(sent_dn)
+    sum_gu.hop(sent_gu)
+
+    def mlp_result(h, mlp_sum):
+        return permute_rows((hidden[h * half : (h + 1) * half] + mlp_sum.astype(F32)).astype(BF), inverse)
+
+    (share,) = fence([shares[0]], *grad_second)
+    mlp_sum = lax.psum_scatter(share, "tensor", scatter_dimension=0, tiled=True)
 
     grad_second = jnp.concatenate(grad_second).astype(F32)
     cot_own = lax.dynamic_index_in_dim(cot, turn, 0).reshape(rows, d_model).astype(F32)
@@ -488,20 +537,25 @@
     grad_hidden = cot_own + norm_back(grad_second, second_unit, second_rate, gain[1])
     hidden_low = grad_hidden.astype(BF)
 
-    def to_owner(left, right):
-        own = collect(dot(left, right, ((0,), (0,))).astype(BF), size)
-        return z_scatter(own.reshape(d_own, n, width // n).transpose(1, 0, 2), n)
+    def by_cols(left, right):
+        parts = [dot(left[:, span], right, ((0,), (0,))).astype(BF) for span in (slice(cut, None), slice(0, cut))]
+        return Collect(parts[1], parts[0], size, d_own)
 
     grad_mixed = wide_dot(hidden_low, w_o)
     lam, reach, edge = kernel_call(
         back_scan_kernel, live_count, [branch_pre, grad_mixed, decay],
-        [keep, keep, (SLAB, width, F32)], [], "back_scan", 10000,
+        [keep, keep, (SLAB, width, F32)], [], "back_scan",
     )
     edges = jnp.concatenate([prod[-1:], edge[:1]])
     came = [z_shift(edges, -k, n, False) for k in range(1, n)]
     arriving = jnp.zeros((1, width), F32)
     for end in came[::-1]:
         arriving = end[1:] + end[:1] * arriving
+    sum_o = by_cols(hidden_low, mixed)
+    sent_dn, sent_gu = sum_dn.sources(), sum_gu.sources()
+    (lam,) = fence([lam], *sent_dn, *sent_gu)
+    sum_dn.hop(sent_dn)
+    sum_gu.hop(sent_gu)
     (grad_pre,) = gelu_pull(grad_mixed * recurrent)
     pre_low = grad_pre.astype(BF)
     first_part = wide_back(pre_low, w_g)
@@ -511,9 +565,9 @@
         [rec_pre, par, lru, lam, reach, tall(arriving, (SLAB, width)), decay, conv, ig, dg, state, prod, tall(carry, (SLAB, width))],
         [(rows + HALO, width, F32), (8, width, F32), (head, 2 * GROUP, BF)],
         [((rows + HALO, GROUP), F32), ((rows + 2 * HALO, GROUP), F32), ((rows + SLAB, GROUP), F32), ((GROUP, 2 * GROUP), F32), dense],
-        "recurrence_back", 24000,
+        "recurrence_back",
     )
-    edge_rows = z_shift(drec[:HALO], -1, n, False)
+    (edge_rows,) = fence([z_shift(drec[:HALO], -1, n, False)], mlp_sum)
     rec_low = (drec[HALO:] + jnp.pad(edge_rows, ((rows - HALO, 0), (0, 0)))) * live
     rec_low = rec_low.astype(BF)
     grad_first = first_part + wide_back(rec_low, w_r)
@@ -521,10 +575,34 @@
     gain_one = jnp.sum(grad_first * first_unit, axis=0)
     grad_tokens = grad_hidden + norm_back(grad_first, first_unit, first_rate, gain[0])
     grad_tokens = permute_rows(grad_tokens.astype(BF), inverse)
-    g_o = to_owner(hidden_low, mixed)
-    g_g = to_owner(first_own, pre_low)
-    g_r = to_owner(first_own, rec_low)
-    grad_tokens = z_line(grad_tokens, n)
+    result_0 = lax.all_gather(mlp_result(0, mlp_sum), "tensor", axis=0)
+    sum_g = by_cols(first_own, pre_low)
+    sum_r = by_cols(first_own, rec_low)
+    d_lru, dpar = fence([d_lru, dpar], grad_tokens)
+    sent = fence(sum_o.sources(), grad_tokens)
+    rounds = [line_round(grad_tokens, grad_tokens, 1, n)]
+    got_o = sum_o.hop(sent)
+    got_g = sum_g.hop(fence(sum_g.sources(), *got_o))
+    (share,) = fence([shares[1]], result_0, *rounds[0])
+    mlp_sum = lax.psum_scatter(share, "tensor", scatter_dimension=0, tiled=True)
+    got_o = sum_o.hop(fence(sum_o.sources(), *rounds[0]))
+    rounds.append(line_round(*rounds[0], 2, n))
+    got_r = sum_r.hop(fence(sum_r.sources(), *got_o, *got_g))
+    (mlp_sum,) = fence([mlp_sum], *rounds[1])
+    result_1 = lax.all_gather(mlp_result(1, mlp_sum), "tensor", axis=0)
+    got_g = sum_g.hop(fence(sum_g.sources(), *rounds[1]))
+    sum_r.hop(fence(sum_r.sources(), *got_r, *got_g))
+    for k in range(3, n):
+        rounds.append(line_round(*rounds[-1], k, n))
+    tokens_out = line_result(grad_tokens, rounds, n)
+    output = jnp.zeros((n, 2, half, d_model), BF)
+    output = lax.dynamic_update_slice(output, result_0[:, None], (0, 0, 0, 0))
+    output = lax.dynamic_update_slice(output, result_1[:, None], (0, 1, 0, 0))
+    output = output.reshape(n * rows, d_model)
+    g_gu, g_dn = sum_gu.finish().astype(F32), sum_dn.finish().astype(F32)
+    owned = jnp.stack([total.finish().reshape(d_own, n, width // n) for total in (sum_o, sum_g, sum_r)])
+    owned = lax.psum_scatter(owned.transpose(2, 0, 1, 3), "tensor", scatter_dimension=0).astype(F32)
+    g_o, g_g, g_r = owned[0], owned[1], owned[2]
 
     d_gain = permute_gain(jnp.stack([gain_one, gain_two]), inverse)
     d_chan = jnp.concatenate([dpar[:7], dpar[7:] * 8.0 * jax.nn.sigmoid(-chans[7:])])
@@ -539,7 +617,7 @@
     d_gain = small[-gains.size :].reshape(gains.shape)
     g_gate, g_up = g_gu[:, :hidden_units], g_gu[:, hidden_units:]
     return (
-        output, grad_tokens, d_gain[0], d_gain[1], g_g, g_r, d_chan, d_lru,
+        output, tokens_out, d_gain[0], d_gain[1], g_g, g_r, d_chan, d_lru,
         g_o.T, jnp.stack([g_gate, g_up]), g_dn.T,
     )
 

time: 1490 us -> 1370 us (0.919)
  waiting for transfers between devices: 582 us -> 514 us
  starting transfers between devices: 148 us -> 93.8 us
  local copies, waits for them, and re-layouts: 213 us -> 166 us
  other arithmetic: 155 us -> 188 us
    ppermute x22 -> x13, waiting for transfers between devices: 186 us -> 3.11 us  [z_shift(): return lax.ppermute(values, 'tensor', pairs)]
    ppermute x6, waiting for transfers between devices: 35.4 us -> 216 us  [the longest x3 179 us: line_round(): lax.ppermute(left, 'tensor', [(s, s - 1) for s in range(1, n - k + 1)])]
    ppermute x56, waiting for transfers between devices: 309 us -> 195 us  [exchange(): return lax.ppermute(values, 'dp', [(k, k ^ 1 << bit) for k in range(size)])]
    ppermute x22 -> x13, starting transfers between devices: 81.9 us -> 26 us  [z_shift(): return lax.ppermute(values, 'tensor', pairs)]
    concatenate x14 -> x24, other arithmetic: 12.1 us -> 54.9 us  [the longest x18 43 us: hop(): return ([jnp.concatenate([p, g]) for p, g in zip(pieces, got)], got)]
    all_gather x3, waiting for transfers between devices: 0.01 us -> 39.9 us  [wide(): own = lax.all_gather(own, 'tensor', axis=0)]
    all_gather x2, waiting for transfers between devices: 0.01 us -> 36.9 us  [the longest x1 36.6 us: on_device(): result_1 = lax.all_gather(mlp_result(1, mlp_sum), 'tensor', axis=0)]
    slice x24 -> x4, local copies, waits for them, and re-layouts: 30.1 us -> 2.41 us  [the longest x3 1.48 us: small_scatter(): values = add_all([values[:half], exchange(values[half:], bit, size)])]
  transfers between devices with their start and end apart: 95 -> 87, of which waited for: 38 -> 36; matrix products, arithmetic and copies ran while one was open for 39% -> 41% of each run, Pallas kernels for 5% -> 6%
where the time goes in v3:
time: 1370 us; the launch traced here: 1360 us
  waiting for transfers between devices  514 us (38%)
  matrix products  300 us (22%)
  other arithmetic  188 us (14%)
  local copies, waits for them, and re-layouts  166 us (12%)
  starting transfers between devices  93.8 us (7%)
  Pallas kernels  81.3 us (6%)
  between operations  17.2 us (1%)
    dot_general x34, matrix products, dot(): lax.dot_general(left, right, (dims, ((), ())), preferred_element_type=F32)  300 us
    ppermute x56, waiting for transfers between devices, exchange(): return lax.ppermute(values, 'dp', [(k, k ^ 1 << bit) for k in range(size)])  195 us
    ppermute x3, waiting for transfers between devices, line_round(): lax.ppermute(left, 'tensor', [(s, s - 1) for s in range(1, n - k + 1)])  179 us
    unnamed x290, local copies, waits for them, and re-layouts  60.6 us
    pallas_call x3, Pallas kernels, kernel_call(): pl.pallas_call(body, grid_spec=pltpu.PrefetchScalarGridSpec(num_scalar_pr...  56.1 us
    ppermute x56, starting transfers between devices, exchange(): return lax.ppermute(values, 'dp', [(k, k ^ 1 << bit) for k in range(size)])  53.7 us
    convert_element_type x18, other arithmetic, add_all(): return total.astype(BF)  53.2 us
    concatenate x18, other arithmetic, hop(): return ([jnp.concatenate([p, g]) for p, g in zip(pieces, got)], got)  43 us
  transfers between devices with their start and end apart: 87, of which 36 were waited for; matrix products, arithmetic and copies ran while one was open for 41% of the time, Pallas kernels for 6%

profile of v3, /device:TPU:0, one launch (start us, length us, event | category | flops | bytes accessed | tf_op | source)
XLA Modules:
  0.0 1360.9 jit_solution(2717385915909171466)
XLA Ops:
  36.5 10.5 permute.6
  54.2 12.6 collective-permute-done.4
  68.2 6.1 fusion.81
  74.3 12.2 collective-permute-done.5
  105.0 7.3 collective-permute-done.10
  124.2 9.9 all-gather.19.cloned.1.call-done
  137.6 7.5 collective-permute-done.11.refs_2_
  165.4 4.9 fusion.42
  170.3 10.0 collective-permute-done.14
  182.6 7.2 convolution_add_fusion.refs_2_.pre_ref
  205.1 18.2 %recurrence.1 = (f32[512,2560]{1,0:T(8,128)}, f32[512,2560]{1,0:T(8,128)}, f32[512,2560]{1,0:T(8,128)}, f32[512,2560]{1,0:T(8,128)}, f32[512,2560]{1,0:T(8,128)}, /*index=5*/f32[512,2560]{1,0:T(8,128)}) custom-call(s32[1]{0:T(128)} %sub.49.live_ref, f32[528,2560]{1,0:T(8,128)} %convolution_add_fusion.refs_2_.pre_ref, f32[8,2560]{1,0:T(8,128)} %pad_maximum_fusion.41.par_ref, ...), custom_call_target="tpu_custom_call" | custom-call | flops 1024 | bytes 1024 | tf_op jit(solution)/shard_map/recurrence/pallas_call | solution.py:380
  236.8 30.0 %all-gather.21.cloned.1.call-done = bf16[1024,640]{1,0:T(8,128)(2,1)} async-done(((bf16[256,640]{1,0:T(8,128)(2,1)}), bf16[1024,640]{1,0:T(8,128)(2,1)}) %all-gather.21.cloned.1.call-update) | async-done | bytes 1310736 | tf_op jit(solution)/shard_map/all_gather | solution.py:431
  281.6 5.0 fusion.54
  286.7 8.1 collective-permute-done.23
  297.4 9.8 multiply_convert_fusion.5
  310.1 26.2 %collective-permute-done.25.refs_2_ = bf16[256,2560]{1,0:T(8,128)(2,1)S(1)} collective-permute-done((bf16[256,2560]{1,0:T(8,128)(2,1)}, bf16[256,2560]{1,0:T(8,128)(2,1)S(1)}, u32[]{:S(2)}, u32[]{:S(2)}) %collective-permute-start.25) | collective-permute-done | bytes 1310752 | tf_op jit(solution)/shard_map/ppermute | solution.py:43
  358.1 6.1 fusion.90
  364.2 4.9 fusion.91
  373.3 17.8 %collective-permute-done.28.refs_2_ = bf16[256,3072]{1,0:T(8,128)(2,1)} collective-permute-done((bf16[256,3072]{1,0:T(8,128)(2,1)}, bf16[256,3072]{1,0:T(8,128)(2,1)}, u32[]{:S(2)}, u32[]{:S(2)}) %collective-permute-start.28) | collective-permute-done | bytes 1572896 | tf_op jit(solution)/shard_map/ppermute | solution.py:43
  398.1 6.0 pad_maximum_fusion.1
  411.4 17.0 %collective-permute-done.31 = bf16[256,1536]{1,0:T(8,128)(2,1)S(1)} collective-permute-done((bf16[256,1536]{1,0:T(8,128)(2,1)}, bf16[256,1536]{1,0:T(8,128)(2,1)S(1)}, u32[]{:S(2)}, u32[]{:S(2)}) %collective-permute-start.31) | collective-permute-done | bytes 786464 | tf_op jit(solution)/shard_map/ppermute | solution.py:43
  455.4 6.2 constant_dynamic-update-slice_fusion.7
  461.6 19.5 %fusion.92 = f32[1024,3072]{1,0:T(8,128)} fusion(bf16[1024,2048]{1,0:T(8,128)(2,1)} %all-gather.13.cloned.1.call-done, bf16[2048,3072]{1,0:T(8,128)(2,1)} %constant_dynamic-update-slice_fusion.7), kind=kOutput, calls=%fused_computation.311 | convolution fusion | flops 12884901888 | bytes 29360128 | tf_op jit(solution)/shard_map/dot_general | solution.py:24
  481.0 16.0 %fusion.6 = (bf16[1024,1536]{1,0:T(8,128)(2,1)S(1)}, bf16[1024,1536]{1,0:T(8,128)(2,1)S(1)}, bf16[1024,1536]{1,0:T(8,128)(2,1)}) fusion(f32[1024,3072]{1,0:T(8,128)} %fusion.92, bf16[1024,2048]{1,0:T(8,128)(2,1)S(1)} %bitcast.180, bf16[2048,1536]{1,0:T(8,128)(2,1)} %constant_dynamic-update-slice_fusion.10), kind=kOutput, calls=%fused_computation.20 | convolution fusion | flops 6483345408 | bytes 32505856 | tf_op jit(solution)/shard_map/dot_general | solution.py:24
  499.7 17.5 %convolution_convert_fusion.7.refs_1_ = bf16[1024,2048]{1,0:T(8,128)(2,1)} fusion(bf16[2048,3072]{1,0:T(8,128)(2,1)} %constant_dynamic-update-slice_fusion.7, bf16[1024,1536]{1,0:T(8,128)(2,1)S(1)} %get-tuple-element.170, bf16[1024,1536]{1,0:T(8,128)(2,1)S(1)} %get-tuple-element.169), kind=kOutput, calls=%fused_computation.78 | convolution fusion | flops 12899581952 | bytes 23068672 | tf_op jit(solution)/shard_map/dot_general | solution.py:24
  517.3 13.9 %all-gather.15.cloned.1.call-done.refs_0_ = bf16[1024,2048]{1,0:T(8,128)(2,1)} async-done(((bf16[256,2048]{1,0:T(8,128)(2,1)}), bf16[1024,2048]{1,0:T(8,128)(2,1)}) %all-gather.15.cloned.1.call-update) | async-done | bytes 4194320 | tf_op jit(solution)/shard_map/all_gather | solution.py:498
  531.3 19.7 %fusion.93 = f32[1024,3072]{1,0:T(8,128)} fusion(bf16[1024,2048]{1,0:T(8,128)(2,1)} %fence.40, bf16[2048,3072]{1,0:T(8,128)(2,1)} %constant_dynamic-update-slice_fusion.7), kind=kOutput, calls=%fused_computation.312 | convolution fusion | flops 12884901888 | bytes 29360128 | tf_op jit(solution)/shard_map/dot_general | solution.py:24
  551.0 16.2 %fusion.13 = (bf16[1024,1536]{1,0:T(8,128)(2,1)S(1)}, bf16[1024,1536]{1,0:T(8,128)(2,1)S(1)}, bf16[1024,1536]{1,0:T(8,128)(2,1)}) fusion(f32[1024,3072]{1,0:T(8,128)} %fusion.93, bf16[1024,2048]{1,0:T(8,128)(2,1)S(1)} %bitcast.176, bf16[2048,1536]{1,0:T(8,128)(2,1)} %constant_dynamic-update-slice_fusion.10), kind=kOutput, calls=%fused_computation.27 | convolution fusion | flops 6483345408 | bytes 32505856 | tf_op jit(solution)/shard_map/dot_general | solution.py:24
  570.7 7.0 add_convert_fusion.2
  577.8 12.9 fusion.29
  590.7 11.9 add_convert_fusion
  603.3 17.6 %convolution_convert_fusion.6 = bf16[1024,2048]{1,0:T(8,128)(2,1)} fusion(bf16[2048,3072]{1,0:T(8,128)(2,1)} %constant_dynamic-update-slice_fusion.7, bf16[1024,1536]{1,0:T(8,128)(2,1)S(1)} %get-tuple-element.168, bf16[1024,1536]{1,0:T(8,128)(2,1)S(1)} %get-tuple-element.167), kind=kOutput, calls=%fused_computation.77 | convolution fusion | flops 12899581952 | bytes 23068672 | tf_op jit(solution)/shard_map/dot_general | solution.py:24
  622.7 11.9 fusion.32
  641.9 12.1 convolution_convert_fusion.9.refs_0_
  659.1 11.9 add_convert_fusion.1
  687.7 8.8 reduce-scatter.8.cloned.1.call-done.refs_1_
  696.5 11.1 convolution_convert_fusion.8.refs_0_
  711.4 11.2 collective-permute-done.39
  733.5 5.6 fusion.47
  739.1 7.3 convolution_add_fusion.1.grad_ref
  746.4 13.2 back_scan.1
  764.6 6.2 convolution_convert_fusion.4
  776.8 24.7 %recurrence_back.1 = (f32[528,2560]{1,0:T(8,128)}, f32[8,2560]{1,0:T(8,128)}, bf16[4,160,1280]{2,1,0:T(8,128)(2,1)}) custom-call(s32[1]{0:T(128)} %sub.49.live_ref, f32[528,2560]{1,0:T(8,128)} %convolution_add_fusion.refs_2_.pre_ref, f32[8,2560]{1,0:T(8,128)} %pad_maximum_fusion.41.par_ref, bf16[4,160,1280]{2,1,0:T(8,128)(2,1)} %reshape_transpose_reshape.3.w_ref, ...), custom_call_target="tpu_custom_call" | custom-call | flops 1024 | bytes 1024 | tf_op jit(solution)/shard_map/recurrence_back/pallas_call | solution.py:380
  812.4 11.4 fusion.20
  823.9 6.8 fusion.96
  830.6 4.9 fusion.94
  835.5 5.0 fusion.97
  840.6 4.9 fusion.95
  861.7 5.3 collective-permute-start.44
  884.7 4.7 gather_fusion.4
  889.4 6.4 convolution_convert_fusion
  902.8 36.8 %collective-permute-done.44.refs_2_ = bf16[512,2048]{1,0:T(8,128)(2,1)} collective-permute-done((bf16[512,2048]{1,0:T(8,128)(2,1)}, bf16[512,2048]{1,0:T(8,128)(2,1)}, u32[]{:S(2)}, u32[]{:S(2)}) %collective-permute-start.44) | collective-permute-done | bytes 2097184 | tf_op jit(solution)/shard_map/ppermute | solution.py:120
  947.5 37.6 %collective-permute-done.45.refs_3_ = bf16[512,2048]{1,0:T(8,128)(2,1)} collective-permute-done((bf16[512,2048]{1,0:T(8,128)(2,1)}, bf16[512,2048]{1,0:T(8,128)(2,1)}, u32[]{:S(2)}, u32[]{:S(2)}) %collective-permute-start.45) | collective-permute-done | bytes 2097184 | tf_op jit(solution)/shard_map/ppermute | solution.py:121
  990.9 5.5 add_convert_fusion.9
  996.9 5.1 convolution_convert_fusion.1
  1014.3 26.8 %collective-permute-done.60.refs_3_ = bf16[128,2560]{1,0:T(8,128)(2,1)S(1)} collective-permute-done((bf16[128,2560]{1,0:T(8,128)(2,1)S(1)}, bf16[128,2560]{1,0:T(8,128)(2,1)S(1)}, u32[]{:S(2)}, u32[]{:S(2)}) %collective-permute-start.60) | collective-permute-done | bytes 655392 | tf_op jit(solution)/shard_map/ppermute | solution.py:43
  1058.4 48.0 %collective-permute-done.47.refs_2_.refs_3_ = bf16[512,2048]{1,0:T(8,128)(2,1)S(1)} collective-permute-done((bf16[512,2048]{1,0:T(8,128)(2,1)}, bf16[512,2048]{1,0:T(8,128)(2,1)S(1)}, u32[]{:S(2)}, u32[]{:S(2)}) %collective-permute-start.47) | collective-permute-done | bytes 2097184 | tf_op jit(solution)/shard_map/ppermute | solution.py:121
  1114.6 10.0 collective-permute-done.64.refs_4_
  1135.4 6.9 collective-permute-done.69
  1155.6 6.3 collective-permute-done.51
  1199.2 93.8 %collective-permute-done.49 = bf16[512,2048]{1,0:T(8,128)(2,1)} collective-permute-done((bf16[512,2048]{1,0:T(8,128)(2,1)S(1)}, bf16[512,2048]{1,0:T(8,128)(2,1)}, u32[]{:S(2)}, u32[]{:S(2)}) %collective-permute-start.49) | collective-permute-done | bytes 2097184 | tf_op jit(solution)/shard_map/ppermute | solution.py:121
  1301.1 36.6 %all-gather.25.cloned.1.call-done = bf16[1024,2048]{1,0:T(8,128)(2,1)} async-done(((bf16[256,2048]{1,0:T(8,128)(2,1)}), bf16[1024,2048]{1,0:T(8,128)(2,1)}) %all-gather.25.cloned.1.call-update) | async-done | bytes 4194320 | tf_op jit(solution)/shard_map/all_gather | solution.py:592
  1337.7 7.5 pad_maximum_fusion
  1345.2 8.4 copy.140
  (680 shorter events, 445.3 us)
Async XLA Ops:
  7.2 86.0 %all-gather.17.cloned.1.call-start = ((), (), s32[]{:S(2)}) async-start(), calls=%async_computation.12 | async-start | bytes 1638400 | tf_op jit(solution)/shard_map/all_gather | solution.py:431
  10.3 37.7 %collective-permute-start.2 = (bf16[26752]{0:T(1024)(128)(2,1)S(1)}, bf16[26752]{0:T(1024)(128)(2,1)S(1)}, u32[]{:S(2)}, u32[]{:S(2)}) collective-permute-start(bf16[26752]{0:T(1024)(128)(2,1)S(1)} %dynamic-update-slice.16), channel_id=1, source_target_pairs={{0,1},{1,2},{2,3},{3,0},{4,5},{5,6},{6,7},{7,4},{8,9},{9,10},{10,1... | collective-permute-start | bytes 160520 | tf_op jit(solution)/shard_map/ppermute | solution.py:107
  13.4 35.2 %collective-permute-start.1 = (bf16[26752]{0:T(1024)(128)(2,1)S(1)}, bf16[26752]{0:T(1024)(128)(2,1)S(1)}, u32[]{:S(2)}, u32[]{:S(2)}) collective-permute-start(bf16[26752]{0:T(1024)(128)(2,1)S(1)} %dynamic-update-slice.16), channel_id=1, source_target_pairs={{0,2},{1,3},{2,0},{3,1},{4,6},{5,7},{6,4},{7,5},{8,10},{9,11},{10,... | collective-permute-start | bytes 160520 | tf_op jit(solution)/shard_map/ppermute | solution.py:107
  15.9 33.4 %collective-permute-start = (bf16[26752]{0:T(1024)(128)(2,1)S(1)}, bf16[26752]{0:T(1024)(128)(2,1)S(1)}, u32[]{:S(2)}, u32[]{:S(2)}) collective-permute-start(bf16[26752]{0:T(1024)(128)(2,1)S(1)} %dynamic-update-slice.16), channel_id=1, source_target_pairs={{0,3},{1,0},{2,1},{3,2},{4,7},{5,4},{6,5},{7,6},{8,11},{9,8},{10,9... | collective-permute-start | bytes 160520 | tf_op jit(solution)/shard_map/ppermute | solution.py:107
  19.2 114.9 %all-gather.19.cloned.1.call-start = ((), (), s32[]{:S(2)}) async-start(), calls=%async_computation.13 | async-start | bytes 1638400 | tf_op jit(solution)/shard_map/all_gather | solution.py:431
  22.8 75.0 %collective-permute-start.6 = (bf16[128,3072]{1,0:T(8,128)(2,1)}, bf16[128,3072]{1,0:T(8,128)(2,1)}, u32[]{:S(2)}, u32[]{:S(2)}) collective-permute-start(bf16[128,3072]{1,0:T(8,128)(2,1)} %get-tuple-element.213), channel_id=1, source_target_pairs={{0,8},{4,12},{8,0},{12,4},{16,24},{20,28},{24,16},{28,20},{1,9},{5... | collective-permute-start | bytes 2359304 | tf_op jit(solution)/shard_map/ppermute | solution.py:43
  24.3 73.5 %collective-permute-start.7 = (bf16[128,3072]{1,0:T(8,128)(2,1)}, bf16[128,3072]{1,0:T(8,128)(2,1)}, u32[]{:S(2)}, u32[]{:S(2)}) collective-permute-start(bf16[128,3072]{1,0:T(8,128)(2,1)} %get-tuple-element.212), channel_id=1, source_target_pairs={{0,16},{4,20},{8,24},{12,28},{16,0},{20,4},{24,8},{28,12},{1,17},{... | collective-permute-start | bytes 2359304 | tf_op jit(solution)/shard_map/ppermute | solution.py:43
  48.1 49.7 %collective-permute-start.8 = (bf16[128,1536]{1,0:T(8,128)(2,1)}, bf16[128,1536]{1,0:T(8,128)(2,1)}, u32[]{:S(2)}, u32[]{:S(2)}) collective-permute-start(bf16[128,1536]{1,0:T(8,128)(2,1)} %get-tuple-element.227), channel_id=1, source_target_pairs={{0,8},{4,12},{8,0},{12,4},{16,24},{20,28},{24,16},{28,20},{1,9},{5... | collective-permute-start | bytes 1179656 | tf_op jit(solution)/shard_map/ppermute | solution.py:43
  48.6 49.2 %collective-permute-start.9 = (bf16[128,1536]{1,0:T(8,128)(2,1)}, bf16[128,1536]{1,0:T(8,128)(2,1)}, u32[]{:S(2)}, u32[]{:S(2)}) collective-permute-start(bf16[128,1536]{1,0:T(8,128)(2,1)} %get-tuple-element.226), channel_id=1, source_target_pairs={{0,16},{4,20},{8,24},{12,28},{16,0},{20,4},{24,8},{28,12},{1,17},{... | collective-permute-start | bytes 1179656 | tf_op jit(solution)/shard_map/ppermute | solution.py:43
  67.4 19.0 %collective-permute-start.5 = (bf16[4,4,26752]{2,1,0:T(4,128)(2,1)S(1)}, bf16[4,4,26752]{2,1,0:T(4,128)(2,1)S(1)}, u32[]{:S(2)}, u32[]{:S(2)}) collective-permute-start(bf16[4,4,26752]{2,1,0:T(4,128)(2,1)S(1)} %pad_maximum_fusion.35), channel_id=1, source_target_pairs={{0,16},{4,20},{8,24},{12,28},{16,0},{20,4},{24,8},{28,12},{1,17},{... | collective-permute-start | bytes 2568200 | tf_op jit(solution)/shard_map/ppermute | solution.py:43
  104.6 162.2 %all-gather.21.cloned.1.call-start = ((), (), s32[]{:S(2)}) async-start(), calls=%async_computation.14 | async-start | bytes 1638400 | tf_op jit(solution)/shard_map/all_gather | solution.py:431
  114.8 30.4 %collective-permute-start.11 = (bf16[256,2560]{1,0:T(8,128)(2,1)}, bf16[256,2560]{1,0:T(8,128)(2,1)}, u32[]{:S(2)}, u32[]{:S(2)}) collective-permute-start(bf16[256,2560]{1,0:T(8,128)(2,1)} %pad_maximum_fusion.26), channel_id=1, source_target_pairs={{0,16},{4,20},{8,24},{12,28},{16,0},{20,4},{24,8},{28,12},{1,17},{... | collective-permute-start | bytes 3932168 | tf_op jit(solution)/shard_map/ppermute | solution.py:43
  120.6 27.7 %collective-permute-start.13 = (bf16[256,2560]{1,0:T(8,128)(2,1)}, bf16[256,2560]{1,0:T(8,128)(2,1)}, u32[]{:S(2)}, u32[]{:S(2)}) collective-permute-start(bf16[256,2560]{1,0:T(8,128)(2,1)} %pad_maximum_fusion.27), channel_id=1, source_target_pairs={{0,8},{4,12},{8,0},{12,4},{16,24},{20,28},{24,16},{28,20},{1,9},{5... | collective-permute-start | bytes 3932168 | tf_op jit(solution)/shard_map/ppermute | solution.py:43
  156.6 26.0 %collective-permute-start.16 = (bf16[1024,2560]{1,0:T(8,128)(2,1)}, bf16[1024,2560]{1,0:T(8,128)(2,1)}, u32[]{:S(2)}, u32[]{:S(2)}) collective-permute-start(bf16[1024,2560]{1,0:T(8,128)(2,1)} %constant_dynamic-update-slice_fusion.1), channel_id=1, source_target_pairs={{0,4},{4,0},{8,12},{12,8},{16,20},{20,16},{24,28},{28,24},{1,5},{5... | collective-permute-start | bytes 15728648 | tf_op jit(solution)/shard_map/ppermute | solution.py:43
  162.9 17.4 %collective-permute-start.14 = (bf16[128,2560]{1,0:T(8,128)(2,1)}, bf16[128,2560]{1,0:T(8,128)(2,1)S(1)}, u32[]{:S(2)}, u32[]{:S(2)}) collective-permute-start(bf16[128,2560]{1,0:T(8,128)(2,1)} %get-tuple-element.64), channel_id=1, source_target_pairs={{0,8},{4,12},{8,0},{12,4},{16,24},{20,28},{24,16},{28,20},{1,9},{5... | collective-permute-start | bytes 1966088 | tf_op jit(solution)/shard_map/ppermute | solution.py:43
  189.8 36.0 %collective-permute-start.17 = (bf16[256,2560]{1,0:T(8,128)(2,1)}, bf16[256,2560]{1,0:T(8,128)(2,1)S(1)}, u32[]{:S(2)}, u32[]{:S(2)}) collective-permute-start(bf16[256,2560]{1,0:T(8,128)(2,1)} %get-tuple-element.68), channel_id=1, source_target_pairs={{0,16},{4,20},{8,24},{12,28},{16,0},{20,4},{24,8},{28,12},{1,17},{... | collective-permute-start | bytes 3932168 | tf_op jit(solution)/shard_map/ppermute | solution.py:43
  191.6 36.1 %collective-permute-start.18 = (bf16[256,2560]{1,0:T(8,128)(2,1)}, bf16[256,2560]{1,0:T(8,128)(2,1)}, u32[]{:S(2)}, u32[]{:S(2)}) collective-permute-start(bf16[256,2560]{1,0:T(8,128)(2,1)} %get-tuple-element.69), channel_id=1, source_target_pairs={{0,8},{4,12},{8,0},{12,4},{16,24},{20,28},{24,16},{28,20},{1,9},{5... | collective-permute-start | bytes 3932168 | tf_op jit(solution)/shard_map/ppermute | solution.py:43
  235.8 61.5 %collective-permute-start.19 = (bf16[1024,2560]{1,0:T(8,128)(2,1)}, bf16[1024,2560]{1,0:T(8,128)(2,1)}, u32[]{:S(2)}, u32[]{:S(2)}) collective-permute-start(bf16[1024,2560]{1,0:T(8,128)(2,1)} %constant_dynamic-update-slice_fusion.3), channel_id=1, source_target_pairs={{0,4},{4,0},{8,12},{12,8},{16,20},{20,16},{24,28},{28,24},{1,5},{5... | collective-permute-start | bytes 15728648 | tf_op jit(solution)/shard_map/ppermute | solution.py:43
  236.8 224.8 %all-gather.13.cloned.1.call-start = ((), (), s32[]{:S(2)}) async-start(), calls=%async_computation.5 | async-start | bytes 5242880 | tf_op jit(solution)/shard_map/all_gather | solution.py:498
  307.2 29.1 %collective-permute-start.25 = (bf16[256,2560]{1,0:T(8,128)(2,1)}, bf16[256,2560]{1,0:T(8,128)(2,1)S(1)}, u32[]{:S(2)}, u32[]{:S(2)}) collective-permute-start(bf16[256,2560]{1,0:T(8,128)(2,1)} %get-tuple-element.76), channel_id=1, source_target_pairs={{0,16},{4,20},{8,24},{12,28},{16,0},{20,4},{24,8},{28,12},{1,17},{... | collective-permute-start | bytes 3932168 | tf_op jit(solution)/shard_map/ppermute | solution.py:43
  308.7 31.1 %collective-permute-start.26 = (bf16[256,2560]{1,0:T(8,128)(2,1)}, bf16[256,2560]{1,0:T(8,128)(2,1)S(1)}, u32[]{:S(2)}, u32[]{:S(2)}) collective-permute-start(bf16[256,2560]{1,0:T(8,128)(2,1)} %get-tuple-element.77), channel_id=1, source_target_pairs={{0,8},{4,12},{8,0},{12,4},{16,24},{20,28},{24,16},{28,20},{1,9},{5... | collective-permute-start | bytes 3932168 | tf_op jit(solution)/shard_map/ppermute | solution.py:43
  347.0 17.3 %collective-permute-start.27 = (bf16[1024,2560]{1,0:T(8,128)(2,1)}, bf16[1024,2560]{1,0:T(8,128)(2,1)}, u32[]{:S(2)}, u32[]{:S(2)}) collective-permute-start(bf16[1024,2560]{1,0:T(8,128)(2,1)} %constant_dynamic-update-slice_fusion.5), channel_id=1, source_target_pairs={{0,4},{4,0},{8,12},{12,8},{16,20},{20,16},{24,28},{28,24},{1,5},{5... | collective-permute-start | bytes 15728648 | tf_op jit(solution)/shard_map/ppermute | solution.py:43
  354.9 36.2 %collective-permute-start.28 = (bf16[256,3072]{1,0:T(8,128)(2,1)}, bf16[256,3072]{1,0:T(8,128)(2,1)}, u32[]{:S(2)}, u32[]{:S(2)}) collective-permute-start(bf16[256,3072]{1,0:T(8,128)(2,1)} %get-tuple-element.80), channel_id=1, source_target_pairs={{0,16},{4,20},{8,24},{12,28},{16,0},{20,4},{24,8},{28,12},{1,17},{... | collective-permute-start | bytes 4718600 | tf_op jit(solution)/shard_map/ppermute | solution.py:43
  356.6 38.3 %collective-permute-start.29 = (bf16[256,3072]{1,0:T(8,128)(2,1)}, bf16[256,3072]{1,0:T(8,128)(2,1)}, u32[]{:S(2)}, u32[]{:S(2)}) collective-permute-start(bf16[256,3072]{1,0:T(8,128)(2,1)} %get-tuple-element.81), channel_id=1, source_target_pairs={{0,8},{4,12},{8,0},{12,4},{16,24},{20,28},{24,16},{28,20},{1,9},{5... | collective-permute-start | bytes 4718600 | tf_op jit(solution)/shard_map/ppermute | solution.py:43
  373.3 158.0 %all-gather.15.cloned.1.call-start = ((), (), s32[]{:S(2)}) async-start(), calls=%async_computation.7 | async-start | bytes 5242880 | tf_op jit(solution)/shard_map/all_gather | solution.py:498
  404.1 51.2 %collective-permute-start.30 = (bf16[1024,3072]{1,0:T(8,128)(2,1)}, bf16[1024,3072]{1,0:T(8,128)(2,1)}, u32[]{:S(2)}, u32[]{:S(2)}) collective-permute-start(bf16[1024,3072]{1,0:T(8,128)(2,1)} %pad_maximum_fusion.1), channel_id=1, source_target_pairs={{0,4},{4,0},{8,12},{12,8},{16,20},{20,16},{24,28},{28,24},{1,5},{5... | collective-permute-start | bytes 18874376 | tf_op jit(solution)/shard_map/ppermute | solution.py:43
  408.2 20.2 %collective-permute-start.31 = (bf16[256,1536]{1,0:T(8,128)(2,1)}, bf16[256,1536]{1,0:T(8,128)(2,1)S(1)}, u32[]{:S(2)}, u32[]{:S(2)}) collective-permute-start(bf16[256,1536]{1,0:T(8,128)(2,1)} %get-tuple-element.84), channel_id=1, source_target_pairs={{0,16},{4,20},{8,24},{12,28},{16,0},{20,4},{24,8},{28,12},{1,17},{... | collective-permute-start | bytes 2359304 | tf_op jit(solution)/shard_map/ppermute | solution.py:43
  410.0 19.9 %collective-permute-start.32 = (bf16[256,1536]{1,0:T(8,128)(2,1)}, bf16[256,1536]{1,0:T(8,128)(2,1)S(1)}, u32[]{:S(2)}, u32[]{:S(2)}) collective-permute-start(bf16[256,1536]{1,0:T(8,128)(2,1)} %get-tuple-element.85), channel_id=1, source_target_pairs={{0,8},{4,12},{8,0},{12,4},{16,24},{20,28},{24,16},{28,20},{1,9},{5... | collective-permute-start | bytes 2359304 | tf_op jit(solution)/shard_map/ppermute | solution.py:43
  433.1 18.5 %collective-permute-start.33 = (bf16[1024,1536]{1,0:T(8,128)(2,1)}, bf16[1024,1536]{1,0:T(8,128)(2,1)}, u32[]{:S(2)}, u32[]{:S(2)}) collective-permute-start(bf16[1024,1536]{1,0:T(8,128)(2,1)} %pad_maximum_fusion.6), channel_id=1, source_target_pairs={{0,4},{4,0},{8,12},{12,8},{16,20},{20,16},{24,28},{28,24},{1,5},{5... | collective-permute-start | bytes 9437192 | tf_op jit(solution)/shard_map/ppermute | solution.py:43
  446.6 241.1 %reduce-scatter.6.cloned.1.call-start = ((), (), s32[]{:S(2)}) async-start(), calls=%async_computation.6 | async-start | bytes 5242880 | tf_op jit(solution)/shard_map/reduce_scatter | solution.py:507
  517.3 179.2 %reduce-scatter.8.cloned.1.call-start = ((), (), s32[]{:S(2)}) async-start(), calls=%async_computation.8 | async-start | bytes 5242880 | tf_op jit(solution)/shard_map/reduce_scatter | solution.py:507
  577.8 76.3 %collective-permute-start.34 = (bf16[1024,1536]{1,0:T(8,128)(2,1)}, bf16[1024,1536]{1,0:T(8,128)(2,1)}, u32[]{:S(2)}, u32[]{:S(2)}) collective-permute-start(bf16[1024,1536]{1,0:T(8,128)(2,1)} %add_convert_fusion.2), channel_id=1, source_target_pairs={{0,4},{4,0},{8,12},{12,8},{16,20},{20,16},{24,28},{28,24},{1,5},{5... | collective-permute-start | bytes 9437192 | tf_op jit(solution)/shard_map/ppermute | solution.py:43
  602.6 78.8 %collective-permute-start.35 = (bf16[1024,3072]{1,0:T(8,128)(2,1)}, bf16[1024,3072]{1,0:T(8,128)(2,1)}, u32[]{:S(2)}, u32[]{:S(2)}) collective-permute-start(bf16[1024,3072]{1,0:T(8,128)(2,1)} %add_convert_fusion), channel_id=1, source_target_pairs={{0,4},{4,0},{8,12},{12,8},{16,20},{20,16},{24,28},{28,24},{1,5},{5... | collective-permute-start | bytes 18874376 | tf_op jit(solution)/shard_map/ppermute | solution.py:43
  620.9 190.9 %reduce-scatter.10.cloned.1.call-start = ((), (), s32[]{:S(2)}) async-start(), calls=%async_computation.9 | async-start | bytes 5242880 | tf_op jit(solution)/shard_map/reduce_scatter | solution.py:532
  656.1 19.5 %collective-permute-start.37 = (bf16[256,1536]{1,0:T(8,128)(2,1)S(1)}, bf16[256,1536]{1,0:T(8,128)(2,1)S(1)}, u32[]{:S(2)}, u32[]{:S(2)}) collective-permute-start(bf16[256,1536]{1,0:T(8,128)(2,1)S(1)} %get-tuple-element.203.refs_3_), channel_id=1, source_target_pairs={{0,8},{4,12},{8,0},{12,4},{16,24},{20,28},{24,16},{28,20},{1,9},{5... | collective-permute-start | bytes 2359304 | tf_op jit(solution)/shard_map/ppermute | solution.py:43
  657.6 19.3 %collective-permute-start.36 = (bf16[256,1536]{1,0:T(8,128)(2,1)S(1)}, bf16[256,1536]{1,0:T(8,128)(2,1)}, u32[]{:S(2)}, u32[]{:S(2)}) collective-permute-start(bf16[256,1536]{1,0:T(8,128)(2,1)S(1)} %get-tuple-element.204.refs_2_), channel_id=1, source_target_pairs={{0,16},{4,20},{8,24},{12,28},{16,0},{20,4},{24,8},{28,12},{1,17},{... | collective-permute-start | bytes 2359304 | tf_op jit(solution)/shard_map/ppermute | solution.py:43
  678.8 28.9 %collective-permute-start.73 = (bf16[128,1536]{1,0:T(8,128)(2,1)S(1)}, bf16[128,1536]{1,0:T(8,128)(2,1)S(1)}, u32[]{:S(2)}, u32[]{:S(2)}) collective-permute-start(bf16[128,1536]{1,0:T(8,128)(2,1)S(1)} %get-tuple-element.202.refs_1_), channel_id=1, source_target_pairs={{0,8},{4,12},{8,0},{12,4},{16,24},{20,28},{24,16},{28,20},{1,9},{5... | collective-permute-start | bytes 1179656 | tf_op jit(solution)/shard_map/ppermute | solution.py:43
  679.9 27.8 %collective-permute-start.74 = (bf16[128,1536]{1,0:T(8,128)(2,1)S(1)}, bf16[128,1536]{1,0:T(8,128)(2,1)S(1)}, u32[]{:S(2)}, u32[]{:S(2)}) collective-permute-start(bf16[128,1536]{1,0:T(8,128)(2,1)S(1)} %get-tuple-element.201.refs_2_), channel_id=1, source_target_pairs={{0,16},{4,20},{8,24},{12,28},{16,0},{20,4},{24,8},{28,12},{1,17},{... | collective-permute-start | bytes 1179656 | tf_op jit(solution)/shard_map/ppermute | solution.py:43
  686.1 36.4 %collective-permute-start.39 = (bf16[256,3072]{1,0:T(8,128)(2,1)}, bf16[256,3072]{1,0:T(8,128)(2,1)}, u32[]{:S(2)}, u32[]{:S(2)}) collective-permute-start(bf16[256,3072]{1,0:T(8,128)(2,1)} %get-tuple-element.175.refs_5_), channel_id=1, source_target_pairs={{0,8},{4,12},{8,0},{12,4},{16,24},{20,28},{24,16},{28,20},{1,9},{5... | collective-permute-start | bytes 4718600 | tf_op jit(solution)/shard_map/ppermute | solution.py:43
  687.1 36.6 %collective-permute-start.38 = (bf16[256,3072]{1,0:T(8,128)(2,1)}, bf16[256,3072]{1,0:T(8,128)(2,1)}, u32[]{:S(2)}, u32[]{:S(2)}) collective-permute-start(bf16[256,3072]{1,0:T(8,128)(2,1)} %get-tuple-element.176.refs_4_), channel_id=1, source_target_pairs={{0,16},{4,20},{8,24},{12,28},{16,0},{20,4},{24,8},{28,12},{1,17},{... | collective-permute-start | bytes 4718600 | tf_op jit(solution)/shard_map/ppermute | solution.py:43
  696.5 288.9 %all-gather.23.cloned.1.call-start = ((), (), s32[]{:S(2)}) async-start(), calls=%async_computation.15 | async-start | bytes 5242880 | tf_op jit(solution)/shard_map/all_gather | solution.py:578
  726.9 76.8 %collective-permute-start.71 = (bf16[128,3072]{1,0:T(8,128)(2,1)S(1)}, bf16[128,3072]{1,0:T(8,128)(2,1)S(1)}, u32[]{:S(2)}, u32[]{:S(2)}) collective-permute-start(bf16[128,3072]{1,0:T(8,128)(2,1)S(1)} %get-tuple-element.174.refs_3_), channel_id=1, source_target_pairs={{0,8},{4,12},{8,0},{12,4},{16,24},{20,28},{24,16},{28,20},{1,9},{5... | collective-permute-start | bytes 2359304 | tf_op jit(solution)/shard_map/ppermute | solution.py:43
  727.5 76.2 %collective-permute-start.72 = (bf16[128,3072]{1,0:T(8,128)(2,1)S(1)}, bf16[128,3072]{1,0:T(8,128)(2,1)}, u32[]{:S(2)}, u32[]{:S(2)}) collective-permute-start(bf16[128,3072]{1,0:T(8,128)(2,1)S(1)} %get-tuple-element.173.refs_4_), channel_id=1, source_target_pairs={{0,16},{4,20},{8,24},{12,28},{16,0},{20,4},{24,8},{28,12},{1,17},{... | collective-permute-start | bytes 2359304 | tf_op jit(solution)/shard_map/ppermute | solution.py:43
  775.4 78.0 %collective-permute-start.56 = (bf16[1024,2560]{1,0:T(8,128)(2,1)}, bf16[1024,2560]{1,0:T(8,128)(2,1)}, u32[]{:S(2)}, u32[]{:S(2)}) collective-permute-start(bf16[1024,2560]{1,0:T(8,128)(2,1)} %convolution_convert_fusion.4), channel_id=1, source_target_pairs={{0,4},{4,0},{8,12},{12,8},{16,20},{20,16},{24,28},{28,24},{1,5},{5... | collective-permute-start | bytes 15728648 | tf_op jit(solution)/shard_map/ppermute | solution.py:43
  861.7 77.9 %collective-permute-start.44 = (bf16[512,2048]{1,0:T(8,128)(2,1)}, bf16[512,2048]{1,0:T(8,128)(2,1)}, u32[]{:S(2)}, u32[]{:S(2)}) collective-permute-start(bf16[512,2048]{1,0:T(8,128)(2,1)} %permute.8.refs_2_), channel_id=1, source_target_pairs={{0,1},{1,2},{2,3},{4,5},{5,6},{6,7},{8,9},{9,10},{10,11},{12,13},{... | collective-permute-start | bytes 6291464 | tf_op jit(solution)/shard_map/ppermute | solution.py:120
  868.3 116.8 %collective-permute-start.45 = (bf16[512,2048]{1,0:T(8,128)(2,1)}, bf16[512,2048]{1,0:T(8,128)(2,1)}, u32[]{:S(2)}, u32[]{:S(2)}) collective-permute-start(bf16[512,2048]{1,0:T(8,128)(2,1)} %permute.8.refs_2_), channel_id=1, source_target_pairs={{1,0},{2,1},{3,2},{5,4},{6,5},{7,6},{9,8},{10,9},{11,10},{13,12},{... | collective-permute-start | bytes 6291464 | tf_op jit(solution)/shard_map/ppermute | solution.py:121
  872.9 289.5 %reduce-scatter.12.cloned.1.call-start = ((), (), s32[]{:S(2)}) async-start(), calls=%async_computation.10 | async-start | bytes 5242880 | tf_op jit(solution)/shard_map/reduce_scatter | solution.py:587
  895.8 113.3 %collective-permute-start.66 = (bf16[1024,2560]{1,0:T(8,128)(2,1)}, bf16[1024,2560]{1,0:T(8,128)(2,1)}, u32[]{:S(2)}, u32[]{:S(2)}) collective-permute-start(bf16[1024,2560]{1,0:T(8,128)(2,1)} %convolution_convert_fusion), channel_id=1, source_target_pairs={{0,4},{4,0},{8,12},{12,8},{16,20},{20,16},{24,28},{28,24},{1,5},{5... | collective-permute-start | bytes 15728648 | tf_op jit(solution)/shard_map/ppermute | solution.py:43
  895.8 89.7 %collective-permute-start.58 = (bf16[256,2560]{1,0:T(8,128)(2,1)}, bf16[256,2560]{1,0:T(8,128)(2,1)S(1)}, u32[]{:S(2)}, u32[]{:S(2)}) collective-permute-start(bf16[256,2560]{1,0:T(8,128)(2,1)} %get-tuple-element.101), channel_id=1, source_target_pairs={{0,8},{4,12},{8,0},{12,4},{16,24},{20,28},{24,16},{28,20},{1,9},{5... | collective-permute-start | bytes 3932168 | tf_op jit(solution)/shard_map/ppermute | solution.py:43
  897.3 88.2 %collective-permute-start.57 = (bf16[256,2560]{1,0:T(8,128)(2,1)}, bf16[256,2560]{1,0:T(8,128)(2,1)}, u32[]{:S(2)}, u32[]{:S(2)}) collective-permute-start(bf16[256,2560]{1,0:T(8,128)(2,1)} %get-tuple-element.100), channel_id=1, source_target_pairs={{0,16},{4,20},{8,24},{12,28},{16,0},{20,4},{24,8},{28,12},{1,17},{... | collective-permute-start | bytes 3932168 | tf_op jit(solution)/shard_map/ppermute | solution.py:43
  939.6 51.4 %collective-permute-start.61 = (bf16[1024,2560]{1,0:T(8,128)(2,1)}, bf16[1024,2560]{1,0:T(8,128)(2,1)}, u32[]{:S(2)}, u32[]{:S(2)}) collective-permute-start(bf16[1024,2560]{1,0:T(8,128)(2,1)} %convolution_convert_fusion.2), channel_id=1, source_target_pairs={{0,4},{4,0},{8,12},{12,8},{16,20},{20,16},{24,28},{28,24},{1,5},{5... | collective-permute-start | bytes 15728648 | tf_op jit(solution)/shard_map/ppermute | solution.py:43
  985.4 312.1 %reduce-scatter.14.cloned.1.call-start = ((), (), s32[]{:S(2)}) async-start(), calls=%async_computation.11 | async-start | bytes 4915200 | tf_op jit(solution)/shard_map/reduce_scatter | solution.py:604
  989.4 17.8 %collective-permute-start.59 = (bf16[128,2560]{1,0:T(8,128)(2,1)}, bf16[128,2560]{1,0:T(8,128)(2,1)S(1)}, u32[]{:S(2)}, u32[]{:S(2)}) collective-permute-start(bf16[128,2560]{1,0:T(8,128)(2,1)} %get-tuple-element.102), channel_id=1, source_target_pairs={{0,8},{4,12},{8,0},{12,4},{16,24},{20,28},{24,16},{28,20},{1,9},{5... | collective-permute-start | bytes 1966088 | tf_op jit(solution)/shard_map/ppermute | solution.py:43
  996.4 45.0 %collective-permute-start.62 = (bf16[256,2560]{1,0:T(8,128)(2,1)}, bf16[256,2560]{1,0:T(8,128)(2,1)S(1)}, u32[]{:S(2)}, u32[]{:S(2)}) collective-permute-start(bf16[256,2560]{1,0:T(8,128)(2,1)} %get-tuple-element.104), channel_id=1, source_target_pairs={{0,16},{4,20},{8,24},{12,28},{16,0},{20,4},{24,8},{28,12},{1,17},{... | collective-permute-start | bytes 3932168 | tf_op jit(solution)/shard_map/ppermute | solution.py:43
  996.6 44.8 %collective-permute-start.63 = (bf16[256,2560]{1,0:T(8,128)(2,1)}, bf16[256,2560]{1,0:T(8,128)(2,1)S(1)}, u32[]{:S(2)}, u32[]{:S(2)}) collective-permute-start(bf16[256,2560]{1,0:T(8,128)(2,1)} %get-tuple-element.105), channel_id=1, source_target_pairs={{0,8},{4,12},{8,0},{12,4},{16,24},{20,28},{24,16},{28,20},{1,9},{5... | collective-permute-start | bytes 3932168 | tf_op jit(solution)/shard_map/ppermute | solution.py:43
  1002.0 39.1 %collective-permute-start.60 = (bf16[128,2560]{1,0:T(8,128)(2,1)S(1)}, bf16[128,2560]{1,0:T(8,128)(2,1)S(1)}, u32[]{:S(2)}, u32[]{:S(2)}) collective-permute-start(bf16[128,2560]{1,0:T(8,128)(2,1)S(1)} %copy-done.79), channel_id=1, source_target_pairs={{0,16},{4,20},{8,24},{12,28},{16,0},{20,4},{24,8},{28,12},{1,17},{... | collective-permute-start | bytes 1966088 | tf_op jit(solution)/shard_map/ppermute | solution.py:43
  1007.2 51.2 %collective-permute-start.46 = (bf16[512,2048]{1,0:T(8,128)(2,1)}, bf16[512,2048]{1,0:T(8,128)(2,1)}, u32[]{:S(2)}, u32[]{:S(2)}) collective-permute-start(bf16[512,2048]{1,0:T(8,128)(2,1)} %collective-permute-done.44.refs_2_), channel_id=1, source_target_pairs={{1,2},{2,3},{5,6},{6,7},{9,10},{10,11},{13,14},{14,15},{17,18},{18... | collective-permute-start | bytes 6291464 | tf_op jit(solution)/shard_map/ppermute | solution.py:120
  1009.1 97.3 %collective-permute-start.47 = (bf16[512,2048]{1,0:T(8,128)(2,1)}, bf16[512,2048]{1,0:T(8,128)(2,1)S(1)}, u32[]{:S(2)}, u32[]{:S(2)}) collective-permute-start(bf16[512,2048]{1,0:T(8,128)(2,1)} %collective-permute-done.45.refs_3_), channel_id=1, source_target_pairs={{1,0},{2,1},{5,4},{6,5},{9,8},{10,9},{13,12},{14,13},{17,16},{18,1... | collective-permute-start | bytes 6291464 | tf_op jit(solution)/shard_map/ppermute | solution.py:121
  1041.1 109.0 %collective-permute-start.50 = (bf16[4,4,26752]{2,1,0:T(4,128)(2,1)}, bf16[4,4,26752]{2,1,0:T(4,128)(2,1)}, u32[]{:S(2)}, u32[]{:S(2)}) collective-permute-start(bf16[4,4,26752]{2,1,0:T(4,128)(2,1)} %slice.810), channel_id=1, source_target_pairs={{0,16},{4,20},{8,24},{12,28},{16,0},{20,4},{24,8},{28,12},{1,17},{... | collective-permute-start | bytes 2568200 | tf_op jit(solution)/shard_map/ppermute | solution.py:43
  1042.9 67.9 %collective-permute-start.68 = (bf16[256,2560]{1,0:T(8,128)(2,1)}, bf16[256,2560]{1,0:T(8,128)(2,1)S(1)}, u32[]{:S(2)}, u32[]{:S(2)}) collective-permute-start(bf16[256,2560]{1,0:T(8,128)(2,1)} %get-tuple-element.109), channel_id=1, source_target_pairs={{0,8},{4,12},{8,0},{12,4},{16,24},{20,28},{24,16},{28,20},{1,9},{5... | collective-permute-start | bytes 3932168 | tf_op jit(solution)/shard_map/ppermute | solution.py:43
  1043.1 67.6 %collective-permute-start.67 = (bf16[256,2560]{1,0:T(8,128)(2,1)}, bf16[256,2560]{1,0:T(8,128)(2,1)}, u32[]{:S(2)}, u32[]{:S(2)}) collective-permute-start(bf16[256,2560]{1,0:T(8,128)(2,1)} %get-tuple-element.108), channel_id=1, source_target_pairs={{0,16},{4,20},{8,24},{12,28},{16,0},{20,4},{24,8},{28,12},{1,17},{... | collective-permute-start | bytes 3932168 | tf_op jit(solution)/shard_map/ppermute | solution.py:43
  1150.0 187.6 %all-gather.25.cloned.1.call-start = ((), (), s32[]{:S(2)}) async-start(), calls=%async_computation.16 | async-start | bytes 5242880 | tf_op jit(solution)/shard_map/all_gather | solution.py:592
  1167.1 23.9 %collective-permute-start.48 = (bf16[512,2048]{1,0:T(8,128)(2,1)}, bf16[512,2048]{1,0:T(8,128)(2,1)}, u32[]{:S(2)}, u32[]{:S(2)}) collective-permute-start(bf16[512,2048]{1,0:T(8,128)(2,1)} %collective-permute-done.46.refs_1_.refs_2_), channel_id=1, source_target_pairs={{2,3},{6,7},{10,11},{14,15},{18,19},{22,23},{26,27},{30,31}} | collective-permute-start | bytes 6291464 | tf_op jit(solution)/shard_map/ppermute | solution.py:120
  1186.8 106.2 %collective-permute-start.49 = (bf16[512,2048]{1,0:T(8,128)(2,1)S(1)}, bf16[512,2048]{1,0:T(8,128)(2,1)}, u32[]{:S(2)}, u32[]{:S(2)}) collective-permute-start(bf16[512,2048]{1,0:T(8,128)(2,1)S(1)} %copy-done.16), channel_id=1, source_target_pairs={{1,0},{5,4},{9,8},{13,12},{17,16},{21,20},{25,24},{29,28}} | collective-permute-start | bytes 6291464 | tf_op jit(solution)/shard_map/ppermute | solution.py:121
  (155 other events, 1722.8 us)
Sparse Core Ops, SparseCore 0:
  19.3 31.0 all-gather.16
  104.7 29.2 all-gather.18
  236.9 29.8 all-gather.20
  373.4 77.0 all-gather.12
  451.9 79.2 all-gather.14
  533.4 75.2 reduce-scatter.5
  621.0 75.4 reduce-scatter.7
  698.7 78.5 reduce-scatter.9
  873.0 112.3 all-gather.22
  987.6 98.5 reduce-scatter.11
  1150.2 92.4 reduce-scatter.13
  1244.1 93.5 all-gather.24

commit v4 on v3

--- a/solution.py
+++ b/solution.py
@@ -28,7 +28,7 @@
     if not others:
         return list(values)
     place = pl.BlockSpec(memory_space=pl.ANY)
-    return pl.pallas_call(
+    call = pl.pallas_call(
         lambda *refs: None,
         in_specs=[place] * (len(values) + len(others)),
         out_specs=[place] * len(values),
@@ -36,37 +36,40 @@
         input_output_aliases={k: k for k in range(len(values))},
         compiler_params=pltpu.CompilerParams(vmem_limit_bytes=VMEM),
         name="fence",
-    )(*values, *others)
+    )
+    return list(call(*values, *others))
 
 
 def exchange(values, bit, size):
     return lax.ppermute(values, "dp", [(k, k ^ (1 << bit)) for k in range(size)])
 
 
-def orders(size, parts):
-    high = list(range(1, size.bit_length() - 1))
-    return [high, high[::-1]][:parts]
-
-
-def parts_of(rows):
-    return 2 if rows % 256 == 0 else 1
-
-
-def hop(pieces, turn, size):
-    got = [exchange(p, o[turn], size) for p, o in zip(pieces, orders(size, len(pieces)))]
-    return [jnp.concatenate([p, g]) for p, g in zip(pieces, got)], got
+def squared(size, rows):
+    return size == 8 and rows % 256 == 0
 
 
 def spread_begin(own, size, *before):
-    pieces, got = fence(jnp.split(own, parts_of(own.shape[0])), *before), ()
-    for turn in range(size.bit_length() - 3):
-        pieces, got = hop(pieces, turn, size)
-    return pieces, got
-
-
-def spread_end(pieces, size, before_last, before_core):
-    pieces, got = hop(fence(pieces, *before_last), size.bit_length() - 3, size)
-    half = jnp.concatenate(fence(pieces, *before_core))
+    (own,) = fence([own], *before)
+    if squared(size, own.shape[0]):
+        return [own, exchange(own, 1, size), exchange(own, 2, size)]
+    pieces = own
+    for bit in range(1, size.bit_length() - 2):
+        pieces = jnp.concatenate([pieces, exchange(pieces, bit, size)])
+    return [pieces]
+
+
+def spread_end(some, size, before_last, before_core):
+    if len(some) > 1:
+        own, by_x, by_y = some
+        unit = own.shape[0] // 2
+        by_x, by_y = fence([by_x, by_y], *before_last)
+        got = [exchange(by_x[:unit], 2, size), exchange(by_y[unit:], 1, size)]
+        low, high = fence(got, *before_core)
+        half = jnp.concatenate([own, by_x, high, low, by_y])
+    else:
+        (pieces,) = fence(some, *before_last)
+        got = [exchange(pieces, size.bit_length() - 2, size)]
+        half = jnp.concatenate([pieces] + fence(got, *before_core))
     return [half, exchange(half, 0, size)], got
 
 
@@ -79,27 +82,45 @@
 
 class Collect:
     def __init__(self, keep, send, size, d_own):
-        self.size = size
-        self.parts = parts_of(d_own)
-        got = exchange(send, 0, size)
-        self.terms = list(zip(jnp.split(keep, self.parts), jnp.split(got, self.parts)))
-        self.turn = size.bit_length() - 2
+        self.size, self.unit = size, d_own // 2
+        self.square = squared(size, d_own)
+        self.bit = size.bit_length() - 2
+        self.terms = [keep, exchange(send, 0, size)]
+        self.first = self.last = None
+
+    def rows(self, start, stop):
+        return [t[start * self.unit : stop * self.unit] for t in self.terms]
 
     def sources(self):
-        cut = self.terms[0][0].shape[0] // 2
-        return [add_all([t[cut:] for t in terms]) for terms in self.terms]
+        if not self.square:
+            cut = self.terms[0].shape[0] // 2
+            return [add_all([t[cut:] for t in self.terms])]
+        if self.first is None:
+            return [add_all(self.rows(3, 5)), add_all(self.rows(5, 7))]
+        by_x, by_y = self.first
+        return [add_all(self.rows(2, 3) + [by_y[: self.unit]]), add_all(self.rows(7, 8) + [by_x[self.unit :]])]
 
     def hop(self, sources):
-        self.turn -= 1
-        cut = sources[0].shape[0]
-        got = [exchange(v, o[self.turn], self.size) for v, o in zip(sources, orders(self.size, self.parts))]
-        self.terms = [[t[:cut] for t in terms] + [g] for terms, g in zip(self.terms, got)]
+        if not self.square:
+            got = exchange(sources[0], self.bit, self.size)
+            self.bit -= 1
+            self.terms = [t[: got.shape[0]] for t in self.terms] + [got]
+            return [got]
+        got = [exchange(v, bit, self.size) for v, bit in zip(sources, (1, 2))]
+        if self.first is None:
+            self.first = got
+        else:
+            self.last = got
         return got
 
     def finish(self):
-        while self.turn:
-            self.hop(self.sources())
-        return jnp.concatenate([add_all(terms) for terms in self.terms])
+        if not self.square:
+            while self.bit:
+                self.hop(self.sources())
+            return add_all(self.terms)
+        low = add_all(self.rows(0, 1) + [self.first[1][self.unit :], self.last[0]])
+        high = add_all(self.rows(1, 2) + [self.first[0][: self.unit], self.last[1]])
+        return jnp.concatenate([low, high])
 
 
 def z_shift(values, by, n, around=True):
@@ -152,17 +173,16 @@
 
 
 def basis(size, rows, place):
-    parts = parts_of(rows)
-    count = size // 2
-    masks, which = [], []
-    for core in range(2):
-        for part, order in enumerate(orders(size, parts)):
-            for q in range(count):
-                masks.append(core | sum(((q >> t) & 1) << b for t, b in enumerate(order)))
-                which.append(part)
-    table = (place ^ jnp.asarray(np.array(masks, np.int32))) * parts
-    table = table + jnp.asarray(np.array(which, np.int32))
-    spots = jnp.arange(len(masks), dtype=jnp.int32)
+    if squared(size, rows):
+        parts = 2
+        spots = [(core | mask, part) for core in range(2) for mask, part in
+                 ((0, 0), (0, 1), (2, 0), (2, 1), (6, 1), (6, 0), (4, 0), (4, 1))]
+    else:
+        parts = 1
+        spots = [(core | q << 1, 0) for core in range(2) for q in range(size // 2)]
+    masks, which = (jnp.asarray(np.array(v, np.int32)) for v in zip(*spots))
+    table = (place ^ masks) * parts + which
+    spots = jnp.arange(table.shape[0], dtype=jnp.int32)
     inverse = jnp.sum(jnp.where(table[None, :] == spots[:, None], spots[None, :], 0), axis=1)
     return table, inverse.astype(jnp.int32)
 
@@ -190,6 +210,26 @@
     )(table, values)
 
 
+def interleave_kernel(one_ref, two_ref, out_ref):
+    out_ref[0] = one_ref[...]
+    out_ref[1] = two_ref[...]
+
+
+def interleave(one, two):
+    n, rows, d_model = one.shape
+    spec = pl.BlockSpec((pl.squeezed, rows, d_model), lambda j: (j, 0, 0))
+    return pl.pallas_call(
+        interleave_kernel,
+        grid=(n,),
+        in_specs=[spec, spec],
+        out_specs=pl.BlockSpec((pl.squeezed, 2, rows, d_model), lambda j: (j, 0, 0, 0)),
+        out_shape=jax.ShapeDtypeStruct((n, 2, rows, d_model), one.dtype),
+        compiler_params=pltpu.CompilerParams(vmem_limit_bytes=VMEM),
+        cost_estimate=LITTLE,
+        name="interleave",
+    )(one, two)
+
+
 def permute_gain(values, table):
     lead = values.shape[0]
     return jnp.take(values.reshape(lead, table.shape[0], -1), table, axis=1).reshape(lead, -1)
@@ -209,11 +249,6 @@
         value = jnp.where(keep, value + decay * moved_value, value)
         decay = jnp.where(keep, decay * moved_decay, decay)
     return decay, value
-
-
-def gelu_parts(v):
-    c = np.float32(np.sqrt(2 / np.pi))
-    return jnp.tanh(c * (v + 0.044715 * v * v * v))
 
 
 def head_mask(head, at, width):
@@ -271,14 +306,23 @@
     lax.fori_loop(0, rows // (4 * SLAB), slab, (jnp.zeros((SLAB, width), F32), jnp.ones((SLAB, width), F32)))
 
 
-def back_scan_kernel(live_ref, pre_ref, grad_ref, decay_ref, lam_ref, reach_ref, edge_ref):
+def back_scan_kernel(
+    live_ref, pre_ref, grad_ref, decay_ref, state_ref, prod_ref, cin_ref, lam_ref, reach_ref, edge_ref, low_ref
+):
     rows, width = grad_ref.shape
     live = live_ref[0]
+    cin = cin_ref[:1, :]
+    c = np.float32(np.sqrt(2 / np.pi))
     for at in range(0, rows, ROWS):
         span = pl.ds(at, ROWS)
-        v = pre_ref[span, :]
-        act = 0.5 * v * (1.0 + gelu_parts(v))
-        lam_ref[span, :] = jnp.where(row_ids(ROWS, width, at) < live, grad_ref[span, :] * act, 0.0)
+        v, grad = pre_ref[span, :], grad_ref[span, :]
+        square = v * v
+        bend = jnp.tanh(v * (c + (c * 0.044715) * square))
+        rise = 0.5 + 0.5 * bend
+        slope = rise + 0.5 * v * (1.0 - bend * bend) * (c + (3 * c * 0.044715) * square)
+        grad = jnp.where(row_ids(ROWS, width, at) < live, grad, 0.0)
+        lam_ref[span, :] = grad * (v * rise)
+        low_ref[span, :] = (grad * (state_ref[span, :] + prod_ref[span, :] * cin) * slope).astype(BF)
     last = row_ids(SLAB, width, 0) == SLAB - 1
 
     def slab(k, carry):
@@ -427,20 +471,18 @@
     live_count = (lengths - turn * rows).astype(jnp.int32)
     live = (lax.iota(jnp.int32, rows)[:, None] < live_count).astype(F32)
 
-    def wide(own):
-        own = lax.all_gather(own, "tensor", axis=0)
-        return own.transpose(1, 0, 2).reshape(d_own, width)
-
-    z_rec = wide(w_rec.astype(BF))
+    def wide(owns):
+        own = lax.all_gather(jnp.stack(owns), "tensor", axis=0)
+        return [own[:, k].transpose(1, 0, 2).reshape(d_own, width) for k in range(len(owns))]
+
+    (z_rec,) = wide([w_rec.astype(BF)])
     own_gu = jnp.concatenate([w_mlp_in[0], w_mlp_in[1]], axis=1).astype(BF)
     own_dn = w_down.T.astype(BF)
+    some_gu = spread_begin(own_gu, size)
     small = [w_lru.transpose(2, 0, 1, 3).reshape(-1), chan.reshape(-1), gains.reshape(-1)]
     small = small_gather(jnp.concatenate(small).astype(BF), size, n)
-    z_gelu = wide(*fence([w_gelu.astype(BF)], z_rec))
-    z_out = wide(*fence([w_out.T.astype(BF)], z_gelu))
-    some_gu, came_gu = spread_begin(own_gu, size)
-    some_dn, came_dn = spread_begin(own_dn, size)
-    some_r, _ = spread_begin(z_rec, size, *came_gu, *came_dn)
+    z_gelu, z_out = wide(fence([w_gelu.astype(BF), w_out.T.astype(BF)], z_rec))
+    some_r = spread_begin(z_rec, size, *some_gu[1:])
 
     gain = small[0, :, -gains.size :].reshape(size, 2, d_own).transpose(1, 0, 2).reshape(2, d_model)
     gain = permute_gain(gain, table).astype(F32)
@@ -458,14 +500,14 @@
     first_rate = norm_rate(extended)
     first = (extended * first_rate * gain[0]).astype(BF)
     inputs, first_own, first_rate = extended[HALO:], first[HALO:], first_rate[HALO:]
-    cot = permute_rows(cotangent, table).reshape(n, 2, half, d_model)
+    cot = permute_rows(cotangent, *fence([table], *some_r[1:])).reshape(n, 2, half, d_model)
     cots = [cot[:, h].reshape(n * half, d_model) for h in range(2)]
     cut = d_model // 2
 
     keep = (rows, width, F32)
     dense = ((GROUP, 2 * GROUP), BF)
-    w_r, came_r = spread_end(some_r, size, (), (first, *cots, z_gelu))
-    some_g, _ = spread_begin(z_gelu, size, *came_r)
+    w_r, came_r = spread_end(some_r, size, (), (first, *cots, lru, par, z_gelu))
+    some_g = spread_begin(z_gelu, size, *came_r)
     rec_pre = wide_dot(first, w_r)
     conv, decay, ig, dg, state, prod = kernel_call(
         forward_kernel, live_count, [rec_pre, par, lru], [keep] * 6,
@@ -477,18 +519,18 @@
     for end in came[::-1]:
         carry = end[1:] + end[:1] * carry
     w_g, came_g = spread_end(some_g, size, (rec_pre,), (ends,))
-    some_o, _ = spread_begin(z_out, size, *came_g, ends)
+    some_o = spread_begin(z_out, size, *came_g, ends)
     branch_pre = wide_dot(first_own, w_g)
     recurrent = (state + prod * carry) * live
-    activated, gelu_pull = jax.vjp(jax.nn.gelu, branch_pre)
-    mixed = (activated * recurrent).astype(BF)
+    mixed = (jax.nn.gelu(branch_pre) * recurrent).astype(BF)
     w_o, came_o = spread_end(some_o, size, (branch_pre,), (mixed,))
     hidden = inputs + wide_back(mixed, w_o)
     second_rate = norm_rate(hidden)
     second_unit = hidden * second_rate
     second_own = (second_unit * gain[1]).astype(BF)
     w_gu, came_gu = spread_end(some_gu, size, came_o, (second_own,))
-    w_dn, _ = spread_end(some_dn, size, came_gu, ())
+    some_dn = spread_begin(own_dn, size, *came_gu)
+    w_dn, _ = spread_end(some_dn, size, (), ())
     w_gu, w_dn = jnp.concatenate(w_gu), jnp.concatenate(w_dn)
 
     hidden_units = w_dn.shape[1]
@@ -509,6 +551,7 @@
         products.append(product)
         grads.append(grad)
 
+    products, grads = [[*pair] for pair in zip(*[fence([p, g], shares[-1]) for p, g in zip(products, grads)])]
     shares = [dot(p, w_dn, ((1,), (1,))).astype(BF) for p in products]
 
     def by_rows(lefts, rights):
@@ -521,15 +564,14 @@
     sum_dn = by_rows(cots, products)
     sum_gu = by_rows(seconds, grads)
     sent_dn, sent_gu = sum_dn.sources(), sum_gu.sources()
-    grad_second = fence(grad_second, *sent_dn, *sent_gu)
-    sum_dn.hop(sent_dn)
-    sum_gu.hop(sent_gu)
+    grad_second = fence(grad_second, *sent_dn, *sent_gu, *shares)
+    came_mlp = sum_dn.hop(sent_dn) + sum_gu.hop(sent_gu)
 
     def mlp_result(h, mlp_sum):
         return permute_rows((hidden[h * half : (h + 1) * half] + mlp_sum.astype(F32)).astype(BF), inverse)
 
-    (share,) = fence([shares[0]], *grad_second)
-    mlp_sum = lax.psum_scatter(share, "tensor", scatter_dimension=0, tiled=True)
+    shares = fence(shares, *grad_second)
+    mlp_sums = [lax.psum_scatter(share, "tensor", scatter_dimension=0, tiled=True) for share in shares]
 
     grad_second = jnp.concatenate(grad_second).astype(F32)
     cot_own = lax.dynamic_index_in_dim(cot, turn, 0).reshape(rows, d_model).astype(F32)
@@ -542,24 +584,17 @@
         return Collect(parts[1], parts[0], size, d_own)
 
     grad_mixed = wide_dot(hidden_low, w_o)
-    lam, reach, edge = kernel_call(
-        back_scan_kernel, live_count, [branch_pre, grad_mixed, decay],
-        [keep, keep, (SLAB, width, F32)], [], "back_scan",
+    tall = jnp.broadcast_to
+    lam, reach, edge, pre_low = kernel_call(
+        back_scan_kernel, live_count, [branch_pre, grad_mixed, decay, state, prod, tall(carry, (SLAB, width))],
+        [keep, keep, (SLAB, width, F32), (rows, width, BF)], [], "back_scan",
     )
     edges = jnp.concatenate([prod[-1:], edge[:1]])
     came = [z_shift(edges, -k, n, False) for k in range(1, n)]
     arriving = jnp.zeros((1, width), F32)
     for end in came[::-1]:
         arriving = end[1:] + end[:1] * arriving
-    sum_o = by_cols(hidden_low, mixed)
-    sent_dn, sent_gu = sum_dn.sources(), sum_gu.sources()
-    (lam,) = fence([lam], *sent_dn, *sent_gu)
-    sum_dn.hop(sent_dn)
-    sum_gu.hop(sent_gu)
-    (grad_pre,) = gelu_pull(grad_mixed * recurrent)
-    pre_low = grad_pre.astype(BF)
-    first_part = wide_back(pre_low, w_g)
-    tall = jnp.broadcast_to
+    (lam,) = fence([lam], *came_mlp)
     drec, dpar, d_lru = kernel_call(
         backward_kernel, live_count,
         [rec_pre, par, lru, lam, reach, tall(arriving, (SLAB, width)), decay, conv, ig, dg, state, prod, tall(carry, (SLAB, width))],
@@ -567,41 +602,41 @@
         [((rows + HALO, GROUP), F32), ((rows + 2 * HALO, GROUP), F32), ((rows + SLAB, GROUP), F32), ((GROUP, 2 * GROUP), F32), dense],
         "recurrence_back",
     )
-    (edge_rows,) = fence([z_shift(drec[:HALO], -1, n, False)], mlp_sum)
+    (edge_rows,) = fence([z_shift(drec[:HALO], -1, n, False)], mlp_sums[0])
     rec_low = (drec[HALO:] + jnp.pad(edge_rows, ((rows - HALO, 0), (0, 0)))) * live
     rec_low = rec_low.astype(BF)
-    grad_first = first_part + wide_back(rec_low, w_r)
+    (pre_low,) = fence([pre_low], drec)
+    grad_first = wide_back(pre_low, w_g) + wide_back(rec_low, w_r)
     first_unit = inputs * first_rate
     gain_one = jnp.sum(grad_first * first_unit, axis=0)
     grad_tokens = grad_hidden + norm_back(grad_first, first_unit, first_rate, gain[0])
     grad_tokens = permute_rows(grad_tokens.astype(BF), inverse)
-    result_0 = lax.all_gather(mlp_result(0, mlp_sum), "tensor", axis=0)
-    sum_g = by_cols(first_own, pre_low)
-    sum_r = by_cols(first_own, rec_low)
-    d_lru, dpar = fence([d_lru, dpar], grad_tokens)
-    sent = fence(sum_o.sources(), grad_tokens)
     rounds = [line_round(grad_tokens, grad_tokens, 1, n)]
-    got_o = sum_o.hop(sent)
-    got_g = sum_g.hop(fence(sum_g.sources(), *got_o))
-    (share,) = fence([shares[1]], result_0, *rounds[0])
-    mlp_sum = lax.psum_scatter(share, "tensor", scatter_dimension=0, tiled=True)
-    got_o = sum_o.hop(fence(sum_o.sources(), *rounds[0]))
-    rounds.append(line_round(*rounds[0], 2, n))
-    got_r = sum_r.hop(fence(sum_r.sources(), *got_o, *got_g))
-    (mlp_sum,) = fence([mlp_sum], *rounds[1])
-    result_1 = lax.all_gather(mlp_result(1, mlp_sum), "tensor", axis=0)
-    got_g = sum_g.hop(fence(sum_g.sources(), *rounds[1]))
-    sum_r.hop(fence(sum_r.sources(), *got_r, *got_g))
+    (mixed,) = fence([mixed], grad_tokens)
+    sum_o = by_cols(hidden_low, mixed)
+    pre_low, rec_low = fence([pre_low, rec_low], sum_o.terms[1])
+    sum_g, sum_r = by_cols(first_own, pre_low), by_cols(first_own, rec_low)
+    results = [mlp_result(h, mlp_sum) for h, mlp_sum in enumerate(fence(mlp_sums, sum_o.terms[1]))]
+    got_o = sum_o.hop(fence(sum_o.sources(), *results))
+    result_0, result_1 = (lax.all_gather(result, "tensor", axis=0) for result in results)
+    rounds.append(line_round(*fence(rounds[0], *got_o), 2, n))
+    sum_o.hop(fence(sum_o.sources(), *rounds[0]))
+    got_g = sum_g.hop(fence(sum_g.sources(), *rounds[0]))
     for k in range(3, n):
-        rounds.append(line_round(*rounds[-1], k, n))
+        rounds.append(line_round(*fence(rounds[-1], result_0, *got_g), k, n))
+    sum_g.hop(fence(sum_g.sources(), *rounds[1]))
+    got_r = sum_r.hop(fence(sum_r.sources(), *rounds[1], *got_g))
+    d_lru, dpar = fence([d_lru, dpar], *rounds[1])
+    sum_r.hop(sum_r.sources())
+    if sum_dn.square:
+        sum_dn.hop(fence(sum_dn.sources(), *rounds[-1]))
+        sum_gu.hop(fence(sum_gu.sources(), *rounds[-1]))
     tokens_out = line_result(grad_tokens, rounds, n)
-    output = jnp.zeros((n, 2, half, d_model), BF)
-    output = lax.dynamic_update_slice(output, result_0[:, None], (0, 0, 0, 0))
-    output = lax.dynamic_update_slice(output, result_1[:, None], (0, 1, 0, 0))
-    output = output.reshape(n * rows, d_model)
+    output = interleave(*fence([result_0, result_1], *rounds[-1])).reshape(n * rows, d_model)
     g_gu, g_dn = sum_gu.finish().astype(F32), sum_dn.finish().astype(F32)
     owned = jnp.stack([total.finish().reshape(d_own, n, width // n) for total in (sum_o, sum_g, sum_r)])
-    owned = lax.psum_scatter(owned.transpose(2, 0, 1, 3), "tensor", scatter_dimension=0).astype(F32)
+    (owned,) = fence([owned.transpose(2, 0, 1, 3)], result_1)
+    owned = lax.psum_scatter(owned, "tensor", scatter_dimension=0).astype(F32)
     g_o, g_g, g_r = owned[0], owned[1], owned[2]
 
     d_gain = permute_gain(jnp.stack([gain_one, gain_two]), inverse)

time: 1370 us -> 1350 us (0.985)
  other arithmetic: 188 us -> 147 us
  local copies, waits for them, and re-layouts: 166 us -> 193 us
  waiting for transfers between devices: 514 us -> 492 us
    ppermute x3, waiting for transfers between devices: 179 us -> 92.9 us  [line_round(): lax.ppermute(left, 'tensor', [(s, s - 1) for s in range(1, n - k + 1)])]
    all_gather x5 -> x4, waiting for transfers between devices: 76.8 us -> 0.02 us  [the longest x2 0.02 us: wide(): own = lax.all_gather(jnp.stack(owns), 'tensor', axis=0)]
    concatenate x24 -> x5, other arithmetic: 54.9 us -> 10.6 us  [the longest x2 9.21 us: on_device(): grad = jnp.concatenate([grad_gate.astype(BF), grad_up.astype(BF)], axis=1)]
    all_gather x2, waiting for transfers between devices: 13.9 us -> 52.8 us  [on_device(): lax.all_gather(second_own[h * half:(h + 1) * half], 'tensor', axis=0, til...]
    unnamed x290 -> x352, local copies, waits for them, and re-layouts: 60.6 us -> 93.5 us
    ppermute x56, waiting for transfers between devices: 195 us -> 228 us  [exchange(): return lax.ppermute(values, 'dp', [(k, k ^ 1 << bit) for k in range(size)])]
    ppermute x3, waiting for transfers between devices: 36.8 us -> 64.8 us  [line_round(): lax.ppermute(right, 'tensor', [(s, s + 1) for s in range(k - 1, n - 1)])]
    reduce_scatter x2 -> x4, waiting for transfers between devices: 8.76 us -> 27.2 us  [on_device(): lax.psum_scatter(share, 'tensor', scatter_dimension=0, tiled=True)]
  transfers between devices with their start and end apart: 87 -> 86, of which waited for: 36 -> 40; matrix products, arithmetic and copies ran while one was open for 41% -> 42% of each run, Pallas kernels for 6% -> 7%
where the time goes in v4:
time: 1350 us; the launch traced here: 1340 us
  waiting for transfers between devices  492 us (36%)
  matrix products  302 us (22%)
  local copies, waits for them, and re-layouts  193 us (14%)
  other arithmetic  147 us (11%)
  starting transfers between devices  95.6 us (7%)
  Pallas kernels  91.9 us (7%)
  between operations  16.8 us (1%)
    dot_general x34, matrix products, dot(): lax.dot_general(left, right, (dims, ((), ())), preferred_element_type=F32)  302 us
    ppermute x56, waiting for transfers between devices, exchange(): return lax.ppermute(values, 'dp', [(k, k ^ 1 << bit) for k in range(size)])  228 us
    unnamed x352, local copies, waits for them, and re-layouts  93.5 us
    ppermute x3, waiting for transfers between devices, line_round(): lax.ppermute(left, 'tensor', [(s, s - 1) for s in range(1, n - k + 1)])  92.9 us
    ppermute x3, waiting for transfers between devices, line_round(): lax.ppermute(right, 'tensor', [(s, s + 1) for s in range(k - 1, n - 1)])  64.8 us
    pallas_call x3, Pallas kernels, kernel_call(): pl.pallas_call(body, grid_spec=pltpu.PrefetchScalarGridSpec(num_scalar_pr...  60 us
    convert_element_type x19, other arithmetic, add_all(): return total.astype(BF)  59.2 us
    all_gather x2, waiting for transfers between devices, on_device(): lax.all_gather(second_own[h * half:(h + 1) * half], 'tensor', axis=0, til...  52.8 us
  transfers between devices with their start and end apart: 86, of which 40 were waited for; matrix products, arithmetic and copies ran while one was open for 42% of the time, Pallas kernels for 7%

profile of v4, /device:TPU:0, one launch (start us, length us, event | category | flops | bytes accessed | tf_op | source)
XLA Modules:
  0.0 1338.6 jit_solution(14548165097627800140)
XLA Ops:
  43.9 15.1 %collective-permute-done.4 = bf16[2,4,26752]{2,1,0:T(4,128)(2,1)S(1)} collective-permute-done((bf16[2,4,26752]{2,1,0:T(4,128)(2,1)S(1)}, bf16[2,4,26752]{2,1,0:T(4,128)(2,1)S(1)}, u32[]{:S(2)}, u32[]{:S(2)}) %collective-permute-start.4) | collective-permute-done | bytes 428064 | tf_op jit(solution)/shard_map/ppermute | solution.py:44
  73.2 7.9 collective-permute-done.5
  112.2 4.9 reshape_transpose_reshape.3.refs_5_.w_ref
  123.5 12.0 collective-permute-done.8.refs_1_
  142.1 10.4 permute.6
  152.5 6.0 fusion.76
  189.0 7.3 convolution_add_fusion.refs_2_.pre_ref
  197.6 18.2 %recurrence.1 = (f32[512,2560]{1,0:T(8,128)}, f32[512,2560]{1,0:T(8,128)}, f32[512,2560]{1,0:T(8,128)}, f32[512,2560]{1,0:T(8,128)}, f32[512,2560]{1,0:T(8,128)}, /*index=5*/f32[512,2560]{1,0:T(8,128)}) custom-call(s32[1]{0:T(128)} %sub.46.live_ref, f32[528,2560]{1,0:T(8,128)} %convolution_add_fusion.refs_2_.pre_ref, ...), custom_call_target="tpu_custom_call" | custom-call | flops 1024 | bytes 1024 | tf_op jit(solution)/shard_map/recurrence/pallas_call | solution.py:424
  226.8 11.1 collective-permute-done.15.refs_0_.refs_1_
  245.3 5.5 collective-permute-start.20
  263.0 9.9 fusion.22
  272.9 13.4 collective-permute-done.21.refs_0_
  293.5 10.8 collective-permute-done.23.refs_0_.refs_2_
  329.1 10.3 collective-permute-done.26.refs_0_.refs_1_
  342.5 5.0 fusion.82
  361.2 18.1 %collective-permute-done.30 = bf16[256,1536]{1,0:T(8,128)(2,1)S(1)} collective-permute-done((bf16[256,1536]{1,0:T(8,128)(2,1)S(1)}, bf16[256,1536]{1,0:T(8,128)(2,1)S(1)}, u32[]{:S(2)}, u32[]{:S(2)}) %collective-permute-start.30) | collective-permute-done | bytes 786464 | tf_op jit(solution)/shard_map/ppermute | solution.py:44
  381.6 8.6 collective-permute-done.31
  391.4 5.6 collective-permute-done.33
  400.4 5.9 constant_dynamic-update-slice_fusion.21
  406.3 25.2 %all-gather.11.cloned.1.call-done = bf16[1024,2048]{1,0:T(8,128)(2,1)} async-done(((bf16[256,2048]{1,0:T(8,128)(2,1)}), bf16[1024,2048]{1,0:T(8,128)(2,1)}) %all-gather.11.cloned.1.call-update) | async-done | bytes 4194320 | tf_op jit(solution)/shard_map/all_gather | solution.py:540
  431.5 19.1 %fusion.83 = f32[1024,3072]{1,0:T(8,128)} fusion(bf16[1024,2048]{1,0:T(8,128)(2,1)} %all-gather.11.cloned.1.call-done, bf16[2048,3072]{1,0:T(8,128)(2,1)} %constant_dynamic-update-slice_fusion.21), kind=kOutput, calls=%fused_computation.297 | convolution fusion | flops 12884901888 | bytes 29360128 | tf_op jit(solution)/shard_map/dot_general | solution.py:24
  450.6 14.6 %fusion.6 = (bf16[1024,1536]{1,0:T(8,128)(2,1)S(1)}, bf16[1024,1536]{1,0:T(8,128)(2,1)S(1)}, bf16[1024,1536]{1,0:T(8,128)(2,1)}) fusion(f32[1024,3072]{1,0:T(8,128)} %fusion.83, bf16[1024,2048]{1,0:T(8,128)(2,1)S(1)} %bitcast.190, bf16[2048,1536]{1,0:T(8,128)(2,1)S(1)} %copy-done.114), kind=kOutput, calls=%fused_computation.18 | convolution fusion | flops 6483345408 | bytes 32505856 | tf_op jit(solution)/shard_map/dot_general | solution.py:24
  466.9 17.6 %convolution_convert_fusion.7.refs_1_ = bf16[1024,2048]{1,0:T(8,128)(2,1)} fusion(bf16[2048,3072]{1,0:T(8,128)(2,1)} %constant_dynamic-update-slice_fusion.21, bf16[1024,1536]{1,0:T(8,128)(2,1)S(1)} %get-tuple-element.207, bf16[1024,1536]{1,0:T(8,128)(2,1)S(1)} %get-tuple-element.206), kind=kOutput, calls=%fused_computation.75 | convolution fusion | flops 12899581952 | bytes 23068672 | tf_op jit(solution)/shard_map/dot_general | solution.py:24
  484.7 27.5 %all-gather.13.cloned.1.call-done.refs_0_ = bf16[1024,2048]{1,0:T(8,128)(2,1)} async-done(((bf16[256,2048]{1,0:T(8,128)(2,1)}), bf16[1024,2048]{1,0:T(8,128)(2,1)}) %all-gather.13.cloned.1.call-update) | async-done | bytes 4194320 | tf_op jit(solution)/shard_map/all_gather | solution.py:540
  512.3 19.1 %fusion.84 = f32[1024,3072]{1,0:T(8,128)} fusion(bf16[1024,2048]{1,0:T(8,128)(2,1)} %fence.49, bf16[2048,3072]{1,0:T(8,128)(2,1)} %constant_dynamic-update-slice_fusion.21), kind=kOutput, calls=%fused_computation.298 | convolution fusion | flops 12884901888 | bytes 29360128 | tf_op jit(solution)/shard_map/dot_general | solution.py:24
  531.4 16.6 %fusion.13 = (bf16[1024,1536]{1,0:T(8,128)(2,1)S(1)}, bf16[1024,1536]{1,0:T(8,128)(2,1)}, bf16[1024,1536]{1,0:T(8,128)(2,1)}) fusion(f32[1024,3072]{1,0:T(8,128)} %fusion.84, bf16[1024,2048]{1,0:T(8,128)(2,1)S(1)} %bitcast.187, bf16[2048,1536]{1,0:T(8,128)(2,1)} %copy-done.113), kind=kOutput, calls=%fused_computation.25 | convolution fusion | flops 6483345408 | bytes 32505856 | tf_op jit(solution)/shard_map/dot_general | solution.py:24
  551.7 18.8 %convolution_convert_fusion.6.refs_2_ = bf16[1024,2048]{1,0:T(8,128)(2,1)} fusion(bf16[2048,3072]{1,0:T(8,128)(2,1)} %constant_dynamic-update-slice_fusion.21, bf16[1024,1536]{1,0:T(8,128)(2,1)} %get-tuple-element.205, bf16[1024,1536]{1,0:T(8,128)(2,1)S(1)} %get-tuple-element.204), kind=kOutput, calls=%fused_computation.74 | convolution fusion | flops 12899581952 | bytes 23068672 | tf_op jit(solution)/shard_map/dot_general | solution.py:24
  572.4 5.5 pad_maximum_fusion.1.refs_1_
  577.9 7.5 fusion.37
  585.4 8.3 convolution_convert_fusion.9.refs_6_.refs_0_
  593.8 9.6 add_convert_fusion.2
  603.5 9.7 fusion.31
  613.2 11.9 add_convert_fusion
  625.6 11.0 fusion.34
  636.6 11.3 convolution_convert_fusion.8.refs_7_.refs_1_
  647.9 5.4 fusion.40
  653.3 7.1 add_convert_fusion.3
  660.3 10.2 add_convert_fusion.1
  691.8 5.6 fusion.49
  702.8 17.0 %back_scan.1 = (f32[512,2560]{1,0:T(8,128)}, f32[512,2560]{1,0:T(8,128)}, f32[8,2560]{1,0:T(8,128)}, bf16[512,2560]{1,0:T(8,128)(2,1)}) custom-call(s32[1]{0:T(128)} %sub.46.live_ref, f32[512,2560]{1,0:T(8,128)} %get-tuple-element.283.refs_2_.pre_ref, f32[512,2560]{1,0:T(8,128)} %convolution_add_fusion.1.grad_ref, f32[512,2560]{1,0:T(8,128)} %get-tuple-element.101.decay_ref, ...), custom_call_target="tpu_custom_call" | custom-call | flops 1024 | bytes 1024 | tf_op jit(solution)/shard_map/back_scan/pallas_call | solution.py:424
  724.8 11.6 collective-permute-done.38.refs_3_
  738.1 24.8 %recurrence_back.1 = (f32[528,2560]{1,0:T(8,128)}, f32[8,2560]{1,0:T(8,128)}, bf16[4,160,1280]{2,1,0:T(8,128)(2,1)}) custom-call(s32[1]{0:T(128)} %sub.46.live_ref, f32[528,2560]{1,0:T(8,128)} %convolution_add_fusion.refs_2_.pre_ref, f32[8,2560]{1,0:T(8,128)} %pad_maximum_fusion.15.refs_6_.par_ref, ...), custom_call_target="tpu_custom_call" | custom-call | flops 1024 | bytes 1024 | tf_op jit(solution)/shard_map/recurrence_back/pallas_call | solution.py:424
  765.9 8.5 fusion.85
  784.3 6.0 fusion.87
  806.0 6.4 convolution_convert_fusion.5
  812.6 27.2 %reduce-scatter.12.cloned.1.call-done.refs_1_ = bf16[256,2048]{1,0:T(8,128)(2,1)} async-done(((bf16[1024,2048]{1,0:T(8,128)(2,1)}), bf16[256,2048]{1,0:T(8,128)(2,1)}) %reduce-scatter.12.cloned.1.call-update) | async-done | bytes 1048592 | tf_op jit(solution)/shard_map/reduce_scatter | solution.py:574
  860.4 7.4 convolution_convert_fusion.4
  877.8 64.8 %collective-permute-done.45.refs_2_ = bf16[512,2048]{1,0:T(8,128)(2,1)S(1)} collective-permute-done((bf16[512,2048]{1,0:T(8,128)(2,1)}, bf16[512,2048]{1,0:T(8,128)(2,1)S(1)}, u32[]{:S(2)}, u32[]{:S(2)}) %collective-permute-start.45) | collective-permute-done | bytes 2097184 | tf_op jit(solution)/shard_map/ppermute | solution.py:141
  943.9 26.9 %collective-permute-done.46.refs_3_ = bf16[512,2048]{1,0:T(8,128)(2,1)} collective-permute-done((bf16[512,2048]{1,0:T(8,128)(2,1)}, bf16[512,2048]{1,0:T(8,128)(2,1)}, u32[]{:S(2)}, u32[]{:S(2)}) %collective-permute-start.46) | collective-permute-done | bytes 2097184 | tf_op jit(solution)/shard_map/ppermute | solution.py:142
  975.6 6.5 convolution_convert_fusion
  995.9 5.9 convolution_convert_fusion.2
  1001.9 7.4 convolution_convert_fusion.3
  1016.0 66.0 %collective-permute-done.50.refs_3_ = bf16[512,2048]{1,0:T(8,128)(2,1)} collective-permute-done((bf16[512,2048]{1,0:T(8,128)(2,1)}, bf16[512,2048]{1,0:T(8,128)(2,1)}, u32[]{:S(2)}, u32[]{:S(2)}) %collective-permute-start.50) | collective-permute-done | bytes 2097184 | tf_op jit(solution)/shard_map/ppermute | solution.py:142
  1111.9 7.1 collective-permute-done.56
  1125.5 17.8 %collective-permute-done.52.refs_3_.refs_4_ = bf16[256,2560]{1,0:T(8,128)(2,1)S(1)} collective-permute-done((bf16[256,2560]{1,0:T(8,128)(2,1)}, bf16[256,2560]{1,0:T(8,128)(2,1)S(1)}, u32[]{:S(2)}, u32[]{:S(2)}) %collective-permute-start.52) | collective-permute-done | bytes 1310752 | tf_op jit(solution)/shard_map/ppermute | solution.py:44
  1150.9 22.9 %collective-permute-done.67 = bf16[256,2560]{1,0:T(8,128)(2,1)S(1)} collective-permute-done((bf16[256,2560]{1,0:T(8,128)(2,1)}, bf16[256,2560]{1,0:T(8,128)(2,1)S(1)}, u32[]{:S(2)}, u32[]{:S(2)}) %collective-permute-start.67) | collective-permute-done | bytes 1310752 | tf_op jit(solution)/shard_map/ppermute | solution.py:44
  1184.8 11.7 collective-permute-done.68
  1201.7 8.4 collective-permute-done.64
  1216.9 9.9 collective-permute-done.70
  1239.7 18.5 %collective-permute-start.60 = (bf16[26752]{0:T(1024)(128)(2,1)S(1)}, bf16[26752]{0:T(1024)(128)(2,1)S(1)}, u32[]{:S(2)}, u32[]{:S(2)}) collective-permute-start(bf16[26752]{0:T(1024)(128)(2,1)S(1)} %get-tuple-element.199), channel_id=1, source_target_pairs={{0,2},{1,3},{2,0},{3,1},{4,6},{5,7},{6,4},{7,5},{8,10},{9,11},{10,... | collective-permute-start | bytes 160520 | tf_op jit(solution)/shard_map/ppermute | solution.py:128
  1263.8 12.9 collective-permute-done.61
  1295.8 5.8 collective-permute-done.73
  1305.1 7.0 interleave.1
  1318.0 10.3 reduce-scatter.14.cloned.1.call-done
  (746 shorter events, 455.8 us)
Async XLA Ops:
  7.2 90.3 %all-gather.15.cloned.1.call-start = ((), (), s32[]{:S(2)}) async-start(), calls=%async_computation.12 | async-start | bytes 1638400 | tf_op jit(solution)/shard_map/all_gather | solution.py:475
  12.3 91.5 %collective-permute-start.6 = (bf16[256,3072]{1,0:T(8,128)(2,1)}, bf16[256,3072]{1,0:T(8,128)(2,1)S(1)}, u32[]{:S(2)}, u32[]{:S(2)}) collective-permute-start(bf16[256,3072]{1,0:T(8,128)(2,1)} %get-tuple-element.257), channel_id=1, source_target_pairs={{0,8},{4,12},{8,0},{12,4},{16,24},{20,28},{24,16},{28,20},{1,9},{5... | collective-permute-start | bytes 4718600 | tf_op jit(solution)/shard_map/ppermute | solution.py:44
  15.2 88.6 %collective-permute-start.7 = (bf16[256,3072]{1,0:T(8,128)(2,1)}, bf16[256,3072]{1,0:T(8,128)(2,1)S(1)}, u32[]{:S(2)}, u32[]{:S(2)}) collective-permute-start(bf16[256,3072]{1,0:T(8,128)(2,1)} %get-tuple-element.257), channel_id=1, source_target_pairs={{0,16},{4,20},{8,24},{12,28},{16,0},{20,4},{24,8},{28,12},{1,17},{... | collective-permute-start | bytes 4718600 | tf_op jit(solution)/shard_map/ppermute | solution.py:44
  28.0 133.0 %all-gather.17.cloned.1.call-start = ((), (), s32[]{:S(2)}) async-start(), calls=%async_computation.13 | async-start | bytes 3276800 | tf_op jit(solution)/shard_map/all_gather | solution.py:475
  39.4 19.6 %collective-permute-start.4 = (bf16[2,4,26752]{2,1,0:T(4,128)(2,1)S(1)}, bf16[2,4,26752]{2,1,0:T(4,128)(2,1)S(1)}, u32[]{:S(2)}, u32[]{:S(2)}) collective-permute-start(bf16[2,4,26752]{2,1,0:T(4,128)(2,1)S(1)} %pad_maximum_fusion.13), channel_id=1, source_target_pairs={{0,8},{4,12},{8,0},{12,4},{16,24},{20,28},{24,16},{28,20},{1,9},{5... | collective-permute-start | bytes 1284104 | tf_op jit(solution)/shard_map/ppermute | solution.py:44
  60.6 20.5 %collective-permute-start.5 = (bf16[4,4,26752]{2,1,0:T(4,128)(2,1)}, bf16[4,4,26752]{2,1,0:T(4,128)(2,1)}, u32[]{:S(2)}, u32[]{:S(2)}) collective-permute-start(bf16[4,4,26752]{2,1,0:T(4,128)(2,1)} %pad_maximum_fusion.11), channel_id=1, source_target_pairs={{0,16},{4,20},{8,24},{12,28},{16,0},{20,4},{24,8},{28,12},{1,17},{... | collective-permute-start | bytes 2568200 | tf_op jit(solution)/shard_map/ppermute | solution.py:44
  103.1 328.4 %all-gather.11.cloned.1.call-start = ((), (), s32[]{:S(2)}) async-start(), calls=%async_computation.5 | async-start | bytes 5242880 | tf_op jit(solution)/shard_map/all_gather | solution.py:540
  106.1 29.4 %collective-permute-start.8 = (bf16[256,2560]{1,0:T(8,128)(2,1)}, bf16[256,2560]{1,0:T(8,128)(2,1)}, u32[]{:S(2)}, u32[]{:S(2)}) collective-permute-start(bf16[256,2560]{1,0:T(8,128)(2,1)} %fence.37), channel_id=1, source_target_pairs={{0,8},{4,12},{8,0},{12,4},{16,24},{20,28},{24,16},{28,20},{1,9},{5... | collective-permute-start | bytes 3932168 | tf_op jit(solution)/shard_map/ppermute | solution.py:44
  107.6 31.0 %collective-permute-start.10 = (bf16[256,2560]{1,0:T(8,128)(2,1)}, bf16[256,2560]{1,0:T(8,128)(2,1)}, u32[]{:S(2)}, u32[]{:S(2)}) collective-permute-start(bf16[256,2560]{1,0:T(8,128)(2,1)} %fence.37), channel_id=1, source_target_pairs={{0,16},{4,20},{8,24},{12,28},{16,0},{20,4},{24,8},{28,12},{1,17},{... | collective-permute-start | bytes 3932168 | tf_op jit(solution)/shard_map/ppermute | solution.py:44
  137.5 28.9 %collective-permute-start.9 = (bf16[128,2560]{1,0:T(8,128)(2,1)}, bf16[128,2560]{1,0:T(8,128)(2,1)S(1)}, u32[]{:S(2)}, u32[]{:S(2)}) collective-permute-start(bf16[128,2560]{1,0:T(8,128)(2,1)} %slice.691), channel_id=1, source_target_pairs={{0,16},{4,20},{8,24},{12,28},{16,0},{20,4},{24,8},{28,12},{1,17},{... | collective-permute-start | bytes 1966088 | tf_op jit(solution)/shard_map/ppermute | solution.py:44
  140.6 25.8 %collective-permute-start.11 = (bf16[128,2560]{1,0:T(8,128)(2,1)}, bf16[128,2560]{1,0:T(8,128)(2,1)S(1)}, u32[]{:S(2)}, u32[]{:S(2)}) collective-permute-start(bf16[128,2560]{1,0:T(8,128)(2,1)} %slice.692), channel_id=1, source_target_pairs={{0,8},{4,12},{8,0},{12,4},{16,24},{20,28},{24,16},{28,20},{1,9},{5... | collective-permute-start | bytes 1966088 | tf_op jit(solution)/shard_map/ppermute | solution.py:44
  175.5 42.1 %collective-permute-start.12 = (bf16[256,2560]{1,0:T(8,128)(2,1)S(1)}, bf16[256,2560]{1,0:T(8,128)(2,1)S(1)}, u32[]{:S(2)}, u32[]{:S(2)}) collective-permute-start(bf16[256,2560]{1,0:T(8,128)(2,1)S(1)} %copy-done.35), channel_id=1, source_target_pairs={{0,8},{4,12},{8,0},{12,4},{16,24},{20,28},{24,16},{28,20},{1,9},{5... | collective-permute-start | bytes 3932168 | tf_op jit(solution)/shard_map/ppermute | solution.py:44
  176.1 41.6 %collective-permute-start.13 = (bf16[256,2560]{1,0:T(8,128)(2,1)S(1)}, bf16[256,2560]{1,0:T(8,128)(2,1)S(1)}, u32[]{:S(2)}, u32[]{:S(2)}) collective-permute-start(bf16[256,2560]{1,0:T(8,128)(2,1)S(1)} %copy-done.35), channel_id=1, source_target_pairs={{0,16},{4,20},{8,24},{12,28},{16,0},{20,4},{24,8},{28,12},{1,17},{... | collective-permute-start | bytes 3932168 | tf_op jit(solution)/shard_map/ppermute | solution.py:44
  256.2 30.1 %collective-permute-start.21 = (bf16[256,2560]{1,0:T(8,128)(2,1)S(1)}, bf16[256,2560]{1,0:T(8,128)(2,1)S(1)}, u32[]{:S(2)}, u32[]{:S(2)}) collective-permute-start(bf16[256,2560]{1,0:T(8,128)(2,1)S(1)} %copy-done.28), channel_id=1, source_target_pairs={{0,8},{4,12},{8,0},{12,4},{16,24},{20,28},{24,16},{28,20},{1,9},{5... | collective-permute-start | bytes 3932168 | tf_op jit(solution)/shard_map/ppermute | solution.py:44
  256.9 29.8 %collective-permute-start.22 = (bf16[256,2560]{1,0:T(8,128)(2,1)S(1)}, bf16[256,2560]{1,0:T(8,128)(2,1)S(1)}, u32[]{:S(2)}, u32[]{:S(2)}) collective-permute-start(bf16[256,2560]{1,0:T(8,128)(2,1)S(1)} %copy-done.28), channel_id=1, source_target_pairs={{0,16},{4,20},{8,24},{12,28},{16,0},{20,4},{24,8},{28,12},{1,17},{... | collective-permute-start | bytes 3932168 | tf_op jit(solution)/shard_map/ppermute | solution.py:44
  312.8 29.7 %collective-permute-start.25 = (bf16[1024,2560]{1,0:T(8,128)(2,1)}, bf16[1024,2560]{1,0:T(8,128)(2,1)}, u32[]{:S(2)}, u32[]{:S(2)}) collective-permute-start(bf16[1024,2560]{1,0:T(8,128)(2,1)} %constant_dynamic-update-slice_fusion.11), channel_id=1, source_target_pairs={{0,4},{4,0},{8,12},{12,8},{16,20},{20,16},{24,28},{28,24},{1,5},{5... | collective-permute-start | bytes 15728648 | tf_op jit(solution)/shard_map/ppermute | solution.py:44
  319.4 20.0 %collective-permute-start.26 = (bf16[128,3072]{1,0:T(8,128)(2,1)S(1)}, bf16[128,3072]{1,0:T(8,128)(2,1)S(1)}, u32[]{:S(2)}, u32[]{:S(2)}) collective-permute-start(bf16[128,3072]{1,0:T(8,128)(2,1)S(1)} %slice.547), channel_id=1, source_target_pairs={{0,16},{4,20},{8,24},{12,28},{16,0},{20,4},{24,8},{28,12},{1,17},{... | collective-permute-start | bytes 2359304 | tf_op jit(solution)/shard_map/ppermute | solution.py:44
  321.8 19.8 %collective-permute-start.27 = (bf16[128,3072]{1,0:T(8,128)(2,1)S(1)}, bf16[128,3072]{1,0:T(8,128)(2,1)S(1)}, u32[]{:S(2)}, u32[]{:S(2)}) collective-permute-start(bf16[128,3072]{1,0:T(8,128)(2,1)S(1)} %slice.548), channel_id=1, source_target_pairs={{0,8},{4,12},{8,0},{12,4},{16,24},{20,28},{24,16},{28,20},{1,9},{5... | collective-permute-start | bytes 2359304 | tf_op jit(solution)/shard_map/ppermute | solution.py:44
  351.8 160.4 %all-gather.13.cloned.1.call-start = ((), (), s32[]{:S(2)}) async-start(), calls=%async_computation.6 | async-start | bytes 5242880 | tf_op jit(solution)/shard_map/all_gather | solution.py:540
  359.3 41.1 %collective-permute-start.28 = (bf16[1024,3072]{1,0:T(8,128)(2,1)}, bf16[1024,3072]{1,0:T(8,128)(2,1)}, u32[]{:S(2)}, u32[]{:S(2)}) collective-permute-start(bf16[1024,3072]{1,0:T(8,128)(2,1)} %get-tuple-element.251), channel_id=1, source_target_pairs={{0,4},{4,0},{8,12},{12,8},{16,20},{20,16},{24,28},{28,24},{1,5},{5... | collective-permute-start | bytes 18874376 | tf_op jit(solution)/shard_map/ppermute | solution.py:44
  359.3 20.0 %collective-permute-start.30 = (bf16[256,1536]{1,0:T(8,128)(2,1)S(1)}, bf16[256,1536]{1,0:T(8,128)(2,1)S(1)}, u32[]{:S(2)}, u32[]{:S(2)}) collective-permute-start(bf16[256,1536]{1,0:T(8,128)(2,1)S(1)} %copy-done.58), channel_id=1, source_target_pairs={{0,16},{4,20},{8,24},{12,28},{16,0},{20,4},{24,8},{28,12},{1,17},{... | collective-permute-start | bytes 2359304 | tf_op jit(solution)/shard_map/ppermute | solution.py:44
  360.2 20.3 %collective-permute-start.29 = (bf16[256,1536]{1,0:T(8,128)(2,1)S(1)}, bf16[256,1536]{1,0:T(8,128)(2,1)S(1)}, u32[]{:S(2)}, u32[]{:S(2)}) collective-permute-start(bf16[256,1536]{1,0:T(8,128)(2,1)S(1)} %copy-done.58), channel_id=1, source_target_pairs={{0,8},{4,12},{8,0},{12,4},{16,24},{20,28},{24,16},{28,20},{1,9},{5... | collective-permute-start | bytes 2359304 | tf_op jit(solution)/shard_map/ppermute | solution.py:44
  400.0 280.9 %reduce-scatter.6.cloned.1.call-start = ((), (), s32[]{:S(2)}) async-start(), calls=%async_computation.7 | async-start | bytes 5242880 | tf_op jit(solution)/shard_map/reduce_scatter | solution.py:549
  484.5 196.4 %reduce-scatter.8.cloned.1.call-start = ((), (), s32[]{:S(2)}) async-start(), calls=%async_computation.8 | async-start | bytes 5242880 | tf_op jit(solution)/shard_map/reduce_scatter | solution.py:549
  593.7 186.8 %reduce-scatter.10.cloned.1.call-start = ((), (), s32[]{:S(2)}) async-start(), calls=%async_computation.9 | async-start | bytes 5242880 | tf_op jit(solution)/shard_map/reduce_scatter | solution.py:574
  603.4 67.1 %collective-permute-start.34 = (bf16[1024,1536]{1,0:T(8,128)(2,1)}, bf16[1024,1536]{1,0:T(8,128)(2,1)S(1)}, u32[]{:S(2)}, u32[]{:S(2)}) collective-permute-start(bf16[1024,1536]{1,0:T(8,128)(2,1)} %add_convert_fusion.2), channel_id=1, source_target_pairs={{0,4},{4,0},{8,12},{12,8},{16,20},{20,16},{24,28},{28,24},{1,5},{5... | collective-permute-start | bytes 9437192 | tf_op jit(solution)/shard_map/ppermute | solution.py:44
  625.1 51.1 %collective-permute-start.35 = (bf16[1024,3072]{1,0:T(8,128)(2,1)}, bf16[1024,3072]{1,0:T(8,128)(2,1)}, u32[]{:S(2)}, u32[]{:S(2)}) collective-permute-start(bf16[1024,3072]{1,0:T(8,128)(2,1)} %add_convert_fusion), channel_id=1, source_target_pairs={{0,4},{4,0},{8,12},{12,8},{16,20},{20,16},{24,28},{28,24},{1,5},{5... | collective-permute-start | bytes 18874376 | tf_op jit(solution)/shard_map/ppermute | solution.py:44
  681.0 158.8 %reduce-scatter.12.cloned.1.call-start = ((), (), s32[]{:S(2)}) async-start(), calls=%async_computation.10 | async-start | bytes 5242880 | tf_op jit(solution)/shard_map/reduce_scatter | solution.py:574
  682.9 39.0 %collective-permute-start.36 = (bf16[256,1536]{1,0:T(8,128)(2,1)}, bf16[256,1536]{1,0:T(8,128)(2,1)S(1)}, u32[]{:S(2)}, u32[]{:S(2)}) collective-permute-start(bf16[256,1536]{1,0:T(8,128)(2,1)} %get-tuple-element.239.refs_2_), channel_id=1, source_target_pairs={{0,8},{4,12},{8,0},{12,4},{16,24},{20,28},{24,16},{28,20},{1,9},{5... | collective-permute-start | bytes 2359304 | tf_op jit(solution)/shard_map/ppermute | solution.py:44
  684.4 38.8 %collective-permute-start.37 = (bf16[256,1536]{1,0:T(8,128)(2,1)S(1)}, bf16[256,1536]{1,0:T(8,128)(2,1)S(1)}, u32[]{:S(2)}, u32[]{:S(2)}) collective-permute-start(bf16[256,1536]{1,0:T(8,128)(2,1)S(1)} %copy-done.83), channel_id=1, source_target_pairs={{0,16},{4,20},{8,24},{12,28},{16,0},{20,4},{24,8},{28,12},{1,17},{... | collective-permute-start | bytes 2359304 | tf_op jit(solution)/shard_map/ppermute | solution.py:44
  685.9 50.5 %collective-permute-start.38 = (bf16[256,3072]{1,0:T(8,128)(2,1)}, bf16[256,3072]{1,0:T(8,128)(2,1)}, u32[]{:S(2)}, u32[]{:S(2)}) collective-permute-start(bf16[256,3072]{1,0:T(8,128)(2,1)} %get-tuple-element.213.refs_4_), channel_id=1, source_target_pairs={{0,8},{4,12},{8,0},{12,4},{16,24},{20,28},{24,16},{28,20},{1,9},{5... | collective-permute-start | bytes 4718600 | tf_op jit(solution)/shard_map/ppermute | solution.py:44
  686.5 50.9 %collective-permute-start.39 = (bf16[256,3072]{1,0:T(8,128)(2,1)}, bf16[256,3072]{1,0:T(8,128)(2,1)}, u32[]{:S(2)}, u32[]{:S(2)}) collective-permute-start(bf16[256,3072]{1,0:T(8,128)(2,1)} %get-tuple-element.212.refs_5_), channel_id=1, source_target_pairs={{0,16},{4,20},{8,24},{12,28},{16,0},{20,4},{24,8},{28,12},{1,17},{... | collective-permute-start | bytes 4718600 | tf_op jit(solution)/shard_map/ppermute | solution.py:44
  724.7 459.1 %all-gather.19.cloned.1.call-start = ((), (), s32[]{:S(2)}) async-start(), calls=%async_computation.14 | async-start | bytes 5242880 | tf_op jit(solution)/shard_map/all_gather | solution.py:621
  812.5 27.3 %collective-permute-start.44 = (bf16[1024,2560]{1,0:T(8,128)(2,1)}, bf16[1024,2560]{1,0:T(8,128)(2,1)}, u32[]{:S(2)}, u32[]{:S(2)}) collective-permute-start(bf16[1024,2560]{1,0:T(8,128)(2,1)} %convolution_convert_fusion.5), channel_id=1, source_target_pairs={{0,4},{4,0},{8,12},{12,8},{16,20},{20,16},{24,28},{28,24},{1,5},{5... | collective-permute-start | bytes 15728648 | tf_op jit(solution)/shard_map/ppermute | solution.py:44
  848.9 387.7 %all-gather.21.cloned.1.call-start = ((), (), s32[]{:S(2)}) async-start(), calls=%async_computation.15 | async-start | bytes 5242880 | tf_op jit(solution)/shard_map/all_gather | solution.py:621
  851.8 90.7 %collective-permute-start.45 = (bf16[512,2048]{1,0:T(8,128)(2,1)}, bf16[512,2048]{1,0:T(8,128)(2,1)S(1)}, u32[]{:S(2)}, u32[]{:S(2)}) collective-permute-start(bf16[512,2048]{1,0:T(8,128)(2,1)} %permute.7.refs_1_), channel_id=1, source_target_pairs={{0,1},{1,2},{2,3},{4,5},{5,6},{6,7},{8,9},{9,10},{10,11},{12,13},{... | collective-permute-start | bytes 6291464 | tf_op jit(solution)/shard_map/ppermute | solution.py:141
  853.7 117.1 %collective-permute-start.46 = (bf16[512,2048]{1,0:T(8,128)(2,1)}, bf16[512,2048]{1,0:T(8,128)(2,1)}, u32[]{:S(2)}, u32[]{:S(2)}) collective-permute-start(bf16[512,2048]{1,0:T(8,128)(2,1)} %permute.7.refs_1_), channel_id=1, source_target_pairs={{1,0},{2,1},{3,2},{5,4},{6,5},{7,6},{9,8},{10,9},{11,10},{13,12},{... | collective-permute-start | bytes 6291464 | tf_op jit(solution)/shard_map/ppermute | solution.py:142
  875.5 111.2 %collective-permute-start.47 = (bf16[256,2560]{1,0:T(8,128)(2,1)}, bf16[256,2560]{1,0:T(8,128)(2,1)S(1)}, u32[]{:S(2)}, u32[]{:S(2)}) collective-permute-start(bf16[256,2560]{1,0:T(8,128)(2,1)} %get-tuple-element.112), channel_id=1, source_target_pairs={{0,8},{4,12},{8,0},{12,4},{16,24},{20,28},{24,16},{28,20},{1,9},{5... | collective-permute-start | bytes 3932168 | tf_op jit(solution)/shard_map/ppermute | solution.py:44
  876.3 110.5 %collective-permute-start.48 = (bf16[256,2560]{1,0:T(8,128)(2,1)}, bf16[256,2560]{1,0:T(8,128)(2,1)}, u32[]{:S(2)}, u32[]{:S(2)}) collective-permute-start(bf16[256,2560]{1,0:T(8,128)(2,1)} %get-tuple-element.113), channel_id=1, source_target_pairs={{0,16},{4,20},{8,24},{12,28},{16,0},{20,4},{24,8},{28,12},{1,17},{... | collective-permute-start | bytes 3932168 | tf_op jit(solution)/shard_map/ppermute | solution.py:44
  982.0 138.8 %collective-permute-start.66 = (bf16[1024,2560]{1,0:T(8,128)(2,1)}, bf16[1024,2560]{1,0:T(8,128)(2,1)}, u32[]{:S(2)}, u32[]{:S(2)}) collective-permute-start(bf16[1024,2560]{1,0:T(8,128)(2,1)} %convolution_convert_fusion), channel_id=1, source_target_pairs={{0,4},{4,0},{8,12},{12,8},{16,20},{20,16},{24,28},{28,24},{1,5},{5... | collective-permute-start | bytes 15728648 | tf_op jit(solution)/shard_map/ppermute | solution.py:44
  987.8 28.2 %collective-permute-start.49 = (bf16[512,2048]{1,0:T(8,128)(2,1)}, bf16[512,2048]{1,0:T(8,128)(2,1)S(1)}, u32[]{:S(2)}, u32[]{:S(2)}) collective-permute-start(bf16[512,2048]{1,0:T(8,128)(2,1)} %get-tuple-element.114), channel_id=1, source_target_pairs={{1,2},{2,3},{5,6},{6,7},{9,10},{10,11},{13,14},{14,15},{17,18},{18... | collective-permute-start | bytes 6291464 | tf_op jit(solution)/shard_map/ppermute | solution.py:141
  988.6 93.4 %collective-permute-start.50 = (bf16[512,2048]{1,0:T(8,128)(2,1)}, bf16[512,2048]{1,0:T(8,128)(2,1)}, u32[]{:S(2)}, u32[]{:S(2)}) collective-permute-start(bf16[512,2048]{1,0:T(8,128)(2,1)} %get-tuple-element.115), channel_id=1, source_target_pairs={{1,0},{2,1},{5,4},{6,5},{9,8},{10,9},{13,12},{14,13},{17,16},{18,1... | collective-permute-start | bytes 6291464 | tf_op jit(solution)/shard_map/ppermute | solution.py:142
  993.5 17.4 %collective-permute-start.62 = (bf16[128,2560]{1,0:T(8,128)(2,1)}, bf16[128,2560]{1,0:T(8,128)(2,1)}, u32[]{:S(2)}, u32[]{:S(2)}) collective-permute-start(bf16[128,2560]{1,0:T(8,128)(2,1)} %get-tuple-element.127), channel_id=1, source_target_pairs={{0,8},{4,12},{8,0},{12,4},{16,24},{20,28},{24,16},{28,20},{1,9},{5... | collective-permute-start | bytes 1966088 | tf_op jit(solution)/shard_map/ppermute | solution.py:44
  1001.9 326.4 %reduce-scatter.14.cloned.1.call-start = ((), (), s32[]{:S(2)}) async-start(), calls=%async_computation.11 | async-start | bytes 4915200 | tf_op jit(solution)/shard_map/reduce_scatter | solution.py:639
  1010.9 95.9 %collective-permute-start.51 = (bf16[1024,2560]{1,0:T(8,128)(2,1)}, bf16[1024,2560]{1,0:T(8,128)(2,1)}, u32[]{:S(2)}, u32[]{:S(2)}) collective-permute-start(bf16[1024,2560]{1,0:T(8,128)(2,1)} %convolution_convert_fusion.2), channel_id=1, source_target_pairs={{0,4},{4,0},{8,12},{12,8},{16,20},{20,16},{24,28},{28,24},{1,5},{5... | collective-permute-start | bytes 15728648 | tf_op jit(solution)/shard_map/ppermute | solution.py:44
  1096.7 22.3 %collective-permute-start.56 = (bf16[4,4,26752]{2,1,0:T(4,128)(2,1)}, bf16[4,4,26752]{2,1,0:T(4,128)(2,1)}, u32[]{:S(2)}, u32[]{:S(2)}) collective-permute-start(bf16[4,4,26752]{2,1,0:T(4,128)(2,1)} %slice.754), channel_id=1, source_target_pairs={{0,16},{4,20},{8,24},{12,28},{16,0},{20,4},{24,8},{28,12},{1,17},{... | collective-permute-start | bytes 2568200 | tf_op jit(solution)/shard_map/ppermute | solution.py:44
  1111.4 31.9 %collective-permute-start.52 = (bf16[256,2560]{1,0:T(8,128)(2,1)}, bf16[256,2560]{1,0:T(8,128)(2,1)S(1)}, u32[]{:S(2)}, u32[]{:S(2)}) collective-permute-start(bf16[256,2560]{1,0:T(8,128)(2,1)} %get-tuple-element.117), channel_id=1, source_target_pairs={{0,8},{4,12},{8,0},{12,4},{16,24},{20,28},{24,16},{28,20},{1,9},{5... | collective-permute-start | bytes 3932168 | tf_op jit(solution)/shard_map/ppermute | solution.py:44
  1111.4 32.9 %collective-permute-start.53 = (bf16[256,2560]{1,0:T(8,128)(2,1)}, bf16[256,2560]{1,0:T(8,128)(2,1)S(1)}, u32[]{:S(2)}, u32[]{:S(2)}) collective-permute-start(bf16[256,2560]{1,0:T(8,128)(2,1)} %get-tuple-element.118), channel_id=1, source_target_pairs={{0,16},{4,20},{8,24},{12,28},{16,0},{20,4},{24,8},{28,12},{1,17},{... | collective-permute-start | bytes 3932168 | tf_op jit(solution)/shard_map/ppermute | solution.py:44
  1120.8 28.7 %collective-permute-start.57 = (bf16[2,4,26752]{2,1,0:T(4,128)(2,1)S(1)}, bf16[2,4,26752]{2,1,0:T(4,128)(2,1)S(1)}, u32[]{:S(2)}, u32[]{:S(2)}) collective-permute-start(bf16[2,4,26752]{2,1,0:T(4,128)(2,1)S(1)} %slice.756), channel_id=1, source_target_pairs={{0,8},{4,12},{8,0},{12,4},{16,24},{20,28},{24,16},{28,20},{1,9},{5... | collective-permute-start | bytes 1284104 | tf_op jit(solution)/shard_map/ppermute | solution.py:44
  1145.4 28.4 %collective-permute-start.67 = (bf16[256,2560]{1,0:T(8,128)(2,1)}, bf16[256,2560]{1,0:T(8,128)(2,1)S(1)}, u32[]{:S(2)}, u32[]{:S(2)}) collective-permute-start(bf16[256,2560]{1,0:T(8,128)(2,1)} %get-tuple-element.132), channel_id=1, source_target_pairs={{0,16},{4,20},{8,24},{12,28},{16,0},{20,4},{24,8},{28,12},{1,17},{... | collective-permute-start | bytes 3932168 | tf_op jit(solution)/shard_map/ppermute | solution.py:44
  1150.6 86.1 %collective-permute-start.58 = (bf16[1,4,26752]{2,1,0:T(4,128)(2,1)}, bf16[1,4,26752]{2,1,0:T(4,128)(2,1)}, u32[]{:S(2)}, u32[]{:S(2)}) collective-permute-start(bf16[1,4,26752]{2,1,0:T(4,128)(2,1)} %slice.758), channel_id=1, source_target_pairs={{0,4},{4,0},{8,12},{12,8},{16,20},{20,16},{24,28},{28,24},{1,5},{5... | collective-permute-start | bytes 642056 | tf_op jit(solution)/shard_map/ppermute | solution.py:44
  1150.6 33.3 %collective-permute-start.69 = (bf16[256,2560]{1,0:T(8,128)(2,1)}, bf16[256,2560]{1,0:T(8,128)(2,1)}, u32[]{:S(2)}, u32[]{:S(2)}) collective-permute-start(bf16[256,2560]{1,0:T(8,128)(2,1)} %get-tuple-element.133), channel_id=1, source_target_pairs={{0,8},{4,12},{8,0},{12,4},{16,24},{20,28},{24,16},{28,20},{1,9},{5... | collective-permute-start | bytes 3932168 | tf_op jit(solution)/shard_map/ppermute | solution.py:44
  1177.2 19.3 %collective-permute-start.68 = (bf16[128,2560]{1,0:T(8,128)(2,1)}, bf16[128,2560]{1,0:T(8,128)(2,1)}, u32[]{:S(2)}, u32[]{:S(2)}) collective-permute-start(bf16[128,2560]{1,0:T(8,128)(2,1)} %add_convert_fusion.23), channel_id=1, source_target_pairs={{0,8},{4,12},{8,0},{12,4},{16,24},{20,28},{24,16},{28,20},{1,9},{5... | collective-permute-start | bytes 1966088 | tf_op jit(solution)/shard_map/ppermute | solution.py:44
  1180.4 29.7 %collective-permute-start.64 = (bf16[128,2560]{1,0:T(8,128)(2,1)}, bf16[128,2560]{1,0:T(8,128)(2,1)S(1)}, u32[]{:S(2)}, u32[]{:S(2)}) collective-permute-start(bf16[128,2560]{1,0:T(8,128)(2,1)} %get-tuple-element.129), channel_id=1, source_target_pairs={{0,8},{4,12},{8,0},{12,4},{16,24},{20,28},{24,16},{28,20},{1,9},{5... | collective-permute-start | bytes 1966088 | tf_op jit(solution)/shard_map/ppermute | solution.py:44
  1182.4 28.1 %collective-permute-start.65 = (bf16[128,2560]{1,0:T(8,128)(2,1)}, bf16[128,2560]{1,0:T(8,128)(2,1)S(1)}, u32[]{:S(2)}, u32[]{:S(2)}) collective-permute-start(bf16[128,2560]{1,0:T(8,128)(2,1)} %get-tuple-element.130), channel_id=1, source_target_pairs={{0,16},{4,20},{8,24},{12,28},{16,0},{20,4},{24,8},{28,12},{1,17},{... | collective-permute-start | bytes 1966088 | tf_op jit(solution)/shard_map/ppermute | solution.py:44
  1183.9 95.0 %collective-permute-start.54 = (bf16[512,2048]{1,0:T(8,128)(2,1)}, bf16[512,2048]{1,0:T(8,128)(2,1)S(1)}, u32[]{:S(2)}, u32[]{:S(2)}) collective-permute-start(bf16[512,2048]{1,0:T(8,128)(2,1)} %get-tuple-element.119), channel_id=1, source_target_pairs={{2,3},{6,7},{10,11},{14,15},{18,19},{22,23},{26,27},{30,31}} | collective-permute-start | bytes 6291464 | tf_op jit(solution)/shard_map/ppermute | solution.py:141
  1196.5 82.4 %collective-permute-start.55 = (bf16[512,2048]{1,0:T(8,128)(2,1)}, bf16[512,2048]{1,0:T(8,128)(2,1)}, u32[]{:S(2)}, u32[]{:S(2)}) collective-permute-start(bf16[512,2048]{1,0:T(8,128)(2,1)} %get-tuple-element.120), channel_id=1, source_target_pairs={{1,0},{5,4},{9,8},{13,12},{17,16},{21,20},{25,24},{29,28}} | collective-permute-start | bytes 6291464 | tf_op jit(solution)/shard_map/ppermute | solution.py:142
  1239.6 37.1 %collective-permute-start.61 = (bf16[26752]{0:T(1024)(128)(2,1)S(1)}, bf16[26752]{0:T(1024)(128)(2,1)S(1)}, u32[]{:S(2)}, u32[]{:S(2)}) collective-permute-start(bf16[26752]{0:T(1024)(128)(2,1)S(1)} %get-tuple-element.198), channel_id=1, source_target_pairs={{0,3},{1,0},{2,1},{3,2},{4,7},{5,4},{6,5},{7,6},{8,11},{9,8},{10,9... | collective-permute-start | bytes 160520 | tf_op jit(solution)/shard_map/ppermute | solution.py:128
  1239.7 37.0 %collective-permute-start.60 = (bf16[26752]{0:T(1024)(128)(2,1)S(1)}, bf16[26752]{0:T(1024)(128)(2,1)S(1)}, u32[]{:S(2)}, u32[]{:S(2)}) collective-permute-start(bf16[26752]{0:T(1024)(128)(2,1)S(1)} %get-tuple-element.199), channel_id=1, source_target_pairs={{0,2},{1,3},{2,0},{3,1},{4,6},{5,7},{6,4},{7,5},{8,10},{9,11},{10,... | collective-permute-start | bytes 160520 | tf_op jit(solution)/shard_map/ppermute | solution.py:128
  1258.2 18.5 %collective-permute-start.59 = (bf16[26752]{0:T(1024)(128)(2,1)S(1)}, bf16[26752]{0:T(1024)(128)(2,1)S(1)}, u32[]{:S(2)}, u32[]{:S(2)}) collective-permute-start(bf16[26752]{0:T(1024)(128)(2,1)S(1)} %get-tuple-element.197), channel_id=1, source_target_pairs={{0,1},{1,2},{2,3},{3,0},{4,5},{5,6},{6,7},{7,4},{8,9},{9,10},{10,1... | collective-permute-start | bytes 160520 | tf_op jit(solution)/shard_map/ppermute | solution.py:128
  1280.2 32.0 %collective-permute-start.71 = (bf16[128,3072]{1,0:T(8,128)(2,1)}, bf16[128,3072]{1,0:T(8,128)(2,1)S(1)}, u32[]{:S(2)}, u32[]{:S(2)}) collective-permute-start(bf16[128,3072]{1,0:T(8,128)(2,1)} %get-tuple-element.134), channel_id=1, source_target_pairs={{0,8},{4,12},{8,0},{12,4},{16,24},{20,28},{24,16},{28,20},{1,9},{5... | collective-permute-start | bytes 2359304 | tf_op jit(solution)/shard_map/ppermute | solution.py:44
  1280.2 32.0 %collective-permute-start.72 = (bf16[128,3072]{1,0:T(8,128)(2,1)}, bf16[128,3072]{1,0:T(8,128)(2,1)S(1)}, u32[]{:S(2)}, u32[]{:S(2)}) collective-permute-start(bf16[128,3072]{1,0:T(8,128)(2,1)} %get-tuple-element.135), channel_id=1, source_target_pairs={{0,16},{4,20},{8,24},{12,28},{16,0},{20,4},{24,8},{28,12},{1,17},{... | collective-permute-start | bytes 2359304 | tf_op jit(solution)/shard_map/ppermute | solution.py:44
  1280.2 21.4 %collective-permute-start.73 = (bf16[128,1536]{1,0:T(8,128)(2,1)}, bf16[128,1536]{1,0:T(8,128)(2,1)S(1)}, u32[]{:S(2)}, u32[]{:S(2)}) collective-permute-start(bf16[128,1536]{1,0:T(8,128)(2,1)} %get-tuple-element.136), channel_id=1, source_target_pairs={{0,8},{4,12},{8,0},{12,4},{16,24},{20,28},{24,16},{28,20},{1,9},{5... | collective-permute-start | bytes 1179656 | tf_op jit(solution)/shard_map/ppermute | solution.py:44
  1282.2 19.4 %collective-permute-start.74 = (bf16[128,1536]{1,0:T(8,128)(2,1)}, bf16[128,1536]{1,0:T(8,128)(2,1)S(1)}, u32[]{:S(2)}, u32[]{:S(2)}) collective-permute-start(bf16[128,1536]{1,0:T(8,128)(2,1)} %get-tuple-element.137), channel_id=1, source_target_pairs={{0,16},{4,20},{8,24},{12,28},{16,0},{20,4},{24,8},{28,12},{1,17},{... | collective-permute-start | bytes 1179656 | tf_op jit(solution)/shard_map/ppermute | solution.py:44
  (180 other events, 1588.5 us)
Sparse Core Ops, SparseCore 0:
  28.1 29.1 all-gather.14
  103.2 55.9 all-gather.16
  351.9 79.5 all-gather.10
  432.9 79.2 all-gather.12
  514.4 75.2 reduce-scatter.5
  593.8 75.4 reduce-scatter.7
  681.1 76.4 reduce-scatter.9
  760.0 79.7 reduce-scatter.11
  849.0 117.5 all-gather.18
  1002.0 106.5 all-gather.20
  1236.7 91.4 reduce-scatter.13

commit v5 on v4

--- a/solution.py
+++ b/solution.py
@@ -40,6 +40,41 @@
     return list(call(*values, *others))
 
 
+def assemble(pieces, *others):
+    count = len(pieces)
+    rows = [p.shape[0] for p in pieces]
+    spans = [pl.ds(sum(rows[:k]), rows[k]) for k in range(count)]
+    shape = (sum(rows), pieces[0].shape[1])
+
+    def body(*refs):
+        out, held, coming, going = refs[count + len(others) :]
+        ins = [pltpu.make_async_copy(refs[k], held.at[spans[k]], coming.at[k]) for k in range(count)]
+        outs = [pltpu.make_async_copy(held.at[spans[k]], out.at[spans[k]], going.at[k]) for k in range(count)]
+        for copy in ins:
+            copy.start()
+        for here, there in zip(ins, outs):
+            here.wait()
+            there.start()
+        for copy in outs:
+            copy.wait()
+
+    place = pl.BlockSpec(memory_space=pl.ANY)
+    return pl.pallas_call(
+        body,
+        in_specs=[place] * (count + len(others)),
+        out_specs=place,
+        out_shape=jax.ShapeDtypeStruct(shape, pieces[0].dtype),
+        scratch_shapes=[
+            pltpu.VMEM(shape, pieces[0].dtype),
+            pltpu.SemaphoreType.DMA((count,)),
+            pltpu.SemaphoreType.DMA((count,)),
+        ],
+        compiler_params=pltpu.CompilerParams(vmem_limit_bytes=VMEM),
+        cost_estimate=LITTLE,
+        name="assemble",
+    )(*pieces, *others)
+
+
 def exchange(values, bit, size):
     return lax.ppermute(values, "dp", [(k, k ^ (1 << bit)) for k in range(size)])
 
@@ -64,8 +99,7 @@
         unit = own.shape[0] // 2
         by_x, by_y = fence([by_x, by_y], *before_last)
         got = [exchange(by_x[:unit], 2, size), exchange(by_y[unit:], 1, size)]
-        low, high = fence(got, *before_core)
-        half = jnp.concatenate([own, by_x, high, low, by_y])
+        half = assemble([own, by_x, got[1], got[0], by_y], *before_core)
     else:
         (pieces,) = fence(some, *before_last)
         got = [exchange(pieces, size.bit_length() - 2, size)]
@@ -137,35 +171,22 @@
     return total
 
 
-def line_round(right, left, k, n):
-    right = lax.ppermute(right, "tensor", [(s, s + 1) for s in range(k - 1, n - 1)])
-    left = lax.ppermute(left, "tensor", [(s, s - 1) for s in range(1, n - k + 1)])
-    return right, left
-
-
-def line_result(own, rounds, n):
+def small_plain(halves, size, n):
+    mask = jnp.arange(size) ^ lax.axis_index("dp")
+    rows = jnp.concatenate(halves).reshape(size, n, -1)
+    return jnp.take(rows, (mask & 1) * (size // 2) + (mask >> 1), axis=0, mode="clip").transpose(1, 0, 2)
+
+
+def z_gather(own, n):
     turn = lax.axis_index("tensor")
-    rows = own.shape[0]
-    out = jnp.zeros((n * rows, own.shape[1]), own.dtype)
-    out = lax.dynamic_update_slice_in_dim(out, own, turn * rows, 0)
-    for k in range(1, n):
-        piece = rounds[k - 1][1] + rounds[n - k - 1][0]
-        out = lax.dynamic_update_slice_in_dim(out, piece, (turn + k) % n * rows, 0)
-    return out
-
-
-def small_gather(own, size, n):
-    turn, place = lax.axis_index("tensor"), lax.axis_index("dp")
-    rows = jnp.stack([own] + [z_shift(own, -k, n) for k in range(1, n)])
-    rows = jnp.take(rows, (jnp.arange(n) - turn) % n, axis=0)[None]
-    for bit in range(size.bit_length() - 1):
-        rows = jnp.concatenate([rows, exchange(rows, bit, size)])
-    return jnp.take(rows, jnp.arange(size) ^ place, axis=0).transpose(1, 0, 2)
+    blocks = jnp.stack([own] + [z_shift(own, -k, n) for k in range(1, n)])
+    blocks = jnp.take(blocks, (jnp.arange(n) - turn) % n, axis=0, mode="clip")
+    return blocks.transpose(1, 0, 2).reshape(own.shape[0], -1)
 
 
 def small_scatter(values, size, n):
     place = lax.axis_index("dp")
-    values = jnp.take(values, jnp.arange(size) ^ place, axis=0)
+    values = jnp.take(values, jnp.arange(size) ^ place, axis=0, mode="clip")
     for bit in reversed(range(size.bit_length() - 1)):
         half = values.shape[0] // 2
         values = add_all([values[:half], exchange(values[half:], bit, size)])
@@ -194,16 +215,18 @@
         out_ref[:, p * width : (p + 1) * width] = in_ref[:, pl.ds(start, width)]
 
 
-def permute_rows(values, table):
+def permute_rows(values, table, step=0, stride=1, offset=0):
     rows, d_model = values.shape
-    step = max(k for k in range(16, 289, 16) if rows % k == 0)
-    spec = pl.BlockSpec((step, d_model), lambda r, tab: (r, 0))
+    step = step or max(k for k in range(16, 289, 16) if rows % k == 0)
     return pl.pallas_call(
         functools.partial(copy_kernel, table.shape[0]),
         grid_spec=pltpu.PrefetchScalarGridSpec(
-            num_scalar_prefetch=1, grid=(rows // step,), in_specs=[spec], out_specs=spec
+            num_scalar_prefetch=1,
+            grid=(rows // (step * stride),),
+            in_specs=[pl.BlockSpec((step, d_model), lambda r, tab: (r * stride + offset, 0))],
+            out_specs=pl.BlockSpec((step, d_model), lambda r, tab: (r, 0)),
         ),
-        out_shape=jax.ShapeDtypeStruct(values.shape, values.dtype),
+        out_shape=jax.ShapeDtypeStruct((rows // stride, d_model), values.dtype),
         compiler_params=pltpu.CompilerParams(vmem_limit_bytes=VMEM),
         cost_estimate=LITTLE,
         name="permute",
@@ -232,7 +255,7 @@
 
 def permute_gain(values, table):
     lead = values.shape[0]
-    return jnp.take(values.reshape(lead, table.shape[0], -1), table, axis=1).reshape(lead, -1)
+    return jnp.take(values.reshape(lead, table.shape[0], -1), table, axis=1, mode="clip").reshape(lead, -1)
 
 
 def row_ids(count, width, first):
@@ -471,18 +494,24 @@
     live_count = (lengths - turn * rows).astype(jnp.int32)
     live = (lax.iota(jnp.int32, rows)[:, None] < live_count).astype(F32)
 
-    def wide(owns):
-        own = lax.all_gather(jnp.stack(owns), "tensor", axis=0)
-        return [own[:, k].transpose(1, 0, 2).reshape(d_own, width) for k in range(len(owns))]
-
-    (z_rec,) = wide([w_rec.astype(BF)])
+    small = [w_lru.transpose(2, 0, 1, 3).reshape(-1), chan.reshape(-1), gains.reshape(-1)]
+    small = jnp.concatenate(small).astype(BF)
+    count, cols = small.shape[0], w_gelu.shape[1]
+    small = jnp.pad(small, (0, -count % (16 * cols))).reshape(-1, cols)
+    whole = jnp.concatenate([w_rec.astype(BF), w_gelu.astype(BF), small])
+    own_dn = w_down.T.astype(BF)
     own_gu = jnp.concatenate([w_mlp_in[0], w_mlp_in[1]], axis=1).astype(BF)
-    own_dn = w_down.T.astype(BF)
-    some_gu = spread_begin(own_gu, size)
-    small = [w_lru.transpose(2, 0, 1, 3).reshape(-1), chan.reshape(-1), gains.reshape(-1)]
-    small = small_gather(jnp.concatenate(small).astype(BF), size, n)
-    z_gelu, z_out = wide(fence([w_gelu.astype(BF), w_out.T.astype(BF)], z_rec))
-    some_r = spread_begin(z_rec, size, *some_gu[1:])
+    some_dn = spread_begin(own_dn, size)
+    whole = lax.all_gather(whole, "tensor", axis=0)
+    z_rec, z_gelu = (
+        whole[:, k * d_own : (k + 1) * d_own].transpose(1, 0, 2).reshape(d_own, width) for k in range(2)
+    )
+    some_r = spread_begin(z_rec, size, *some_dn[1:])
+    some_small = spread_begin(whole[:, 2 * d_own :].reshape(n, -1), size)
+    z_out = z_gather(*fence([w_out.T.astype(BF)], z_rec), n)
+    w_r, came_r = spread_end(some_r, size, (), ())
+    small, _ = spread_end(some_small, size, (), ())
+    small = small_plain(fence(small, *came_r), size, n)[..., :count]
 
     gain = small[0, :, -gains.size :].reshape(size, 2, d_own).transpose(1, 0, 2).reshape(2, d_model)
     gain = permute_gain(gain, table).astype(F32)
@@ -500,13 +529,10 @@
     first_rate = norm_rate(extended)
     first = (extended * first_rate * gain[0]).astype(BF)
     inputs, first_own, first_rate = extended[HALO:], first[HALO:], first_rate[HALO:]
-    cot = permute_rows(cotangent, *fence([table], *some_r[1:])).reshape(n, 2, half, d_model)
-    cots = [cot[:, h].reshape(n * half, d_model) for h in range(2)]
     cut = d_model // 2
 
     keep = (rows, width, F32)
     dense = ((GROUP, 2 * GROUP), BF)
-    w_r, came_r = spread_end(some_r, size, (), (first, *cots, lru, par, z_gelu))
     some_g = spread_begin(z_gelu, size, *came_r)
     rec_pre = wide_dot(first, w_r)
     conv, decay, ig, dg, state, prod = kernel_call(
@@ -518,7 +544,7 @@
     carry = jnp.zeros((1, width), F32)
     for end in came[::-1]:
         carry = end[1:] + end[:1] * carry
-    w_g, came_g = spread_end(some_g, size, (rec_pre,), (ends,))
+    w_g, came_g = spread_end(some_g, size, (rec_pre, z_out), (ends,))
     some_o = spread_begin(z_out, size, *came_g, ends)
     branch_pre = wide_dot(first_own, w_g)
     recurrent = (state + prod * carry) * live
@@ -528,10 +554,12 @@
     second_rate = norm_rate(hidden)
     second_unit = hidden * second_rate
     second_own = (second_unit * gain[1]).astype(BF)
-    w_gu, came_gu = spread_end(some_gu, size, came_o, (second_own,))
-    some_dn = spread_begin(own_dn, size, *came_gu)
-    w_dn, _ = spread_end(some_dn, size, (), ())
-    w_gu, w_dn = jnp.concatenate(w_gu), jnp.concatenate(w_dn)
+    some_gu = spread_begin(own_gu, size, *came_o)
+    w_gu, came_gu = spread_end(some_gu, size, (), (second_own,))
+    w_dn, _ = spread_end(some_dn, size, came_gu, ())
+    w_gu, w_dn = assemble(w_gu), assemble(w_dn)
+    late = fence([table], second_own)[0]
+    cots = [permute_rows(cotangent, late, half, 2, h) for h in range(2)]
 
     hidden_units = w_dn.shape[1]
     grad_products = [dot(c, w_dn) for c in cots]
@@ -574,7 +602,7 @@
     mlp_sums = [lax.psum_scatter(share, "tensor", scatter_dimension=0, tiled=True) for share in shares]
 
     grad_second = jnp.concatenate(grad_second).astype(F32)
-    cot_own = lax.dynamic_index_in_dim(cot, turn, 0).reshape(rows, d_model).astype(F32)
+    cot_own = jnp.concatenate([lax.dynamic_slice_in_dim(c, turn * half, half) for c in cots]).astype(F32)
     gain_two = jnp.sum(grad_second * second_unit, axis=0)
     grad_hidden = cot_own + norm_back(grad_second, second_unit, second_rate, gain[1])
     hidden_low = grad_hidden.astype(BF)
@@ -611,31 +639,29 @@
     gain_one = jnp.sum(grad_first * first_unit, axis=0)
     grad_tokens = grad_hidden + norm_back(grad_first, first_unit, first_rate, gain[0])
     grad_tokens = permute_rows(grad_tokens.astype(BF), inverse)
-    rounds = [line_round(grad_tokens, grad_tokens, 1, n)]
+    gathered = [lax.all_gather(grad_tokens[h * half : (h + 1) * half], "tensor", axis=0) for h in range(2)]
     (mixed,) = fence([mixed], grad_tokens)
     sum_o = by_cols(hidden_low, mixed)
     pre_low, rec_low = fence([pre_low, rec_low], sum_o.terms[1])
     sum_g, sum_r = by_cols(first_own, pre_low), by_cols(first_own, rec_low)
     results = [mlp_result(h, mlp_sum) for h, mlp_sum in enumerate(fence(mlp_sums, sum_o.terms[1]))]
-    got_o = sum_o.hop(fence(sum_o.sources(), *results))
-    result_0, result_1 = (lax.all_gather(result, "tensor", axis=0) for result in results)
-    rounds.append(line_round(*fence(rounds[0], *got_o), 2, n))
-    sum_o.hop(fence(sum_o.sources(), *rounds[0]))
-    got_g = sum_g.hop(fence(sum_g.sources(), *rounds[0]))
-    for k in range(3, n):
-        rounds.append(line_round(*fence(rounds[-1], result_0, *got_g), k, n))
-    sum_g.hop(fence(sum_g.sources(), *rounds[1]))
-    got_r = sum_r.hop(fence(sum_r.sources(), *rounds[1], *got_g))
-    d_lru, dpar = fence([d_lru, dpar], *rounds[1])
-    sum_r.hop(sum_r.sources())
+    got_o = sum_o.hop(sum_o.sources())
+    sum_o.hop(fence(sum_o.sources(), gathered[0]))
+    got_g = sum_g.hop(fence(sum_g.sources(), gathered[0]))
+    results = fence(results, gathered[0])
+    results = [lax.all_gather(result, "tensor", axis=0) for result in results]
+    sum_g.hop(fence(sum_g.sources(), gathered[1]))
+    got_r = sum_r.hop(fence(sum_r.sources(), gathered[1], *got_g))
+    d_lru, dpar = fence([d_lru, dpar], gathered[1])
+    sum_r.hop(fence(sum_r.sources(), results[0]))
     if sum_dn.square:
-        sum_dn.hop(fence(sum_dn.sources(), *rounds[-1]))
-        sum_gu.hop(fence(sum_gu.sources(), *rounds[-1]))
-    tokens_out = line_result(grad_tokens, rounds, n)
-    output = interleave(*fence([result_0, result_1], *rounds[-1])).reshape(n * rows, d_model)
+        sum_dn.hop(fence(sum_dn.sources(), results[0]))
+        sum_gu.hop(fence(sum_gu.sources(), results[0]))
+    tokens_out = interleave(*fence(gathered, results[0])).reshape(n * rows, d_model)
     g_gu, g_dn = sum_gu.finish().astype(F32), sum_dn.finish().astype(F32)
     owned = jnp.stack([total.finish().reshape(d_own, n, width // n) for total in (sum_o, sum_g, sum_r)])
-    (owned,) = fence([owned.transpose(2, 0, 1, 3)], result_1)
+    (owned,) = fence([owned.transpose(2, 0, 1, 3)], results[1])
+    output = interleave(*results).reshape(n * rows, d_model)
     owned = lax.psum_scatter(owned, "tensor", scatter_dimension=0).astype(F32)
     g_o, g_g, g_r = owned[0], owned[1], owned[2]
 

time: 1350 us -> 1280 us (0.948)
  local copies, waits for them, and re-layouts: 193 us -> 135 us
  Pallas kernels: 91.9 us -> 136 us
  waiting for transfers between devices: 492 us -> 467 us
  other arithmetic: 147 us -> 129 us
  starting transfers between devices: 95.6 us -> 81.9 us
    all_gather x4 -> x5, waiting for transfers between devices: 0.02 us -> 185 us  [the longest x2 126 us: on_device(): lax.all_gather(grad_tokens[h * half:(h + 1) * half], 'tensor', axis=0)]
    ppermute x6 -> x0, waiting for transfers between devices: 158 us -> none  [the longest x3 92.9 us: line_round(): lax.ppermute(left, 'tensor', [(s, s - 1) for s in range(1, n - k + 1)])]
    unnamed x352 -> x244, local copies, waits for them, and re-layouts: 93.5 us -> 38.7 us
    ppermute x56, waiting for transfers between devices: 228 us -> 188 us  [exchange(): return lax.ppermute(values, 'dp', [(k, k ^ 1 << bit) for k in range(size)])]
    pallas_call x0 -> x7, Pallas kernels: none -> 35 us  [assemble(): pl.pallas_call(body, in_specs=[place] * (count + len(others)), out_specs=...]
    reduce_scatter x4, waiting for transfers between devices: 27.2 us -> 9.7 us  [on_device(): lax.psum_scatter(share, 'tensor', scatter_dimension=0, tiled=True)]
    reduce_scatter x1, waiting for transfers between devices: 10.3 us -> 26.4 us  [on_device(): owned = lax.psum_scatter(owned, 'tensor', scatter_dimension=0).astype(F32)]
    concatenate x10 -> x0, local copies, waits for them, and re-layouts: 14.8 us -> none  [the longest x5 7.04 us: spread_end(): half = jnp.concatenate([own, by_x, high, low, by_y])]
  transfers between devices with their start and end apart: 86 -> 81, of which waited for: 40 -> 38; matrix products, arithmetic and copies ran while one was open for 42% -> 41% of each run, Pallas kernels for 7% -> 10%
where the time goes in v5:
time: 1280 us; the launch traced here: 1270 us
  waiting for transfers between devices  467 us (36%)
  matrix products  302 us (24%)
  Pallas kernels  136 us (11%)
  local copies, waits for them, and re-layouts  135 us (11%)
  other arithmetic  129 us (10%)
  starting transfers between devices  81.9 us (6%)
  between operations  17 us (1%)
    dot_general x34, matrix products, dot(): lax.dot_general(left, right, (dims, ((), ())), preferred_element_type=F32)  302 us
    ppermute x56, waiting for transfers between devices, exchange(): return lax.ppermute(values, 'dp', [(k, k ^ 1 << bit) for k in range(size)])  188 us
    all_gather x2, waiting for transfers between devices, on_device(): lax.all_gather(grad_tokens[h * half:(h + 1) * half], 'tensor', axis=0)  126 us
    pallas_call x3, Pallas kernels, kernel_call(): pl.pallas_call(body, grid_spec=pltpu.PrefetchScalarGridSpec(num_scalar_pr...  60.3 us
    convert_element_type x18, other arithmetic, add_all(): return total.astype(BF)  57.8 us
    ppermute x56, starting transfers between devices, exchange(): return lax.ppermute(values, 'dp', [(k, k ^ 1 << bit) for k in range(size)])  55 us
    all_gather x1, waiting for transfers between devices, on_device(): whole = lax.all_gather(whole, 'tensor', axis=0)  53.4 us
    all_gather x2, waiting for transfers between devices, on_device(): lax.all_gather(second_own[h * half:(h + 1) * half], 'tensor', axis=0, til...  46.2 us
  transfers between devices with their start and end apart: 81, of which 38 were waited for; matrix products, arithmetic and copies ran while one was open for 41% of the time, Pallas kernels for 10%

profile of v5, /device:TPU:0, one launch (start us, length us, event | category | flops | bytes accessed | tf_op | source)
XLA Modules:
  0.0 1268.8 jit_solution(12689734460312966231)
XLA Ops:
  21.7 53.4 %all-gather.17.cloned.1.call-done = bf16[2240,640]{1,0:T(8,128)(2,1)} async-done(((bf16[560,640]{1,0:T(8,128)(2,1)}), bf16[2240,640]{1,0:T(8,128)(2,1)}) %all-gather.17.cloned.1.call-update) | async-done | bytes 2867216 | tf_op jit(solution)/shard_map/all_gather | solution.py:505
  103.7 23.5 %collective-permute-done.7.refs_4_ = bf16[256,2560]{1,0:T(8,128)(2,1)S(1)} collective-permute-done((bf16[256,2560]{1,0:T(8,128)(2,1)}, bf16[256,2560]{1,0:T(8,128)(2,1)S(1)}, u32[]{:S(2)}, u32[]{:S(2)}) %collective-permute-start.7) | collective-permute-done | bytes 1310752 | tf_op jit(solution)/shard_map/ppermute | solution.py:79
  135.7 10.0 collective-permute-done.13
  163.2 4.9 gather_fusion
  190.8 5.7 fusion.43
  216.8 18.4 %recurrence.1 = (f32[512,2560]{1,0:T(8,128)}, f32[512,2560]{1,0:T(8,128)}, f32[512,2560]{1,0:T(8,128)}, f32[512,2560]{1,0:T(8,128)}, f32[512,2560]{1,0:T(8,128)}, /*index=5*/f32[512,2560]{1,0:T(8,128)}) custom-call(s32[1]{0:T(128)} %sub.38.live_ref, f32[528,2560]{1,0:T(8,128)} %convolution_add_fusion.refs_2_.pre_ref, f32[8,2560]{1,0:T(8,128)} %pad_maximum_fusion.15.par_ref, ...), custom_call_target="tpu_custom_call" | custom-call | flops 1024 | bytes 1024 | tf_op jit(solution)/shard_map/recurrence/pallas_call | solution.py:447
  243.7 10.7 collective-permute-start.20
  262.1 5.1 fusion.53
  267.3 9.7 fusion.22
  277.0 13.0 %collective-permute-done.22.refs_1_ = bf16[256,2560]{1,0:T(8,128)(2,1)S(1)} collective-permute-done((bf16[256,2560]{1,0:T(8,128)(2,1)}, bf16[256,2560]{1,0:T(8,128)(2,1)S(1)}, u32[]{:S(2)}, u32[]{:S(2)}) %collective-permute-start.22) | collective-permute-done | bytes 1310752 | tf_op jit(solution)/shard_map/ppermute | solution.py:79
  296.7 12.2 collective-permute-done.23.refs_2_
  321.1 6.4 fusion.84
  327.5 28.4 %collective-permute-done.27.refs_4_ = bf16[256,3072]{1,0:T(8,128)(2,1)S(1)} collective-permute-done((bf16[256,3072]{1,0:T(8,128)(2,1)}, bf16[256,3072]{1,0:T(8,128)(2,1)S(1)}, u32[]{:S(2)}, u32[]{:S(2)}) %collective-permute-start.27) | collective-permute-done | bytes 1572896 | tf_op jit(solution)/shard_map/ppermute | solution.py:79
  368.7 7.6 collective-permute-done.28.refs_2_.refs_3_
  377.8 5.2 assemble.10.refs_0_
  388.2 8.5 collective-permute-done.31.refs_2_
  402.4 5.8 permute.8
  408.2 5.9 permute.7
  420.6 9.4 assemble.11
  430.0 18.6 %all-gather.13.cloned.1.call-done = bf16[1024,2048]{1,0:T(8,128)(2,1)} async-done(((bf16[256,2048]{1,0:T(8,128)(2,1)}), bf16[1024,2048]{1,0:T(8,128)(2,1)}) %all-gather.13.cloned.1.call-update) | async-done | bytes 4194320 | tf_op jit(solution)/shard_map/all_gather | solution.py:568
  448.6 19.3 %fusion.86 = f32[1024,3072]{1,0:T(8,128)} fusion(bf16[1024,2048]{1,0:T(8,128)(2,1)} %all-gather.13.cloned.1.call-done, bf16[2048,3072]{1,0:T(8,128)(2,1)} %assemble.11), kind=kOutput, calls=%fused_computation.245 | convolution fusion | flops 12884901888 | bytes 29360128 | tf_op jit(solution)/shard_map/dot_general | solution.py:24
  467.9 14.6 %fusion.6 = (bf16[1024,1536]{1,0:T(8,128)(2,1)S(1)}, bf16[1024,1536]{1,0:T(8,128)(2,1)S(1)}, bf16[1024,1536]{1,0:T(8,128)(2,1)}) fusion(f32[1024,3072]{1,0:T(8,128)} %fusion.86, bf16[1024,2048]{1,0:T(8,128)(2,1)S(1)} %copy-done.26, bf16[2048,1536]{1,0:T(8,128)(2,1)S(1)} %copy-done.31), kind=kOutput, calls=%fused_computation.18 | convolution fusion | flops 6483345408 | bytes 32505856 | tf_op jit(solution)/shard_map/dot_general | solution.py:24
  484.2 17.6 %convolution_convert_fusion.7.refs_1_ = bf16[1024,2048]{1,0:T(8,128)(2,1)} fusion(bf16[2048,3072]{1,0:T(8,128)(2,1)} %assemble.11, bf16[1024,1536]{1,0:T(8,128)(2,1)S(1)} %get-tuple-element.184, bf16[1024,1536]{1,0:T(8,128)(2,1)S(1)} %get-tuple-element.183), kind=kOutput, calls=%fused_computation.75 | convolution fusion | flops 12899581952 | bytes 23068672 | tf_op jit(solution)/shard_map/dot_general | solution.py:24
  501.9 27.6 %all-gather.15.cloned.1.call-done.refs_0_ = bf16[1024,2048]{1,0:T(8,128)(2,1)} async-done(((bf16[256,2048]{1,0:T(8,128)(2,1)}), bf16[1024,2048]{1,0:T(8,128)(2,1)}) %all-gather.15.cloned.1.call-update) | async-done | bytes 4194320 | tf_op jit(solution)/shard_map/all_gather | solution.py:568
  529.5 19.4 %fusion.87 = f32[1024,3072]{1,0:T(8,128)} fusion(bf16[1024,2048]{1,0:T(8,128)(2,1)} %fence.42, bf16[2048,3072]{1,0:T(8,128)(2,1)} %assemble.11), kind=kOutput, calls=%fused_computation.246 | convolution fusion | flops 12884901888 | bytes 29360128 | tf_op jit(solution)/shard_map/dot_general | solution.py:24
  548.9 15.3 %fusion.13 = (bf16[1024,1536]{1,0:T(8,128)(2,1)}, bf16[1024,1536]{1,0:T(8,128)(2,1)}, bf16[1024,1536]{1,0:T(8,128)(2,1)}) fusion(f32[1024,3072]{1,0:T(8,128)} %fusion.87, bf16[1024,2048]{1,0:T(8,128)(2,1)S(1)} %copy-done.29, bf16[2048,1536]{1,0:T(8,128)(2,1)S(1)} %bitcast.182), kind=kOutput, calls=%fused_computation.25 | convolution fusion | flops 6483345408 | bytes 32505856 | tf_op jit(solution)/shard_map/dot_general | solution.py:24
  564.2 5.6 pad_maximum_fusion.refs_1_
  569.8 18.9 %convolution_convert_fusion.6.refs_2_ = bf16[1024,2048]{1,0:T(8,128)(2,1)} fusion(bf16[2048,3072]{1,0:T(8,128)(2,1)} %assemble.11, bf16[1024,1536]{1,0:T(8,128)(2,1)} %get-tuple-element.182, bf16[1024,1536]{1,0:T(8,128)(2,1)S(1)} %copy-done.45), kind=kOutput, calls=%fused_computation.74 | convolution fusion | flops 12899581952 | bytes 23068672 | tf_op jit(solution)/shard_map/dot_general | solution.py:24
  590.6 5.6 pad_maximum_fusion.1.refs_1_
  596.2 7.4 fusion.37
  603.7 8.4 convolution_convert_fusion.9.refs_6_.refs_0_
  612.2 9.7 add_convert_fusion.2
  621.9 9.4 fusion.31
  631.4 11.8 add_convert_fusion
  643.7 11.0 fusion.34
  654.6 11.2 convolution_convert_fusion.8.refs_7_.refs_1_
  665.8 5.4 fusion.40
  671.2 7.1 add_convert_fusion.3
  678.3 10.2 add_convert_fusion.1
  712.9 5.6 fusion.49
  723.8 17.1 %back_scan.1 = (f32[512,2560]{1,0:T(8,128)}, f32[512,2560]{1,0:T(8,128)}, f32[8,2560]{1,0:T(8,128)}, bf16[512,2560]{1,0:T(8,128)(2,1)}) custom-call(s32[1]{0:T(128)} %sub.38.live_ref, f32[512,2560]{1,0:T(8,128)} %get-tuple-element.239.refs_2_.pre_ref, f32[512,2560]{1,0:T(8,128)} %convolution_add_fusion.1.grad_ref, f32[512,2560]{1,0:T(8,128)} %get-tuple-element.82.decay_ref, ...), custom_call_target="tpu_custom_call" | custom-call | flops 1024 | bytes 1024 | tf_op jit(solution)/shard_map/back_scan/pallas_call | solution.py:447
  745.8 11.3 collective-permute-done.39.refs_4_
  759.0 24.9 %recurrence_back.1 = (f32[528,2560]{1,0:T(8,128)}, f32[8,2560]{1,0:T(8,128)}, bf16[4,160,1280]{2,1,0:T(8,128)(2,1)}) custom-call(s32[1]{0:T(128)} %sub.38.live_ref, f32[528,2560]{1,0:T(8,128)} %convolution_add_fusion.refs_2_.pre_ref, f32[8,2560]{1,0:T(8,128)} %pad_maximum_fusion.15.par_ref, bf16[4,160,1280]{2,1,0:T(8,128)(2,1)} %reshape_transpose_reshape.3.w_ref, ...), custom_call_target="tpu_custom_call" | custom-call | flops 1024 | bytes 1024 | tf_op jit(solution)/shard_map/recurrence_back/pallas_call | solution.py:447
  786.6 7.5 fusion.88
  794.1 6.9 fusion.89
  805.3 5.8 fusion.90
  811.2 5.0 fusion.91
  818.8 6.1 add_convert_fusion.4.in_ref
  833.2 6.4 convolution_convert_fusion.5
  843.5 6.0 convolution_convert_fusion.4
  849.5 9.7 reduce-scatter.12.cloned.1.call-done.refs_1_
  878.9 62.2 %all-gather.19.cloned.1.call-done = bf16[1024,2048]{1,0:T(8,128)(2,1)} async-done(((bf16[256,2048]{1,0:T(8,128)(2,1)}), bf16[1024,2048]{1,0:T(8,128)(2,1)}) %all-gather.19.cloned.1.call-update) | async-done | bytes 4194320 | tf_op jit(solution)/shard_map/all_gather | solution.py:642
  942.9 6.1 convolution_convert_fusion.3
  958.4 63.7 %all-gather.25.cloned.1.call-done = bf16[1024,2048]{1,0:T(8,128)(2,1)} async-done(((bf16[256,2048]{1,0:T(8,128)(2,1)}), bf16[1024,2048]{1,0:T(8,128)(2,1)}) %all-gather.25.cloned.1.call-update) | async-done | bytes 4194320 | tf_op jit(solution)/shard_map/all_gather | solution.py:642
  1045.6 5.9 convolution_convert_fusion
  1057.9 8.2 collective-permute-done.45
  1093.7 13.4 %collective-permute-done.56.refs_4_ = bf16[256,2560]{1,0:T(8,128)(2,1)S(1)} collective-permute-done((bf16[256,2560]{1,0:T(8,128)(2,1)}, bf16[256,2560]{1,0:T(8,128)(2,1)S(1)}, u32[]{:S(2)}, u32[]{:S(2)}) %collective-permute-start.56) | collective-permute-done | bytes 1310752 | tf_op jit(solution)/shard_map/ppermute | solution.py:79
  1121.6 21.4 %collective-permute-done.61 = bf16[256,2560]{1,0:T(8,128)(2,1)S(1)} collective-permute-done((bf16[256,2560]{1,0:T(8,128)(2,1)}, bf16[256,2560]{1,0:T(8,128)(2,1)S(1)}, u32[]{:S(2)}, u32[]{:S(2)}) %collective-permute-start.61) | collective-permute-done | bytes 1310752 | tf_op jit(solution)/shard_map/ppermute | solution.py:79
  1150.9 6.6 collective-permute-done.58
  1162.2 7.3 collective-permute-done.63
  1178.3 5.4 all-gather.23.cloned.1.call-done
  1200.6 7.0 interleave.2
  1210.6 7.0 interleave.3
  1231.7 26.4 %reduce-scatter.14.cloned.1.call-done = bf16[1,3,256,640]{3,2,1,0:T(8,128)(2,1)} async-done(((bf16[4,3,256,640]{3,2,1,0:T(8,128)(2,1)}), bf16[1,3,256,640]{3,2,1,0:T(8,128)(2,1)}) %reduce-scatter.14.cloned.1.call-update) | async-done | bytes 983056 | tf_op jit(solution)/shard_map/reduce_scatter | solution.py:665
  (604 shorter events, 400.9 us)
Async XLA Ops:
  7.2 67.9 %all-gather.17.cloned.1.call-start = ((), (), s32[]{:S(2)}) async-start(), calls=%async_computation.12 | async-start | bytes 3584000 | tf_op jit(solution)/shard_map/all_gather | solution.py:505
  13.3 435.3 %all-gather.13.cloned.1.call-start = ((), (), s32[]{:S(2)}) async-start(), calls=%async_computation.5 | async-start | bytes 5242880 | tf_op jit(solution)/shard_map/all_gather | solution.py:568
  14.6 82.2 %collective-permute-start.4 = (bf16[256,1536]{1,0:T(8,128)(2,1)}, bf16[256,1536]{1,0:T(8,128)(2,1)S(1)}, u32[]{:S(2)}, u32[]{:S(2)}) collective-permute-start(bf16[256,1536]{1,0:T(8,128)(2,1)} %bitcast.95.refs_0_), channel_id=1, source_target_pairs={{0,16},{4,20},{8,24},{12,28},{16,0},{20,4},{24,8},{28,12},{1,17},{... | collective-permute-start | bytes 2359304 | tf_op jit(solution)/shard_map/ppermute | solution.py:79
  17.5 79.3 %collective-permute-start.3 = (bf16[256,1536]{1,0:T(8,128)(2,1)}, bf16[256,1536]{1,0:T(8,128)(2,1)}, u32[]{:S(2)}, u32[]{:S(2)}) collective-permute-start(bf16[256,1536]{1,0:T(8,128)(2,1)} %bitcast.95.refs_0_), channel_id=1, source_target_pairs={{0,8},{4,12},{8,0},{12,4},{16,24},{20,28},{24,16},{28,20},{1,9},{5... | collective-permute-start | bytes 2359304 | tf_op jit(solution)/shard_map/ppermute | solution.py:79
  97.7 29.5 %collective-permute-start.7 = (bf16[256,2560]{1,0:T(8,128)(2,1)}, bf16[256,2560]{1,0:T(8,128)(2,1)S(1)}, u32[]{:S(2)}, u32[]{:S(2)}) collective-permute-start(bf16[256,2560]{1,0:T(8,128)(2,1)} %fence.32.refs_0_), channel_id=1, source_target_pairs={{0,16},{4,20},{8,24},{12,28},{16,0},{20,4},{24,8},{28,12},{1,17},{... | collective-permute-start | bytes 3932168 | tf_op jit(solution)/shard_map/ppermute | solution.py:79
  98.2 31.4 %collective-permute-start.5 = (bf16[256,2560]{1,0:T(8,128)(2,1)}, bf16[256,2560]{1,0:T(8,128)(2,1)S(1)}, u32[]{:S(2)}, u32[]{:S(2)}) collective-permute-start(bf16[256,2560]{1,0:T(8,128)(2,1)} %fence.32.refs_0_), channel_id=1, source_target_pairs={{0,8},{4,12},{8,0},{12,4},{16,24},{20,28},{24,16},{28,20},{1,9},{5... | collective-permute-start | bytes 3932168 | tf_op jit(solution)/shard_map/ppermute | solution.py:79
  101.3 55.9 %collective-permute-start.2 = (bf16[16,30720]{1,0:T(8,128)(2,1)S(1)}, bf16[16,30720]{1,0:T(8,128)(2,1)}, u32[]{:S(2)}, u32[]{:S(2)}) collective-permute-start(bf16[16,30720]{1,0:T(8,128)(2,1)S(1)} %pad_maximum_fusion.12.refs_0_), channel_id=1, source_target_pairs={{0,4},{4,0},{8,12},{12,8},{16,20},{20,16},{24,28},{28,24},{1,5},{5... | collective-permute-start | bytes 2949128 | tf_op jit(solution)/shard_map/ppermute | solution.py:79
  103.2 29.2 %collective-permute-start.14 = (bf16[256,640]{1,0:T(8,128)(2,1)S(1)}, bf16[256,640]{1,0:T(8,128)(2,1)S(1)}, u32[]{:S(2)}, u32[]{:S(2)}) collective-permute-start(bf16[256,640]{1,0:T(8,128)(2,1)S(1)} %copy-done.54), channel_id=1, source_target_pairs={{0,1},{1,2},{2,3},{3,0},{4,5},{5,6},{6,7},{7,4},{8,9},{9,10},{10,1... | collective-permute-start | bytes 983048 | tf_op jit(solution)/shard_map/ppermute | solution.py:162
  128.1 24.7 %collective-permute-start.8 = (bf16[128,2560]{1,0:T(8,128)(2,1)}, bf16[128,2560]{1,0:T(8,128)(2,1)}, u32[]{:S(2)}, u32[]{:S(2)}) collective-permute-start(bf16[128,2560]{1,0:T(8,128)(2,1)} %slice.698), channel_id=1, source_target_pairs={{0,8},{4,12},{8,0},{12,4},{16,24},{20,28},{24,16},{28,20},{1,9},{5... | collective-permute-start | bytes 1966088 | tf_op jit(solution)/shard_map/ppermute | solution.py:79
  130.6 22.3 %collective-permute-start.6 = (bf16[128,2560]{1,0:T(8,128)(2,1)}, bf16[128,2560]{1,0:T(8,128)(2,1)}, u32[]{:S(2)}, u32[]{:S(2)}) collective-permute-start(bf16[128,2560]{1,0:T(8,128)(2,1)} %slice.697), channel_id=1, source_target_pairs={{0,16},{4,20},{8,24},{12,28},{16,0},{20,4},{24,8},{28,12},{1,17},{... | collective-permute-start | bytes 1966088 | tf_op jit(solution)/shard_map/ppermute | solution.py:79
  157.1 33.6 %collective-permute-start.11 = (bf16[1024,2560]{1,0:T(8,128)(2,1)}, bf16[1024,2560]{1,0:T(8,128)(2,1)}, u32[]{:S(2)}, u32[]{:S(2)}) collective-permute-start(bf16[1024,2560]{1,0:T(8,128)(2,1)} %assemble.7), channel_id=1, source_target_pairs={{0,4},{4,0},{8,12},{12,8},{16,20},{20,16},{24,28},{28,24},{1,5},{5... | collective-permute-start | bytes 15728648 | tf_op jit(solution)/shard_map/ppermute | solution.py:79
  173.3 31.4 %collective-permute-start.10 = (bf16[256,2560]{1,0:T(8,128)(2,1)}, bf16[256,2560]{1,0:T(8,128)(2,1)S(1)}, u32[]{:S(2)}, u32[]{:S(2)}) collective-permute-start(bf16[256,2560]{1,0:T(8,128)(2,1)} %fence.34.refs_0_), channel_id=1, source_target_pairs={{0,16},{4,20},{8,24},{12,28},{16,0},{20,4},{24,8},{28,12},{1,17},{... | collective-permute-start | bytes 3932168 | tf_op jit(solution)/shard_map/ppermute | solution.py:79
  174.8 31.2 %collective-permute-start.9 = (bf16[256,2560]{1,0:T(8,128)(2,1)}, bf16[256,2560]{1,0:T(8,128)(2,1)}, u32[]{:S(2)}, u32[]{:S(2)}) collective-permute-start(bf16[256,2560]{1,0:T(8,128)(2,1)} %fence.34.refs_0_), channel_id=1, source_target_pairs={{0,8},{4,12},{8,0},{12,4},{16,24},{20,28},{24,16},{28,20},{1,9},{5... | collective-permute-start | bytes 3932168 | tf_op jit(solution)/shard_map/ppermute | solution.py:79
  209.9 27.7 %collective-permute-start.15 = (bf16[128,2560]{1,0:T(8,128)(2,1)}, bf16[128,2560]{1,0:T(8,128)(2,1)S(1)}, u32[]{:S(2)}, u32[]{:S(2)}) collective-permute-start(bf16[128,2560]{1,0:T(8,128)(2,1)} %slice.532), channel_id=1, source_target_pairs={{0,8},{4,12},{8,0},{12,4},{16,24},{20,28},{24,16},{28,20},{1,9},{5... | collective-permute-start | bytes 1966088 | tf_op jit(solution)/shard_map/ppermute | solution.py:79
  210.4 27.2 %collective-permute-start.16 = (bf16[128,2560]{1,0:T(8,128)(2,1)}, bf16[128,2560]{1,0:T(8,128)(2,1)S(1)}, u32[]{:S(2)}, u32[]{:S(2)}) collective-permute-start(bf16[128,2560]{1,0:T(8,128)(2,1)} %slice.533), channel_id=1, source_target_pairs={{0,16},{4,20},{8,24},{12,28},{16,0},{20,4},{24,8},{28,12},{1,17},{... | collective-permute-start | bytes 1966088 | tf_op jit(solution)/shard_map/ppermute | solution.py:79
  243.6 18.6 %collective-permute-start.17 = (bf16[1024,2560]{1,0:T(8,128)(2,1)}, bf16[1024,2560]{1,0:T(8,128)(2,1)}, u32[]{:S(2)}, u32[]{:S(2)}) collective-permute-start(bf16[1024,2560]{1,0:T(8,128)(2,1)} %assemble.8), channel_id=1, source_target_pairs={{0,4},{4,0},{8,12},{12,8},{16,20},{20,16},{24,28},{28,24},{1,5},{5... | collective-permute-start | bytes 15728648 | tf_op jit(solution)/shard_map/ppermute | solution.py:79
  259.8 30.3 %collective-permute-start.22 = (bf16[256,2560]{1,0:T(8,128)(2,1)}, bf16[256,2560]{1,0:T(8,128)(2,1)S(1)}, u32[]{:S(2)}, u32[]{:S(2)}) collective-permute-start(bf16[256,2560]{1,0:T(8,128)(2,1)} %fence.37.refs_0_), channel_id=1, source_target_pairs={{0,16},{4,20},{8,24},{12,28},{16,0},{20,4},{24,8},{28,12},{1,17},{... | collective-permute-start | bytes 3932168 | tf_op jit(solution)/shard_map/ppermute | solution.py:79
  260.6 30.0 %collective-permute-start.21 = (bf16[256,2560]{1,0:T(8,128)(2,1)}, bf16[256,2560]{1,0:T(8,128)(2,1)S(1)}, u32[]{:S(2)}, u32[]{:S(2)}) collective-permute-start(bf16[256,2560]{1,0:T(8,128)(2,1)} %fence.37.refs_0_), channel_id=1, source_target_pairs={{0,8},{4,12},{8,0},{12,4},{16,24},{20,28},{24,16},{28,20},{1,9},{5... | collective-permute-start | bytes 3932168 | tf_op jit(solution)/shard_map/ppermute | solution.py:79
  315.4 44.2 %collective-permute-start.25 = (bf16[1024,2560]{1,0:T(8,128)(2,1)}, bf16[1024,2560]{1,0:T(8,128)(2,1)}, u32[]{:S(2)}, u32[]{:S(2)}) collective-permute-start(bf16[1024,2560]{1,0:T(8,128)(2,1)} %assemble.9), channel_id=1, source_target_pairs={{0,4},{4,0},{8,12},{12,8},{16,20},{20,16},{24,28},{28,24},{1,5},{5... | collective-permute-start | bytes 15728648 | tf_op jit(solution)/shard_map/ppermute | solution.py:79
  319.0 37.0 %collective-permute-start.27 = (bf16[256,3072]{1,0:T(8,128)(2,1)}, bf16[256,3072]{1,0:T(8,128)(2,1)S(1)}, u32[]{:S(2)}, u32[]{:S(2)}) collective-permute-start(bf16[256,3072]{1,0:T(8,128)(2,1)} %fence.39.refs_0_), channel_id=1, source_target_pairs={{0,16},{4,20},{8,24},{12,28},{16,0},{20,4},{24,8},{28,12},{1,17},{... | collective-permute-start | bytes 4718600 | tf_op jit(solution)/shard_map/ppermute | solution.py:79
  320.0 37.5 %collective-permute-start.26 = (bf16[256,3072]{1,0:T(8,128)(2,1)}, bf16[256,3072]{1,0:T(8,128)(2,1)S(1)}, u32[]{:S(2)}, u32[]{:S(2)}) collective-permute-start(bf16[256,3072]{1,0:T(8,128)(2,1)} %fence.39.refs_0_), channel_id=1, source_target_pairs={{0,8},{4,12},{8,0},{12,4},{16,24},{20,28},{24,16},{28,20},{1,9},{5... | collective-permute-start | bytes 4718600 | tf_op jit(solution)/shard_map/ppermute | solution.py:79
  357.0 19.4 %collective-permute-start.28 = (bf16[128,3072]{1,0:T(8,128)(2,1)}, bf16[128,3072]{1,0:T(8,128)(2,1)S(1)}, u32[]{:S(2)}, u32[]{:S(2)}) collective-permute-start(bf16[128,3072]{1,0:T(8,128)(2,1)} %slice.721), channel_id=1, source_target_pairs={{0,8},{4,12},{8,0},{12,4},{16,24},{20,28},{24,16},{28,20},{1,9},{5... | collective-permute-start | bytes 2359304 | tf_op jit(solution)/shard_map/ppermute | solution.py:79
  358.6 19.2 %collective-permute-start.29 = (bf16[128,3072]{1,0:T(8,128)(2,1)}, bf16[128,3072]{1,0:T(8,128)(2,1)}, u32[]{:S(2)}, u32[]{:S(2)}) collective-permute-start(bf16[128,3072]{1,0:T(8,128)(2,1)} %slice.722), channel_id=1, source_target_pairs={{0,16},{4,20},{8,24},{12,28},{16,0},{20,4},{24,8},{28,12},{1,17},{... | collective-permute-start | bytes 2359304 | tf_op jit(solution)/shard_map/ppermute | solution.py:79
  368.7 160.9 %all-gather.15.cloned.1.call-start = ((), (), s32[]{:S(2)}) async-start(), calls=%async_computation.6 | async-start | bytes 5242880 | tf_op jit(solution)/shard_map/all_gather | solution.py:568
  383.0 37.6 %collective-permute-start.30 = (bf16[1024,3072]{1,0:T(8,128)(2,1)}, bf16[1024,3072]{1,0:T(8,128)(2,1)}, u32[]{:S(2)}, u32[]{:S(2)}) collective-permute-start(bf16[1024,3072]{1,0:T(8,128)(2,1)} %assemble.10.refs_0_), channel_id=1, source_target_pairs={{0,4},{4,0},{8,12},{12,8},{16,20},{20,16},{24,28},{28,24},{1,5},{5... | collective-permute-start | bytes 18874376 | tf_op jit(solution)/shard_map/ppermute | solution.py:79
  414.1 284.9 %reduce-scatter.6.cloned.1.call-start = ((), (), s32[]{:S(2)}) async-start(), calls=%async_computation.7 | async-start | bytes 5242880 | tf_op jit(solution)/shard_map/reduce_scatter | solution.py:577
  501.9 197.2 %reduce-scatter.8.cloned.1.call-start = ((), (), s32[]{:S(2)}) async-start(), calls=%async_computation.8 | async-start | bytes 5242880 | tf_op jit(solution)/shard_map/reduce_scatter | solution.py:577
  612.1 189.5 %reduce-scatter.10.cloned.1.call-start = ((), (), s32[]{:S(2)}) async-start(), calls=%async_computation.9 | async-start | bytes 5242880 | tf_op jit(solution)/shard_map/reduce_scatter | solution.py:602
  621.9 66.6 %collective-permute-start.34 = (bf16[1024,1536]{1,0:T(8,128)(2,1)}, bf16[1024,1536]{1,0:T(8,128)(2,1)S(1)}, u32[]{:S(2)}, u32[]{:S(2)}) collective-permute-start(bf16[1024,1536]{1,0:T(8,128)(2,1)} %add_convert_fusion.2), channel_id=1, source_target_pairs={{0,4},{4,0},{8,12},{12,8},{16,20},{20,16},{24,28},{28,24},{1,5},{5... | collective-permute-start | bytes 9437192 | tf_op jit(solution)/shard_map/ppermute | solution.py:79
  643.2 51.1 %collective-permute-start.35 = (bf16[1024,3072]{1,0:T(8,128)(2,1)}, bf16[1024,3072]{1,0:T(8,128)(2,1)}, u32[]{:S(2)}, u32[]{:S(2)}) collective-permute-start(bf16[1024,3072]{1,0:T(8,128)(2,1)} %add_convert_fusion), channel_id=1, source_target_pairs={{0,4},{4,0},{8,12},{12,8},{16,20},{20,16},{24,28},{28,24},{1,5},{5... | collective-permute-start | bytes 18874376 | tf_op jit(solution)/shard_map/ppermute | solution.py:79
  699.1 160.0 %reduce-scatter.12.cloned.1.call-start = ((), (), s32[]{:S(2)}) async-start(), calls=%async_computation.10 | async-start | bytes 5242880 | tf_op jit(solution)/shard_map/reduce_scatter | solution.py:602
  703.7 39.4 %collective-permute-start.37 = (bf16[256,1536]{1,0:T(8,128)(2,1)}, bf16[256,1536]{1,0:T(8,128)(2,1)}, u32[]{:S(2)}, u32[]{:S(2)}) collective-permute-start(bf16[256,1536]{1,0:T(8,128)(2,1)} %get-tuple-element.215.refs_3_), channel_id=1, source_target_pairs={{0,16},{4,20},{8,24},{12,28},{16,0},{20,4},{24,8},{28,12},{1,17},{... | collective-permute-start | bytes 2359304 | tf_op jit(solution)/shard_map/ppermute | solution.py:79
  705.1 39.3 %collective-permute-start.36 = (bf16[256,1536]{1,0:T(8,128)(2,1)}, bf16[256,1536]{1,0:T(8,128)(2,1)}, u32[]{:S(2)}, u32[]{:S(2)}) collective-permute-start(bf16[256,1536]{1,0:T(8,128)(2,1)} %get-tuple-element.216.refs_2_), channel_id=1, source_target_pairs={{0,8},{4,12},{8,0},{12,4},{16,24},{20,28},{24,16},{28,20},{1,9},{5... | collective-permute-start | bytes 2359304 | tf_op jit(solution)/shard_map/ppermute | solution.py:79
  706.6 50.5 %collective-permute-start.39 = (bf16[256,3072]{1,0:T(8,128)(2,1)}, bf16[256,3072]{1,0:T(8,128)(2,1)}, u32[]{:S(2)}, u32[]{:S(2)}) collective-permute-start(bf16[256,3072]{1,0:T(8,128)(2,1)} %get-tuple-element.189.refs_5_), channel_id=1, source_target_pairs={{0,16},{4,20},{8,24},{12,28},{16,0},{20,4},{24,8},{28,12},{1,17},{... | collective-permute-start | bytes 4718600 | tf_op jit(solution)/shard_map/ppermute | solution.py:79
  707.1 51.2 %collective-permute-start.38 = (bf16[256,3072]{1,0:T(8,128)(2,1)}, bf16[256,3072]{1,0:T(8,128)(2,1)}, u32[]{:S(2)}, u32[]{:S(2)}) collective-permute-start(bf16[256,3072]{1,0:T(8,128)(2,1)} %get-tuple-element.190.refs_4_), channel_id=1, source_target_pairs={{0,8},{4,12},{8,0},{12,4},{16,24},{20,28},{24,16},{28,20},{1,9},{5... | collective-permute-start | bytes 4718600 | tf_op jit(solution)/shard_map/ppermute | solution.py:79
  709.0 232.1 %all-gather.19.cloned.1.call-start = ((), (), s32[]{:S(2)}) async-start(), calls=%async_computation.13 | async-start | bytes 5242880 | tf_op jit(solution)/shard_map/all_gather | solution.py:642
  741.8 16.5 %collective-permute-start.42 = (f32[2,2560]{1,0:T(2,128)S(1)}, f32[2,2560]{1,0:T(2,128)S(1)}, u32[]{:S(2)}, u32[]{:S(2)}) collective-permute-start(f32[2,2560]{1,0:T(2,128)S(1)} %pad_maximum_fusion.17), channel_id=1, source_target_pairs={{3,0},{7,4},{11,8},{15,12},{19,16},{23,20},{27,24},{31,28}} | collective-permute-start | bytes 61448 | tf_op jit(solution)/shard_map/ppermute | solution.py:162
  784.9 16.7 %collective-permute-start.43 = (f32[16,2560]{1,0:T(8,128)S(1)}, f32[16,2560]{1,0:T(8,128)S(1)}, u32[]{:S(2)}, u32[]{:S(2)}) collective-permute-start(f32[16,2560]{1,0:T(8,128)S(1)} %slice.591), channel_id=1, source_target_pairs={{1,0},{2,1},{3,2},{5,4},{6,5},{7,6},{9,8},{10,9},{11,10},{13,12},{... | collective-permute-start | bytes 491528 | tf_op jit(solution)/shard_map/ppermute | solution.py:162
  831.6 190.4 %all-gather.25.cloned.1.call-start = ((), (), s32[]{:S(2)}) async-start(), calls=%async_computation.16 | async-start | bytes 5242880 | tf_op jit(solution)/shard_map/all_gather | solution.py:642
  839.6 19.6 %collective-permute-start.44 = (bf16[1024,2560]{1,0:T(8,128)(2,1)}, bf16[1024,2560]{1,0:T(8,128)(2,1)}, u32[]{:S(2)}, u32[]{:S(2)}) collective-permute-start(bf16[1024,2560]{1,0:T(8,128)(2,1)} %convolution_convert_fusion.5), channel_id=1, source_target_pairs={{0,4},{4,0},{8,12},{12,8},{16,20},{20,16},{24,28},{28,24},{1,5},{5... | collective-permute-start | bytes 15728648 | tf_op jit(solution)/shard_map/ppermute | solution.py:79
  839.6 308.7 %all-gather.21.cloned.1.call-start = ((), (), s32[]{:S(2)}) async-start(), calls=%async_computation.14 | async-start | bytes 5242880 | tf_op jit(solution)/shard_map/all_gather | solution.py:652
  876.0 176.3 %collective-permute-start.52 = (bf16[256,2560]{1,0:T(8,128)(2,1)}, bf16[256,2560]{1,0:T(8,128)(2,1)}, u32[]{:S(2)}, u32[]{:S(2)}) collective-permute-start(bf16[256,2560]{1,0:T(8,128)(2,1)} %get-tuple-element.197), channel_id=1, source_target_pairs={{0,8},{4,12},{8,0},{12,4},{16,24},{20,28},{24,16},{28,20},{1,9},{5... | collective-permute-start | bytes 3932168 | tf_op jit(solution)/shard_map/ppermute | solution.py:79
  877.5 174.8 %collective-permute-start.51 = (bf16[256,2560]{1,0:T(8,128)(2,1)}, bf16[256,2560]{1,0:T(8,128)(2,1)}, u32[]{:S(2)}, u32[]{:S(2)}) collective-permute-start(bf16[256,2560]{1,0:T(8,128)(2,1)} %get-tuple-element.198), channel_id=1, source_target_pairs={{0,16},{4,20},{8,24},{12,28},{16,0},{20,4},{24,8},{28,12},{1,17},{... | collective-permute-start | bytes 3932168 | tf_op jit(solution)/shard_map/ppermute | solution.py:79
  941.2 242.5 %all-gather.23.cloned.1.call-start = ((), (), s32[]{:S(2)}) async-start(), calls=%async_computation.15 | async-start | bytes 5242880 | tf_op jit(solution)/shard_map/all_gather | solution.py:652
  1044.0 22.1 %collective-permute-start.45 = (bf16[4,4,26752]{2,1,0:T(4,128)(2,1)S(1)}, bf16[4,4,26752]{2,1,0:T(4,128)(2,1)}, u32[]{:S(2)}, u32[]{:S(2)}) collective-permute-start(bf16[4,4,26752]{2,1,0:T(4,128)(2,1)S(1)} %slice.757), channel_id=1, source_target_pairs={{0,16},{4,20},{8,24},{12,28},{16,0},{20,4},{24,8},{28,12},{1,17},{... | collective-permute-start | bytes 2568200 | tf_op jit(solution)/shard_map/ppermute | solution.py:79
  1051.5 37.6 %collective-permute-start.60 = (bf16[1024,2560]{1,0:T(8,128)(2,1)}, bf16[1024,2560]{1,0:T(8,128)(2,1)}, u32[]{:S(2)}, u32[]{:S(2)}) collective-permute-start(bf16[1024,2560]{1,0:T(8,128)(2,1)} %convolution_convert_fusion), channel_id=1, source_target_pairs={{0,4},{4,0},{8,12},{12,8},{16,20},{20,16},{24,28},{28,24},{1,5},{5... | collective-permute-start | bytes 15728648 | tf_op jit(solution)/shard_map/ppermute | solution.py:79
  1051.5 18.7 %collective-permute-start.55 = (bf16[1024,2560]{1,0:T(8,128)(2,1)}, bf16[1024,2560]{1,0:T(8,128)(2,1)}, u32[]{:S(2)}, u32[]{:S(2)}) collective-permute-start(bf16[1024,2560]{1,0:T(8,128)(2,1)} %convolution_convert_fusion.2), channel_id=1, source_target_pairs={{0,4},{4,0},{8,12},{12,8},{16,20},{20,16},{24,28},{28,24},{1,5},{5... | collective-permute-start | bytes 15728648 | tf_op jit(solution)/shard_map/ppermute | solution.py:79
  1052.0 206.1 %reduce-scatter.14.cloned.1.call-start = ((), (), s32[]{:S(2)}) async-start(), calls=%async_computation.11 | async-start | bytes 4915200 | tf_op jit(solution)/shard_map/reduce_scatter | solution.py:665
  1055.9 20.4 %collective-permute-start.53 = (bf16[128,2560]{1,0:T(8,128)(2,1)}, bf16[128,2560]{1,0:T(8,128)(2,1)S(1)}, u32[]{:S(2)}, u32[]{:S(2)}) collective-permute-start(bf16[128,2560]{1,0:T(8,128)(2,1)} %get-tuple-element.101), channel_id=1, source_target_pairs={{0,8},{4,12},{8,0},{12,4},{16,24},{20,28},{24,16},{28,20},{1,9},{5... | collective-permute-start | bytes 1966088 | tf_op jit(solution)/shard_map/ppermute | solution.py:79
  1057.4 22.7 %collective-permute-start.54 = (bf16[128,2560]{1,0:T(8,128)(2,1)}, bf16[128,2560]{1,0:T(8,128)(2,1)}, u32[]{:S(2)}, u32[]{:S(2)}) collective-permute-start(bf16[128,2560]{1,0:T(8,128)(2,1)} %get-tuple-element.102), channel_id=1, source_target_pairs={{0,16},{4,20},{8,24},{12,28},{16,0},{20,4},{24,8},{28,12},{1,17},{... | collective-permute-start | bytes 1966088 | tf_op jit(solution)/shard_map/ppermute | solution.py:79
  1068.6 44.5 %collective-permute-start.46 = (bf16[2,4,26752]{2,1,0:T(4,128)(2,1)}, bf16[2,4,26752]{2,1,0:T(4,128)(2,1)}, u32[]{:S(2)}, u32[]{:S(2)}) collective-permute-start(bf16[2,4,26752]{2,1,0:T(4,128)(2,1)} %slice.759), channel_id=1, source_target_pairs={{0,8},{4,12},{8,0},{12,4},{16,24},{20,28},{24,16},{28,20},{1,9},{5... | collective-permute-start | bytes 1284104 | tf_op jit(solution)/shard_map/ppermute | solution.py:79
  1074.8 32.2 %collective-permute-start.56 = (bf16[256,2560]{1,0:T(8,128)(2,1)}, bf16[256,2560]{1,0:T(8,128)(2,1)S(1)}, u32[]{:S(2)}, u32[]{:S(2)}) collective-permute-start(bf16[256,2560]{1,0:T(8,128)(2,1)} %get-tuple-element.104), channel_id=1, source_target_pairs={{0,16},{4,20},{8,24},{12,28},{16,0},{20,4},{24,8},{28,12},{1,17},{... | collective-permute-start | bytes 3932168 | tf_op jit(solution)/shard_map/ppermute | solution.py:79
  1076.3 33.7 %collective-permute-start.57 = (bf16[256,2560]{1,0:T(8,128)(2,1)}, bf16[256,2560]{1,0:T(8,128)(2,1)S(1)}, u32[]{:S(2)}, u32[]{:S(2)}) collective-permute-start(bf16[256,2560]{1,0:T(8,128)(2,1)} %get-tuple-element.105), channel_id=1, source_target_pairs={{0,8},{4,12},{8,0},{12,4},{16,24},{20,28},{24,16},{28,20},{1,9},{5... | collective-permute-start | bytes 3932168 | tf_op jit(solution)/shard_map/ppermute | solution.py:79
  1111.1 31.9 %collective-permute-start.61 = (bf16[256,2560]{1,0:T(8,128)(2,1)}, bf16[256,2560]{1,0:T(8,128)(2,1)S(1)}, u32[]{:S(2)}, u32[]{:S(2)}) collective-permute-start(bf16[256,2560]{1,0:T(8,128)(2,1)} %get-tuple-element.109), channel_id=1, source_target_pairs={{0,16},{4,20},{8,24},{12,28},{16,0},{20,4},{24,8},{28,12},{1,17},{... | collective-permute-start | bytes 3932168 | tf_op jit(solution)/shard_map/ppermute | solution.py:79
  1111.5 31.9 %collective-permute-start.62 = (bf16[256,2560]{1,0:T(8,128)(2,1)}, bf16[256,2560]{1,0:T(8,128)(2,1)S(1)}, u32[]{:S(2)}, u32[]{:S(2)}) collective-permute-start(bf16[256,2560]{1,0:T(8,128)(2,1)} %get-tuple-element.110), channel_id=1, source_target_pairs={{0,8},{4,12},{8,0},{12,4},{16,24},{20,28},{24,16},{28,20},{1,9},{5... | collective-permute-start | bytes 3932168 | tf_op jit(solution)/shard_map/ppermute | solution.py:79
  1115.9 67.8 %collective-permute-start.47 = (bf16[1,4,26752]{2,1,0:T(4,128)(2,1)}, bf16[1,4,26752]{2,1,0:T(4,128)(2,1)S(1)}, u32[]{:S(2)}, u32[]{:S(2)}) collective-permute-start(bf16[1,4,26752]{2,1,0:T(4,128)(2,1)} %slice.761), channel_id=1, source_target_pairs={{0,4},{4,0},{8,12},{12,8},{16,20},{20,16},{24,28},{28,24},{1,5},{5... | collective-permute-start | bytes 642056 | tf_op jit(solution)/shard_map/ppermute | solution.py:79
  1119.5 38.0 %collective-permute-start.58 = (bf16[128,2560]{1,0:T(8,128)(2,1)}, bf16[128,2560]{1,0:T(8,128)(2,1)S(1)}, u32[]{:S(2)}, u32[]{:S(2)}) collective-permute-start(bf16[128,2560]{1,0:T(8,128)(2,1)} %get-tuple-element.106), channel_id=1, source_target_pairs={{0,8},{4,12},{8,0},{12,4},{16,24},{20,28},{24,16},{28,20},{1,9},{5... | collective-permute-start | bytes 1966088 | tf_op jit(solution)/shard_map/ppermute | solution.py:79
  1120.0 37.5 %collective-permute-start.59 = (bf16[128,2560]{1,0:T(8,128)(2,1)}, bf16[128,2560]{1,0:T(8,128)(2,1)}, u32[]{:S(2)}, u32[]{:S(2)}) collective-permute-start(bf16[128,2560]{1,0:T(8,128)(2,1)} %get-tuple-element.107), channel_id=1, source_target_pairs={{0,16},{4,20},{8,24},{12,28},{16,0},{20,4},{24,8},{28,12},{1,17},{... | collective-permute-start | bytes 1966088 | tf_op jit(solution)/shard_map/ppermute | solution.py:79
  1148.4 21.1 %collective-permute-start.63 = (bf16[128,2560]{1,0:T(8,128)(2,1)}, bf16[128,2560]{1,0:T(8,128)(2,1)}, u32[]{:S(2)}, u32[]{:S(2)}) collective-permute-start(bf16[128,2560]{1,0:T(8,128)(2,1)} %get-tuple-element.111), channel_id=1, source_target_pairs={{0,8},{4,12},{8,0},{12,4},{16,24},{20,28},{24,16},{28,20},{1,9},{5... | collective-permute-start | bytes 1966088 | tf_op jit(solution)/shard_map/ppermute | solution.py:79
  1149.9 19.6 %collective-permute-start.64 = (bf16[128,2560]{1,0:T(8,128)(2,1)}, bf16[128,2560]{1,0:T(8,128)(2,1)}, u32[]{:S(2)}, u32[]{:S(2)}) collective-permute-start(bf16[128,2560]{1,0:T(8,128)(2,1)} %get-tuple-element.112), channel_id=1, source_target_pairs={{0,16},{4,20},{8,24},{12,28},{16,0},{20,4},{24,8},{28,12},{1,17},{... | collective-permute-start | bytes 1966088 | tf_op jit(solution)/shard_map/ppermute | solution.py:79
  1194.9 22.7 %collective-permute-start.67 = (bf16[128,1536]{1,0:T(8,128)(2,1)}, bf16[128,1536]{1,0:T(8,128)(2,1)S(1)}, u32[]{:S(2)}, u32[]{:S(2)}) collective-permute-start(bf16[128,1536]{1,0:T(8,128)(2,1)} %get-tuple-element.115), channel_id=1, source_target_pairs={{0,8},{4,12},{8,0},{12,4},{16,24},{20,28},{24,16},{28,20},{1,9},{5... | collective-permute-start | bytes 1179656 | tf_op jit(solution)/shard_map/ppermute | solution.py:79
  1196.7 20.9 %collective-permute-start.68 = (bf16[128,1536]{1,0:T(8,128)(2,1)}, bf16[128,1536]{1,0:T(8,128)(2,1)S(1)}, u32[]{:S(2)}, u32[]{:S(2)}) collective-permute-start(bf16[128,1536]{1,0:T(8,128)(2,1)} %get-tuple-element.116), channel_id=1, source_target_pairs={{0,16},{4,20},{8,24},{12,28},{16,0},{20,4},{24,8},{28,12},{1,17},{... | collective-permute-start | bytes 1179656 | tf_op jit(solution)/shard_map/ppermute | solution.py:79
  1207.6 18.1 %collective-permute-start.65 = (bf16[128,3072]{1,0:T(8,128)(2,1)}, bf16[128,3072]{1,0:T(8,128)(2,1)S(1)}, u32[]{:S(2)}, u32[]{:S(2)}) collective-permute-start(bf16[128,3072]{1,0:T(8,128)(2,1)} %get-tuple-element.113), channel_id=1, source_target_pairs={{0,8},{4,12},{8,0},{12,4},{16,24},{20,28},{24,16},{28,20},{1,9},{5... | collective-permute-start | bytes 2359304 | tf_op jit(solution)/shard_map/ppermute | solution.py:79
  1209.1 16.8 %collective-permute-start.66 = (bf16[128,3072]{1,0:T(8,128)(2,1)}, bf16[128,3072]{1,0:T(8,128)(2,1)S(1)}, u32[]{:S(2)}, u32[]{:S(2)}) collective-permute-start(bf16[128,3072]{1,0:T(8,128)(2,1)} %get-tuple-element.114), channel_id=1, source_target_pairs={{0,16},{4,20},{8,24},{12,28},{16,0},{20,4},{24,8},{28,12},{1,17},{... | collective-permute-start | bytes 2359304 | tf_op jit(solution)/shard_map/ppermute | solution.py:79
  (133 other events, 1002.5 us)
Sparse Core Ops, SparseCore 0:
  13.4 61.5 all-gather.16
  368.8 79.7 all-gather.12
  450.2 79.2 all-gather.14
  531.7 75.2 reduce-scatter.5
  612.2 75.2 reduce-scatter.7
  699.3 76.6 reduce-scatter.9
  778.4 80.7 reduce-scatter.11
  860.8 80.3 all-gather.18
  942.7 79.2 all-gather.24
  1023.5 79.2 all-gather.20
  1104.4 79.2 all-gather.22
  1185.9 72.2 reduce-scatter.13

commit v6 on v5

--- a/solution.py
+++ b/solution.py
@@ -171,15 +171,54 @@
     return total
 
 
-def small_plain(halves, size, n):
-    mask = jnp.arange(size) ^ lax.axis_index("dp")
-    rows = jnp.concatenate(halves).reshape(size, n, -1)
-    return jnp.take(rows, (mask & 1) * (size // 2) + (mask >> 1), axis=0, mode="clip").transpose(1, 0, 2)
-
-
-def z_gather(own, n):
+class Line:
+    def __init__(self, own, n):
+        self.own, self.n, self.rounds = own, n, []
+
+    def go(self, *others):
+        k = len(self.rounds) + 1
+        if k >= self.n:
+            return ()
+        right, left = fence(self.rounds[-1], *others) if self.rounds else (self.own, self.own)
+        right = lax.ppermute(right, "tensor", [(s, s + 1) for s in range(k - 1, self.n - 1)])
+        left = lax.ppermute(left, "tensor", [(s, s - 1) for s in range(1, self.n - k + 1)])
+        self.rounds.append((right, left))
+        return self.rounds[-1]
+
+    def place(self, out, at):
+        turn = lax.axis_index("tensor")
+        out = lax.dynamic_update_slice(out, self.own[None, None], (turn, at, 0, 0))
+        while len(self.rounds) < self.n - 1:
+            self.go()
+        for k in range(1, self.n):
+            piece = self.rounds[k - 1][1] + self.rounds[self.n - k - 1][0]
+            out = lax.dynamic_update_slice(out, piece[None, None], ((turn + k) % self.n, at, 0, 0))
+        return out
+
+
+def small_begin(own, size):
+    if size == 8:
+        return [own, exchange(own, 1, size), exchange(own, 2, size)]
+    rows = own[None]
+    for bit in range(1, size.bit_length() - 1):
+        rows = jnp.concatenate([rows, exchange(rows, bit, size)])
+    return [rows]
+
+
+def small_end(some, size):
+    if size == 8:
+        own, by_x, by_y = some
+        cut = own.shape[0] // 2
+        far = jnp.concatenate([exchange(by_x[:cut], 2, size), exchange(by_y[cut:], 1, size)])
+        rows = jnp.stack([own, by_x, by_y, far])
+    else:
+        (rows,) = some
+    return jnp.concatenate([rows, exchange(rows, 0, size)])
+
+
+def z_gather(own, n, *others):
     turn = lax.axis_index("tensor")
-    blocks = jnp.stack([own] + [z_shift(own, -k, n) for k in range(1, n)])
+    blocks = jnp.stack([own] + fence([z_shift(own, -k, n) for k in range(1, n)], *others))
     blocks = jnp.take(blocks, (jnp.arange(n) - turn) % n, axis=0, mode="clip")
     return blocks.transpose(1, 0, 2).reshape(own.shape[0], -1)
 
@@ -193,14 +232,15 @@
     return z_scatter(values[0], n)
 
 
+def basis_spots(size, rows):
+    if squared(size, rows):
+        turns = ((0, 0), (0, 1), (2, 0), (2, 1), (6, 1), (6, 0), (4, 0), (4, 1))
+        return [(core | mask, part) for core in range(2) for mask, part in turns], 2
+    return [(core | q << 1, 0) for core in range(2) for q in range(size // 2)], 1
+
+
 def basis(size, rows, place):
-    if squared(size, rows):
-        parts = 2
-        spots = [(core | mask, part) for core in range(2) for mask, part in
-                 ((0, 0), (0, 1), (2, 0), (2, 1), (6, 1), (6, 0), (4, 0), (4, 1))]
-    else:
-        parts = 1
-        spots = [(core | q << 1, 0) for core in range(2) for q in range(size // 2)]
+    spots, parts = basis_spots(size, rows)
     masks, which = (jnp.asarray(np.array(v, np.int32)) for v in zip(*spots))
     table = (place ^ masks) * parts + which
     spots = jnp.arange(table.shape[0], dtype=jnp.int32)
@@ -280,19 +320,25 @@
     return (lanes >= at * head) & (lanes < (at + 1) * head)
 
 
-def fill_dense(w_ref, dense_ref):
-    head = w_ref.shape[0]
-    blocks = w_ref[...].astype(F32)
-    for k in range(dense_ref.shape[0] // head):
-        block = jnp.where(head_mask(head, k, dense_ref.shape[0]), blocks, 0.0)
-        dense_ref[k * head : (k + 1) * head, :] = block.astype(BF)
+def fill_dense(w_ref, order_ref, dense_ref):
+    head, count = order_ref.shape
+    pad = count // w_ref.shape[0]
+    width = dense_ref.shape[0]
+    for gate in range(2):
+        rows = w_ref[:, gate * pad : (gate + 1) * pad, :].reshape(count, width)
+        rows = dot(order_ref[...], rows)
+        for k in range(width // head):
+            lanes = lax.broadcasted_iota(jnp.int32, (head, width), 1)
+            block = jnp.where((lanes >= k * head) & (lanes < (k + 1) * head), rows, 0.0)
+            dense_ref[k * head : (k + 1) * head, gate * width : (gate + 1) * width] = block.astype(BF)
 
 
 def forward_kernel(
-    live_ref, pre_ref, par_ref, w_ref, conv_ref, decay_ref, ig_ref, dg_ref, state_ref, prod_ref, rec_ref, dense_ref
+    live_ref, pre_ref, par_ref, w_ref, order_ref, conv_ref, decay_ref, ig_ref, dg_ref, state_ref, prod_ref,
+    rec_ref, dense_ref,
 ):
     rows, width = conv_ref.shape
-    fill_dense(w_ref, dense_ref)
+    fill_dense(w_ref, order_ref, dense_ref)
     live = live_ref[0]
     rec_ref[...] = jnp.where(row_ids(rows + HALO, width, -HALO) < live, pre_ref[...], 0.0)
     par = [par_ref[k : k + 1, :] for k in range(8)]
@@ -371,14 +417,14 @@
 
 
 def backward_kernel(
-    live_ref, pre_ref, par_ref, w_ref, lam_ref, reach_ref, edge_ref, decay_ref, conv_ref, ig_ref, dg_ref, state_ref, prod_ref, cin_ref,
+    live_ref, pre_ref, par_ref, w_ref, order_ref, lam_ref, reach_ref, edge_ref, decay_ref, conv_ref, ig_ref, dg_ref, state_ref, prod_ref, cin_ref,
     drec_ref, dpar_ref, dw_ref, rec_ref, dconv_ref, full_ref, dw_acc, dense_ref,
 ):
     rows, width = conv_ref.shape
     live = live_ref[0]
     rec_ref[...] = jnp.where(row_ids(rows + HALO, width, -HALO) < live, pre_ref[...], 0.0)
     par = [par_ref[k : k + 1, :] for k in range(8)]
-    fill_dense(w_ref, dense_ref)
+    fill_dense(w_ref, order_ref, dense_ref)
     cin = cin_ref[:1, :]
     edge = edge_ref[:1, :]
     full_ref[:SLAB, :] = jnp.broadcast_to(cin, (SLAB, width))
@@ -432,8 +478,11 @@
     steps = width // GROUP
     specs = []
     for array in arrays:
-        if array.ndim == 3:
-            specs.append(pl.BlockSpec((pl.squeezed,) + array.shape[1:], lambda j, s: (j, 0, 0)))
+        if array.ndim == 4:
+            block = (array.shape[0], pl.squeezed) + array.shape[2:]
+            specs.append(pl.BlockSpec(block, lambda j, s: (0, j, 0, 0)))
+        elif array.shape[1] != width:
+            specs.append(pl.BlockSpec(array.shape, lambda j, s: (0, 0)))
         else:
             specs.append(pl.BlockSpec((array.shape[0], GROUP), lambda j, s: (0, j)))
     out_specs, out_shapes = [], []
@@ -494,11 +543,14 @@
     live_count = (lengths - turn * rows).astype(jnp.int32)
     live = (lax.iota(jnp.int32, rows)[:, None] < live_count).astype(F32)
 
-    small = [w_lru.transpose(2, 0, 1, 3).reshape(-1), chan.reshape(-1), gains.reshape(-1)]
-    small = jnp.concatenate(small).astype(BF)
-    count, cols = small.shape[0], w_gelu.shape[1]
-    small = jnp.pad(small, (0, -count % (16 * cols))).reshape(-1, cols)
-    whole = jnp.concatenate([w_rec.astype(BF), w_gelu.astype(BF), small])
+    cols = w_gelu.shape[1]
+    pad = -(-part // 16) * 16
+    own_lru = jnp.pad(w_lru.transpose(0, 2, 1, 3).reshape(2, part, cols), ((0, 0), (0, pad - part), (0, 0)))
+    own_chan = jnp.zeros((8, heads_own, head), F32)
+    own_chan = lax.dynamic_update_slice(own_chan, chan, (0, 0, place * part)).reshape(8, cols)
+    own_gain = jnp.pad(gains.reshape(1, -1), ((0, 7), (0, cols - gains.size)))
+    small = jnp.concatenate([own_lru.reshape(2 * pad, cols), own_chan, own_gain])
+    whole = jnp.concatenate([w_rec, w_gelu, small]).astype(BF)
     own_dn = w_down.T.astype(BF)
     own_gu = jnp.concatenate([w_mlp_in[0], w_mlp_in[1]], axis=1).astype(BF)
     some_dn = spread_begin(own_dn, size)
@@ -507,20 +559,26 @@
         whole[:, k * d_own : (k + 1) * d_own].transpose(1, 0, 2).reshape(d_own, width) for k in range(2)
     )
     some_r = spread_begin(z_rec, size, *some_dn[1:])
-    some_small = spread_begin(whole[:, 2 * d_own :].reshape(n, -1), size)
-    z_out = z_gather(*fence([w_out.T.astype(BF)], z_rec), n)
+    some_small = small_begin(whole[:, 2 * d_own :].reshape(-1, cols), size)
     w_r, came_r = spread_end(some_r, size, (), ())
-    small, _ = spread_end(some_small, size, (), ())
-    small = small_plain(fence(small, *came_r), size, n)[..., :count]
-
-    gain = small[0, :, -gains.size :].reshape(size, 2, d_own).transpose(1, 0, 2).reshape(2, d_model)
-    gain = permute_gain(gain, table).astype(F32)
-    chans = small[..., w_lru.size : w_lru.size + chan.size].reshape((n, size) + chan.shape)
-    chans = chans.transpose(2, 0, 3, 1, 4).reshape(8, width).astype(F32)
+    small = small_end(some_small, size).reshape(size, n, -1, cols)
+
+    spots, parts = basis_spots(size, d_own)
+    unit = d_own // parts
+    gain = small[:, 0, 2 * pad + 8, : gains.size].reshape(size, 2, d_own)
+    gain = [gain[(mask & 1) * (size // 2) + (mask >> 1), :, k * unit : (k + 1) * unit] for mask, k in spots]
+    gain = jnp.concatenate(gain, axis=1).astype(F32)
+    chans = jnp.sum(small[:, :, 2 * pad : 2 * pad + 8].astype(F32), axis=0)
+    chans = chans.transpose(1, 0, 2).reshape(8, width)
     par = jnp.concatenate([chans[:7], -8.0 * jax.nn.softplus(-chans[7:])])
     each = n // groups
-    lru = small[..., : w_lru.size].reshape(groups, each, head, 2, heads_own * head)
-    lru = lru.transpose(0, 2, 3, 1, 4).reshape(groups, head, 2 * GROUP)
+    lru = small
+    if each > 1:
+        lru = lru.reshape(size, groups, each, -1, cols).transpose(0, 1, 3, 2, 4).reshape(size, groups, -1, GROUP)
+    spot, row = jnp.arange(size * pad) // pad, jnp.arange(size * pad) % pad
+    spot = place ^ (spot // (size // 2) | (spot % (size // 2)) << 1)
+    row = jnp.where(row < part, spot * part + row, head)
+    order = (jnp.arange(head)[:, None] == row[None, :]).astype(BF)
 
     main = lax.dynamic_slice_in_dim(tokens, turn * rows, rows)
     before = lax.dynamic_slice_in_dim(tokens, jnp.maximum(turn * rows - HALO, 0), HALO)
@@ -536,7 +594,7 @@
     some_g = spread_begin(z_gelu, size, *came_r)
     rec_pre = wide_dot(first, w_r)
     conv, decay, ig, dg, state, prod = kernel_call(
-        forward_kernel, live_count, [rec_pre, par, lru], [keep] * 6,
+        forward_kernel, live_count, [rec_pre, par, lru, order], [keep] * 6,
         [((rows + HALO, GROUP), F32), dense], "recurrence",
     )
     ends = jnp.concatenate([prod[-1:], state[-1:]])
@@ -544,7 +602,8 @@
     carry = jnp.zeros((1, width), F32)
     for end in came[::-1]:
         carry = end[1:] + end[:1] * carry
-    w_g, came_g = spread_end(some_g, size, (rec_pre, z_out), (ends,))
+    z_out = z_gather(*fence([w_out.T.astype(BF)], z_rec), n, ends)
+    w_g, came_g = spread_end(some_g, size, (rec_pre,), (ends, z_out))
     some_o = spread_begin(z_out, size, *came_g, ends)
     branch_pre = wide_dot(first_own, w_g)
     recurrent = (state + prod * carry) * live
@@ -555,7 +614,7 @@
     second_unit = hidden * second_rate
     second_own = (second_unit * gain[1]).astype(BF)
     some_gu = spread_begin(own_gu, size, *came_o)
-    w_gu, came_gu = spread_end(some_gu, size, (), (second_own,))
+    w_gu, came_gu = spread_end(some_gu, size, (second_own,), ())
     w_dn, _ = spread_end(some_dn, size, came_gu, ())
     w_gu, w_dn = assemble(w_gu), assemble(w_dn)
     late = fence([table], second_own)[0]
@@ -625,16 +684,19 @@
     (lam,) = fence([lam], *came_mlp)
     drec, dpar, d_lru = kernel_call(
         backward_kernel, live_count,
-        [rec_pre, par, lru, lam, reach, tall(arriving, (SLAB, width)), decay, conv, ig, dg, state, prod, tall(carry, (SLAB, width))],
+        [rec_pre, par, lru, order, lam, reach, tall(arriving, (SLAB, width)), decay, conv, ig, dg, state, prod, tall(carry, (SLAB, width))],
         [(rows + HALO, width, F32), (8, width, F32), (head, 2 * GROUP, BF)],
         [((rows + HALO, GROUP), F32), ((rows + 2 * HALO, GROUP), F32), ((rows + SLAB, GROUP), F32), ((GROUP, 2 * GROUP), F32), dense],
         "recurrence_back",
     )
-    (edge_rows,) = fence([z_shift(drec[:HALO], -1, n, False)], mlp_sums[0])
+    line_0 = Line(mlp_result(0, mlp_sums[0]), n)
+    (edge_rows,) = fence([z_shift(drec[:HALO], -1, n, False)], line_0.own)
+    came_0 = line_0.go()
     rec_low = (drec[HALO:] + jnp.pad(edge_rows, ((rows - HALO, 0), (0, 0)))) * live
     rec_low = rec_low.astype(BF)
     (pre_low,) = fence([pre_low], drec)
-    grad_first = wide_back(pre_low, w_g) + wide_back(rec_low, w_r)
+    (grad_first,) = fence([wide_back(pre_low, w_g) + wide_back(rec_low, w_r)], *came_0)
+    came_0 = line_0.go()
     first_unit = inputs * first_rate
     gain_one = jnp.sum(grad_first * first_unit, axis=0)
     grad_tokens = grad_hidden + norm_back(grad_first, first_unit, first_rate, gain[0])
@@ -644,26 +706,29 @@
     sum_o = by_cols(hidden_low, mixed)
     pre_low, rec_low = fence([pre_low, rec_low], sum_o.terms[1])
     sum_g, sum_r = by_cols(first_own, pre_low), by_cols(first_own, rec_low)
-    results = [mlp_result(h, mlp_sum) for h, mlp_sum in enumerate(fence(mlp_sums, sum_o.terms[1]))]
-    got_o = sum_o.hop(sum_o.sources())
-    sum_o.hop(fence(sum_o.sources(), gathered[0]))
-    got_g = sum_g.hop(fence(sum_g.sources(), gathered[0]))
-    results = fence(results, gathered[0])
-    results = [lax.all_gather(result, "tensor", axis=0) for result in results]
-    sum_g.hop(fence(sum_g.sources(), gathered[1]))
-    got_r = sum_r.hop(fence(sum_r.sources(), gathered[1], *got_g))
-    d_lru, dpar = fence([d_lru, dpar], gathered[1])
-    sum_r.hop(fence(sum_r.sources(), results[0]))
+    line_1 = Line(mlp_result(1, *fence(mlp_sums[1:], sum_o.terms[1])), n)
+    got_o = sum_o.hop(fence(sum_o.sources(), line_1.own, *came_0))
+    came_0, came_1 = line_0.go(), line_1.go()
+    got_g = sum_g.hop(fence(sum_g.sources(), *got_o))
     if sum_dn.square:
-        sum_dn.hop(fence(sum_dn.sources(), results[0]))
-        sum_gu.hop(fence(sum_gu.sources(), results[0]))
-    tokens_out = interleave(*fence(gathered, results[0])).reshape(n * rows, d_model)
+        sum_dn.hop(fence(sum_dn.sources(), *got_o))
+        sum_gu.hop(fence(sum_gu.sources(), *got_o))
+    pause = (gathered[0], *came_0, *came_1, *got_g)
+    sum_o.hop(fence(sum_o.sources(), *pause))
+    got_r = sum_r.hop(fence(sum_r.sources(), *pause))
+    came_1 = line_1.go(gathered[0], *got_g)
+    sum_g.hop(fence(sum_g.sources(), *pause))
+    pause = (gathered[1], *came_1, *got_r)
+    sum_r.hop(fence(sum_r.sources(), *pause))
+    d_lru, dpar = fence([d_lru, dpar], *pause)
+    line_1.go(gathered[1])
+    tokens_out = interleave(*fence(gathered, *got_r)).reshape(n * rows, d_model)
     g_gu, g_dn = sum_gu.finish().astype(F32), sum_dn.finish().astype(F32)
     owned = jnp.stack([total.finish().reshape(d_own, n, width // n) for total in (sum_o, sum_g, sum_r)])
-    (owned,) = fence([owned.transpose(2, 0, 1, 3)], results[1])
-    output = interleave(*results).reshape(n * rows, d_model)
-    owned = lax.psum_scatter(owned, "tensor", scatter_dimension=0).astype(F32)
+    owned = lax.psum_scatter(owned.transpose(2, 0, 1, 3), "tensor", scatter_dimension=0).astype(F32)
     g_o, g_g, g_r = owned[0], owned[1], owned[2]
+    output = line_0.place(jnp.zeros((n, 2, half, d_model), BF), 0)
+    output = line_1.place(output, 1).reshape(n * rows, d_model)
 
     d_gain = permute_gain(jnp.stack([gain_one, gain_two]), inverse)
     d_chan = jnp.concatenate([dpar[:7], dpar[7:] * 8.0 * jax.nn.sigmoid(-chans[7:])])

time: 1280 us -> 1380 us (1.078)
  waiting for transfers between devices: 467 us -> 517 us
  other arithmetic: 129 us -> 148 us
  starting transfers between devices: 81.9 us -> 97 us
  local copies, waits for them, and re-layouts: 135 us -> 150 us
    ppermute x0 -> x12, waiting for transfers between devices: none -> 197 us  [the longest x6 161 us: go(): lax.ppermute(left, 'tensor', [(s, s - 1) for s in range(1, self.n - k + 1)])]
    all_gather x2, waiting for transfers between devices: 126 us -> 0.01 us  [on_device(): lax.all_gather(grad_tokens[h * half:(h + 1) * half], 'tensor', axis=0)]
    unnamed x244 -> x292, local copies, waits for them, and re-layouts: 38.7 us -> 60.4 us
    ppermute x0 -> x12, starting transfers between devices: none -> 20.6 us  [the longest x6 12.8 us: go(): lax.ppermute(right, 'tensor', [(s, s + 1) for s in range(k - 1, self.n -...]
    dynamic_update_slice x0 -> x6, other arithmetic: none -> 16.9 us  [place(): lax.dynamic_update_slice(out, piece[None, None], ((turn + k) % self.n, at...]
    ppermute x56 -> x58, waiting for transfers between devices: 188 us -> 171 us  [exchange(): return lax.ppermute(values, 'dp', [(k, k ^ 1 << bit) for k in range(size)])]
    reduce_scatter x1, waiting for transfers between devices: 26.4 us -> 41.9 us  [on_device(): lax.psum_scatter(owned.transpose(2, 0, 1, 3), 'tensor', scatter_dimension=0)]
    ppermute x56 -> x58, starting transfers between devices: 55 us -> 55.1 us  [exchange(): return lax.ppermute(values, 'dp', [(k, k ^ 1 << bit) for k in range(size)])]
  transfers between devices with their start and end apart: 81 -> 93, of which waited for: 38 -> 39; matrix products, arithmetic and copies ran while one was open for 41% -> 41% of each run, Pallas kernels for 10% -> 9%
where the time goes in v6:
time: 1380 us; the launch traced here: 1360 us
  waiting for transfers between devices  517 us (37%)
  matrix products  305 us (22%)
  local copies, waits for them, and re-layouts  150 us (11%)
  other arithmetic  148 us (11%)
  Pallas kernels  130 us (9%)
  starting transfers between devices  97 us (7%)
  between operations  17 us (1%)
    dot_general x34, matrix products, dot(): lax.dot_general(left, right, (dims, ((), ())), preferred_element_type=F32)  305 us
    ppermute x58, waiting for transfers between devices, exchange(): return lax.ppermute(values, 'dp', [(k, k ^ 1 << bit) for k in range(size)])  171 us
    ppermute x6, waiting for transfers between devices, go(): lax.ppermute(left, 'tensor', [(s, s - 1) for s in range(1, self.n - k + 1)])  161 us
    pallas_call x3, Pallas kernels, kernel_call(): pl.pallas_call(body, grid_spec=pltpu.PrefetchScalarGridSpec(num_scalar_pr...  62.2 us
    unnamed x292, local copies, waits for them, and re-layouts  60.4 us
    ppermute x58, starting transfers between devices, exchange(): return lax.ppermute(values, 'dp', [(k, k ^ 1 << bit) for k in range(size)])  55.1 us
    all_gather x1, waiting for transfers between devices, on_device(): whole = lax.all_gather(whole, 'tensor', axis=0)  54.6 us
    convert_element_type x18, other arithmetic, add_all(): return total.astype(BF)  54 us
  transfers between devices with their start and end apart: 93, of which 39 were waited for; matrix products, arithmetic and copies ran while one was open for 41% of the time, Pallas kernels for 9%

profile of v6, /device:TPU:0, one launch (start us, length us, event | category | flops | bytes accessed | tf_op | source)
XLA Modules:
  0.0 1364.2 jit_solution(7123584895886531694)
XLA Ops:
  24.3 54.6 %all-gather.8.cloned.1.call-done = bf16[4,592,640]{2,1,0:T(8,128)(2,1)} async-done(((bf16[1,592,640]{2,1,0:T(8,128)(2,1)}), bf16[4,592,640]{2,1,0:T(8,128)(2,1)}) %all-gather.8.cloned.1.call-update) | async-done | bytes 3031056 | tf_op jit(solution)/shard_map/all_gather | solution.py:557
  107.4 23.6 %collective-permute-done.2 = bf16[160,640]{1,0:T(8,128)(2,1)} collective-permute-done((bf16[160,640]{1,0:T(8,128)(2,1)S(1)}, bf16[160,640]{1,0:T(8,128)(2,1)}, u32[]{:S(2)}, u32[]{:S(2)}) %collective-permute-start.2) | collective-permute-done | bytes 204832 | tf_op jit(solution)/shard_map/ppermute | solution.py:79
  185.1 5.7 fusion.43
  204.6 18.8 %recurrence.1 = (f32[512,2560]{1,0:T(8,128)}, f32[512,2560]{1,0:T(8,128)}, f32[512,2560]{1,0:T(8,128)}, f32[512,2560]{1,0:T(8,128)}, f32[512,2560]{1,0:T(8,128)}, /*index=5*/f32[512,2560]{1,0:T(8,128)}) custom-call(s32[1]{0:T(128)} %sub.46.live_ref, f32[528,2560]{1,0:T(8,128)} %convolution_add_fusion.refs_2_.pre_ref, f32[8,2560]{1,0:T(8,128)} %pad_maximum_fusion.12.par_ref, ...), custom_call_target="tpu_custom_call" | custom-call | flops 1024 | bytes 1024 | tf_op jit(solution)/shard_map/recurrence/pallas_call | solution.py:496
  251.2 9.8 fusion.22
  261.0 13.3 collective-permute-done.24.refs_1_
  280.9 12.1 collective-permute-done.25.refs_2_
  305.5 5.7 fusion.81
  311.2 4.9 fusion.82
  319.3 21.4 %collective-permute-done.29.refs_1_ = bf16[256,3072]{1,0:T(8,128)(2,1)S(1)} collective-permute-done((bf16[256,3072]{1,0:T(8,128)(2,1)}, bf16[256,3072]{1,0:T(8,128)(2,1)S(1)}, u32[]{:S(2)}, u32[]{:S(2)}) %collective-permute-start.29) | collective-permute-done | bytes 1572896 | tf_op jit(solution)/shard_map/ppermute | solution.py:79
  349.6 15.7 %collective-permute-done.30.refs_2_.refs_3_ = bf16[128,3072]{1,0:T(8,128)(2,1)S(1)} collective-permute-done((bf16[128,3072]{1,0:T(8,128)(2,1)}, bf16[128,3072]{1,0:T(8,128)(2,1)S(1)}, u32[]{:S(2)}, u32[]{:S(2)}) %collective-permute-start.30) | collective-permute-done | bytes 786464 | tf_op jit(solution)/shard_map/ppermute | solution.py:79
  366.2 5.2 assemble.10.refs_0_
  375.6 9.6 collective-permute-done.33.refs_2_
  390.3 5.8 permute.8
  396.1 5.9 permute.7
  408.4 9.3 assemble.11
  417.6 11.7 all-gather.10.cloned.1.call-done
  429.3 19.1 %fusion.83 = f32[1024,3072]{1,0:T(8,128)} fusion(bf16[1024,2048]{1,0:T(8,128)(2,1)} %all-gather.10.cloned.1.call-done, bf16[2048,3072]{1,0:T(8,128)(2,1)} %assemble.11), kind=kOutput, calls=%fused_computation.293 | convolution fusion | flops 12884901888 | bytes 29360128 | tf_op jit(solution)/shard_map/dot_general | solution.py:24
  448.4 14.6 %fusion.6 = (bf16[1024,1536]{1,0:T(8,128)(2,1)S(1)}, bf16[1024,1536]{1,0:T(8,128)(2,1)S(1)}, bf16[1024,1536]{1,0:T(8,128)(2,1)}) fusion(f32[1024,3072]{1,0:T(8,128)} %fusion.83, bf16[1024,2048]{1,0:T(8,128)(2,1)S(1)} %copy-done.42, bf16[2048,1536]{1,0:T(8,128)(2,1)S(1)} %copy-done.45), kind=kOutput, calls=%fused_computation.16 | convolution fusion | flops 6483345408 | bytes 32505856 | tf_op jit(solution)/shard_map/dot_general | solution.py:24
  464.8 17.6 %convolution_convert_fusion.7.refs_1_ = bf16[1024,2048]{1,0:T(8,128)(2,1)} fusion(bf16[2048,3072]{1,0:T(8,128)(2,1)} %assemble.11, bf16[1024,1536]{1,0:T(8,128)(2,1)S(1)} %get-tuple-element.205, bf16[1024,1536]{1,0:T(8,128)(2,1)S(1)} %get-tuple-element.204), kind=kOutput, calls=%fused_computation.73 | convolution fusion | flops 12899581952 | bytes 23068672 | tf_op jit(solution)/shard_map/dot_general | solution.py:24
  482.6 27.6 %all-gather.12.cloned.1.call-done.refs_0_ = bf16[1024,2048]{1,0:T(8,128)(2,1)} async-done(((bf16[256,2048]{1,0:T(8,128)(2,1)}), bf16[1024,2048]{1,0:T(8,128)(2,1)}) %all-gather.12.cloned.1.call-update) | async-done | bytes 4194320 | tf_op jit(solution)/shard_map/all_gather | solution.py:627
  510.2 19.1 %fusion.84 = f32[1024,3072]{1,0:T(8,128)} fusion(bf16[1024,2048]{1,0:T(8,128)(2,1)} %fence.46, bf16[2048,3072]{1,0:T(8,128)(2,1)} %assemble.11), kind=kOutput, calls=%fused_computation.294 | convolution fusion | flops 12884901888 | bytes 29360128 | tf_op jit(solution)/shard_map/dot_general | solution.py:24
  529.4 15.4 %fusion.13 = (bf16[1024,1536]{1,0:T(8,128)(2,1)}, bf16[1024,1536]{1,0:T(8,128)(2,1)}, bf16[1024,1536]{1,0:T(8,128)(2,1)}) fusion(f32[1024,3072]{1,0:T(8,128)} %fusion.84, bf16[1024,2048]{1,0:T(8,128)(2,1)S(1)} %copy-done.40, bf16[2048,1536]{1,0:T(8,128)(2,1)S(1)} %bitcast.247), kind=kOutput, calls=%fused_computation.23 | convolution fusion | flops 6483345408 | bytes 32505856 | tf_op jit(solution)/shard_map/dot_general | solution.py:24
  544.8 5.6 pad_maximum_fusion.refs_1_
  550.3 18.7 %convolution_convert_fusion.6.refs_2_ = bf16[1024,2048]{1,0:T(8,128)(2,1)} fusion(bf16[2048,3072]{1,0:T(8,128)(2,1)} %assemble.11, bf16[1024,1536]{1,0:T(8,128)(2,1)} %get-tuple-element.203, bf16[1024,1536]{1,0:T(8,128)(2,1)S(1)} %copy-done.57), kind=kOutput, calls=%fused_computation.72 | convolution fusion | flops 12899581952 | bytes 23068672 | tf_op jit(solution)/shard_map/dot_general | solution.py:24
  570.9 5.7 pad_maximum_fusion.1.refs_1_
  576.6 7.4 fusion.37
  584.1 8.4 convolution_convert_fusion.9.refs_6_.refs_0_
  592.6 9.7 add_convert_fusion.2
  602.3 9.7 fusion.31
  612.0 11.8 add_convert_fusion
  624.3 11.0 fusion.34
  635.4 11.2 convolution_convert_fusion.8.refs_7_.refs_1_
  646.6 5.4 fusion.40
  652.0 7.1 add_convert_fusion.3
  659.0 10.2 add_convert_fusion.1
  692.4 5.6 fusion.49
  703.4 17.1 %back_scan.1 = (f32[512,2560]{1,0:T(8,128)}, f32[512,2560]{1,0:T(8,128)}, f32[8,2560]{1,0:T(8,128)}, bf16[512,2560]{1,0:T(8,128)(2,1)}) custom-call(s32[1]{0:T(128)} %sub.46.live_ref, f32[512,2560]{1,0:T(8,128)} %get-tuple-element.258.refs_2_.pre_ref, f32[512,2560]{1,0:T(8,128)} %convolution_add_fusion.1.grad_ref, f32[512,2560]{1,0:T(8,128)} %get-tuple-element.90.decay_ref, ...), custom_call_target="tpu_custom_call" | custom-call | flops 1024 | bytes 1024 | tf_op jit(solution)/shard_map/back_scan/pallas_call | solution.py:496
  725.4 11.1 collective-permute-done.47.refs_4_
  738.1 26.3 %recurrence_back.1 = (f32[528,2560]{1,0:T(8,128)}, f32[8,2560]{1,0:T(8,128)}, bf16[4,160,1280]{2,1,0:T(8,128)(2,1)}) custom-call(s32[1]{0:T(128)} %sub.46.live_ref, f32[528,2560]{1,0:T(8,128)} %convolution_add_fusion.refs_2_.pre_ref, f32[8,2560]{1,0:T(8,128)} %pad_maximum_fusion.12.par_ref, ...), custom_call_target="tpu_custom_call" | custom-call | flops 1024 | bytes 1024 | tf_op jit(solution)/shard_map/recurrence_back/pallas_call | solution.py:496
  767.2 7.5 fusion.85
  778.0 6.8 fusion.86
  788.1 5.6 collective-permute-start.39
  798.6 5.8 fusion.87
  804.4 5.0 fusion.88
  812.3 26.0 %collective-permute-done.39.refs_1_ = bf16[256,2048]{1,0:T(8,128)(2,1)} collective-permute-done((bf16[256,2048]{1,0:T(8,128)(2,1)}, bf16[256,2048]{1,0:T(8,128)(2,1)}, u32[]{:S(2)}, u32[]{:S(2)}) %collective-permute-start.39) | collective-permute-done | bytes 1048608 | tf_op jit(solution)/shard_map/ppermute | solution.py:183
  838.3 22.6 %collective-permute-done.38.refs_2_ = bf16[256,2048]{1,0:T(8,128)(2,1)} collective-permute-done((bf16[256,2048]{1,0:T(8,128)(2,1)}, bf16[256,2048]{1,0:T(8,128)(2,1)}, u32[]{:S(2)}, u32[]{:S(2)}) %collective-permute-start.38) | collective-permute-done | bytes 1048608 | tf_op jit(solution)/shard_map/ppermute | solution.py:184
  865.7 6.9 add_convert_fusion.4.in_ref
  880.8 6.4 convolution_convert_fusion.5
  904.4 6.4 convolution_convert_fusion.2
  910.7 55.9 %collective-permute-done.42.refs_4_ = bf16[256,2048]{1,0:T(8,128)(2,1)} collective-permute-done((bf16[256,2048]{1,0:T(8,128)(2,1)}, bf16[256,2048]{1,0:T(8,128)(2,1)}, u32[]{:S(2)}, u32[]{:S(2)}) %collective-permute-start.42) | collective-permute-done | bytes 1048608 | tf_op jit(solution)/shard_map/ppermute | solution.py:184
  978.5 71.3 %collective-permute-done.43.refs_4_ = bf16[256,2048]{1,0:T(8,128)(2,1)S(1)} collective-permute-done((bf16[256,2048]{1,0:T(8,128)(2,1)}, bf16[256,2048]{1,0:T(8,128)(2,1)S(1)}, u32[]{:S(2)}, u32[]{:S(2)}) %collective-permute-start.43) | collective-permute-done | bytes 1048608 | tf_op jit(solution)/shard_map/ppermute | solution.py:184
  1058.8 7.3 convolution_convert_fusion.3
  1073.9 7.5 convolution_convert_fusion.4
  1081.4 5.1 convolution_convert_fusion
  1086.5 9.9 collective-permute-done.54.refs_5_
  1112.5 5.4 collective-permute-done.81
  1123.2 11.2 collective-permute-done.79
  1157.1 18.4 %collective-permute-done.58.refs_3_.refs_7_ = bf16[256,2560]{1,0:T(8,128)(2,1)S(1)} collective-permute-done((bf16[256,2560]{1,0:T(8,128)(2,1)}, bf16[256,2560]{1,0:T(8,128)(2,1)S(1)}, u32[]{:S(2)}, u32[]{:S(2)}) %collective-permute-start.58) | collective-permute-done | bytes 1310752 | tf_op jit(solution)/shard_map/ppermute | solution.py:79
  1186.8 8.9 collective-permute-done.73
  1217.5 11.7 collective-permute-done.61.refs_4_
  1255.3 7.0 interleave.1
  1303.1 6.4 collective-permute-done.71
  1311.7 41.9 %reduce-scatter.14.cloned.1.call-done = bf16[1,3,256,640]{3,2,1,0:T(8,128)(2,1)} async-done(((bf16[4,3,256,640]{3,2,1,0:T(8,128)(2,1)}), bf16[1,3,256,640]{3,2,1,0:T(8,128)(2,1)}) %reduce-scatter.14.cloned.1.call-update) | async-done | bytes 983056 | tf_op jit(solution)/shard_map/reduce_scatter | solution.py:728
  (680 shorter events, 452.0 us)
Async XLA Ops:
  7.2 71.7 %all-gather.8.cloned.1.call-start = ((), (), s32[]{:S(2)}) async-start(), calls=%async_computation.5 | async-start | bytes 3788800 | tf_op jit(solution)/shard_map/all_gather | solution.py:557
  13.3 416.0 %all-gather.10.cloned.1.call-start = ((), (), s32[]{:S(2)}) async-start(), calls=%async_computation.6 | async-start | bytes 5242880 | tf_op jit(solution)/shard_map/all_gather | solution.py:627
  14.6 80.1 %collective-permute-start.6 = (bf16[256,1536]{1,0:T(8,128)(2,1)}, bf16[256,1536]{1,0:T(8,128)(2,1)S(1)}, u32[]{:S(2)}, u32[]{:S(2)}) collective-permute-start(bf16[256,1536]{1,0:T(8,128)(2,1)} %bitcast.173.refs_0_), channel_id=1, source_target_pairs={{0,16},{4,20},{8,24},{12,28},{16,0},{20,4},{24,8},{28,12},{1,17},{... | collective-permute-start | bytes 2359304 | tf_op jit(solution)/shard_map/ppermute | solution.py:79
  18.6 76.0 %collective-permute-start.5 = (bf16[256,1536]{1,0:T(8,128)(2,1)}, bf16[256,1536]{1,0:T(8,128)(2,1)S(1)}, u32[]{:S(2)}, u32[]{:S(2)}) collective-permute-start(bf16[256,1536]{1,0:T(8,128)(2,1)} %bitcast.173.refs_0_), channel_id=1, source_target_pairs={{0,8},{4,12},{8,0},{12,4},{16,24},{20,28},{24,16},{28,20},{1,9},{5... | collective-permute-start | bytes 2359304 | tf_op jit(solution)/shard_map/ppermute | solution.py:79
  96.4 40.8 %collective-permute-start.9 = (bf16[256,2560]{1,0:T(8,128)(2,1)}, bf16[256,2560]{1,0:T(8,128)(2,1)S(1)}, u32[]{:S(2)}, u32[]{:S(2)}) collective-permute-start(bf16[256,2560]{1,0:T(8,128)(2,1)} %fence.35.refs_0_), channel_id=1, source_target_pairs={{0,16},{4,20},{8,24},{12,28},{16,0},{20,4},{24,8},{28,12},{1,17},{... | collective-permute-start | bytes 3932168 | tf_op jit(solution)/shard_map/ppermute | solution.py:79
  96.9 42.7 %collective-permute-start.7 = (bf16[256,2560]{1,0:T(8,128)(2,1)}, bf16[256,2560]{1,0:T(8,128)(2,1)S(1)}, u32[]{:S(2)}, u32[]{:S(2)}) collective-permute-start(bf16[256,2560]{1,0:T(8,128)(2,1)} %fence.35.refs_0_), channel_id=1, source_target_pairs={{0,8},{4,12},{8,0},{12,4},{16,24},{20,28},{24,16},{28,20},{1,9},{5... | collective-permute-start | bytes 3932168 | tf_op jit(solution)/shard_map/ppermute | solution.py:79
  98.2 33.7 %collective-permute-start.3 = (bf16[160,640]{1,0:T(8,128)(2,1)}, bf16[160,640]{1,0:T(8,128)(2,1)S(1)}, u32[]{:S(2)}, u32[]{:S(2)}) collective-permute-start(bf16[160,640]{1,0:T(8,128)(2,1)} %slice.755), channel_id=1, source_target_pairs={{0,8},{4,12},{8,0},{12,4},{16,24},{20,28},{24,16},{28,20},{1,9},{5... | collective-permute-start | bytes 614408 | tf_op jit(solution)/shard_map/ppermute | solution.py:79
  100.7 30.3 %collective-permute-start.2 = (bf16[160,640]{1,0:T(8,128)(2,1)S(1)}, bf16[160,640]{1,0:T(8,128)(2,1)}, u32[]{:S(2)}, u32[]{:S(2)}) collective-permute-start(bf16[160,640]{1,0:T(8,128)(2,1)S(1)} %slice.754), channel_id=1, source_target_pairs={{0,16},{4,20},{8,24},{12,28},{16,0},{20,4},{24,8},{28,12},{1,17},{... | collective-permute-start | bytes 614408 | tf_op jit(solution)/shard_map/ppermute | solution.py:79
  135.3 29.8 %collective-permute-start.4 = (bf16[4,320,640]{2,1,0:T(8,128)(2,1)}, bf16[4,320,640]{2,1,0:T(8,128)(2,1)}, u32[]{:S(2)}, u32[]{:S(2)}) collective-permute-start(bf16[4,320,640]{2,1,0:T(8,128)(2,1)} %pad_maximum_fusion.6), channel_id=1, source_target_pairs={{0,4},{4,0},{8,12},{12,8},{16,20},{20,16},{24,28},{28,24},{1,5},{5... | collective-permute-start | bytes 4915208 | tf_op jit(solution)/shard_map/ppermute | solution.py:79
  143.6 82.3 %collective-permute-start.18 = (bf16[256,640]{1,0:T(8,128)(2,1)}, bf16[256,640]{1,0:T(8,128)(2,1)}, u32[]{:S(2)}, u32[]{:S(2)}) collective-permute-start(bf16[256,640]{1,0:T(8,128)(2,1)} %fence.38), channel_id=1, source_target_pairs={{0,1},{1,2},{2,3},{3,0},{4,5},{5,6},{6,7},{7,4},{8,9},{9,10},{10,1... | collective-permute-start | bytes 983048 | tf_op jit(solution)/shard_map/ppermute | solution.py:162
  143.6 82.3 %collective-permute-start.17 = (bf16[256,640]{1,0:T(8,128)(2,1)}, bf16[256,640]{1,0:T(8,128)(2,1)}, u32[]{:S(2)}, u32[]{:S(2)}) collective-permute-start(bf16[256,640]{1,0:T(8,128)(2,1)} %fence.38), channel_id=1, source_target_pairs={{0,2},{1,3},{2,0},{3,1},{4,6},{5,7},{6,4},{7,5},{8,10},{9,11},{10,... | collective-permute-start | bytes 983048 | tf_op jit(solution)/shard_map/ppermute | solution.py:162
  158.8 36.9 %collective-permute-start.12 = (bf16[256,2560]{1,0:T(8,128)(2,1)}, bf16[256,2560]{1,0:T(8,128)(2,1)S(1)}, u32[]{:S(2)}, u32[]{:S(2)}) collective-permute-start(bf16[256,2560]{1,0:T(8,128)(2,1)} %fence.36.refs_0_), channel_id=1, source_target_pairs={{0,16},{4,20},{8,24},{12,28},{16,0},{20,4},{24,8},{28,12},{1,17},{... | collective-permute-start | bytes 3932168 | tf_op jit(solution)/shard_map/ppermute | solution.py:79
  159.5 36.2 %collective-permute-start.11 = (bf16[256,2560]{1,0:T(8,128)(2,1)}, bf16[256,2560]{1,0:T(8,128)(2,1)}, u32[]{:S(2)}, u32[]{:S(2)}) collective-permute-start(bf16[256,2560]{1,0:T(8,128)(2,1)} %fence.36.refs_0_), channel_id=1, source_target_pairs={{0,8},{4,12},{8,0},{12,4},{16,24},{20,28},{24,16},{28,20},{1,9},{5... | collective-permute-start | bytes 3932168 | tf_op jit(solution)/shard_map/ppermute | solution.py:79
  165.2 19.9 %collective-permute-start.13 = (bf16[1024,2560]{1,0:T(8,128)(2,1)}, bf16[1024,2560]{1,0:T(8,128)(2,1)}, u32[]{:S(2)}, u32[]{:S(2)}) collective-permute-start(bf16[1024,2560]{1,0:T(8,128)(2,1)} %assemble.7), channel_id=1, source_target_pairs={{0,4},{4,0},{8,12},{12,8},{16,20},{20,16},{24,28},{28,24},{1,5},{5... | collective-permute-start | bytes 15728648 | tf_op jit(solution)/shard_map/ppermute | solution.py:79
  200.6 29.5 %collective-permute-start.14 = (bf16[128,2560]{1,0:T(8,128)(2,1)}, bf16[128,2560]{1,0:T(8,128)(2,1)S(1)}, u32[]{:S(2)}, u32[]{:S(2)}) collective-permute-start(bf16[128,2560]{1,0:T(8,128)(2,1)} %slice.595), channel_id=1, source_target_pairs={{0,8},{4,12},{8,0},{12,4},{16,24},{20,28},{24,16},{28,20},{1,9},{5... | collective-permute-start | bytes 1966088 | tf_op jit(solution)/shard_map/ppermute | solution.py:79
  201.2 29.0 %collective-permute-start.15 = (bf16[128,2560]{1,0:T(8,128)(2,1)}, bf16[128,2560]{1,0:T(8,128)(2,1)}, u32[]{:S(2)}, u32[]{:S(2)}) collective-permute-start(bf16[128,2560]{1,0:T(8,128)(2,1)} %slice.596), channel_id=1, source_target_pairs={{0,16},{4,20},{8,24},{12,28},{16,0},{20,4},{24,8},{28,12},{1,17},{... | collective-permute-start | bytes 1966088 | tf_op jit(solution)/shard_map/ppermute | solution.py:79
  203.2 22.7 %collective-permute-start.16 = (bf16[256,640]{1,0:T(8,128)(2,1)}, bf16[256,640]{1,0:T(8,128)(2,1)S(1)}, u32[]{:S(2)}, u32[]{:S(2)}) collective-permute-start(bf16[256,640]{1,0:T(8,128)(2,1)} %fence.38), channel_id=1, source_target_pairs={{0,3},{1,0},{2,1},{3,2},{4,7},{5,4},{6,5},{7,6},{8,11},{9,8},{10,9... | collective-permute-start | bytes 983048 | tf_op jit(solution)/shard_map/ppermute | solution.py:162
  244.1 30.2 %collective-permute-start.24 = (bf16[256,2560]{1,0:T(8,128)(2,1)}, bf16[256,2560]{1,0:T(8,128)(2,1)S(1)}, u32[]{:S(2)}, u32[]{:S(2)}) collective-permute-start(bf16[256,2560]{1,0:T(8,128)(2,1)} %fence.40.refs_0_), channel_id=1, source_target_pairs={{0,16},{4,20},{8,24},{12,28},{16,0},{20,4},{24,8},{28,12},{1,17},{... | collective-permute-start | bytes 3932168 | tf_op jit(solution)/shard_map/ppermute | solution.py:79
  244.9 29.8 %collective-permute-start.23 = (bf16[256,2560]{1,0:T(8,128)(2,1)}, bf16[256,2560]{1,0:T(8,128)(2,1)S(1)}, u32[]{:S(2)}, u32[]{:S(2)}) collective-permute-start(bf16[256,2560]{1,0:T(8,128)(2,1)} %fence.40.refs_0_), channel_id=1, source_target_pairs={{0,8},{4,12},{8,0},{12,4},{16,24},{20,28},{24,16},{28,20},{1,9},{5... | collective-permute-start | bytes 3932168 | tf_op jit(solution)/shard_map/ppermute | solution.py:79
  303.9 36.8 %collective-permute-start.29 = (bf16[256,3072]{1,0:T(8,128)(2,1)}, bf16[256,3072]{1,0:T(8,128)(2,1)S(1)}, u32[]{:S(2)}, u32[]{:S(2)}) collective-permute-start(bf16[256,3072]{1,0:T(8,128)(2,1)} %fence.42.refs_0_), channel_id=1, source_target_pairs={{0,16},{4,20},{8,24},{12,28},{16,0},{20,4},{24,8},{28,12},{1,17},{... | collective-permute-start | bytes 4718600 | tf_op jit(solution)/shard_map/ppermute | solution.py:79
  305.0 36.9 %collective-permute-start.28 = (bf16[256,3072]{1,0:T(8,128)(2,1)}, bf16[256,3072]{1,0:T(8,128)(2,1)}, u32[]{:S(2)}, u32[]{:S(2)}) collective-permute-start(bf16[256,3072]{1,0:T(8,128)(2,1)} %fence.42.refs_0_), channel_id=1, source_target_pairs={{0,8},{4,12},{8,0},{12,4},{16,24},{20,28},{24,16},{28,20},{1,9},{5... | collective-permute-start | bytes 4718600 | tf_op jit(solution)/shard_map/ppermute | solution.py:79
  346.1 19.2 %collective-permute-start.30 = (bf16[128,3072]{1,0:T(8,128)(2,1)}, bf16[128,3072]{1,0:T(8,128)(2,1)S(1)}, u32[]{:S(2)}, u32[]{:S(2)}) collective-permute-start(bf16[128,3072]{1,0:T(8,128)(2,1)} %slice.617), channel_id=1, source_target_pairs={{0,8},{4,12},{8,0},{12,4},{16,24},{20,28},{24,16},{28,20},{1,9},{5... | collective-permute-start | bytes 2359304 | tf_op jit(solution)/shard_map/ppermute | solution.py:79
  346.6 19.0 %collective-permute-start.31 = (bf16[128,3072]{1,0:T(8,128)(2,1)}, bf16[128,3072]{1,0:T(8,128)(2,1)}, u32[]{:S(2)}, u32[]{:S(2)}) collective-permute-start(bf16[128,3072]{1,0:T(8,128)(2,1)} %slice.618), channel_id=1, source_target_pairs={{0,16},{4,20},{8,24},{12,28},{16,0},{20,4},{24,8},{28,12},{1,17},{... | collective-permute-start | bytes 2359304 | tf_op jit(solution)/shard_map/ppermute | solution.py:79
  349.1 161.1 %all-gather.12.cloned.1.call-start = ((), (), s32[]{:S(2)}) async-start(), calls=%async_computation.7 | async-start | bytes 5242880 | tf_op jit(solution)/shard_map/all_gather | solution.py:627
  371.4 36.9 %collective-permute-start.32 = (bf16[1024,3072]{1,0:T(8,128)(2,1)}, bf16[1024,3072]{1,0:T(8,128)(2,1)}, u32[]{:S(2)}, u32[]{:S(2)}) collective-permute-start(bf16[1024,3072]{1,0:T(8,128)(2,1)} %assemble.10.refs_0_), channel_id=1, source_target_pairs={{0,4},{4,0},{8,12},{12,8},{16,20},{20,16},{24,28},{28,24},{1,5},{5... | collective-permute-start | bytes 18874376 | tf_op jit(solution)/shard_map/ppermute | solution.py:79
  402.0 277.8 %reduce-scatter.6.cloned.1.call-start = ((), (), s32[]{:S(2)}) async-start(), calls=%async_computation.8 | async-start | bytes 5242880 | tf_op jit(solution)/shard_map/reduce_scatter | solution.py:636
  482.4 197.4 %reduce-scatter.8.cloned.1.call-start = ((), (), s32[]{:S(2)}) async-start(), calls=%async_computation.9 | async-start | bytes 5242880 | tf_op jit(solution)/shard_map/reduce_scatter | solution.py:636
  592.5 182.2 %reduce-scatter.10.cloned.1.call-start = ((), (), s32[]{:S(2)}) async-start(), calls=%async_computation.10 | async-start | bytes 5242880 | tf_op jit(solution)/shard_map/reduce_scatter | solution.py:661
  602.3 67.0 %collective-permute-start.36 = (bf16[1024,1536]{1,0:T(8,128)(2,1)}, bf16[1024,1536]{1,0:T(8,128)(2,1)S(1)}, u32[]{:S(2)}, u32[]{:S(2)}) collective-permute-start(bf16[1024,1536]{1,0:T(8,128)(2,1)} %add_convert_fusion.2), channel_id=1, source_target_pairs={{0,4},{4,0},{8,12},{12,8},{16,20},{20,16},{24,28},{28,24},{1,5},{5... | collective-permute-start | bytes 9437192 | tf_op jit(solution)/shard_map/ppermute | solution.py:79
  623.8 51.2 %collective-permute-start.37 = (bf16[1024,3072]{1,0:T(8,128)(2,1)}, bf16[1024,3072]{1,0:T(8,128)(2,1)}, u32[]{:S(2)}, u32[]{:S(2)}) collective-permute-start(bf16[1024,3072]{1,0:T(8,128)(2,1)} %add_convert_fusion), channel_id=1, source_target_pairs={{0,4},{4,0},{8,12},{12,8},{16,20},{20,16},{24,28},{28,24},{1,5},{5... | collective-permute-start | bytes 18874376 | tf_op jit(solution)/shard_map/ppermute | solution.py:79
  679.8 294.0 %reduce-scatter.12.cloned.1.call-start = ((), (), s32[]{:S(2)}) async-start(), calls=%async_computation.11 | async-start | bytes 5242880 | tf_op jit(solution)/shard_map/reduce_scatter | solution.py:661
  683.2 39.6 %collective-permute-start.45 = (bf16[256,1536]{1,0:T(8,128)(2,1)}, bf16[256,1536]{1,0:T(8,128)(2,1)}, u32[]{:S(2)}, u32[]{:S(2)}) collective-permute-start(bf16[256,1536]{1,0:T(8,128)(2,1)} %get-tuple-element.236.refs_3_), channel_id=1, source_target_pairs={{0,16},{4,20},{8,24},{12,28},{16,0},{20,4},{24,8},{28,12},{1,17},{... | collective-permute-start | bytes 2359304 | tf_op jit(solution)/shard_map/ppermute | solution.py:79
  684.5 39.6 %collective-permute-start.44 = (bf16[256,1536]{1,0:T(8,128)(2,1)S(1)}, bf16[256,1536]{1,0:T(8,128)(2,1)}, u32[]{:S(2)}, u32[]{:S(2)}) collective-permute-start(bf16[256,1536]{1,0:T(8,128)(2,1)S(1)} %copy-done.64), channel_id=1, source_target_pairs={{0,8},{4,12},{8,0},{12,4},{16,24},{20,28},{24,16},{28,20},{1,9},{5... | collective-permute-start | bytes 2359304 | tf_op jit(solution)/shard_map/ppermute | solution.py:79
  686.0 50.6 %collective-permute-start.47 = (bf16[256,3072]{1,0:T(8,128)(2,1)}, bf16[256,3072]{1,0:T(8,128)(2,1)}, u32[]{:S(2)}, u32[]{:S(2)}) collective-permute-start(bf16[256,3072]{1,0:T(8,128)(2,1)} %get-tuple-element.210.refs_5_), channel_id=1, source_target_pairs={{0,16},{4,20},{8,24},{12,28},{16,0},{20,4},{24,8},{28,12},{1,17},{... | collective-permute-start | bytes 4718600 | tf_op jit(solution)/shard_map/ppermute | solution.py:79
  686.5 50.9 %collective-permute-start.46 = (bf16[256,3072]{1,0:T(8,128)(2,1)}, bf16[256,3072]{1,0:T(8,128)(2,1)}, u32[]{:S(2)}, u32[]{:S(2)}) collective-permute-start(bf16[256,3072]{1,0:T(8,128)(2,1)} %get-tuple-element.211.refs_4_), channel_id=1, source_target_pairs={{0,8},{4,12},{8,0},{12,4},{16,24},{20,28},{24,16},{28,20},{1,9},{5... | collective-permute-start | bytes 4718600 | tf_op jit(solution)/shard_map/ppermute | solution.py:79
  688.6 468.5 %all-gather.14.cloned.1.call-start = ((), (), s32[]{:S(2)}) async-start(), calls=%async_computation.13 | async-start | bytes 5242880 | tf_op jit(solution)/shard_map/all_gather | solution.py:704
  765.5 29.5 %collective-permute-start.51 = (f32[16,2560]{1,0:T(8,128)S(1)}, f32[16,2560]{1,0:T(8,128)S(1)}, u32[]{:S(2)}, u32[]{:S(2)}) collective-permute-start(f32[16,2560]{1,0:T(8,128)S(1)} %slice.654), channel_id=1, source_target_pairs={{1,0},{2,1},{3,2},{5,4},{6,5},{7,6},{9,8},{10,9},{11,10},{13,12},{... | collective-permute-start | bytes 491528 | tf_op jit(solution)/shard_map/ppermute | solution.py:162
  788.1 50.2 %collective-permute-start.39 = (bf16[256,2048]{1,0:T(8,128)(2,1)}, bf16[256,2048]{1,0:T(8,128)(2,1)}, u32[]{:S(2)}, u32[]{:S(2)}) collective-permute-start(bf16[256,2048]{1,0:T(8,128)(2,1)} %permute.9.refs_1_), channel_id=1, source_target_pairs={{0,1},{1,2},{2,3},{4,5},{5,6},{6,7},{8,9},{9,10},{10,11},{12,13},{... | collective-permute-start | bytes 3145736 | tf_op jit(solution)/shard_map/ppermute | solution.py:183
  793.7 67.2 %collective-permute-start.38 = (bf16[256,2048]{1,0:T(8,128)(2,1)}, bf16[256,2048]{1,0:T(8,128)(2,1)}, u32[]{:S(2)}, u32[]{:S(2)}) collective-permute-start(bf16[256,2048]{1,0:T(8,128)(2,1)} %permute.9.refs_1_), channel_id=1, source_target_pairs={{1,0},{2,1},{3,2},{5,4},{6,5},{7,6},{9,8},{10,9},{11,10},{13,12},{... | collective-permute-start | bytes 3145736 | tf_op jit(solution)/shard_map/ppermute | solution.py:184
  879.3 352.3 %all-gather.16.cloned.1.call-start = ((), (), s32[]{:S(2)}) async-start(), calls=%async_computation.14 | async-start | bytes 5242880 | tf_op jit(solution)/shard_map/all_gather | solution.py:704
  887.3 86.6 %collective-permute-start.52 = (bf16[1024,2560]{1,0:T(8,128)(2,1)}, bf16[1024,2560]{1,0:T(8,128)(2,1)}, u32[]{:S(2)}, u32[]{:S(2)}) collective-permute-start(bf16[1024,2560]{1,0:T(8,128)(2,1)} %convolution_convert_fusion.5), channel_id=1, source_target_pairs={{0,4},{4,0},{8,12},{12,8},{16,20},{20,16},{24,28},{28,24},{1,5},{5... | collective-permute-start | bytes 15728648 | tf_op jit(solution)/shard_map/ppermute | solution.py:79
  896.0 70.6 %collective-permute-start.42 = (bf16[256,2048]{1,0:T(8,128)(2,1)}, bf16[256,2048]{1,0:T(8,128)(2,1)}, u32[]{:S(2)}, u32[]{:S(2)}) collective-permute-start(bf16[256,2048]{1,0:T(8,128)(2,1)} %collective-permute-done.38.refs_2_), channel_id=1, source_target_pairs={{1,0},{2,1},{5,4},{6,5},{9,8},{10,9},{13,12},{14,13},{17,16},{18,1... | collective-permute-start | bytes 3145736 | tf_op jit(solution)/shard_map/ppermute | solution.py:184
  897.4 70.5 %collective-permute-start.41 = (bf16[256,2048]{1,0:T(8,128)(2,1)}, bf16[256,2048]{1,0:T(8,128)(2,1)S(1)}, u32[]{:S(2)}, u32[]{:S(2)}) collective-permute-start(bf16[256,2048]{1,0:T(8,128)(2,1)} %collective-permute-done.40.refs_3_), channel_id=1, source_target_pairs={{2,3},{6,7},{10,11},{14,15},{18,19},{22,23},{26,27},{30,31}} | collective-permute-start | bytes 3145736 | tf_op jit(solution)/shard_map/ppermute | solution.py:183
  904.3 449.2 %reduce-scatter.14.cloned.1.call-start = ((), (), s32[]{:S(2)}) async-start(), calls=%async_computation.12 | async-start | bytes 4915200 | tf_op jit(solution)/shard_map/reduce_scatter | solution.py:728
  966.6 83.1 %collective-permute-start.43 = (bf16[256,2048]{1,0:T(8,128)(2,1)}, bf16[256,2048]{1,0:T(8,128)(2,1)S(1)}, u32[]{:S(2)}, u32[]{:S(2)}) collective-permute-start(bf16[256,2048]{1,0:T(8,128)(2,1)} %collective-permute-done.42.refs_4_), channel_id=1, source_target_pairs={{1,0},{5,4},{9,8},{13,12},{17,16},{21,20},{25,24},{29,28}} | collective-permute-start | bytes 3145736 | tf_op jit(solution)/shard_map/ppermute | solution.py:184
  1055.9 40.4 %collective-permute-start.54 = (bf16[256,2048]{1,0:T(8,128)(2,1)}, bf16[256,2048]{1,0:T(8,128)(2,1)S(1)}, u32[]{:S(2)}, u32[]{:S(2)}) collective-permute-start(bf16[256,2048]{1,0:T(8,128)(2,1)} %permute.11.refs_2_), channel_id=1, source_target_pairs={{0,1},{1,2},{2,3},{4,5},{5,6},{6,7},{8,9},{9,10},{10,11},{12,13},{... | collective-permute-start | bytes 3145736 | tf_op jit(solution)/shard_map/ppermute | solution.py:183
  1057.5 45.7 %collective-permute-start.53 = (bf16[256,2048]{1,0:T(8,128)(2,1)}, bf16[256,2048]{1,0:T(8,128)(2,1)S(1)}, u32[]{:S(2)}, u32[]{:S(2)}) collective-permute-start(bf16[256,2048]{1,0:T(8,128)(2,1)} %permute.11.refs_2_), channel_id=1, source_target_pairs={{1,0},{2,1},{3,2},{5,4},{6,5},{7,6},{9,8},{10,9},{11,10},{13,12},{... | collective-permute-start | bytes 3145736 | tf_op jit(solution)/shard_map/ppermute | solution.py:184
  1066.2 76.3 %collective-permute-start.55 = (bf16[1024,2560]{1,0:T(8,128)(2,1)}, bf16[1024,2560]{1,0:T(8,128)(2,1)}, u32[]{:S(2)}, u32[]{:S(2)}) collective-permute-start(bf16[1024,2560]{1,0:T(8,128)(2,1)} %convolution_convert_fusion.3), channel_id=1, source_target_pairs={{0,4},{4,0},{8,12},{12,8},{16,20},{20,16},{24,28},{28,24},{1,5},{5... | collective-permute-start | bytes 15728648 | tf_op jit(solution)/shard_map/ppermute | solution.py:79
  1070.8 33.4 %collective-permute-start.56 = (bf16[256,2560]{1,0:T(8,128)(2,1)}, bf16[256,2560]{1,0:T(8,128)(2,1)S(1)}, u32[]{:S(2)}, u32[]{:S(2)}) collective-permute-start(bf16[256,2560]{1,0:T(8,128)(2,1)} %get-tuple-element.100), channel_id=1, source_target_pairs={{0,8},{4,12},{8,0},{12,4},{16,24},{20,28},{24,16},{28,20},{1,9},{5... | collective-permute-start | bytes 3932168 | tf_op jit(solution)/shard_map/ppermute | solution.py:79
  1072.7 31.6 %collective-permute-start.57 = (bf16[256,2560]{1,0:T(8,128)(2,1)}, bf16[256,2560]{1,0:T(8,128)(2,1)S(1)}, u32[]{:S(2)}, u32[]{:S(2)}) collective-permute-start(bf16[256,2560]{1,0:T(8,128)(2,1)} %get-tuple-element.101), channel_id=1, source_target_pairs={{0,16},{4,20},{8,24},{12,28},{16,0},{20,4},{24,8},{28,12},{1,17},{... | collective-permute-start | bytes 3932168 | tf_op jit(solution)/shard_map/ppermute | solution.py:79
  1096.4 56.9 %collective-permute-start.64 = (bf16[1024,2560]{1,0:T(8,128)(2,1)}, bf16[1024,2560]{1,0:T(8,128)(2,1)}, u32[]{:S(2)}, u32[]{:S(2)}) collective-permute-start(bf16[1024,2560]{1,0:T(8,128)(2,1)} %convolution_convert_fusion), channel_id=1, source_target_pairs={{0,4},{4,0},{8,12},{12,8},{16,20},{20,16},{24,28},{28,24},{1,5},{5... | collective-permute-start | bytes 15728648 | tf_op jit(solution)/shard_map/ppermute | solution.py:79
  1108.7 25.7 %collective-permute-start.79 = (bf16[128,3072]{1,0:T(8,128)(2,1)}, bf16[128,3072]{1,0:T(8,128)(2,1)}, u32[]{:S(2)}, u32[]{:S(2)}) collective-permute-start(bf16[128,3072]{1,0:T(8,128)(2,1)} %get-tuple-element.123), channel_id=1, source_target_pairs={{0,8},{4,12},{8,0},{12,4},{16,24},{20,28},{24,16},{28,20},{1,9},{5... | collective-permute-start | bytes 2359304 | tf_op jit(solution)/shard_map/ppermute | solution.py:79
  1117.9 18.7 %collective-permute-start.80 = (bf16[128,3072]{1,0:T(8,128)(2,1)S(1)}, bf16[128,3072]{1,0:T(8,128)(2,1)}, u32[]{:S(2)}, u32[]{:S(2)}) collective-permute-start(bf16[128,3072]{1,0:T(8,128)(2,1)S(1)} %copy-done.52), channel_id=1, source_target_pairs={{0,16},{4,20},{8,24},{12,28},{16,0},{20,4},{24,8},{28,12},{1,17},{... | collective-permute-start | bytes 2359304 | tf_op jit(solution)/shard_map/ppermute | solution.py:79
  1146.3 29.1 %collective-permute-start.58 = (bf16[256,2560]{1,0:T(8,128)(2,1)}, bf16[256,2560]{1,0:T(8,128)(2,1)S(1)}, u32[]{:S(2)}, u32[]{:S(2)}) collective-permute-start(bf16[256,2560]{1,0:T(8,128)(2,1)} %get-tuple-element.102), channel_id=1, source_target_pairs={{0,8},{4,12},{8,0},{12,4},{16,24},{20,28},{24,16},{28,20},{1,9},{5... | collective-permute-start | bytes 3932168 | tf_op jit(solution)/shard_map/ppermute | solution.py:79
  1147.8 28.9 %collective-permute-start.59 = (bf16[256,2560]{1,0:T(8,128)(2,1)}, bf16[256,2560]{1,0:T(8,128)(2,1)S(1)}, u32[]{:S(2)}, u32[]{:S(2)}) collective-permute-start(bf16[256,2560]{1,0:T(8,128)(2,1)} %get-tuple-element.103), channel_id=1, source_target_pairs={{0,16},{4,20},{8,24},{12,28},{16,0},{20,4},{24,8},{28,12},{1,17},{... | collective-permute-start | bytes 3932168 | tf_op jit(solution)/shard_map/ppermute | solution.py:79
  1179.9 35.2 %collective-permute-start.60 = (bf16[256,2048]{1,0:T(8,128)(2,1)}, bf16[256,2048]{1,0:T(8,128)(2,1)}, u32[]{:S(2)}, u32[]{:S(2)}) collective-permute-start(bf16[256,2048]{1,0:T(8,128)(2,1)} %get-tuple-element.104), channel_id=1, source_target_pairs={{1,2},{2,3},{5,6},{6,7},{9,10},{10,11},{13,14},{14,15},{17,18},{18... | collective-permute-start | bytes 3145736 | tf_op jit(solution)/shard_map/ppermute | solution.py:183
  1184.8 24.9 %collective-permute-start.75 = (bf16[128,2560]{1,0:T(8,128)(2,1)}, bf16[128,2560]{1,0:T(8,128)(2,1)S(1)}, u32[]{:S(2)}, u32[]{:S(2)}) collective-permute-start(bf16[128,2560]{1,0:T(8,128)(2,1)} %get-tuple-element.119), channel_id=1, source_target_pairs={{0,8},{4,12},{8,0},{12,4},{16,24},{20,28},{24,16},{28,20},{1,9},{5... | collective-permute-start | bytes 1966088 | tf_op jit(solution)/shard_map/ppermute | solution.py:79
  1186.1 24.8 %collective-permute-start.76 = (bf16[128,2560]{1,0:T(8,128)(2,1)}, bf16[128,2560]{1,0:T(8,128)(2,1)}, u32[]{:S(2)}, u32[]{:S(2)}) collective-permute-start(bf16[128,2560]{1,0:T(8,128)(2,1)} %get-tuple-element.120), channel_id=1, source_target_pairs={{0,16},{4,20},{8,24},{12,28},{16,0},{20,4},{24,8},{28,12},{1,17},{... | collective-permute-start | bytes 1966088 | tf_op jit(solution)/shard_map/ppermute | solution.py:79
  1195.7 38.7 %collective-permute-start.65 = (bf16[256,2560]{1,0:T(8,128)(2,1)}, bf16[256,2560]{1,0:T(8,128)(2,1)}, u32[]{:S(2)}, u32[]{:S(2)}) collective-permute-start(bf16[256,2560]{1,0:T(8,128)(2,1)} %get-tuple-element.109), channel_id=1, source_target_pairs={{0,8},{4,12},{8,0},{12,4},{16,24},{20,28},{24,16},{28,20},{1,9},{5... | collective-permute-start | bytes 3932168 | tf_op jit(solution)/shard_map/ppermute | solution.py:79
  1196.4 38.1 %collective-permute-start.66 = (bf16[256,2560]{1,0:T(8,128)(2,1)}, bf16[256,2560]{1,0:T(8,128)(2,1)}, u32[]{:S(2)}, u32[]{:S(2)}) collective-permute-start(bf16[256,2560]{1,0:T(8,128)(2,1)} %get-tuple-element.110), channel_id=1, source_target_pairs={{0,16},{4,20},{8,24},{12,28},{16,0},{20,4},{24,8},{28,12},{1,17},{... | collective-permute-start | bytes 3932168 | tf_op jit(solution)/shard_map/ppermute | solution.py:79
  1209.6 19.6 %collective-permute-start.61 = (bf16[256,2048]{1,0:T(8,128)(2,1)}, bf16[256,2048]{1,0:T(8,128)(2,1)}, u32[]{:S(2)}, u32[]{:S(2)}) collective-permute-start(bf16[256,2048]{1,0:T(8,128)(2,1)} %get-tuple-element.105), channel_id=1, source_target_pairs={{1,0},{2,1},{5,4},{6,5},{9,8},{10,9},{13,12},{14,13},{17,16},{18,1... | collective-permute-start | bytes 3145736 | tf_op jit(solution)/shard_map/ppermute | solution.py:184
  1231.5 49.1 %collective-permute-start.62 = (bf16[256,2048]{1,0:T(8,128)(2,1)}, bf16[256,2048]{1,0:T(8,128)(2,1)}, u32[]{:S(2)}, u32[]{:S(2)}) collective-permute-start(bf16[256,2048]{1,0:T(8,128)(2,1)} %get-tuple-element.106), channel_id=1, source_target_pairs={{2,3},{6,7},{10,11},{14,15},{18,19},{22,23},{26,27},{30,31}} | collective-permute-start | bytes 3145736 | tf_op jit(solution)/shard_map/ppermute | solution.py:183
  1233.1 62.9 %collective-permute-start.63 = (bf16[256,2048]{1,0:T(8,128)(2,1)}, bf16[256,2048]{1,0:T(8,128)(2,1)}, u32[]{:S(2)}, u32[]{:S(2)}) collective-permute-start(bf16[256,2048]{1,0:T(8,128)(2,1)} %get-tuple-element.107), channel_id=1, source_target_pairs={{1,0},{5,4},{9,8},{13,12},{17,16},{21,20},{25,24},{29,28}} | collective-permute-start | bytes 3145736 | tf_op jit(solution)/shard_map/ppermute | solution.py:184
  1254.8 22.8 %collective-permute-start.67 = (bf16[4,4,26752]{2,1,0:T(4,128)(2,1)}, bf16[4,4,26752]{2,1,0:T(4,128)(2,1)}, u32[]{:S(2)}, u32[]{:S(2)}) collective-permute-start(bf16[4,4,26752]{2,1,0:T(4,128)(2,1)} %slice.842), channel_id=1, source_target_pairs={{0,16},{4,20},{8,24},{12,28},{16,0},{20,4},{24,8},{28,12},{1,17},{... | collective-permute-start | bytes 2568200 | tf_op jit(solution)/shard_map/ppermute | solution.py:79
  (158 other events, 1481.7 us)
Sparse Core Ops, SparseCore 0:
  13.5 65.4 all-gather.7
  349.2 80.0 all-gather.9
  430.9 79.2 all-gather.11
  512.3 75.2 reduce-scatter.5
  592.6 75.2 reduce-scatter.7
  679.9 76.5 reduce-scatter.9
  758.9 102.4 reduce-scatter.11
  879.4 100.9 all-gather.13
  981.9 109.9 all-gather.15
  1276.8 76.6 reduce-scatter.13

commit v7 on v6

--- a/solution.py
+++ b/solution.py
@@ -171,29 +171,44 @@
     return total
 
 
-class Line:
-    def __init__(self, own, n):
-        self.own, self.n, self.rounds = own, n, []
-
-    def go(self, *others):
-        k = len(self.rounds) + 1
-        if k >= self.n:
-            return ()
-        right, left = fence(self.rounds[-1], *others) if self.rounds else (self.own, self.own)
-        right = lax.ppermute(right, "tensor", [(s, s + 1) for s in range(k - 1, self.n - 1)])
-        left = lax.ppermute(left, "tensor", [(s, s - 1) for s in range(1, self.n - k + 1)])
-        self.rounds.append((right, left))
-        return self.rounds[-1]
-
-    def place(self, out, at):
-        turn = lax.axis_index("tensor")
-        out = lax.dynamic_update_slice(out, self.own[None, None], (turn, at, 0, 0))
-        while len(self.rounds) < self.n - 1:
-            self.go()
-        for k in range(1, self.n):
-            piece = self.rounds[k - 1][1] + self.rounds[self.n - k - 1][0]
-            out = lax.dynamic_update_slice(out, piece[None, None], ((turn + k) % self.n, at, 0, 0))
-        return out
+def z_spread(own, n):
+    return [z_shift(own, k, n) for k in range(1, n)]
+
+
+def place_rows(pieces, starts):
+    count, rows = len(pieces), pieces[0].shape[0]
+    shape = (count * rows, pieces[0].shape[1])
+
+    def body(starts_ref, *refs):
+        out, held, coming, going = refs[count:]
+        ins, outs = [], []
+        for k in range(count):
+            span = pl.ds(pl.multiple_of(starts_ref[k], rows), rows)
+            ins.append(pltpu.make_async_copy(refs[k], held.at[k], coming.at[k]))
+            outs.append(pltpu.make_async_copy(held.at[k], out.at[span], going.at[k]))
+        for copy in ins:
+            copy.start()
+        for here, there in zip(ins, outs):
+            here.wait()
+            there.start()
+        for copy in outs:
+            copy.wait()
+
+    place = pl.BlockSpec(memory_space=pl.ANY)
+    return pl.pallas_call(
+        body,
+        in_specs=[pl.BlockSpec(memory_space=pltpu.SMEM)] + [place] * count,
+        out_specs=place,
+        out_shape=jax.ShapeDtypeStruct(shape, pieces[0].dtype),
+        scratch_shapes=[
+            pltpu.VMEM((count, rows, shape[1]), pieces[0].dtype),
+            pltpu.SemaphoreType.DMA((count,)),
+            pltpu.SemaphoreType.DMA((count,)),
+        ],
+        compiler_params=pltpu.CompilerParams(vmem_limit_bytes=VMEM),
+        cost_estimate=LITTLE,
+        name="place_rows",
+    )(starts, *pieces)
 
 
 def small_begin(own, size):
@@ -558,7 +573,7 @@
     z_rec, z_gelu = (
         whole[:, k * d_own : (k + 1) * d_own].transpose(1, 0, 2).reshape(d_own, width) for k in range(2)
     )
-    some_r = spread_begin(z_rec, size, *some_dn[1:])
+    some_r = spread_begin(z_rec, size, *some_dn[1:], own_gu)
     some_small = small_begin(whole[:, 2 * d_own :].reshape(-1, cols), size)
     w_r, came_r = spread_end(some_r, size, (), ())
     small = small_end(some_small, size).reshape(size, n, -1, cols)
@@ -602,9 +617,9 @@
     carry = jnp.zeros((1, width), F32)
     for end in came[::-1]:
         carry = end[1:] + end[:1] * carry
-    z_out = z_gather(*fence([w_out.T.astype(BF)], z_rec), n, ends)
+    z_out = z_gather(w_out.T.astype(BF), n, ends)
     w_g, came_g = spread_end(some_g, size, (rec_pre,), (ends, z_out))
-    some_o = spread_begin(z_out, size, *came_g, ends)
+    some_o = spread_begin(z_out, size, *came_g)
     branch_pre = wide_dot(first_own, w_g)
     recurrent = (state + prod * carry) * live
     mixed = (jax.nn.gelu(branch_pre) * recurrent).astype(BF)
@@ -614,11 +629,11 @@
     second_unit = hidden * second_rate
     second_own = (second_unit * gain[1]).astype(BF)
     some_gu = spread_begin(own_gu, size, *came_o)
-    w_gu, came_gu = spread_end(some_gu, size, (second_own,), ())
+    late = fence([table], second_own)[0]
+    cots = [permute_rows(cotangent, late, half, 2, h) for h in range(2)]
+    w_gu, came_gu = spread_end(some_gu, size, cots, ())
     w_dn, _ = spread_end(some_dn, size, came_gu, ())
     w_gu, w_dn = assemble(w_gu), assemble(w_dn)
-    late = fence([table], second_own)[0]
-    cots = [permute_rows(cotangent, late, half, 2, h) for h in range(2)]
 
     hidden_units = w_dn.shape[1]
     grad_products = [dot(c, w_dn) for c in cots]
@@ -689,14 +704,11 @@
         [((rows + HALO, GROUP), F32), ((rows + 2 * HALO, GROUP), F32), ((rows + SLAB, GROUP), F32), ((GROUP, 2 * GROUP), F32), dense],
         "recurrence_back",
     )
-    line_0 = Line(mlp_result(0, mlp_sums[0]), n)
-    (edge_rows,) = fence([z_shift(drec[:HALO], -1, n, False)], line_0.own)
-    came_0 = line_0.go()
+    (edge_rows,) = fence([z_shift(drec[:HALO], -1, n, False)], mlp_sums[0])
     rec_low = (drec[HALO:] + jnp.pad(edge_rows, ((rows - HALO, 0), (0, 0)))) * live
     rec_low = rec_low.astype(BF)
     (pre_low,) = fence([pre_low], drec)
-    (grad_first,) = fence([wide_back(pre_low, w_g) + wide_back(rec_low, w_r)], *came_0)
-    came_0 = line_0.go()
+    grad_first = wide_back(pre_low, w_g) + wide_back(rec_low, w_r)
     first_unit = inputs * first_rate
     gain_one = jnp.sum(grad_first * first_unit, axis=0)
     grad_tokens = grad_hidden + norm_back(grad_first, first_unit, first_rate, gain[0])
@@ -706,29 +718,29 @@
     sum_o = by_cols(hidden_low, mixed)
     pre_low, rec_low = fence([pre_low, rec_low], sum_o.terms[1])
     sum_g, sum_r = by_cols(first_own, pre_low), by_cols(first_own, rec_low)
-    line_1 = Line(mlp_result(1, *fence(mlp_sums[1:], sum_o.terms[1])), n)
-    got_o = sum_o.hop(fence(sum_o.sources(), line_1.own, *came_0))
-    came_0, came_1 = line_0.go(), line_1.go()
+    results = [mlp_result(h, mlp_sum) for h, mlp_sum in enumerate(fence(mlp_sums, sum_o.terms[1]))]
+    got_o = sum_o.hop(fence(sum_o.sources(), *results))
     got_g = sum_g.hop(fence(sum_g.sources(), *got_o))
     if sum_dn.square:
         sum_dn.hop(fence(sum_dn.sources(), *got_o))
         sum_gu.hop(fence(sum_gu.sources(), *got_o))
-    pause = (gathered[0], *came_0, *came_1, *got_g)
+    pause = (gathered[0], *got_g)
     sum_o.hop(fence(sum_o.sources(), *pause))
     got_r = sum_r.hop(fence(sum_r.sources(), *pause))
-    came_1 = line_1.go(gathered[0], *got_g)
+    results = fence(results, *pause)
+    came_0 = z_spread(results[0], n)
     sum_g.hop(fence(sum_g.sources(), *pause))
-    pause = (gathered[1], *came_1, *got_r)
-    sum_r.hop(fence(sum_r.sources(), *pause))
     d_lru, dpar = fence([d_lru, dpar], *pause)
-    line_1.go(gathered[1])
-    tokens_out = interleave(*fence(gathered, *got_r)).reshape(n * rows, d_model)
+    sum_r.hop(fence(sum_r.sources(), *got_r))
+    owned = jnp.stack([total.finish().reshape(d_own, n, width // n) for total in (sum_o, sum_g, sum_r)])
+    (owned,) = fence([owned.transpose(2, 0, 1, 3)], *came_0)
+    came_1 = z_spread(results[1], n)
+    owned = lax.psum_scatter(owned, "tensor", scatter_dimension=0).astype(F32)
+    tokens_out = interleave(*fence(gathered, *came_0)).reshape(n * rows, d_model)
     g_gu, g_dn = sum_gu.finish().astype(F32), sum_dn.finish().astype(F32)
-    owned = jnp.stack([total.finish().reshape(d_own, n, width // n) for total in (sum_o, sum_g, sum_r)])
-    owned = lax.psum_scatter(owned.transpose(2, 0, 1, 3), "tensor", scatter_dimension=0).astype(F32)
+    starts = [(turn - k) % n * rows + h * half for h in range(2) for k in range(n)]
+    output = place_rows([results[0], *came_0, results[1], *came_1], jnp.stack(starts).astype(jnp.int32))
     g_o, g_g, g_r = owned[0], owned[1], owned[2]
-    output = line_0.place(jnp.zeros((n, 2, half, d_model), BF), 0)
-    output = line_1.place(output, 1).reshape(n * rows, d_model)
 
     d_gain = permute_gain(jnp.stack([gain_one, gain_two]), inverse)
     d_chan = jnp.concatenate([dpar[:7], dpar[7:] * 8.0 * jax.nn.sigmoid(-chans[7:])])

time: 1380 us -> 1300 us (0.942)
  waiting for transfers between devices: 517 us -> 480 us
  other arithmetic: 148 us -> 126 us
  local copies, waits for them, and re-layouts: 150 us -> 135 us
    ppermute x12 -> x0, waiting for transfers between devices: 197 us -> none  [the longest x6 161 us: go(): lax.ppermute(left, 'tensor', [(s, s - 1) for s in range(1, self.n - k + 1)])]
    ppermute x13 -> x19, waiting for transfers between devices: 12 us -> 168 us  [z_shift(): return lax.ppermute(values, 'tensor', pairs)]
    ppermute x58, waiting for transfers between devices: 171 us -> 216 us  [exchange(): return lax.ppermute(values, 'dp', [(k, k ^ 1 << bit) for k in range(size)])]
    reduce_scatter x1, waiting for transfers between devices: 41.9 us -> 0.01 us  [on_device(): owned = lax.psum_scatter(owned, 'tensor', scatter_dimension=0).astype(F32)]
    ppermute x12 -> x0, starting transfers between devices: 20.6 us -> none  [the longest x6 12.8 us: go(): lax.ppermute(right, 'tensor', [(s, s + 1) for s in range(k - 1, self.n -...]
    dynamic_update_slice x6 -> x0, other arithmetic: 16.9 us -> none  [place(): lax.dynamic_update_slice(out, piece[None, None], ((turn + k) % self.n, at...]
    ppermute x13 -> x19, starting transfers between devices: 20.1 us -> 28.8 us  [z_shift(): return lax.ppermute(values, 'tensor', pairs)]
    unnamed x292 -> x278, local copies, waits for them, and re-layouts: 60.4 us -> 53.5 us
  transfers between devices with their start and end apart: 93 -> 87, of which waited for: 39 -> 40; matrix products, arithmetic and copies ran while one was open for 41% -> 41% of each run, Pallas kernels for 9% -> 10%
where the time goes in v7:
time: 1300 us; the launch traced here: 1290 us
  waiting for transfers between devices  480 us (37%)
  matrix products  308 us (24%)
  Pallas kernels  138 us (11%)
  local copies, waits for them, and re-layouts  135 us (10%)
  other arithmetic  126 us (10%)
  starting transfers between devices  83.3 us (6%)
  between operations  17.3 us (1%)
    dot_general x34, matrix products, dot(): lax.dot_general(left, right, (dims, ((), ())), preferred_element_type=F32)  308 us
    ppermute x58, waiting for transfers between devices, exchange(): return lax.ppermute(values, 'dp', [(k, k ^ 1 << bit) for k in range(size)])  216 us
    ppermute x19, waiting for transfers between devices, z_shift(): return lax.ppermute(values, 'tensor', pairs)  168 us
    pallas_call x3, Pallas kernels, kernel_call(): pl.pallas_call(body, grid_spec=pltpu.PrefetchScalarGridSpec(num_scalar_pr...  62.5 us
    convert_element_type x18, other arithmetic, add_all(): return total.astype(BF)  55.2 us
    unnamed x278, local copies, waits for them, and re-layouts  53.5 us
    ppermute x58, starting transfers between devices, exchange(): return lax.ppermute(values, 'dp', [(k, k ^ 1 << bit) for k in range(size)])  53.4 us
    all_gather x1, waiting for transfers between devices, on_device(): whole = lax.all_gather(whole, 'tensor', axis=0)  51.1 us
  transfers between devices with their start and end apart: 87, of which 40 were waited for; matrix products, arithmetic and copies ran while one was open for 41% of the time, Pallas kernels for 10%

profile of v7, /device:TPU:0, one launch (start us, length us, event | category | flops | bytes accessed | tf_op | source)
XLA Modules:
  0.0 1288.3 jit_solution(11726472084044141620)
XLA Ops:
  27.8 51.1 %all-gather.8.cloned.1.call-done = bf16[4,592,640]{2,1,0:T(8,128)(2,1)} async-done(((bf16[1,592,640]{2,1,0:T(8,128)(2,1)}), bf16[4,592,640]{2,1,0:T(8,128)(2,1)}) %all-gather.8.cloned.1.call-update) | async-done | bytes 3031056 | tf_op jit(solution)/shard_map/all_gather | solution.py:572
  109.6 19.9 %collective-permute-done.2 = bf16[160,640]{1,0:T(8,128)(2,1)} collective-permute-done((bf16[160,640]{1,0:T(8,128)(2,1)}, bf16[160,640]{1,0:T(8,128)(2,1)}, u32[]{:S(2)}, u32[]{:S(2)}) %collective-permute-start.2) | collective-permute-done | bytes 204832 | tf_op jit(solution)/shard_map/ppermute | solution.py:79
  185.8 5.4 fusion.43
  196.0 19.3 %collective-permute-done.11.refs_0_ = bf16[256,2560]{1,0:T(8,128)(2,1)S(1)} collective-permute-done((bf16[256,2560]{1,0:T(8,128)(2,1)S(1)}, bf16[256,2560]{1,0:T(8,128)(2,1)S(1)}, u32[]{:S(2)}, u32[]{:S(2)}) %collective-permute-start.11) | collective-permute-done | bytes 1310752 | tf_op jit(solution)/shard_map/ppermute | solution.py:79
  224.7 18.9 %recurrence.1 = (f32[512,2560]{1,0:T(8,128)}, f32[512,2560]{1,0:T(8,128)}, f32[512,2560]{1,0:T(8,128)}, f32[512,2560]{1,0:T(8,128)}, f32[512,2560]{1,0:T(8,128)}, /*index=5*/f32[512,2560]{1,0:T(8,128)}) custom-call(s32[1]{0:T(128)} %sub.61.live_ref, f32[528,2560]{1,0:T(8,128)} %convolution_add_fusion.refs_2_.pre_ref, f32[8,2560]{1,0:T(8,128)} %pad_maximum_fusion.12.par_ref, ...), custom_call_target="tpu_custom_call" | custom-call | flops 1024 | bytes 1024 | tf_op jit(solution)/shard_map/recurrence/pallas_call | solution.py:511
  269.9 9.7 fusion.22
  279.6 14.0 %collective-permute-done.24.refs_1_ = bf16[256,2560]{1,0:T(8,128)(2,1)S(1)} collective-permute-done((bf16[256,2560]{1,0:T(8,128)(2,1)}, bf16[256,2560]{1,0:T(8,128)(2,1)S(1)}, u32[]{:S(2)}, u32[]{:S(2)}) %collective-permute-start.24) | collective-permute-done | bytes 1310752 | tf_op jit(solution)/shard_map/ppermute | solution.py:79
  299.7 12.6 collective-permute-done.25.refs_2_
  323.3 5.7 fusion.81
  338.2 5.8 permute.8.refs_3_
  344.0 5.9 permute.7.refs_2_
  349.9 8.4 collective-permute-done.29.refs_1_
  365.6 15.6 %collective-permute-done.30.refs_2_.refs_3_ = bf16[128,3072]{1,0:T(8,128)(2,1)S(1)} collective-permute-done((bf16[128,3072]{1,0:T(8,128)(2,1)S(1)}, bf16[128,3072]{1,0:T(8,128)(2,1)S(1)}, u32[]{:S(2)}, u32[]{:S(2)}) %collective-permute-start.30) | collective-permute-done | bytes 786464 | tf_op jit(solution)/shard_map/ppermute | solution.py:79
  383.0 5.3 assemble.10.refs_0_
  392.5 9.5 collective-permute-done.33.refs_2_
  407.0 5.3 collective-permute-done.35.refs_1_
  418.7 9.3 assemble.11
  428.0 17.3 %all-gather.10.cloned.1.call-done = bf16[1024,2048]{1,0:T(8,128)(2,1)} async-done(((bf16[256,2048]{1,0:T(8,128)(2,1)}), bf16[1024,2048]{1,0:T(8,128)(2,1)}) %all-gather.10.cloned.1.call-update) | async-done | bytes 4194320 | tf_op jit(solution)/shard_map/all_gather | solution.py:642
  445.3 19.2 %fusion.83 = f32[1024,3072]{1,0:T(8,128)} fusion(bf16[1024,2048]{1,0:T(8,128)(2,1)} %all-gather.10.cloned.1.call-done, bf16[2048,3072]{1,0:T(8,128)(2,1)} %assemble.11), kind=kOutput, calls=%fused_computation.286 | convolution fusion | flops 12884901888 | bytes 29360128 | tf_op jit(solution)/shard_map/dot_general | solution.py:24
  464.4 14.6 %fusion.6 = (bf16[1024,1536]{1,0:T(8,128)(2,1)S(1)}, bf16[1024,1536]{1,0:T(8,128)(2,1)S(1)}, bf16[1024,1536]{1,0:T(8,128)(2,1)}) fusion(f32[1024,3072]{1,0:T(8,128)} %fusion.83, bf16[1024,2048]{1,0:T(8,128)(2,1)S(1)} %copy-done.14, bf16[2048,1536]{1,0:T(8,128)(2,1)S(1)} %copy-done.47), kind=kOutput, calls=%fused_computation.16 | convolution fusion | flops 6483345408 | bytes 32505856 | tf_op jit(solution)/shard_map/dot_general | solution.py:24
  480.7 17.6 %convolution_convert_fusion.7.refs_1_ = bf16[1024,2048]{1,0:T(8,128)(2,1)} fusion(bf16[2048,3072]{1,0:T(8,128)(2,1)} %assemble.11, bf16[1024,1536]{1,0:T(8,128)(2,1)S(1)} %get-tuple-element.205, bf16[1024,1536]{1,0:T(8,128)(2,1)S(1)} %get-tuple-element.204), kind=kOutput, calls=%fused_computation.73 | convolution fusion | flops 12899581952 | bytes 23068672 | tf_op jit(solution)/shard_map/dot_general | solution.py:24
  498.6 27.6 %all-gather.12.cloned.1.call-done.refs_0_ = bf16[1024,2048]{1,0:T(8,128)(2,1)} async-done(((bf16[256,2048]{1,0:T(8,128)(2,1)}), bf16[1024,2048]{1,0:T(8,128)(2,1)}) %all-gather.12.cloned.1.call-update) | async-done | bytes 4194320 | tf_op jit(solution)/shard_map/all_gather | solution.py:642
  526.2 19.2 %fusion.84 = f32[1024,3072]{1,0:T(8,128)} fusion(bf16[1024,2048]{1,0:T(8,128)(2,1)} %fence.43, bf16[2048,3072]{1,0:T(8,128)(2,1)} %assemble.11), kind=kOutput, calls=%fused_computation.287 | convolution fusion | flops 12884901888 | bytes 29360128 | tf_op jit(solution)/shard_map/dot_general | solution.py:24
  545.4 15.4 %fusion.13 = (bf16[1024,1536]{1,0:T(8,128)(2,1)}, bf16[1024,1536]{1,0:T(8,128)(2,1)}, bf16[1024,1536]{1,0:T(8,128)(2,1)}) fusion(f32[1024,3072]{1,0:T(8,128)} %fusion.84, bf16[1024,2048]{1,0:T(8,128)(2,1)S(1)} %copy-done.17, bf16[2048,1536]{1,0:T(8,128)(2,1)S(1)} %bitcast.241), kind=kOutput, calls=%fused_computation.23 | convolution fusion | flops 6483345408 | bytes 32505856 | tf_op jit(solution)/shard_map/dot_general | solution.py:24
  560.8 5.6 pad_maximum_fusion.refs_1_
  566.3 18.7 %convolution_convert_fusion.6.refs_2_ = bf16[1024,2048]{1,0:T(8,128)(2,1)} fusion(bf16[2048,3072]{1,0:T(8,128)(2,1)} %assemble.11, bf16[1024,1536]{1,0:T(8,128)(2,1)} %get-tuple-element.203, bf16[1024,1536]{1,0:T(8,128)(2,1)S(1)} %copy-done.58), kind=kOutput, calls=%fused_computation.72 | convolution fusion | flops 12899581952 | bytes 23068672 | tf_op jit(solution)/shard_map/dot_general | solution.py:24
  586.9 5.7 pad_maximum_fusion.1.refs_1_
  592.6 7.4 fusion.37
  600.1 8.4 convolution_convert_fusion.9.refs_6_.refs_0_
  608.6 9.7 add_convert_fusion.2
  618.3 9.7 fusion.31
  628.1 11.8 add_convert_fusion
  640.3 11.1 fusion.34
  651.4 11.3 convolution_convert_fusion.8.refs_7_.refs_1_
  662.7 5.4 fusion.40
  668.1 7.1 add_convert_fusion.3
  675.1 10.2 add_convert_fusion.1
  708.5 5.7 fusion.49
  719.5 17.1 %back_scan.1 = (f32[512,2560]{1,0:T(8,128)}, f32[512,2560]{1,0:T(8,128)}, f32[8,2560]{1,0:T(8,128)}, bf16[512,2560]{1,0:T(8,128)(2,1)}) custom-call(s32[1]{0:T(128)} %sub.61.live_ref, f32[512,2560]{1,0:T(8,128)} %get-tuple-element.260.refs_2_.pre_ref, f32[512,2560]{1,0:T(8,128)} %convolution_add_fusion.1.grad_ref, f32[512,2560]{1,0:T(8,128)} %get-tuple-element.90.decay_ref, ...), custom_call_target="tpu_custom_call" | custom-call | flops 1024 | bytes 1024 | tf_op jit(solution)/shard_map/back_scan/pallas_call | solution.py:511
  741.6 11.2 collective-permute-done.41.refs_4_
  754.6 26.6 %recurrence_back.1 = (f32[528,2560]{1,0:T(8,128)}, f32[8,2560]{1,0:T(8,128)}, bf16[4,160,1280]{2,1,0:T(8,128)(2,1)}) custom-call(s32[1]{0:T(128)} %sub.61.live_ref, f32[528,2560]{1,0:T(8,128)} %convolution_add_fusion.refs_2_.pre_ref, f32[8,2560]{1,0:T(8,128)} %pad_maximum_fusion.12.par_ref, ...), custom_call_target="tpu_custom_call" | custom-call | flops 1024 | bytes 1024 | tf_op jit(solution)/shard_map/recurrence_back/pallas_call | solution.py:511
  781.2 8.0 fusion.85
  791.4 6.8 fusion.86
  798.2 6.7 collective-permute-done.45.refs_0_
  808.4 6.5 fusion.87
  822.6 6.1 add_convert_fusion.4.in_ref
  833.9 6.5 convolution_convert_fusion.5
  845.6 6.2 convolution_convert_fusion.2
  851.8 7.3 convolution_convert_fusion.3
  879.1 6.0 convolution_convert_fusion
  890.1 7.5 convolution_convert_fusion.4
  897.5 6.2 convolution_convert_fusion.1
  916.1 6.1 collective-permute-done.75
  933.3 5.8 collective-permute-done.73
  952.7 12.3 collective-permute-done.50.refs_3_
  1016.2 10.8 collective-permute-done.58
  1030.1 22.2 %collective-permute-done.69.refs_3_ = bf16[256,2560]{1,0:T(8,128)(2,1)} collective-permute-done((bf16[256,2560]{1,0:T(8,128)(2,1)}, bf16[256,2560]{1,0:T(8,128)(2,1)}, u32[]{:S(2)}, u32[]{:S(2)}) %collective-permute-start.69) | collective-permute-done | bytes 1310752 | tf_op jit(solution)/shard_map/ppermute | solution.py:79
  1058.2 6.9 collective-permute-done.59
  1066.3 9.3 collective-permute-done.71
  1084.2 24.5 %collective-permute-done.53.refs_2_.refs_3_ = bf16[256,2048]{1,0:T(8,128)(2,1)} collective-permute-done((bf16[256,2048]{1,0:T(8,128)(2,1)}, bf16[256,2048]{1,0:T(8,128)(2,1)}, u32[]{:S(2)}, u32[]{:S(2)}) %collective-permute-start.53) | collective-permute-done | bytes 1048608 | tf_op jit(solution)/shard_map/ppermute | solution.py:162
  1117.9 52.8 %collective-permute-done.57.refs_7_ = bf16[256,2048]{1,0:T(8,128)(2,1)S(1)} collective-permute-done((bf16[256,2048]{1,0:T(8,128)(2,1)S(1)}, bf16[256,2048]{1,0:T(8,128)(2,1)S(1)}, u32[]{:S(2)}, u32[]{:S(2)}) %collective-permute-start.57) | collective-permute-done | bytes 1048608 | tf_op jit(solution)/shard_map/ppermute | solution.py:162
  1177.6 7.0 interleave.1
  1184.6 83.1 %collective-permute-done.56.refs_6_ = bf16[256,2048]{1,0:T(8,128)(2,1)} collective-permute-done((bf16[256,2048]{1,0:T(8,128)(2,1)S(1)}, bf16[256,2048]{1,0:T(8,128)(2,1)}, u32[]{:S(2)}, u32[]{:S(2)}) %collective-permute-start.56) | collective-permute-done | bytes 1048608 | tf_op jit(solution)/shard_map/ppermute | solution.py:162
  1267.7 7.1 place_rows.1
  (642 shorter events, 414.4 us)
Async XLA Ops:
  7.2 71.7 %all-gather.8.cloned.1.call-start = ((), (), s32[]{:S(2)}) async-start(), calls=%async_computation.5 | async-start | bytes 3788800 | tf_op jit(solution)/shard_map/all_gather | solution.py:572
  13.3 431.9 %all-gather.10.cloned.1.call-start = ((), (), s32[]{:S(2)}) async-start(), calls=%async_computation.6 | async-start | bytes 5242880 | tf_op jit(solution)/shard_map/all_gather | solution.py:642
  14.6 78.5 %collective-permute-start.6 = (bf16[256,1536]{1,0:T(8,128)(2,1)}, bf16[256,1536]{1,0:T(8,128)(2,1)S(1)}, u32[]{:S(2)}, u32[]{:S(2)}) collective-permute-start(bf16[256,1536]{1,0:T(8,128)(2,1)} %bitcast.168.refs_0_), channel_id=1, source_target_pairs={{0,16},{4,20},{8,24},{12,28},{16,0},{20,4},{24,8},{28,12},{1,17},{... | collective-permute-start | bytes 2359304 | tf_op jit(solution)/shard_map/ppermute | solution.py:79
  18.7 74.5 %collective-permute-start.5 = (bf16[256,1536]{1,0:T(8,128)(2,1)}, bf16[256,1536]{1,0:T(8,128)(2,1)S(1)}, u32[]{:S(2)}, u32[]{:S(2)}) collective-permute-start(bf16[256,1536]{1,0:T(8,128)(2,1)} %bitcast.168.refs_0_), channel_id=1, source_target_pairs={{0,8},{4,12},{8,0},{12,4},{16,24},{20,28},{24,16},{28,20},{1,9},{5... | collective-permute-start | bytes 2359304 | tf_op jit(solution)/shard_map/ppermute | solution.py:79
  82.3 15.9 %collective-permute-start = (bf16[320,640]{1,0:T(8,128)(2,1)}, bf16[320,640]{1,0:T(8,128)(2,1)}, u32[]{:S(2)}, u32[]{:S(2)}) collective-permute-start(bf16[320,640]{1,0:T(8,128)(2,1)} %bitcast.14), channel_id=1, source_target_pairs={{0,8},{4,12},{8,0},{12,4},{16,24},{20,28},{24,16},{28,20},{1,9},{5... | collective-permute-start | bytes 1228808 | tf_op jit(solution)/shard_map/ppermute | solution.py:79
  94.9 42.9 %collective-permute-start.9 = (bf16[256,2560]{1,0:T(8,128)(2,1)}, bf16[256,2560]{1,0:T(8,128)(2,1)}, u32[]{:S(2)}, u32[]{:S(2)}) collective-permute-start(bf16[256,2560]{1,0:T(8,128)(2,1)} %fence.33.refs_0_), channel_id=1, source_target_pairs={{0,16},{4,20},{8,24},{12,28},{16,0},{20,4},{24,8},{28,12},{1,17},{... | collective-permute-start | bytes 3932168 | tf_op jit(solution)/shard_map/ppermute | solution.py:79
  95.5 44.8 %collective-permute-start.7 = (bf16[256,2560]{1,0:T(8,128)(2,1)}, bf16[256,2560]{1,0:T(8,128)(2,1)}, u32[]{:S(2)}, u32[]{:S(2)}) collective-permute-start(bf16[256,2560]{1,0:T(8,128)(2,1)} %fence.33.refs_0_), channel_id=1, source_target_pairs={{0,8},{4,12},{8,0},{12,4},{16,24},{20,28},{24,16},{28,20},{1,9},{5... | collective-permute-start | bytes 3932168 | tf_op jit(solution)/shard_map/ppermute | solution.py:79
  96.8 35.0 %collective-permute-start.3 = (bf16[160,640]{1,0:T(8,128)(2,1)}, bf16[160,640]{1,0:T(8,128)(2,1)}, u32[]{:S(2)}, u32[]{:S(2)}) collective-permute-start(bf16[160,640]{1,0:T(8,128)(2,1)} %slice.755), channel_id=1, source_target_pairs={{0,8},{4,12},{8,0},{12,4},{16,24},{20,28},{24,16},{28,20},{1,9},{5... | collective-permute-start | bytes 614408 | tf_op jit(solution)/shard_map/ppermute | solution.py:79
  99.9 29.7 %collective-permute-start.2 = (bf16[160,640]{1,0:T(8,128)(2,1)}, bf16[160,640]{1,0:T(8,128)(2,1)}, u32[]{:S(2)}, u32[]{:S(2)}) collective-permute-start(bf16[160,640]{1,0:T(8,128)(2,1)} %slice.754), channel_id=1, source_target_pairs={{0,16},{4,20},{8,24},{12,28},{16,0},{20,4},{24,8},{28,12},{1,17},{... | collective-permute-start | bytes 614408 | tf_op jit(solution)/shard_map/ppermute | solution.py:79
  103.8 142.2 %collective-permute-start.17 = (bf16[256,640]{1,0:T(8,128)(2,1)}, bf16[256,640]{1,0:T(8,128)(2,1)}, u32[]{:S(2)}, u32[]{:S(2)}) collective-permute-start(bf16[256,640]{1,0:T(8,128)(2,1)} %bitcast.170), channel_id=1, source_target_pairs={{0,2},{1,3},{2,0},{3,1},{4,6},{5,7},{6,4},{7,5},{8,10},{9,11},{10,... | collective-permute-start | bytes 983048 | tf_op jit(solution)/shard_map/ppermute | solution.py:162
  129.5 116.5 %collective-permute-start.16 = (bf16[256,640]{1,0:T(8,128)(2,1)}, bf16[256,640]{1,0:T(8,128)(2,1)}, u32[]{:S(2)}, u32[]{:S(2)}) collective-permute-start(bf16[256,640]{1,0:T(8,128)(2,1)} %bitcast.170), channel_id=1, source_target_pairs={{0,3},{1,0},{2,1},{3,2},{4,7},{5,4},{6,5},{7,6},{8,11},{9,8},{10,9... | collective-permute-start | bytes 983048 | tf_op jit(solution)/shard_map/ppermute | solution.py:162
  135.5 28.5 %collective-permute-start.4 = (bf16[4,320,640]{2,1,0:T(8,128)(2,1)}, bf16[4,320,640]{2,1,0:T(8,128)(2,1)}, u32[]{:S(2)}, u32[]{:S(2)}) collective-permute-start(bf16[4,320,640]{2,1,0:T(8,128)(2,1)} %pad_maximum_fusion.6), channel_id=1, source_target_pairs={{0,4},{4,0},{8,12},{12,8},{16,20},{20,16},{24,28},{28,24},{1,5},{5... | collective-permute-start | bytes 4915208 | tf_op jit(solution)/shard_map/ppermute | solution.py:79
  139.8 17.5 %collective-permute-start.10 = (bf16[128,2560]{1,0:T(8,128)(2,1)}, bf16[128,2560]{1,0:T(8,128)(2,1)}, u32[]{:S(2)}, u32[]{:S(2)}) collective-permute-start(bf16[128,2560]{1,0:T(8,128)(2,1)} %slice.780), channel_id=1, source_target_pairs={{0,8},{4,12},{8,0},{12,4},{16,24},{20,28},{24,16},{28,20},{1,9},{5... | collective-permute-start | bytes 1966088 | tf_op jit(solution)/shard_map/ppermute | solution.py:79
  142.3 17.2 %collective-permute-start.8 = (bf16[128,2560]{1,0:T(8,128)(2,1)}, bf16[128,2560]{1,0:T(8,128)(2,1)}, u32[]{:S(2)}, u32[]{:S(2)}) collective-permute-start(bf16[128,2560]{1,0:T(8,128)(2,1)} %slice.779), channel_id=1, source_target_pairs={{0,16},{4,20},{8,24},{12,28},{16,0},{20,4},{24,8},{28,12},{1,17},{... | collective-permute-start | bytes 1966088 | tf_op jit(solution)/shard_map/ppermute | solution.py:79
  157.2 88.8 %collective-permute-start.18 = (bf16[256,640]{1,0:T(8,128)(2,1)}, bf16[256,640]{1,0:T(8,128)(2,1)}, u32[]{:S(2)}, u32[]{:S(2)}) collective-permute-start(bf16[256,640]{1,0:T(8,128)(2,1)} %bitcast.170), channel_id=1, source_target_pairs={{0,1},{1,2},{2,3},{3,0},{4,5},{5,6},{6,7},{7,4},{8,9},{9,10},{10,1... | collective-permute-start | bytes 983048 | tf_op jit(solution)/shard_map/ppermute | solution.py:162
  159.5 36.6 %collective-permute-start.12 = (bf16[256,2560]{1,0:T(8,128)(2,1)}, bf16[256,2560]{1,0:T(8,128)(2,1)}, u32[]{:S(2)}, u32[]{:S(2)}) collective-permute-start(bf16[256,2560]{1,0:T(8,128)(2,1)} %fence.34.refs_0_), channel_id=1, source_target_pairs={{0,16},{4,20},{8,24},{12,28},{16,0},{20,4},{24,8},{28,12},{1,17},{... | collective-permute-start | bytes 3932168 | tf_op jit(solution)/shard_map/ppermute | solution.py:79
  164.0 20.0 %collective-permute-start.13 = (bf16[1024,2560]{1,0:T(8,128)(2,1)}, bf16[1024,2560]{1,0:T(8,128)(2,1)}, u32[]{:S(2)}, u32[]{:S(2)}) collective-permute-start(bf16[1024,2560]{1,0:T(8,128)(2,1)} %assemble.7), channel_id=1, source_target_pairs={{0,4},{4,0},{8,12},{12,8},{16,20},{20,16},{24,28},{28,24},{1,5},{5... | collective-permute-start | bytes 15728648 | tf_op jit(solution)/shard_map/ppermute | solution.py:79
  184.1 31.2 %collective-permute-start.11 = (bf16[256,2560]{1,0:T(8,128)(2,1)S(1)}, bf16[256,2560]{1,0:T(8,128)(2,1)S(1)}, u32[]{:S(2)}, u32[]{:S(2)}) collective-permute-start(bf16[256,2560]{1,0:T(8,128)(2,1)S(1)} %copy-done.28), channel_id=1, source_target_pairs={{0,8},{4,12},{8,0},{12,4},{16,24},{20,28},{24,16},{28,20},{1,9},{5... | collective-permute-start | bytes 3932168 | tf_op jit(solution)/shard_map/ppermute | solution.py:79
  220.3 29.2 %collective-permute-start.14 = (bf16[128,2560]{1,0:T(8,128)(2,1)}, bf16[128,2560]{1,0:T(8,128)(2,1)S(1)}, u32[]{:S(2)}, u32[]{:S(2)}) collective-permute-start(bf16[128,2560]{1,0:T(8,128)(2,1)} %slice.597), channel_id=1, source_target_pairs={{0,8},{4,12},{8,0},{12,4},{16,24},{20,28},{24,16},{28,20},{1,9},{5... | collective-permute-start | bytes 1966088 | tf_op jit(solution)/shard_map/ppermute | solution.py:79
  222.0 27.5 %collective-permute-start.15 = (bf16[128,2560]{1,0:T(8,128)(2,1)}, bf16[128,2560]{1,0:T(8,128)(2,1)}, u32[]{:S(2)}, u32[]{:S(2)}) collective-permute-start(bf16[128,2560]{1,0:T(8,128)(2,1)} %slice.598), channel_id=1, source_target_pairs={{0,16},{4,20},{8,24},{12,28},{16,0},{20,4},{24,8},{28,12},{1,17},{... | collective-permute-start | bytes 1966088 | tf_op jit(solution)/shard_map/ppermute | solution.py:79
  263.4 30.2 %collective-permute-start.24 = (bf16[256,2560]{1,0:T(8,128)(2,1)}, bf16[256,2560]{1,0:T(8,128)(2,1)S(1)}, u32[]{:S(2)}, u32[]{:S(2)}) collective-permute-start(bf16[256,2560]{1,0:T(8,128)(2,1)} %fence.37.refs_0_), channel_id=1, source_target_pairs={{0,16},{4,20},{8,24},{12,28},{16,0},{20,4},{24,8},{28,12},{1,17},{... | collective-permute-start | bytes 3932168 | tf_op jit(solution)/shard_map/ppermute | solution.py:79
  264.1 29.8 %collective-permute-start.23 = (bf16[256,2560]{1,0:T(8,128)(2,1)}, bf16[256,2560]{1,0:T(8,128)(2,1)S(1)}, u32[]{:S(2)}, u32[]{:S(2)}) collective-permute-start(bf16[256,2560]{1,0:T(8,128)(2,1)} %fence.37.refs_0_), channel_id=1, source_target_pairs={{0,8},{4,12},{8,0},{12,4},{16,24},{20,28},{24,16},{28,20},{1,9},{5... | collective-permute-start | bytes 3932168 | tf_op jit(solution)/shard_map/ppermute | solution.py:79
  321.2 37.0 %collective-permute-start.29 = (bf16[256,3072]{1,0:T(8,128)(2,1)}, bf16[256,3072]{1,0:T(8,128)(2,1)S(1)}, u32[]{:S(2)}, u32[]{:S(2)}) collective-permute-start(bf16[256,3072]{1,0:T(8,128)(2,1)} %fence.39.refs_0_), channel_id=1, source_target_pairs={{0,16},{4,20},{8,24},{12,28},{16,0},{20,4},{24,8},{28,12},{1,17},{... | collective-permute-start | bytes 4718600 | tf_op jit(solution)/shard_map/ppermute | solution.py:79
  322.3 36.8 %collective-permute-start.28 = (bf16[256,3072]{1,0:T(8,128)(2,1)}, bf16[256,3072]{1,0:T(8,128)(2,1)}, u32[]{:S(2)}, u32[]{:S(2)}) collective-permute-start(bf16[256,3072]{1,0:T(8,128)(2,1)} %fence.39.refs_0_), channel_id=1, source_target_pairs={{0,8},{4,12},{8,0},{12,4},{16,24},{20,28},{24,16},{28,20},{1,9},{5... | collective-permute-start | bytes 4718600 | tf_op jit(solution)/shard_map/ppermute | solution.py:79
  361.9 19.3 %collective-permute-start.30 = (bf16[128,3072]{1,0:T(8,128)(2,1)S(1)}, bf16[128,3072]{1,0:T(8,128)(2,1)S(1)}, u32[]{:S(2)}, u32[]{:S(2)}) collective-permute-start(bf16[128,3072]{1,0:T(8,128)(2,1)S(1)} %slice.617), channel_id=1, source_target_pairs={{0,8},{4,12},{8,0},{12,4},{16,24},{20,28},{24,16},{28,20},{1,9},{5... | collective-permute-start | bytes 2359304 | tf_op jit(solution)/shard_map/ppermute | solution.py:79
  363.0 19.0 %collective-permute-start.31 = (bf16[128,3072]{1,0:T(8,128)(2,1)S(1)}, bf16[128,3072]{1,0:T(8,128)(2,1)S(1)}, u32[]{:S(2)}, u32[]{:S(2)}) collective-permute-start(bf16[128,3072]{1,0:T(8,128)(2,1)S(1)} %slice.618), channel_id=1, source_target_pairs={{0,16},{4,20},{8,24},{12,28},{16,0},{20,4},{24,8},{28,12},{1,17},{... | collective-permute-start | bytes 2359304 | tf_op jit(solution)/shard_map/ppermute | solution.py:79
  365.6 160.6 %all-gather.12.cloned.1.call-start = ((), (), s32[]{:S(2)}) async-start(), calls=%async_computation.7 | async-start | bytes 5242880 | tf_op jit(solution)/shard_map/all_gather | solution.py:642
  388.3 30.4 %collective-permute-start.32 = (bf16[1024,3072]{1,0:T(8,128)(2,1)}, bf16[1024,3072]{1,0:T(8,128)(2,1)}, u32[]{:S(2)}, u32[]{:S(2)}) collective-permute-start(bf16[1024,3072]{1,0:T(8,128)(2,1)} %assemble.10.refs_0_), channel_id=1, source_target_pairs={{0,4},{4,0},{8,12},{12,8},{16,20},{20,16},{24,28},{28,24},{1,5},{5... | collective-permute-start | bytes 18874376 | tf_op jit(solution)/shard_map/ppermute | solution.py:79
  406.5 289.3 %reduce-scatter.6.cloned.1.call-start = ((), (), s32[]{:S(2)}) async-start(), calls=%async_computation.8 | async-start | bytes 5242880 | tf_op jit(solution)/shard_map/reduce_scatter | solution.py:651
  498.4 197.4 %reduce-scatter.8.cloned.1.call-start = ((), (), s32[]{:S(2)}) async-start(), calls=%async_computation.9 | async-start | bytes 5242880 | tf_op jit(solution)/shard_map/reduce_scatter | solution.py:651
  608.5 196.4 %reduce-scatter.10.cloned.1.call-start = ((), (), s32[]{:S(2)}) async-start(), calls=%async_computation.10 | async-start | bytes 5242880 | tf_op jit(solution)/shard_map/reduce_scatter | solution.py:676
  618.3 67.0 %collective-permute-start.36 = (bf16[1024,1536]{1,0:T(8,128)(2,1)}, bf16[1024,1536]{1,0:T(8,128)(2,1)S(1)}, u32[]{:S(2)}, u32[]{:S(2)}) collective-permute-start(bf16[1024,1536]{1,0:T(8,128)(2,1)} %add_convert_fusion.2), channel_id=1, source_target_pairs={{0,4},{4,0},{8,12},{12,8},{16,20},{20,16},{24,28},{28,24},{1,5},{5... | collective-permute-start | bytes 9437192 | tf_op jit(solution)/shard_map/ppermute | solution.py:79
  639.8 51.2 %collective-permute-start.37 = (bf16[1024,3072]{1,0:T(8,128)(2,1)}, bf16[1024,3072]{1,0:T(8,128)(2,1)}, u32[]{:S(2)}, u32[]{:S(2)}) collective-permute-start(bf16[1024,3072]{1,0:T(8,128)(2,1)} %add_convert_fusion), channel_id=1, source_target_pairs={{0,4},{4,0},{8,12},{12,8},{16,20},{20,16},{24,28},{28,24},{1,5},{5... | collective-permute-start | bytes 18874376 | tf_op jit(solution)/shard_map/ppermute | solution.py:79
  695.9 163.8 %reduce-scatter.12.cloned.1.call-start = ((), (), s32[]{:S(2)}) async-start(), calls=%async_computation.11 | async-start | bytes 5242880 | tf_op jit(solution)/shard_map/reduce_scatter | solution.py:676
  699.3 39.5 %collective-permute-start.39 = (bf16[256,1536]{1,0:T(8,128)(2,1)}, bf16[256,1536]{1,0:T(8,128)(2,1)}, u32[]{:S(2)}, u32[]{:S(2)}) collective-permute-start(bf16[256,1536]{1,0:T(8,128)(2,1)} %get-tuple-element.236.refs_3_), channel_id=1, source_target_pairs={{0,16},{4,20},{8,24},{12,28},{16,0},{20,4},{24,8},{28,12},{1,17},{... | collective-permute-start | bytes 2359304 | tf_op jit(solution)/shard_map/ppermute | solution.py:79
  700.7 39.4 %collective-permute-start.38 = (bf16[256,1536]{1,0:T(8,128)(2,1)}, bf16[256,1536]{1,0:T(8,128)(2,1)}, u32[]{:S(2)}, u32[]{:S(2)}) collective-permute-start(bf16[256,1536]{1,0:T(8,128)(2,1)} %get-tuple-element.237.refs_2_), channel_id=1, source_target_pairs={{0,8},{4,12},{8,0},{12,4},{16,24},{20,28},{24,16},{28,20},{1,9},{5... | collective-permute-start | bytes 2359304 | tf_op jit(solution)/shard_map/ppermute | solution.py:79
  702.2 50.6 %collective-permute-start.41 = (bf16[256,3072]{1,0:T(8,128)(2,1)}, bf16[256,3072]{1,0:T(8,128)(2,1)}, u32[]{:S(2)}, u32[]{:S(2)}) collective-permute-start(bf16[256,3072]{1,0:T(8,128)(2,1)} %get-tuple-element.210.refs_5_), channel_id=1, source_target_pairs={{0,16},{4,20},{8,24},{12,28},{16,0},{20,4},{24,8},{28,12},{1,17},{... | collective-permute-start | bytes 4718600 | tf_op jit(solution)/shard_map/ppermute | solution.py:79
  702.7 51.1 %collective-permute-start.40 = (bf16[256,3072]{1,0:T(8,128)(2,1)}, bf16[256,3072]{1,0:T(8,128)(2,1)}, u32[]{:S(2)}, u32[]{:S(2)}) collective-permute-start(bf16[256,3072]{1,0:T(8,128)(2,1)} %get-tuple-element.211.refs_4_), channel_id=1, source_target_pairs={{0,8},{4,12},{8,0},{12,4},{16,24},{20,28},{24,16},{28,20},{1,9},{5... | collective-permute-start | bytes 4718600 | tf_op jit(solution)/shard_map/ppermute | solution.py:79
  737.5 16.4 %collective-permute-start.44 = (f32[2,2560]{1,0:T(2,128)S(1)}, f32[2,2560]{1,0:T(2,128)S(1)}, u32[]{:S(2)}, u32[]{:S(2)}) collective-permute-start(f32[2,2560]{1,0:T(2,128)S(1)} %pad_maximum_fusion.14), channel_id=1, source_target_pairs={{3,0},{7,4},{11,8},{15,12},{19,16},{23,20},{27,24},{31,28}} | collective-permute-start | bytes 61448 | tf_op jit(solution)/shard_map/ppermute | solution.py:162
  741.5 211.2 %all-gather.14.cloned.1.call-start = ((), (), s32[]{:S(2)}) async-start(), calls=%async_computation.13 | async-start | bytes 5242880 | tf_op jit(solution)/shard_map/all_gather | solution.py:716
  842.0 335.6 %all-gather.16.cloned.1.call-start = ((), (), s32[]{:S(2)}) async-start(), calls=%async_computation.14 | async-start | bytes 5242880 | tf_op jit(solution)/shard_map/all_gather | solution.py:716
  859.1 67.7 %collective-permute-start.47 = (bf16[1024,2560]{1,0:T(8,128)(2,1)}, bf16[1024,2560]{1,0:T(8,128)(2,1)}, u32[]{:S(2)}, u32[]{:S(2)}) collective-permute-start(bf16[1024,2560]{1,0:T(8,128)(2,1)} %convolution_convert_fusion.3), channel_id=1, source_target_pairs={{0,4},{4,0},{8,12},{12,8},{16,20},{20,16},{24,28},{28,24},{1,5},{5... | collective-permute-start | bytes 15728648 | tf_op jit(solution)/shard_map/ppermute | solution.py:79
  876.5 30.9 %collective-permute-start.48 = (bf16[256,2560]{1,0:T(8,128)(2,1)}, bf16[256,2560]{1,0:T(8,128)(2,1)S(1)}, u32[]{:S(2)}, u32[]{:S(2)}) collective-permute-start(bf16[256,2560]{1,0:T(8,128)(2,1)} %get-tuple-element.102), channel_id=1, source_target_pairs={{0,8},{4,12},{8,0},{12,4},{16,24},{20,28},{24,16},{28,20},{1,9},{5... | collective-permute-start | bytes 3932168 | tf_op jit(solution)/shard_map/ppermute | solution.py:79
  878.2 30.6 %collective-permute-start.49 = (bf16[256,2560]{1,0:T(8,128)(2,1)}, bf16[256,2560]{1,0:T(8,128)(2,1)S(1)}, u32[]{:S(2)}, u32[]{:S(2)}) collective-permute-start(bf16[256,2560]{1,0:T(8,128)(2,1)} %get-tuple-element.103), channel_id=1, source_target_pairs={{0,16},{4,20},{8,24},{12,28},{16,0},{20,4},{24,8},{28,12},{1,17},{... | collective-permute-start | bytes 3932168 | tf_op jit(solution)/shard_map/ppermute | solution.py:79
  885.1 63.7 %collective-permute-start.68 = (bf16[1024,2560]{1,0:T(8,128)(2,1)}, bf16[1024,2560]{1,0:T(8,128)(2,1)}, u32[]{:S(2)}, u32[]{:S(2)}) collective-permute-start(bf16[1024,2560]{1,0:T(8,128)(2,1)} %convolution_convert_fusion), channel_id=1, source_target_pairs={{0,4},{4,0},{8,12},{12,8},{16,20},{20,16},{24,28},{28,24},{1,5},{5... | collective-permute-start | bytes 15728648 | tf_op jit(solution)/shard_map/ppermute | solution.py:79
  890.0 387.4 %reduce-scatter.14.cloned.1.call-start = ((), (), s32[]{:S(2)}) async-start(), calls=%async_computation.12 | async-start | bytes 4915200 | tf_op jit(solution)/shard_map/reduce_scatter | solution.py:738
  911.5 27.6 %collective-permute-start.73 = (bf16[128,3072]{1,0:T(8,128)(2,1)}, bf16[128,3072]{1,0:T(8,128)(2,1)}, u32[]{:S(2)}, u32[]{:S(2)}) collective-permute-start(bf16[128,3072]{1,0:T(8,128)(2,1)} %get-tuple-element.123), channel_id=1, source_target_pairs={{0,8},{4,12},{8,0},{12,4},{16,24},{20,28},{24,16},{28,20},{1,9},{5... | collective-permute-start | bytes 2359304 | tf_op jit(solution)/shard_map/ppermute | solution.py:79
  922.2 20.6 %collective-permute-start.74 = (bf16[128,3072]{1,0:T(8,128)(2,1)S(1)}, bf16[128,3072]{1,0:T(8,128)(2,1)}, u32[]{:S(2)}, u32[]{:S(2)}) collective-permute-start(bf16[128,3072]{1,0:T(8,128)(2,1)S(1)} %copy-done.54), channel_id=1, source_target_pairs={{0,16},{4,20},{8,24},{12,28},{16,0},{20,4},{24,8},{28,12},{1,17},{... | collective-permute-start | bytes 2359304 | tf_op jit(solution)/shard_map/ppermute | solution.py:79
  931.5 33.6 %collective-permute-start.50 = (bf16[256,2560]{1,0:T(8,128)(2,1)}, bf16[256,2560]{1,0:T(8,128)(2,1)S(1)}, u32[]{:S(2)}, u32[]{:S(2)}) collective-permute-start(bf16[256,2560]{1,0:T(8,128)(2,1)} %get-tuple-element.104), channel_id=1, source_target_pairs={{0,8},{4,12},{8,0},{12,4},{16,24},{20,28},{24,16},{28,20},{1,9},{5... | collective-permute-start | bytes 3932168 | tf_op jit(solution)/shard_map/ppermute | solution.py:79
  932.2 33.6 %collective-permute-start.51 = (bf16[256,2560]{1,0:T(8,128)(2,1)}, bf16[256,2560]{1,0:T(8,128)(2,1)S(1)}, u32[]{:S(2)}, u32[]{:S(2)}) collective-permute-start(bf16[256,2560]{1,0:T(8,128)(2,1)} %get-tuple-element.105), channel_id=1, source_target_pairs={{0,16},{4,20},{8,24},{12,28},{16,0},{20,4},{24,8},{28,12},{1,17},{... | collective-permute-start | bytes 3932168 | tf_op jit(solution)/shard_map/ppermute | solution.py:79
  966.9 117.4 %collective-permute-start.54 = (bf16[256,2048]{1,0:T(8,128)(2,1)}, bf16[256,2048]{1,0:T(8,128)(2,1)}, u32[]{:S(2)}, u32[]{:S(2)}) collective-permute-start(bf16[256,2048]{1,0:T(8,128)(2,1)} %get-tuple-element.106.refs_0_), channel_id=1, source_target_pairs={{0,3},{1,0},{2,1},{3,2},{4,7},{5,4},{6,5},{7,6},{8,11},{9,8},{10,9... | collective-permute-start | bytes 3145736 | tf_op jit(solution)/shard_map/ppermute | solution.py:162
  966.9 141.8 %collective-permute-start.53 = (bf16[256,2048]{1,0:T(8,128)(2,1)}, bf16[256,2048]{1,0:T(8,128)(2,1)}, u32[]{:S(2)}, u32[]{:S(2)}) collective-permute-start(bf16[256,2048]{1,0:T(8,128)(2,1)} %get-tuple-element.106.refs_0_), channel_id=1, source_target_pairs={{0,2},{1,3},{2,0},{3,1},{4,6},{5,7},{6,4},{7,5},{8,10},{9,11},{10,... | collective-permute-start | bytes 3145736 | tf_op jit(solution)/shard_map/ppermute | solution.py:162
  968.4 140.3 %collective-permute-start.52 = (bf16[256,2048]{1,0:T(8,128)(2,1)}, bf16[256,2048]{1,0:T(8,128)(2,1)}, u32[]{:S(2)}, u32[]{:S(2)}) collective-permute-start(bf16[256,2048]{1,0:T(8,128)(2,1)} %get-tuple-element.106.refs_0_), channel_id=1, source_target_pairs={{0,1},{1,2},{2,3},{3,0},{4,5},{5,6},{6,7},{7,4},{8,9},{9,10},{10,1... | collective-permute-start | bytes 3145736 | tf_op jit(solution)/shard_map/ppermute | solution.py:162
  1004.7 22.3 %collective-permute-start.58 = (bf16[4,4,26752]{2,1,0:T(4,128)(2,1)}, bf16[4,4,26752]{2,1,0:T(4,128)(2,1)}, u32[]{:S(2)}, u32[]{:S(2)}) collective-permute-start(bf16[4,4,26752]{2,1,0:T(4,128)(2,1)} %slice.838), channel_id=1, source_target_pairs={{0,16},{4,20},{8,24},{12,28},{16,0},{20,4},{24,8},{28,12},{1,17},{... | collective-permute-start | bytes 2568200 | tf_op jit(solution)/shard_map/ppermute | solution.py:79
  1008.5 43.8 %collective-permute-start.69 = (bf16[256,2560]{1,0:T(8,128)(2,1)}, bf16[256,2560]{1,0:T(8,128)(2,1)}, u32[]{:S(2)}, u32[]{:S(2)}) collective-permute-start(bf16[256,2560]{1,0:T(8,128)(2,1)} %get-tuple-element.119), channel_id=1, source_target_pairs={{0,16},{4,20},{8,24},{12,28},{16,0},{20,4},{24,8},{28,12},{1,17},{... | collective-permute-start | bytes 3932168 | tf_op jit(solution)/shard_map/ppermute | solution.py:79
  1027.0 26.0 %collective-permute-start.70 = (bf16[256,2560]{1,0:T(8,128)(2,1)}, bf16[256,2560]{1,0:T(8,128)(2,1)S(1)}, u32[]{:S(2)}, u32[]{:S(2)}) collective-permute-start(bf16[256,2560]{1,0:T(8,128)(2,1)} %get-tuple-element.120), channel_id=1, source_target_pairs={{0,8},{4,12},{8,0},{12,4},{16,24},{20,28},{24,16},{28,20},{1,9},{5... | collective-permute-start | bytes 3932168 | tf_op jit(solution)/shard_map/ppermute | solution.py:79
  1056.9 18.8 %collective-permute-start.71 = (bf16[128,2560]{1,0:T(8,128)(2,1)}, bf16[128,2560]{1,0:T(8,128)(2,1)S(1)}, u32[]{:S(2)}, u32[]{:S(2)}) collective-permute-start(bf16[128,2560]{1,0:T(8,128)(2,1)} %get-tuple-element.121), channel_id=1, source_target_pairs={{0,8},{4,12},{8,0},{12,4},{16,24},{20,28},{24,16},{28,20},{1,9},{5... | collective-permute-start | bytes 1966088 | tf_op jit(solution)/shard_map/ppermute | solution.py:79
  1075.7 37.3 %collective-permute-start.60 = (bf16[1,4,26752]{2,1,0:T(4,128)(2,1)S(1)}, bf16[1,4,26752]{2,1,0:T(4,128)(2,1)S(1)}, u32[]{:S(2)}, u32[]{:S(2)}) collective-permute-start(bf16[1,4,26752]{2,1,0:T(4,128)(2,1)S(1)} %slice.842), channel_id=1, source_target_pairs={{0,4},{4,0},{8,12},{12,8},{16,20},{20,16},{24,28},{28,24},{1,5},{5... | collective-permute-start | bytes 642056 | tf_op jit(solution)/shard_map/ppermute | solution.py:79
  1110.9 59.8 %collective-permute-start.57 = (bf16[256,2048]{1,0:T(8,128)(2,1)S(1)}, bf16[256,2048]{1,0:T(8,128)(2,1)S(1)}, u32[]{:S(2)}, u32[]{:S(2)}) collective-permute-start(bf16[256,2048]{1,0:T(8,128)(2,1)S(1)} %copy-done.27), channel_id=1, source_target_pairs={{0,3},{1,0},{2,1},{3,2},{4,7},{5,4},{6,5},{7,6},{8,11},{9,8},{10,9... | collective-permute-start | bytes 3145736 | tf_op jit(solution)/shard_map/ppermute | solution.py:162
  1111.0 156.7 %collective-permute-start.56 = (bf16[256,2048]{1,0:T(8,128)(2,1)S(1)}, bf16[256,2048]{1,0:T(8,128)(2,1)}, u32[]{:S(2)}, u32[]{:S(2)}) collective-permute-start(bf16[256,2048]{1,0:T(8,128)(2,1)S(1)} %copy-done.27), channel_id=1, source_target_pairs={{0,2},{1,3},{2,0},{3,1},{4,6},{5,7},{6,4},{7,5},{8,10},{9,11},{10,... | collective-permute-start | bytes 3145736 | tf_op jit(solution)/shard_map/ppermute | solution.py:162
  1111.1 156.6 %collective-permute-start.55 = (bf16[256,2048]{1,0:T(8,128)(2,1)S(1)}, bf16[256,2048]{1,0:T(8,128)(2,1)}, u32[]{:S(2)}, u32[]{:S(2)}) collective-permute-start(bf16[256,2048]{1,0:T(8,128)(2,1)S(1)} %copy-done.27), channel_id=1, source_target_pairs={{0,1},{1,2},{2,3},{3,0},{4,5},{5,6},{6,7},{7,4},{8,9},{9,10},{10,1... | collective-permute-start | bytes 3145736 | tf_op jit(solution)/shard_map/ppermute | solution.py:162
  1114.1 161.1 %collective-permute-start.61 = (bf16[26752]{0:T(1024)(128)(2,1)S(1)}, bf16[26752]{0:T(1024)(128)(2,1)S(1)}, u32[]{:S(2)}, u32[]{:S(2)}) collective-permute-start(bf16[26752]{0:T(1024)(128)(2,1)S(1)} %get-tuple-element.197), channel_id=1, source_target_pairs={{0,1},{1,2},{2,3},{3,0},{4,5},{5,6},{6,7},{7,4},{8,9},{9,10},{10,1... | collective-permute-start | bytes 160520 | tf_op jit(solution)/shard_map/ppermute | solution.py:162
  1115.7 159.5 %collective-permute-start.63 = (bf16[26752]{0:T(1024)(128)(2,1)S(1)}, bf16[26752]{0:T(1024)(128)(2,1)S(1)}, u32[]{:S(2)}, u32[]{:S(2)}) collective-permute-start(bf16[26752]{0:T(1024)(128)(2,1)S(1)} %get-tuple-element.198), channel_id=1, source_target_pairs={{0,3},{1,0},{2,1},{3,2},{4,7},{5,4},{6,5},{7,6},{8,11},{9,8},{10,9... | collective-permute-start | bytes 160520 | tf_op jit(solution)/shard_map/ppermute | solution.py:162
  1170.7 104.4 %collective-permute-start.62 = (bf16[26752]{0:T(1024)(128)(2,1)S(1)}, bf16[26752]{0:T(1024)(128)(2,1)S(1)}, u32[]{:S(2)}, u32[]{:S(2)}) collective-permute-start(bf16[26752]{0:T(1024)(128)(2,1)S(1)} %get-tuple-element.199), channel_id=1, source_target_pairs={{0,2},{1,3},{2,0},{3,1},{4,6},{5,7},{6,4},{7,5},{8,10},{9,11},{10,... | collective-permute-start | bytes 160520 | tf_op jit(solution)/shard_map/ppermute | solution.py:162
  (147 other events, 1150.1 us)
Sparse Core Ops, SparseCore 0:
  13.5 65.4 all-gather.7
  365.7 79.5 all-gather.9
  446.9 79.2 all-gather.11
  528.3 75.2 reduce-scatter.5
  608.6 75.2 reduce-scatter.7
  696.0 76.5 reduce-scatter.9
  774.9 80.7 reduce-scatter.11
  857.3 81.2 all-gather.13
  940.1 149.5 all-gather.15
  1108.8 146.3 reduce-scatter.13

commit v8 on v6

--- a/solution.py
+++ b/solution.py
@@ -171,29 +171,9 @@
     return total
 
 
-class Line:
-    def __init__(self, own, n):
-        self.own, self.n, self.rounds = own, n, []
-
-    def go(self, *others):
-        k = len(self.rounds) + 1
-        if k >= self.n:
-            return ()
-        right, left = fence(self.rounds[-1], *others) if self.rounds else (self.own, self.own)
-        right = lax.ppermute(right, "tensor", [(s, s + 1) for s in range(k - 1, self.n - 1)])
-        left = lax.ppermute(left, "tensor", [(s, s - 1) for s in range(1, self.n - k + 1)])
-        self.rounds.append((right, left))
-        return self.rounds[-1]
-
-    def place(self, out, at):
-        turn = lax.axis_index("tensor")
-        out = lax.dynamic_update_slice(out, self.own[None, None], (turn, at, 0, 0))
-        while len(self.rounds) < self.n - 1:
-            self.go()
-        for k in range(1, self.n):
-            piece = self.rounds[k - 1][1] + self.rounds[self.n - k - 1][0]
-            out = lax.dynamic_update_slice(out, piece[None, None], ((turn + k) % self.n, at, 0, 0))
-        return out
+def small_masks(size):
+    turns = (0, 2, 6, 4) if size == 8 else tuple(q << 1 for q in range(size // 2))
+    return np.array([core | mask for core in range(2) for mask in turns], np.int32)
 
 
 def small_begin(own, size):
@@ -210,17 +190,10 @@
         own, by_x, by_y = some
         cut = own.shape[0] // 2
         far = jnp.concatenate([exchange(by_x[:cut], 2, size), exchange(by_y[cut:], 1, size)])
-        rows = jnp.stack([own, by_x, by_y, far])
+        rows = jnp.stack([own, by_x, far, by_y])
     else:
         (rows,) = some
     return jnp.concatenate([rows, exchange(rows, 0, size)])
-
-
-def z_gather(own, n, *others):
-    turn = lax.axis_index("tensor")
-    blocks = jnp.stack([own] + fence([z_shift(own, -k, n) for k in range(1, n)], *others))
-    blocks = jnp.take(blocks, (jnp.arange(n) - turn) % n, axis=0, mode="clip")
-    return blocks.transpose(1, 0, 2).reshape(own.shape[0], -1)
 
 
 def small_scatter(values, size, n):
@@ -550,24 +523,35 @@
     own_chan = lax.dynamic_update_slice(own_chan, chan, (0, 0, place * part)).reshape(8, cols)
     own_gain = jnp.pad(gains.reshape(1, -1), ((0, 7), (0, cols - gains.size)))
     small = jnp.concatenate([own_lru.reshape(2 * pad, cols), own_chan, own_gain])
-    whole = jnp.concatenate([w_rec, w_gelu, small]).astype(BF)
+    whole = jnp.concatenate([w_rec, small]).astype(BF)
+    others = jnp.concatenate([w_gelu, w_out.T]).astype(BF)
+    own_gu = jnp.concatenate([w_mlp_in[0], w_mlp_in[1]], axis=1).astype(BF)
     own_dn = w_down.T.astype(BF)
-    own_gu = jnp.concatenate([w_mlp_in[0], w_mlp_in[1]], axis=1).astype(BF)
-    some_dn = spread_begin(own_dn, size)
-    whole = lax.all_gather(whole, "tensor", axis=0)
-    z_rec, z_gelu = (
-        whole[:, k * d_own : (k + 1) * d_own].transpose(1, 0, 2).reshape(d_own, width) for k in range(2)
-    )
-    some_r = spread_begin(z_rec, size, *some_dn[1:])
-    some_small = small_begin(whole[:, 2 * d_own :].reshape(-1, cols), size)
-    w_r, came_r = spread_end(some_r, size, (), ())
+    some_gu = spread_begin(own_gu, size)
+
+    main = lax.dynamic_slice_in_dim(tokens, turn * rows, rows)
+    before = lax.dynamic_slice_in_dim(tokens, jnp.maximum(turn * rows - HALO, 0), HALO)
+    before = jnp.where(turn > 0, before, jnp.zeros_like(before))
+    turned = permute_rows(jnp.concatenate([before, main]), table)
+    extended = turned.astype(F32)
+    first_rate = norm_rate(extended)
+
+    def wide(blocks):
+        return blocks.transpose(1, 0, 2).reshape(d_own, width)
+
+    (whole,) = fence([lax.all_gather(whole, "tensor", axis=0)], *some_gu[1:], others, turned, first_rate)
+    others = lax.all_gather(*fence([others], whole), "tensor", axis=0)
+    z_gelu, z_out = wide(others[:, :d_own]), wide(others[:, d_own:])
+    some_r = spread_begin(wide(whole[:, :d_own]), size)
+    some_small = small_begin(whole[:, d_own:].reshape(-1, cols), size)
     small = small_end(some_small, size).reshape(size, n, -1, cols)
 
-    spots, parts = basis_spots(size, d_own)
-    unit = d_own // parts
+    masks = small_masks(size)
     gain = small[:, 0, 2 * pad + 8, : gains.size].reshape(size, 2, d_own)
-    gain = [gain[(mask & 1) * (size // 2) + (mask >> 1), :, k * unit : (k + 1) * unit] for mask, k in spots]
-    gain = jnp.concatenate(gain, axis=1).astype(F32)
+    if squared(size, d_own):
+        swapped = jnp.concatenate([gain[..., d_own // 2 :], gain[..., : d_own // 2]], axis=-1)
+        gain = jnp.where(((jnp.asarray(masks) & 6) == 6)[:, None, None], swapped, gain)
+    gain = gain.transpose(1, 0, 2).reshape(2, d_model).astype(F32)
     chans = jnp.sum(small[:, :, 2 * pad : 2 * pad + 8].astype(F32), axis=0)
     chans = chans.transpose(1, 0, 2).reshape(8, width)
     par = jnp.concatenate([chans[:7], -8.0 * jax.nn.softplus(-chans[7:])])
@@ -575,16 +559,12 @@
     lru = small
     if each > 1:
         lru = lru.reshape(size, groups, each, -1, cols).transpose(0, 1, 3, 2, 4).reshape(size, groups, -1, GROUP)
-    spot, row = jnp.arange(size * pad) // pad, jnp.arange(size * pad) % pad
-    spot = place ^ (spot // (size // 2) | (spot % (size // 2)) << 1)
+    spot = (place ^ jnp.asarray(masks))[jnp.arange(size * pad) // pad]
+    row = jnp.arange(size * pad) % pad
     row = jnp.where(row < part, spot * part + row, head)
     order = (jnp.arange(head)[:, None] == row[None, :]).astype(BF)
 
-    main = lax.dynamic_slice_in_dim(tokens, turn * rows, rows)
-    before = lax.dynamic_slice_in_dim(tokens, jnp.maximum(turn * rows - HALO, 0), HALO)
-    before = jnp.where(turn > 0, before, jnp.zeros_like(before))
-    extended = permute_rows(jnp.concatenate([before, main]), table).astype(F32)
-    first_rate = norm_rate(extended)
+    w_r, came_r = spread_end(some_r, size, some_small[1:], (others, gain, par, order, lru))
     first = (extended * first_rate * gain[0]).astype(BF)
     inputs, first_own, first_rate = extended[HALO:], first[HALO:], first_rate[HALO:]
     cut = d_model // 2
@@ -602,9 +582,8 @@
     carry = jnp.zeros((1, width), F32)
     for end in came[::-1]:
         carry = end[1:] + end[:1] * carry
-    z_out = z_gather(*fence([w_out.T.astype(BF)], z_rec), n, ends)
-    w_g, came_g = spread_end(some_g, size, (rec_pre,), (ends, z_out))
-    some_o = spread_begin(z_out, size, *came_g, ends)
+    w_g, came_g = spread_end(some_g, size, (ends,), ())
+    some_o = spread_begin(z_out, size, *came_g)
     branch_pre = wide_dot(first_own, w_g)
     recurrent = (state + prod * carry) * live
     mixed = (jax.nn.gelu(branch_pre) * recurrent).astype(BF)
@@ -613,9 +592,8 @@
     second_rate = norm_rate(hidden)
     second_unit = hidden * second_rate
     second_own = (second_unit * gain[1]).astype(BF)
-    some_gu = spread_begin(own_gu, size, *came_o)
-    w_gu, came_gu = spread_end(some_gu, size, (second_own,), ())
-    w_dn, _ = spread_end(some_dn, size, came_gu, ())
+    w_gu, came_gu = spread_end(some_gu, size, came_o, (second_own,))
+    w_dn, _ = spread_end(spread_begin(own_dn, size, *came_gu), size, (), ())
     w_gu, w_dn = assemble(w_gu), assemble(w_dn)
     late = fence([table], second_own)[0]
     cots = [permute_rows(cotangent, late, half, 2, h) for h in range(2)]
@@ -689,14 +667,11 @@
         [((rows + HALO, GROUP), F32), ((rows + 2 * HALO, GROUP), F32), ((rows + SLAB, GROUP), F32), ((GROUP, 2 * GROUP), F32), dense],
         "recurrence_back",
     )
-    line_0 = Line(mlp_result(0, mlp_sums[0]), n)
-    (edge_rows,) = fence([z_shift(drec[:HALO], -1, n, False)], line_0.own)
-    came_0 = line_0.go()
+    (edge_rows,) = fence([z_shift(drec[:HALO], -1, n, False)], mlp_sums[0])
     rec_low = (drec[HALO:] + jnp.pad(edge_rows, ((rows - HALO, 0), (0, 0)))) * live
     rec_low = rec_low.astype(BF)
     (pre_low,) = fence([pre_low], drec)
-    (grad_first,) = fence([wide_back(pre_low, w_g) + wide_back(rec_low, w_r)], *came_0)
-    came_0 = line_0.go()
+    grad_first = wide_back(pre_low, w_g) + wide_back(rec_low, w_r)
     first_unit = inputs * first_rate
     gain_one = jnp.sum(grad_first * first_unit, axis=0)
     grad_tokens = grad_hidden + norm_back(grad_first, first_unit, first_rate, gain[0])
@@ -706,29 +681,26 @@
     sum_o = by_cols(hidden_low, mixed)
     pre_low, rec_low = fence([pre_low, rec_low], sum_o.terms[1])
     sum_g, sum_r = by_cols(first_own, pre_low), by_cols(first_own, rec_low)
-    line_1 = Line(mlp_result(1, *fence(mlp_sums[1:], sum_o.terms[1])), n)
-    got_o = sum_o.hop(fence(sum_o.sources(), line_1.own, *came_0))
-    came_0, came_1 = line_0.go(), line_1.go()
-    got_g = sum_g.hop(fence(sum_g.sources(), *got_o))
+    results = [mlp_result(h, mlp_sum) for h, mlp_sum in enumerate(fence(mlp_sums, sum_o.terms[1]))]
+    got_o = sum_o.hop(sum_o.sources())
+    sum_o.hop(fence(sum_o.sources(), gathered[0]))
+    got_g = sum_g.hop(fence(sum_g.sources(), gathered[0]))
+    results = fence(results, gathered[0])
+    results = [lax.all_gather(result, "tensor", axis=0) for result in results]
+    sum_g.hop(fence(sum_g.sources(), gathered[1]))
+    got_r = sum_r.hop(fence(sum_r.sources(), gathered[1], *got_g))
+    d_lru, dpar = fence([d_lru, dpar], gathered[1])
+    sum_r.hop(fence(sum_r.sources(), results[0]))
     if sum_dn.square:
-        sum_dn.hop(fence(sum_dn.sources(), *got_o))
-        sum_gu.hop(fence(sum_gu.sources(), *got_o))
-    pause = (gathered[0], *came_0, *came_1, *got_g)
-    sum_o.hop(fence(sum_o.sources(), *pause))
-    got_r = sum_r.hop(fence(sum_r.sources(), *pause))
-    came_1 = line_1.go(gathered[0], *got_g)
-    sum_g.hop(fence(sum_g.sources(), *pause))
-    pause = (gathered[1], *came_1, *got_r)
-    sum_r.hop(fence(sum_r.sources(), *pause))
-    d_lru, dpar = fence([d_lru, dpar], *pause)
-    line_1.go(gathered[1])
-    tokens_out = interleave(*fence(gathered, *got_r)).reshape(n * rows, d_model)
+        sum_dn.hop(fence(sum_dn.sources(), results[0]))
+        sum_gu.hop(fence(sum_gu.sources(), results[0]))
+    tokens_out = interleave(*fence(gathered, results[0])).reshape(n * rows, d_model)
     g_gu, g_dn = sum_gu.finish().astype(F32), sum_dn.finish().astype(F32)
     owned = jnp.stack([total.finish().reshape(d_own, n, width // n) for total in (sum_o, sum_g, sum_r)])
-    owned = lax.psum_scatter(owned.transpose(2, 0, 1, 3), "tensor", scatter_dimension=0).astype(F32)
+    (owned,) = fence([owned.transpose(2, 0, 1, 3)], results[1])
+    output = interleave(*results).reshape(n * rows, d_model)
+    owned = lax.psum_scatter(owned, "tensor", scatter_dimension=0).astype(F32)
     g_o, g_g, g_r = owned[0], owned[1], owned[2]
-    output = line_0.place(jnp.zeros((n, 2, half, d_model), BF), 0)
-    output = line_1.place(output, 1).reshape(n * rows, d_model)
 
     d_gain = permute_gain(jnp.stack([gain_one, gain_two]), inverse)
     d_chan = jnp.concatenate([dpar[:7], dpar[7:] * 8.0 * jax.nn.sigmoid(-chans[7:])])

time: 1380 us -> 1200 us (0.87)
  waiting for transfers between devices: 517 us -> 417 us
  local copies, waits for them, and re-layouts: 150 us -> 113 us
  starting transfers between devices: 97 us -> 78.2 us
  other arithmetic: 148 us -> 130 us
    ppermute x12 -> x0, waiting for transfers between devices: 197 us -> none  [the longest x6 161 us: go(): lax.ppermute(left, 'tensor', [(s, s - 1) for s in range(1, self.n - k + 1)])]
    all_gather x2, waiting for transfers between devices: 0.01 us -> 126 us  [on_device(): lax.all_gather(grad_tokens[h * half:(h + 1) * half], 'tensor', axis=0)]
    ppermute x58, waiting for transfers between devices: 171 us -> 228 us  [exchange(): return lax.ppermute(values, 'dp', [(k, k ^ 1 << bit) for k in range(size)])]
    all_gather x1 -> x4, waiting for transfers between devices: 54.6 us -> 5.27 us  [the longest x2 5.27 us: on_device(): results = [lax.all_gather(result, 'tensor', axis=0) for result in results]]
    unnamed x292 -> x245, local copies, waits for them, and re-layouts: 60.4 us -> 37.9 us
    ppermute x12 -> x0, starting transfers between devices: 20.6 us -> none  [the longest x6 12.8 us: go(): lax.ppermute(right, 'tensor', [(s, s + 1) for s in range(k - 1, self.n -...]
    all_gather x2, waiting for transfers between devices: 39.3 us -> 20.4 us  [on_device(): lax.all_gather(second_own[h * half:(h + 1) * half], 'tensor', axis=0, til...]
    dynamic_update_slice x6 -> x0, other arithmetic: 16.9 us -> none  [place(): lax.dynamic_update_slice(out, piece[None, None], ((turn + k) % self.n, at...]
  transfers between devices with their start and end apart: 93 -> 81, of which waited for: 39 -> 42; matrix products, arithmetic and copies ran while one was open for 41% -> 42% of each run, Pallas kernels for 9% -> 10%
where the time goes in v8:
time: 1200 us
  waiting for transfers between devices  417 us (35%)
  matrix products  304 us (25%)
  Pallas kernels  138 us (12%)
  other arithmetic  130 us (11%)
  local copies, waits for them, and re-layouts  113 us (9%)
  starting transfers between devices  78.2 us (7%)
  between operations  16.9 us (1%)
    dot_general x34, matrix products, dot(): lax.dot_general(left, right, (dims, ((), ())), preferred_element_type=F32)  304 us
    ppermute x58, waiting for transfers between devices, exchange(): return lax.ppermute(values, 'dp', [(k, k ^ 1 << bit) for k in range(size)])  228 us
    all_gather x2, waiting for transfers between devices, on_device(): lax.all_gather(grad_tokens[h * half:(h + 1) * half], 'tensor', axis=0)  126 us
    pallas_call x3, Pallas kernels, kernel_call(): pl.pallas_call(body, grid_spec=pltpu.PrefetchScalarGridSpec(num_scalar_pr...  62.2 us
    convert_element_type x18, other arithmetic, add_all(): return total.astype(BF)  57.8 us
    ppermute x58, starting transfers between devices, exchange(): return lax.ppermute(values, 'dp', [(k, k ^ 1 << bit) for k in range(size)])  57.2 us
    unnamed x245, local copies, waits for them, and re-layouts  37.9 us
    pallas_call x7, Pallas kernels, assemble(): pl.pallas_call(body, in_specs=[place] * (count + len(others)), out_specs=...  35.7 us
  transfers between devices with their start and end apart: 81, of which 42 were waited for; matrix products, arithmetic and copies ran while one was open for 42% of the time, Pallas kernels for 10%

profile of v8, /device:TPU:0, one launch (start us, length us, event | category | flops | bytes accessed | tf_op | source)
XLA Modules:
  0.0 1196.5 jit_solution(5723880526748306005)
XLA Ops:
  37.5 16.7 %collective-permute-done.1.refs_2_.refs_1_ = bf16[256,3072]{1,0:T(8,128)(2,1)S(1)} collective-permute-done((bf16[256,3072]{1,0:T(8,128)(2,1)}, bf16[256,3072]{1,0:T(8,128)(2,1)S(1)}, u32[]{:S(2)}, u32[]{:S(2)}) %collective-permute-start.1) | collective-permute-done | bytes 1572896 | tf_op jit(solution)/shard_map/ppermute | solution.py:79
  60.2 7.8 collective-permute-done.2.refs_2_
  88.7 21.9 %collective-permute-done.8.refs_1_ = bf16[256,2560]{1,0:T(8,128)(2,1)S(1)} collective-permute-done((bf16[256,2560]{1,0:T(8,128)(2,1)S(1)}, bf16[256,2560]{1,0:T(8,128)(2,1)S(1)}, u32[]{:S(2)}, u32[]{:S(2)}) %collective-permute-start.8) | collective-permute-done | bytes 1310752 | tf_op jit(solution)/shard_map/ppermute | solution.py:79
  122.6 10.9 collective-permute-done.10.refs_2_
  147.6 4.9 fusion.43
  152.5 7.3 convolution_add_fusion.pre_ref
  159.8 18.9 %recurrence.1 = (f32[512,2560]{1,0:T(8,128)}, f32[512,2560]{1,0:T(8,128)}, f32[512,2560]{1,0:T(8,128)}, f32[512,2560]{1,0:T(8,128)}, f32[512,2560]{1,0:T(8,128)}, /*index=5*/f32[512,2560]{1,0:T(8,128)}) custom-call(s32[1]{0:T(128)} %sub.29.live_ref, f32[528,2560]{1,0:T(8,128)} %convolution_add_fusion.pre_ref, f32[8,2560]{1,0:T(8,128)} %pad_maximum_fusion.13.refs_7_.par_ref, ...), custom_call_target="tpu_custom_call" | custom-call | flops 1024 | bytes 1024 | tf_op jit(solution)/shard_map/recurrence/pallas_call | solution.py:469
  187.7 14.6 %collective-permute-done.14.refs_2_ = bf16[128,2560]{1,0:T(8,128)(2,1)S(1)} collective-permute-done((bf16[128,2560]{1,0:T(8,128)(2,1)S(1)}, bf16[128,2560]{1,0:T(8,128)(2,1)S(1)}, u32[]{:S(2)}, u32[]{:S(2)}) %collective-permute-start.14) | collective-permute-done | bytes 655392 | tf_op jit(solution)/shard_map/ppermute | solution.py:79
  208.3 5.3 collective-permute-start.19
  226.0 9.7 fusion.22
  235.7 14.1 %collective-permute-done.21.refs_1_ = bf16[256,2560]{1,0:T(8,128)(2,1)S(1)} collective-permute-done((bf16[256,2560]{1,0:T(8,128)(2,1)}, bf16[256,2560]{1,0:T(8,128)(2,1)S(1)}, u32[]{:S(2)}, u32[]{:S(2)}) %collective-permute-start.21) | collective-permute-done | bytes 1310752 | tf_op jit(solution)/shard_map/ppermute | solution.py:79
  255.9 13.4 %collective-permute-done.22.refs_2_.refs_3_ = bf16[128,2560]{1,0:T(8,128)(2,1)S(1)} collective-permute-done((bf16[128,2560]{1,0:T(8,128)(2,1)S(1)}, bf16[128,2560]{1,0:T(8,128)(2,1)S(1)}, u32[]{:S(2)}, u32[]{:S(2)}) %collective-permute-start.22) | collective-permute-done | bytes 655392 | tf_op jit(solution)/shard_map/ppermute | solution.py:79
  289.3 4.9 fusion.81
  303.4 5.9 assemble.10.refs_0_
  314.3 17.8 %collective-permute-done.29.refs_4_ = bf16[256,1536]{1,0:T(8,128)(2,1)S(1)} collective-permute-done((bf16[256,1536]{1,0:T(8,128)(2,1)}, bf16[256,1536]{1,0:T(8,128)(2,1)S(1)}, u32[]{:S(2)}, u32[]{:S(2)}) %collective-permute-start.29) | collective-permute-done | bytes 786464 | tf_op jit(solution)/shard_map/ppermute | solution.py:79
  334.7 8.4 collective-permute-done.30.refs_2_
  348.6 5.2 collective-permute-done.32.refs_1_
  360.2 5.8 permute.8
  366.0 5.9 permute.7
  372.3 9.3 assemble.11
  381.6 20.0 %fusion.82 = f32[1024,3072]{1,0:T(8,128)} fusion(bf16[1024,2048]{1,0:T(8,128)(2,1)} %all-gather.16.cloned.1.call-done, bf16[2048,3072]{1,0:T(8,128)(2,1)} %assemble.11), kind=kOutput, calls=%fused_computation.255 | convolution fusion | flops 12884901888 | bytes 29360128 | tf_op jit(solution)/shard_map/dot_general | solution.py:24
  401.6 16.0 %fusion.6 = (bf16[1024,1536]{1,0:T(8,128)(2,1)S(1)}, bf16[1024,1536]{1,0:T(8,128)(2,1)S(1)}, bf16[1024,1536]{1,0:T(8,128)(2,1)}) fusion(f32[1024,3072]{1,0:T(8,128)} %fusion.82, bf16[1024,2048]{1,0:T(8,128)(2,1)S(1)} %copy-done.33, bf16[2048,1536]{1,0:T(8,128)(2,1)} %assemble.13), kind=kOutput, calls=%fused_computation.15 | convolution fusion | flops 6483345408 | bytes 32505856 | tf_op jit(solution)/shard_map/dot_general | solution.py:24
  419.3 17.6 %convolution_convert_fusion.7.refs_1_ = bf16[1024,2048]{1,0:T(8,128)(2,1)} fusion(bf16[2048,3072]{1,0:T(8,128)(2,1)} %assemble.11, bf16[1024,1536]{1,0:T(8,128)(2,1)S(1)} %get-tuple-element.195, bf16[1024,1536]{1,0:T(8,128)(2,1)S(1)} %get-tuple-element.194), kind=kOutput, calls=%fused_computation.72 | convolution fusion | flops 12899581952 | bytes 23068672 | tf_op jit(solution)/shard_map/dot_general | solution.py:24
  437.2 20.4 %all-gather.18.cloned.1.call-done.refs_0_ = bf16[1024,2048]{1,0:T(8,128)(2,1)} async-done(((bf16[256,2048]{1,0:T(8,128)(2,1)}), bf16[1024,2048]{1,0:T(8,128)(2,1)}) %all-gather.18.cloned.1.call-update) | async-done | bytes 4194320 | tf_op jit(solution)/shard_map/all_gather | solution.py:605
  457.5 19.3 %fusion.83 = f32[1024,3072]{1,0:T(8,128)} fusion(bf16[1024,2048]{1,0:T(8,128)(2,1)} %fence.42, bf16[2048,3072]{1,0:T(8,128)(2,1)} %assemble.11), kind=kOutput, calls=%fused_computation.256 | convolution fusion | flops 12884901888 | bytes 29360128 | tf_op jit(solution)/shard_map/dot_general | solution.py:24
  476.8 15.4 %fusion.13 = (bf16[1024,1536]{1,0:T(8,128)(2,1)}, bf16[1024,1536]{1,0:T(8,128)(2,1)}, bf16[1024,1536]{1,0:T(8,128)(2,1)}) fusion(f32[1024,3072]{1,0:T(8,128)} %fusion.83, bf16[1024,2048]{1,0:T(8,128)(2,1)S(1)} %copy-done.31, bf16[2048,1536]{1,0:T(8,128)(2,1)S(1)} %bitcast.186), kind=kOutput, calls=%fused_computation.22 | convolution fusion | flops 6483345408 | bytes 32505856 | tf_op jit(solution)/shard_map/dot_general | solution.py:24
  492.3 5.5 pad_maximum_fusion.refs_1_
  497.8 18.8 %convolution_convert_fusion.6.refs_2_ = bf16[1024,2048]{1,0:T(8,128)(2,1)} fusion(bf16[2048,3072]{1,0:T(8,128)(2,1)} %assemble.11, bf16[1024,1536]{1,0:T(8,128)(2,1)} %get-tuple-element.193, bf16[1024,1536]{1,0:T(8,128)(2,1)S(1)} %copy-done.51), kind=kOutput, calls=%fused_computation.71 | convolution fusion | flops 12899581952 | bytes 23068672 | tf_op jit(solution)/shard_map/dot_general | solution.py:24
  518.5 5.7 pad_maximum_fusion.1.refs_1_
  524.2 7.4 fusion.37
  531.6 8.3 convolution_convert_fusion.9.refs_6_.refs_0_
  540.1 9.7 add_convert_fusion.2
  549.8 9.7 fusion.31
  559.5 11.8 add_convert_fusion
  571.8 11.0 fusion.34
  582.8 11.2 convolution_convert_fusion.8.refs_7_.refs_1_
  594.1 5.4 fusion.40
  599.4 7.1 add_convert_fusion.3
  606.5 10.2 add_convert_fusion.1
  639.2 5.7 fusion.49
  650.2 17.0 %back_scan.1 = (f32[512,2560]{1,0:T(8,128)}, f32[512,2560]{1,0:T(8,128)}, f32[8,2560]{1,0:T(8,128)}, bf16[512,2560]{1,0:T(8,128)(2,1)}) custom-call(s32[1]{0:T(128)} %sub.29.live_ref, f32[512,2560]{1,0:T(8,128)} %get-tuple-element.260.refs_2_.pre_ref, f32[512,2560]{1,0:T(8,128)} %convolution_add_fusion.1.grad_ref, f32[512,2560]{1,0:T(8,128)} %get-tuple-element.82.decay_ref, ...), custom_call_target="tpu_custom_call" | custom-call | flops 1024 | bytes 1024 | tf_op jit(solution)/shard_map/back_scan/pallas_call | solution.py:469
  672.1 11.5 collective-permute-done.38.refs_4_
  685.6 26.4 %recurrence_back.1 = (f32[528,2560]{1,0:T(8,128)}, f32[8,2560]{1,0:T(8,128)}, bf16[4,160,1280]{2,1,0:T(8,128)(2,1)}) custom-call(s32[1]{0:T(128)} %sub.29.live_ref, f32[528,2560]{1,0:T(8,128)} %convolution_add_fusion.pre_ref, f32[8,2560]{1,0:T(8,128)} %pad_maximum_fusion.13.refs_7_.par_ref, bf16[8,4,80,640]{3,2,1,0:T(8,128)(2,1)} %copy-done.6, ...), custom_call_target="tpu_custom_call" | custom-call | flops 1024 | bytes 1024 | tf_op jit(solution)/shard_map/recurrence_back/pallas_call | solution.py:469
  714.9 7.5 fusion.84
  722.4 6.8 fusion.85
  733.3 5.8 fusion.86
  739.3 5.0 fusion.87
  746.8 6.1 add_convert_fusion.4.in_ref
  761.2 6.4 convolution_convert_fusion.5
  771.3 5.9 convolution_convert_fusion.4
  777.2 10.0 reduce-scatter.12.cloned.1.call-done.refs_1_
  807.0 62.2 %all-gather.22.cloned.1.call-done = bf16[1024,2048]{1,0:T(8,128)(2,1)} async-done(((bf16[256,2048]{1,0:T(8,128)(2,1)}), bf16[1024,2048]{1,0:T(8,128)(2,1)}) %all-gather.22.cloned.1.call-update) | async-done | bytes 4194320 | tf_op jit(solution)/shard_map/all_gather | solution.py:679
  870.9 6.2 convolution_convert_fusion.3
  886.5 63.5 %all-gather.28.cloned.1.call-done = bf16[1024,2048]{1,0:T(8,128)(2,1)} async-done(((bf16[256,2048]{1,0:T(8,128)(2,1)}), bf16[1024,2048]{1,0:T(8,128)(2,1)}) %all-gather.28.cloned.1.call-update) | async-done | bytes 4194320 | tf_op jit(solution)/shard_map/all_gather | solution.py:679
  973.5 5.9 convolution_convert_fusion
  985.9 8.1 collective-permute-done.44
  1021.6 13.3 %collective-permute-done.55.refs_4_ = bf16[256,2560]{1,0:T(8,128)(2,1)S(1)} collective-permute-done((bf16[256,2560]{1,0:T(8,128)(2,1)}, bf16[256,2560]{1,0:T(8,128)(2,1)S(1)}, u32[]{:S(2)}, u32[]{:S(2)}) %collective-permute-start.55) | collective-permute-done | bytes 1310752 | tf_op jit(solution)/shard_map/ppermute | solution.py:79
  1049.5 21.4 %collective-permute-done.60 = bf16[256,2560]{1,0:T(8,128)(2,1)S(1)} collective-permute-done((bf16[256,2560]{1,0:T(8,128)(2,1)}, bf16[256,2560]{1,0:T(8,128)(2,1)S(1)}, u32[]{:S(2)}, u32[]{:S(2)}) %collective-permute-start.60) | collective-permute-done | bytes 1310752 | tf_op jit(solution)/shard_map/ppermute | solution.py:79
  1078.8 6.6 collective-permute-done.57
  1090.2 7.3 collective-permute-done.62
  1106.3 5.3 all-gather.26.cloned.1.call-done
  1128.5 7.0 interleave.2
  1138.5 7.0 interleave.3
  1159.5 26.6 %reduce-scatter.14.cloned.1.call-done = bf16[1,3,256,640]{3,2,1,0:T(8,128)(2,1)} async-done(((bf16[4,3,256,640]{3,2,1,0:T(8,128)(2,1)}), bf16[1,3,256,640]{3,2,1,0:T(8,128)(2,1)}) %reduce-scatter.14.cloned.1.call-update) | async-done | bytes 983056 | tf_op jit(solution)/shard_map/reduce_scatter | solution.py:702
  (600 shorter events, 386.1 us)
Async XLA Ops:
  7.2 48.5 %all-gather.14.cloned.1.call-start = ((), (), s32[]{:S(2)}) async-start(), calls=%async_computation.5 | async-start | bytes 2150400 | tf_op jit(solution)/shard_map/all_gather | solution.py:542
  12.0 122.1 %all-gather.20.cloned.1.call-start = ((), (), s32[]{:S(2)}) async-start(), calls=%async_computation.13 | async-start | bytes 3276800 | tf_op jit(solution)/shard_map/all_gather | solution.py:543
  15.5 38.7 %collective-permute-start.1 = (bf16[256,3072]{1,0:T(8,128)(2,1)}, bf16[256,3072]{1,0:T(8,128)(2,1)S(1)}, u32[]{:S(2)}, u32[]{:S(2)}) collective-permute-start(bf16[256,3072]{1,0:T(8,128)(2,1)} %pad_maximum_fusion.7.refs_0_), channel_id=1, source_target_pairs={{0,16},{4,20},{8,24},{12,28},{16,0},{20,4},{24,8},{28,12},{1,17},{... | collective-permute-start | bytes 4718600 | tf_op jit(solution)/shard_map/ppermute | solution.py:79
  19.6 36.1 %collective-permute-start = (bf16[256,3072]{1,0:T(8,128)(2,1)}, bf16[256,3072]{1,0:T(8,128)(2,1)S(1)}, u32[]{:S(2)}, u32[]{:S(2)}) collective-permute-start(bf16[256,3072]{1,0:T(8,128)(2,1)} %pad_maximum_fusion.7.refs_0_), channel_id=1, source_target_pairs={{0,8},{4,12},{8,0},{12,4},{16,24},{20,28},{24,16},{28,20},{1,9},{5... | collective-permute-start | bytes 4718600 | tf_op jit(solution)/shard_map/ppermute | solution.py:79
  71.6 310.1 %all-gather.16.cloned.1.call-start = ((), (), s32[]{:S(2)}) async-start(), calls=%async_computation.6 | async-start | bytes 5242880 | tf_op jit(solution)/shard_map/all_gather | solution.py:605
  79.1 39.4 %collective-permute-start.6 = (bf16[4,320,640]{2,1,0:T(8,128)(2,1)}, bf16[4,320,640]{2,1,0:T(8,128)(2,1)}, u32[]{:S(2)}, u32[]{:S(2)}) collective-permute-start(bf16[4,320,640]{2,1,0:T(8,128)(2,1)} %pad_maximum_fusion.6), channel_id=1, source_target_pairs={{0,4},{4,0},{8,12},{12,8},{16,20},{20,16},{24,28},{28,24},{1,5},{5... | collective-permute-start | bytes 4915208 | tf_op jit(solution)/shard_map/ppermute | solution.py:79
  79.4 31.2 %collective-permute-start.8 = (bf16[256,2560]{1,0:T(8,128)(2,1)S(1)}, bf16[256,2560]{1,0:T(8,128)(2,1)S(1)}, u32[]{:S(2)}, u32[]{:S(2)}) collective-permute-start(bf16[256,2560]{1,0:T(8,128)(2,1)S(1)} %bitcast.189), channel_id=1, source_target_pairs={{0,16},{4,20},{8,24},{12,28},{16,0},{20,4},{24,8},{28,12},{1,17},{... | collective-permute-start | bytes 3932168 | tf_op jit(solution)/shard_map/ppermute | solution.py:79
  80.2 30.9 %collective-permute-start.7 = (bf16[256,2560]{1,0:T(8,128)(2,1)S(1)}, bf16[256,2560]{1,0:T(8,128)(2,1)S(1)}, u32[]{:S(2)}, u32[]{:S(2)}) collective-permute-start(bf16[256,2560]{1,0:T(8,128)(2,1)S(1)} %bitcast.190), channel_id=1, source_target_pairs={{0,8},{4,12},{8,0},{12,4},{16,24},{20,28},{24,16},{28,20},{1,9},{5... | collective-permute-start | bytes 3932168 | tf_op jit(solution)/shard_map/ppermute | solution.py:79
  116.7 16.8 %collective-permute-start.10 = (bf16[128,2560]{1,0:T(8,128)(2,1)}, bf16[128,2560]{1,0:T(8,128)(2,1)}, u32[]{:S(2)}, u32[]{:S(2)}) collective-permute-start(bf16[128,2560]{1,0:T(8,128)(2,1)} %slice.543), channel_id=1, source_target_pairs={{0,8},{4,12},{8,0},{12,4},{16,24},{20,28},{24,16},{28,20},{1,9},{5... | collective-permute-start | bytes 1966088 | tf_op jit(solution)/shard_map/ppermute | solution.py:79
  117.6 16.5 %collective-permute-start.9 = (bf16[128,2560]{1,0:T(8,128)(2,1)}, bf16[128,2560]{1,0:T(8,128)(2,1)}, u32[]{:S(2)}, u32[]{:S(2)}) collective-permute-start(bf16[128,2560]{1,0:T(8,128)(2,1)} %slice.542), channel_id=1, source_target_pairs={{0,16},{4,20},{8,24},{12,28},{16,0},{20,4},{24,8},{28,12},{1,17},{... | collective-permute-start | bytes 1966088 | tf_op jit(solution)/shard_map/ppermute | solution.py:79
  145.7 35.4 %collective-permute-start.12 = (bf16[256,2560]{1,0:T(8,128)(2,1)}, bf16[256,2560]{1,0:T(8,128)(2,1)S(1)}, u32[]{:S(2)}, u32[]{:S(2)}) collective-permute-start(bf16[256,2560]{1,0:T(8,128)(2,1)} %fence.35.refs_0_), channel_id=1, source_target_pairs={{0,16},{4,20},{8,24},{12,28},{16,0},{20,4},{24,8},{28,12},{1,17},{... | collective-permute-start | bytes 3932168 | tf_op jit(solution)/shard_map/ppermute | solution.py:79
  146.6 34.5 %collective-permute-start.11 = (bf16[256,2560]{1,0:T(8,128)(2,1)}, bf16[256,2560]{1,0:T(8,128)(2,1)S(1)}, u32[]{:S(2)}, u32[]{:S(2)}) collective-permute-start(bf16[256,2560]{1,0:T(8,128)(2,1)} %fence.35.refs_0_), channel_id=1, source_target_pairs={{0,8},{4,12},{8,0},{12,4},{16,24},{20,28},{24,16},{28,20},{1,9},{5... | collective-permute-start | bytes 3932168 | tf_op jit(solution)/shard_map/ppermute | solution.py:79
  185.5 16.8 %collective-permute-start.14 = (bf16[128,2560]{1,0:T(8,128)(2,1)S(1)}, bf16[128,2560]{1,0:T(8,128)(2,1)S(1)}, u32[]{:S(2)}, u32[]{:S(2)}) collective-permute-start(bf16[128,2560]{1,0:T(8,128)(2,1)S(1)} %slice.552), channel_id=1, source_target_pairs={{0,8},{4,12},{8,0},{12,4},{16,24},{20,28},{24,16},{28,20},{1,9},{5... | collective-permute-start | bytes 1966088 | tf_op jit(solution)/shard_map/ppermute | solution.py:79
  186.6 16.5 %collective-permute-start.15 = (bf16[128,2560]{1,0:T(8,128)(2,1)S(1)}, bf16[128,2560]{1,0:T(8,128)(2,1)S(1)}, u32[]{:S(2)}, u32[]{:S(2)}) collective-permute-start(bf16[128,2560]{1,0:T(8,128)(2,1)S(1)} %slice.553), channel_id=1, source_target_pairs={{0,16},{4,20},{8,24},{12,28},{16,0},{20,4},{24,8},{28,12},{1,17},{... | collective-permute-start | bytes 1966088 | tf_op jit(solution)/shard_map/ppermute | solution.py:79
  219.0 30.8 %collective-permute-start.21 = (bf16[256,2560]{1,0:T(8,128)(2,1)}, bf16[256,2560]{1,0:T(8,128)(2,1)S(1)}, u32[]{:S(2)}, u32[]{:S(2)}) collective-permute-start(bf16[256,2560]{1,0:T(8,128)(2,1)} %fence.37.refs_0_), channel_id=1, source_target_pairs={{0,16},{4,20},{8,24},{12,28},{16,0},{20,4},{24,8},{28,12},{1,17},{... | collective-permute-start | bytes 3932168 | tf_op jit(solution)/shard_map/ppermute | solution.py:79
  220.0 30.5 %collective-permute-start.20 = (bf16[256,2560]{1,0:T(8,128)(2,1)}, bf16[256,2560]{1,0:T(8,128)(2,1)S(1)}, u32[]{:S(2)}, u32[]{:S(2)}) collective-permute-start(bf16[256,2560]{1,0:T(8,128)(2,1)} %fence.37.refs_0_), channel_id=1, source_target_pairs={{0,8},{4,12},{8,0},{12,4},{16,24},{20,28},{24,16},{28,20},{1,9},{5... | collective-permute-start | bytes 3932168 | tf_op jit(solution)/shard_map/ppermute | solution.py:79
  253.8 15.5 %collective-permute-start.22 = (bf16[128,2560]{1,0:T(8,128)(2,1)S(1)}, bf16[128,2560]{1,0:T(8,128)(2,1)S(1)}, u32[]{:S(2)}, u32[]{:S(2)}) collective-permute-start(bf16[128,2560]{1,0:T(8,128)(2,1)S(1)} %slice.562), channel_id=1, source_target_pairs={{0,8},{4,12},{8,0},{12,4},{16,24},{20,28},{24,16},{28,20},{1,9},{5... | collective-permute-start | bytes 1966088 | tf_op jit(solution)/shard_map/ppermute | solution.py:79
  255.0 15.1 %collective-permute-start.23 = (bf16[128,2560]{1,0:T(8,128)(2,1)S(1)}, bf16[128,2560]{1,0:T(8,128)(2,1)S(1)}, u32[]{:S(2)}, u32[]{:S(2)}) collective-permute-start(bf16[128,2560]{1,0:T(8,128)(2,1)S(1)} %slice.563), channel_id=1, source_target_pairs={{0,16},{4,20},{8,24},{12,28},{16,0},{20,4},{24,8},{28,12},{1,17},{... | collective-permute-start | bytes 1966088 | tf_op jit(solution)/shard_map/ppermute | solution.py:79
  282.4 20.1 %collective-permute-start.25 = (bf16[128,3072]{1,0:T(8,128)(2,1)}, bf16[128,3072]{1,0:T(8,128)(2,1)S(1)}, u32[]{:S(2)}, u32[]{:S(2)}) collective-permute-start(bf16[128,3072]{1,0:T(8,128)(2,1)} %slice.567), channel_id=1, source_target_pairs={{0,8},{4,12},{8,0},{12,4},{16,24},{20,28},{24,16},{28,20},{1,9},{5... | collective-permute-start | bytes 2359304 | tf_op jit(solution)/shard_map/ppermute | solution.py:79
  283.4 20.0 %collective-permute-start.26 = (bf16[128,3072]{1,0:T(8,128)(2,1)}, bf16[128,3072]{1,0:T(8,128)(2,1)}, u32[]{:S(2)}, u32[]{:S(2)}) collective-permute-start(bf16[128,3072]{1,0:T(8,128)(2,1)} %slice.568), channel_id=1, source_target_pairs={{0,16},{4,20},{8,24},{12,28},{16,0},{20,4},{24,8},{28,12},{1,17},{... | collective-permute-start | bytes 2359304 | tf_op jit(solution)/shard_map/ppermute | solution.py:79
  298.4 159.1 %all-gather.18.cloned.1.call-start = ((), (), s32[]{:S(2)}) async-start(), calls=%async_computation.7 | async-start | bytes 5242880 | tf_op jit(solution)/shard_map/all_gather | solution.py:605
  309.3 63.0 %collective-permute-start.27 = (bf16[1024,3072]{1,0:T(8,128)(2,1)}, bf16[1024,3072]{1,0:T(8,128)(2,1)}, u32[]{:S(2)}, u32[]{:S(2)}) collective-permute-start(bf16[1024,3072]{1,0:T(8,128)(2,1)} %assemble.10.refs_0_), channel_id=1, source_target_pairs={{0,4},{4,0},{8,12},{12,8},{16,20},{20,16},{24,28},{28,24},{1,5},{5... | collective-permute-start | bytes 18874376 | tf_op jit(solution)/shard_map/ppermute | solution.py:79
  312.0 20.1 %collective-permute-start.29 = (bf16[256,1536]{1,0:T(8,128)(2,1)}, bf16[256,1536]{1,0:T(8,128)(2,1)S(1)}, u32[]{:S(2)}, u32[]{:S(2)}) collective-permute-start(bf16[256,1536]{1,0:T(8,128)(2,1)} %fence.41.refs_0_), channel_id=1, source_target_pairs={{0,16},{4,20},{8,24},{12,28},{16,0},{20,4},{24,8},{28,12},{1,17},{... | collective-permute-start | bytes 2359304 | tf_op jit(solution)/shard_map/ppermute | solution.py:79
  313.3 20.2 %collective-permute-start.28 = (bf16[256,1536]{1,0:T(8,128)(2,1)}, bf16[256,1536]{1,0:T(8,128)(2,1)S(1)}, u32[]{:S(2)}, u32[]{:S(2)}) collective-permute-start(bf16[256,1536]{1,0:T(8,128)(2,1)} %fence.41.refs_0_), channel_id=1, source_target_pairs={{0,8},{4,12},{8,0},{12,4},{16,24},{20,28},{24,16},{28,20},{1,9},{5... | collective-permute-start | bytes 2359304 | tf_op jit(solution)/shard_map/ppermute | solution.py:79
  371.9 255.3 %reduce-scatter.6.cloned.1.call-start = ((), (), s32[]{:S(2)}) async-start(), calls=%async_computation.8 | async-start | bytes 5242880 | tf_op jit(solution)/shard_map/reduce_scatter | solution.py:614
  436.9 190.3 %reduce-scatter.8.cloned.1.call-start = ((), (), s32[]{:S(2)}) async-start(), calls=%async_computation.9 | async-start | bytes 5242880 | tf_op jit(solution)/shard_map/reduce_scatter | solution.py:614
  540.0 189.7 %reduce-scatter.10.cloned.1.call-start = ((), (), s32[]{:S(2)}) async-start(), calls=%async_computation.10 | async-start | bytes 5242880 | tf_op jit(solution)/shard_map/reduce_scatter | solution.py:639
  549.7 66.9 %collective-permute-start.33 = (bf16[1024,1536]{1,0:T(8,128)(2,1)}, bf16[1024,1536]{1,0:T(8,128)(2,1)S(1)}, u32[]{:S(2)}, u32[]{:S(2)}) collective-permute-start(bf16[1024,1536]{1,0:T(8,128)(2,1)} %add_convert_fusion.2), channel_id=1, source_target_pairs={{0,4},{4,0},{8,12},{12,8},{16,20},{20,16},{24,28},{28,24},{1,5},{5... | collective-permute-start | bytes 9437192 | tf_op jit(solution)/shard_map/ppermute | solution.py:79
  571.3 51.2 %collective-permute-start.34 = (bf16[1024,3072]{1,0:T(8,128)(2,1)}, bf16[1024,3072]{1,0:T(8,128)(2,1)}, u32[]{:S(2)}, u32[]{:S(2)}) collective-permute-start(bf16[1024,3072]{1,0:T(8,128)(2,1)} %add_convert_fusion), channel_id=1, source_target_pairs={{0,4},{4,0},{8,12},{12,8},{16,20},{20,16},{24,28},{28,24},{1,5},{5... | collective-permute-start | bytes 18874376 | tf_op jit(solution)/shard_map/ppermute | solution.py:79
  627.3 160.0 %reduce-scatter.12.cloned.1.call-start = ((), (), s32[]{:S(2)}) async-start(), calls=%async_computation.11 | async-start | bytes 5242880 | tf_op jit(solution)/shard_map/reduce_scatter | solution.py:639
  630.2 39.2 %collective-permute-start.36 = (bf16[256,1536]{1,0:T(8,128)(2,1)}, bf16[256,1536]{1,0:T(8,128)(2,1)}, u32[]{:S(2)}, u32[]{:S(2)}) collective-permute-start(bf16[256,1536]{1,0:T(8,128)(2,1)} %get-tuple-element.226.refs_3_), channel_id=1, source_target_pairs={{0,16},{4,20},{8,24},{12,28},{16,0},{20,4},{24,8},{28,12},{1,17},{... | collective-permute-start | bytes 2359304 | tf_op jit(solution)/shard_map/ppermute | solution.py:79
  631.7 39.0 %collective-permute-start.35 = (bf16[256,1536]{1,0:T(8,128)(2,1)}, bf16[256,1536]{1,0:T(8,128)(2,1)}, u32[]{:S(2)}, u32[]{:S(2)}) collective-permute-start(bf16[256,1536]{1,0:T(8,128)(2,1)} %get-tuple-element.227.refs_2_), channel_id=1, source_target_pairs={{0,8},{4,12},{8,0},{12,4},{16,24},{20,28},{24,16},{28,20},{1,9},{5... | collective-permute-start | bytes 2359304 | tf_op jit(solution)/shard_map/ppermute | solution.py:79
  633.2 50.5 %collective-permute-start.38 = (bf16[256,3072]{1,0:T(8,128)(2,1)}, bf16[256,3072]{1,0:T(8,128)(2,1)}, u32[]{:S(2)}, u32[]{:S(2)}) collective-permute-start(bf16[256,3072]{1,0:T(8,128)(2,1)} %get-tuple-element.200.refs_5_), channel_id=1, source_target_pairs={{0,16},{4,20},{8,24},{12,28},{16,0},{20,4},{24,8},{28,12},{1,17},{... | collective-permute-start | bytes 4718600 | tf_op jit(solution)/shard_map/ppermute | solution.py:79
  633.7 51.1 %collective-permute-start.37 = (bf16[256,3072]{1,0:T(8,128)(2,1)}, bf16[256,3072]{1,0:T(8,128)(2,1)}, u32[]{:S(2)}, u32[]{:S(2)}) collective-permute-start(bf16[256,3072]{1,0:T(8,128)(2,1)} %get-tuple-element.201.refs_4_), channel_id=1, source_target_pairs={{0,8},{4,12},{8,0},{12,4},{16,24},{20,28},{24,16},{28,20},{1,9},{5... | collective-permute-start | bytes 4718600 | tf_op jit(solution)/shard_map/ppermute | solution.py:79
  635.6 233.6 %all-gather.22.cloned.1.call-start = ((), (), s32[]{:S(2)}) async-start(), calls=%async_computation.14 | async-start | bytes 5242880 | tf_op jit(solution)/shard_map/all_gather | solution.py:679
  668.1 16.7 %collective-permute-start.41 = (f32[2,2560]{1,0:T(2,128)S(1)}, f32[2,2560]{1,0:T(2,128)S(1)}, u32[]{:S(2)}, u32[]{:S(2)}) collective-permute-start(f32[2,2560]{1,0:T(2,128)S(1)} %pad_maximum_fusion.15), channel_id=1, source_target_pairs={{3,0},{7,4},{11,8},{15,12},{19,16},{23,20},{27,24},{31,28}} | collective-permute-start | bytes 61448 | tf_op jit(solution)/shard_map/ppermute | solution.py:162
  669.4 15.4 %collective-permute-start.40 = (f32[2,2560]{1,0:T(2,128)S(1)}, f32[2,2560]{1,0:T(2,128)S(1)}, u32[]{:S(2)}, u32[]{:S(2)}) collective-permute-start(f32[2,2560]{1,0:T(2,128)S(1)} %pad_maximum_fusion.15), channel_id=1, source_target_pairs={{2,0},{3,1},{6,4},{7,5},{10,8},{11,9},{14,12},{15,13},{18,16},{19,... | collective-permute-start | bytes 61448 | tf_op jit(solution)/shard_map/ppermute | solution.py:162
  712.9 16.7 %collective-permute-start.42 = (f32[16,2560]{1,0:T(8,128)S(1)}, f32[16,2560]{1,0:T(8,128)S(1)}, u32[]{:S(2)}, u32[]{:S(2)}) collective-permute-start(f32[16,2560]{1,0:T(8,128)S(1)} %slice.603), channel_id=1, source_target_pairs={{1,0},{2,1},{3,2},{5,4},{6,5},{7,6},{9,8},{10,9},{11,10},{13,12},{... | collective-permute-start | bytes 491528 | tf_op jit(solution)/shard_map/ppermute | solution.py:162
  759.6 190.3 %all-gather.28.cloned.1.call-start = ((), (), s32[]{:S(2)}) async-start(), calls=%async_computation.17 | async-start | bytes 5242880 | tf_op jit(solution)/shard_map/all_gather | solution.py:679
  767.6 19.7 %collective-permute-start.43 = (bf16[1024,2560]{1,0:T(8,128)(2,1)}, bf16[1024,2560]{1,0:T(8,128)(2,1)}, u32[]{:S(2)}, u32[]{:S(2)}) collective-permute-start(bf16[1024,2560]{1,0:T(8,128)(2,1)} %convolution_convert_fusion.5), channel_id=1, source_target_pairs={{0,4},{4,0},{8,12},{12,8},{16,20},{20,16},{24,28},{28,24},{1,5},{5... | collective-permute-start | bytes 15728648 | tf_op jit(solution)/shard_map/ppermute | solution.py:79
  767.6 308.7 %all-gather.24.cloned.1.call-start = ((), (), s32[]{:S(2)}) async-start(), calls=%async_computation.15 | async-start | bytes 5242880 | tf_op jit(solution)/shard_map/all_gather | solution.py:689
  804.1 176.2 %collective-permute-start.51 = (bf16[256,2560]{1,0:T(8,128)(2,1)}, bf16[256,2560]{1,0:T(8,128)(2,1)}, u32[]{:S(2)}, u32[]{:S(2)}) collective-permute-start(bf16[256,2560]{1,0:T(8,128)(2,1)} %get-tuple-element.208), channel_id=1, source_target_pairs={{0,8},{4,12},{8,0},{12,4},{16,24},{20,28},{24,16},{28,20},{1,9},{5... | collective-permute-start | bytes 3932168 | tf_op jit(solution)/shard_map/ppermute | solution.py:79
  805.5 174.7 %collective-permute-start.50 = (bf16[256,2560]{1,0:T(8,128)(2,1)}, bf16[256,2560]{1,0:T(8,128)(2,1)}, u32[]{:S(2)}, u32[]{:S(2)}) collective-permute-start(bf16[256,2560]{1,0:T(8,128)(2,1)} %get-tuple-element.209), channel_id=1, source_target_pairs={{0,16},{4,20},{8,24},{12,28},{16,0},{20,4},{24,8},{28,12},{1,17},{... | collective-permute-start | bytes 3932168 | tf_op jit(solution)/shard_map/ppermute | solution.py:79
  869.2 242.4 %all-gather.26.cloned.1.call-start = ((), (), s32[]{:S(2)}) async-start(), calls=%async_computation.16 | async-start | bytes 5242880 | tf_op jit(solution)/shard_map/all_gather | solution.py:689
  971.9 22.1 %collective-permute-start.44 = (bf16[4,4,26752]{2,1,0:T(4,128)(2,1)S(1)}, bf16[4,4,26752]{2,1,0:T(4,128)(2,1)}, u32[]{:S(2)}, u32[]{:S(2)}) collective-permute-start(bf16[4,4,26752]{2,1,0:T(4,128)(2,1)S(1)} %slice.774), channel_id=1, source_target_pairs={{0,16},{4,20},{8,24},{12,28},{16,0},{20,4},{24,8},{28,12},{1,17},{... | collective-permute-start | bytes 2568200 | tf_op jit(solution)/shard_map/ppermute | solution.py:79
  979.4 37.6 %collective-permute-start.59 = (bf16[1024,2560]{1,0:T(8,128)(2,1)}, bf16[1024,2560]{1,0:T(8,128)(2,1)}, u32[]{:S(2)}, u32[]{:S(2)}) collective-permute-start(bf16[1024,2560]{1,0:T(8,128)(2,1)} %convolution_convert_fusion), channel_id=1, source_target_pairs={{0,4},{4,0},{8,12},{12,8},{16,20},{20,16},{24,28},{28,24},{1,5},{5... | collective-permute-start | bytes 15728648 | tf_op jit(solution)/shard_map/ppermute | solution.py:79
  979.4 18.7 %collective-permute-start.54 = (bf16[1024,2560]{1,0:T(8,128)(2,1)}, bf16[1024,2560]{1,0:T(8,128)(2,1)}, u32[]{:S(2)}, u32[]{:S(2)}) collective-permute-start(bf16[1024,2560]{1,0:T(8,128)(2,1)} %convolution_convert_fusion.2), channel_id=1, source_target_pairs={{0,4},{4,0},{8,12},{12,8},{16,20},{20,16},{24,28},{28,24},{1,5},{5... | collective-permute-start | bytes 15728648 | tf_op jit(solution)/shard_map/ppermute | solution.py:79
  979.9 206.2 %reduce-scatter.14.cloned.1.call-start = ((), (), s32[]{:S(2)}) async-start(), calls=%async_computation.12 | async-start | bytes 4915200 | tf_op jit(solution)/shard_map/reduce_scatter | solution.py:702
  983.9 20.3 %collective-permute-start.52 = (bf16[128,2560]{1,0:T(8,128)(2,1)}, bf16[128,2560]{1,0:T(8,128)(2,1)S(1)}, u32[]{:S(2)}, u32[]{:S(2)}) collective-permute-start(bf16[128,2560]{1,0:T(8,128)(2,1)} %get-tuple-element.101), channel_id=1, source_target_pairs={{0,8},{4,12},{8,0},{12,4},{16,24},{20,28},{24,16},{28,20},{1,9},{5... | collective-permute-start | bytes 1966088 | tf_op jit(solution)/shard_map/ppermute | solution.py:79
  985.3 22.7 %collective-permute-start.53 = (bf16[128,2560]{1,0:T(8,128)(2,1)}, bf16[128,2560]{1,0:T(8,128)(2,1)}, u32[]{:S(2)}, u32[]{:S(2)}) collective-permute-start(bf16[128,2560]{1,0:T(8,128)(2,1)} %get-tuple-element.102), channel_id=1, source_target_pairs={{0,16},{4,20},{8,24},{12,28},{16,0},{20,4},{24,8},{28,12},{1,17},{... | collective-permute-start | bytes 1966088 | tf_op jit(solution)/shard_map/ppermute | solution.py:79
  996.5 44.6 %collective-permute-start.45 = (bf16[2,4,26752]{2,1,0:T(4,128)(2,1)}, bf16[2,4,26752]{2,1,0:T(4,128)(2,1)}, u32[]{:S(2)}, u32[]{:S(2)}) collective-permute-start(bf16[2,4,26752]{2,1,0:T(4,128)(2,1)} %slice.776), channel_id=1, source_target_pairs={{0,8},{4,12},{8,0},{12,4},{16,24},{20,28},{24,16},{28,20},{1,9},{5... | collective-permute-start | bytes 1284104 | tf_op jit(solution)/shard_map/ppermute | solution.py:79
  1002.7 32.2 %collective-permute-start.55 = (bf16[256,2560]{1,0:T(8,128)(2,1)}, bf16[256,2560]{1,0:T(8,128)(2,1)S(1)}, u32[]{:S(2)}, u32[]{:S(2)}) collective-permute-start(bf16[256,2560]{1,0:T(8,128)(2,1)} %get-tuple-element.104), channel_id=1, source_target_pairs={{0,16},{4,20},{8,24},{12,28},{16,0},{20,4},{24,8},{28,12},{1,17},{... | collective-permute-start | bytes 3932168 | tf_op jit(solution)/shard_map/ppermute | solution.py:79
  1004.2 33.8 %collective-permute-start.56 = (bf16[256,2560]{1,0:T(8,128)(2,1)}, bf16[256,2560]{1,0:T(8,128)(2,1)S(1)}, u32[]{:S(2)}, u32[]{:S(2)}) collective-permute-start(bf16[256,2560]{1,0:T(8,128)(2,1)} %get-tuple-element.105), channel_id=1, source_target_pairs={{0,8},{4,12},{8,0},{12,4},{16,24},{20,28},{24,16},{28,20},{1,9},{5... | collective-permute-start | bytes 3932168 | tf_op jit(solution)/shard_map/ppermute | solution.py:79
  1039.0 31.9 %collective-permute-start.60 = (bf16[256,2560]{1,0:T(8,128)(2,1)}, bf16[256,2560]{1,0:T(8,128)(2,1)S(1)}, u32[]{:S(2)}, u32[]{:S(2)}) collective-permute-start(bf16[256,2560]{1,0:T(8,128)(2,1)} %get-tuple-element.109), channel_id=1, source_target_pairs={{0,16},{4,20},{8,24},{12,28},{16,0},{20,4},{24,8},{28,12},{1,17},{... | collective-permute-start | bytes 3932168 | tf_op jit(solution)/shard_map/ppermute | solution.py:79
  1039.5 31.9 %collective-permute-start.61 = (bf16[256,2560]{1,0:T(8,128)(2,1)}, bf16[256,2560]{1,0:T(8,128)(2,1)S(1)}, u32[]{:S(2)}, u32[]{:S(2)}) collective-permute-start(bf16[256,2560]{1,0:T(8,128)(2,1)} %get-tuple-element.110), channel_id=1, source_target_pairs={{0,8},{4,12},{8,0},{12,4},{16,24},{20,28},{24,16},{28,20},{1,9},{5... | collective-permute-start | bytes 3932168 | tf_op jit(solution)/shard_map/ppermute | solution.py:79
  1043.8 67.8 %collective-permute-start.46 = (bf16[1,4,26752]{2,1,0:T(4,128)(2,1)}, bf16[1,4,26752]{2,1,0:T(4,128)(2,1)S(1)}, u32[]{:S(2)}, u32[]{:S(2)}) collective-permute-start(bf16[1,4,26752]{2,1,0:T(4,128)(2,1)} %slice.778), channel_id=1, source_target_pairs={{0,4},{4,0},{8,12},{12,8},{16,20},{20,16},{24,28},{28,24},{1,5},{5... | collective-permute-start | bytes 642056 | tf_op jit(solution)/shard_map/ppermute | solution.py:79
  1047.4 38.0 %collective-permute-start.57 = (bf16[128,2560]{1,0:T(8,128)(2,1)}, bf16[128,2560]{1,0:T(8,128)(2,1)S(1)}, u32[]{:S(2)}, u32[]{:S(2)}) collective-permute-start(bf16[128,2560]{1,0:T(8,128)(2,1)} %get-tuple-element.106), channel_id=1, source_target_pairs={{0,8},{4,12},{8,0},{12,4},{16,24},{20,28},{24,16},{28,20},{1,9},{5... | collective-permute-start | bytes 1966088 | tf_op jit(solution)/shard_map/ppermute | solution.py:79
  1047.9 37.5 %collective-permute-start.58 = (bf16[128,2560]{1,0:T(8,128)(2,1)}, bf16[128,2560]{1,0:T(8,128)(2,1)}, u32[]{:S(2)}, u32[]{:S(2)}) collective-permute-start(bf16[128,2560]{1,0:T(8,128)(2,1)} %get-tuple-element.107), channel_id=1, source_target_pairs={{0,16},{4,20},{8,24},{12,28},{16,0},{20,4},{24,8},{28,12},{1,17},{... | collective-permute-start | bytes 1966088 | tf_op jit(solution)/shard_map/ppermute | solution.py:79
  1076.3 21.1 %collective-permute-start.62 = (bf16[128,2560]{1,0:T(8,128)(2,1)}, bf16[128,2560]{1,0:T(8,128)(2,1)}, u32[]{:S(2)}, u32[]{:S(2)}) collective-permute-start(bf16[128,2560]{1,0:T(8,128)(2,1)} %get-tuple-element.111), channel_id=1, source_target_pairs={{0,8},{4,12},{8,0},{12,4},{16,24},{20,28},{24,16},{28,20},{1,9},{5... | collective-permute-start | bytes 1966088 | tf_op jit(solution)/shard_map/ppermute | solution.py:79
  1077.9 19.6 %collective-permute-start.63 = (bf16[128,2560]{1,0:T(8,128)(2,1)}, bf16[128,2560]{1,0:T(8,128)(2,1)}, u32[]{:S(2)}, u32[]{:S(2)}) collective-permute-start(bf16[128,2560]{1,0:T(8,128)(2,1)} %get-tuple-element.112), channel_id=1, source_target_pairs={{0,16},{4,20},{8,24},{12,28},{16,0},{20,4},{24,8},{28,12},{1,17},{... | collective-permute-start | bytes 1966088 | tf_op jit(solution)/shard_map/ppermute | solution.py:79
  1122.9 22.6 %collective-permute-start.66 = (bf16[128,1536]{1,0:T(8,128)(2,1)}, bf16[128,1536]{1,0:T(8,128)(2,1)S(1)}, u32[]{:S(2)}, u32[]{:S(2)}) collective-permute-start(bf16[128,1536]{1,0:T(8,128)(2,1)} %get-tuple-element.115), channel_id=1, source_target_pairs={{0,8},{4,12},{8,0},{12,4},{16,24},{20,28},{24,16},{28,20},{1,9},{5... | collective-permute-start | bytes 1179656 | tf_op jit(solution)/shard_map/ppermute | solution.py:79
  1124.6 20.9 %collective-permute-start.67 = (bf16[128,1536]{1,0:T(8,128)(2,1)}, bf16[128,1536]{1,0:T(8,128)(2,1)S(1)}, u32[]{:S(2)}, u32[]{:S(2)}) collective-permute-start(bf16[128,1536]{1,0:T(8,128)(2,1)} %get-tuple-element.116), channel_id=1, source_target_pairs={{0,16},{4,20},{8,24},{12,28},{16,0},{20,4},{24,8},{28,12},{1,17},{... | collective-permute-start | bytes 1179656 | tf_op jit(solution)/shard_map/ppermute | solution.py:79
  1135.5 17.9 %collective-permute-start.64 = (bf16[128,3072]{1,0:T(8,128)(2,1)}, bf16[128,3072]{1,0:T(8,128)(2,1)S(1)}, u32[]{:S(2)}, u32[]{:S(2)}) collective-permute-start(bf16[128,3072]{1,0:T(8,128)(2,1)} %get-tuple-element.113), channel_id=1, source_target_pairs={{0,8},{4,12},{8,0},{12,4},{16,24},{20,28},{24,16},{28,20},{1,9},{5... | collective-permute-start | bytes 2359304 | tf_op jit(solution)/shard_map/ppermute | solution.py:79
  1137.0 16.7 %collective-permute-start.65 = (bf16[128,3072]{1,0:T(8,128)(2,1)}, bf16[128,3072]{1,0:T(8,128)(2,1)S(1)}, u32[]{:S(2)}, u32[]{:S(2)}) collective-permute-start(bf16[128,3072]{1,0:T(8,128)(2,1)} %get-tuple-element.114), channel_id=1, source_target_pairs={{0,16},{4,20},{8,24},{12,28},{16,0},{20,4},{24,8},{28,12},{1,17},{... | collective-permute-start | bytes 2359304 | tf_op jit(solution)/shard_map/ppermute | solution.py:79
  (133 other events, 1217.6 us)
Sparse Core Ops, SparseCore 0:
  12.1 43.3 all-gather.13
  71.7 54.9 all-gather.19
  298.5 78.2 all-gather.15
  378.2 79.2 all-gather.17
  459.6 75.2 reduce-scatter.5
  540.1 75.2 reduce-scatter.7
  627.4 76.6 reduce-scatter.9
  706.5 80.7 reduce-scatter.11
  788.8 80.3 all-gather.21
  870.6 79.2 all-gather.27
  951.5 79.2 all-gather.23
  1032.3 79.2 all-gather.25
  1113.9 72.2 reduce-scatter.13

commit v9 on v8

--- a/solution.py
+++ b/solution.py
@@ -169,6 +169,30 @@
         block = lax.dynamic_index_in_dim(values, (turn + k) % n, 0, keepdims=False)
         total = total + z_shift(block, k, n).astype(F32)
     return total
+
+
+class LineSum:
+    def __init__(self, blocks, n):
+        self.blocks, self.n, self.turn, self.rounds = blocks, n, lax.axis_index("tensor"), 0
+        self.right = self.left = None
+
+    def block(self, k):
+        return lax.dynamic_index_in_dim(self.blocks, k % self.n, 0, keepdims=False)
+
+    def go(self, *others):
+        self.rounds += 1
+        t, n = self.rounds, self.n
+        right, left = self.block(self.turn + n - t), self.block(self.turn + t)
+        if t > 1:
+            before = fence([self.right, self.left], *others)
+            right, left = add_all([right, before[0]]), add_all([left, before[1]])
+        self.right = lax.ppermute(right, "tensor", [(k, k + 1) for k in range(min(t, n - 1))])
+        self.left = lax.ppermute(left, "tensor", [(k, k - 1) for k in range(max(n - t, 1), n)])
+
+    def finish(self):
+        while self.rounds < self.n - 1:
+            self.go()
+        return self.block(self.turn).astype(F32) + self.right.astype(F32) + self.left.astype(F32)
 
 
 def small_masks(size):
@@ -564,7 +588,7 @@
     row = jnp.where(row < part, spot * part + row, head)
     order = (jnp.arange(head)[:, None] == row[None, :]).astype(BF)
 
-    w_r, came_r = spread_end(some_r, size, some_small[1:], (others, gain, par, order, lru))
+    w_r, came_r = spread_end(some_r, size, (), (others, order))
     first = (extended * first_rate * gain[0]).astype(BF)
     inputs, first_own, first_rate = extended[HALO:], first[HALO:], first_rate[HALO:]
     cut = d_model // 2
@@ -579,10 +603,10 @@
     )
     ends = jnp.concatenate([prod[-1:], state[-1:]])
     came = [z_shift(ends, k, n, False) for k in range(1, n)]
+    w_g, came_g = spread_end(some_g, size, (ends,), came)
     carry = jnp.zeros((1, width), F32)
     for end in came[::-1]:
         carry = end[1:] + end[:1] * carry
-    w_g, came_g = spread_end(some_g, size, (ends,), ())
     some_o = spread_begin(z_out, size, *came_g)
     branch_pre = wide_dot(first_own, w_g)
     recurrent = (state + prod * carry) * live
@@ -683,24 +707,30 @@
     sum_g, sum_r = by_cols(first_own, pre_low), by_cols(first_own, rec_low)
     results = [mlp_result(h, mlp_sum) for h, mlp_sum in enumerate(fence(mlp_sums, sum_o.terms[1]))]
     got_o = sum_o.hop(sum_o.sources())
-    sum_o.hop(fence(sum_o.sources(), gathered[0]))
-    got_g = sum_g.hop(fence(sum_g.sources(), gathered[0]))
-    results = fence(results, gathered[0])
+    got_g = sum_g.hop(fence(sum_g.sources(), *got_o))
+    pause = (gathered[0], *got_g)
+    sum_o.hop(fence(sum_o.sources(), *pause))
+    got_r = sum_r.hop(fence(sum_r.sources(), *pause))
+    results = fence(results, gathered[0], *got_g)
     results = [lax.all_gather(result, "tensor", axis=0) for result in results]
-    sum_g.hop(fence(sum_g.sources(), gathered[1]))
-    got_r = sum_r.hop(fence(sum_r.sources(), gathered[1], *got_g))
-    d_lru, dpar = fence([d_lru, dpar], gathered[1])
-    sum_r.hop(fence(sum_r.sources(), results[0]))
+    sum_g.hop(fence(sum_g.sources(), *pause))
+    got_r = sum_r.hop(fence(sum_r.sources(), *got_r))
+    owned = jnp.stack([total.finish().reshape(d_own, n, width // n) for total in (sum_o, sum_g, sum_r)])
+    owned = LineSum(owned.transpose(2, 0, 1, 3), n)
+    owned.go()
+    pause = (gathered[1], owned.right, owned.left)
+    d_lru, dpar = fence([d_lru, dpar], *pause)
     if sum_dn.square:
-        sum_dn.hop(fence(sum_dn.sources(), results[0]))
-        sum_gu.hop(fence(sum_gu.sources(), results[0]))
-    tokens_out = interleave(*fence(gathered, results[0])).reshape(n * rows, d_model)
+        sum_dn.hop(fence(sum_dn.sources(), *pause))
+        sum_gu.hop(fence(sum_gu.sources(), *pause))
+    owned.go(gathered[1])
+    tokens_out = interleave(*fence(gathered, owned.right)).reshape(n * rows, d_model)
+    if n > 3:
+        owned.go(results[0])
     g_gu, g_dn = sum_gu.finish().astype(F32), sum_dn.finish().astype(F32)
-    owned = jnp.stack([total.finish().reshape(d_own, n, width // n) for total in (sum_o, sum_g, sum_r)])
-    (owned,) = fence([owned.transpose(2, 0, 1, 3)], results[1])
-    output = interleave(*results).reshape(n * rows, d_model)
-    owned = lax.psum_scatter(owned, "tensor", scatter_dimension=0).astype(F32)
-    g_o, g_g, g_r = owned[0], owned[1], owned[2]
+    g_all = owned.finish()
+    output = interleave(*fence(results, owned.right, owned.left)).reshape(n * rows, d_model)
+    g_o, g_g, g_r = g_all[0], g_all[1], g_all[2]
 
     d_gain = permute_gain(jnp.stack([gain_one, gain_two]), inverse)
     d_chan = jnp.concatenate([dpar[:7], dpar[7:] * 8.0 * jax.nn.sigmoid(-chans[7:])])

time: 1200 us -> 1190 us (level)
  waiting for transfers between devices: 417 us -> 388 us
  starting transfers between devices: 78.2 us -> 90.9 us
    all_gather x2, waiting for transfers between devices: 126 us -> 15.1 us  [on_device(): lax.all_gather(grad_tokens[h * half:(h + 1) * half], 'tensor', axis=0)]
    ppermute x0 -> x6, waiting for transfers between devices: none -> 93.3 us  [the longest x3 60.1 us: go(): lax.ppermute(left, 'tensor', [(k, k - 1) for k in range(max(n - t, 1), n)])]
    reduce_scatter x1 -> x0, waiting for transfers between devices: 26.6 us -> none  [on_device(): owned = lax.psum_scatter(owned, 'tensor', scatter_dimension=0).astype(F32)]
    ppermute x0 -> x6, starting transfers between devices: none -> 17.4 us  [the longest x3 13.8 us: go(): lax.ppermute(right, 'tensor', [(k, k + 1) for k in range(min(t, n - 1))])]
    unnamed x245 -> x287, local copies, waits for them, and re-layouts: 37.9 us -> 43.1 us
    convert_element_type x18 -> x21, other arithmetic: 57.8 us -> 62.9 us  [add_all(): return total.astype(BF)]
  transfers between devices with their start and end apart: 81 -> 86, of which waited for: 42 -> 42; matrix products, arithmetic and copies ran while one was open for 42% -> 43% of each run, Pallas kernels for 10% -> 10%
where the time goes in v9:
time: 1190 us; the launch traced here: 1180 us
  waiting for transfers between devices  388 us (33%)
  matrix products  305 us (26%)
  Pallas kernels  138 us (12%)
  other arithmetic  136 us (11%)
  local copies, waits for them, and re-layouts  103 us (9%)
  starting transfers between devices  90.9 us (8%)
  between operations  17.4 us (1%)
    dot_general x34, matrix products, dot(): lax.dot_general(left, right, (dims, ((), ())), preferred_element_type=F32)  305 us
    ppermute x58, waiting for transfers between devices, exchange(): return lax.ppermute(values, 'dp', [(k, k ^ 1 << bit) for k in range(size)])  239 us
    convert_element_type x21, other arithmetic, add_all(): return total.astype(BF)  62.9 us
    pallas_call x3, Pallas kernels, kernel_call(): pl.pallas_call(body, grid_spec=pltpu.PrefetchScalarGridSpec(num_scalar_pr...  62.2 us
    ppermute x3, waiting for transfers between devices, go(): lax.ppermute(left, 'tensor', [(k, k - 1) for k in range(max(n - t, 1), n)])  60.1 us
    ppermute x58, starting transfers between devices, exchange(): return lax.ppermute(values, 'dp', [(k, k ^ 1 << bit) for k in range(size)])  52.5 us
    unnamed x287, local copies, waits for them, and re-layouts  43.1 us
    pallas_call x7, Pallas kernels, assemble(): pl.pallas_call(body, in_specs=[place] * (count + len(others)), out_specs=...  35.7 us
  transfers between devices with their start and end apart: 86, of which 42 were waited for; matrix products, arithmetic and copies ran while one was open for 43% of the time, Pallas kernels for 10%

profile of v9, /device:TPU:0, one launch (start us, length us, event | category | flops | bytes accessed | tf_op | source)
XLA Modules:
  0.0 1179.5 jit_solution(17672134596065254611)
XLA Ops:
  37.5 16.7 %collective-permute-done.1.refs_2_.refs_1_ = bf16[256,3072]{1,0:T(8,128)(2,1)S(1)} collective-permute-done((bf16[256,3072]{1,0:T(8,128)(2,1)}, bf16[256,3072]{1,0:T(8,128)(2,1)S(1)}, u32[]{:S(2)}, u32[]{:S(2)}) %collective-permute-start.1) | collective-permute-done | bytes 1572896 | tf_op jit(solution)/shard_map/ppermute | solution.py:79
  62.8 27.5 %collective-permute-done.9.refs_4_ = bf16[256,2560]{1,0:T(8,128)(2,1)S(1)} collective-permute-done((bf16[256,2560]{1,0:T(8,128)(2,1)S(1)}, bf16[256,2560]{1,0:T(8,128)(2,1)S(1)}, u32[]{:S(2)}, u32[]{:S(2)}) %collective-permute-start.9) | collective-permute-done | bytes 1310752 | tf_op jit(solution)/shard_map/ppermute | solution.py:79
  104.7 9.4 collective-permute-done.10.refs_2_
  122.1 7.3 collective-permute-done.6
  142.8 4.9 fusion.46
  147.7 7.2 convolution_add_fusion.pre_ref
  155.0 18.8 %recurrence.1 = (f32[512,2560]{1,0:T(8,128)}, f32[512,2560]{1,0:T(8,128)}, f32[512,2560]{1,0:T(8,128)}, f32[512,2560]{1,0:T(8,128)}, f32[512,2560]{1,0:T(8,128)}, /*index=5*/f32[512,2560]{1,0:T(8,128)}) custom-call(s32[1]{0:T(128)} %sub.38.live_ref, f32[528,2560]{1,0:T(8,128)} %convolution_add_fusion.pre_ref, f32[8,2560]{1,0:T(8,128)} %pad_maximum_fusion.14.par_ref, ...), custom_call_target="tpu_custom_call" | custom-call | flops 1024 | bytes 1024 | tf_op jit(solution)/shard_map/recurrence/pallas_call | solution.py:493
  182.5 5.3 collective-permute-start.18
  216.8 9.7 fusion.22
  226.6 10.0 collective-permute-done.21.refs_1_
  242.6 14.2 %collective-permute-done.22.refs_2_.refs_3_ = bf16[128,2560]{1,0:T(8,128)(2,1)S(1)} collective-permute-done((bf16[128,2560]{1,0:T(8,128)(2,1)S(1)}, bf16[128,2560]{1,0:T(8,128)(2,1)S(1)}, u32[]{:S(2)}, u32[]{:S(2)}) %collective-permute-start.22) | collective-permute-done | bytes 655392 | tf_op jit(solution)/shard_map/ppermute | solution.py:79
  290.9 6.1 assemble.10.refs_0_
  301.2 18.6 %collective-permute-done.29.refs_4_ = bf16[256,1536]{1,0:T(8,128)(2,1)S(1)} collective-permute-done((bf16[256,1536]{1,0:T(8,128)(2,1)}, bf16[256,1536]{1,0:T(8,128)(2,1)S(1)}, u32[]{:S(2)}, u32[]{:S(2)}) %collective-permute-start.29) | collective-permute-done | bytes 786464 | tf_op jit(solution)/shard_map/ppermute | solution.py:79
  321.7 9.1 collective-permute-done.30.refs_2_
  335.9 5.2 collective-permute-done.32.refs_1_
  347.4 5.8 permute.8
  353.2 5.9 permute.7
  359.6 9.3 assemble.11
  368.9 19.1 %fusion.84 = f32[1024,3072]{1,0:T(8,128)} fusion(bf16[1024,2048]{1,0:T(8,128)(2,1)} %all-gather.16.cloned.1.call-done, bf16[2048,3072]{1,0:T(8,128)(2,1)} %assemble.11), kind=kOutput, calls=%fused_computation.265 | convolution fusion | flops 12884901888 | bytes 29360128 | tf_op jit(solution)/shard_map/dot_general | solution.py:24
  388.1 16.0 %fusion.6 = (bf16[1024,1536]{1,0:T(8,128)(2,1)S(1)}, bf16[1024,1536]{1,0:T(8,128)(2,1)S(1)}, bf16[1024,1536]{1,0:T(8,128)(2,1)}) fusion(f32[1024,3072]{1,0:T(8,128)} %fusion.84, bf16[1024,2048]{1,0:T(8,128)(2,1)S(1)} %copy-done.40, bf16[2048,1536]{1,0:T(8,128)(2,1)} %assemble.13), kind=kOutput, calls=%fused_computation.15 | convolution fusion | flops 6483345408 | bytes 32505856 | tf_op jit(solution)/shard_map/dot_general | solution.py:24
  405.8 17.5 %convolution_convert_fusion.7.refs_1_ = bf16[1024,2048]{1,0:T(8,128)(2,1)} fusion(bf16[2048,3072]{1,0:T(8,128)(2,1)} %assemble.11, bf16[1024,1536]{1,0:T(8,128)(2,1)S(1)} %get-tuple-element.203, bf16[1024,1536]{1,0:T(8,128)(2,1)S(1)} %get-tuple-element.202), kind=kOutput, calls=%fused_computation.72 | convolution fusion | flops 12899581952 | bytes 23068672 | tf_op jit(solution)/shard_map/dot_general | solution.py:24
  423.6 23.9 %all-gather.18.cloned.1.call-done.refs_0_ = bf16[1024,2048]{1,0:T(8,128)(2,1)} async-done(((bf16[256,2048]{1,0:T(8,128)(2,1)}), bf16[1024,2048]{1,0:T(8,128)(2,1)}) %all-gather.18.cloned.1.call-update) | async-done | bytes 4194320 | tf_op jit(solution)/shard_map/all_gather | solution.py:629
  447.5 19.1 %fusion.85 = f32[1024,3072]{1,0:T(8,128)} fusion(bf16[1024,2048]{1,0:T(8,128)(2,1)} %fence.42, bf16[2048,3072]{1,0:T(8,128)(2,1)} %assemble.11), kind=kOutput, calls=%fused_computation.266 | convolution fusion | flops 12884901888 | bytes 29360128 | tf_op jit(solution)/shard_map/dot_general | solution.py:24
  466.7 15.4 %fusion.13 = (bf16[1024,1536]{1,0:T(8,128)(2,1)}, bf16[1024,1536]{1,0:T(8,128)(2,1)}, bf16[1024,1536]{1,0:T(8,128)(2,1)}) fusion(f32[1024,3072]{1,0:T(8,128)} %fusion.85, bf16[1024,2048]{1,0:T(8,128)(2,1)S(1)} %copy-done.38, bf16[2048,1536]{1,0:T(8,128)(2,1)S(1)} %bitcast.192), kind=kOutput, calls=%fused_computation.22 | convolution fusion | flops 6483345408 | bytes 32505856 | tf_op jit(solution)/shard_map/dot_general | solution.py:24
  482.1 5.6 pad_maximum_fusion.refs_1_
  487.7 18.7 %convolution_convert_fusion.6.refs_2_ = bf16[1024,2048]{1,0:T(8,128)(2,1)} fusion(bf16[2048,3072]{1,0:T(8,128)(2,1)} %assemble.11, bf16[1024,1536]{1,0:T(8,128)(2,1)} %get-tuple-element.201, bf16[1024,1536]{1,0:T(8,128)(2,1)S(1)} %copy-done.64), kind=kOutput, calls=%fused_computation.71 | convolution fusion | flops 12899581952 | bytes 23068672 | tf_op jit(solution)/shard_map/dot_general | solution.py:24
  508.3 5.7 pad_maximum_fusion.1.refs_1_
  514.0 7.4 fusion.37
  521.4 8.4 convolution_convert_fusion.9.refs_6_.refs_0_
  529.9 9.7 add_convert_fusion.2
  539.6 9.7 fusion.31
  549.3 11.8 %add_convert_fusion = bf16[1024,3072]{1,0:T(8,128)(2,1)} fusion(f32[1024,3072]{1,0:T(8,128)} %fusion.31, bf16[1024,3072]{1,0:T(8,128)(2,1)S(1)} %bitcast.178, bf16[1024,2048]{1,0:T(8,128)(2,1)S(1)} %copy-done.56), kind=kOutput, calls=%fused_computation.2 | convolution fusion | flops 6448742400 | bytes 27262976 | tf_op jit(solution)/shard_map/dot_general | solution.py:24
  561.6 11.0 fusion.34
  572.6 11.2 convolution_convert_fusion.8.refs_7_.refs_1_
  583.9 5.4 fusion.40
  589.3 7.1 add_convert_fusion.3
  596.3 10.2 add_convert_fusion.1
  629.6 5.7 fusion.52
  640.5 17.1 %back_scan.1 = (f32[512,2560]{1,0:T(8,128)}, f32[512,2560]{1,0:T(8,128)}, f32[8,2560]{1,0:T(8,128)}, bf16[512,2560]{1,0:T(8,128)(2,1)}) custom-call(s32[1]{0:T(128)} %sub.38.live_ref, f32[512,2560]{1,0:T(8,128)} %get-tuple-element.272.refs_2_.pre_ref, f32[512,2560]{1,0:T(8,128)} %convolution_add_fusion.1.grad_ref, f32[512,2560]{1,0:T(8,128)} %get-tuple-element.84.decay_ref, ...), custom_call_target="tpu_custom_call" | custom-call | flops 1024 | bytes 1024 | tf_op jit(solution)/shard_map/back_scan/pallas_call | solution.py:493
  662.6 10.9 collective-permute-done.38.refs_4_
  675.3 26.3 %recurrence_back.1 = (f32[528,2560]{1,0:T(8,128)}, f32[8,2560]{1,0:T(8,128)}, bf16[4,160,1280]{2,1,0:T(8,128)(2,1)}) custom-call(s32[1]{0:T(128)} %sub.38.live_ref, f32[528,2560]{1,0:T(8,128)} %convolution_add_fusion.pre_ref, f32[8,2560]{1,0:T(8,128)} %pad_maximum_fusion.14.par_ref, bf16[8,4,80,640]{3,2,1,0:T(8,128)(2,1)} %copy-done.21, ...), custom_call_target="tpu_custom_call" | custom-call | flops 1024 | bytes 1024 | tf_op jit(solution)/shard_map/recurrence_back/pallas_call | solution.py:493
  704.6 7.6 fusion.86
  712.2 6.8 fusion.87
  723.1 5.8 fusion.88
  729.0 5.0 fusion.89
  736.6 6.1 add_convert_fusion.4.in_ref
  747.9 6.6 convolution_convert_fusion.5
  756.0 7.4 collective-permute-done.43.refs_2_
  763.4 7.5 convolution_convert_fusion.3
  771.3 6.0 convolution_convert_fusion
  777.7 7.4 convolution_convert_fusion.2
  815.4 16.6 %collective-permute-done.46.refs_3_ = bf16[256,2560]{1,0:T(8,128)(2,1)S(1)} collective-permute-done((bf16[256,2560]{1,0:T(8,128)(2,1)S(1)}, bf16[256,2560]{1,0:T(8,128)(2,1)S(1)}, u32[]{:S(2)}, u32[]{:S(2)}) %collective-permute-start.46) | collective-permute-done | bytes 1310752 | tf_op jit(solution)/shard_map/ppermute | solution.py:79
  843.8 15.1 %all-gather.22.cloned.1.call-done = bf16[1024,2048]{1,0:T(8,128)(2,1)} async-done(((bf16[256,2048]{1,0:T(8,128)(2,1)}), bf16[1024,2048]{1,0:T(8,128)(2,1)}) %all-gather.22.cloned.1.call-update) | async-done | bytes 4194320 | tf_op jit(solution)/shard_map/all_gather | solution.py:703
  859.0 4.9 collective-permute-done.47.refs_3_
  875.5 8.5 collective-permute-done.49
  888.6 9.5 collective-permute-done.51
  902.7 21.1 %collective-permute-done.54.refs_3_ = bf16[256,2560]{1,0:T(8,128)(2,1)S(1)} collective-permute-done((bf16[256,2560]{1,0:T(8,128)(2,1)}, bf16[256,2560]{1,0:T(8,128)(2,1)S(1)}, u32[]{:S(2)}, u32[]{:S(2)}) %collective-permute-start.54) | collective-permute-done | bytes 1310752 | tf_op jit(solution)/shard_map/ppermute | solution.py:79
  964.5 33.2 %collective-permute-done.58.refs_0_.refs_3_ = bf16[3,256,640]{2,1,0:T(8,128)(2,1)S(1)} collective-permute-done((bf16[3,256,640]{2,1,0:T(8,128)(2,1)S(1)}, bf16[3,256,640]{2,1,0:T(8,128)(2,1)S(1)}, u32[]{:S(2)}, u32[]{:S(2)}) %collective-permute-start.58) | collective-permute-done | bytes 983072 | tf_op jit(solution)/shard_map/ppermute | solution.py:189
  1040.8 7.5 collective-permute-done.64
  1049.8 7.4 collective-permute-done.65
  1060.4 7.1 interleave.3
  1086.7 60.1 %collective-permute-done.63.refs_3_ = bf16[3,256,640]{2,1,0:T(8,128)(2,1)S(1)} collective-permute-done((bf16[3,256,640]{2,1,0:T(8,128)(2,1)}, bf16[3,256,640]{2,1,0:T(8,128)(2,1)S(1)}, u32[]{:S(2)}, u32[]{:S(2)}) %collective-permute-start.63) | collective-permute-done | bytes 983072 | tf_op jit(solution)/shard_map/ppermute | solution.py:190
  1151.2 13.9 %all-gather.26.cloned.1.call-done = bf16[1024,2048]{1,0:T(8,128)(2,1)} async-done(((bf16[256,2048]{1,0:T(8,128)(2,1)}), bf16[1024,2048]{1,0:T(8,128)(2,1)}) %all-gather.26.cloned.1.call-update) | async-done | bytes 4194320 | tf_op jit(solution)/shard_map/all_gather | solution.py:715
  1165.1 7.0 interleave.2
  (656 shorter events, 400.1 us)
Async XLA Ops:
  7.2 48.5 %all-gather.14.cloned.1.call-start = ((), (), s32[]{:S(2)}) async-start(), calls=%async_computation.4 | async-start | bytes 2150400 | tf_op jit(solution)/shard_map/all_gather | solution.py:566
  12.0 102.1 %all-gather.20.cloned.1.call-start = ((), (), s32[]{:S(2)}) async-start(), calls=%async_computation.11 | async-start | bytes 3276800 | tf_op jit(solution)/shard_map/all_gather | solution.py:567
  15.5 38.7 %collective-permute-start.1 = (bf16[256,3072]{1,0:T(8,128)(2,1)}, bf16[256,3072]{1,0:T(8,128)(2,1)S(1)}, u32[]{:S(2)}, u32[]{:S(2)}) collective-permute-start(bf16[256,3072]{1,0:T(8,128)(2,1)} %pad_maximum_fusion.8.refs_0_), channel_id=1, source_target_pairs={{0,16},{4,20},{8,24},{12,28},{16,0},{20,4},{24,8},{28,12},{1,17},{... | collective-permute-start | bytes 4718600 | tf_op jit(solution)/shard_map/ppermute | solution.py:79
  19.6 36.1 %collective-permute-start = (bf16[256,3072]{1,0:T(8,128)(2,1)}, bf16[256,3072]{1,0:T(8,128)(2,1)S(1)}, u32[]{:S(2)}, u32[]{:S(2)}) collective-permute-start(bf16[256,3072]{1,0:T(8,128)(2,1)} %pad_maximum_fusion.8.refs_0_), channel_id=1, source_target_pairs={{0,8},{4,12},{8,0},{12,4},{16,24},{20,28},{24,16},{28,20},{1,9},{5... | collective-permute-start | bytes 4718600 | tf_op jit(solution)/shard_map/ppermute | solution.py:79
  56.9 312.0 %all-gather.16.cloned.1.call-start = ((), (), s32[]{:S(2)}) async-start(), calls=%async_computation.5 | async-start | bytes 5242880 | tf_op jit(solution)/shard_map/all_gather | solution.py:629
  58.5 31.8 %collective-permute-start.9 = (bf16[256,2560]{1,0:T(8,128)(2,1)S(1)}, bf16[256,2560]{1,0:T(8,128)(2,1)S(1)}, u32[]{:S(2)}, u32[]{:S(2)}) collective-permute-start(bf16[256,2560]{1,0:T(8,128)(2,1)S(1)} %bitcast.197), channel_id=1, source_target_pairs={{0,16},{4,20},{8,24},{12,28},{16,0},{20,4},{24,8},{28,12},{1,17},{... | collective-permute-start | bytes 3932168 | tf_op jit(solution)/shard_map/ppermute | solution.py:79
  59.4 32.5 %collective-permute-start.7 = (bf16[256,2560]{1,0:T(8,128)(2,1)S(1)}, bf16[256,2560]{1,0:T(8,128)(2,1)S(1)}, u32[]{:S(2)}, u32[]{:S(2)}) collective-permute-start(bf16[256,2560]{1,0:T(8,128)(2,1)S(1)} %bitcast.198), channel_id=1, source_target_pairs={{0,8},{4,12},{8,0},{12,4},{16,24},{20,28},{24,16},{28,20},{1,9},{5... | collective-permute-start | bytes 3932168 | tf_op jit(solution)/shard_map/ppermute | solution.py:79
  61.0 38.6 %collective-permute-start.4 = (bf16[320,640]{1,0:T(8,128)(2,1)S(1)}, bf16[320,640]{1,0:T(8,128)(2,1)S(1)}, u32[]{:S(2)}, u32[]{:S(2)}) collective-permute-start(bf16[320,640]{1,0:T(8,128)(2,1)S(1)} %bitcast.210), channel_id=1, source_target_pairs={{0,16},{4,20},{8,24},{12,28},{16,0},{20,4},{24,8},{28,12},{1,17},{... | collective-permute-start | bytes 1228808 | tf_op jit(solution)/shard_map/ppermute | solution.py:79
  62.3 39.1 %collective-permute-start.2 = (bf16[320,640]{1,0:T(8,128)(2,1)S(1)}, bf16[320,640]{1,0:T(8,128)(2,1)S(1)}, u32[]{:S(2)}, u32[]{:S(2)}) collective-permute-start(bf16[320,640]{1,0:T(8,128)(2,1)S(1)} %bitcast.211), channel_id=1, source_target_pairs={{0,8},{4,12},{8,0},{12,4},{16,24},{20,28},{24,16},{28,20},{1,9},{5... | collective-permute-start | bytes 1228808 | tf_op jit(solution)/shard_map/ppermute | solution.py:79
  90.4 23.7 %collective-permute-start.10 = (bf16[128,2560]{1,0:T(8,128)(2,1)S(1)}, bf16[128,2560]{1,0:T(8,128)(2,1)}, u32[]{:S(2)}, u32[]{:S(2)}) collective-permute-start(bf16[128,2560]{1,0:T(8,128)(2,1)S(1)} %slice.720), channel_id=1, source_target_pairs={{0,8},{4,12},{8,0},{12,4},{16,24},{20,28},{24,16},{28,20},{1,9},{5... | collective-permute-start | bytes 1966088 | tf_op jit(solution)/shard_map/ppermute | solution.py:79
  93.0 21.0 %collective-permute-start.8 = (bf16[128,2560]{1,0:T(8,128)(2,1)S(1)}, bf16[128,2560]{1,0:T(8,128)(2,1)}, u32[]{:S(2)}, u32[]{:S(2)}) collective-permute-start(bf16[128,2560]{1,0:T(8,128)(2,1)S(1)} %slice.719), channel_id=1, source_target_pairs={{0,16},{4,20},{8,24},{12,28},{16,0},{20,4},{24,8},{28,12},{1,17},{... | collective-permute-start | bytes 1966088 | tf_op jit(solution)/shard_map/ppermute | solution.py:79
  100.3 19.1 %collective-permute-start.5 = (bf16[160,640]{1,0:T(8,128)(2,1)}, bf16[160,640]{1,0:T(8,128)(2,1)}, u32[]{:S(2)}, u32[]{:S(2)}) collective-permute-start(bf16[160,640]{1,0:T(8,128)(2,1)} %slice.711), channel_id=1, source_target_pairs={{0,8},{4,12},{8,0},{12,4},{16,24},{20,28},{24,16},{28,20},{1,9},{5... | collective-permute-start | bytes 614408 | tf_op jit(solution)/shard_map/ppermute | solution.py:79
  102.9 15.6 %collective-permute-start.3 = (bf16[160,640]{1,0:T(8,128)(2,1)}, bf16[160,640]{1,0:T(8,128)(2,1)}, u32[]{:S(2)}, u32[]{:S(2)}) collective-permute-start(bf16[160,640]{1,0:T(8,128)(2,1)} %slice.710), channel_id=1, source_target_pairs={{0,16},{4,20},{8,24},{12,28},{16,0},{20,4},{24,8},{28,12},{1,17},{... | collective-permute-start | bytes 614408 | tf_op jit(solution)/shard_map/ppermute | solution.py:79
  118.4 24.4 %collective-permute-start.13 = (bf16[1024,2560]{1,0:T(8,128)(2,1)}, bf16[1024,2560]{1,0:T(8,128)(2,1)}, u32[]{:S(2)}, u32[]{:S(2)}) collective-permute-start(bf16[1024,2560]{1,0:T(8,128)(2,1)} %assemble.7), channel_id=1, source_target_pairs={{0,4},{4,0},{8,12},{12,8},{16,20},{20,16},{24,28},{28,24},{1,5},{5... | collective-permute-start | bytes 15728648 | tf_op jit(solution)/shard_map/ppermute | solution.py:79
  140.5 35.8 %collective-permute-start.12 = (bf16[256,2560]{1,0:T(8,128)(2,1)}, bf16[256,2560]{1,0:T(8,128)(2,1)S(1)}, u32[]{:S(2)}, u32[]{:S(2)}) collective-permute-start(bf16[256,2560]{1,0:T(8,128)(2,1)} %fence.35.refs_0_), channel_id=1, source_target_pairs={{0,16},{4,20},{8,24},{12,28},{16,0},{20,4},{24,8},{28,12},{1,17},{... | collective-permute-start | bytes 3932168 | tf_op jit(solution)/shard_map/ppermute | solution.py:79
  141.3 34.9 %collective-permute-start.11 = (bf16[256,2560]{1,0:T(8,128)(2,1)}, bf16[256,2560]{1,0:T(8,128)(2,1)S(1)}, u32[]{:S(2)}, u32[]{:S(2)}) collective-permute-start(bf16[256,2560]{1,0:T(8,128)(2,1)} %fence.35.refs_0_), channel_id=1, source_target_pairs={{0,8},{4,12},{8,0},{12,4},{16,24},{20,28},{24,16},{28,20},{1,9},{5... | collective-permute-start | bytes 3932168 | tf_op jit(solution)/shard_map/ppermute | solution.py:79
  180.7 16.3 %collective-permute-start.14 = (bf16[128,2560]{1,0:T(8,128)(2,1)S(1)}, bf16[128,2560]{1,0:T(8,128)(2,1)S(1)}, u32[]{:S(2)}, u32[]{:S(2)}) collective-permute-start(bf16[128,2560]{1,0:T(8,128)(2,1)S(1)} %slice.549), channel_id=1, source_target_pairs={{0,8},{4,12},{8,0},{12,4},{16,24},{20,28},{24,16},{28,20},{1,9},{5... | collective-permute-start | bytes 1966088 | tf_op jit(solution)/shard_map/ppermute | solution.py:79
  181.3 15.9 %collective-permute-start.15 = (bf16[128,2560]{1,0:T(8,128)(2,1)S(1)}, bf16[128,2560]{1,0:T(8,128)(2,1)S(1)}, u32[]{:S(2)}, u32[]{:S(2)}) collective-permute-start(bf16[128,2560]{1,0:T(8,128)(2,1)S(1)} %slice.550), channel_id=1, source_target_pairs={{0,16},{4,20},{8,24},{12,28},{16,0},{20,4},{24,8},{28,12},{1,17},{... | collective-permute-start | bytes 1966088 | tf_op jit(solution)/shard_map/ppermute | solution.py:79
  205.1 31.4 %collective-permute-start.21 = (bf16[256,2560]{1,0:T(8,128)(2,1)}, bf16[256,2560]{1,0:T(8,128)(2,1)S(1)}, u32[]{:S(2)}, u32[]{:S(2)}) collective-permute-start(bf16[256,2560]{1,0:T(8,128)(2,1)} %fence.37.refs_0_), channel_id=1, source_target_pairs={{0,16},{4,20},{8,24},{12,28},{16,0},{20,4},{24,8},{28,12},{1,17},{... | collective-permute-start | bytes 3932168 | tf_op jit(solution)/shard_map/ppermute | solution.py:79
  206.3 31.1 %collective-permute-start.20 = (bf16[256,2560]{1,0:T(8,128)(2,1)}, bf16[256,2560]{1,0:T(8,128)(2,1)S(1)}, u32[]{:S(2)}, u32[]{:S(2)}) collective-permute-start(bf16[256,2560]{1,0:T(8,128)(2,1)} %fence.37.refs_0_), channel_id=1, source_target_pairs={{0,8},{4,12},{8,0},{12,4},{16,24},{20,28},{24,16},{28,20},{1,9},{5... | collective-permute-start | bytes 3932168 | tf_op jit(solution)/shard_map/ppermute | solution.py:79
  240.7 16.1 %collective-permute-start.22 = (bf16[128,2560]{1,0:T(8,128)(2,1)S(1)}, bf16[128,2560]{1,0:T(8,128)(2,1)S(1)}, u32[]{:S(2)}, u32[]{:S(2)}) collective-permute-start(bf16[128,2560]{1,0:T(8,128)(2,1)S(1)} %slice.559), channel_id=1, source_target_pairs={{0,8},{4,12},{8,0},{12,4},{16,24},{20,28},{24,16},{28,20},{1,9},{5... | collective-permute-start | bytes 1966088 | tf_op jit(solution)/shard_map/ppermute | solution.py:79
  241.7 15.7 %collective-permute-start.23 = (bf16[128,2560]{1,0:T(8,128)(2,1)S(1)}, bf16[128,2560]{1,0:T(8,128)(2,1)S(1)}, u32[]{:S(2)}, u32[]{:S(2)}) collective-permute-start(bf16[128,2560]{1,0:T(8,128)(2,1)S(1)} %slice.560), channel_id=1, source_target_pairs={{0,16},{4,20},{8,24},{12,28},{16,0},{20,4},{24,8},{28,12},{1,17},{... | collective-permute-start | bytes 1966088 | tf_op jit(solution)/shard_map/ppermute | solution.py:79
  269.8 20.1 %collective-permute-start.25 = (bf16[128,3072]{1,0:T(8,128)(2,1)}, bf16[128,3072]{1,0:T(8,128)(2,1)S(1)}, u32[]{:S(2)}, u32[]{:S(2)}) collective-permute-start(bf16[128,3072]{1,0:T(8,128)(2,1)} %slice.564), channel_id=1, source_target_pairs={{0,8},{4,12},{8,0},{12,4},{16,24},{20,28},{24,16},{28,20},{1,9},{5... | collective-permute-start | bytes 2359304 | tf_op jit(solution)/shard_map/ppermute | solution.py:79
  270.9 20.0 %collective-permute-start.26 = (bf16[128,3072]{1,0:T(8,128)(2,1)}, bf16[128,3072]{1,0:T(8,128)(2,1)}, u32[]{:S(2)}, u32[]{:S(2)}) collective-permute-start(bf16[128,3072]{1,0:T(8,128)(2,1)} %slice.565), channel_id=1, source_target_pairs={{0,16},{4,20},{8,24},{12,28},{16,0},{20,4},{24,8},{28,12},{1,17},{... | collective-permute-start | bytes 2359304 | tf_op jit(solution)/shard_map/ppermute | solution.py:79
  285.9 161.6 %all-gather.18.cloned.1.call-start = ((), (), s32[]{:S(2)}) async-start(), calls=%async_computation.6 | async-start | bytes 5242880 | tf_op jit(solution)/shard_map/all_gather | solution.py:629
  297.0 62.6 %collective-permute-start.27 = (bf16[1024,3072]{1,0:T(8,128)(2,1)}, bf16[1024,3072]{1,0:T(8,128)(2,1)}, u32[]{:S(2)}, u32[]{:S(2)}) collective-permute-start(bf16[1024,3072]{1,0:T(8,128)(2,1)} %assemble.10.refs_0_), channel_id=1, source_target_pairs={{0,4},{4,0},{8,12},{12,8},{16,20},{20,16},{24,28},{28,24},{1,5},{5... | collective-permute-start | bytes 18874376 | tf_op jit(solution)/shard_map/ppermute | solution.py:79
  299.7 20.1 %collective-permute-start.29 = (bf16[256,1536]{1,0:T(8,128)(2,1)}, bf16[256,1536]{1,0:T(8,128)(2,1)S(1)}, u32[]{:S(2)}, u32[]{:S(2)}) collective-permute-start(bf16[256,1536]{1,0:T(8,128)(2,1)} %fence.41.refs_0_), channel_id=1, source_target_pairs={{0,16},{4,20},{8,24},{12,28},{16,0},{20,4},{24,8},{28,12},{1,17},{... | collective-permute-start | bytes 2359304 | tf_op jit(solution)/shard_map/ppermute | solution.py:79
  300.3 20.1 %collective-permute-start.28 = (bf16[256,1536]{1,0:T(8,128)(2,1)}, bf16[256,1536]{1,0:T(8,128)(2,1)S(1)}, u32[]{:S(2)}, u32[]{:S(2)}) collective-permute-start(bf16[256,1536]{1,0:T(8,128)(2,1)} %fence.41.refs_0_), channel_id=1, source_target_pairs={{0,8},{4,12},{8,0},{12,4},{16,24},{20,28},{24,16},{28,20},{1,9},{5... | collective-permute-start | bytes 2359304 | tf_op jit(solution)/shard_map/ppermute | solution.py:79
  359.1 258.0 %reduce-scatter.5.cloned.1.call-start = ((), (), s32[]{:S(2)}) async-start(), calls=%async_computation.7 | async-start | bytes 5242880 | tf_op jit(solution)/shard_map/reduce_scatter | solution.py:638
  423.3 193.8 %reduce-scatter.7.cloned.1.call-start = ((), (), s32[]{:S(2)}) async-start(), calls=%async_computation.8 | async-start | bytes 5242880 | tf_op jit(solution)/shard_map/reduce_scatter | solution.py:638
  529.8 189.6 %reduce-scatter.9.cloned.1.call-start = ((), (), s32[]{:S(2)}) async-start(), calls=%async_computation.9 | async-start | bytes 5242880 | tf_op jit(solution)/shard_map/reduce_scatter | solution.py:663
  539.6 66.9 %collective-permute-start.33 = (bf16[1024,1536]{1,0:T(8,128)(2,1)}, bf16[1024,1536]{1,0:T(8,128)(2,1)S(1)}, u32[]{:S(2)}, u32[]{:S(2)}) collective-permute-start(bf16[1024,1536]{1,0:T(8,128)(2,1)} %add_convert_fusion.2), channel_id=1, source_target_pairs={{0,4},{4,0},{8,12},{12,8},{16,20},{20,16},{24,28},{28,24},{1,5},{5... | collective-permute-start | bytes 9437192 | tf_op jit(solution)/shard_map/ppermute | solution.py:79
  561.1 51.2 %collective-permute-start.34 = (bf16[1024,3072]{1,0:T(8,128)(2,1)}, bf16[1024,3072]{1,0:T(8,128)(2,1)}, u32[]{:S(2)}, u32[]{:S(2)}) collective-permute-start(bf16[1024,3072]{1,0:T(8,128)(2,1)} %add_convert_fusion), channel_id=1, source_target_pairs={{0,4},{4,0},{8,12},{12,8},{16,20},{20,16},{24,28},{28,24},{1,5},{5... | collective-permute-start | bytes 18874376 | tf_op jit(solution)/shard_map/ppermute | solution.py:79
  617.2 167.9 %reduce-scatter.11.cloned.1.call-start = ((), (), s32[]{:S(2)}) async-start(), calls=%async_computation.10 | async-start | bytes 5242880 | tf_op jit(solution)/shard_map/reduce_scatter | solution.py:663
  620.1 39.8 %collective-permute-start.36 = (bf16[256,1536]{1,0:T(8,128)(2,1)}, bf16[256,1536]{1,0:T(8,128)(2,1)}, u32[]{:S(2)}, u32[]{:S(2)}) collective-permute-start(bf16[256,1536]{1,0:T(8,128)(2,1)} %get-tuple-element.234.refs_3_), channel_id=1, source_target_pairs={{0,16},{4,20},{8,24},{12,28},{16,0},{20,4},{24,8},{28,12},{1,17},{... | collective-permute-start | bytes 2359304 | tf_op jit(solution)/shard_map/ppermute | solution.py:79
  621.5 39.7 %collective-permute-start.35 = (bf16[256,1536]{1,0:T(8,128)(2,1)}, bf16[256,1536]{1,0:T(8,128)(2,1)}, u32[]{:S(2)}, u32[]{:S(2)}) collective-permute-start(bf16[256,1536]{1,0:T(8,128)(2,1)} %get-tuple-element.235.refs_2_), channel_id=1, source_target_pairs={{0,8},{4,12},{8,0},{12,4},{16,24},{20,28},{24,16},{28,20},{1,9},{5... | collective-permute-start | bytes 2359304 | tf_op jit(solution)/shard_map/ppermute | solution.py:79
  623.0 50.5 %collective-permute-start.38 = (bf16[256,3072]{1,0:T(8,128)(2,1)}, bf16[256,3072]{1,0:T(8,128)(2,1)}, u32[]{:S(2)}, u32[]{:S(2)}) collective-permute-start(bf16[256,3072]{1,0:T(8,128)(2,1)} %get-tuple-element.208.refs_5_), channel_id=1, source_target_pairs={{0,16},{4,20},{8,24},{12,28},{16,0},{20,4},{24,8},{28,12},{1,17},{... | collective-permute-start | bytes 4718600 | tf_op jit(solution)/shard_map/ppermute | solution.py:79
  623.5 51.1 %collective-permute-start.37 = (bf16[256,3072]{1,0:T(8,128)(2,1)}, bf16[256,3072]{1,0:T(8,128)(2,1)}, u32[]{:S(2)}, u32[]{:S(2)}) collective-permute-start(bf16[256,3072]{1,0:T(8,128)(2,1)} %get-tuple-element.209.refs_4_), channel_id=1, source_target_pairs={{0,8},{4,12},{8,0},{12,4},{16,24},{20,28},{24,16},{28,20},{1,9},{5... | collective-permute-start | bytes 4718600 | tf_op jit(solution)/shard_map/ppermute | solution.py:79
  626.0 233.0 %all-gather.22.cloned.1.call-start = ((), (), s32[]{:S(2)}) async-start(), calls=%async_computation.12 | async-start | bytes 5242880 | tf_op jit(solution)/shard_map/all_gather | solution.py:703
  658.5 16.1 %collective-permute-start.41 = (f32[2,2560]{1,0:T(2,128)S(1)}, f32[2,2560]{1,0:T(2,128)S(1)}, u32[]{:S(2)}, u32[]{:S(2)}) collective-permute-start(f32[2,2560]{1,0:T(2,128)S(1)} %pad_maximum_fusion.16), channel_id=1, source_target_pairs={{3,0},{7,4},{11,8},{15,12},{19,16},{23,20},{27,24},{31,28}} | collective-permute-start | bytes 61448 | tf_op jit(solution)/shard_map/ppermute | solution.py:162
  702.6 16.8 %collective-permute-start.42 = (f32[16,2560]{1,0:T(8,128)S(1)}, f32[16,2560]{1,0:T(8,128)S(1)}, u32[]{:S(2)}, u32[]{:S(2)}) collective-permute-start(f32[16,2560]{1,0:T(8,128)S(1)} %slice.600), channel_id=1, source_target_pairs={{1,0},{2,1},{3,2},{5,4},{6,5},{7,6},{9,8},{10,9},{11,10},{13,12},{... | collective-permute-start | bytes 491528 | tf_op jit(solution)/shard_map/ppermute | solution.py:162
  756.0 208.5 %all-gather.28.cloned.1.call-start = ((), (), s32[]{:S(2)}) async-start(), calls=%async_computation.15 | async-start | bytes 5242880 | tf_op jit(solution)/shard_map/all_gather | solution.py:703
  770.9 40.6 %collective-permute-start.44 = (bf16[1024,2560]{1,0:T(8,128)(2,1)}, bf16[1024,2560]{1,0:T(8,128)(2,1)}, u32[]{:S(2)}, u32[]{:S(2)}) collective-permute-start(bf16[1024,2560]{1,0:T(8,128)(2,1)} %convolution_convert_fusion.3), channel_id=1, source_target_pairs={{0,4},{4,0},{8,12},{12,8},{16,20},{20,16},{24,28},{28,24},{1,5},{5... | collective-permute-start | bytes 15728648 | tf_op jit(solution)/shard_map/ppermute | solution.py:79
  771.1 301.9 %all-gather.24.cloned.1.call-start = ((), (), s32[]{:S(2)}) async-start(), calls=%async_computation.13 | async-start | bytes 5242880 | tf_op jit(solution)/shard_map/all_gather | solution.py:715
  777.3 62.6 %collective-permute-start.53 = (bf16[1024,2560]{1,0:T(8,128)(2,1)}, bf16[1024,2560]{1,0:T(8,128)(2,1)}, u32[]{:S(2)}, u32[]{:S(2)}) collective-permute-start(bf16[1024,2560]{1,0:T(8,128)(2,1)} %convolution_convert_fusion), channel_id=1, source_target_pairs={{0,4},{4,0},{8,12},{12,8},{16,20},{20,16},{24,28},{28,24},{1,5},{5... | collective-permute-start | bytes 15728648 | tf_op jit(solution)/shard_map/ppermute | solution.py:79
  801.1 30.9 %collective-permute-start.46 = (bf16[256,2560]{1,0:T(8,128)(2,1)S(1)}, bf16[256,2560]{1,0:T(8,128)(2,1)S(1)}, u32[]{:S(2)}, u32[]{:S(2)}) collective-permute-start(bf16[256,2560]{1,0:T(8,128)(2,1)S(1)} %get-tuple-element.226), channel_id=1, source_target_pairs={{0,16},{4,20},{8,24},{12,28},{16,0},{20,4},{24,8},{28,12},{1,17},{... | collective-permute-start | bytes 3932168 | tf_op jit(solution)/shard_map/ppermute | solution.py:79
  802.1 30.6 %collective-permute-start.45 = (bf16[256,2560]{1,0:T(8,128)(2,1)S(1)}, bf16[256,2560]{1,0:T(8,128)(2,1)S(1)}, u32[]{:S(2)}, u32[]{:S(2)}) collective-permute-start(bf16[256,2560]{1,0:T(8,128)(2,1)S(1)} %get-tuple-element.227), channel_id=1, source_target_pairs={{0,8},{4,12},{8,0},{12,4},{16,24},{20,28},{24,16},{28,20},{1,9},{5... | collective-permute-start | bytes 3932168 | tf_op jit(solution)/shard_map/ppermute | solution.py:79
  833.8 30.0 %collective-permute-start.47 = (bf16[256,2560]{1,0:T(8,128)(2,1)}, bf16[256,2560]{1,0:T(8,128)(2,1)S(1)}, u32[]{:S(2)}, u32[]{:S(2)}) collective-permute-start(bf16[256,2560]{1,0:T(8,128)(2,1)} %get-tuple-element.96), channel_id=1, source_target_pairs={{0,8},{4,12},{8,0},{12,4},{16,24},{20,28},{24,16},{28,20},{1,9},{5... | collective-permute-start | bytes 3932168 | tf_op jit(solution)/shard_map/ppermute | solution.py:79
  835.3 29.7 %collective-permute-start.48 = (bf16[256,2560]{1,0:T(8,128)(2,1)}, bf16[256,2560]{1,0:T(8,128)(2,1)S(1)}, u32[]{:S(2)}, u32[]{:S(2)}) collective-permute-start(bf16[256,2560]{1,0:T(8,128)(2,1)} %get-tuple-element.97), channel_id=1, source_target_pairs={{0,16},{4,20},{8,24},{12,28},{16,0},{20,4},{24,8},{28,12},{1,17},{... | collective-permute-start | bytes 3932168 | tf_op jit(solution)/shard_map/ppermute | solution.py:79
  866.1 17.9 %collective-permute-start.49 = (bf16[128,2560]{1,0:T(8,128)(2,1)}, bf16[128,2560]{1,0:T(8,128)(2,1)S(1)}, u32[]{:S(2)}, u32[]{:S(2)}) collective-permute-start(bf16[128,2560]{1,0:T(8,128)(2,1)} %get-tuple-element.100), channel_id=1, source_target_pairs={{0,8},{4,12},{8,0},{12,4},{16,24},{20,28},{24,16},{28,20},{1,9},{5... | collective-permute-start | bytes 1966088 | tf_op jit(solution)/shard_map/ppermute | solution.py:79
  866.8 18.0 %collective-permute-start.50 = (bf16[128,2560]{1,0:T(8,128)(2,1)}, bf16[128,2560]{1,0:T(8,128)(2,1)}, u32[]{:S(2)}, u32[]{:S(2)}) collective-permute-start(bf16[128,2560]{1,0:T(8,128)(2,1)} %get-tuple-element.101), channel_id=1, source_target_pairs={{0,16},{4,20},{8,24},{12,28},{16,0},{20,4},{24,8},{28,12},{1,17},{... | collective-permute-start | bytes 1966088 | tf_op jit(solution)/shard_map/ppermute | solution.py:79
  867.9 297.2 %all-gather.26.cloned.1.call-start = ((), (), s32[]{:S(2)}) async-start(), calls=%async_computation.14 | async-start | bytes 5242880 | tf_op jit(solution)/shard_map/all_gather | solution.py:715
  872.0 26.2 %collective-permute-start.51 = (bf16[128,2560]{1,0:T(8,128)(2,1)}, bf16[128,2560]{1,0:T(8,128)(2,1)}, u32[]{:S(2)}, u32[]{:S(2)}) collective-permute-start(bf16[128,2560]{1,0:T(8,128)(2,1)} %get-tuple-element.102), channel_id=1, source_target_pairs={{0,8},{4,12},{8,0},{12,4},{16,24},{20,28},{24,16},{28,20},{1,9},{5... | collective-permute-start | bytes 1966088 | tf_op jit(solution)/shard_map/ppermute | solution.py:79
  873.5 25.4 %collective-permute-start.52 = (bf16[128,2560]{1,0:T(8,128)(2,1)}, bf16[128,2560]{1,0:T(8,128)(2,1)}, u32[]{:S(2)}, u32[]{:S(2)}) collective-permute-start(bf16[128,2560]{1,0:T(8,128)(2,1)} %get-tuple-element.103), channel_id=1, source_target_pairs={{0,16},{4,20},{8,24},{12,28},{16,0},{20,4},{24,8},{28,12},{1,17},{... | collective-permute-start | bytes 1966088 | tf_op jit(solution)/shard_map/ppermute | solution.py:79
  874.6 49.1 %collective-permute-start.54 = (bf16[256,2560]{1,0:T(8,128)(2,1)}, bf16[256,2560]{1,0:T(8,128)(2,1)S(1)}, u32[]{:S(2)}, u32[]{:S(2)}) collective-permute-start(bf16[256,2560]{1,0:T(8,128)(2,1)} %get-tuple-element.105), channel_id=1, source_target_pairs={{0,16},{4,20},{8,24},{12,28},{16,0},{20,4},{24,8},{28,12},{1,17},{... | collective-permute-start | bytes 3932168 | tf_op jit(solution)/shard_map/ppermute | solution.py:79
  884.0 39.7 %collective-permute-start.55 = (bf16[256,2560]{1,0:T(8,128)(2,1)}, bf16[256,2560]{1,0:T(8,128)(2,1)S(1)}, u32[]{:S(2)}, u32[]{:S(2)}) collective-permute-start(bf16[256,2560]{1,0:T(8,128)(2,1)} %get-tuple-element.106), channel_id=1, source_target_pairs={{0,8},{4,12},{8,0},{12,4},{16,24},{20,28},{24,16},{28,20},{1,9},{5... | collective-permute-start | bytes 3932168 | tf_op jit(solution)/shard_map/ppermute | solution.py:79
  952.0 45.7 %collective-permute-start.58 = (bf16[3,256,640]{2,1,0:T(8,128)(2,1)S(1)}, bf16[3,256,640]{2,1,0:T(8,128)(2,1)S(1)}, u32[]{:S(2)}, u32[]{:S(2)}) collective-permute-start(bf16[3,256,640]{2,1,0:T(8,128)(2,1)S(1)} %get-tuple-element.241), channel_id=1, source_target_pairs={{0,1},{4,5},{8,9},{12,13},{16,17},{20,21},{24,25},{28,29}} | collective-permute-start | bytes 2949128 | tf_op jit(solution)/shard_map/ppermute | solution.py:189
  1007.9 25.5 %collective-permute-start.70 = (bf16[128,3072]{1,0:T(8,128)(2,1)}, bf16[128,3072]{1,0:T(8,128)(2,1)}, u32[]{:S(2)}, u32[]{:S(2)}) collective-permute-start(bf16[128,3072]{1,0:T(8,128)(2,1)} %get-tuple-element.121), channel_id=1, source_target_pairs={{0,8},{4,12},{8,0},{12,4},{16,24},{20,28},{24,16},{28,20},{1,9},{5... | collective-permute-start | bytes 2359304 | tf_op jit(solution)/shard_map/ppermute | solution.py:79
  1008.7 27.9 %collective-permute-start.71 = (bf16[128,3072]{1,0:T(8,128)(2,1)}, bf16[128,3072]{1,0:T(8,128)(2,1)}, u32[]{:S(2)}, u32[]{:S(2)}) collective-permute-start(bf16[128,3072]{1,0:T(8,128)(2,1)} %get-tuple-element.122), channel_id=1, source_target_pairs={{0,16},{4,20},{8,24},{12,28},{16,0},{20,4},{24,8},{28,12},{1,17},{... | collective-permute-start | bytes 2359304 | tf_op jit(solution)/shard_map/ppermute | solution.py:79
  1016.6 31.8 %collective-permute-start.64 = (bf16[4,4,26752]{2,1,0:T(4,128)(2,1)}, bf16[4,4,26752]{2,1,0:T(4,128)(2,1)S(1)}, u32[]{:S(2)}, u32[]{:S(2)}) collective-permute-start(bf16[4,4,26752]{2,1,0:T(4,128)(2,1)} %slice.821), channel_id=1, source_target_pairs={{0,16},{4,20},{8,24},{12,28},{16,0},{20,4},{24,8},{28,12},{1,17},{... | collective-permute-start | bytes 2568200 | tf_op jit(solution)/shard_map/ppermute | solution.py:79
  1020.8 52.2 %collective-permute-start.61 = (bf16[3,256,640]{2,1,0:T(8,128)(2,1)}, bf16[3,256,640]{2,1,0:T(8,128)(2,1)}, u32[]{:S(2)}, u32[]{:S(2)}) collective-permute-start(bf16[3,256,640]{2,1,0:T(8,128)(2,1)} %get-tuple-element.238), channel_id=1, source_target_pairs={{2,1},{3,2},{6,5},{7,6},{10,9},{11,10},{14,13},{15,14},{18,17},{19... | collective-permute-start | bytes 2949128 | tf_op jit(solution)/shard_map/ppermute | solution.py:190
  1022.4 37.1 %collective-permute-start.60 = (bf16[3,256,640]{2,1,0:T(8,128)(2,1)}, bf16[3,256,640]{2,1,0:T(8,128)(2,1)S(1)}, u32[]{:S(2)}, u32[]{:S(2)}) collective-permute-start(bf16[3,256,640]{2,1,0:T(8,128)(2,1)} %get-tuple-element.239), channel_id=1, source_target_pairs={{0,1},{1,2},{4,5},{5,6},{8,9},{9,10},{12,13},{13,14},{16,17},{17,1... | collective-permute-start | bytes 2949128 | tf_op jit(solution)/shard_map/ppermute | solution.py:189
  1077.2 69.5 %collective-permute-start.63 = (bf16[3,256,640]{2,1,0:T(8,128)(2,1)}, bf16[3,256,640]{2,1,0:T(8,128)(2,1)S(1)}, u32[]{:S(2)}, u32[]{:S(2)}) collective-permute-start(bf16[3,256,640]{2,1,0:T(8,128)(2,1)} %add_convert_fusion.13), channel_id=1, source_target_pairs={{1,0},{2,1},{3,2},{5,4},{6,5},{7,6},{9,8},{10,9},{11,10},{13,12},{... | collective-permute-start | bytes 2949128 | tf_op jit(solution)/shard_map/ppermute | solution.py:190
  1078.5 68.2 %collective-permute-start.62 = (bf16[3,256,640]{2,1,0:T(8,128)(2,1)S(1)}, bf16[3,256,640]{2,1,0:T(8,128)(2,1)S(1)}, u32[]{:S(2)}, u32[]{:S(2)}) collective-permute-start(bf16[3,256,640]{2,1,0:T(8,128)(2,1)S(1)} %add_convert_fusion.14), channel_id=1, source_target_pairs={{0,1},{1,2},{2,3},{4,5},{5,6},{6,7},{8,9},{9,10},{10,11},{12,13},{... | collective-permute-start | bytes 2949128 | tf_op jit(solution)/shard_map/ppermute | solution.py:189
  (159 other events, 1454.4 us)
Sparse Core Ops, SparseCore 0:
  12.1 43.3 all-gather.13
  57.6 54.7 all-gather.19
  286.0 80.6 all-gather.15
  368.2 79.2 all-gather.17
  449.6 75.2 reduce-scatter.4
  529.9 75.2 reduce-scatter.6
  617.3 76.6 reduce-scatter.8
  696.3 80.7 reduce-scatter.10
  778.7 80.2 all-gather.21
  860.4 79.2 all-gather.27
  941.3 110.7 all-gather.23
  1053.5 111.5 all-gather.25

commit v10 on v9

--- a/solution.py
+++ b/solution.py
@@ -75,8 +75,12 @@
     )(*pieces, *others)
 
 
+def swap(values, mask, size):
+    return lax.ppermute(values, "dp", [(k, k ^ mask) for k in range(size)])
+
+
 def exchange(values, bit, size):
-    return lax.ppermute(values, "dp", [(k, k ^ (1 << bit)) for k in range(size)])
+    return swap(values, 1 << bit, size)
 
 
 def squared(size, rows):
@@ -202,7 +206,7 @@
 
 def small_begin(own, size):
     if size == 8:
-        return [own, exchange(own, 1, size), exchange(own, 2, size)]
+        return [own] + [swap(own, mask, size) for mask in (2, 6, 4)]
     rows = own[None]
     for bit in range(1, size.bit_length() - 1):
         rows = jnp.concatenate([rows, exchange(rows, bit, size)])
@@ -211,10 +215,7 @@
 
 def small_end(some, size):
     if size == 8:
-        own, by_x, by_y = some
-        cut = own.shape[0] // 2
-        far = jnp.concatenate([exchange(by_x[:cut], 2, size), exchange(by_y[cut:], 1, size)])
-        rows = jnp.stack([own, by_x, far, by_y])
+        rows = jnp.stack(some)
     else:
         (rows,) = some
     return jnp.concatenate([rows, exchange(rows, 0, size)])
@@ -588,7 +589,7 @@
     row = jnp.where(row < part, spot * part + row, head)
     order = (jnp.arange(head)[:, None] == row[None, :]).astype(BF)
 
-    w_r, came_r = spread_end(some_r, size, (), (others, order))
+    w_r, came_r = spread_end(some_r, size, (), (z_gelu, order))
     first = (extended * first_rate * gain[0]).astype(BF)
     inputs, first_own, first_rate = extended[HALO:], first[HALO:], first_rate[HALO:]
     cut = d_model // 2
@@ -596,14 +597,16 @@
     keep = (rows, width, F32)
     dense = ((GROUP, 2 * GROUP), BF)
     some_g = spread_begin(z_gelu, size, *came_r)
-    rec_pre = wide_dot(first, w_r)
+    rec_pre = dot(first[:, :cut], w_r[0])
+    w_r[1:] = fence(w_r[1:], *some_g[1:], rec_pre)
+    rec_pre = rec_pre + dot(first[:, cut:], w_r[1])
     conv, decay, ig, dg, state, prod = kernel_call(
         forward_kernel, live_count, [rec_pre, par, lru, order], [keep] * 6,
         [((rows + HALO, GROUP), F32), dense], "recurrence",
     )
     ends = jnp.concatenate([prod[-1:], state[-1:]])
     came = [z_shift(ends, k, n, False) for k in range(1, n)]
-    w_g, came_g = spread_end(some_g, size, (ends,), came)
+    w_g, came_g = spread_end(some_g, size, (), came)
     carry = jnp.zeros((1, width), F32)
     for end in came[::-1]:
         carry = end[1:] + end[:1] * carry

time: 1190 us -> 1200 us (level)
  waiting for transfers between devices: 388 us -> 405 us
    all_gather x1, waiting for transfers between devices: 0.01 us -> 13.7 us  [on_device(): others = lax.all_gather(*fence([others], whole), 'tensor', axis=0)]
    ppermute x58 -> x57, starting transfers between devices: 52.5 us -> 50.6 us  [swap(): return lax.ppermute(values, 'dp', [(k, k ^ mask) for k in range(size)])]
    ppermute x58 -> x57, waiting for transfers between devices: 239 us -> 241 us  [swap(): return lax.ppermute(values, 'dp', [(k, k ^ mask) for k in range(size)])]
    unnamed x287 -> x293, local copies, waits for them, and re-layouts: 43.1 us -> 44.2 us
  transfers between devices with their start and end apart: 86 -> 85, of which waited for: 42 -> 45; matrix products, arithmetic and copies ran while one was open for 43% -> 43% of each run, Pallas kernels for 10% -> 10%
where the time goes in v10:
time: 1200 us; the launch traced here: 1190 us
  waiting for transfers between devices  405 us (34%)
  matrix products  308 us (26%)
  Pallas kernels  138 us (12%)
  other arithmetic  135 us (11%)
  local copies, waits for them, and re-layouts  100 us (8%)
  starting transfers between devices  89.5 us (7%)
  between operations  17.5 us (1%)
    dot_general x34, matrix products, dot(): lax.dot_general(left, right, (dims, ((), ())), preferred_element_type=F32)  308 us
    ppermute x57, waiting for transfers between devices, swap(): return lax.ppermute(values, 'dp', [(k, k ^ mask) for k in range(size)])  241 us
    convert_element_type x21, other arithmetic, add_all(): return total.astype(BF)  62.9 us
    pallas_call x3, Pallas kernels, kernel_call(): pl.pallas_call(body, grid_spec=pltpu.PrefetchScalarGridSpec(num_scalar_pr...  62.4 us
    ppermute x3, waiting for transfers between devices, go(): lax.ppermute(left, 'tensor', [(k, k - 1) for k in range(max(n - t, 1), n)])  58.2 us
    ppermute x57, starting transfers between devices, swap(): return lax.ppermute(values, 'dp', [(k, k ^ mask) for k in range(size)])  50.6 us
    unnamed x293, local copies, waits for them, and re-layouts  44.2 us
    pallas_call x7, Pallas kernels, assemble(): pl.pallas_call(body, in_specs=[place] * (count + len(others)), out_specs=...  35.7 us
  transfers between devices with their start and end apart: 85, of which 45 were waited for; matrix products, arithmetic and copies ran while one was open for 43% of the time, Pallas kernels for 10%

profile of v10, /device:TPU:0, one launch (start us, length us, event | category | flops | bytes accessed | tf_op | source)
XLA Modules:
  0.0 1193.6 jit_solution(17138941592243333203)
XLA Ops:
  37.5 16.7 %collective-permute-done.1.refs_2_.refs_1_ = bf16[256,3072]{1,0:T(8,128)(2,1)S(1)} collective-permute-done((bf16[256,3072]{1,0:T(8,128)(2,1)}, bf16[256,3072]{1,0:T(8,128)(2,1)S(1)}, u32[]{:S(2)}, u32[]{:S(2)}) %collective-permute-start.1) | collective-permute-done | bytes 1572896 | tf_op jit(solution)/shard_map/ppermute | solution.py:79
  66.3 21.7 %collective-permute-done.8.refs_4_ = bf16[256,2560]{1,0:T(8,128)(2,1)S(1)} collective-permute-done((bf16[256,2560]{1,0:T(8,128)(2,1)S(1)}, bf16[256,2560]{1,0:T(8,128)(2,1)S(1)}, u32[]{:S(2)}, u32[]{:S(2)}) %collective-permute-start.8) | collective-permute-done | bytes 1310752 | tf_op jit(solution)/shard_map/ppermute | solution.py:79
  98.6 13.7 %all-gather.20.cloned.1.call-done = bf16[2048,640]{1,0:T(8,128)(2,1)} async-done(((bf16[512,640]{1,0:T(8,128)(2,1)}), bf16[2048,640]{1,0:T(8,128)(2,1)}) %all-gather.20.cloned.1.call-update) | async-done | bytes 2621456 | tf_op jit(solution)/shard_map/all_gather | solution.py:568
  128.4 5.6 collective-permute-done.5
  141.0 8.0 fusion.47.refs_3_
  149.0 20.7 %collective-permute-done.11.refs_2_.refs_4_ = bf16[256,2560]{1,0:T(8,128)(2,1)S(1)} collective-permute-done((bf16[256,2560]{1,0:T(8,128)(2,1)}, bf16[256,2560]{1,0:T(8,128)(2,1)S(1)}, u32[]{:S(2)}, u32[]{:S(2)}) %collective-permute-start.11) | collective-permute-done | bytes 1310752 | tf_op jit(solution)/shard_map/ppermute | solution.py:79
  172.5 9.8 convolution_add_fusion.pre_ref
  182.2 18.9 %recurrence.1 = (f32[512,2560]{1,0:T(8,128)}, f32[512,2560]{1,0:T(8,128)}, f32[512,2560]{1,0:T(8,128)}, f32[512,2560]{1,0:T(8,128)}, f32[512,2560]{1,0:T(8,128)}, /*index=5*/f32[512,2560]{1,0:T(8,128)}) custom-call(s32[1]{0:T(128)} %sub.38.live_ref, f32[528,2560]{1,0:T(8,128)} %convolution_add_fusion.pre_ref, f32[8,2560]{1,0:T(8,128)} %pad_maximum_fusion.14.par_ref, ...), custom_call_target="tpu_custom_call" | custom-call | flops 1024 | bytes 1024 | tf_op jit(solution)/shard_map/recurrence/pallas_call | solution.py:494
  203.0 5.3 collective-permute-start.17
  232.4 9.0 fusion.22
  241.4 10.8 collective-permute-done.20.refs_1_
  258.8 13.6 %collective-permute-done.21.refs_2_.refs_3_ = bf16[128,2560]{1,0:T(8,128)(2,1)S(1)} collective-permute-done((bf16[128,2560]{1,0:T(8,128)(2,1)S(1)}, bf16[128,2560]{1,0:T(8,128)(2,1)S(1)}, u32[]{:S(2)}, u32[]{:S(2)}) %collective-permute-start.21) | collective-permute-done | bytes 655392 | tf_op jit(solution)/shard_map/ppermute | solution.py:79
  306.9 6.2 assemble.10.refs_0_
  317.4 18.5 %collective-permute-done.28.refs_4_ = bf16[256,1536]{1,0:T(8,128)(2,1)S(1)} collective-permute-done((bf16[256,1536]{1,0:T(8,128)(2,1)}, bf16[256,1536]{1,0:T(8,128)(2,1)S(1)}, u32[]{:S(2)}, u32[]{:S(2)}) %collective-permute-start.28) | collective-permute-done | bytes 786464 | tf_op jit(solution)/shard_map/ppermute | solution.py:79
  337.8 9.0 collective-permute-done.29.refs_2_
  352.0 5.2 collective-permute-done.31.refs_1_
  363.5 5.8 permute.8
  369.4 5.8 permute.7
  375.8 9.3 assemble.11
  385.1 19.3 %fusion.85 = f32[1024,3072]{1,0:T(8,128)} fusion(bf16[1024,2048]{1,0:T(8,128)(2,1)} %all-gather.16.cloned.1.call-done, bf16[2048,3072]{1,0:T(8,128)(2,1)} %assemble.11), kind=kOutput, calls=%fused_computation.262 | convolution fusion | flops 12884901888 | bytes 29360128 | tf_op jit(solution)/shard_map/dot_general | solution.py:24
  404.4 16.0 %fusion.6 = (bf16[1024,1536]{1,0:T(8,128)(2,1)S(1)}, bf16[1024,1536]{1,0:T(8,128)(2,1)S(1)}, bf16[1024,1536]{1,0:T(8,128)(2,1)}) fusion(f32[1024,3072]{1,0:T(8,128)} %fusion.85, bf16[1024,2048]{1,0:T(8,128)(2,1)S(1)} %copy-done.39, bf16[2048,1536]{1,0:T(8,128)(2,1)} %assemble.13), kind=kOutput, calls=%fused_computation.15 | convolution fusion | flops 6483345408 | bytes 32505856 | tf_op jit(solution)/shard_map/dot_general | solution.py:24
  422.1 17.6 %convolution_convert_fusion.7.refs_1_ = bf16[1024,2048]{1,0:T(8,128)(2,1)} fusion(bf16[2048,3072]{1,0:T(8,128)(2,1)} %assemble.11, bf16[1024,1536]{1,0:T(8,128)(2,1)S(1)} %get-tuple-element.199, bf16[1024,1536]{1,0:T(8,128)(2,1)S(1)} %get-tuple-element.198), kind=kOutput, calls=%fused_computation.72 | convolution fusion | flops 12899581952 | bytes 23068672 | tf_op jit(solution)/shard_map/dot_general | solution.py:24
  439.9 22.5 %all-gather.18.cloned.1.call-done.refs_0_ = bf16[1024,2048]{1,0:T(8,128)(2,1)} async-done(((bf16[256,2048]{1,0:T(8,128)(2,1)}), bf16[1024,2048]{1,0:T(8,128)(2,1)}) %all-gather.18.cloned.1.call-update) | async-done | bytes 4194320 | tf_op jit(solution)/shard_map/all_gather | solution.py:632
  462.4 19.1 %fusion.86 = f32[1024,3072]{1,0:T(8,128)} fusion(bf16[1024,2048]{1,0:T(8,128)(2,1)} %fence.42, bf16[2048,3072]{1,0:T(8,128)(2,1)} %assemble.11), kind=kOutput, calls=%fused_computation.263 | convolution fusion | flops 12884901888 | bytes 29360128 | tf_op jit(solution)/shard_map/dot_general | solution.py:24
  481.5 15.3 %fusion.13 = (bf16[1024,1536]{1,0:T(8,128)(2,1)}, bf16[1024,1536]{1,0:T(8,128)(2,1)}, bf16[1024,1536]{1,0:T(8,128)(2,1)}) fusion(f32[1024,3072]{1,0:T(8,128)} %fusion.86, bf16[1024,2048]{1,0:T(8,128)(2,1)S(1)} %copy-done.37, bf16[2048,1536]{1,0:T(8,128)(2,1)S(1)} %bitcast.193), kind=kOutput, calls=%fused_computation.22 | convolution fusion | flops 6483345408 | bytes 32505856 | tf_op jit(solution)/shard_map/dot_general | solution.py:24
  496.8 5.5 pad_maximum_fusion.refs_1_
  502.3 18.7 %convolution_convert_fusion.6.refs_2_ = bf16[1024,2048]{1,0:T(8,128)(2,1)} fusion(bf16[2048,3072]{1,0:T(8,128)(2,1)} %assemble.11, bf16[1024,1536]{1,0:T(8,128)(2,1)} %get-tuple-element.197, bf16[1024,1536]{1,0:T(8,128)(2,1)S(1)} %copy-done.63), kind=kOutput, calls=%fused_computation.71 | convolution fusion | flops 12899581952 | bytes 23068672 | tf_op jit(solution)/shard_map/dot_general | solution.py:24
  522.9 5.7 pad_maximum_fusion.1.refs_1_
  528.6 7.5 fusion.37
  536.1 8.3 convolution_convert_fusion.9.refs_6_.refs_0_
  544.6 9.7 add_convert_fusion.2
  554.3 9.7 fusion.31
  564.0 11.8 add_convert_fusion
  576.3 11.0 fusion.34
  587.3 11.2 convolution_convert_fusion.8.refs_7_.refs_1_
  598.5 5.4 fusion.40
  603.9 7.0 add_convert_fusion.3
  611.0 10.2 add_convert_fusion.1
  644.2 5.7 fusion.52
  655.2 17.1 %back_scan.1 = (f32[512,2560]{1,0:T(8,128)}, f32[512,2560]{1,0:T(8,128)}, f32[8,2560]{1,0:T(8,128)}, bf16[512,2560]{1,0:T(8,128)(2,1)}) custom-call(s32[1]{0:T(128)} %sub.38.live_ref, f32[512,2560]{1,0:T(8,128)} %get-tuple-element.268.refs_2_.pre_ref, f32[512,2560]{1,0:T(8,128)} %convolution_add_fusion.1.grad_ref, f32[512,2560]{1,0:T(8,128)} %get-tuple-element.80.decay_ref, ...), custom_call_target="tpu_custom_call" | custom-call | flops 1024 | bytes 1024 | tf_op jit(solution)/shard_map/back_scan/pallas_call | solution.py:494
  677.2 10.9 collective-permute-done.37.refs_4_
  690.0 26.3 %recurrence_back.1 = (f32[528,2560]{1,0:T(8,128)}, f32[8,2560]{1,0:T(8,128)}, bf16[4,160,1280]{2,1,0:T(8,128)(2,1)}) custom-call(s32[1]{0:T(128)} %sub.38.live_ref, f32[528,2560]{1,0:T(8,128)} %convolution_add_fusion.pre_ref, f32[8,2560]{1,0:T(8,128)} %pad_maximum_fusion.14.par_ref, bf16[8,4,80,640]{3,2,1,0:T(8,128)(2,1)} %copy-done.21, ...), custom_call_target="tpu_custom_call" | custom-call | flops 1024 | bytes 1024 | tf_op jit(solution)/shard_map/recurrence_back/pallas_call | solution.py:494
  719.3 7.5 fusion.87
  726.8 6.8 fusion.88
  737.9 6.6 fusion.90
  750.0 6.1 add_convert_fusion.4.in_ref
  761.2 6.5 convolution_convert_fusion.5
  769.4 7.4 collective-permute-done.42.refs_2_
  776.7 7.5 convolution_convert_fusion.3
  784.6 6.0 convolution_convert_fusion
  791.0 7.4 convolution_convert_fusion.2
  828.4 16.7 %collective-permute-done.45.refs_3_ = bf16[256,2560]{1,0:T(8,128)(2,1)S(1)} collective-permute-done((bf16[256,2560]{1,0:T(8,128)(2,1)S(1)}, bf16[256,2560]{1,0:T(8,128)(2,1)S(1)}, u32[]{:S(2)}, u32[]{:S(2)}) %collective-permute-start.45) | collective-permute-done | bytes 1310752 | tf_op jit(solution)/shard_map/ppermute | solution.py:79
  856.9 16.7 %all-gather.22.cloned.1.call-done = bf16[1024,2048]{1,0:T(8,128)(2,1)} async-done(((bf16[256,2048]{1,0:T(8,128)(2,1)}), bf16[1024,2048]{1,0:T(8,128)(2,1)}) %all-gather.22.cloned.1.call-update) | async-done | bytes 4194320 | tf_op jit(solution)/shard_map/all_gather | solution.py:706
  888.5 8.5 collective-permute-done.48
  901.6 9.5 collective-permute-done.50
  915.7 21.1 %collective-permute-done.53.refs_3_ = bf16[256,2560]{1,0:T(8,128)(2,1)S(1)} collective-permute-done((bf16[256,2560]{1,0:T(8,128)(2,1)}, bf16[256,2560]{1,0:T(8,128)(2,1)S(1)}, u32[]{:S(2)}, u32[]{:S(2)}) %collective-permute-start.53) | collective-permute-done | bytes 1310752 | tf_op jit(solution)/shard_map/ppermute | solution.py:79
  964.9 5.4 collective-permute-start.57
  978.1 33.2 %collective-permute-done.57.refs_0_.refs_3_ = bf16[3,256,640]{2,1,0:T(8,128)(2,1)S(1)} collective-permute-done((bf16[3,256,640]{2,1,0:T(8,128)(2,1)S(1)}, bf16[3,256,640]{2,1,0:T(8,128)(2,1)S(1)}, u32[]{:S(2)}, u32[]{:S(2)}) %collective-permute-start.57) | collective-permute-done | bytes 983072 | tf_op jit(solution)/shard_map/ppermute | solution.py:193
  1054.2 7.5 collective-permute-done.63
  1063.3 7.2 collective-permute-done.64
  1073.9 7.0 interleave.3
  1100.6 58.2 %collective-permute-done.62.refs_3_ = bf16[3,256,640]{2,1,0:T(8,128)(2,1)S(1)} collective-permute-done((bf16[3,256,640]{2,1,0:T(8,128)(2,1)}, bf16[3,256,640]{2,1,0:T(8,128)(2,1)S(1)}, u32[]{:S(2)}, u32[]{:S(2)}) %collective-permute-start.62) | collective-permute-done | bytes 983072 | tf_op jit(solution)/shard_map/ppermute | solution.py:194
  1163.3 15.9 %all-gather.26.cloned.1.call-done = bf16[1024,2048]{1,0:T(8,128)(2,1)} async-done(((bf16[256,2048]{1,0:T(8,128)(2,1)}), bf16[1024,2048]{1,0:T(8,128)(2,1)}) %all-gather.26.cloned.1.call-update) | async-done | bytes 4194320 | tf_op jit(solution)/shard_map/all_gather | solution.py:718
  1179.2 7.0 interleave.2
  (657 shorter events, 395.4 us)
Async XLA Ops:
  7.2 48.5 %all-gather.14.cloned.1.call-start = ((), (), s32[]{:S(2)}) async-start(), calls=%async_computation.4 | async-start | bytes 2150400 | tf_op jit(solution)/shard_map/all_gather | solution.py:567
  12.0 100.4 %all-gather.20.cloned.1.call-start = ((), (), s32[]{:S(2)}) async-start(), calls=%async_computation.11 | async-start | bytes 3276800 | tf_op jit(solution)/shard_map/all_gather | solution.py:568
  15.5 38.7 %collective-permute-start.1 = (bf16[256,3072]{1,0:T(8,128)(2,1)}, bf16[256,3072]{1,0:T(8,128)(2,1)S(1)}, u32[]{:S(2)}, u32[]{:S(2)}) collective-permute-start(bf16[256,3072]{1,0:T(8,128)(2,1)} %pad_maximum_fusion.8.refs_0_), channel_id=1, source_target_pairs={{0,16},{4,20},{8,24},{12,28},{16,0},{20,4},{24,8},{28,12},{1,17},{... | collective-permute-start | bytes 4718600 | tf_op jit(solution)/shard_map/ppermute | solution.py:79
  19.6 36.1 %collective-permute-start = (bf16[256,3072]{1,0:T(8,128)(2,1)}, bf16[256,3072]{1,0:T(8,128)(2,1)S(1)}, u32[]{:S(2)}, u32[]{:S(2)}) collective-permute-start(bf16[256,3072]{1,0:T(8,128)(2,1)} %pad_maximum_fusion.8.refs_0_), channel_id=1, source_target_pairs={{0,8},{4,12},{8,0},{12,4},{16,24},{20,28},{24,16},{28,20},{1,9},{5... | collective-permute-start | bytes 4718600 | tf_op jit(solution)/shard_map/ppermute | solution.py:79
  56.9 328.2 %all-gather.16.cloned.1.call-start = ((), (), s32[]{:S(2)}) async-start(), calls=%async_computation.5 | async-start | bytes 5242880 | tf_op jit(solution)/shard_map/all_gather | solution.py:632
  58.5 29.5 %collective-permute-start.8 = (bf16[256,2560]{1,0:T(8,128)(2,1)S(1)}, bf16[256,2560]{1,0:T(8,128)(2,1)S(1)}, u32[]{:S(2)}, u32[]{:S(2)}) collective-permute-start(bf16[256,2560]{1,0:T(8,128)(2,1)S(1)} %bitcast.205), channel_id=1, source_target_pairs={{0,16},{4,20},{8,24},{12,28},{16,0},{20,4},{24,8},{28,12},{1,17},{... | collective-permute-start | bytes 3932168 | tf_op jit(solution)/shard_map/ppermute | solution.py:79
  59.6 30.9 %collective-permute-start.6 = (bf16[256,2560]{1,0:T(8,128)(2,1)S(1)}, bf16[256,2560]{1,0:T(8,128)(2,1)S(1)}, u32[]{:S(2)}, u32[]{:S(2)}) collective-permute-start(bf16[256,2560]{1,0:T(8,128)(2,1)S(1)} %bitcast.206), channel_id=1, source_target_pairs={{0,8},{4,12},{8,0},{12,4},{16,24},{20,28},{24,16},{28,20},{1,9},{5... | collective-permute-start | bytes 3932168 | tf_op jit(solution)/shard_map/ppermute | solution.py:79
  89.0 27.6 %collective-permute-start.9 = (bf16[128,2560]{1,0:T(8,128)(2,1)}, bf16[128,2560]{1,0:T(8,128)(2,1)}, u32[]{:S(2)}, u32[]{:S(2)}) collective-permute-start(bf16[128,2560]{1,0:T(8,128)(2,1)} %slice.710), channel_id=1, source_target_pairs={{0,8},{4,12},{8,0},{12,4},{16,24},{20,28},{24,16},{28,20},{1,9},{5... | collective-permute-start | bytes 1966088 | tf_op jit(solution)/shard_map/ppermute | solution.py:79
  91.8 26.8 %collective-permute-start.7 = (bf16[128,2560]{1,0:T(8,128)(2,1)}, bf16[128,2560]{1,0:T(8,128)(2,1)}, u32[]{:S(2)}, u32[]{:S(2)}) collective-permute-start(bf16[128,2560]{1,0:T(8,128)(2,1)} %slice.709), channel_id=1, source_target_pairs={{0,16},{4,20},{8,24},{12,28},{16,0},{20,4},{24,8},{28,12},{1,17},{... | collective-permute-start | bytes 1966088 | tf_op jit(solution)/shard_map/ppermute | solution.py:79
  94.5 29.4 %collective-permute-start.4 = (bf16[320,640]{1,0:T(8,128)(2,1)}, bf16[320,640]{1,0:T(8,128)(2,1)S(1)}, u32[]{:S(2)}, u32[]{:S(2)}) collective-permute-start(bf16[320,640]{1,0:T(8,128)(2,1)} %bitcast.8), channel_id=1, source_target_pairs={{0,16},{4,20},{8,24},{12,28},{16,0},{20,4},{24,8},{28,12},{1,17},{... | collective-permute-start | bytes 1228808 | tf_op jit(solution)/shard_map/ppermute | solution.py:79
  95.4 28.5 %collective-permute-start.3 = (bf16[320,640]{1,0:T(8,128)(2,1)}, bf16[320,640]{1,0:T(8,128)(2,1)}, u32[]{:S(2)}, u32[]{:S(2)}) collective-permute-start(bf16[320,640]{1,0:T(8,128)(2,1)} %bitcast.8), channel_id=1, source_target_pairs={{0,24},{4,28},{8,16},{12,20},{16,8},{20,12},{24,0},{28,4},{1,25},{... | collective-permute-start | bytes 1228808 | tf_op jit(solution)/shard_map/ppermute | solution.py:79
  96.5 27.4 %collective-permute-start.2 = (bf16[320,640]{1,0:T(8,128)(2,1)}, bf16[320,640]{1,0:T(8,128)(2,1)}, u32[]{:S(2)}, u32[]{:S(2)}) collective-permute-start(bf16[320,640]{1,0:T(8,128)(2,1)} %bitcast.8), channel_id=1, source_target_pairs={{0,8},{4,12},{8,0},{12,4},{16,24},{20,28},{24,16},{28,20},{1,9},{5... | collective-permute-start | bytes 1228808 | tf_op jit(solution)/shard_map/ppermute | solution.py:79
  122.9 49.6 %collective-permute-start.14 = (bf16[1024,2560]{1,0:T(8,128)(2,1)}, bf16[1024,2560]{1,0:T(8,128)(2,1)}, u32[]{:S(2)}, u32[]{:S(2)}) collective-permute-start(bf16[1024,2560]{1,0:T(8,128)(2,1)} %assemble.7), channel_id=1, source_target_pairs={{0,4},{4,0},{8,12},{12,8},{16,20},{20,16},{24,28},{28,24},{1,5},{5... | collective-permute-start | bytes 15728648 | tf_op jit(solution)/shard_map/ppermute | solution.py:79
  138.6 31.0 %collective-permute-start.11 = (bf16[256,2560]{1,0:T(8,128)(2,1)}, bf16[256,2560]{1,0:T(8,128)(2,1)S(1)}, u32[]{:S(2)}, u32[]{:S(2)}) collective-permute-start(bf16[256,2560]{1,0:T(8,128)(2,1)} %fence.35.refs_0_), channel_id=1, source_target_pairs={{0,16},{4,20},{8,24},{12,28},{16,0},{20,4},{24,8},{28,12},{1,17},{... | collective-permute-start | bytes 3932168 | tf_op jit(solution)/shard_map/ppermute | solution.py:79
  139.8 30.7 %collective-permute-start.10 = (bf16[256,2560]{1,0:T(8,128)(2,1)}, bf16[256,2560]{1,0:T(8,128)(2,1)S(1)}, u32[]{:S(2)}, u32[]{:S(2)}) collective-permute-start(bf16[256,2560]{1,0:T(8,128)(2,1)} %fence.35.refs_0_), channel_id=1, source_target_pairs={{0,8},{4,12},{8,0},{12,4},{16,24},{20,28},{24,16},{28,20},{1,9},{5... | collective-permute-start | bytes 3932168 | tf_op jit(solution)/shard_map/ppermute | solution.py:79
  169.7 42.6 %collective-permute-start.12 = (bf16[128,2560]{1,0:T(8,128)(2,1)S(1)}, bf16[128,2560]{1,0:T(8,128)(2,1)S(1)}, u32[]{:S(2)}, u32[]{:S(2)}) collective-permute-start(bf16[128,2560]{1,0:T(8,128)(2,1)S(1)} %slice.711), channel_id=1, source_target_pairs={{0,8},{4,12},{8,0},{12,4},{16,24},{20,28},{24,16},{28,20},{1,9},{5... | collective-permute-start | bytes 1966088 | tf_op jit(solution)/shard_map/ppermute | solution.py:79
  171.5 40.9 %collective-permute-start.13 = (bf16[128,2560]{1,0:T(8,128)(2,1)}, bf16[128,2560]{1,0:T(8,128)(2,1)S(1)}, u32[]{:S(2)}, u32[]{:S(2)}) collective-permute-start(bf16[128,2560]{1,0:T(8,128)(2,1)} %slice.712), channel_id=1, source_target_pairs={{0,16},{4,20},{8,24},{12,28},{16,0},{20,4},{24,8},{28,12},{1,17},{... | collective-permute-start | bytes 1966088 | tf_op jit(solution)/shard_map/ppermute | solution.py:79
  220.8 31.4 %collective-permute-start.20 = (bf16[256,2560]{1,0:T(8,128)(2,1)}, bf16[256,2560]{1,0:T(8,128)(2,1)S(1)}, u32[]{:S(2)}, u32[]{:S(2)}) collective-permute-start(bf16[256,2560]{1,0:T(8,128)(2,1)} %fence.37.refs_0_), channel_id=1, source_target_pairs={{0,16},{4,20},{8,24},{12,28},{16,0},{20,4},{24,8},{28,12},{1,17},{... | collective-permute-start | bytes 3932168 | tf_op jit(solution)/shard_map/ppermute | solution.py:79
  221.9 31.1 %collective-permute-start.19 = (bf16[256,2560]{1,0:T(8,128)(2,1)}, bf16[256,2560]{1,0:T(8,128)(2,1)S(1)}, u32[]{:S(2)}, u32[]{:S(2)}) collective-permute-start(bf16[256,2560]{1,0:T(8,128)(2,1)} %fence.37.refs_0_), channel_id=1, source_target_pairs={{0,8},{4,12},{8,0},{12,4},{16,24},{20,28},{24,16},{28,20},{1,9},{5... | collective-permute-start | bytes 3932168 | tf_op jit(solution)/shard_map/ppermute | solution.py:79
  256.3 16.1 %collective-permute-start.21 = (bf16[128,2560]{1,0:T(8,128)(2,1)S(1)}, bf16[128,2560]{1,0:T(8,128)(2,1)S(1)}, u32[]{:S(2)}, u32[]{:S(2)}) collective-permute-start(bf16[128,2560]{1,0:T(8,128)(2,1)S(1)} %slice.551), channel_id=1, source_target_pairs={{0,8},{4,12},{8,0},{12,4},{16,24},{20,28},{24,16},{28,20},{1,9},{5... | collective-permute-start | bytes 1966088 | tf_op jit(solution)/shard_map/ppermute | solution.py:79
  257.7 15.8 %collective-permute-start.22 = (bf16[128,2560]{1,0:T(8,128)(2,1)S(1)}, bf16[128,2560]{1,0:T(8,128)(2,1)S(1)}, u32[]{:S(2)}, u32[]{:S(2)}) collective-permute-start(bf16[128,2560]{1,0:T(8,128)(2,1)S(1)} %slice.552), channel_id=1, source_target_pairs={{0,16},{4,20},{8,24},{12,28},{16,0},{20,4},{24,8},{28,12},{1,17},{... | collective-permute-start | bytes 1966088 | tf_op jit(solution)/shard_map/ppermute | solution.py:79
  285.8 20.1 %collective-permute-start.24 = (bf16[128,3072]{1,0:T(8,128)(2,1)}, bf16[128,3072]{1,0:T(8,128)(2,1)S(1)}, u32[]{:S(2)}, u32[]{:S(2)}) collective-permute-start(bf16[128,3072]{1,0:T(8,128)(2,1)} %slice.556), channel_id=1, source_target_pairs={{0,8},{4,12},{8,0},{12,4},{16,24},{20,28},{24,16},{28,20},{1,9},{5... | collective-permute-start | bytes 2359304 | tf_op jit(solution)/shard_map/ppermute | solution.py:79
  286.4 20.0 %collective-permute-start.25 = (bf16[128,3072]{1,0:T(8,128)(2,1)}, bf16[128,3072]{1,0:T(8,128)(2,1)}, u32[]{:S(2)}, u32[]{:S(2)}) collective-permute-start(bf16[128,3072]{1,0:T(8,128)(2,1)} %slice.557), channel_id=1, source_target_pairs={{0,16},{4,20},{8,24},{12,28},{16,0},{20,4},{24,8},{28,12},{1,17},{... | collective-permute-start | bytes 2359304 | tf_op jit(solution)/shard_map/ppermute | solution.py:79
  301.4 161.0 %all-gather.18.cloned.1.call-start = ((), (), s32[]{:S(2)}) async-start(), calls=%async_computation.6 | async-start | bytes 5242880 | tf_op jit(solution)/shard_map/all_gather | solution.py:632
  313.1 62.6 %collective-permute-start.26 = (bf16[1024,3072]{1,0:T(8,128)(2,1)}, bf16[1024,3072]{1,0:T(8,128)(2,1)}, u32[]{:S(2)}, u32[]{:S(2)}) collective-permute-start(bf16[1024,3072]{1,0:T(8,128)(2,1)} %assemble.10.refs_0_), channel_id=1, source_target_pairs={{0,4},{4,0},{8,12},{12,8},{16,20},{20,16},{24,28},{28,24},{1,5},{5... | collective-permute-start | bytes 18874376 | tf_op jit(solution)/shard_map/ppermute | solution.py:79
  315.8 20.1 %collective-permute-start.28 = (bf16[256,1536]{1,0:T(8,128)(2,1)}, bf16[256,1536]{1,0:T(8,128)(2,1)S(1)}, u32[]{:S(2)}, u32[]{:S(2)}) collective-permute-start(bf16[256,1536]{1,0:T(8,128)(2,1)} %fence.41.refs_0_), channel_id=1, source_target_pairs={{0,16},{4,20},{8,24},{12,28},{16,0},{20,4},{24,8},{28,12},{1,17},{... | collective-permute-start | bytes 2359304 | tf_op jit(solution)/shard_map/ppermute | solution.py:79
  316.7 20.2 %collective-permute-start.27 = (bf16[256,1536]{1,0:T(8,128)(2,1)}, bf16[256,1536]{1,0:T(8,128)(2,1)S(1)}, u32[]{:S(2)}, u32[]{:S(2)}) collective-permute-start(bf16[256,1536]{1,0:T(8,128)(2,1)} %fence.41.refs_0_), channel_id=1, source_target_pairs={{0,8},{4,12},{8,0},{12,4},{16,24},{20,28},{24,16},{28,20},{1,9},{5... | collective-permute-start | bytes 2359304 | tf_op jit(solution)/shard_map/ppermute | solution.py:79
  375.2 256.5 %reduce-scatter.5.cloned.1.call-start = ((), (), s32[]{:S(2)}) async-start(), calls=%async_computation.7 | async-start | bytes 5242880 | tf_op jit(solution)/shard_map/reduce_scatter | solution.py:641
  439.7 192.0 %reduce-scatter.7.cloned.1.call-start = ((), (), s32[]{:S(2)}) async-start(), calls=%async_computation.8 | async-start | bytes 5242880 | tf_op jit(solution)/shard_map/reduce_scatter | solution.py:641
  544.5 189.6 %reduce-scatter.9.cloned.1.call-start = ((), (), s32[]{:S(2)}) async-start(), calls=%async_computation.9 | async-start | bytes 5242880 | tf_op jit(solution)/shard_map/reduce_scatter | solution.py:666
  554.2 66.9 %collective-permute-start.32 = (bf16[1024,1536]{1,0:T(8,128)(2,1)}, bf16[1024,1536]{1,0:T(8,128)(2,1)S(1)}, u32[]{:S(2)}, u32[]{:S(2)}) collective-permute-start(bf16[1024,1536]{1,0:T(8,128)(2,1)} %add_convert_fusion.2), channel_id=1, source_target_pairs={{0,4},{4,0},{8,12},{12,8},{16,20},{20,16},{24,28},{28,24},{1,5},{5... | collective-permute-start | bytes 9437192 | tf_op jit(solution)/shard_map/ppermute | solution.py:79
  575.8 51.2 %collective-permute-start.33 = (bf16[1024,3072]{1,0:T(8,128)(2,1)}, bf16[1024,3072]{1,0:T(8,128)(2,1)}, u32[]{:S(2)}, u32[]{:S(2)}) collective-permute-start(bf16[1024,3072]{1,0:T(8,128)(2,1)} %add_convert_fusion), channel_id=1, source_target_pairs={{0,4},{4,0},{8,12},{12,8},{16,20},{20,16},{24,28},{28,24},{1,5},{5... | collective-permute-start | bytes 18874376 | tf_op jit(solution)/shard_map/ppermute | solution.py:79
  631.8 166.7 %reduce-scatter.11.cloned.1.call-start = ((), (), s32[]{:S(2)}) async-start(), calls=%async_computation.10 | async-start | bytes 5242880 | tf_op jit(solution)/shard_map/reduce_scatter | solution.py:666
  634.7 39.8 %collective-permute-start.35 = (bf16[256,1536]{1,0:T(8,128)(2,1)}, bf16[256,1536]{1,0:T(8,128)(2,1)}, u32[]{:S(2)}, u32[]{:S(2)}) collective-permute-start(bf16[256,1536]{1,0:T(8,128)(2,1)} %get-tuple-element.230.refs_3_), channel_id=1, source_target_pairs={{0,16},{4,20},{8,24},{12,28},{16,0},{20,4},{24,8},{28,12},{1,17},{... | collective-permute-start | bytes 2359304 | tf_op jit(solution)/shard_map/ppermute | solution.py:79
  636.1 39.7 %collective-permute-start.34 = (bf16[256,1536]{1,0:T(8,128)(2,1)}, bf16[256,1536]{1,0:T(8,128)(2,1)}, u32[]{:S(2)}, u32[]{:S(2)}) collective-permute-start(bf16[256,1536]{1,0:T(8,128)(2,1)} %get-tuple-element.231.refs_2_), channel_id=1, source_target_pairs={{0,8},{4,12},{8,0},{12,4},{16,24},{20,28},{24,16},{28,20},{1,9},{5... | collective-permute-start | bytes 2359304 | tf_op jit(solution)/shard_map/ppermute | solution.py:79
  637.6 50.5 %collective-permute-start.37 = (bf16[256,3072]{1,0:T(8,128)(2,1)}, bf16[256,3072]{1,0:T(8,128)(2,1)}, u32[]{:S(2)}, u32[]{:S(2)}) collective-permute-start(bf16[256,3072]{1,0:T(8,128)(2,1)} %get-tuple-element.204.refs_5_), channel_id=1, source_target_pairs={{0,16},{4,20},{8,24},{12,28},{16,0},{20,4},{24,8},{28,12},{1,17},{... | collective-permute-start | bytes 4718600 | tf_op jit(solution)/shard_map/ppermute | solution.py:79
  638.1 51.1 %collective-permute-start.36 = (bf16[256,3072]{1,0:T(8,128)(2,1)}, bf16[256,3072]{1,0:T(8,128)(2,1)}, u32[]{:S(2)}, u32[]{:S(2)}) collective-permute-start(bf16[256,3072]{1,0:T(8,128)(2,1)} %get-tuple-element.205.refs_4_), channel_id=1, source_target_pairs={{0,8},{4,12},{8,0},{12,4},{16,24},{20,28},{24,16},{28,20},{1,9},{5... | collective-permute-start | bytes 4718600 | tf_op jit(solution)/shard_map/ppermute | solution.py:79
  640.6 233.0 %all-gather.22.cloned.1.call-start = ((), (), s32[]{:S(2)}) async-start(), calls=%async_computation.12 | async-start | bytes 5242880 | tf_op jit(solution)/shard_map/all_gather | solution.py:706
  673.2 16.0 %collective-permute-start.40 = (f32[2,2560]{1,0:T(2,128)S(1)}, f32[2,2560]{1,0:T(2,128)S(1)}, u32[]{:S(2)}, u32[]{:S(2)}) collective-permute-start(f32[2,2560]{1,0:T(2,128)S(1)} %pad_maximum_fusion.16), channel_id=1, source_target_pairs={{3,0},{7,4},{11,8},{15,12},{19,16},{23,20},{27,24},{31,28}} | collective-permute-start | bytes 61448 | tf_op jit(solution)/shard_map/ppermute | solution.py:166
  674.5 14.7 %collective-permute-start.39 = (f32[2,2560]{1,0:T(2,128)S(1)}, f32[2,2560]{1,0:T(2,128)S(1)}, u32[]{:S(2)}, u32[]{:S(2)}) collective-permute-start(f32[2,2560]{1,0:T(2,128)S(1)} %pad_maximum_fusion.16), channel_id=1, source_target_pairs={{2,0},{3,1},{6,4},{7,5},{10,8},{11,9},{14,12},{15,13},{18,16},{19,... | collective-permute-start | bytes 61448 | tf_op jit(solution)/shard_map/ppermute | solution.py:166
  717.3 16.7 %collective-permute-start.41 = (f32[16,2560]{1,0:T(8,128)S(1)}, f32[16,2560]{1,0:T(8,128)S(1)}, u32[]{:S(2)}, u32[]{:S(2)}) collective-permute-start(f32[16,2560]{1,0:T(8,128)S(1)} %slice.592), channel_id=1, source_target_pairs={{1,0},{2,1},{3,2},{5,4},{6,5},{7,6},{9,8},{10,9},{11,10},{13,12},{... | collective-permute-start | bytes 491528 | tf_op jit(solution)/shard_map/ppermute | solution.py:166
  769.3 208.7 %all-gather.28.cloned.1.call-start = ((), (), s32[]{:S(2)}) async-start(), calls=%async_computation.15 | async-start | bytes 5242880 | tf_op jit(solution)/shard_map/all_gather | solution.py:706
  784.2 40.3 %collective-permute-start.43 = (bf16[1024,2560]{1,0:T(8,128)(2,1)}, bf16[1024,2560]{1,0:T(8,128)(2,1)}, u32[]{:S(2)}, u32[]{:S(2)}) collective-permute-start(bf16[1024,2560]{1,0:T(8,128)(2,1)} %convolution_convert_fusion.3), channel_id=1, source_target_pairs={{0,4},{4,0},{8,12},{12,8},{16,20},{20,16},{24,28},{28,24},{1,5},{5... | collective-permute-start | bytes 15728648 | tf_op jit(solution)/shard_map/ppermute | solution.py:79
  784.4 301.9 %all-gather.24.cloned.1.call-start = ((), (), s32[]{:S(2)}) async-start(), calls=%async_computation.13 | async-start | bytes 5242880 | tf_op jit(solution)/shard_map/all_gather | solution.py:718
  790.6 62.5 %collective-permute-start.52 = (bf16[1024,2560]{1,0:T(8,128)(2,1)}, bf16[1024,2560]{1,0:T(8,128)(2,1)}, u32[]{:S(2)}, u32[]{:S(2)}) collective-permute-start(bf16[1024,2560]{1,0:T(8,128)(2,1)} %convolution_convert_fusion), channel_id=1, source_target_pairs={{0,4},{4,0},{8,12},{12,8},{16,20},{20,16},{24,28},{28,24},{1,5},{5... | collective-permute-start | bytes 15728648 | tf_op jit(solution)/shard_map/ppermute | solution.py:79
  814.3 30.8 %collective-permute-start.45 = (bf16[256,2560]{1,0:T(8,128)(2,1)S(1)}, bf16[256,2560]{1,0:T(8,128)(2,1)S(1)}, u32[]{:S(2)}, u32[]{:S(2)}) collective-permute-start(bf16[256,2560]{1,0:T(8,128)(2,1)S(1)} %get-tuple-element.222), channel_id=1, source_target_pairs={{0,16},{4,20},{8,24},{12,28},{16,0},{20,4},{24,8},{28,12},{1,17},{... | collective-permute-start | bytes 3932168 | tf_op jit(solution)/shard_map/ppermute | solution.py:79
  815.2 30.6 %collective-permute-start.44 = (bf16[256,2560]{1,0:T(8,128)(2,1)S(1)}, bf16[256,2560]{1,0:T(8,128)(2,1)S(1)}, u32[]{:S(2)}, u32[]{:S(2)}) collective-permute-start(bf16[256,2560]{1,0:T(8,128)(2,1)S(1)} %get-tuple-element.223), channel_id=1, source_target_pairs={{0,8},{4,12},{8,0},{12,4},{16,24},{20,28},{24,16},{28,20},{1,9},{5... | collective-permute-start | bytes 3932168 | tf_op jit(solution)/shard_map/ppermute | solution.py:79
  846.9 30.0 %collective-permute-start.46 = (bf16[256,2560]{1,0:T(8,128)(2,1)}, bf16[256,2560]{1,0:T(8,128)(2,1)S(1)}, u32[]{:S(2)}, u32[]{:S(2)}) collective-permute-start(bf16[256,2560]{1,0:T(8,128)(2,1)} %get-tuple-element.92), channel_id=1, source_target_pairs={{0,8},{4,12},{8,0},{12,4},{16,24},{20,28},{24,16},{28,20},{1,9},{5... | collective-permute-start | bytes 3932168 | tf_op jit(solution)/shard_map/ppermute | solution.py:79
  848.3 29.7 %collective-permute-start.47 = (bf16[256,2560]{1,0:T(8,128)(2,1)}, bf16[256,2560]{1,0:T(8,128)(2,1)S(1)}, u32[]{:S(2)}, u32[]{:S(2)}) collective-permute-start(bf16[256,2560]{1,0:T(8,128)(2,1)} %get-tuple-element.93), channel_id=1, source_target_pairs={{0,16},{4,20},{8,24},{12,28},{16,0},{20,4},{24,8},{28,12},{1,17},{... | collective-permute-start | bytes 3932168 | tf_op jit(solution)/shard_map/ppermute | solution.py:79
  879.1 17.9 %collective-permute-start.48 = (bf16[128,2560]{1,0:T(8,128)(2,1)}, bf16[128,2560]{1,0:T(8,128)(2,1)S(1)}, u32[]{:S(2)}, u32[]{:S(2)}) collective-permute-start(bf16[128,2560]{1,0:T(8,128)(2,1)} %get-tuple-element.96), channel_id=1, source_target_pairs={{0,8},{4,12},{8,0},{12,4},{16,24},{20,28},{24,16},{28,20},{1,9},{5... | collective-permute-start | bytes 1966088 | tf_op jit(solution)/shard_map/ppermute | solution.py:79
  879.8 18.0 %collective-permute-start.49 = (bf16[128,2560]{1,0:T(8,128)(2,1)}, bf16[128,2560]{1,0:T(8,128)(2,1)}, u32[]{:S(2)}, u32[]{:S(2)}) collective-permute-start(bf16[128,2560]{1,0:T(8,128)(2,1)} %get-tuple-element.97), channel_id=1, source_target_pairs={{0,16},{4,20},{8,24},{12,28},{16,0},{20,4},{24,8},{28,12},{1,17},{... | collective-permute-start | bytes 1966088 | tf_op jit(solution)/shard_map/ppermute | solution.py:79
  880.9 298.4 %all-gather.26.cloned.1.call-start = ((), (), s32[]{:S(2)}) async-start(), calls=%async_computation.14 | async-start | bytes 5242880 | tf_op jit(solution)/shard_map/all_gather | solution.py:718
  885.2 26.0 %collective-permute-start.50 = (bf16[128,2560]{1,0:T(8,128)(2,1)}, bf16[128,2560]{1,0:T(8,128)(2,1)}, u32[]{:S(2)}, u32[]{:S(2)}) collective-permute-start(bf16[128,2560]{1,0:T(8,128)(2,1)} %get-tuple-element.98), channel_id=1, source_target_pairs={{0,8},{4,12},{8,0},{12,4},{16,24},{20,28},{24,16},{28,20},{1,9},{5... | collective-permute-start | bytes 1966088 | tf_op jit(solution)/shard_map/ppermute | solution.py:79
  886.5 25.4 %collective-permute-start.51 = (bf16[128,2560]{1,0:T(8,128)(2,1)}, bf16[128,2560]{1,0:T(8,128)(2,1)}, u32[]{:S(2)}, u32[]{:S(2)}) collective-permute-start(bf16[128,2560]{1,0:T(8,128)(2,1)} %get-tuple-element.99), channel_id=1, source_target_pairs={{0,16},{4,20},{8,24},{12,28},{16,0},{20,4},{24,8},{28,12},{1,17},{... | collective-permute-start | bytes 1966088 | tf_op jit(solution)/shard_map/ppermute | solution.py:79
  887.6 49.2 %collective-permute-start.53 = (bf16[256,2560]{1,0:T(8,128)(2,1)}, bf16[256,2560]{1,0:T(8,128)(2,1)S(1)}, u32[]{:S(2)}, u32[]{:S(2)}) collective-permute-start(bf16[256,2560]{1,0:T(8,128)(2,1)} %get-tuple-element.101), channel_id=1, source_target_pairs={{0,16},{4,20},{8,24},{12,28},{16,0},{20,4},{24,8},{28,12},{1,17},{... | collective-permute-start | bytes 3932168 | tf_op jit(solution)/shard_map/ppermute | solution.py:79
  897.0 39.7 %collective-permute-start.54 = (bf16[256,2560]{1,0:T(8,128)(2,1)}, bf16[256,2560]{1,0:T(8,128)(2,1)S(1)}, u32[]{:S(2)}, u32[]{:S(2)}) collective-permute-start(bf16[256,2560]{1,0:T(8,128)(2,1)} %get-tuple-element.102), channel_id=1, source_target_pairs={{0,8},{4,12},{8,0},{12,4},{16,24},{20,28},{24,16},{28,20},{1,9},{5... | collective-permute-start | bytes 3932168 | tf_op jit(solution)/shard_map/ppermute | solution.py:79
  964.9 46.4 %collective-permute-start.57 = (bf16[3,256,640]{2,1,0:T(8,128)(2,1)S(1)}, bf16[3,256,640]{2,1,0:T(8,128)(2,1)S(1)}, u32[]{:S(2)}, u32[]{:S(2)}) collective-permute-start(bf16[3,256,640]{2,1,0:T(8,128)(2,1)S(1)} %get-tuple-element.237), channel_id=1, source_target_pairs={{0,1},{4,5},{8,9},{12,13},{16,17},{20,21},{24,25},{28,29}} | collective-permute-start | bytes 2949128 | tf_op jit(solution)/shard_map/ppermute | solution.py:193
  1021.0 25.4 %collective-permute-start.69 = (bf16[128,3072]{1,0:T(8,128)(2,1)}, bf16[128,3072]{1,0:T(8,128)(2,1)}, u32[]{:S(2)}, u32[]{:S(2)}) collective-permute-start(bf16[128,3072]{1,0:T(8,128)(2,1)} %get-tuple-element.117), channel_id=1, source_target_pairs={{0,8},{4,12},{8,0},{12,4},{16,24},{20,28},{24,16},{28,20},{1,9},{5... | collective-permute-start | bytes 2359304 | tf_op jit(solution)/shard_map/ppermute | solution.py:79
  1021.7 28.3 %collective-permute-start.70 = (bf16[128,3072]{1,0:T(8,128)(2,1)}, bf16[128,3072]{1,0:T(8,128)(2,1)}, u32[]{:S(2)}, u32[]{:S(2)}) collective-permute-start(bf16[128,3072]{1,0:T(8,128)(2,1)} %get-tuple-element.118), channel_id=1, source_target_pairs={{0,16},{4,20},{8,24},{12,28},{16,0},{20,4},{24,8},{28,12},{1,17},{... | collective-permute-start | bytes 2359304 | tf_op jit(solution)/shard_map/ppermute | solution.py:79
  1030.1 31.5 %collective-permute-start.63 = (bf16[4,4,26752]{2,1,0:T(4,128)(2,1)}, bf16[4,4,26752]{2,1,0:T(4,128)(2,1)S(1)}, u32[]{:S(2)}, u32[]{:S(2)}) collective-permute-start(bf16[4,4,26752]{2,1,0:T(4,128)(2,1)} %slice.813), channel_id=1, source_target_pairs={{0,16},{4,20},{8,24},{12,28},{16,0},{20,4},{24,8},{28,12},{1,17},{... | collective-permute-start | bytes 2568200 | tf_op jit(solution)/shard_map/ppermute | solution.py:79
  1033.7 52.6 %collective-permute-start.60 = (bf16[3,256,640]{2,1,0:T(8,128)(2,1)}, bf16[3,256,640]{2,1,0:T(8,128)(2,1)}, u32[]{:S(2)}, u32[]{:S(2)}) collective-permute-start(bf16[3,256,640]{2,1,0:T(8,128)(2,1)} %get-tuple-element.234), channel_id=1, source_target_pairs={{2,1},{3,2},{6,5},{7,6},{10,9},{11,10},{14,13},{15,14},{18,17},{19... | collective-permute-start | bytes 2949128 | tf_op jit(solution)/shard_map/ppermute | solution.py:194
  1035.3 37.7 %collective-permute-start.59 = (bf16[3,256,640]{2,1,0:T(8,128)(2,1)}, bf16[3,256,640]{2,1,0:T(8,128)(2,1)S(1)}, u32[]{:S(2)}, u32[]{:S(2)}) collective-permute-start(bf16[3,256,640]{2,1,0:T(8,128)(2,1)} %get-tuple-element.235), channel_id=1, source_target_pairs={{0,1},{1,2},{4,5},{5,6},{8,9},{9,10},{12,13},{13,14},{16,17},{17,1... | collective-permute-start | bytes 2949128 | tf_op jit(solution)/shard_map/ppermute | solution.py:193
  1090.6 68.3 %collective-permute-start.62 = (bf16[3,256,640]{2,1,0:T(8,128)(2,1)}, bf16[3,256,640]{2,1,0:T(8,128)(2,1)S(1)}, u32[]{:S(2)}, u32[]{:S(2)}) collective-permute-start(bf16[3,256,640]{2,1,0:T(8,128)(2,1)} %add_convert_fusion.13), channel_id=1, source_target_pairs={{1,0},{2,1},{3,2},{5,4},{6,5},{7,6},{9,8},{10,9},{11,10},{13,12},{... | collective-permute-start | bytes 2949128 | tf_op jit(solution)/shard_map/ppermute | solution.py:194
  1091.9 67.0 %collective-permute-start.61 = (bf16[3,256,640]{2,1,0:T(8,128)(2,1)S(1)}, bf16[3,256,640]{2,1,0:T(8,128)(2,1)S(1)}, u32[]{:S(2)}, u32[]{:S(2)}) collective-permute-start(bf16[3,256,640]{2,1,0:T(8,128)(2,1)S(1)} %add_convert_fusion.14), channel_id=1, source_target_pairs={{0,1},{1,2},{2,3},{4,5},{5,6},{6,7},{8,9},{9,10},{10,11},{12,13},{... | collective-permute-start | bytes 2949128 | tf_op jit(solution)/shard_map/ppermute | solution.py:193
  (160 other events, 1361.6 us)
Sparse Core Ops, SparseCore 0:
  12.1 43.3 all-gather.13
  57.6 54.7 all-gather.19
  301.5 80.1 all-gather.15
  383.1 79.2 all-gather.17
  464.5 75.2 reduce-scatter.4
  544.6 75.2 reduce-scatter.6
  631.9 76.5 reduce-scatter.8
  710.9 80.7 reduce-scatter.10
  793.2 80.3 all-gather.21
  875.0 79.2 all-gather.27
  955.9 112.1 all-gather.23
  1069.6 109.6 all-gather.25

commit v11 on v10

--- a/solution.py
+++ b/solution.py
@@ -17,6 +17,7 @@
 VMEM = 58 * 1024 * 1024
 BF = jnp.bfloat16
 F32 = jnp.float32
+EARLY = pl.CostEstimate(flops=14 * 10**9, bytes_accessed=1024, transcendentals=0)
 LITTLE = pl.CostEstimate(flops=1024, bytes_accessed=1024, transcendentals=0)
 
 
@@ -24,7 +25,7 @@
     return lax.dot_general(left, right, (dims, ((), ())), preferred_element_type=F32)
 
 
-def fence(values, *others):
+def fence(values, *others, cost=LITTLE):
     if not others:
         return list(values)
     place = pl.BlockSpec(memory_space=pl.ANY)
@@ -35,6 +36,7 @@
         out_shape=[jax.ShapeDtypeStruct(v.shape, v.dtype) for v in values],
         input_output_aliases={k: k for k in range(len(values))},
         compiler_params=pltpu.CompilerParams(vmem_limit_bytes=VMEM),
+        cost_estimate=cost,
         name="fence",
     )
     return list(call(*values, *others))
@@ -97,11 +99,11 @@
     return [pieces]
 
 
-def spread_end(some, size, before_last, before_core):
+def spread_end(some, size, before_last, before_core, cost=LITTLE):
     if len(some) > 1:
         own, by_x, by_y = some
         unit = own.shape[0] // 2
-        by_x, by_y = fence([by_x, by_y], *before_last)
+        by_x, by_y = fence([by_x, by_y], *before_last, cost=cost)
         got = [exchange(by_x[:unit], 2, size), exchange(by_y[unit:], 1, size)]
         half = assemble([own, by_x, got[1], got[0], by_y], *before_core)
     else:
@@ -589,7 +591,7 @@
     row = jnp.where(row < part, spot * part + row, head)
     order = (jnp.arange(head)[:, None] == row[None, :]).astype(BF)
 
-    w_r, came_r = spread_end(some_r, size, (), (z_gelu, order))
+    w_r, came_r = spread_end(some_r, size, (table,), (z_gelu, order, gain, par, lru), EARLY)
     first = (extended * first_rate * gain[0]).astype(BF)
     inputs, first_own, first_rate = extended[HALO:], first[HALO:], first_rate[HALO:]
     cut = d_model // 2
@@ -597,16 +599,14 @@
     keep = (rows, width, F32)
     dense = ((GROUP, 2 * GROUP), BF)
     some_g = spread_begin(z_gelu, size, *came_r)
-    rec_pre = dot(first[:, :cut], w_r[0])
-    w_r[1:] = fence(w_r[1:], *some_g[1:], rec_pre)
-    rec_pre = rec_pre + dot(first[:, cut:], w_r[1])
+    rec_pre = wide_dot(first, w_r)
     conv, decay, ig, dg, state, prod = kernel_call(
         forward_kernel, live_count, [rec_pre, par, lru, order], [keep] * 6,
         [((rows + HALO, GROUP), F32), dense], "recurrence",
     )
     ends = jnp.concatenate([prod[-1:], state[-1:]])
     came = [z_shift(ends, k, n, False) for k in range(1, n)]
-    w_g, came_g = spread_end(some_g, size, (), came)
+    w_g, came_g = spread_end(some_g, size, (ends,), came)
     carry = jnp.zeros((1, width), F32)
     for end in came[::-1]:
         carry = end[1:] + end[:1] * carry

time: 1200 us -> 1190 us (level)
  waiting for transfers between devices: 405 us -> 391 us
    unnamed x293 -> x281, local copies, waits for them, and re-layouts: 44.2 us -> 47 us
where the time goes in v11:
time: 1190 us
  waiting for transfers between devices  391 us (33%)
  matrix products  305 us (26%)
  Pallas kernels  138 us (12%)
  other arithmetic  135 us (11%)
  local copies, waits for them, and re-layouts  111 us (9%)
  starting transfers between devices  88.3 us (7%)
  between operations  17.4 us (1%)
    dot_general x34, matrix products, dot(): lax.dot_general(left, right, (dims, ((), ())), preferred_element_type=F32)  305 us
    ppermute x57, waiting for transfers between devices, swap(): return lax.ppermute(values, 'dp', [(k, k ^ mask) for k in range(size)])  237 us
    convert_element_type x21, other arithmetic, add_all(): return total.astype(BF)  63 us
    pallas_call x3, Pallas kernels, kernel_call(): pl.pallas_call(body, grid_spec=pltpu.PrefetchScalarGridSpec(num_scalar_pr...  62.2 us
    ppermute x3, waiting for transfers between devices, go(): lax.ppermute(left, 'tensor', [(k, k - 1) for k in range(max(n - t, 1), n)])  59.7 us
    ppermute x57, starting transfers between devices, swap(): return lax.ppermute(values, 'dp', [(k, k ^ mask) for k in range(size)])  49.7 us
    unnamed x281, local copies, waits for them, and re-layouts  47 us
    pallas_call x7, Pallas kernels, assemble(): pl.pallas_call(body, in_specs=[place] * (count + len(others)), out_specs=...  35.8 us
  transfers between devices with their start and end apart: 85, of which 45 were waited for; matrix products, arithmetic and copies ran while one was open for 43% of the time, Pallas kernels for 10%

profile of v11, /device:TPU:0, one launch (start us, length us, event | category | flops | bytes accessed | tf_op | source)
XLA Modules:
  0.0 1186.2 jit_solution(16525003421675100049)
XLA Ops:
  38.2 16.0 %collective-permute-done.1.refs_2_.refs_1_ = bf16[256,3072]{1,0:T(8,128)(2,1)S(1)} collective-permute-done((bf16[256,3072]{1,0:T(8,128)(2,1)}, bf16[256,3072]{1,0:T(8,128)(2,1)S(1)}, u32[]{:S(2)}, u32[]{:S(2)}) %collective-permute-start.1) | collective-permute-done | bytes 1572896 | tf_op jit(solution)/shard_map/ppermute | solution.py:81
  74.3 32.6 %collective-permute-done.4 = bf16[320,640]{1,0:T(8,128)(2,1)} collective-permute-done((bf16[320,640]{1,0:T(8,128)(2,1)}, bf16[320,640]{1,0:T(8,128)(2,1)}, u32[]{:S(2)}, u32[]{:S(2)}) %collective-permute-start.4) | collective-permute-done | bytes 409632 | tf_op jit(solution)/shard_map/ppermute | solution.py:81
  142.5 6.2 collective-permute-done.12
  148.7 4.9 fusion.46
  153.6 7.3 convolution_add_fusion.pre_ref
  160.9 18.8 %recurrence.1 = (f32[512,2560]{1,0:T(8,128)}, f32[512,2560]{1,0:T(8,128)}, f32[512,2560]{1,0:T(8,128)}, f32[512,2560]{1,0:T(8,128)}, f32[512,2560]{1,0:T(8,128)}, /*index=5*/f32[512,2560]{1,0:T(8,128)}) custom-call(s32[1]{0:T(128)} %sub.38.live_ref, f32[528,2560]{1,0:T(8,128)} %convolution_add_fusion.pre_ref, f32[8,2560]{1,0:T(8,128)} %pad_maximum_fusion.14.refs_8_.par_ref, ...), custom_call_target="tpu_custom_call" | custom-call | flops 1024 | bytes 1024 | tf_op jit(solution)/shard_map/recurrence/pallas_call | solution.py:496
  188.1 5.5 collective-permute-start.17
  223.3 9.7 fusion.22
  233.1 10.2 collective-permute-done.20.refs_1_
  249.4 14.2 %collective-permute-done.21.refs_2_.refs_3_ = bf16[128,2560]{1,0:T(8,128)(2,1)S(1)} collective-permute-done((bf16[128,2560]{1,0:T(8,128)(2,1)S(1)}, bf16[128,2560]{1,0:T(8,128)(2,1)S(1)}, u32[]{:S(2)}, u32[]{:S(2)}) %collective-permute-start.21) | collective-permute-done | bytes 655392 | tf_op jit(solution)/shard_map/ppermute | solution.py:81
  283.4 4.9 fusion.85
  297.7 6.1 assemble.10.refs_0_
  307.7 18.9 %collective-permute-done.28.refs_4_ = bf16[256,1536]{1,0:T(8,128)(2,1)S(1)} collective-permute-done((bf16[256,1536]{1,0:T(8,128)(2,1)}, bf16[256,1536]{1,0:T(8,128)(2,1)S(1)}, u32[]{:S(2)}, u32[]{:S(2)}) %collective-permute-start.28) | collective-permute-done | bytes 786464 | tf_op jit(solution)/shard_map/ppermute | solution.py:81
  328.4 9.1 collective-permute-done.29.refs_2_
  342.6 5.2 collective-permute-done.31.refs_1_
  354.2 5.8 permute.8
  360.0 5.9 permute.7
  366.4 9.3 assemble.11
  375.7 19.2 %fusion.86 = f32[1024,3072]{1,0:T(8,128)} fusion(bf16[1024,2048]{1,0:T(8,128)(2,1)} %all-gather.16.cloned.1.call-done, bf16[2048,3072]{1,0:T(8,128)(2,1)} %assemble.11), kind=kOutput, calls=%fused_computation.262 | convolution fusion | flops 12884901888 | bytes 29360128 | tf_op jit(solution)/shard_map/dot_general | solution.py:25
  394.8 16.0 %fusion.6 = (bf16[1024,1536]{1,0:T(8,128)(2,1)S(1)}, bf16[1024,1536]{1,0:T(8,128)(2,1)S(1)}, bf16[1024,1536]{1,0:T(8,128)(2,1)}) fusion(f32[1024,3072]{1,0:T(8,128)} %fusion.86, bf16[1024,2048]{1,0:T(8,128)(2,1)S(1)} %copy-done.38, bf16[2048,1536]{1,0:T(8,128)(2,1)} %assemble.13), kind=kOutput, calls=%fused_computation.15 | convolution fusion | flops 6483345408 | bytes 32505856 | tf_op jit(solution)/shard_map/dot_general | solution.py:25
  412.5 17.5 %convolution_convert_fusion.7.refs_1_ = bf16[1024,2048]{1,0:T(8,128)(2,1)} fusion(bf16[2048,3072]{1,0:T(8,128)(2,1)} %assemble.11, bf16[1024,1536]{1,0:T(8,128)(2,1)S(1)} %get-tuple-element.207, bf16[1024,1536]{1,0:T(8,128)(2,1)S(1)} %get-tuple-element.206), kind=kOutput, calls=%fused_computation.72 | convolution fusion | flops 12899581952 | bytes 23068672 | tf_op jit(solution)/shard_map/dot_general | solution.py:25
  430.3 24.0 %all-gather.18.cloned.1.call-done.refs_0_ = bf16[1024,2048]{1,0:T(8,128)(2,1)} async-done(((bf16[256,2048]{1,0:T(8,128)(2,1)}), bf16[1024,2048]{1,0:T(8,128)(2,1)}) %all-gather.18.cloned.1.call-update) | async-done | bytes 4194320 | tf_op jit(solution)/shard_map/all_gather | solution.py:632
  454.3 19.1 %fusion.87 = f32[1024,3072]{1,0:T(8,128)} fusion(bf16[1024,2048]{1,0:T(8,128)(2,1)} %fence.44, bf16[2048,3072]{1,0:T(8,128)(2,1)} %assemble.11), kind=kOutput, calls=%fused_computation.263 | convolution fusion | flops 12884901888 | bytes 29360128 | tf_op jit(solution)/shard_map/dot_general | solution.py:25
  473.5 15.4 %fusion.13 = (bf16[1024,1536]{1,0:T(8,128)(2,1)}, bf16[1024,1536]{1,0:T(8,128)(2,1)}, bf16[1024,1536]{1,0:T(8,128)(2,1)}) fusion(f32[1024,3072]{1,0:T(8,128)} %fusion.87, bf16[1024,2048]{1,0:T(8,128)(2,1)S(1)} %copy-done.36, bf16[2048,1536]{1,0:T(8,128)(2,1)S(1)} %bitcast.192), kind=kOutput, calls=%fused_computation.22 | convolution fusion | flops 6483345408 | bytes 32505856 | tf_op jit(solution)/shard_map/dot_general | solution.py:25
  488.9 5.6 pad_maximum_fusion.refs_1_
  494.4 18.7 %convolution_convert_fusion.6.refs_2_ = bf16[1024,2048]{1,0:T(8,128)(2,1)} fusion(bf16[2048,3072]{1,0:T(8,128)(2,1)} %assemble.11, bf16[1024,1536]{1,0:T(8,128)(2,1)} %get-tuple-element.205, bf16[1024,1536]{1,0:T(8,128)(2,1)S(1)} %copy-done.62), kind=kOutput, calls=%fused_computation.71 | convolution fusion | flops 12899581952 | bytes 23068672 | tf_op jit(solution)/shard_map/dot_general | solution.py:25
  515.0 5.7 pad_maximum_fusion.1.refs_1_
  520.7 7.4 fusion.37
  528.2 8.4 convolution_convert_fusion.9.refs_6_.refs_0_
  536.7 9.7 add_convert_fusion.2
  546.4 9.7 fusion.31
  556.1 11.8 add_convert_fusion
  568.4 11.0 fusion.34
  579.5 11.2 convolution_convert_fusion.8.refs_7_.refs_1_
  590.7 5.4 fusion.40
  596.1 7.1 add_convert_fusion.3
  603.2 10.2 add_convert_fusion.1
  636.4 5.7 fusion.52
  647.4 17.1 %back_scan.1 = (f32[512,2560]{1,0:T(8,128)}, f32[512,2560]{1,0:T(8,128)}, f32[8,2560]{1,0:T(8,128)}, bf16[512,2560]{1,0:T(8,128)(2,1)}) custom-call(s32[1]{0:T(128)} %sub.38.live_ref, f32[512,2560]{1,0:T(8,128)} %get-tuple-element.276.refs_2_.pre_ref, f32[512,2560]{1,0:T(8,128)} %convolution_add_fusion.1.grad_ref, f32[512,2560]{1,0:T(8,128)} %get-tuple-element.88.decay_ref, ...), custom_call_target="tpu_custom_call" | custom-call | flops 1024 | bytes 1024 | tf_op jit(solution)/shard_map/back_scan/pallas_call | solution.py:496
  669.4 10.9 collective-permute-done.37.refs_4_
  682.1 26.3 %recurrence_back.1 = (f32[528,2560]{1,0:T(8,128)}, f32[8,2560]{1,0:T(8,128)}, bf16[4,160,1280]{2,1,0:T(8,128)(2,1)}) custom-call(s32[1]{0:T(128)} %sub.38.live_ref, f32[528,2560]{1,0:T(8,128)} %convolution_add_fusion.pre_ref, f32[8,2560]{1,0:T(8,128)} %pad_maximum_fusion.14.refs_8_.par_ref, bf16[8,4,80,640]{3,2,1,0:T(8,128)(2,1)} %copy-done.6, ...), custom_call_target="tpu_custom_call" | custom-call | flops 1024 | bytes 1024 | tf_op jit(solution)/shard_map/recurrence_back/pallas_call | solution.py:496
  711.4 7.6 fusion.88
  719.0 6.8 fusion.89
  729.9 5.8 fusion.90
  735.8 5.0 fusion.91
  743.3 6.1 add_convert_fusion.4.in_ref
  754.6 6.6 convolution_convert_fusion.5
  762.7 7.4 collective-permute-done.42.refs_2_
  770.1 7.5 convolution_convert_fusion.3
  778.0 6.0 convolution_convert_fusion
  784.4 7.4 convolution_convert_fusion.2
  822.1 16.6 %collective-permute-done.45.refs_3_ = bf16[256,2560]{1,0:T(8,128)(2,1)S(1)} collective-permute-done((bf16[256,2560]{1,0:T(8,128)(2,1)S(1)}, bf16[256,2560]{1,0:T(8,128)(2,1)S(1)}, u32[]{:S(2)}, u32[]{:S(2)}) %collective-permute-start.45) | collective-permute-done | bytes 1310752 | tf_op jit(solution)/shard_map/ppermute | solution.py:81
  850.5 15.1 %all-gather.22.cloned.1.call-done = bf16[1024,2048]{1,0:T(8,128)(2,1)} async-done(((bf16[256,2048]{1,0:T(8,128)(2,1)}), bf16[1024,2048]{1,0:T(8,128)(2,1)}) %all-gather.22.cloned.1.call-update) | async-done | bytes 4194320 | tf_op jit(solution)/shard_map/all_gather | solution.py:706
  865.7 4.9 collective-permute-done.46.refs_3_
  882.2 8.5 collective-permute-done.48
  895.3 9.5 collective-permute-done.50
  909.3 21.1 %collective-permute-done.53.refs_3_ = bf16[256,2560]{1,0:T(8,128)(2,1)S(1)} collective-permute-done((bf16[256,2560]{1,0:T(8,128)(2,1)}, bf16[256,2560]{1,0:T(8,128)(2,1)S(1)}, u32[]{:S(2)}, u32[]{:S(2)}) %collective-permute-start.53) | collective-permute-done | bytes 1310752 | tf_op jit(solution)/shard_map/ppermute | solution.py:81
  971.2 33.2 %collective-permute-done.57.refs_0_.refs_3_ = bf16[3,256,640]{2,1,0:T(8,128)(2,1)S(1)} collective-permute-done((bf16[3,256,640]{2,1,0:T(8,128)(2,1)S(1)}, bf16[3,256,640]{2,1,0:T(8,128)(2,1)S(1)}, u32[]{:S(2)}, u32[]{:S(2)}) %collective-permute-start.57) | collective-permute-done | bytes 983072 | tf_op jit(solution)/shard_map/ppermute | solution.py:195
  1047.5 7.5 collective-permute-done.63
  1056.5 7.4 collective-permute-done.64
  1067.1 7.0 interleave.3
  1093.4 59.6 %collective-permute-done.62.refs_3_ = bf16[3,256,640]{2,1,0:T(8,128)(2,1)S(1)} collective-permute-done((bf16[3,256,640]{2,1,0:T(8,128)(2,1)}, bf16[3,256,640]{2,1,0:T(8,128)(2,1)S(1)}, u32[]{:S(2)}, u32[]{:S(2)}) %collective-permute-start.62) | collective-permute-done | bytes 983072 | tf_op jit(solution)/shard_map/ppermute | solution.py:196
  1157.6 14.3 %all-gather.26.cloned.1.call-done = bf16[1024,2048]{1,0:T(8,128)(2,1)} async-done(((bf16[256,2048]{1,0:T(8,128)(2,1)}), bf16[1024,2048]{1,0:T(8,128)(2,1)}) %all-gather.26.cloned.1.call-update) | async-done | bytes 4194320 | tf_op jit(solution)/shard_map/all_gather | solution.py:718
  1171.9 7.0 interleave.2
  (644 shorter events, 407.3 us)
Async XLA Ops:
  7.2 48.5 %all-gather.14.cloned.1.call-start = ((), (), s32[]{:S(2)}) async-start(), calls=%async_computation.4 | async-start | bytes 2150400 | tf_op jit(solution)/shard_map/all_gather | solution.py:569
  12.0 116.0 %all-gather.20.cloned.1.call-start = ((), (), s32[]{:S(2)}) async-start(), calls=%async_computation.11 | async-start | bytes 3276800 | tf_op jit(solution)/shard_map/all_gather | solution.py:570
  15.5 38.7 %collective-permute-start.1 = (bf16[256,3072]{1,0:T(8,128)(2,1)}, bf16[256,3072]{1,0:T(8,128)(2,1)S(1)}, u32[]{:S(2)}, u32[]{:S(2)}) collective-permute-start(bf16[256,3072]{1,0:T(8,128)(2,1)} %pad_maximum_fusion.8.refs_0_), channel_id=1, source_target_pairs={{0,16},{4,20},{8,24},{12,28},{16,0},{20,4},{24,8},{28,12},{1,17},{... | collective-permute-start | bytes 4718600 | tf_op jit(solution)/shard_map/ppermute | solution.py:81
  19.6 36.1 %collective-permute-start = (bf16[256,3072]{1,0:T(8,128)(2,1)}, bf16[256,3072]{1,0:T(8,128)(2,1)S(1)}, u32[]{:S(2)}, u32[]{:S(2)}) collective-permute-start(bf16[256,3072]{1,0:T(8,128)(2,1)} %pad_maximum_fusion.8.refs_0_), channel_id=1, source_target_pairs={{0,8},{4,12},{8,0},{12,4},{16,24},{20,28},{24,16},{28,20},{1,9},{5... | collective-permute-start | bytes 4718600 | tf_op jit(solution)/shard_map/ppermute | solution.py:81
  59.5 53.1 %collective-permute-start.7 = (bf16[256,2560]{1,0:T(8,128)(2,1)}, bf16[256,2560]{1,0:T(8,128)(2,1)}, u32[]{:S(2)}, u32[]{:S(2)}) collective-permute-start(bf16[256,2560]{1,0:T(8,128)(2,1)} %bitcast.76.refs_0_), channel_id=1, source_target_pairs={{0,16},{4,20},{8,24},{12,28},{16,0},{20,4},{24,8},{28,12},{1,17},{... | collective-permute-start | bytes 3932168 | tf_op jit(solution)/shard_map/ppermute | solution.py:81
  60.3 52.3 %collective-permute-start.6 = (bf16[256,2560]{1,0:T(8,128)(2,1)}, bf16[256,2560]{1,0:T(8,128)(2,1)}, u32[]{:S(2)}, u32[]{:S(2)}) collective-permute-start(bf16[256,2560]{1,0:T(8,128)(2,1)} %bitcast.76.refs_0_), channel_id=1, source_target_pairs={{0,8},{4,12},{8,0},{12,4},{16,24},{20,28},{24,16},{28,20},{1,9},{5... | collective-permute-start | bytes 3932168 | tf_op jit(solution)/shard_map/ppermute | solution.py:81
  68.8 38.1 %collective-permute-start.4 = (bf16[320,640]{1,0:T(8,128)(2,1)}, bf16[320,640]{1,0:T(8,128)(2,1)}, u32[]{:S(2)}, u32[]{:S(2)}) collective-permute-start(bf16[320,640]{1,0:T(8,128)(2,1)} %bitcast.8), channel_id=1, source_target_pairs={{0,16},{4,20},{8,24},{12,28},{16,0},{20,4},{24,8},{28,12},{1,17},{... | collective-permute-start | bytes 1228808 | tf_op jit(solution)/shard_map/ppermute | solution.py:81
  70.0 36.8 %collective-permute-start.3 = (bf16[320,640]{1,0:T(8,128)(2,1)}, bf16[320,640]{1,0:T(8,128)(2,1)}, u32[]{:S(2)}, u32[]{:S(2)}) collective-permute-start(bf16[320,640]{1,0:T(8,128)(2,1)} %bitcast.8), channel_id=1, source_target_pairs={{0,24},{4,28},{8,16},{12,20},{16,8},{20,12},{24,0},{28,4},{1,25},{... | collective-permute-start | bytes 1228808 | tf_op jit(solution)/shard_map/ppermute | solution.py:81
  70.8 37.0 %collective-permute-start.2 = (bf16[320,640]{1,0:T(8,128)(2,1)}, bf16[320,640]{1,0:T(8,128)(2,1)}, u32[]{:S(2)}, u32[]{:S(2)}) collective-permute-start(bf16[320,640]{1,0:T(8,128)(2,1)} %bitcast.8), channel_id=1, source_target_pairs={{0,8},{4,12},{8,0},{12,4},{16,24},{20,28},{24,16},{28,20},{1,9},{5... | collective-permute-start | bytes 1228808 | tf_op jit(solution)/shard_map/ppermute | solution.py:81
  73.0 302.7 %all-gather.16.cloned.1.call-start = ((), (), s32[]{:S(2)}) async-start(), calls=%async_computation.5 | async-start | bytes 5242880 | tf_op jit(solution)/shard_map/all_gather | solution.py:632
  116.7 17.4 %collective-permute-start.9 = (bf16[128,2560]{1,0:T(8,128)(2,1)}, bf16[128,2560]{1,0:T(8,128)(2,1)}, u32[]{:S(2)}, u32[]{:S(2)}) collective-permute-start(bf16[128,2560]{1,0:T(8,128)(2,1)} %slice.532), channel_id=1, source_target_pairs={{0,8},{4,12},{8,0},{12,4},{16,24},{20,28},{24,16},{28,20},{1,9},{5... | collective-permute-start | bytes 1966088 | tf_op jit(solution)/shard_map/ppermute | solution.py:81
  118.1 17.2 %collective-permute-start.8 = (bf16[128,2560]{1,0:T(8,128)(2,1)}, bf16[128,2560]{1,0:T(8,128)(2,1)}, u32[]{:S(2)}, u32[]{:S(2)}) collective-permute-start(bf16[128,2560]{1,0:T(8,128)(2,1)} %slice.531), channel_id=1, source_target_pairs={{0,16},{4,20},{8,24},{12,28},{16,0},{20,4},{24,8},{28,12},{1,17},{... | collective-permute-start | bytes 1966088 | tf_op jit(solution)/shard_map/ppermute | solution.py:81
  141.0 41.1 %collective-permute-start.11 = (bf16[256,2560]{1,0:T(8,128)(2,1)}, bf16[256,2560]{1,0:T(8,128)(2,1)S(1)}, u32[]{:S(2)}, u32[]{:S(2)}) collective-permute-start(bf16[256,2560]{1,0:T(8,128)(2,1)} %fence.37.refs_0_), channel_id=1, source_target_pairs={{0,16},{4,20},{8,24},{12,28},{16,0},{20,4},{24,8},{28,12},{1,17},{... | collective-permute-start | bytes 3932168 | tf_op jit(solution)/shard_map/ppermute | solution.py:81
  142.0 40.2 %collective-permute-start.10 = (bf16[256,2560]{1,0:T(8,128)(2,1)}, bf16[256,2560]{1,0:T(8,128)(2,1)S(1)}, u32[]{:S(2)}, u32[]{:S(2)}) collective-permute-start(bf16[256,2560]{1,0:T(8,128)(2,1)} %fence.37.refs_0_), channel_id=1, source_target_pairs={{0,8},{4,12},{8,0},{12,4},{16,24},{20,28},{24,16},{28,20},{1,9},{5... | collective-permute-start | bytes 3932168 | tf_op jit(solution)/shard_map/ppermute | solution.py:81
  186.6 16.8 %collective-permute-start.13 = (bf16[128,2560]{1,0:T(8,128)(2,1)S(1)}, bf16[128,2560]{1,0:T(8,128)(2,1)S(1)}, u32[]{:S(2)}, u32[]{:S(2)}) collective-permute-start(bf16[128,2560]{1,0:T(8,128)(2,1)S(1)} %slice.541), channel_id=1, source_target_pairs={{0,8},{4,12},{8,0},{12,4},{16,24},{20,28},{24,16},{28,20},{1,9},{5... | collective-permute-start | bytes 1966088 | tf_op jit(solution)/shard_map/ppermute | solution.py:81
  187.2 16.5 %collective-permute-start.14 = (bf16[128,2560]{1,0:T(8,128)(2,1)S(1)}, bf16[128,2560]{1,0:T(8,128)(2,1)S(1)}, u32[]{:S(2)}, u32[]{:S(2)}) collective-permute-start(bf16[128,2560]{1,0:T(8,128)(2,1)S(1)} %slice.542), channel_id=1, source_target_pairs={{0,16},{4,20},{8,24},{12,28},{16,0},{20,4},{24,8},{28,12},{1,17},{... | collective-permute-start | bytes 1966088 | tf_op jit(solution)/shard_map/ppermute | solution.py:81
  211.9 31.4 %collective-permute-start.20 = (bf16[256,2560]{1,0:T(8,128)(2,1)}, bf16[256,2560]{1,0:T(8,128)(2,1)S(1)}, u32[]{:S(2)}, u32[]{:S(2)}) collective-permute-start(bf16[256,2560]{1,0:T(8,128)(2,1)} %fence.39.refs_0_), channel_id=1, source_target_pairs={{0,16},{4,20},{8,24},{12,28},{16,0},{20,4},{24,8},{28,12},{1,17},{... | collective-permute-start | bytes 3932168 | tf_op jit(solution)/shard_map/ppermute | solution.py:81
  212.8 31.1 %collective-permute-start.19 = (bf16[256,2560]{1,0:T(8,128)(2,1)}, bf16[256,2560]{1,0:T(8,128)(2,1)S(1)}, u32[]{:S(2)}, u32[]{:S(2)}) collective-permute-start(bf16[256,2560]{1,0:T(8,128)(2,1)} %fence.39.refs_0_), channel_id=1, source_target_pairs={{0,8},{4,12},{8,0},{12,4},{16,24},{20,28},{24,16},{28,20},{1,9},{5... | collective-permute-start | bytes 3932168 | tf_op jit(solution)/shard_map/ppermute | solution.py:81
  247.2 16.3 %collective-permute-start.21 = (bf16[128,2560]{1,0:T(8,128)(2,1)S(1)}, bf16[128,2560]{1,0:T(8,128)(2,1)S(1)}, u32[]{:S(2)}, u32[]{:S(2)}) collective-permute-start(bf16[128,2560]{1,0:T(8,128)(2,1)S(1)} %slice.551), channel_id=1, source_target_pairs={{0,8},{4,12},{8,0},{12,4},{16,24},{20,28},{24,16},{28,20},{1,9},{5... | collective-permute-start | bytes 1966088 | tf_op jit(solution)/shard_map/ppermute | solution.py:81
  248.2 16.0 %collective-permute-start.22 = (bf16[128,2560]{1,0:T(8,128)(2,1)S(1)}, bf16[128,2560]{1,0:T(8,128)(2,1)S(1)}, u32[]{:S(2)}, u32[]{:S(2)}) collective-permute-start(bf16[128,2560]{1,0:T(8,128)(2,1)S(1)} %slice.552), channel_id=1, source_target_pairs={{0,16},{4,20},{8,24},{12,28},{16,0},{20,4},{24,8},{28,12},{1,17},{... | collective-permute-start | bytes 1966088 | tf_op jit(solution)/shard_map/ppermute | solution.py:81
  276.6 20.1 %collective-permute-start.24 = (bf16[128,3072]{1,0:T(8,128)(2,1)}, bf16[128,3072]{1,0:T(8,128)(2,1)S(1)}, u32[]{:S(2)}, u32[]{:S(2)}) collective-permute-start(bf16[128,3072]{1,0:T(8,128)(2,1)} %slice.556), channel_id=1, source_target_pairs={{0,8},{4,12},{8,0},{12,4},{16,24},{20,28},{24,16},{28,20},{1,9},{5... | collective-permute-start | bytes 2359304 | tf_op jit(solution)/shard_map/ppermute | solution.py:81
  277.7 20.0 %collective-permute-start.25 = (bf16[128,3072]{1,0:T(8,128)(2,1)}, bf16[128,3072]{1,0:T(8,128)(2,1)}, u32[]{:S(2)}, u32[]{:S(2)}) collective-permute-start(bf16[128,3072]{1,0:T(8,128)(2,1)} %slice.557), channel_id=1, source_target_pairs={{0,16},{4,20},{8,24},{12,28},{16,0},{20,4},{24,8},{28,12},{1,17},{... | collective-permute-start | bytes 2359304 | tf_op jit(solution)/shard_map/ppermute | solution.py:81
  292.5 161.8 %all-gather.18.cloned.1.call-start = ((), (), s32[]{:S(2)}) async-start(), calls=%async_computation.6 | async-start | bytes 5242880 | tf_op jit(solution)/shard_map/all_gather | solution.py:632
  303.8 62.6 %collective-permute-start.26 = (bf16[1024,3072]{1,0:T(8,128)(2,1)}, bf16[1024,3072]{1,0:T(8,128)(2,1)}, u32[]{:S(2)}, u32[]{:S(2)}) collective-permute-start(bf16[1024,3072]{1,0:T(8,128)(2,1)} %assemble.10.refs_0_), channel_id=1, source_target_pairs={{0,4},{4,0},{8,12},{12,8},{16,20},{20,16},{24,28},{28,24},{1,5},{5... | collective-permute-start | bytes 18874376 | tf_op jit(solution)/shard_map/ppermute | solution.py:81
  306.4 20.1 %collective-permute-start.28 = (bf16[256,1536]{1,0:T(8,128)(2,1)}, bf16[256,1536]{1,0:T(8,128)(2,1)S(1)}, u32[]{:S(2)}, u32[]{:S(2)}) collective-permute-start(bf16[256,1536]{1,0:T(8,128)(2,1)} %fence.43.refs_0_), channel_id=1, source_target_pairs={{0,16},{4,20},{8,24},{12,28},{16,0},{20,4},{24,8},{28,12},{1,17},{... | collective-permute-start | bytes 2359304 | tf_op jit(solution)/shard_map/ppermute | solution.py:81
  306.7 20.5 %collective-permute-start.27 = (bf16[256,1536]{1,0:T(8,128)(2,1)}, bf16[256,1536]{1,0:T(8,128)(2,1)S(1)}, u32[]{:S(2)}, u32[]{:S(2)}) collective-permute-start(bf16[256,1536]{1,0:T(8,128)(2,1)} %fence.43.refs_0_), channel_id=1, source_target_pairs={{0,8},{4,12},{8,0},{12,4},{16,24},{20,28},{24,16},{28,20},{1,9},{5... | collective-permute-start | bytes 2359304 | tf_op jit(solution)/shard_map/ppermute | solution.py:81
  365.9 258.1 %reduce-scatter.5.cloned.1.call-start = ((), (), s32[]{:S(2)}) async-start(), calls=%async_computation.7 | async-start | bytes 5242880 | tf_op jit(solution)/shard_map/reduce_scatter | solution.py:641
  430.1 193.9 %reduce-scatter.7.cloned.1.call-start = ((), (), s32[]{:S(2)}) async-start(), calls=%async_computation.8 | async-start | bytes 5242880 | tf_op jit(solution)/shard_map/reduce_scatter | solution.py:641
  536.6 189.6 %reduce-scatter.9.cloned.1.call-start = ((), (), s32[]{:S(2)}) async-start(), calls=%async_computation.9 | async-start | bytes 5242880 | tf_op jit(solution)/shard_map/reduce_scatter | solution.py:666
  546.4 67.0 %collective-permute-start.32 = (bf16[1024,1536]{1,0:T(8,128)(2,1)}, bf16[1024,1536]{1,0:T(8,128)(2,1)S(1)}, u32[]{:S(2)}, u32[]{:S(2)}) collective-permute-start(bf16[1024,1536]{1,0:T(8,128)(2,1)} %add_convert_fusion.2), channel_id=1, source_target_pairs={{0,4},{4,0},{8,12},{12,8},{16,20},{20,16},{24,28},{28,24},{1,5},{5... | collective-permute-start | bytes 9437192 | tf_op jit(solution)/shard_map/ppermute | solution.py:81
  567.9 51.3 %collective-permute-start.33 = (bf16[1024,3072]{1,0:T(8,128)(2,1)}, bf16[1024,3072]{1,0:T(8,128)(2,1)}, u32[]{:S(2)}, u32[]{:S(2)}) collective-permute-start(bf16[1024,3072]{1,0:T(8,128)(2,1)} %add_convert_fusion), channel_id=1, source_target_pairs={{0,4},{4,0},{8,12},{12,8},{16,20},{20,16},{24,28},{28,24},{1,5},{5... | collective-permute-start | bytes 18874376 | tf_op jit(solution)/shard_map/ppermute | solution.py:81
  624.0 167.7 %reduce-scatter.11.cloned.1.call-start = ((), (), s32[]{:S(2)}) async-start(), calls=%async_computation.10 | async-start | bytes 5242880 | tf_op jit(solution)/shard_map/reduce_scatter | solution.py:666
  627.0 39.8 %collective-permute-start.35 = (bf16[256,1536]{1,0:T(8,128)(2,1)}, bf16[256,1536]{1,0:T(8,128)(2,1)}, u32[]{:S(2)}, u32[]{:S(2)}) collective-permute-start(bf16[256,1536]{1,0:T(8,128)(2,1)} %get-tuple-element.238.refs_3_), channel_id=1, source_target_pairs={{0,16},{4,20},{8,24},{12,28},{16,0},{20,4},{24,8},{28,12},{1,17},{... | collective-permute-start | bytes 2359304 | tf_op jit(solution)/shard_map/ppermute | solution.py:81
  628.3 39.8 %collective-permute-start.34 = (bf16[256,1536]{1,0:T(8,128)(2,1)}, bf16[256,1536]{1,0:T(8,128)(2,1)}, u32[]{:S(2)}, u32[]{:S(2)}) collective-permute-start(bf16[256,1536]{1,0:T(8,128)(2,1)} %get-tuple-element.239.refs_2_), channel_id=1, source_target_pairs={{0,8},{4,12},{8,0},{12,4},{16,24},{20,28},{24,16},{28,20},{1,9},{5... | collective-permute-start | bytes 2359304 | tf_op jit(solution)/shard_map/ppermute | solution.py:81
  629.7 50.6 %collective-permute-start.37 = (bf16[256,3072]{1,0:T(8,128)(2,1)}, bf16[256,3072]{1,0:T(8,128)(2,1)}, u32[]{:S(2)}, u32[]{:S(2)}) collective-permute-start(bf16[256,3072]{1,0:T(8,128)(2,1)} %get-tuple-element.212.refs_5_), channel_id=1, source_target_pairs={{0,16},{4,20},{8,24},{12,28},{16,0},{20,4},{24,8},{28,12},{1,17},{... | collective-permute-start | bytes 4718600 | tf_op jit(solution)/shard_map/ppermute | solution.py:81
  630.3 51.1 %collective-permute-start.36 = (bf16[256,3072]{1,0:T(8,128)(2,1)}, bf16[256,3072]{1,0:T(8,128)(2,1)}, u32[]{:S(2)}, u32[]{:S(2)}) collective-permute-start(bf16[256,3072]{1,0:T(8,128)(2,1)} %get-tuple-element.213.refs_4_), channel_id=1, source_target_pairs={{0,8},{4,12},{8,0},{12,4},{16,24},{20,28},{24,16},{28,20},{1,9},{5... | collective-permute-start | bytes 4718600 | tf_op jit(solution)/shard_map/ppermute | solution.py:81
  632.9 232.8 %all-gather.22.cloned.1.call-start = ((), (), s32[]{:S(2)}) async-start(), calls=%async_computation.12 | async-start | bytes 5242880 | tf_op jit(solution)/shard_map/all_gather | solution.py:706
  665.4 16.0 %collective-permute-start.40 = (f32[2,2560]{1,0:T(2,128)S(1)}, f32[2,2560]{1,0:T(2,128)S(1)}, u32[]{:S(2)}, u32[]{:S(2)}) collective-permute-start(f32[2,2560]{1,0:T(2,128)S(1)} %pad_maximum_fusion.16), channel_id=1, source_target_pairs={{3,0},{7,4},{11,8},{15,12},{19,16},{23,20},{27,24},{31,28}} | collective-permute-start | bytes 61448 | tf_op jit(solution)/shard_map/ppermute | solution.py:168
  709.4 16.7 %collective-permute-start.41 = (f32[16,2560]{1,0:T(8,128)S(1)}, f32[16,2560]{1,0:T(8,128)S(1)}, u32[]{:S(2)}, u32[]{:S(2)}) collective-permute-start(f32[16,2560]{1,0:T(8,128)S(1)} %slice.592), channel_id=1, source_target_pairs={{1,0},{2,1},{3,2},{5,4},{6,5},{7,6},{9,8},{10,9},{11,10},{13,12},{... | collective-permute-start | bytes 491528 | tf_op jit(solution)/shard_map/ppermute | solution.py:168
  762.7 208.5 %all-gather.28.cloned.1.call-start = ((), (), s32[]{:S(2)}) async-start(), calls=%async_computation.15 | async-start | bytes 5242880 | tf_op jit(solution)/shard_map/all_gather | solution.py:706
  777.6 40.6 %collective-permute-start.43 = (bf16[1024,2560]{1,0:T(8,128)(2,1)}, bf16[1024,2560]{1,0:T(8,128)(2,1)}, u32[]{:S(2)}, u32[]{:S(2)}) collective-permute-start(bf16[1024,2560]{1,0:T(8,128)(2,1)} %convolution_convert_fusion.3), channel_id=1, source_target_pairs={{0,4},{4,0},{8,12},{12,8},{16,20},{20,16},{24,28},{28,24},{1,5},{5... | collective-permute-start | bytes 15728648 | tf_op jit(solution)/shard_map/ppermute | solution.py:81
  777.8 301.9 %all-gather.24.cloned.1.call-start = ((), (), s32[]{:S(2)}) async-start(), calls=%async_computation.13 | async-start | bytes 5242880 | tf_op jit(solution)/shard_map/all_gather | solution.py:718
  784.0 62.6 %collective-permute-start.52 = (bf16[1024,2560]{1,0:T(8,128)(2,1)}, bf16[1024,2560]{1,0:T(8,128)(2,1)}, u32[]{:S(2)}, u32[]{:S(2)}) collective-permute-start(bf16[1024,2560]{1,0:T(8,128)(2,1)} %convolution_convert_fusion), channel_id=1, source_target_pairs={{0,4},{4,0},{8,12},{12,8},{16,20},{20,16},{24,28},{28,24},{1,5},{5... | collective-permute-start | bytes 15728648 | tf_op jit(solution)/shard_map/ppermute | solution.py:81
  807.8 30.9 %collective-permute-start.45 = (bf16[256,2560]{1,0:T(8,128)(2,1)S(1)}, bf16[256,2560]{1,0:T(8,128)(2,1)S(1)}, u32[]{:S(2)}, u32[]{:S(2)}) collective-permute-start(bf16[256,2560]{1,0:T(8,128)(2,1)S(1)} %get-tuple-element.230), channel_id=1, source_target_pairs={{0,16},{4,20},{8,24},{12,28},{16,0},{20,4},{24,8},{28,12},{1,17},{... | collective-permute-start | bytes 3932168 | tf_op jit(solution)/shard_map/ppermute | solution.py:81
  808.8 30.6 %collective-permute-start.44 = (bf16[256,2560]{1,0:T(8,128)(2,1)S(1)}, bf16[256,2560]{1,0:T(8,128)(2,1)S(1)}, u32[]{:S(2)}, u32[]{:S(2)}) collective-permute-start(bf16[256,2560]{1,0:T(8,128)(2,1)S(1)} %get-tuple-element.231), channel_id=1, source_target_pairs={{0,8},{4,12},{8,0},{12,4},{16,24},{20,28},{24,16},{28,20},{1,9},{5... | collective-permute-start | bytes 3932168 | tf_op jit(solution)/shard_map/ppermute | solution.py:81
  840.5 30.1 %collective-permute-start.46 = (bf16[256,2560]{1,0:T(8,128)(2,1)}, bf16[256,2560]{1,0:T(8,128)(2,1)S(1)}, u32[]{:S(2)}, u32[]{:S(2)}) collective-permute-start(bf16[256,2560]{1,0:T(8,128)(2,1)} %get-tuple-element.100), channel_id=1, source_target_pairs={{0,8},{4,12},{8,0},{12,4},{16,24},{20,28},{24,16},{28,20},{1,9},{5... | collective-permute-start | bytes 3932168 | tf_op jit(solution)/shard_map/ppermute | solution.py:81
  842.0 29.8 %collective-permute-start.47 = (bf16[256,2560]{1,0:T(8,128)(2,1)}, bf16[256,2560]{1,0:T(8,128)(2,1)S(1)}, u32[]{:S(2)}, u32[]{:S(2)}) collective-permute-start(bf16[256,2560]{1,0:T(8,128)(2,1)} %get-tuple-element.101), channel_id=1, source_target_pairs={{0,16},{4,20},{8,24},{12,28},{16,0},{20,4},{24,8},{28,12},{1,17},{... | collective-permute-start | bytes 3932168 | tf_op jit(solution)/shard_map/ppermute | solution.py:81
  872.8 17.9 %collective-permute-start.48 = (bf16[128,2560]{1,0:T(8,128)(2,1)}, bf16[128,2560]{1,0:T(8,128)(2,1)S(1)}, u32[]{:S(2)}, u32[]{:S(2)}) collective-permute-start(bf16[128,2560]{1,0:T(8,128)(2,1)} %get-tuple-element.104), channel_id=1, source_target_pairs={{0,8},{4,12},{8,0},{12,4},{16,24},{20,28},{24,16},{28,20},{1,9},{5... | collective-permute-start | bytes 1966088 | tf_op jit(solution)/shard_map/ppermute | solution.py:81
  873.5 18.0 %collective-permute-start.49 = (bf16[128,2560]{1,0:T(8,128)(2,1)}, bf16[128,2560]{1,0:T(8,128)(2,1)}, u32[]{:S(2)}, u32[]{:S(2)}) collective-permute-start(bf16[128,2560]{1,0:T(8,128)(2,1)} %get-tuple-element.105), channel_id=1, source_target_pairs={{0,16},{4,20},{8,24},{12,28},{16,0},{20,4},{24,8},{28,12},{1,17},{... | collective-permute-start | bytes 1966088 | tf_op jit(solution)/shard_map/ppermute | solution.py:81
  874.5 297.3 %all-gather.26.cloned.1.call-start = ((), (), s32[]{:S(2)}) async-start(), calls=%async_computation.14 | async-start | bytes 5242880 | tf_op jit(solution)/shard_map/all_gather | solution.py:718
  878.6 26.2 %collective-permute-start.50 = (bf16[128,2560]{1,0:T(8,128)(2,1)}, bf16[128,2560]{1,0:T(8,128)(2,1)}, u32[]{:S(2)}, u32[]{:S(2)}) collective-permute-start(bf16[128,2560]{1,0:T(8,128)(2,1)} %get-tuple-element.106), channel_id=1, source_target_pairs={{0,8},{4,12},{8,0},{12,4},{16,24},{20,28},{24,16},{28,20},{1,9},{5... | collective-permute-start | bytes 1966088 | tf_op jit(solution)/shard_map/ppermute | solution.py:81
  880.2 25.4 %collective-permute-start.51 = (bf16[128,2560]{1,0:T(8,128)(2,1)}, bf16[128,2560]{1,0:T(8,128)(2,1)}, u32[]{:S(2)}, u32[]{:S(2)}) collective-permute-start(bf16[128,2560]{1,0:T(8,128)(2,1)} %get-tuple-element.107), channel_id=1, source_target_pairs={{0,16},{4,20},{8,24},{12,28},{16,0},{20,4},{24,8},{28,12},{1,17},{... | collective-permute-start | bytes 1966088 | tf_op jit(solution)/shard_map/ppermute | solution.py:81
  881.3 49.2 %collective-permute-start.53 = (bf16[256,2560]{1,0:T(8,128)(2,1)}, bf16[256,2560]{1,0:T(8,128)(2,1)S(1)}, u32[]{:S(2)}, u32[]{:S(2)}) collective-permute-start(bf16[256,2560]{1,0:T(8,128)(2,1)} %get-tuple-element.109), channel_id=1, source_target_pairs={{0,16},{4,20},{8,24},{12,28},{16,0},{20,4},{24,8},{28,12},{1,17},{... | collective-permute-start | bytes 3932168 | tf_op jit(solution)/shard_map/ppermute | solution.py:81
  890.7 39.8 %collective-permute-start.54 = (bf16[256,2560]{1,0:T(8,128)(2,1)}, bf16[256,2560]{1,0:T(8,128)(2,1)S(1)}, u32[]{:S(2)}, u32[]{:S(2)}) collective-permute-start(bf16[256,2560]{1,0:T(8,128)(2,1)} %get-tuple-element.110), channel_id=1, source_target_pairs={{0,8},{4,12},{8,0},{12,4},{16,24},{20,28},{24,16},{28,20},{1,9},{5... | collective-permute-start | bytes 3932168 | tf_op jit(solution)/shard_map/ppermute | solution.py:81
  958.7 45.7 %collective-permute-start.57 = (bf16[3,256,640]{2,1,0:T(8,128)(2,1)S(1)}, bf16[3,256,640]{2,1,0:T(8,128)(2,1)S(1)}, u32[]{:S(2)}, u32[]{:S(2)}) collective-permute-start(bf16[3,256,640]{2,1,0:T(8,128)(2,1)S(1)} %get-tuple-element.245), channel_id=1, source_target_pairs={{0,1},{4,5},{8,9},{12,13},{16,17},{20,21},{24,25},{28,29}} | collective-permute-start | bytes 2949128 | tf_op jit(solution)/shard_map/ppermute | solution.py:195
  1012.7 14.7 %collective-permute-start.71 = (bf16[128,1536]{1,0:T(8,128)(2,1)}, bf16[128,1536]{1,0:T(8,128)(2,1)}, u32[]{:S(2)}, u32[]{:S(2)}) collective-permute-start(bf16[128,1536]{1,0:T(8,128)(2,1)} %get-tuple-element.127), channel_id=1, source_target_pairs={{0,8},{4,12},{8,0},{12,4},{16,24},{20,28},{24,16},{28,20},{1,9},{5... | collective-permute-start | bytes 1179656 | tf_op jit(solution)/shard_map/ppermute | solution.py:81
  1014.1 14.9 %collective-permute-start.72 = (bf16[128,1536]{1,0:T(8,128)(2,1)}, bf16[128,1536]{1,0:T(8,128)(2,1)}, u32[]{:S(2)}, u32[]{:S(2)}) collective-permute-start(bf16[128,1536]{1,0:T(8,128)(2,1)} %get-tuple-element.128), channel_id=1, source_target_pairs={{0,16},{4,20},{8,24},{12,28},{16,0},{20,4},{24,8},{28,12},{1,17},{... | collective-permute-start | bytes 1179656 | tf_op jit(solution)/shard_map/ppermute | solution.py:81
  1014.6 25.4 %collective-permute-start.69 = (bf16[128,3072]{1,0:T(8,128)(2,1)}, bf16[128,3072]{1,0:T(8,128)(2,1)}, u32[]{:S(2)}, u32[]{:S(2)}) collective-permute-start(bf16[128,3072]{1,0:T(8,128)(2,1)} %get-tuple-element.125), channel_id=1, source_target_pairs={{0,8},{4,12},{8,0},{12,4},{16,24},{20,28},{24,16},{28,20},{1,9},{5... | collective-permute-start | bytes 2359304 | tf_op jit(solution)/shard_map/ppermute | solution.py:81
  1015.4 28.0 %collective-permute-start.70 = (bf16[128,3072]{1,0:T(8,128)(2,1)}, bf16[128,3072]{1,0:T(8,128)(2,1)}, u32[]{:S(2)}, u32[]{:S(2)}) collective-permute-start(bf16[128,3072]{1,0:T(8,128)(2,1)} %get-tuple-element.126), channel_id=1, source_target_pairs={{0,16},{4,20},{8,24},{12,28},{16,0},{20,4},{24,8},{28,12},{1,17},{... | collective-permute-start | bytes 2359304 | tf_op jit(solution)/shard_map/ppermute | solution.py:81
  1023.3 31.8 %collective-permute-start.63 = (bf16[4,4,26752]{2,1,0:T(4,128)(2,1)}, bf16[4,4,26752]{2,1,0:T(4,128)(2,1)S(1)}, u32[]{:S(2)}, u32[]{:S(2)}) collective-permute-start(bf16[4,4,26752]{2,1,0:T(4,128)(2,1)} %slice.809), channel_id=1, source_target_pairs={{0,16},{4,20},{8,24},{12,28},{16,0},{20,4},{24,8},{28,12},{1,17},{... | collective-permute-start | bytes 2568200 | tf_op jit(solution)/shard_map/ppermute | solution.py:81
  1027.4 52.2 %collective-permute-start.60 = (bf16[3,256,640]{2,1,0:T(8,128)(2,1)}, bf16[3,256,640]{2,1,0:T(8,128)(2,1)}, u32[]{:S(2)}, u32[]{:S(2)}) collective-permute-start(bf16[3,256,640]{2,1,0:T(8,128)(2,1)} %get-tuple-element.242), channel_id=1, source_target_pairs={{2,1},{3,2},{6,5},{7,6},{10,9},{11,10},{14,13},{15,14},{18,17},{19... | collective-permute-start | bytes 2949128 | tf_op jit(solution)/shard_map/ppermute | solution.py:196
  1029.0 37.1 %collective-permute-start.59 = (bf16[3,256,640]{2,1,0:T(8,128)(2,1)}, bf16[3,256,640]{2,1,0:T(8,128)(2,1)S(1)}, u32[]{:S(2)}, u32[]{:S(2)}) collective-permute-start(bf16[3,256,640]{2,1,0:T(8,128)(2,1)} %get-tuple-element.243), channel_id=1, source_target_pairs={{0,1},{1,2},{4,5},{5,6},{8,9},{9,10},{12,13},{13,14},{16,17},{17,1... | collective-permute-start | bytes 2949128 | tf_op jit(solution)/shard_map/ppermute | solution.py:195
  1083.9 69.1 %collective-permute-start.62 = (bf16[3,256,640]{2,1,0:T(8,128)(2,1)}, bf16[3,256,640]{2,1,0:T(8,128)(2,1)S(1)}, u32[]{:S(2)}, u32[]{:S(2)}) collective-permute-start(bf16[3,256,640]{2,1,0:T(8,128)(2,1)} %add_convert_fusion.13), channel_id=1, source_target_pairs={{1,0},{2,1},{3,2},{5,4},{6,5},{7,6},{9,8},{10,9},{11,10},{13,12},{... | collective-permute-start | bytes 2949128 | tf_op jit(solution)/shard_map/ppermute | solution.py:196
  1085.2 67.8 %collective-permute-start.61 = (bf16[3,256,640]{2,1,0:T(8,128)(2,1)S(1)}, bf16[3,256,640]{2,1,0:T(8,128)(2,1)S(1)}, u32[]{:S(2)}, u32[]{:S(2)}) collective-permute-start(bf16[3,256,640]{2,1,0:T(8,128)(2,1)S(1)} %add_convert_fusion.14), channel_id=1, source_target_pairs={{0,1},{1,2},{2,3},{4,5},{5,6},{6,7},{8,9},{9,10},{10,11},{12,13},{... | collective-permute-start | bytes 2949128 | tf_op jit(solution)/shard_map/ppermute | solution.py:195
  (154 other events, 1411.0 us)
Sparse Core Ops, SparseCore 0:
  12.1 43.3 all-gather.13
  73.1 54.8 all-gather.19
  292.6 80.8 all-gather.15
  374.9 79.3 all-gather.17
  456.4 75.2 reduce-scatter.4
  536.7 75.1 reduce-scatter.6
  624.1 76.4 reduce-scatter.8
  703.0 80.7 reduce-scatter.10
  785.4 80.2 all-gather.21
  867.1 79.2 all-gather.27
  948.0 110.8 all-gather.23
  1060.3 111.5 all-gather.25

commit v12 on v9

--- a/solution.py
+++ b/solution.py
@@ -17,6 +17,7 @@
 VMEM = 58 * 1024 * 1024
 BF = jnp.bfloat16
 F32 = jnp.float32
+MUCH = pl.CostEstimate(flops=60 * 10**9, bytes_accessed=1024, transcendentals=0)
 LITTLE = pl.CostEstimate(flops=1024, bytes_accessed=1024, transcendentals=0)
 
 
@@ -24,7 +25,7 @@
     return lax.dot_general(left, right, (dims, ((), ())), preferred_element_type=F32)
 
 
-def fence(values, *others):
+def fence(values, *others, cost=LITTLE):
     if not others:
         return list(values)
     place = pl.BlockSpec(memory_space=pl.ANY)
@@ -35,6 +36,7 @@
         out_shape=[jax.ShapeDtypeStruct(v.shape, v.dtype) for v in values],
         input_output_aliases={k: k for k in range(len(values))},
         compiler_params=pltpu.CompilerParams(vmem_limit_bytes=VMEM),
+        cost_estimate=cost,
         name="fence",
     )
     return list(call(*values, *others))
@@ -268,26 +270,6 @@
         cost_estimate=LITTLE,
         name="permute",
     )(table, values)
-
-
-def interleave_kernel(one_ref, two_ref, out_ref):
-    out_ref[0] = one_ref[...]
-    out_ref[1] = two_ref[...]
-
-
-def interleave(one, two):
-    n, rows, d_model = one.shape
-    spec = pl.BlockSpec((pl.squeezed, rows, d_model), lambda j: (j, 0, 0))
-    return pl.pallas_call(
-        interleave_kernel,
-        grid=(n,),
-        in_specs=[spec, spec],
-        out_specs=pl.BlockSpec((pl.squeezed, 2, rows, d_model), lambda j: (j, 0, 0, 0)),
-        out_shape=jax.ShapeDtypeStruct((n, 2, rows, d_model), one.dtype),
-        compiler_params=pltpu.CompilerParams(vmem_limit_bytes=VMEM),
-        cost_estimate=LITTLE,
-        name="interleave",
-    )(one, two)
 
 
 def permute_gain(values, table):
@@ -656,9 +638,6 @@
     grad_second = fence(grad_second, *sent_dn, *sent_gu, *shares)
     came_mlp = sum_dn.hop(sent_dn) + sum_gu.hop(sent_gu)
 
-    def mlp_result(h, mlp_sum):
-        return permute_rows((hidden[h * half : (h + 1) * half] + mlp_sum.astype(F32)).astype(BF), inverse)
-
     shares = fence(shares, *grad_second)
     mlp_sums = [lax.psum_scatter(share, "tensor", scatter_dimension=0, tiled=True) for share in shares]
 
@@ -700,36 +679,31 @@
     gain_one = jnp.sum(grad_first * first_unit, axis=0)
     grad_tokens = grad_hidden + norm_back(grad_first, first_unit, first_rate, gain[0])
     grad_tokens = permute_rows(grad_tokens.astype(BF), inverse)
-    gathered = [lax.all_gather(grad_tokens[h * half : (h + 1) * half], "tensor", axis=0) for h in range(2)]
+    gathered = lax.all_gather(grad_tokens, "tensor", axis=0, tiled=True)
     (mixed,) = fence([mixed], grad_tokens)
     sum_o = by_cols(hidden_low, mixed)
     pre_low, rec_low = fence([pre_low, rec_low], sum_o.terms[1])
     sum_g, sum_r = by_cols(first_own, pre_low), by_cols(first_own, rec_low)
-    results = [mlp_result(h, mlp_sum) for h, mlp_sum in enumerate(fence(mlp_sums, sum_o.terms[1]))]
-    got_o = sum_o.hop(sum_o.sources())
+    mlp_sum = jnp.concatenate(fence(mlp_sums, sum_o.terms[1])).astype(F32)
+    result = permute_rows((hidden + mlp_sum).astype(BF), inverse)
+    got_o = sum_o.hop(fence(sum_o.sources(), result))
+    result = lax.all_gather(result, "tensor", axis=0, tiled=True)
     got_g = sum_g.hop(fence(sum_g.sources(), *got_o))
-    pause = (gathered[0], *got_g)
-    sum_o.hop(fence(sum_o.sources(), *pause))
-    got_r = sum_r.hop(fence(sum_r.sources(), *pause))
-    results = fence(results, gathered[0], *got_g)
-    results = [lax.all_gather(result, "tensor", axis=0) for result in results]
-    sum_g.hop(fence(sum_g.sources(), *pause))
+    sum_o.hop(fence(sum_o.sources(), *got_g))
+    got_r = sum_r.hop(fence(sum_r.sources(), *got_g))
+    sum_g.hop(fence(sum_g.sources(), *got_g))
     got_r = sum_r.hop(fence(sum_r.sources(), *got_r))
+    (tokens_out,) = fence([gathered], *got_r, cost=MUCH)
     owned = jnp.stack([total.finish().reshape(d_own, n, width // n) for total in (sum_o, sum_g, sum_r)])
     owned = LineSum(owned.transpose(2, 0, 1, 3), n)
     owned.go()
-    pause = (gathered[1], owned.right, owned.left)
-    d_lru, dpar = fence([d_lru, dpar], *pause)
+    d_lru, dpar = fence([d_lru, dpar], *got_r)
     if sum_dn.square:
-        sum_dn.hop(fence(sum_dn.sources(), *pause))
-        sum_gu.hop(fence(sum_gu.sources(), *pause))
-    owned.go(gathered[1])
-    tokens_out = interleave(*fence(gathered, owned.right)).reshape(n * rows, d_model)
-    if n > 3:
-        owned.go(results[0])
+        sum_dn.hop(fence(sum_dn.sources(), *got_r))
+        sum_gu.hop(fence(sum_gu.sources(), *got_r))
     g_gu, g_dn = sum_gu.finish().astype(F32), sum_dn.finish().astype(F32)
     g_all = owned.finish()
-    output = interleave(*fence(results, owned.right, owned.left)).reshape(n * rows, d_model)
+    (output,) = fence([result], owned.right, owned.left, g_gu, g_dn, cost=MUCH)
     g_o, g_g, g_r = g_all[0], g_all[1], g_all[2]
 
     d_gain = permute_gain(jnp.stack([gain_one, gain_two]), inverse)

time: 1190 us -> 1180 us (level)
  waiting for transfers between devices: 388 us -> 329 us
  starting transfers between devices: 90.9 us -> 143 us
  Pallas kernels: 138 us -> 121 us
  local copies, waits for them, and re-layouts: 103 us -> 119 us
    ppermute x3, waiting for transfers between devices: 60.1 us -> 0.01 us  [go(): lax.ppermute(left, 'tensor', [(k, k - 1) for k in range(max(n - t, 1), n)])]
    ppermute x3, starting transfers between devices: 13.8 us -> 64.2 us  [go(): lax.ppermute(right, 'tensor', [(k, k + 1) for k in range(min(t, n - 1))])]
    all_gather x4 -> x2, waiting for transfers between devices: 29 us -> 0.01 us  [the longest x1 0.01 us: on_device(): gathered = lax.all_gather(grad_tokens, 'tensor', axis=0, tiled=True)]
    ppermute x3, waiting for transfers between devices: 33.2 us -> 58.5 us  [go(): lax.ppermute(right, 'tensor', [(k, k + 1) for k in range(min(t, n - 1))])]
    unnamed x287 -> x269, local copies, waits for them, and re-layouts: 43.1 us -> 59.8 us
    pallas_call x2 -> x0, Pallas kernels: 14.1 us -> none  [interleave(): pl.pallas_call(interleave_kernel, grid=(n,), in_specs=[spec, spec], out_s...]
    pallas_call x6 -> x5, Pallas kernels: 26.2 us -> 23.5 us  [permute_rows(): pl.pallas_call(functools.partial(copy_kernel, table.shape[0]), grid_spec=...]
    convert_element_type x21 -> x22, other arithmetic: 62.9 us -> 61.9 us  [add_all(): return total.astype(BF)]
  transfers between devices with their start and end apart: 86 -> 84, of which waited for: 42 -> 39; matrix products, arithmetic and copies ran while one was open for 43% -> 43% of each run, Pallas kernels for 10% -> 10%
where the time goes in v12:
time: 1180 us; the launch traced here: 1170 us
  waiting for transfers between devices  329 us (28%)
  matrix products  306 us (26%)
  starting transfers between devices  143 us (12%)
  other arithmetic  135 us (11%)
  Pallas kernels  121 us (10%)
  local copies, waits for them, and re-layouts  119 us (10%)
  between operations  17.2 us (1%)
    dot_general x34, matrix products, dot(): lax.dot_general(left, right, (dims, ((), ())), preferred_element_type=F32)  306 us
    ppermute x58, waiting for transfers between devices, exchange(): return lax.ppermute(values, 'dp', [(k, k ^ 1 << bit) for k in range(size)])  244 us
    ppermute x3, starting transfers between devices, go(): lax.ppermute(right, 'tensor', [(k, k + 1) for k in range(min(t, n - 1))])  64.2 us
    pallas_call x3, Pallas kernels, kernel_call(): pl.pallas_call(body, grid_spec=pltpu.PrefetchScalarGridSpec(num_scalar_pr...  62.1 us
    convert_element_type x22, other arithmetic, add_all(): return total.astype(BF)  61.9 us
    unnamed x269, local copies, waits for them, and re-layouts  59.8 us
    ppermute x3, waiting for transfers between devices, go(): lax.ppermute(right, 'tensor', [(k, k + 1) for k in range(min(t, n - 1))])  58.5 us
    ppermute x58, starting transfers between devices, exchange(): return lax.ppermute(values, 'dp', [(k, k ^ 1 << bit) for k in range(size)])  54 us
  transfers between devices with their start and end apart: 84, of which 39 were waited for; matrix products, arithmetic and copies ran while one was open for 43% of the time, Pallas kernels for 10%

profile of v12, /device:TPU:0, one launch (start us, length us, event | category | flops | bytes accessed | tf_op | source)
XLA Modules:
  0.0 1170.0 jit_solution(16273599040938850238)
XLA Ops:
  38.1 16.2 %collective-permute-done.1.refs_2_.refs_1_ = bf16[256,3072]{1,0:T(8,128)(2,1)S(1)} collective-permute-done((bf16[256,3072]{1,0:T(8,128)(2,1)}, bf16[256,3072]{1,0:T(8,128)(2,1)S(1)}, u32[]{:S(2)}, u32[]{:S(2)}) %collective-permute-start.1) | collective-permute-done | bytes 1572896 | tf_op jit(solution)/shard_map/ppermute | solution.py:81
  62.8 27.5 %collective-permute-done.9.refs_4_ = bf16[256,2560]{1,0:T(8,128)(2,1)S(1)} collective-permute-done((bf16[256,2560]{1,0:T(8,128)(2,1)S(1)}, bf16[256,2560]{1,0:T(8,128)(2,1)S(1)}, u32[]{:S(2)}, u32[]{:S(2)}) %collective-permute-start.9) | collective-permute-done | bytes 1310752 | tf_op jit(solution)/shard_map/ppermute | solution.py:81
  104.6 9.5 collective-permute-done.10.refs_2_
  122.2 7.3 collective-permute-done.6
  149.7 7.3 convolution_add_fusion.pre_ref
  157.0 18.8 %recurrence.1 = (f32[512,2560]{1,0:T(8,128)}, f32[512,2560]{1,0:T(8,128)}, f32[512,2560]{1,0:T(8,128)}, f32[512,2560]{1,0:T(8,128)}, f32[512,2560]{1,0:T(8,128)}, /*index=5*/f32[512,2560]{1,0:T(8,128)}) custom-call(s32[1]{0:T(128)} %sub.38.live_ref, f32[528,2560]{1,0:T(8,128)} %convolution_add_fusion.pre_ref, f32[8,2560]{1,0:T(8,128)} %pad_maximum_fusion.14.par_ref, ...), custom_call_target="tpu_custom_call" | custom-call | flops 1024 | bytes 1024 | tf_op jit(solution)/shard_map/recurrence/pallas_call | solution.py:475
  184.4 5.3 collective-permute-start.18
  218.8 9.7 fusion.22
  228.6 10.0 collective-permute-done.21.refs_1_
  244.6 14.2 %collective-permute-done.22.refs_2_.refs_3_ = bf16[128,2560]{1,0:T(8,128)(2,1)S(1)} collective-permute-done((bf16[128,2560]{1,0:T(8,128)(2,1)S(1)}, bf16[128,2560]{1,0:T(8,128)(2,1)S(1)}, u32[]{:S(2)}, u32[]{:S(2)}) %collective-permute-start.22) | collective-permute-done | bytes 655392 | tf_op jit(solution)/shard_map/ppermute | solution.py:81
  292.9 6.1 assemble.10.refs_0_
  302.9 18.8 %collective-permute-done.29.refs_4_ = bf16[256,1536]{1,0:T(8,128)(2,1)S(1)} collective-permute-done((bf16[256,1536]{1,0:T(8,128)(2,1)}, bf16[256,1536]{1,0:T(8,128)(2,1)S(1)}, u32[]{:S(2)}, u32[]{:S(2)}) %collective-permute-start.29) | collective-permute-done | bytes 786464 | tf_op jit(solution)/shard_map/ppermute | solution.py:81
  323.6 9.1 collective-permute-done.30.refs_2_
  337.8 5.2 collective-permute-done.32.refs_1_
  349.3 5.9 permute.7
  355.1 5.8 permute.6
  361.4 9.2 assemble.11
  370.7 19.1 %fusion.82 = f32[1024,3072]{1,0:T(8,128)} fusion(bf16[1024,2048]{1,0:T(8,128)(2,1)} %all-gather.10.cloned.1.call-done, bf16[2048,3072]{1,0:T(8,128)(2,1)} %assemble.11), kind=kOutput, calls=%fused_computation.262 | convolution fusion | flops 12884901888 | bytes 29360128 | tf_op jit(solution)/shard_map/dot_general | solution.py:25
  389.8 16.0 %fusion.6 = (bf16[1024,1536]{1,0:T(8,128)(2,1)S(1)}, bf16[1024,1536]{1,0:T(8,128)(2,1)S(1)}, bf16[1024,1536]{1,0:T(8,128)(2,1)}) fusion(f32[1024,3072]{1,0:T(8,128)} %fusion.82, bf16[1024,2048]{1,0:T(8,128)(2,1)S(1)} %copy-done.37, bf16[2048,1536]{1,0:T(8,128)(2,1)} %assemble.13), kind=kOutput, calls=%fused_computation.15 | convolution fusion | flops 6483345408 | bytes 32505856 | tf_op jit(solution)/shard_map/dot_general | solution.py:25
  407.4 17.6 %convolution_convert_fusion.7.refs_1_ = bf16[1024,2048]{1,0:T(8,128)(2,1)} fusion(bf16[2048,3072]{1,0:T(8,128)(2,1)} %assemble.11, bf16[1024,1536]{1,0:T(8,128)(2,1)S(1)} %get-tuple-element.189, bf16[1024,1536]{1,0:T(8,128)(2,1)S(1)} %get-tuple-element.188), kind=kOutput, calls=%fused_computation.73 | convolution fusion | flops 12899581952 | bytes 23068672 | tf_op jit(solution)/shard_map/dot_general | solution.py:25
  425.3 24.3 %all-gather.12.cloned.1.call-done.refs_0_ = bf16[1024,2048]{1,0:T(8,128)(2,1)} async-done(((bf16[256,2048]{1,0:T(8,128)(2,1)}), bf16[1024,2048]{1,0:T(8,128)(2,1)}) %all-gather.12.cloned.1.call-update) | async-done | bytes 4194320 | tf_op jit(solution)/shard_map/all_gather | solution.py:611
  449.6 19.1 %fusion.83 = f32[1024,3072]{1,0:T(8,128)} fusion(bf16[1024,2048]{1,0:T(8,128)(2,1)} %fence.40, bf16[2048,3072]{1,0:T(8,128)(2,1)} %assemble.11), kind=kOutput, calls=%fused_computation.263 | convolution fusion | flops 12884901888 | bytes 29360128 | tf_op jit(solution)/shard_map/dot_general | solution.py:25
  468.6 15.5 %fusion.13 = (bf16[1024,1536]{1,0:T(8,128)(2,1)}, bf16[1024,1536]{1,0:T(8,128)(2,1)}, bf16[1024,1536]{1,0:T(8,128)(2,1)}) fusion(f32[1024,3072]{1,0:T(8,128)} %fusion.83, bf16[1024,2048]{1,0:T(8,128)(2,1)S(1)} %copy-done.35, bf16[2048,1536]{1,0:T(8,128)(2,1)S(1)} %bitcast.175), kind=kOutput, calls=%fused_computation.22 | convolution fusion | flops 6483345408 | bytes 32505856 | tf_op jit(solution)/shard_map/dot_general | solution.py:25
  484.1 5.5 pad_maximum_fusion.refs_1_
  489.6 18.8 %convolution_convert_fusion.6.refs_2_ = bf16[1024,2048]{1,0:T(8,128)(2,1)} fusion(bf16[2048,3072]{1,0:T(8,128)(2,1)} %assemble.11, bf16[1024,1536]{1,0:T(8,128)(2,1)} %get-tuple-element.187, bf16[1024,1536]{1,0:T(8,128)(2,1)S(1)} %copy-done.51), kind=kOutput, calls=%fused_computation.72 | convolution fusion | flops 12899581952 | bytes 23068672 | tf_op jit(solution)/shard_map/dot_general | solution.py:25
  510.3 5.7 pad_maximum_fusion.1.refs_1_
  516.0 7.5 fusion.36
  523.5 8.2 convolution_convert_fusion.9.refs_6_.refs_0_
  531.9 9.7 add_convert_fusion.2
  541.6 9.7 fusion.30
  551.3 11.8 %add_convert_fusion = bf16[1024,3072]{1,0:T(8,128)(2,1)} fusion(f32[1024,3072]{1,0:T(8,128)} %fusion.30, bf16[1024,3072]{1,0:T(8,128)(2,1)S(1)} %bitcast.164, bf16[1024,2048]{1,0:T(8,128)(2,1)S(1)} %copy-done.47), kind=kOutput, calls=%fused_computation.2 | convolution fusion | flops 6448742400 | bytes 27262976 | tf_op jit(solution)/shard_map/dot_general | solution.py:25
  563.6 11.0 fusion.33
  574.6 11.3 convolution_convert_fusion.8.refs_7_.refs_1_
  585.9 5.4 fusion.39
  591.2 7.1 add_convert_fusion.3
  598.3 10.2 add_convert_fusion.1
  630.9 5.7 fusion.50
  641.9 17.0 %back_scan.1 = (f32[512,2560]{1,0:T(8,128)}, f32[512,2560]{1,0:T(8,128)}, f32[8,2560]{1,0:T(8,128)}, bf16[512,2560]{1,0:T(8,128)(2,1)}) custom-call(s32[1]{0:T(128)} %sub.38.live_ref, f32[512,2560]{1,0:T(8,128)} %get-tuple-element.252.refs_2_.pre_ref, f32[512,2560]{1,0:T(8,128)} %convolution_add_fusion.1.grad_ref, f32[512,2560]{1,0:T(8,128)} %get-tuple-element.76.decay_ref, ...), custom_call_target="tpu_custom_call" | custom-call | flops 1024 | bytes 1024 | tf_op jit(solution)/shard_map/back_scan/pallas_call | solution.py:475
  663.9 11.5 collective-permute-done.38.refs_4_
  677.3 26.3 %recurrence_back.1 = (f32[528,2560]{1,0:T(8,128)}, f32[8,2560]{1,0:T(8,128)}, bf16[4,160,1280]{2,1,0:T(8,128)(2,1)}) custom-call(s32[1]{0:T(128)} %sub.38.live_ref, f32[528,2560]{1,0:T(8,128)} %convolution_add_fusion.pre_ref, f32[8,2560]{1,0:T(8,128)} %pad_maximum_fusion.14.par_ref, bf16[8,4,80,640]{3,2,1,0:T(8,128)(2,1)} %copy-done.15, ...), custom_call_target="tpu_custom_call" | custom-call | flops 1024 | bytes 1024 | tf_op jit(solution)/shard_map/recurrence_back/pallas_call | solution.py:475
  706.4 7.5 fusion.84
  713.9 6.8 fusion.85
  725.0 5.8 fusion.86
  730.9 5.0 fusion.87
  738.5 6.1 add_convert_fusion.5.in_ref
  749.8 4.9 convolution_convert_fusion.5
  754.8 8.6 collective-permute-done.43.refs_2_
  765.8 7.2 convolution_convert_fusion.2
  776.2 5.9 convolution_convert_fusion
  787.5 6.1 convolution_convert_fusion.4
  810.4 5.2 convolution_convert_fusion.3
  815.6 6.9 convolution_convert_fusion.1
  826.4 12.5 %collective-permute-done.44.refs_3_ = bf16[256,2560]{1,0:T(8,128)(2,1)} collective-permute-done((bf16[256,2560]{1,0:T(8,128)(2,1)}, bf16[256,2560]{1,0:T(8,128)(2,1)}, u32[]{:S(2)}, u32[]{:S(2)}) %collective-permute-start.44) | collective-permute-done | bytes 1310752 | tf_op jit(solution)/shard_map/ppermute | solution.py:81
  849.3 20.4 %collective-permute-done.47.refs_2_ = bf16[256,2560]{1,0:T(8,128)(2,1)} collective-permute-done((bf16[256,2560]{1,0:T(8,128)(2,1)}, bf16[256,2560]{1,0:T(8,128)(2,1)}, u32[]{:S(2)}, u32[]{:S(2)}) %collective-permute-start.47) | collective-permute-done | bytes 1310752 | tf_op jit(solution)/shard_map/ppermute | solution.py:81
  879.6 9.2 collective-permute-done.49
  893.1 9.7 collective-permute-done.51
  907.7 20.3 %collective-permute-done.54.refs_3_ = bf16[256,2560]{1,0:T(8,128)(2,1)S(1)} collective-permute-done((bf16[256,2560]{1,0:T(8,128)(2,1)}, bf16[256,2560]{1,0:T(8,128)(2,1)S(1)}, u32[]{:S(2)}, u32[]{:S(2)}) %collective-permute-start.54) | collective-permute-done | bytes 1310752 | tf_op jit(solution)/shard_map/ppermute | solution.py:81
  983.4 5.7 collective-permute-done.65
  1008.5 55.3 %collective-permute-start.58 = (bf16[3,256,640]{2,1,0:T(8,128)(2,1)S(1)}, bf16[3,256,640]{2,1,0:T(8,128)(2,1)S(1)}, u32[]{:S(2)}, u32[]{:S(2)}) collective-permute-start(bf16[3,256,640]{2,1,0:T(8,128)(2,1)S(1)} %get-tuple-element.183), channel_id=1, source_target_pairs={{0,1},{4,5},{8,9},{12,13},{16,17},{20,21},{24,25},{28,29}} | collective-permute-start | bytes 2949128 | tf_op jit(solution)/shard_map/ppermute | solution.py:191
  1064.2 35.9 %collective-permute-done.58 = bf16[3,256,640]{2,1,0:T(8,128)(2,1)S(1)} collective-permute-done((bf16[3,256,640]{2,1,0:T(8,128)(2,1)S(1)}, bf16[3,256,640]{2,1,0:T(8,128)(2,1)S(1)}, u32[]{:S(2)}, u32[]{:S(2)}) %collective-permute-start.58) | collective-permute-done | bytes 983072 | tf_op jit(solution)/shard_map/ppermute | solution.py:191
  1111.4 12.9 %collective-permute-done.59 = bf16[3,256,640]{2,1,0:T(8,128)(2,1)S(1)} collective-permute-done((bf16[3,256,640]{2,1,0:T(8,128)(2,1)S(1)}, bf16[3,256,640]{2,1,0:T(8,128)(2,1)S(1)}, u32[]{:S(2)}, u32[]{:S(2)}) %collective-permute-start.59) | collective-permute-done | bytes 983072 | tf_op jit(solution)/shard_map/ppermute | solution.py:191
  1132.2 9.6 collective-permute-done.60.refs_1_
  1146.0 8.4 copy.250
  1154.4 8.4 copy.251
  (628 shorter events, 388.6 us)
Async XLA Ops:
  7.2 48.5 %all-gather.8.cloned.1.call-start = ((), (), s32[]{:S(2)}) async-start(), calls=%async_computation.4 | async-start | bytes 2150400 | tf_op jit(solution)/shard_map/all_gather | solution.py:548
  12.0 102.1 %all-gather.18.cloned.1.call-start = ((), (), s32[]{:S(2)}) async-start(), calls=%async_computation.13 | async-start | bytes 3276800 | tf_op jit(solution)/shard_map/all_gather | solution.py:549
  15.5 38.7 %collective-permute-start.1 = (bf16[256,3072]{1,0:T(8,128)(2,1)}, bf16[256,3072]{1,0:T(8,128)(2,1)S(1)}, u32[]{:S(2)}, u32[]{:S(2)}) collective-permute-start(bf16[256,3072]{1,0:T(8,128)(2,1)} %pad_maximum_fusion.8.refs_0_), channel_id=1, source_target_pairs={{0,16},{4,20},{8,24},{12,28},{16,0},{20,4},{24,8},{28,12},{1,17},{... | collective-permute-start | bytes 4718600 | tf_op jit(solution)/shard_map/ppermute | solution.py:81
  19.6 36.1 %collective-permute-start = (bf16[256,3072]{1,0:T(8,128)(2,1)}, bf16[256,3072]{1,0:T(8,128)(2,1)S(1)}, u32[]{:S(2)}, u32[]{:S(2)}) collective-permute-start(bf16[256,3072]{1,0:T(8,128)(2,1)} %pad_maximum_fusion.8.refs_0_), channel_id=1, source_target_pairs={{0,8},{4,12},{8,0},{12,4},{16,24},{20,28},{24,16},{28,20},{1,9},{5... | collective-permute-start | bytes 4718600 | tf_op jit(solution)/shard_map/ppermute | solution.py:81
  56.9 313.8 %all-gather.10.cloned.1.call-start = ((), (), s32[]{:S(2)}) async-start(), calls=%async_computation.5 | async-start | bytes 5242880 | tf_op jit(solution)/shard_map/all_gather | solution.py:611
  58.5 31.8 %collective-permute-start.9 = (bf16[256,2560]{1,0:T(8,128)(2,1)S(1)}, bf16[256,2560]{1,0:T(8,128)(2,1)S(1)}, u32[]{:S(2)}, u32[]{:S(2)}) collective-permute-start(bf16[256,2560]{1,0:T(8,128)(2,1)S(1)} %bitcast.180), channel_id=1, source_target_pairs={{0,16},{4,20},{8,24},{12,28},{16,0},{20,4},{24,8},{28,12},{1,17},{... | collective-permute-start | bytes 3932168 | tf_op jit(solution)/shard_map/ppermute | solution.py:81
  59.4 32.5 %collective-permute-start.7 = (bf16[256,2560]{1,0:T(8,128)(2,1)S(1)}, bf16[256,2560]{1,0:T(8,128)(2,1)S(1)}, u32[]{:S(2)}, u32[]{:S(2)}) collective-permute-start(bf16[256,2560]{1,0:T(8,128)(2,1)S(1)} %bitcast.181), channel_id=1, source_target_pairs={{0,8},{4,12},{8,0},{12,4},{16,24},{20,28},{24,16},{28,20},{1,9},{5... | collective-permute-start | bytes 3932168 | tf_op jit(solution)/shard_map/ppermute | solution.py:81
  61.0 38.5 %collective-permute-start.4 = (bf16[320,640]{1,0:T(8,128)(2,1)S(1)}, bf16[320,640]{1,0:T(8,128)(2,1)S(1)}, u32[]{:S(2)}, u32[]{:S(2)}) collective-permute-start(bf16[320,640]{1,0:T(8,128)(2,1)S(1)} %bitcast.192), channel_id=1, source_target_pairs={{0,16},{4,20},{8,24},{12,28},{16,0},{20,4},{24,8},{28,12},{1,17},{... | collective-permute-start | bytes 1228808 | tf_op jit(solution)/shard_map/ppermute | solution.py:81
  62.3 39.0 %collective-permute-start.2 = (bf16[320,640]{1,0:T(8,128)(2,1)S(1)}, bf16[320,640]{1,0:T(8,128)(2,1)S(1)}, u32[]{:S(2)}, u32[]{:S(2)}) collective-permute-start(bf16[320,640]{1,0:T(8,128)(2,1)S(1)} %bitcast.193), channel_id=1, source_target_pairs={{0,8},{4,12},{8,0},{12,4},{16,24},{20,28},{24,16},{28,20},{1,9},{5... | collective-permute-start | bytes 1228808 | tf_op jit(solution)/shard_map/ppermute | solution.py:81
  90.4 23.7 %collective-permute-start.10 = (bf16[128,2560]{1,0:T(8,128)(2,1)S(1)}, bf16[128,2560]{1,0:T(8,128)(2,1)}, u32[]{:S(2)}, u32[]{:S(2)}) collective-permute-start(bf16[128,2560]{1,0:T(8,128)(2,1)S(1)} %slice.704), channel_id=1, source_target_pairs={{0,8},{4,12},{8,0},{12,4},{16,24},{20,28},{24,16},{28,20},{1,9},{5... | collective-permute-start | bytes 1966088 | tf_op jit(solution)/shard_map/ppermute | solution.py:81
  93.0 21.1 %collective-permute-start.8 = (bf16[128,2560]{1,0:T(8,128)(2,1)S(1)}, bf16[128,2560]{1,0:T(8,128)(2,1)}, u32[]{:S(2)}, u32[]{:S(2)}) collective-permute-start(bf16[128,2560]{1,0:T(8,128)(2,1)S(1)} %slice.703), channel_id=1, source_target_pairs={{0,16},{4,20},{8,24},{12,28},{16,0},{20,4},{24,8},{28,12},{1,17},{... | collective-permute-start | bytes 1966088 | tf_op jit(solution)/shard_map/ppermute | solution.py:81
  100.2 19.3 %collective-permute-start.5 = (bf16[160,640]{1,0:T(8,128)(2,1)}, bf16[160,640]{1,0:T(8,128)(2,1)}, u32[]{:S(2)}, u32[]{:S(2)}) collective-permute-start(bf16[160,640]{1,0:T(8,128)(2,1)} %slice.695), channel_id=1, source_target_pairs={{0,8},{4,12},{8,0},{12,4},{16,24},{20,28},{24,16},{28,20},{1,9},{5... | collective-permute-start | bytes 614408 | tf_op jit(solution)/shard_map/ppermute | solution.py:81
  118.4 26.3 %collective-permute-start.13 = (bf16[1024,2560]{1,0:T(8,128)(2,1)}, bf16[1024,2560]{1,0:T(8,128)(2,1)}, u32[]{:S(2)}, u32[]{:S(2)}) collective-permute-start(bf16[1024,2560]{1,0:T(8,128)(2,1)} %assemble.7), channel_id=1, source_target_pairs={{0,4},{4,0},{8,12},{12,8},{16,20},{20,16},{24,28},{28,24},{1,5},{5... | collective-permute-start | bytes 15728648 | tf_op jit(solution)/shard_map/ppermute | solution.py:81
  142.4 35.8 %collective-permute-start.12 = (bf16[256,2560]{1,0:T(8,128)(2,1)}, bf16[256,2560]{1,0:T(8,128)(2,1)S(1)}, u32[]{:S(2)}, u32[]{:S(2)}) collective-permute-start(bf16[256,2560]{1,0:T(8,128)(2,1)} %fence.33.refs_0_), channel_id=1, source_target_pairs={{0,16},{4,20},{8,24},{12,28},{16,0},{20,4},{24,8},{28,12},{1,17},{... | collective-permute-start | bytes 3932168 | tf_op jit(solution)/shard_map/ppermute | solution.py:81
  143.3 34.9 %collective-permute-start.11 = (bf16[256,2560]{1,0:T(8,128)(2,1)}, bf16[256,2560]{1,0:T(8,128)(2,1)S(1)}, u32[]{:S(2)}, u32[]{:S(2)}) collective-permute-start(bf16[256,2560]{1,0:T(8,128)(2,1)} %fence.33.refs_0_), channel_id=1, source_target_pairs={{0,8},{4,12},{8,0},{12,4},{16,24},{20,28},{24,16},{28,20},{1,9},{5... | collective-permute-start | bytes 3932168 | tf_op jit(solution)/shard_map/ppermute | solution.py:81
  182.7 16.3 %collective-permute-start.14 = (bf16[128,2560]{1,0:T(8,128)(2,1)S(1)}, bf16[128,2560]{1,0:T(8,128)(2,1)S(1)}, u32[]{:S(2)}, u32[]{:S(2)}) collective-permute-start(bf16[128,2560]{1,0:T(8,128)(2,1)S(1)} %slice.537), channel_id=1, source_target_pairs={{0,8},{4,12},{8,0},{12,4},{16,24},{20,28},{24,16},{28,20},{1,9},{5... | collective-permute-start | bytes 1966088 | tf_op jit(solution)/shard_map/ppermute | solution.py:81
  207.1 31.4 %collective-permute-start.21 = (bf16[256,2560]{1,0:T(8,128)(2,1)}, bf16[256,2560]{1,0:T(8,128)(2,1)S(1)}, u32[]{:S(2)}, u32[]{:S(2)}) collective-permute-start(bf16[256,2560]{1,0:T(8,128)(2,1)} %fence.35.refs_0_), channel_id=1, source_target_pairs={{0,16},{4,20},{8,24},{12,28},{16,0},{20,4},{24,8},{28,12},{1,17},{... | collective-permute-start | bytes 3932168 | tf_op jit(solution)/shard_map/ppermute | solution.py:81
  208.3 31.1 %collective-permute-start.20 = (bf16[256,2560]{1,0:T(8,128)(2,1)}, bf16[256,2560]{1,0:T(8,128)(2,1)S(1)}, u32[]{:S(2)}, u32[]{:S(2)}) collective-permute-start(bf16[256,2560]{1,0:T(8,128)(2,1)} %fence.35.refs_0_), channel_id=1, source_target_pairs={{0,8},{4,12},{8,0},{12,4},{16,24},{20,28},{24,16},{28,20},{1,9},{5... | collective-permute-start | bytes 3932168 | tf_op jit(solution)/shard_map/ppermute | solution.py:81
  242.8 16.1 %collective-permute-start.22 = (bf16[128,2560]{1,0:T(8,128)(2,1)S(1)}, bf16[128,2560]{1,0:T(8,128)(2,1)S(1)}, u32[]{:S(2)}, u32[]{:S(2)}) collective-permute-start(bf16[128,2560]{1,0:T(8,128)(2,1)S(1)} %slice.547), channel_id=1, source_target_pairs={{0,8},{4,12},{8,0},{12,4},{16,24},{20,28},{24,16},{28,20},{1,9},{5... | collective-permute-start | bytes 1966088 | tf_op jit(solution)/shard_map/ppermute | solution.py:81
  271.8 20.1 %collective-permute-start.25 = (bf16[128,3072]{1,0:T(8,128)(2,1)}, bf16[128,3072]{1,0:T(8,128)(2,1)S(1)}, u32[]{:S(2)}, u32[]{:S(2)}) collective-permute-start(bf16[128,3072]{1,0:T(8,128)(2,1)} %slice.551), channel_id=1, source_target_pairs={{0,8},{4,12},{8,0},{12,4},{16,24},{20,28},{24,16},{28,20},{1,9},{5... | collective-permute-start | bytes 2359304 | tf_op jit(solution)/shard_map/ppermute | solution.py:81
  272.9 20.0 %collective-permute-start.26 = (bf16[128,3072]{1,0:T(8,128)(2,1)}, bf16[128,3072]{1,0:T(8,128)(2,1)}, u32[]{:S(2)}, u32[]{:S(2)}) collective-permute-start(bf16[128,3072]{1,0:T(8,128)(2,1)} %slice.552), channel_id=1, source_target_pairs={{0,16},{4,20},{8,24},{12,28},{16,0},{20,4},{24,8},{28,12},{1,17},{... | collective-permute-start | bytes 2359304 | tf_op jit(solution)/shard_map/ppermute | solution.py:81
  287.8 161.7 %all-gather.12.cloned.1.call-start = ((), (), s32[]{:S(2)}) async-start(), calls=%async_computation.6 | async-start | bytes 5242880 | tf_op jit(solution)/shard_map/all_gather | solution.py:611
  298.9 62.5 %collective-permute-start.27 = (bf16[1024,3072]{1,0:T(8,128)(2,1)}, bf16[1024,3072]{1,0:T(8,128)(2,1)}, u32[]{:S(2)}, u32[]{:S(2)}) collective-permute-start(bf16[1024,3072]{1,0:T(8,128)(2,1)} %assemble.10.refs_0_), channel_id=1, source_target_pairs={{0,4},{4,0},{8,12},{12,8},{16,20},{20,16},{24,28},{28,24},{1,5},{5... | collective-permute-start | bytes 18874376 | tf_op jit(solution)/shard_map/ppermute | solution.py:81
  301.6 20.1 %collective-permute-start.29 = (bf16[256,1536]{1,0:T(8,128)(2,1)}, bf16[256,1536]{1,0:T(8,128)(2,1)S(1)}, u32[]{:S(2)}, u32[]{:S(2)}) collective-permute-start(bf16[256,1536]{1,0:T(8,128)(2,1)} %fence.39.refs_0_), channel_id=1, source_target_pairs={{0,16},{4,20},{8,24},{12,28},{16,0},{20,4},{24,8},{28,12},{1,17},{... | collective-permute-start | bytes 2359304 | tf_op jit(solution)/shard_map/ppermute | solution.py:81
  302.0 20.3 %collective-permute-start.28 = (bf16[256,1536]{1,0:T(8,128)(2,1)}, bf16[256,1536]{1,0:T(8,128)(2,1)S(1)}, u32[]{:S(2)}, u32[]{:S(2)}) collective-permute-start(bf16[256,1536]{1,0:T(8,128)(2,1)} %fence.39.refs_0_), channel_id=1, source_target_pairs={{0,8},{4,12},{8,0},{12,4},{16,24},{20,28},{24,16},{28,20},{1,9},{5... | collective-permute-start | bytes 2359304 | tf_op jit(solution)/shard_map/ppermute | solution.py:81
  360.9 258.1 %reduce-scatter.5.cloned.1.call-start = ((), (), s32[]{:S(2)}) async-start(), calls=%async_computation.7 | async-start | bytes 5242880 | tf_op jit(solution)/shard_map/reduce_scatter | solution.py:620
  425.0 194.0 %reduce-scatter.7.cloned.1.call-start = ((), (), s32[]{:S(2)}) async-start(), calls=%async_computation.8 | async-start | bytes 5242880 | tf_op jit(solution)/shard_map/reduce_scatter | solution.py:620
  531.8 189.6 %reduce-scatter.9.cloned.1.call-start = ((), (), s32[]{:S(2)}) async-start(), calls=%async_computation.9 | async-start | bytes 5242880 | tf_op jit(solution)/shard_map/reduce_scatter | solution.py:642
  541.5 66.9 %collective-permute-start.33 = (bf16[1024,1536]{1,0:T(8,128)(2,1)}, bf16[1024,1536]{1,0:T(8,128)(2,1)S(1)}, u32[]{:S(2)}, u32[]{:S(2)}) collective-permute-start(bf16[1024,1536]{1,0:T(8,128)(2,1)} %add_convert_fusion.2), channel_id=1, source_target_pairs={{0,4},{4,0},{8,12},{12,8},{16,20},{20,16},{24,28},{28,24},{1,5},{5... | collective-permute-start | bytes 9437192 | tf_op jit(solution)/shard_map/ppermute | solution.py:81
  563.1 51.2 %collective-permute-start.34 = (bf16[1024,3072]{1,0:T(8,128)(2,1)}, bf16[1024,3072]{1,0:T(8,128)(2,1)}, u32[]{:S(2)}, u32[]{:S(2)}) collective-permute-start(bf16[1024,3072]{1,0:T(8,128)(2,1)} %add_convert_fusion), channel_id=1, source_target_pairs={{0,4},{4,0},{8,12},{12,8},{16,20},{20,16},{24,28},{28,24},{1,5},{5... | collective-permute-start | bytes 18874376 | tf_op jit(solution)/shard_map/ppermute | solution.py:81
  619.1 174.6 %reduce-scatter.11.cloned.1.call-start = ((), (), s32[]{:S(2)}) async-start(), calls=%async_computation.10 | async-start | bytes 5242880 | tf_op jit(solution)/shard_map/reduce_scatter | solution.py:642
  622.0 39.2 %collective-permute-start.36 = (bf16[256,1536]{1,0:T(8,128)(2,1)}, bf16[256,1536]{1,0:T(8,128)(2,1)}, u32[]{:S(2)}, u32[]{:S(2)}) collective-permute-start(bf16[256,1536]{1,0:T(8,128)(2,1)} %get-tuple-element.220.refs_3_), channel_id=1, source_target_pairs={{0,16},{4,20},{8,24},{12,28},{16,0},{20,4},{24,8},{28,12},{1,17},{... | collective-permute-start | bytes 2359304 | tf_op jit(solution)/shard_map/ppermute | solution.py:81
  623.4 39.1 %collective-permute-start.35 = (bf16[256,1536]{1,0:T(8,128)(2,1)}, bf16[256,1536]{1,0:T(8,128)(2,1)}, u32[]{:S(2)}, u32[]{:S(2)}) collective-permute-start(bf16[256,1536]{1,0:T(8,128)(2,1)} %get-tuple-element.221.refs_2_), channel_id=1, source_target_pairs={{0,8},{4,12},{8,0},{12,4},{16,24},{20,28},{24,16},{28,20},{1,9},{5... | collective-permute-start | bytes 2359304 | tf_op jit(solution)/shard_map/ppermute | solution.py:81
  624.9 50.5 %collective-permute-start.38 = (bf16[256,3072]{1,0:T(8,128)(2,1)}, bf16[256,3072]{1,0:T(8,128)(2,1)}, u32[]{:S(2)}, u32[]{:S(2)}) collective-permute-start(bf16[256,3072]{1,0:T(8,128)(2,1)} %get-tuple-element.194.refs_5_), channel_id=1, source_target_pairs={{0,16},{4,20},{8,24},{12,28},{16,0},{20,4},{24,8},{28,12},{1,17},{... | collective-permute-start | bytes 4718600 | tf_op jit(solution)/shard_map/ppermute | solution.py:81
  625.4 51.1 %collective-permute-start.37 = (bf16[256,3072]{1,0:T(8,128)(2,1)}, bf16[256,3072]{1,0:T(8,128)(2,1)}, u32[]{:S(2)}, u32[]{:S(2)}) collective-permute-start(bf16[256,3072]{1,0:T(8,128)(2,1)} %get-tuple-element.195.refs_4_), channel_id=1, source_target_pairs={{0,8},{4,12},{8,0},{12,4},{16,24},{20,28},{24,16},{28,20},{1,9},{5... | collective-permute-start | bytes 4718600 | tf_op jit(solution)/shard_map/ppermute | solution.py:81
  627.4 324.4 %all-gather.16.cloned.1.call-start = ((), (), s32[]{:S(2)}) async-start(), calls=%async_computation.12 | async-start | bytes 10485760 | tf_op jit(solution)/shard_map/all_gather | solution.py:682
  659.9 16.7 %collective-permute-start.41 = (f32[2,2560]{1,0:T(2,128)S(1)}, f32[2,2560]{1,0:T(2,128)S(1)}, u32[]{:S(2)}, u32[]{:S(2)}) collective-permute-start(f32[2,2560]{1,0:T(2,128)S(1)} %pad_maximum_fusion.16), channel_id=1, source_target_pairs={{3,0},{7,4},{11,8},{15,12},{19,16},{23,20},{27,24},{31,28}} | collective-permute-start | bytes 61448 | tf_op jit(solution)/shard_map/ppermute | solution.py:164
  704.6 16.7 %collective-permute-start.42 = (f32[16,2560]{1,0:T(8,128)S(1)}, f32[16,2560]{1,0:T(8,128)S(1)}, u32[]{:S(2)}, u32[]{:S(2)}) collective-permute-start(f32[16,2560]{1,0:T(8,128)S(1)} %slice.587), channel_id=1, source_target_pairs={{1,0},{2,1},{3,2},{5,4},{6,5},{7,6},{9,8},{10,9},{11,10},{13,12},{... | collective-permute-start | bytes 491528 | tf_op jit(solution)/shard_map/ppermute | solution.py:164
  748.2 397.8 %all-gather.14.cloned.1.call-start = ((), (), s32[]{:S(2)}) async-start(), calls=%async_computation.11 | async-start | bytes 10485760 | tf_op jit(solution)/shard_map/all_gather | solution.py:690
  773.0 49.5 %collective-permute-start.46 = (bf16[1024,2560]{1,0:T(8,128)(2,1)}, bf16[1024,2560]{1,0:T(8,128)(2,1)}, u32[]{:S(2)}, u32[]{:S(2)}) collective-permute-start(bf16[1024,2560]{1,0:T(8,128)(2,1)} %convolution_convert_fusion.2), channel_id=1, source_target_pairs={{0,4},{4,0},{8,12},{12,8},{16,20},{20,16},{24,28},{28,24},{1,5},{5... | collective-permute-start | bytes 15728648 | tf_op jit(solution)/shard_map/ppermute | solution.py:81
  782.1 63.3 %collective-permute-start.53 = (bf16[1024,2560]{1,0:T(8,128)(2,1)}, bf16[1024,2560]{1,0:T(8,128)(2,1)}, u32[]{:S(2)}, u32[]{:S(2)}) collective-permute-start(bf16[1024,2560]{1,0:T(8,128)(2,1)} %convolution_convert_fusion), channel_id=1, source_target_pairs={{0,4},{4,0},{8,12},{12,8},{16,20},{20,16},{24,28},{28,24},{1,5},{5... | collective-permute-start | bytes 15728648 | tf_op jit(solution)/shard_map/ppermute | solution.py:81
  807.8 31.1 %collective-permute-start.44 = (bf16[256,2560]{1,0:T(8,128)(2,1)}, bf16[256,2560]{1,0:T(8,128)(2,1)}, u32[]{:S(2)}, u32[]{:S(2)}) collective-permute-start(bf16[256,2560]{1,0:T(8,128)(2,1)} %get-tuple-element.87), channel_id=1, source_target_pairs={{0,16},{4,20},{8,24},{12,28},{16,0},{20,4},{24,8},{28,12},{1,17},{... | collective-permute-start | bytes 3932168 | tf_op jit(solution)/shard_map/ppermute | solution.py:81
  808.9 30.8 %collective-permute-start.45 = (bf16[256,2560]{1,0:T(8,128)(2,1)}, bf16[256,2560]{1,0:T(8,128)(2,1)}, u32[]{:S(2)}, u32[]{:S(2)}) collective-permute-start(bf16[256,2560]{1,0:T(8,128)(2,1)} %get-tuple-element.88), channel_id=1, source_target_pairs={{0,8},{4,12},{8,0},{12,4},{16,24},{20,28},{24,16},{28,20},{1,9},{5... | collective-permute-start | bytes 3932168 | tf_op jit(solution)/shard_map/ppermute | solution.py:81
  839.8 29.9 %collective-permute-start.47 = (bf16[256,2560]{1,0:T(8,128)(2,1)}, bf16[256,2560]{1,0:T(8,128)(2,1)}, u32[]{:S(2)}, u32[]{:S(2)}) collective-permute-start(bf16[256,2560]{1,0:T(8,128)(2,1)} %get-tuple-element.90), channel_id=1, source_target_pairs={{0,8},{4,12},{8,0},{12,4},{16,24},{20,28},{24,16},{28,20},{1,9},{5... | collective-permute-start | bytes 3932168 | tf_op jit(solution)/shard_map/ppermute | solution.py:81
  841.2 29.6 %collective-permute-start.48 = (bf16[256,2560]{1,0:T(8,128)(2,1)}, bf16[256,2560]{1,0:T(8,128)(2,1)}, u32[]{:S(2)}, u32[]{:S(2)}) collective-permute-start(bf16[256,2560]{1,0:T(8,128)(2,1)} %get-tuple-element.91), channel_id=1, source_target_pairs={{0,16},{4,20},{8,24},{12,28},{16,0},{20,4},{24,8},{28,12},{1,17},{... | collective-permute-start | bytes 3932168 | tf_op jit(solution)/shard_map/ppermute | solution.py:81
  870.9 17.9 %collective-permute-start.49 = (bf16[128,2560]{1,0:T(8,128)(2,1)}, bf16[128,2560]{1,0:T(8,128)(2,1)S(1)}, u32[]{:S(2)}, u32[]{:S(2)}) collective-permute-start(bf16[128,2560]{1,0:T(8,128)(2,1)} %get-tuple-element.92), channel_id=1, source_target_pairs={{0,8},{4,12},{8,0},{12,4},{16,24},{20,28},{24,16},{28,20},{1,9},{5... | collective-permute-start | bytes 1966088 | tf_op jit(solution)/shard_map/ppermute | solution.py:81
  871.5 18.1 %collective-permute-start.50 = (bf16[128,2560]{1,0:T(8,128)(2,1)}, bf16[128,2560]{1,0:T(8,128)(2,1)}, u32[]{:S(2)}, u32[]{:S(2)}) collective-permute-start(bf16[128,2560]{1,0:T(8,128)(2,1)} %get-tuple-element.93), channel_id=1, source_target_pairs={{0,16},{4,20},{8,24},{12,28},{16,0},{20,4},{24,8},{28,12},{1,17},{... | collective-permute-start | bytes 1966088 | tf_op jit(solution)/shard_map/ppermute | solution.py:81
  876.0 26.9 %collective-permute-start.51 = (bf16[128,2560]{1,0:T(8,128)(2,1)}, bf16[128,2560]{1,0:T(8,128)(2,1)}, u32[]{:S(2)}, u32[]{:S(2)}) collective-permute-start(bf16[128,2560]{1,0:T(8,128)(2,1)} %get-tuple-element.94), channel_id=1, source_target_pairs={{0,8},{4,12},{8,0},{12,4},{16,24},{20,28},{24,16},{28,20},{1,9},{5... | collective-permute-start | bytes 1966088 | tf_op jit(solution)/shard_map/ppermute | solution.py:81
  877.5 25.9 %collective-permute-start.52 = (bf16[128,2560]{1,0:T(8,128)(2,1)}, bf16[128,2560]{1,0:T(8,128)(2,1)}, u32[]{:S(2)}, u32[]{:S(2)}) collective-permute-start(bf16[128,2560]{1,0:T(8,128)(2,1)} %get-tuple-element.95), channel_id=1, source_target_pairs={{0,16},{4,20},{8,24},{12,28},{16,0},{20,4},{24,8},{28,12},{1,17},{... | collective-permute-start | bytes 1966088 | tf_op jit(solution)/shard_map/ppermute | solution.py:81
  878.5 49.4 %collective-permute-start.54 = (bf16[256,2560]{1,0:T(8,128)(2,1)}, bf16[256,2560]{1,0:T(8,128)(2,1)S(1)}, u32[]{:S(2)}, u32[]{:S(2)}) collective-permute-start(bf16[256,2560]{1,0:T(8,128)(2,1)} %get-tuple-element.97), channel_id=1, source_target_pairs={{0,16},{4,20},{8,24},{12,28},{16,0},{20,4},{24,8},{28,12},{1,17},{... | collective-permute-start | bytes 3932168 | tf_op jit(solution)/shard_map/ppermute | solution.py:81
  888.7 39.2 %collective-permute-start.55 = (bf16[256,2560]{1,0:T(8,128)(2,1)}, bf16[256,2560]{1,0:T(8,128)(2,1)S(1)}, u32[]{:S(2)}, u32[]{:S(2)}) collective-permute-start(bf16[256,2560]{1,0:T(8,128)(2,1)} %get-tuple-element.98), channel_id=1, source_target_pairs={{0,8},{4,12},{8,0},{12,4},{16,24},{20,28},{24,16},{28,20},{1,9},{5... | collective-permute-start | bytes 3932168 | tf_op jit(solution)/shard_map/ppermute | solution.py:81
  961.0 22.4 %collective-permute-start.64 = (bf16[128,3072]{1,0:T(8,128)(2,1)}, bf16[128,3072]{1,0:T(8,128)(2,1)}, u32[]{:S(2)}, u32[]{:S(2)}) collective-permute-start(bf16[128,3072]{1,0:T(8,128)(2,1)} %get-tuple-element.101), channel_id=1, source_target_pairs={{0,8},{4,12},{8,0},{12,4},{16,24},{20,28},{24,16},{28,20},{1,9},{5... | collective-permute-start | bytes 2359304 | tf_op jit(solution)/shard_map/ppermute | solution.py:81
  962.4 26.6 %collective-permute-start.65 = (bf16[128,3072]{1,0:T(8,128)(2,1)}, bf16[128,3072]{1,0:T(8,128)(2,1)}, u32[]{:S(2)}, u32[]{:S(2)}) collective-permute-start(bf16[128,3072]{1,0:T(8,128)(2,1)} %get-tuple-element.102), channel_id=1, source_target_pairs={{0,16},{4,20},{8,24},{12,28},{16,0},{20,4},{24,8},{28,12},{1,17},{... | collective-permute-start | bytes 2359304 | tf_op jit(solution)/shard_map/ppermute | solution.py:81
  967.6 34.5 %collective-permute-start.68 = (bf16[4,4,26752]{2,1,0:T(4,128)(2,1)}, bf16[4,4,26752]{2,1,0:T(4,128)(2,1)}, u32[]{:S(2)}, u32[]{:S(2)}) collective-permute-start(bf16[4,4,26752]{2,1,0:T(4,128)(2,1)} %slice.825), channel_id=1, source_target_pairs={{0,16},{4,20},{8,24},{12,28},{16,0},{20,4},{24,8},{28,12},{1,17},{... | collective-permute-start | bytes 2568200 | tf_op jit(solution)/shard_map/ppermute | solution.py:81
  972.4 21.3 %collective-permute-start.61 = (bf16[3,256,640]{2,1,0:T(8,128)(2,1)}, bf16[3,256,640]{2,1,0:T(8,128)(2,1)}, u32[]{:S(2)}, u32[]{:S(2)}) collective-permute-start(bf16[3,256,640]{2,1,0:T(8,128)(2,1)} %dynamic-slice_bitcast_fusion.1), channel_id=1, source_target_pairs={{3,2},{7,6},{11,10},{15,14},{19,18},{23,22},{27,26},{31,30}} | collective-permute-start | bytes 2949128 | tf_op jit(solution)/shard_map/ppermute | solution.py:192
  1003.8 59.9 %collective-permute-start.69 = (bf16[2,4,26752]{2,1,0:T(4,128)(2,1)S(1)}, bf16[2,4,26752]{2,1,0:T(4,128)(2,1)S(1)}, u32[]{:S(2)}, u32[]{:S(2)}) collective-permute-start(bf16[2,4,26752]{2,1,0:T(4,128)(2,1)S(1)} %slice.827), channel_id=1, source_target_pairs={{0,8},{4,12},{8,0},{12,4},{16,24},{20,28},{24,16},{28,20},{1,9},{5... | collective-permute-start | bytes 1284104 | tf_op jit(solution)/shard_map/ppermute | solution.py:81
  1008.5 91.6 %collective-permute-start.58 = (bf16[3,256,640]{2,1,0:T(8,128)(2,1)S(1)}, bf16[3,256,640]{2,1,0:T(8,128)(2,1)S(1)}, u32[]{:S(2)}, u32[]{:S(2)}) collective-permute-start(bf16[3,256,640]{2,1,0:T(8,128)(2,1)S(1)} %get-tuple-element.183), channel_id=1, source_target_pairs={{0,1},{4,5},{8,9},{12,13},{16,17},{20,21},{24,25},{28,29}} | collective-permute-start | bytes 2949128 | tf_op jit(solution)/shard_map/ppermute | solution.py:191
  1064.1 40.7 %collective-permute-start.70 = (bf16[1,4,26752]{2,1,0:T(4,128)(2,1)S(1)}, bf16[1,4,26752]{2,1,0:T(4,128)(2,1)S(1)}, u32[]{:S(2)}, u32[]{:S(2)}) collective-permute-start(bf16[1,4,26752]{2,1,0:T(4,128)(2,1)S(1)} %slice.829), channel_id=1, source_target_pairs={{0,4},{4,0},{8,12},{12,8},{16,20},{20,16},{24,28},{28,24},{1,5},{5... | collective-permute-start | bytes 642056 | tf_op jit(solution)/shard_map/ppermute | solution.py:81
  1100.4 24.0 %collective-permute-start.59 = (bf16[3,256,640]{2,1,0:T(8,128)(2,1)S(1)}, bf16[3,256,640]{2,1,0:T(8,128)(2,1)S(1)}, u32[]{:S(2)}, u32[]{:S(2)}) collective-permute-start(bf16[3,256,640]{2,1,0:T(8,128)(2,1)S(1)} %fusion.41), channel_id=1, source_target_pairs={{0,1},{1,2},{4,5},{5,6},{8,9},{9,10},{12,13},{13,14},{16,17},{17,1... | collective-permute-start | bytes 2949128 | tf_op jit(solution)/shard_map/ppermute | solution.py:191
  1105.9 24.1 %collective-permute-start.71 = (bf16[26752]{0:T(1024)(128)(2,1)S(1)}, bf16[26752]{0:T(1024)(128)(2,1)S(1)}, u32[]{:S(2)}, u32[]{:S(2)}) collective-permute-start(bf16[26752]{0:T(1024)(128)(2,1)S(1)} %get-tuple-element.179), channel_id=1, source_target_pairs={{0,1},{1,2},{2,3},{3,0},{4,5},{5,6},{6,7},{7,4},{8,9},{9,10},{10,1... | collective-permute-start | bytes 160520 | tf_op jit(solution)/shard_map/ppermute | solution.py:164
  1106.0 24.0 %collective-permute-start.73 = (bf16[26752]{0:T(1024)(128)(2,1)S(1)}, bf16[26752]{0:T(1024)(128)(2,1)S(1)}, u32[]{:S(2)}, u32[]{:S(2)}) collective-permute-start(bf16[26752]{0:T(1024)(128)(2,1)S(1)} %get-tuple-element.180), channel_id=1, source_target_pairs={{0,3},{1,0},{2,1},{3,2},{4,7},{5,4},{6,5},{7,6},{8,11},{9,8},{10,9... | collective-permute-start | bytes 160520 | tf_op jit(solution)/shard_map/ppermute | solution.py:164
  1109.8 20.2 %collective-permute-start.72 = (bf16[26752]{0:T(1024)(128)(2,1)S(1)}, bf16[26752]{0:T(1024)(128)(2,1)S(1)}, u32[]{:S(2)}, u32[]{:S(2)}) collective-permute-start(bf16[26752]{0:T(1024)(128)(2,1)S(1)} %get-tuple-element.181), channel_id=1, source_target_pairs={{0,2},{1,3},{2,0},{3,1},{4,6},{5,7},{6,4},{7,5},{8,10},{9,11},{10,... | collective-permute-start | bytes 160520 | tf_op jit(solution)/shard_map/ppermute | solution.py:164
  1110.1 22.1 %collective-permute-start.63 = (bf16[3,256,640]{2,1,0:T(8,128)(2,1)}, bf16[3,256,640]{2,1,0:T(8,128)(2,1)S(1)}, u32[]{:S(2)}, u32[]{:S(2)}) collective-permute-start(bf16[3,256,640]{2,1,0:T(8,128)(2,1)} %get-tuple-element.182), channel_id=1, source_target_pairs={{1,0},{2,1},{3,2},{5,4},{6,5},{7,6},{9,8},{10,9},{11,10},{13,12},{... | collective-permute-start | bytes 2949128 | tf_op jit(solution)/shard_map/ppermute | solution.py:192
  1125.5 16.3 %collective-permute-start.60 = (bf16[3,256,640]{2,1,0:T(8,128)(2,1)}, bf16[3,256,640]{2,1,0:T(8,128)(2,1)S(1)}, u32[]{:S(2)}, u32[]{:S(2)}) collective-permute-start(bf16[3,256,640]{2,1,0:T(8,128)(2,1)} %add_convert_fusion.15), channel_id=1, source_target_pairs={{0,1},{1,2},{2,3},{4,5},{5,6},{6,7},{8,9},{9,10},{10,11},{12,13},{... | collective-permute-start | bytes 2949128 | tf_op jit(solution)/shard_map/ppermute | solution.py:191
  (147 other events, 1166.6 us)
Sparse Core Ops, SparseCore 0:
  12.1 43.3 all-gather.7
  57.6 54.7 all-gather.17
  288.0 80.7 all-gather.9
  370.2 79.2 all-gather.11
  451.7 75.2 reduce-scatter.4
  531.9 75.2 reduce-scatter.6
  619.2 76.5 reduce-scatter.8
  698.2 80.7 reduce-scatter.10
  780.5 149.0 all-gather.15
  931.1 164.0 all-gather.13

commit v13 on v12

--- a/solution.py
+++ b/solution.py
@@ -186,7 +186,7 @@
         t, n = self.rounds, self.n
         right, left = self.block(self.turn + n - t), self.block(self.turn + t)
         if t > 1:
-            before = fence([self.right, self.left], *others)
+            before = fence([self.right, self.left], self.blocks, *others)
             right, left = add_all([right, before[0]]), add_all([left, before[1]])
         self.right = lax.ppermute(right, "tensor", [(k, k + 1) for k in range(min(t, n - 1))])
         self.left = lax.ppermute(left, "tensor", [(k, k - 1) for k in range(max(n - t, 1), n)])
@@ -270,6 +270,25 @@
         cost_estimate=LITTLE,
         name="permute",
     )(table, values)
+
+
+def move_kernel(in_ref, out_ref):
+    out_ref[...] = in_ref[...]
+
+
+def move(values):
+    rows, d_model = values.shape
+    spec = pl.BlockSpec((max(k for k in range(16, 289, 16) if rows % k == 0), d_model), lambda r: (r, 0))
+    return pl.pallas_call(
+        move_kernel,
+        grid=(rows // spec.block_shape[0],),
+        in_specs=[spec],
+        out_specs=spec,
+        out_shape=jax.ShapeDtypeStruct(values.shape, values.dtype),
+        compiler_params=pltpu.CompilerParams(vmem_limit_bytes=VMEM),
+        cost_estimate=LITTLE,
+        name="move",
+    )(values)
 
 
 def permute_gain(values, table):
@@ -697,6 +716,9 @@
     owned = jnp.stack([total.finish().reshape(d_own, n, width // n) for total in (sum_o, sum_g, sum_r)])
     owned = LineSum(owned.transpose(2, 0, 1, 3), n)
     owned.go()
+    tokens_out = move(tokens_out)
+    if n > 2:
+        owned.go(tokens_out)
     d_lru, dpar = fence([d_lru, dpar], *got_r)
     if sum_dn.square:
         sum_dn.hop(fence(sum_dn.sources(), *got_r))
@@ -704,6 +726,7 @@
     g_gu, g_dn = sum_gu.finish().astype(F32), sum_dn.finish().astype(F32)
     g_all = owned.finish()
     (output,) = fence([result], owned.right, owned.left, g_gu, g_dn, cost=MUCH)
+    output = move(output)
     g_o, g_g, g_r = g_all[0], g_all[1], g_all[2]
 
     d_gain = permute_gain(jnp.stack([gain_one, gain_two]), inverse)

time: 1180 us -> 1170 us (level)
  starting transfers between devices: 143 us -> 97.3 us
  waiting for transfers between devices: 329 us -> 360 us
  Pallas kernels: 121 us -> 139 us
  local copies, waits for them, and re-layouts: 119 us -> 101 us
    ppermute x3, starting transfers between devices: 64.2 us -> 18.9 us  [go(): lax.ppermute(right, 'tensor', [(k, k + 1) for k in range(min(t, n - 1))])]
    unnamed x269 -> x271, local copies, waits for them, and re-layouts: 59.8 us -> 41 us
    ppermute x3, waiting for transfers between devices: 0.01 us -> 18 us  [go(): lax.ppermute(left, 'tensor', [(k, k - 1) for k in range(max(n - t, 1), n)])]
    pallas_call x0 -> x2, Pallas kernels: none -> 17.9 us  [move(): pl.pallas_call(move_kernel, grid=(rows // spec.block_shape[0],), in_specs...]
    ppermute x3, waiting for transfers between devices: 58.5 us -> 73.2 us  [go(): lax.ppermute(right, 'tensor', [(k, k + 1) for k in range(min(t, n - 1))])]
    convert_element_type x22 -> x21, other arithmetic: 61.9 us -> 65.1 us  [add_all(): return total.astype(BF)]
  transfers between devices with their start and end apart: 84 -> 84, of which waited for: 39 -> 39; matrix products, arithmetic and copies ran while one was open for 43% -> 43% of each run, Pallas kernels for 10% -> 11%
where the time goes in v13:
time: 1170 us; the launch traced here: 1160 us
  waiting for transfers between devices  360 us (31%)
  matrix products  306 us (26%)
  other arithmetic  140 us (12%)
  Pallas kernels  139 us (12%)
  local copies, waits for them, and re-layouts  101 us (9%)
  starting transfers between devices  97.3 us (8%)
  between operations  17.2 us (1%)
    dot_general x34, matrix products, dot(): lax.dot_general(left, right, (dims, ((), ())), preferred_element_type=F32)  306 us
    ppermute x58, waiting for transfers between devices, exchange(): return lax.ppermute(values, 'dp', [(k, k ^ 1 << bit) for k in range(size)])  243 us
    ppermute x3, waiting for transfers between devices, go(): lax.ppermute(right, 'tensor', [(k, k + 1) for k in range(min(t, n - 1))])  73.2 us
    convert_element_type x21, other arithmetic, add_all(): return total.astype(BF)  65.1 us
    pallas_call x3, Pallas kernels, kernel_call(): pl.pallas_call(body, grid_spec=pltpu.PrefetchScalarGridSpec(num_scalar_pr...  62.3 us
    ppermute x58, starting transfers between devices, exchange(): return lax.ppermute(values, 'dp', [(k, k ^ 1 << bit) for k in range(size)])  54 us
    unnamed x271, local copies, waits for them, and re-layouts  41 us
    pallas_call x7, Pallas kernels, assemble(): pl.pallas_call(body, in_specs=[place] * (count + len(others)), out_specs=...  35.6 us
  transfers between devices with their start and end apart: 84, of which 39 were waited for; matrix products, arithmetic and copies ran while one was open for 43% of the time, Pallas kernels for 11%

profile of v13, /device:TPU:0, one launch (start us, length us, event | category | flops | bytes accessed | tf_op | source)
XLA Modules:
  0.0 1160.7 jit_solution(5533176252313046453)
XLA Ops:
  38.1 16.2 %collective-permute-done.1.refs_2_.refs_1_ = bf16[256,3072]{1,0:T(8,128)(2,1)S(1)} collective-permute-done((bf16[256,3072]{1,0:T(8,128)(2,1)}, bf16[256,3072]{1,0:T(8,128)(2,1)S(1)}, u32[]{:S(2)}, u32[]{:S(2)}) %collective-permute-start.1) | collective-permute-done | bytes 1572896 | tf_op jit(solution)/shard_map/ppermute | solution.py:81
  62.8 27.5 %collective-permute-done.9.refs_4_ = bf16[256,2560]{1,0:T(8,128)(2,1)S(1)} collective-permute-done((bf16[256,2560]{1,0:T(8,128)(2,1)S(1)}, bf16[256,2560]{1,0:T(8,128)(2,1)S(1)}, u32[]{:S(2)}, u32[]{:S(2)}) %collective-permute-start.9) | collective-permute-done | bytes 1310752 | tf_op jit(solution)/shard_map/ppermute | solution.py:81
  104.6 9.5 collective-permute-done.10.refs_2_
  122.2 7.3 collective-permute-done.6
  149.7 7.3 convolution_add_fusion.pre_ref
  157.0 18.8 %recurrence.1 = (f32[512,2560]{1,0:T(8,128)}, f32[512,2560]{1,0:T(8,128)}, f32[512,2560]{1,0:T(8,128)}, f32[512,2560]{1,0:T(8,128)}, f32[512,2560]{1,0:T(8,128)}, /*index=5*/f32[512,2560]{1,0:T(8,128)}) custom-call(s32[1]{0:T(128)} %sub.38.live_ref, f32[528,2560]{1,0:T(8,128)} %convolution_add_fusion.pre_ref, f32[8,2560]{1,0:T(8,128)} %pad_maximum_fusion.14.par_ref, ...), custom_call_target="tpu_custom_call" | custom-call | flops 1024 | bytes 1024 | tf_op jit(solution)/shard_map/recurrence/pallas_call | solution.py:494
  184.5 5.4 collective-permute-start.18
  218.9 9.8 fusion.22
  228.7 9.9 collective-permute-done.21.refs_1_
  244.7 14.2 %collective-permute-done.22.refs_2_.refs_3_ = bf16[128,2560]{1,0:T(8,128)(2,1)S(1)} collective-permute-done((bf16[128,2560]{1,0:T(8,128)(2,1)S(1)}, bf16[128,2560]{1,0:T(8,128)(2,1)S(1)}, u32[]{:S(2)}, u32[]{:S(2)}) %collective-permute-start.22) | collective-permute-done | bytes 655392 | tf_op jit(solution)/shard_map/ppermute | solution.py:81
  292.9 6.1 assemble.10.refs_0_
  303.0 18.7 %collective-permute-done.29.refs_4_ = bf16[256,1536]{1,0:T(8,128)(2,1)S(1)} collective-permute-done((bf16[256,1536]{1,0:T(8,128)(2,1)}, bf16[256,1536]{1,0:T(8,128)(2,1)S(1)}, u32[]{:S(2)}, u32[]{:S(2)}) %collective-permute-start.29) | collective-permute-done | bytes 786464 | tf_op jit(solution)/shard_map/ppermute | solution.py:81
  323.6 9.1 collective-permute-done.30.refs_2_
  337.8 5.2 collective-permute-done.32.refs_1_
  349.3 5.9 permute.7
  355.2 5.8 permute.6
  361.4 9.2 assemble.11
  370.7 19.1 %fusion.83 = f32[1024,3072]{1,0:T(8,128)} fusion(bf16[1024,2048]{1,0:T(8,128)(2,1)} %all-gather.10.cloned.1.call-done, bf16[2048,3072]{1,0:T(8,128)(2,1)} %assemble.11), kind=kOutput, calls=%fused_computation.263 | convolution fusion | flops 12884901888 | bytes 29360128 | tf_op jit(solution)/shard_map/dot_general | solution.py:25
  389.8 16.0 %fusion.6 = (bf16[1024,1536]{1,0:T(8,128)(2,1)S(1)}, bf16[1024,1536]{1,0:T(8,128)(2,1)S(1)}, bf16[1024,1536]{1,0:T(8,128)(2,1)}) fusion(f32[1024,3072]{1,0:T(8,128)} %fusion.83, bf16[1024,2048]{1,0:T(8,128)(2,1)S(1)} %copy-done.36, bf16[2048,1536]{1,0:T(8,128)(2,1)} %assemble.13), kind=kOutput, calls=%fused_computation.15 | convolution fusion | flops 6483345408 | bytes 32505856 | tf_op jit(solution)/shard_map/dot_general | solution.py:25
  407.4 17.6 %convolution_convert_fusion.7.refs_1_ = bf16[1024,2048]{1,0:T(8,128)(2,1)} fusion(bf16[2048,3072]{1,0:T(8,128)(2,1)} %assemble.11, bf16[1024,1536]{1,0:T(8,128)(2,1)S(1)} %get-tuple-element.195, bf16[1024,1536]{1,0:T(8,128)(2,1)S(1)} %get-tuple-element.194), kind=kOutput, calls=%fused_computation.73 | convolution fusion | flops 12899581952 | bytes 23068672 | tf_op jit(solution)/shard_map/dot_general | solution.py:25
  425.3 24.3 %all-gather.12.cloned.1.call-done.refs_0_ = bf16[1024,2048]{1,0:T(8,128)(2,1)} async-done(((bf16[256,2048]{1,0:T(8,128)(2,1)}), bf16[1024,2048]{1,0:T(8,128)(2,1)}) %all-gather.12.cloned.1.call-update) | async-done | bytes 4194320 | tf_op jit(solution)/shard_map/all_gather | solution.py:630
  449.6 19.0 %fusion.84 = f32[1024,3072]{1,0:T(8,128)} fusion(bf16[1024,2048]{1,0:T(8,128)(2,1)} %fence.42, bf16[2048,3072]{1,0:T(8,128)(2,1)} %assemble.11), kind=kOutput, calls=%fused_computation.264 | convolution fusion | flops 12884901888 | bytes 29360128 | tf_op jit(solution)/shard_map/dot_general | solution.py:25
  468.7 15.5 %fusion.13 = (bf16[1024,1536]{1,0:T(8,128)(2,1)}, bf16[1024,1536]{1,0:T(8,128)(2,1)}, bf16[1024,1536]{1,0:T(8,128)(2,1)}) fusion(f32[1024,3072]{1,0:T(8,128)} %fusion.84, bf16[1024,2048]{1,0:T(8,128)(2,1)S(1)} %copy-done.34, bf16[2048,1536]{1,0:T(8,128)(2,1)S(1)} %bitcast.174), kind=kOutput, calls=%fused_computation.22 | convolution fusion | flops 6483345408 | bytes 32505856 | tf_op jit(solution)/shard_map/dot_general | solution.py:25
  484.1 5.6 pad_maximum_fusion.refs_1_
  489.7 18.8 %convolution_convert_fusion.6.refs_2_ = bf16[1024,2048]{1,0:T(8,128)(2,1)} fusion(bf16[2048,3072]{1,0:T(8,128)(2,1)} %assemble.11, bf16[1024,1536]{1,0:T(8,128)(2,1)} %get-tuple-element.193, bf16[1024,1536]{1,0:T(8,128)(2,1)S(1)} %copy-done.53), kind=kOutput, calls=%fused_computation.72 | convolution fusion | flops 12899581952 | bytes 23068672 | tf_op jit(solution)/shard_map/dot_general | solution.py:25
  510.4 5.7 pad_maximum_fusion.1.refs_1_
  516.1 7.4 fusion.36
  523.5 8.3 convolution_convert_fusion.9.refs_6_.refs_0_
  531.9 9.7 add_convert_fusion.2
  541.6 9.7 fusion.30
  551.4 11.8 %add_convert_fusion = bf16[1024,3072]{1,0:T(8,128)(2,1)} fusion(f32[1024,3072]{1,0:T(8,128)} %fusion.30, bf16[1024,3072]{1,0:T(8,128)(2,1)S(1)} %bitcast.163, bf16[1024,2048]{1,0:T(8,128)(2,1)S(1)} %copy-done.46), kind=kOutput, calls=%fused_computation.2 | convolution fusion | flops 6448742400 | bytes 27262976 | tf_op jit(solution)/shard_map/dot_general | solution.py:25
  563.6 11.0 fusion.33
  574.7 11.3 convolution_convert_fusion.8.refs_7_.refs_1_
  586.0 5.4 fusion.39
  591.3 7.1 add_convert_fusion.3
  598.4 10.2 add_convert_fusion.1
  631.1 5.7 fusion.50
  642.1 17.1 %back_scan.1 = (f32[512,2560]{1,0:T(8,128)}, f32[512,2560]{1,0:T(8,128)}, f32[8,2560]{1,0:T(8,128)}, bf16[512,2560]{1,0:T(8,128)(2,1)}) custom-call(s32[1]{0:T(128)} %sub.38.live_ref, f32[512,2560]{1,0:T(8,128)} %get-tuple-element.264.refs_2_.pre_ref, f32[512,2560]{1,0:T(8,128)} %convolution_add_fusion.1.grad_ref, f32[512,2560]{1,0:T(8,128)} %get-tuple-element.80.decay_ref, ...), custom_call_target="tpu_custom_call" | custom-call | flops 1024 | bytes 1024 | tf_op jit(solution)/shard_map/back_scan/pallas_call | solution.py:494
  664.1 11.5 collective-permute-done.38.refs_4_
  677.3 26.3 %recurrence_back.1 = (f32[528,2560]{1,0:T(8,128)}, f32[8,2560]{1,0:T(8,128)}, bf16[4,160,1280]{2,1,0:T(8,128)(2,1)}) custom-call(s32[1]{0:T(128)} %sub.38.live_ref, f32[528,2560]{1,0:T(8,128)} %convolution_add_fusion.pre_ref, f32[8,2560]{1,0:T(8,128)} %pad_maximum_fusion.14.par_ref, bf16[8,4,80,640]{3,2,1,0:T(8,128)(2,1)} %copy-done.13, ...), custom_call_target="tpu_custom_call" | custom-call | flops 1024 | bytes 1024 | tf_op jit(solution)/shard_map/recurrence_back/pallas_call | solution.py:494
  706.5 7.5 fusion.85
  714.0 6.8 fusion.86
  725.1 5.8 fusion.87
  738.6 6.1 add_convert_fusion.5.in_ref
  754.9 8.6 collective-permute-done.43.refs_2_
  765.9 7.3 convolution_convert_fusion.2
  776.3 6.0 convolution_convert_fusion
  787.6 6.1 convolution_convert_fusion.4
  810.5 5.2 convolution_convert_fusion.3
  815.8 6.9 convolution_convert_fusion.1
  826.5 12.5 %collective-permute-done.44.refs_3_ = bf16[256,2560]{1,0:T(8,128)(2,1)} collective-permute-done((bf16[256,2560]{1,0:T(8,128)(2,1)}, bf16[256,2560]{1,0:T(8,128)(2,1)}, u32[]{:S(2)}, u32[]{:S(2)}) %collective-permute-start.44) | collective-permute-done | bytes 1310752 | tf_op jit(solution)/shard_map/ppermute | solution.py:81
  849.4 20.4 %collective-permute-done.47.refs_2_ = bf16[256,2560]{1,0:T(8,128)(2,1)} collective-permute-done((bf16[256,2560]{1,0:T(8,128)(2,1)}, bf16[256,2560]{1,0:T(8,128)(2,1)}, u32[]{:S(2)}, u32[]{:S(2)}) %collective-permute-start.47) | collective-permute-done | bytes 1310752 | tf_op jit(solution)/shard_map/ppermute | solution.py:81
  879.7 9.2 collective-permute-done.49
  893.3 9.7 collective-permute-done.51
  907.8 20.3 %collective-permute-done.54.refs_3_ = bf16[256,2560]{1,0:T(8,128)(2,1)S(1)} collective-permute-done((bf16[256,2560]{1,0:T(8,128)(2,1)}, bf16[256,2560]{1,0:T(8,128)(2,1)S(1)}, u32[]{:S(2)}, u32[]{:S(2)}) %collective-permute-start.54) | collective-permute-done | bytes 1310752 | tf_op jit(solution)/shard_map/ppermute | solution.py:81
  952.0 9.0 move.2.refs_3_
  1002.5 8.7 collective-permute-done.68
  1016.6 13.1 %collective-permute-done.58.refs_0_ = bf16[3,256,640]{2,1,0:T(8,128)(2,1)} collective-permute-done((bf16[3,256,640]{2,1,0:T(8,128)(2,1)}, bf16[3,256,640]{2,1,0:T(8,128)(2,1)}, u32[]{:S(2)}, u32[]{:S(2)}) %collective-permute-start.58) | collective-permute-done | bytes 983072 | tf_op jit(solution)/shard_map/ppermute | solution.py:191
  1033.0 5.0 collective-permute-start.60
  1043.6 37.5 %collective-permute-done.60.refs_0_ = bf16[3,256,640]{2,1,0:T(8,128)(2,1)S(1)} collective-permute-done((bf16[3,256,640]{2,1,0:T(8,128)(2,1)S(1)}, bf16[3,256,640]{2,1,0:T(8,128)(2,1)S(1)}, u32[]{:S(2)}, u32[]{:S(2)}) %collective-permute-start.60) | collective-permute-done | bytes 983072 | tf_op jit(solution)/shard_map/ppermute | solution.py:191
  1088.6 9.2 collective-permute-start.62
  1100.0 18.0 %collective-permute-done.63.refs_2_ = bf16[3,256,640]{2,1,0:T(8,128)(2,1)S(1)} collective-permute-done((bf16[3,256,640]{2,1,0:T(8,128)(2,1)}, bf16[3,256,640]{2,1,0:T(8,128)(2,1)S(1)}, u32[]{:S(2)}, u32[]{:S(2)}) %collective-permute-start.63) | collective-permute-done | bytes 983072 | tf_op jit(solution)/shard_map/ppermute | solution.py:192
  1118.0 22.5 %collective-permute-done.62.refs_1_ = bf16[3,256,640]{2,1,0:T(8,128)(2,1)S(1)} collective-permute-done((bf16[3,256,640]{2,1,0:T(8,128)(2,1)}, bf16[3,256,640]{2,1,0:T(8,128)(2,1)S(1)}, u32[]{:S(2)}, u32[]{:S(2)}) %collective-permute-start.62) | collective-permute-done | bytes 983072 | tf_op jit(solution)/shard_map/ppermute | solution.py:191
  1144.7 8.9 move.3
  (633 shorter events, 393.6 us)
Async XLA Ops:
  7.2 48.5 %all-gather.8.cloned.1.call-start = ((), (), s32[]{:S(2)}) async-start(), calls=%async_computation.4 | async-start | bytes 2150400 | tf_op jit(solution)/shard_map/all_gather | solution.py:567
  12.0 102.1 %all-gather.18.cloned.1.call-start = ((), (), s32[]{:S(2)}) async-start(), calls=%async_computation.13 | async-start | bytes 3276800 | tf_op jit(solution)/shard_map/all_gather | solution.py:568
  15.5 38.7 %collective-permute-start.1 = (bf16[256,3072]{1,0:T(8,128)(2,1)}, bf16[256,3072]{1,0:T(8,128)(2,1)S(1)}, u32[]{:S(2)}, u32[]{:S(2)}) collective-permute-start(bf16[256,3072]{1,0:T(8,128)(2,1)} %pad_maximum_fusion.8.refs_0_), channel_id=1, source_target_pairs={{0,16},{4,20},{8,24},{12,28},{16,0},{20,4},{24,8},{28,12},{1,17},{... | collective-permute-start | bytes 4718600 | tf_op jit(solution)/shard_map/ppermute | solution.py:81
  19.6 36.1 %collective-permute-start = (bf16[256,3072]{1,0:T(8,128)(2,1)}, bf16[256,3072]{1,0:T(8,128)(2,1)S(1)}, u32[]{:S(2)}, u32[]{:S(2)}) collective-permute-start(bf16[256,3072]{1,0:T(8,128)(2,1)} %pad_maximum_fusion.8.refs_0_), channel_id=1, source_target_pairs={{0,8},{4,12},{8,0},{12,4},{16,24},{20,28},{24,16},{28,20},{1,9},{5... | collective-permute-start | bytes 4718600 | tf_op jit(solution)/shard_map/ppermute | solution.py:81
  56.9 313.8 %all-gather.10.cloned.1.call-start = ((), (), s32[]{:S(2)}) async-start(), calls=%async_computation.5 | async-start | bytes 5242880 | tf_op jit(solution)/shard_map/all_gather | solution.py:630
  58.5 31.8 %collective-permute-start.9 = (bf16[256,2560]{1,0:T(8,128)(2,1)S(1)}, bf16[256,2560]{1,0:T(8,128)(2,1)S(1)}, u32[]{:S(2)}, u32[]{:S(2)}) collective-permute-start(bf16[256,2560]{1,0:T(8,128)(2,1)S(1)} %bitcast.179), channel_id=1, source_target_pairs={{0,16},{4,20},{8,24},{12,28},{16,0},{20,4},{24,8},{28,12},{1,17},{... | collective-permute-start | bytes 3932168 | tf_op jit(solution)/shard_map/ppermute | solution.py:81
  59.4 32.5 %collective-permute-start.7 = (bf16[256,2560]{1,0:T(8,128)(2,1)S(1)}, bf16[256,2560]{1,0:T(8,128)(2,1)S(1)}, u32[]{:S(2)}, u32[]{:S(2)}) collective-permute-start(bf16[256,2560]{1,0:T(8,128)(2,1)S(1)} %bitcast.180), channel_id=1, source_target_pairs={{0,8},{4,12},{8,0},{12,4},{16,24},{20,28},{24,16},{28,20},{1,9},{5... | collective-permute-start | bytes 3932168 | tf_op jit(solution)/shard_map/ppermute | solution.py:81
  61.0 38.5 %collective-permute-start.4 = (bf16[320,640]{1,0:T(8,128)(2,1)S(1)}, bf16[320,640]{1,0:T(8,128)(2,1)S(1)}, u32[]{:S(2)}, u32[]{:S(2)}) collective-permute-start(bf16[320,640]{1,0:T(8,128)(2,1)S(1)} %bitcast.191), channel_id=1, source_target_pairs={{0,16},{4,20},{8,24},{12,28},{16,0},{20,4},{24,8},{28,12},{1,17},{... | collective-permute-start | bytes 1228808 | tf_op jit(solution)/shard_map/ppermute | solution.py:81
  62.3 39.0 %collective-permute-start.2 = (bf16[320,640]{1,0:T(8,128)(2,1)S(1)}, bf16[320,640]{1,0:T(8,128)(2,1)S(1)}, u32[]{:S(2)}, u32[]{:S(2)}) collective-permute-start(bf16[320,640]{1,0:T(8,128)(2,1)S(1)} %bitcast.192), channel_id=1, source_target_pairs={{0,8},{4,12},{8,0},{12,4},{16,24},{20,28},{24,16},{28,20},{1,9},{5... | collective-permute-start | bytes 1228808 | tf_op jit(solution)/shard_map/ppermute | solution.py:81
  90.4 23.7 %collective-permute-start.10 = (bf16[128,2560]{1,0:T(8,128)(2,1)S(1)}, bf16[128,2560]{1,0:T(8,128)(2,1)}, u32[]{:S(2)}, u32[]{:S(2)}) collective-permute-start(bf16[128,2560]{1,0:T(8,128)(2,1)S(1)} %slice.704), channel_id=1, source_target_pairs={{0,8},{4,12},{8,0},{12,4},{16,24},{20,28},{24,16},{28,20},{1,9},{5... | collective-permute-start | bytes 1966088 | tf_op jit(solution)/shard_map/ppermute | solution.py:81
  93.0 21.1 %collective-permute-start.8 = (bf16[128,2560]{1,0:T(8,128)(2,1)S(1)}, bf16[128,2560]{1,0:T(8,128)(2,1)}, u32[]{:S(2)}, u32[]{:S(2)}) collective-permute-start(bf16[128,2560]{1,0:T(8,128)(2,1)S(1)} %slice.703), channel_id=1, source_target_pairs={{0,16},{4,20},{8,24},{12,28},{16,0},{20,4},{24,8},{28,12},{1,17},{... | collective-permute-start | bytes 1966088 | tf_op jit(solution)/shard_map/ppermute | solution.py:81
  100.2 19.3 %collective-permute-start.5 = (bf16[160,640]{1,0:T(8,128)(2,1)}, bf16[160,640]{1,0:T(8,128)(2,1)}, u32[]{:S(2)}, u32[]{:S(2)}) collective-permute-start(bf16[160,640]{1,0:T(8,128)(2,1)} %slice.695), channel_id=1, source_target_pairs={{0,8},{4,12},{8,0},{12,4},{16,24},{20,28},{24,16},{28,20},{1,9},{5... | collective-permute-start | bytes 614408 | tf_op jit(solution)/shard_map/ppermute | solution.py:81
  118.5 26.3 %collective-permute-start.13 = (bf16[1024,2560]{1,0:T(8,128)(2,1)}, bf16[1024,2560]{1,0:T(8,128)(2,1)}, u32[]{:S(2)}, u32[]{:S(2)}) collective-permute-start(bf16[1024,2560]{1,0:T(8,128)(2,1)} %assemble.7), channel_id=1, source_target_pairs={{0,4},{4,0},{8,12},{12,8},{16,20},{20,16},{24,28},{28,24},{1,5},{5... | collective-permute-start | bytes 15728648 | tf_op jit(solution)/shard_map/ppermute | solution.py:81
  142.5 35.9 %collective-permute-start.12 = (bf16[256,2560]{1,0:T(8,128)(2,1)}, bf16[256,2560]{1,0:T(8,128)(2,1)S(1)}, u32[]{:S(2)}, u32[]{:S(2)}) collective-permute-start(bf16[256,2560]{1,0:T(8,128)(2,1)} %fence.35.refs_0_), channel_id=1, source_target_pairs={{0,16},{4,20},{8,24},{12,28},{16,0},{20,4},{24,8},{28,12},{1,17},{... | collective-permute-start | bytes 3932168 | tf_op jit(solution)/shard_map/ppermute | solution.py:81
  143.3 35.0 %collective-permute-start.11 = (bf16[256,2560]{1,0:T(8,128)(2,1)}, bf16[256,2560]{1,0:T(8,128)(2,1)S(1)}, u32[]{:S(2)}, u32[]{:S(2)}) collective-permute-start(bf16[256,2560]{1,0:T(8,128)(2,1)} %fence.35.refs_0_), channel_id=1, source_target_pairs={{0,8},{4,12},{8,0},{12,4},{16,24},{20,28},{24,16},{28,20},{1,9},{5... | collective-permute-start | bytes 3932168 | tf_op jit(solution)/shard_map/ppermute | solution.py:81
  182.7 16.3 %collective-permute-start.14 = (bf16[128,2560]{1,0:T(8,128)(2,1)S(1)}, bf16[128,2560]{1,0:T(8,128)(2,1)S(1)}, u32[]{:S(2)}, u32[]{:S(2)}) collective-permute-start(bf16[128,2560]{1,0:T(8,128)(2,1)S(1)} %slice.537), channel_id=1, source_target_pairs={{0,8},{4,12},{8,0},{12,4},{16,24},{20,28},{24,16},{28,20},{1,9},{5... | collective-permute-start | bytes 1966088 | tf_op jit(solution)/shard_map/ppermute | solution.py:81
  183.4 15.9 %collective-permute-start.15 = (bf16[128,2560]{1,0:T(8,128)(2,1)S(1)}, bf16[128,2560]{1,0:T(8,128)(2,1)S(1)}, u32[]{:S(2)}, u32[]{:S(2)}) collective-permute-start(bf16[128,2560]{1,0:T(8,128)(2,1)S(1)} %slice.538), channel_id=1, source_target_pairs={{0,16},{4,20},{8,24},{12,28},{16,0},{20,4},{24,8},{28,12},{1,17},{... | collective-permute-start | bytes 1966088 | tf_op jit(solution)/shard_map/ppermute | solution.py:81
  207.2 31.4 %collective-permute-start.21 = (bf16[256,2560]{1,0:T(8,128)(2,1)}, bf16[256,2560]{1,0:T(8,128)(2,1)S(1)}, u32[]{:S(2)}, u32[]{:S(2)}) collective-permute-start(bf16[256,2560]{1,0:T(8,128)(2,1)} %fence.37.refs_0_), channel_id=1, source_target_pairs={{0,16},{4,20},{8,24},{12,28},{16,0},{20,4},{24,8},{28,12},{1,17},{... | collective-permute-start | bytes 3932168 | tf_op jit(solution)/shard_map/ppermute | solution.py:81
  208.4 31.1 %collective-permute-start.20 = (bf16[256,2560]{1,0:T(8,128)(2,1)}, bf16[256,2560]{1,0:T(8,128)(2,1)S(1)}, u32[]{:S(2)}, u32[]{:S(2)}) collective-permute-start(bf16[256,2560]{1,0:T(8,128)(2,1)} %fence.37.refs_0_), channel_id=1, source_target_pairs={{0,8},{4,12},{8,0},{12,4},{16,24},{20,28},{24,16},{28,20},{1,9},{5... | collective-permute-start | bytes 3932168 | tf_op jit(solution)/shard_map/ppermute | solution.py:81
  242.8 16.1 %collective-permute-start.22 = (bf16[128,2560]{1,0:T(8,128)(2,1)S(1)}, bf16[128,2560]{1,0:T(8,128)(2,1)S(1)}, u32[]{:S(2)}, u32[]{:S(2)}) collective-permute-start(bf16[128,2560]{1,0:T(8,128)(2,1)S(1)} %slice.547), channel_id=1, source_target_pairs={{0,8},{4,12},{8,0},{12,4},{16,24},{20,28},{24,16},{28,20},{1,9},{5... | collective-permute-start | bytes 1966088 | tf_op jit(solution)/shard_map/ppermute | solution.py:81
  271.8 20.1 %collective-permute-start.25 = (bf16[128,3072]{1,0:T(8,128)(2,1)}, bf16[128,3072]{1,0:T(8,128)(2,1)S(1)}, u32[]{:S(2)}, u32[]{:S(2)}) collective-permute-start(bf16[128,3072]{1,0:T(8,128)(2,1)} %slice.551), channel_id=1, source_target_pairs={{0,8},{4,12},{8,0},{12,4},{16,24},{20,28},{24,16},{28,20},{1,9},{5... | collective-permute-start | bytes 2359304 | tf_op jit(solution)/shard_map/ppermute | solution.py:81
  272.9 20.0 %collective-permute-start.26 = (bf16[128,3072]{1,0:T(8,128)(2,1)}, bf16[128,3072]{1,0:T(8,128)(2,1)}, u32[]{:S(2)}, u32[]{:S(2)}) collective-permute-start(bf16[128,3072]{1,0:T(8,128)(2,1)} %slice.552), channel_id=1, source_target_pairs={{0,16},{4,20},{8,24},{12,28},{16,0},{20,4},{24,8},{28,12},{1,17},{... | collective-permute-start | bytes 2359304 | tf_op jit(solution)/shard_map/ppermute | solution.py:81
  287.9 161.7 %all-gather.12.cloned.1.call-start = ((), (), s32[]{:S(2)}) async-start(), calls=%async_computation.6 | async-start | bytes 5242880 | tf_op jit(solution)/shard_map/all_gather | solution.py:630
  299.0 62.5 %collective-permute-start.27 = (bf16[1024,3072]{1,0:T(8,128)(2,1)}, bf16[1024,3072]{1,0:T(8,128)(2,1)}, u32[]{:S(2)}, u32[]{:S(2)}) collective-permute-start(bf16[1024,3072]{1,0:T(8,128)(2,1)} %assemble.10.refs_0_), channel_id=1, source_target_pairs={{0,4},{4,0},{8,12},{12,8},{16,20},{20,16},{24,28},{28,24},{1,5},{5... | collective-permute-start | bytes 18874376 | tf_op jit(solution)/shard_map/ppermute | solution.py:81
  301.6 20.1 %collective-permute-start.29 = (bf16[256,1536]{1,0:T(8,128)(2,1)}, bf16[256,1536]{1,0:T(8,128)(2,1)S(1)}, u32[]{:S(2)}, u32[]{:S(2)}) collective-permute-start(bf16[256,1536]{1,0:T(8,128)(2,1)} %fence.41.refs_0_), channel_id=1, source_target_pairs={{0,16},{4,20},{8,24},{12,28},{16,0},{20,4},{24,8},{28,12},{1,17},{... | collective-permute-start | bytes 2359304 | tf_op jit(solution)/shard_map/ppermute | solution.py:81
  302.0 20.3 %collective-permute-start.28 = (bf16[256,1536]{1,0:T(8,128)(2,1)}, bf16[256,1536]{1,0:T(8,128)(2,1)S(1)}, u32[]{:S(2)}, u32[]{:S(2)}) collective-permute-start(bf16[256,1536]{1,0:T(8,128)(2,1)} %fence.41.refs_0_), channel_id=1, source_target_pairs={{0,8},{4,12},{8,0},{12,4},{16,24},{20,28},{24,16},{28,20},{1,9},{5... | collective-permute-start | bytes 2359304 | tf_op jit(solution)/shard_map/ppermute | solution.py:81
  361.0 258.1 %reduce-scatter.5.cloned.1.call-start = ((), (), s32[]{:S(2)}) async-start(), calls=%async_computation.7 | async-start | bytes 5242880 | tf_op jit(solution)/shard_map/reduce_scatter | solution.py:639
  425.1 194.1 %reduce-scatter.7.cloned.1.call-start = ((), (), s32[]{:S(2)}) async-start(), calls=%async_computation.8 | async-start | bytes 5242880 | tf_op jit(solution)/shard_map/reduce_scatter | solution.py:639
  531.8 189.6 %reduce-scatter.9.cloned.1.call-start = ((), (), s32[]{:S(2)}) async-start(), calls=%async_computation.9 | async-start | bytes 5242880 | tf_op jit(solution)/shard_map/reduce_scatter | solution.py:661
  541.6 67.0 %collective-permute-start.33 = (bf16[1024,1536]{1,0:T(8,128)(2,1)}, bf16[1024,1536]{1,0:T(8,128)(2,1)S(1)}, u32[]{:S(2)}, u32[]{:S(2)}) collective-permute-start(bf16[1024,1536]{1,0:T(8,128)(2,1)} %add_convert_fusion.2), channel_id=1, source_target_pairs={{0,4},{4,0},{8,12},{12,8},{16,20},{20,16},{24,28},{28,24},{1,5},{5... | collective-permute-start | bytes 9437192 | tf_op jit(solution)/shard_map/ppermute | solution.py:81
  563.1 51.3 %collective-permute-start.34 = (bf16[1024,3072]{1,0:T(8,128)(2,1)}, bf16[1024,3072]{1,0:T(8,128)(2,1)}, u32[]{:S(2)}, u32[]{:S(2)}) collective-permute-start(bf16[1024,3072]{1,0:T(8,128)(2,1)} %add_convert_fusion), channel_id=1, source_target_pairs={{0,4},{4,0},{8,12},{12,8},{16,20},{20,16},{24,28},{28,24},{1,5},{5... | collective-permute-start | bytes 18874376 | tf_op jit(solution)/shard_map/ppermute | solution.py:81
  619.2 174.5 %reduce-scatter.11.cloned.1.call-start = ((), (), s32[]{:S(2)}) async-start(), calls=%async_computation.10 | async-start | bytes 5242880 | tf_op jit(solution)/shard_map/reduce_scatter | solution.py:661
  622.1 39.2 %collective-permute-start.36 = (bf16[256,1536]{1,0:T(8,128)(2,1)}, bf16[256,1536]{1,0:T(8,128)(2,1)}, u32[]{:S(2)}, u32[]{:S(2)}) collective-permute-start(bf16[256,1536]{1,0:T(8,128)(2,1)} %get-tuple-element.226.refs_3_), channel_id=1, source_target_pairs={{0,16},{4,20},{8,24},{12,28},{16,0},{20,4},{24,8},{28,12},{1,17},{... | collective-permute-start | bytes 2359304 | tf_op jit(solution)/shard_map/ppermute | solution.py:81
  623.5 39.2 %collective-permute-start.35 = (bf16[256,1536]{1,0:T(8,128)(2,1)}, bf16[256,1536]{1,0:T(8,128)(2,1)}, u32[]{:S(2)}, u32[]{:S(2)}) collective-permute-start(bf16[256,1536]{1,0:T(8,128)(2,1)} %get-tuple-element.227.refs_2_), channel_id=1, source_target_pairs={{0,8},{4,12},{8,0},{12,4},{16,24},{20,28},{24,16},{28,20},{1,9},{5... | collective-permute-start | bytes 2359304 | tf_op jit(solution)/shard_map/ppermute | solution.py:81
  624.9 50.6 %collective-permute-start.38 = (bf16[256,3072]{1,0:T(8,128)(2,1)}, bf16[256,3072]{1,0:T(8,128)(2,1)}, u32[]{:S(2)}, u32[]{:S(2)}) collective-permute-start(bf16[256,3072]{1,0:T(8,128)(2,1)} %get-tuple-element.200.refs_5_), channel_id=1, source_target_pairs={{0,16},{4,20},{8,24},{12,28},{16,0},{20,4},{24,8},{28,12},{1,17},{... | collective-permute-start | bytes 4718600 | tf_op jit(solution)/shard_map/ppermute | solution.py:81
  625.5 51.1 %collective-permute-start.37 = (bf16[256,3072]{1,0:T(8,128)(2,1)}, bf16[256,3072]{1,0:T(8,128)(2,1)}, u32[]{:S(2)}, u32[]{:S(2)}) collective-permute-start(bf16[256,3072]{1,0:T(8,128)(2,1)} %get-tuple-element.201.refs_4_), channel_id=1, source_target_pairs={{0,8},{4,12},{8,0},{12,4},{16,24},{20,28},{24,16},{28,20},{1,9},{5... | collective-permute-start | bytes 4718600 | tf_op jit(solution)/shard_map/ppermute | solution.py:81
  627.5 323.3 %all-gather.16.cloned.1.call-start = ((), (), s32[]{:S(2)}) async-start(), calls=%async_computation.12 | async-start | bytes 10485760 | tf_op jit(solution)/shard_map/all_gather | solution.py:701
  660.1 16.6 %collective-permute-start.41 = (f32[2,2560]{1,0:T(2,128)S(1)}, f32[2,2560]{1,0:T(2,128)S(1)}, u32[]{:S(2)}, u32[]{:S(2)}) collective-permute-start(f32[2,2560]{1,0:T(2,128)S(1)} %pad_maximum_fusion.16), channel_id=1, source_target_pairs={{3,0},{7,4},{11,8},{15,12},{19,16},{23,20},{27,24},{31,28}} | collective-permute-start | bytes 61448 | tf_op jit(solution)/shard_map/ppermute | solution.py:164
  704.7 16.7 %collective-permute-start.42 = (f32[16,2560]{1,0:T(8,128)S(1)}, f32[16,2560]{1,0:T(8,128)S(1)}, u32[]{:S(2)}, u32[]{:S(2)}) collective-permute-start(f32[16,2560]{1,0:T(8,128)S(1)} %slice.587), channel_id=1, source_target_pairs={{1,0},{2,1},{3,2},{5,4},{6,5},{7,6},{9,8},{10,9},{11,10},{13,12},{... | collective-permute-start | bytes 491528 | tf_op jit(solution)/shard_map/ppermute | solution.py:164
  748.3 395.3 %all-gather.14.cloned.1.call-start = ((), (), s32[]{:S(2)}) async-start(), calls=%async_computation.11 | async-start | bytes 10485760 | tf_op jit(solution)/shard_map/all_gather | solution.py:709
  773.1 49.5 %collective-permute-start.46 = (bf16[1024,2560]{1,0:T(8,128)(2,1)}, bf16[1024,2560]{1,0:T(8,128)(2,1)}, u32[]{:S(2)}, u32[]{:S(2)}) collective-permute-start(bf16[1024,2560]{1,0:T(8,128)(2,1)} %convolution_convert_fusion.2), channel_id=1, source_target_pairs={{0,4},{4,0},{8,12},{12,8},{16,20},{20,16},{24,28},{28,24},{1,5},{5... | collective-permute-start | bytes 15728648 | tf_op jit(solution)/shard_map/ppermute | solution.py:81
  782.2 63.4 %collective-permute-start.53 = (bf16[1024,2560]{1,0:T(8,128)(2,1)}, bf16[1024,2560]{1,0:T(8,128)(2,1)}, u32[]{:S(2)}, u32[]{:S(2)}) collective-permute-start(bf16[1024,2560]{1,0:T(8,128)(2,1)} %convolution_convert_fusion), channel_id=1, source_target_pairs={{0,4},{4,0},{8,12},{12,8},{16,20},{20,16},{24,28},{28,24},{1,5},{5... | collective-permute-start | bytes 15728648 | tf_op jit(solution)/shard_map/ppermute | solution.py:81
  808.0 31.1 %collective-permute-start.44 = (bf16[256,2560]{1,0:T(8,128)(2,1)}, bf16[256,2560]{1,0:T(8,128)(2,1)}, u32[]{:S(2)}, u32[]{:S(2)}) collective-permute-start(bf16[256,2560]{1,0:T(8,128)(2,1)} %get-tuple-element.91), channel_id=1, source_target_pairs={{0,16},{4,20},{8,24},{12,28},{16,0},{20,4},{24,8},{28,12},{1,17},{... | collective-permute-start | bytes 3932168 | tf_op jit(solution)/shard_map/ppermute | solution.py:81
  809.1 30.8 %collective-permute-start.45 = (bf16[256,2560]{1,0:T(8,128)(2,1)}, bf16[256,2560]{1,0:T(8,128)(2,1)}, u32[]{:S(2)}, u32[]{:S(2)}) collective-permute-start(bf16[256,2560]{1,0:T(8,128)(2,1)} %get-tuple-element.92), channel_id=1, source_target_pairs={{0,8},{4,12},{8,0},{12,4},{16,24},{20,28},{24,16},{28,20},{1,9},{5... | collective-permute-start | bytes 3932168 | tf_op jit(solution)/shard_map/ppermute | solution.py:81
  839.9 30.0 %collective-permute-start.47 = (bf16[256,2560]{1,0:T(8,128)(2,1)}, bf16[256,2560]{1,0:T(8,128)(2,1)}, u32[]{:S(2)}, u32[]{:S(2)}) collective-permute-start(bf16[256,2560]{1,0:T(8,128)(2,1)} %get-tuple-element.94), channel_id=1, source_target_pairs={{0,8},{4,12},{8,0},{12,4},{16,24},{20,28},{24,16},{28,20},{1,9},{5... | collective-permute-start | bytes 3932168 | tf_op jit(solution)/shard_map/ppermute | solution.py:81
  841.4 29.6 %collective-permute-start.48 = (bf16[256,2560]{1,0:T(8,128)(2,1)}, bf16[256,2560]{1,0:T(8,128)(2,1)}, u32[]{:S(2)}, u32[]{:S(2)}) collective-permute-start(bf16[256,2560]{1,0:T(8,128)(2,1)} %get-tuple-element.95), channel_id=1, source_target_pairs={{0,16},{4,20},{8,24},{12,28},{16,0},{20,4},{24,8},{28,12},{1,17},{... | collective-permute-start | bytes 3932168 | tf_op jit(solution)/shard_map/ppermute | solution.py:81
  871.0 17.9 %collective-permute-start.49 = (bf16[128,2560]{1,0:T(8,128)(2,1)}, bf16[128,2560]{1,0:T(8,128)(2,1)S(1)}, u32[]{:S(2)}, u32[]{:S(2)}) collective-permute-start(bf16[128,2560]{1,0:T(8,128)(2,1)} %get-tuple-element.96), channel_id=1, source_target_pairs={{0,8},{4,12},{8,0},{12,4},{16,24},{20,28},{24,16},{28,20},{1,9},{5... | collective-permute-start | bytes 1966088 | tf_op jit(solution)/shard_map/ppermute | solution.py:81
  871.6 18.1 %collective-permute-start.50 = (bf16[128,2560]{1,0:T(8,128)(2,1)}, bf16[128,2560]{1,0:T(8,128)(2,1)}, u32[]{:S(2)}, u32[]{:S(2)}) collective-permute-start(bf16[128,2560]{1,0:T(8,128)(2,1)} %get-tuple-element.97), channel_id=1, source_target_pairs={{0,16},{4,20},{8,24},{12,28},{16,0},{20,4},{24,8},{28,12},{1,17},{... | collective-permute-start | bytes 1966088 | tf_op jit(solution)/shard_map/ppermute | solution.py:81
  876.1 26.9 %collective-permute-start.51 = (bf16[128,2560]{1,0:T(8,128)(2,1)}, bf16[128,2560]{1,0:T(8,128)(2,1)}, u32[]{:S(2)}, u32[]{:S(2)}) collective-permute-start(bf16[128,2560]{1,0:T(8,128)(2,1)} %get-tuple-element.98), channel_id=1, source_target_pairs={{0,8},{4,12},{8,0},{12,4},{16,24},{20,28},{24,16},{28,20},{1,9},{5... | collective-permute-start | bytes 1966088 | tf_op jit(solution)/shard_map/ppermute | solution.py:81
  877.7 26.0 %collective-permute-start.52 = (bf16[128,2560]{1,0:T(8,128)(2,1)}, bf16[128,2560]{1,0:T(8,128)(2,1)}, u32[]{:S(2)}, u32[]{:S(2)}) collective-permute-start(bf16[128,2560]{1,0:T(8,128)(2,1)} %get-tuple-element.99), channel_id=1, source_target_pairs={{0,16},{4,20},{8,24},{12,28},{16,0},{20,4},{24,8},{28,12},{1,17},{... | collective-permute-start | bytes 1966088 | tf_op jit(solution)/shard_map/ppermute | solution.py:81
  878.7 49.4 %collective-permute-start.54 = (bf16[256,2560]{1,0:T(8,128)(2,1)}, bf16[256,2560]{1,0:T(8,128)(2,1)S(1)}, u32[]{:S(2)}, u32[]{:S(2)}) collective-permute-start(bf16[256,2560]{1,0:T(8,128)(2,1)} %get-tuple-element.101), channel_id=1, source_target_pairs={{0,16},{4,20},{8,24},{12,28},{16,0},{20,4},{24,8},{28,12},{1,17},{... | collective-permute-start | bytes 3932168 | tf_op jit(solution)/shard_map/ppermute | solution.py:81
  888.9 39.2 %collective-permute-start.55 = (bf16[256,2560]{1,0:T(8,128)(2,1)}, bf16[256,2560]{1,0:T(8,128)(2,1)S(1)}, u32[]{:S(2)}, u32[]{:S(2)}) collective-permute-start(bf16[256,2560]{1,0:T(8,128)(2,1)} %get-tuple-element.102), channel_id=1, source_target_pairs={{0,8},{4,12},{8,0},{12,4},{16,24},{20,28},{24,16},{28,20},{1,9},{5... | collective-permute-start | bytes 3932168 | tf_op jit(solution)/shard_map/ppermute | solution.py:81
  970.2 24.9 %collective-permute-start.64 = (bf16[128,3072]{1,0:T(8,128)(2,1)}, bf16[128,3072]{1,0:T(8,128)(2,1)}, u32[]{:S(2)}, u32[]{:S(2)}) collective-permute-start(bf16[128,3072]{1,0:T(8,128)(2,1)} %get-tuple-element.109), channel_id=1, source_target_pairs={{0,8},{4,12},{8,0},{12,4},{16,24},{20,28},{24,16},{28,20},{1,9},{5... | collective-permute-start | bytes 2359304 | tf_op jit(solution)/shard_map/ppermute | solution.py:81
  971.6 26.7 %collective-permute-start.65 = (bf16[128,3072]{1,0:T(8,128)(2,1)}, bf16[128,3072]{1,0:T(8,128)(2,1)}, u32[]{:S(2)}, u32[]{:S(2)}) collective-permute-start(bf16[128,3072]{1,0:T(8,128)(2,1)} %get-tuple-element.110), channel_id=1, source_target_pairs={{0,16},{4,20},{8,24},{12,28},{16,0},{20,4},{24,8},{28,12},{1,17},{... | collective-permute-start | bytes 2359304 | tf_op jit(solution)/shard_map/ppermute | solution.py:81
  976.8 34.4 %collective-permute-start.68 = (bf16[4,4,26752]{2,1,0:T(4,128)(2,1)}, bf16[4,4,26752]{2,1,0:T(4,128)(2,1)}, u32[]{:S(2)}, u32[]{:S(2)}) collective-permute-start(bf16[4,4,26752]{2,1,0:T(4,128)(2,1)} %slice.825), channel_id=1, source_target_pairs={{0,16},{4,20},{8,24},{12,28},{16,0},{20,4},{24,8},{28,12},{1,17},{... | collective-permute-start | bytes 2568200 | tf_op jit(solution)/shard_map/ppermute | solution.py:81
  983.4 33.2 %collective-permute-start.59 = (bf16[3,256,640]{2,1,0:T(8,128)(2,1)}, bf16[3,256,640]{2,1,0:T(8,128)(2,1)}, u32[]{:S(2)}, u32[]{:S(2)}) collective-permute-start(bf16[3,256,640]{2,1,0:T(8,128)(2,1)} %get-tuple-element.232), channel_id=1, source_target_pairs={{3,2},{7,6},{11,10},{15,14},{19,18},{23,22},{27,26},{31,30}} | collective-permute-start | bytes 2949128 | tf_op jit(solution)/shard_map/ppermute | solution.py:192
  985.0 44.7 %collective-permute-start.58 = (bf16[3,256,640]{2,1,0:T(8,128)(2,1)}, bf16[3,256,640]{2,1,0:T(8,128)(2,1)}, u32[]{:S(2)}, u32[]{:S(2)}) collective-permute-start(bf16[3,256,640]{2,1,0:T(8,128)(2,1)} %get-tuple-element.233), channel_id=1, source_target_pairs={{0,1},{4,5},{8,9},{12,13},{16,17},{20,21},{24,25},{28,29}} | collective-permute-start | bytes 2949128 | tf_op jit(solution)/shard_map/ppermute | solution.py:191
  1013.0 16.7 %collective-permute-start.69 = (bf16[2,4,26752]{2,1,0:T(4,128)(2,1)S(1)}, bf16[2,4,26752]{2,1,0:T(4,128)(2,1)S(1)}, u32[]{:S(2)}, u32[]{:S(2)}) collective-permute-start(bf16[2,4,26752]{2,1,0:T(4,128)(2,1)S(1)} %slice.827), channel_id=1, source_target_pairs={{0,8},{4,12},{8,0},{12,4},{16,24},{20,28},{24,16},{28,20},{1,9},{5... | collective-permute-start | bytes 1284104 | tf_op jit(solution)/shard_map/ppermute | solution.py:81
  1033.0 48.1 %collective-permute-start.60 = (bf16[3,256,640]{2,1,0:T(8,128)(2,1)S(1)}, bf16[3,256,640]{2,1,0:T(8,128)(2,1)S(1)}, u32[]{:S(2)}, u32[]{:S(2)}) collective-permute-start(bf16[3,256,640]{2,1,0:T(8,128)(2,1)S(1)} %get-tuple-element.229), channel_id=1, source_target_pairs={{0,1},{1,2},{4,5},{5,6},{8,9},{9,10},{12,13},{13,14},{16,17},{17,1... | collective-permute-start | bytes 2949128 | tf_op jit(solution)/shard_map/ppermute | solution.py:191
  1039.1 58.6 %collective-permute-start.71 = (bf16[26752]{0:T(1024)(128)(2,1)S(1)}, bf16[26752]{0:T(1024)(128)(2,1)S(1)}, u32[]{:S(2)}, u32[]{:S(2)}) collective-permute-start(bf16[26752]{0:T(1024)(128)(2,1)S(1)} %get-tuple-element.187), channel_id=1, source_target_pairs={{0,1},{1,2},{2,3},{3,0},{4,5},{5,6},{6,7},{7,4},{8,9},{9,10},{10,1... | collective-permute-start | bytes 160520 | tf_op jit(solution)/shard_map/ppermute | solution.py:164
  1041.8 56.0 %collective-permute-start.73 = (bf16[26752]{0:T(1024)(128)(2,1)S(1)}, bf16[26752]{0:T(1024)(128)(2,1)S(1)}, u32[]{:S(2)}, u32[]{:S(2)}) collective-permute-start(bf16[26752]{0:T(1024)(128)(2,1)S(1)} %get-tuple-element.188), channel_id=1, source_target_pairs={{0,3},{1,0},{2,1},{3,2},{4,7},{5,4},{6,5},{7,6},{8,11},{9,8},{10,9... | collective-permute-start | bytes 160520 | tf_op jit(solution)/shard_map/ppermute | solution.py:164
  1043.0 54.7 %collective-permute-start.72 = (bf16[26752]{0:T(1024)(128)(2,1)S(1)}, bf16[26752]{0:T(1024)(128)(2,1)S(1)}, u32[]{:S(2)}, u32[]{:S(2)}) collective-permute-start(bf16[26752]{0:T(1024)(128)(2,1)S(1)} %get-tuple-element.189), channel_id=1, source_target_pairs={{0,2},{1,3},{2,0},{3,1},{4,6},{5,7},{6,4},{7,5},{8,10},{9,11},{10,... | collective-permute-start | bytes 160520 | tf_op jit(solution)/shard_map/ppermute | solution.py:164
  1087.3 30.7 %collective-permute-start.63 = (bf16[3,256,640]{2,1,0:T(8,128)(2,1)}, bf16[3,256,640]{2,1,0:T(8,128)(2,1)S(1)}, u32[]{:S(2)}, u32[]{:S(2)}) collective-permute-start(bf16[3,256,640]{2,1,0:T(8,128)(2,1)} %add_convert_fusion.14), channel_id=1, source_target_pairs={{1,0},{2,1},{3,2},{5,4},{6,5},{7,6},{9,8},{10,9},{11,10},{13,12},{... | collective-permute-start | bytes 2949128 | tf_op jit(solution)/shard_map/ppermute | solution.py:192
  1088.6 52.0 %collective-permute-start.62 = (bf16[3,256,640]{2,1,0:T(8,128)(2,1)}, bf16[3,256,640]{2,1,0:T(8,128)(2,1)S(1)}, u32[]{:S(2)}, u32[]{:S(2)}) collective-permute-start(bf16[3,256,640]{2,1,0:T(8,128)(2,1)} %add_convert_fusion.15), channel_id=1, source_target_pairs={{0,1},{1,2},{2,3},{4,5},{5,6},{6,7},{8,9},{9,10},{10,11},{12,13},{... | collective-permute-start | bytes 2949128 | tf_op jit(solution)/shard_map/ppermute | solution.py:191
  (149 other events, 1228.5 us)
Sparse Core Ops, SparseCore 0:
  12.1 43.3 all-gather.7
  57.6 54.7 all-gather.17
  288.0 80.7 all-gather.9
  370.3 79.2 all-gather.11
  451.7 75.2 reduce-scatter.4
  531.9 75.2 reduce-scatter.6
  619.3 76.5 reduce-scatter.8
  698.3 80.7 reduce-scatter.10
  780.6 149.1 all-gather.15
  931.2 210.0 all-gather.13

commit v14 on v13

--- a/solution.py
+++ b/solution.py
@@ -716,13 +716,14 @@
     owned = jnp.stack([total.finish().reshape(d_own, n, width // n) for total in (sum_o, sum_g, sum_r)])
     owned = LineSum(owned.transpose(2, 0, 1, 3), n)
     owned.go()
+    pause = (owned.right, owned.left)
     tokens_out = move(tokens_out)
     if n > 2:
         owned.go(tokens_out)
-    d_lru, dpar = fence([d_lru, dpar], *got_r)
+    d_lru, dpar = fence([d_lru, dpar], *pause)
     if sum_dn.square:
-        sum_dn.hop(fence(sum_dn.sources(), *got_r))
-        sum_gu.hop(fence(sum_gu.sources(), *got_r))
+        sum_dn.hop(fence(sum_dn.sources(), *pause))
+        sum_gu.hop(fence(sum_gu.sources(), *pause))
     g_gu, g_dn = sum_gu.finish().astype(F32), sum_dn.finish().astype(F32)
     g_all = owned.finish()
     (output,) = fence([result], owned.right, owned.left, g_gu, g_dn, cost=MUCH)

time: 1170 us -> 1190 us (1.017)
  starting transfers between devices: 97.3 us -> 118 us
    ppermute x10, starting transfers between devices: 19.2 us -> 48.4 us  [z_shift(): return lax.ppermute(values, 'tensor', pairs)]
    ppermute x3, waiting for transfers between devices: 73.2 us -> 51.1 us  [go(): lax.ppermute(right, 'tensor', [(k, k + 1) for k in range(min(t, n - 1))])]
    ppermute x3, waiting for transfers between devices: 18 us -> 30.6 us  [go(): lax.ppermute(left, 'tensor', [(k, k - 1) for k in range(max(n - t, 1), n)])]
    unnamed x271 -> x275, local copies, waits for them, and re-layouts: 41 us -> 43.2 us
  transfers between devices with their start and end apart: 84 -> 84, of which waited for: 39 -> 39; matrix products, arithmetic and copies ran while one was open for 43% -> 43% of each run, Pallas kernels for 11% -> 10%
where the time goes in v14:
time: 1190 us; the launch traced here: 1180 us
  waiting for transfers between devices  356 us (30%)
  matrix products  308 us (26%)
  other arithmetic  141 us (12%)
  Pallas kernels  140 us (12%)
  starting transfers between devices  118 us (10%)
  local copies, waits for them, and re-layouts  100 us (8%)
  between operations  17.4 us (1%)
    dot_general x34, matrix products, dot(): lax.dot_general(left, right, (dims, ((), ())), preferred_element_type=F32)  308 us
    ppermute x58, waiting for transfers between devices, exchange(): return lax.ppermute(values, 'dp', [(k, k ^ 1 << bit) for k in range(size)])  233 us
    convert_element_type x21, other arithmetic, add_all(): return total.astype(BF)  67.1 us
    pallas_call x3, Pallas kernels, kernel_call(): pl.pallas_call(body, grid_spec=pltpu.PrefetchScalarGridSpec(num_scalar_pr...  62.3 us
    ppermute x58, starting transfers between devices, exchange(): return lax.ppermute(values, 'dp', [(k, k ^ 1 << bit) for k in range(size)])  52.6 us
    ppermute x3, waiting for transfers between devices, go(): lax.ppermute(right, 'tensor', [(k, k + 1) for k in range(min(t, n - 1))])  51.1 us
    ppermute x10, starting transfers between devices, z_shift(): return lax.ppermute(values, 'tensor', pairs)  48.4 us
    unnamed x275, local copies, waits for them, and re-layouts  43.2 us
  transfers between devices with their start and end apart: 84, of which 39 were waited for; matrix products, arithmetic and copies ran while one was open for 43% of the time, Pallas kernels for 10%

profile of v14, /device:TPU:0, one launch (start us, length us, event | category | flops | bytes accessed | tf_op | source)
XLA Modules:
  0.0 1180.4 jit_solution(2540493755719847289)
XLA Ops:
  38.1 16.2 %collective-permute-done.1.refs_2_.refs_1_ = bf16[256,3072]{1,0:T(8,128)(2,1)S(1)} collective-permute-done((bf16[256,3072]{1,0:T(8,128)(2,1)}, bf16[256,3072]{1,0:T(8,128)(2,1)S(1)}, u32[]{:S(2)}, u32[]{:S(2)}) %collective-permute-start.1) | collective-permute-done | bytes 1572896 | tf_op jit(solution)/shard_map/ppermute | solution.py:81
  62.8 27.5 %collective-permute-done.9.refs_4_ = bf16[256,2560]{1,0:T(8,128)(2,1)S(1)} collective-permute-done((bf16[256,2560]{1,0:T(8,128)(2,1)S(1)}, bf16[256,2560]{1,0:T(8,128)(2,1)S(1)}, u32[]{:S(2)}, u32[]{:S(2)}) %collective-permute-start.9) | collective-permute-done | bytes 1310752 | tf_op jit(solution)/shard_map/ppermute | solution.py:81
  104.5 9.5 collective-permute-done.10.refs_2_
  122.2 7.3 collective-permute-done.6
  149.7 7.3 convolution_add_fusion.pre_ref
  157.0 18.7 %recurrence.1 = (f32[512,2560]{1,0:T(8,128)}, f32[512,2560]{1,0:T(8,128)}, f32[512,2560]{1,0:T(8,128)}, f32[512,2560]{1,0:T(8,128)}, f32[512,2560]{1,0:T(8,128)}, /*index=5*/f32[512,2560]{1,0:T(8,128)}) custom-call(s32[1]{0:T(128)} %sub.38.live_ref, f32[528,2560]{1,0:T(8,128)} %convolution_add_fusion.pre_ref, f32[8,2560]{1,0:T(8,128)} %pad_maximum_fusion.14.par_ref, ...), custom_call_target="tpu_custom_call" | custom-call | flops 1024 | bytes 1024 | tf_op jit(solution)/shard_map/recurrence/pallas_call | solution.py:494
  184.4 5.3 collective-permute-start.18
  218.8 9.8 fusion.22
  228.6 9.9 collective-permute-done.21.refs_1_
  244.6 14.2 %collective-permute-done.22.refs_2_.refs_3_ = bf16[128,2560]{1,0:T(8,128)(2,1)S(1)} collective-permute-done((bf16[128,2560]{1,0:T(8,128)(2,1)S(1)}, bf16[128,2560]{1,0:T(8,128)(2,1)S(1)}, u32[]{:S(2)}, u32[]{:S(2)}) %collective-permute-start.22) | collective-permute-done | bytes 655392 | tf_op jit(solution)/shard_map/ppermute | solution.py:81
  292.8 6.1 assemble.10.refs_0_
  302.9 18.7 %collective-permute-done.29.refs_4_ = bf16[256,1536]{1,0:T(8,128)(2,1)S(1)} collective-permute-done((bf16[256,1536]{1,0:T(8,128)(2,1)}, bf16[256,1536]{1,0:T(8,128)(2,1)S(1)}, u32[]{:S(2)}, u32[]{:S(2)}) %collective-permute-start.29) | collective-permute-done | bytes 786464 | tf_op jit(solution)/shard_map/ppermute | solution.py:81
  323.5 9.1 collective-permute-done.30.refs_2_
  349.2 5.9 permute.7
  355.0 5.8 permute.6
  361.4 9.2 assemble.11
  370.7 19.2 %fusion.83 = f32[1024,3072]{1,0:T(8,128)} fusion(bf16[1024,2048]{1,0:T(8,128)(2,1)} %all-gather.10.cloned.1.call-done, bf16[2048,3072]{1,0:T(8,128)(2,1)} %assemble.11), kind=kOutput, calls=%fused_computation.263 | convolution fusion | flops 12884901888 | bytes 29360128 | tf_op jit(solution)/shard_map/dot_general | solution.py:25
  389.8 16.0 %fusion.6 = (bf16[1024,1536]{1,0:T(8,128)(2,1)S(1)}, bf16[1024,1536]{1,0:T(8,128)(2,1)S(1)}, bf16[1024,1536]{1,0:T(8,128)(2,1)}) fusion(f32[1024,3072]{1,0:T(8,128)} %fusion.83, bf16[1024,2048]{1,0:T(8,128)(2,1)S(1)} %copy-done.37, bf16[2048,1536]{1,0:T(8,128)(2,1)} %assemble.13), kind=kOutput, calls=%fused_computation.15 | convolution fusion | flops 6483345408 | bytes 32505856 | tf_op jit(solution)/shard_map/dot_general | solution.py:25
  407.5 17.6 %convolution_convert_fusion.7.refs_1_ = bf16[1024,2048]{1,0:T(8,128)(2,1)} fusion(bf16[2048,3072]{1,0:T(8,128)(2,1)} %assemble.11, bf16[1024,1536]{1,0:T(8,128)(2,1)S(1)} %get-tuple-element.195, bf16[1024,1536]{1,0:T(8,128)(2,1)S(1)} %get-tuple-element.194), kind=kOutput, calls=%fused_computation.73 | convolution fusion | flops 12899581952 | bytes 23068672 | tf_op jit(solution)/shard_map/dot_general | solution.py:25
  425.4 24.1 %all-gather.12.cloned.1.call-done.refs_0_ = bf16[1024,2048]{1,0:T(8,128)(2,1)} async-done(((bf16[256,2048]{1,0:T(8,128)(2,1)}), bf16[1024,2048]{1,0:T(8,128)(2,1)}) %all-gather.12.cloned.1.call-update) | async-done | bytes 4194320 | tf_op jit(solution)/shard_map/all_gather | solution.py:630
  449.4 19.2 %fusion.84 = f32[1024,3072]{1,0:T(8,128)} fusion(bf16[1024,2048]{1,0:T(8,128)(2,1)} %fence.42, bf16[2048,3072]{1,0:T(8,128)(2,1)} %assemble.11), kind=kOutput, calls=%fused_computation.264 | convolution fusion | flops 12884901888 | bytes 29360128 | tf_op jit(solution)/shard_map/dot_general | solution.py:25
  468.6 15.3 %fusion.13 = (bf16[1024,1536]{1,0:T(8,128)(2,1)}, bf16[1024,1536]{1,0:T(8,128)(2,1)}, bf16[1024,1536]{1,0:T(8,128)(2,1)}) fusion(f32[1024,3072]{1,0:T(8,128)} %fusion.84, bf16[1024,2048]{1,0:T(8,128)(2,1)S(1)} %copy-done.35, bf16[2048,1536]{1,0:T(8,128)(2,1)S(1)} %bitcast.175), kind=kOutput, calls=%fused_computation.22 | convolution fusion | flops 6483345408 | bytes 32505856 | tf_op jit(solution)/shard_map/dot_general | solution.py:25
  484.0 5.5 pad_maximum_fusion.refs_1_
  489.5 18.8 %convolution_convert_fusion.6.refs_2_ = bf16[1024,2048]{1,0:T(8,128)(2,1)} fusion(bf16[2048,3072]{1,0:T(8,128)(2,1)} %assemble.11, bf16[1024,1536]{1,0:T(8,128)(2,1)} %get-tuple-element.193, bf16[1024,1536]{1,0:T(8,128)(2,1)S(1)} %copy-done.55), kind=kOutput, calls=%fused_computation.72 | convolution fusion | flops 12899581952 | bytes 23068672 | tf_op jit(solution)/shard_map/dot_general | solution.py:25
  510.2 5.7 pad_maximum_fusion.1.refs_1_
  515.9 7.4 fusion.36
  523.3 8.3 convolution_convert_fusion.9.refs_6_.refs_0_
  531.7 9.7 add_convert_fusion.2
  541.5 9.7 fusion.30
  551.2 11.8 add_convert_fusion
  563.4 11.0 fusion.33
  574.4 11.3 convolution_convert_fusion.8.refs_7_.refs_1_
  585.7 5.4 fusion.39
  591.1 7.0 add_convert_fusion.3
  598.2 10.2 add_convert_fusion.1
  630.0 5.6 fusion.50
  641.0 17.0 %back_scan.1 = (f32[512,2560]{1,0:T(8,128)}, f32[512,2560]{1,0:T(8,128)}, f32[8,2560]{1,0:T(8,128)}, bf16[512,2560]{1,0:T(8,128)(2,1)}) custom-call(s32[1]{0:T(128)} %sub.38.live_ref, f32[512,2560]{1,0:T(8,128)} %get-tuple-element.264.refs_2_.pre_ref, f32[512,2560]{1,0:T(8,128)} %convolution_add_fusion.1.grad_ref, f32[512,2560]{1,0:T(8,128)} %get-tuple-element.80.decay_ref, ...), custom_call_target="tpu_custom_call" | custom-call | flops 1024 | bytes 1024 | tf_op jit(solution)/shard_map/back_scan/pallas_call | solution.py:494
  663.0 11.3 collective-permute-done.38.refs_4_
  676.2 26.5 %recurrence_back.1 = (f32[528,2560]{1,0:T(8,128)}, f32[8,2560]{1,0:T(8,128)}, bf16[4,160,1280]{2,1,0:T(8,128)(2,1)}) custom-call(s32[1]{0:T(128)} %sub.38.live_ref, f32[528,2560]{1,0:T(8,128)} %convolution_add_fusion.pre_ref, f32[8,2560]{1,0:T(8,128)} %pad_maximum_fusion.14.par_ref, bf16[8,4,80,640]{3,2,1,0:T(8,128)(2,1)} %copy-done.15, ...), custom_call_target="tpu_custom_call" | custom-call | flops 1024 | bytes 1024 | tf_op jit(solution)/shard_map/recurrence_back/pallas_call | solution.py:494
  703.6 8.4 fusion.85
  713.4 6.7 fusion.86
  720.2 7.1 collective-permute-done.42.refs_0_
  731.0 6.4 fusion.87
  745.1 6.1 add_convert_fusion.5.in_ref
  761.2 8.6 collective-permute-done.43.refs_2_
  772.2 7.3 convolution_convert_fusion.2
  782.7 6.2 convolution_convert_fusion
  789.4 5.3 add_convert_fusion.19
  795.3 6.0 convolution_convert_fusion.4
  823.4 7.3 convolution_convert_fusion.1
  834.6 11.4 collective-permute-done.44.refs_3_
  856.5 20.4 %collective-permute-done.47.refs_2_ = bf16[256,2560]{1,0:T(8,128)(2,1)} collective-permute-done((bf16[256,2560]{1,0:T(8,128)(2,1)}, bf16[256,2560]{1,0:T(8,128)(2,1)}, u32[]{:S(2)}, u32[]{:S(2)}) %collective-permute-start.47) | collective-permute-done | bytes 1310752 | tf_op jit(solution)/shard_map/ppermute | solution.py:81
  886.3 9.6 collective-permute-done.49
  900.3 9.7 collective-permute-done.51
  914.8 19.9 %collective-permute-done.54.refs_3_ = bf16[256,2560]{1,0:T(8,128)(2,1)S(1)} collective-permute-done((bf16[256,2560]{1,0:T(8,128)(2,1)}, bf16[256,2560]{1,0:T(8,128)(2,1)S(1)}, u32[]{:S(2)}, u32[]{:S(2)}) %collective-permute-start.54) | collective-permute-done | bytes 1310752 | tf_op jit(solution)/shard_map/ppermute | solution.py:81
  966.3 9.4 move.2.refs_3_
  975.7 20.8 %collective-permute-done.58.refs_0_.refs_2_ = bf16[3,256,640]{2,1,0:T(8,128)(2,1)S(1)} collective-permute-done((bf16[3,256,640]{2,1,0:T(8,128)(2,1)S(1)}, bf16[3,256,640]{2,1,0:T(8,128)(2,1)S(1)}, u32[]{:S(2)}, u32[]{:S(2)}) %collective-permute-start.58) | collective-permute-done | bytes 983072 | tf_op jit(solution)/shard_map/ppermute | solution.py:191
  1020.4 5.4 collective-permute-start.60
  1040.9 20.4 %collective-permute-done.60.refs_0_ = bf16[3,256,640]{2,1,0:T(8,128)(2,1)} collective-permute-done((bf16[3,256,640]{2,1,0:T(8,128)(2,1)}, bf16[3,256,640]{2,1,0:T(8,128)(2,1)}, u32[]{:S(2)}, u32[]{:S(2)}) %collective-permute-start.60) | collective-permute-done | bytes 983072 | tf_op jit(solution)/shard_map/ppermute | solution.py:191
  1065.4 32.2 %collective-permute-start.71 = (bf16[26752]{0:T(1024)(128)(2,1)S(1)}, bf16[26752]{0:T(1024)(128)(2,1)S(1)}, u32[]{:S(2)}, u32[]{:S(2)}) collective-permute-start(bf16[26752]{0:T(1024)(128)(2,1)S(1)} %get-tuple-element.187), channel_id=1, source_target_pairs={{0,1},{1,2},{2,3},{3,0},{4,5},{5,6},{6,7},{7,4},{8,9},{9,10},{10,1... | collective-permute-start | bytes 160520 | tf_op jit(solution)/shard_map/ppermute | solution.py:164
  1110.0 30.6 %collective-permute-done.63.refs_2_ = bf16[3,256,640]{2,1,0:T(8,128)(2,1)S(1)} collective-permute-done((bf16[3,256,640]{2,1,0:T(8,128)(2,1)}, bf16[3,256,640]{2,1,0:T(8,128)(2,1)S(1)}, u32[]{:S(2)}, u32[]{:S(2)}) %collective-permute-start.63) | collective-permute-done | bytes 983072 | tf_op jit(solution)/shard_map/ppermute | solution.py:192
  1140.6 9.8 collective-permute-done.62.refs_1_
  1153.5 9.5 all-gather.14.cloned.1.call-done.refs_0_
  1164.1 8.9 move.3
  (637 shorter events, 395.3 us)
Async XLA Ops:
  7.2 48.5 %all-gather.8.cloned.1.call-start = ((), (), s32[]{:S(2)}) async-start(), calls=%async_computation.4 | async-start | bytes 2150400 | tf_op jit(solution)/shard_map/all_gather | solution.py:567
  12.0 102.1 %all-gather.18.cloned.1.call-start = ((), (), s32[]{:S(2)}) async-start(), calls=%async_computation.13 | async-start | bytes 3276800 | tf_op jit(solution)/shard_map/all_gather | solution.py:568
  15.5 38.7 %collective-permute-start.1 = (bf16[256,3072]{1,0:T(8,128)(2,1)}, bf16[256,3072]{1,0:T(8,128)(2,1)S(1)}, u32[]{:S(2)}, u32[]{:S(2)}) collective-permute-start(bf16[256,3072]{1,0:T(8,128)(2,1)} %pad_maximum_fusion.8.refs_0_), channel_id=1, source_target_pairs={{0,16},{4,20},{8,24},{12,28},{16,0},{20,4},{24,8},{28,12},{1,17},{... | collective-permute-start | bytes 4718600 | tf_op jit(solution)/shard_map/ppermute | solution.py:81
  19.6 36.1 %collective-permute-start = (bf16[256,3072]{1,0:T(8,128)(2,1)}, bf16[256,3072]{1,0:T(8,128)(2,1)S(1)}, u32[]{:S(2)}, u32[]{:S(2)}) collective-permute-start(bf16[256,3072]{1,0:T(8,128)(2,1)} %pad_maximum_fusion.8.refs_0_), channel_id=1, source_target_pairs={{0,8},{4,12},{8,0},{12,4},{16,24},{20,28},{24,16},{28,20},{1,9},{5... | collective-permute-start | bytes 4718600 | tf_op jit(solution)/shard_map/ppermute | solution.py:81
  56.9 313.8 %all-gather.10.cloned.1.call-start = ((), (), s32[]{:S(2)}) async-start(), calls=%async_computation.5 | async-start | bytes 5242880 | tf_op jit(solution)/shard_map/all_gather | solution.py:630
  58.5 31.8 %collective-permute-start.9 = (bf16[256,2560]{1,0:T(8,128)(2,1)S(1)}, bf16[256,2560]{1,0:T(8,128)(2,1)S(1)}, u32[]{:S(2)}, u32[]{:S(2)}) collective-permute-start(bf16[256,2560]{1,0:T(8,128)(2,1)S(1)} %bitcast.180), channel_id=1, source_target_pairs={{0,16},{4,20},{8,24},{12,28},{16,0},{20,4},{24,8},{28,12},{1,17},{... | collective-permute-start | bytes 3932168 | tf_op jit(solution)/shard_map/ppermute | solution.py:81
  59.4 32.5 %collective-permute-start.7 = (bf16[256,2560]{1,0:T(8,128)(2,1)S(1)}, bf16[256,2560]{1,0:T(8,128)(2,1)S(1)}, u32[]{:S(2)}, u32[]{:S(2)}) collective-permute-start(bf16[256,2560]{1,0:T(8,128)(2,1)S(1)} %bitcast.181), channel_id=1, source_target_pairs={{0,8},{4,12},{8,0},{12,4},{16,24},{20,28},{24,16},{28,20},{1,9},{5... | collective-permute-start | bytes 3932168 | tf_op jit(solution)/shard_map/ppermute | solution.py:81
  61.0 38.5 %collective-permute-start.4 = (bf16[320,640]{1,0:T(8,128)(2,1)S(1)}, bf16[320,640]{1,0:T(8,128)(2,1)S(1)}, u32[]{:S(2)}, u32[]{:S(2)}) collective-permute-start(bf16[320,640]{1,0:T(8,128)(2,1)S(1)} %bitcast.193), channel_id=1, source_target_pairs={{0,16},{4,20},{8,24},{12,28},{16,0},{20,4},{24,8},{28,12},{1,17},{... | collective-permute-start | bytes 1228808 | tf_op jit(solution)/shard_map/ppermute | solution.py:81
  62.3 39.0 %collective-permute-start.2 = (bf16[320,640]{1,0:T(8,128)(2,1)S(1)}, bf16[320,640]{1,0:T(8,128)(2,1)S(1)}, u32[]{:S(2)}, u32[]{:S(2)}) collective-permute-start(bf16[320,640]{1,0:T(8,128)(2,1)S(1)} %bitcast.194), channel_id=1, source_target_pairs={{0,8},{4,12},{8,0},{12,4},{16,24},{20,28},{24,16},{28,20},{1,9},{5... | collective-permute-start | bytes 1228808 | tf_op jit(solution)/shard_map/ppermute | solution.py:81
  90.4 23.7 %collective-permute-start.10 = (bf16[128,2560]{1,0:T(8,128)(2,1)S(1)}, bf16[128,2560]{1,0:T(8,128)(2,1)}, u32[]{:S(2)}, u32[]{:S(2)}) collective-permute-start(bf16[128,2560]{1,0:T(8,128)(2,1)S(1)} %slice.704), channel_id=1, source_target_pairs={{0,8},{4,12},{8,0},{12,4},{16,24},{20,28},{24,16},{28,20},{1,9},{5... | collective-permute-start | bytes 1966088 | tf_op jit(solution)/shard_map/ppermute | solution.py:81
  93.0 21.1 %collective-permute-start.8 = (bf16[128,2560]{1,0:T(8,128)(2,1)S(1)}, bf16[128,2560]{1,0:T(8,128)(2,1)}, u32[]{:S(2)}, u32[]{:S(2)}) collective-permute-start(bf16[128,2560]{1,0:T(8,128)(2,1)S(1)} %slice.703), channel_id=1, source_target_pairs={{0,16},{4,20},{8,24},{12,28},{16,0},{20,4},{24,8},{28,12},{1,17},{... | collective-permute-start | bytes 1966088 | tf_op jit(solution)/shard_map/ppermute | solution.py:81
  100.2 19.3 %collective-permute-start.5 = (bf16[160,640]{1,0:T(8,128)(2,1)}, bf16[160,640]{1,0:T(8,128)(2,1)}, u32[]{:S(2)}, u32[]{:S(2)}) collective-permute-start(bf16[160,640]{1,0:T(8,128)(2,1)} %slice.695), channel_id=1, source_target_pairs={{0,8},{4,12},{8,0},{12,4},{16,24},{20,28},{24,16},{28,20},{1,9},{5... | collective-permute-start | bytes 614408 | tf_op jit(solution)/shard_map/ppermute | solution.py:81
  102.8 15.8 %collective-permute-start.3 = (bf16[160,640]{1,0:T(8,128)(2,1)}, bf16[160,640]{1,0:T(8,128)(2,1)}, u32[]{:S(2)}, u32[]{:S(2)}) collective-permute-start(bf16[160,640]{1,0:T(8,128)(2,1)} %slice.694), channel_id=1, source_target_pairs={{0,16},{4,20},{8,24},{12,28},{16,0},{20,4},{24,8},{28,12},{1,17},{... | collective-permute-start | bytes 614408 | tf_op jit(solution)/shard_map/ppermute | solution.py:81
  118.4 26.4 %collective-permute-start.13 = (bf16[1024,2560]{1,0:T(8,128)(2,1)}, bf16[1024,2560]{1,0:T(8,128)(2,1)}, u32[]{:S(2)}, u32[]{:S(2)}) collective-permute-start(bf16[1024,2560]{1,0:T(8,128)(2,1)} %assemble.7), channel_id=1, source_target_pairs={{0,4},{4,0},{8,12},{12,8},{16,20},{20,16},{24,28},{28,24},{1,5},{5... | collective-permute-start | bytes 15728648 | tf_op jit(solution)/shard_map/ppermute | solution.py:81
  142.5 35.7 %collective-permute-start.12 = (bf16[256,2560]{1,0:T(8,128)(2,1)}, bf16[256,2560]{1,0:T(8,128)(2,1)S(1)}, u32[]{:S(2)}, u32[]{:S(2)}) collective-permute-start(bf16[256,2560]{1,0:T(8,128)(2,1)} %fence.35.refs_0_), channel_id=1, source_target_pairs={{0,16},{4,20},{8,24},{12,28},{16,0},{20,4},{24,8},{28,12},{1,17},{... | collective-permute-start | bytes 3932168 | tf_op jit(solution)/shard_map/ppermute | solution.py:81
  143.3 34.9 %collective-permute-start.11 = (bf16[256,2560]{1,0:T(8,128)(2,1)}, bf16[256,2560]{1,0:T(8,128)(2,1)S(1)}, u32[]{:S(2)}, u32[]{:S(2)}) collective-permute-start(bf16[256,2560]{1,0:T(8,128)(2,1)} %fence.35.refs_0_), channel_id=1, source_target_pairs={{0,8},{4,12},{8,0},{12,4},{16,24},{20,28},{24,16},{28,20},{1,9},{5... | collective-permute-start | bytes 3932168 | tf_op jit(solution)/shard_map/ppermute | solution.py:81
  182.6 16.3 %collective-permute-start.14 = (bf16[128,2560]{1,0:T(8,128)(2,1)S(1)}, bf16[128,2560]{1,0:T(8,128)(2,1)S(1)}, u32[]{:S(2)}, u32[]{:S(2)}) collective-permute-start(bf16[128,2560]{1,0:T(8,128)(2,1)S(1)} %slice.537), channel_id=1, source_target_pairs={{0,8},{4,12},{8,0},{12,4},{16,24},{20,28},{24,16},{28,20},{1,9},{5... | collective-permute-start | bytes 1966088 | tf_op jit(solution)/shard_map/ppermute | solution.py:81
  183.2 15.9 %collective-permute-start.15 = (bf16[128,2560]{1,0:T(8,128)(2,1)S(1)}, bf16[128,2560]{1,0:T(8,128)(2,1)S(1)}, u32[]{:S(2)}, u32[]{:S(2)}) collective-permute-start(bf16[128,2560]{1,0:T(8,128)(2,1)S(1)} %slice.538), channel_id=1, source_target_pairs={{0,16},{4,20},{8,24},{12,28},{16,0},{20,4},{24,8},{28,12},{1,17},{... | collective-permute-start | bytes 1966088 | tf_op jit(solution)/shard_map/ppermute | solution.py:81
  207.1 31.4 %collective-permute-start.21 = (bf16[256,2560]{1,0:T(8,128)(2,1)}, bf16[256,2560]{1,0:T(8,128)(2,1)S(1)}, u32[]{:S(2)}, u32[]{:S(2)}) collective-permute-start(bf16[256,2560]{1,0:T(8,128)(2,1)} %fence.37.refs_0_), channel_id=1, source_target_pairs={{0,16},{4,20},{8,24},{12,28},{16,0},{20,4},{24,8},{28,12},{1,17},{... | collective-permute-start | bytes 3932168 | tf_op jit(solution)/shard_map/ppermute | solution.py:81
  208.3 31.1 %collective-permute-start.20 = (bf16[256,2560]{1,0:T(8,128)(2,1)}, bf16[256,2560]{1,0:T(8,128)(2,1)S(1)}, u32[]{:S(2)}, u32[]{:S(2)}) collective-permute-start(bf16[256,2560]{1,0:T(8,128)(2,1)} %fence.37.refs_0_), channel_id=1, source_target_pairs={{0,8},{4,12},{8,0},{12,4},{16,24},{20,28},{24,16},{28,20},{1,9},{5... | collective-permute-start | bytes 3932168 | tf_op jit(solution)/shard_map/ppermute | solution.py:81
  242.7 16.1 %collective-permute-start.22 = (bf16[128,2560]{1,0:T(8,128)(2,1)S(1)}, bf16[128,2560]{1,0:T(8,128)(2,1)S(1)}, u32[]{:S(2)}, u32[]{:S(2)}) collective-permute-start(bf16[128,2560]{1,0:T(8,128)(2,1)S(1)} %slice.547), channel_id=1, source_target_pairs={{0,8},{4,12},{8,0},{12,4},{16,24},{20,28},{24,16},{28,20},{1,9},{5... | collective-permute-start | bytes 1966088 | tf_op jit(solution)/shard_map/ppermute | solution.py:81
  243.7 15.7 %collective-permute-start.23 = (bf16[128,2560]{1,0:T(8,128)(2,1)S(1)}, bf16[128,2560]{1,0:T(8,128)(2,1)S(1)}, u32[]{:S(2)}, u32[]{:S(2)}) collective-permute-start(bf16[128,2560]{1,0:T(8,128)(2,1)S(1)} %slice.548), channel_id=1, source_target_pairs={{0,16},{4,20},{8,24},{12,28},{16,0},{20,4},{24,8},{28,12},{1,17},{... | collective-permute-start | bytes 1966088 | tf_op jit(solution)/shard_map/ppermute | solution.py:81
  271.7 20.1 %collective-permute-start.25 = (bf16[128,3072]{1,0:T(8,128)(2,1)}, bf16[128,3072]{1,0:T(8,128)(2,1)S(1)}, u32[]{:S(2)}, u32[]{:S(2)}) collective-permute-start(bf16[128,3072]{1,0:T(8,128)(2,1)} %slice.551), channel_id=1, source_target_pairs={{0,8},{4,12},{8,0},{12,4},{16,24},{20,28},{24,16},{28,20},{1,9},{5... | collective-permute-start | bytes 2359304 | tf_op jit(solution)/shard_map/ppermute | solution.py:81
  272.8 20.0 %collective-permute-start.26 = (bf16[128,3072]{1,0:T(8,128)(2,1)}, bf16[128,3072]{1,0:T(8,128)(2,1)}, u32[]{:S(2)}, u32[]{:S(2)}) collective-permute-start(bf16[128,3072]{1,0:T(8,128)(2,1)} %slice.552), channel_id=1, source_target_pairs={{0,16},{4,20},{8,24},{12,28},{16,0},{20,4},{24,8},{28,12},{1,17},{... | collective-permute-start | bytes 2359304 | tf_op jit(solution)/shard_map/ppermute | solution.py:81
  287.8 161.7 %all-gather.12.cloned.1.call-start = ((), (), s32[]{:S(2)}) async-start(), calls=%async_computation.6 | async-start | bytes 5242880 | tf_op jit(solution)/shard_map/all_gather | solution.py:630
  298.8 62.5 %collective-permute-start.27 = (bf16[1024,3072]{1,0:T(8,128)(2,1)}, bf16[1024,3072]{1,0:T(8,128)(2,1)}, u32[]{:S(2)}, u32[]{:S(2)}) collective-permute-start(bf16[1024,3072]{1,0:T(8,128)(2,1)} %assemble.10.refs_0_), channel_id=1, source_target_pairs={{0,4},{4,0},{8,12},{12,8},{16,20},{20,16},{24,28},{28,24},{1,5},{5... | collective-permute-start | bytes 18874376 | tf_op jit(solution)/shard_map/ppermute | solution.py:81
  301.5 20.1 %collective-permute-start.29 = (bf16[256,1536]{1,0:T(8,128)(2,1)}, bf16[256,1536]{1,0:T(8,128)(2,1)S(1)}, u32[]{:S(2)}, u32[]{:S(2)}) collective-permute-start(bf16[256,1536]{1,0:T(8,128)(2,1)} %fence.41.refs_0_), channel_id=1, source_target_pairs={{0,16},{4,20},{8,24},{12,28},{16,0},{20,4},{24,8},{28,12},{1,17},{... | collective-permute-start | bytes 2359304 | tf_op jit(solution)/shard_map/ppermute | solution.py:81
  302.0 20.3 %collective-permute-start.28 = (bf16[256,1536]{1,0:T(8,128)(2,1)}, bf16[256,1536]{1,0:T(8,128)(2,1)S(1)}, u32[]{:S(2)}, u32[]{:S(2)}) collective-permute-start(bf16[256,1536]{1,0:T(8,128)(2,1)} %fence.41.refs_0_), channel_id=1, source_target_pairs={{0,8},{4,12},{8,0},{12,4},{16,24},{20,28},{24,16},{28,20},{1,9},{5... | collective-permute-start | bytes 2359304 | tf_op jit(solution)/shard_map/ppermute | solution.py:81
  360.8 258.0 %reduce-scatter.5.cloned.1.call-start = ((), (), s32[]{:S(2)}) async-start(), calls=%async_computation.7 | async-start | bytes 5242880 | tf_op jit(solution)/shard_map/reduce_scatter | solution.py:639
  425.1 193.8 %reduce-scatter.7.cloned.1.call-start = ((), (), s32[]{:S(2)}) async-start(), calls=%async_computation.8 | async-start | bytes 5242880 | tf_op jit(solution)/shard_map/reduce_scatter | solution.py:639
  531.6 195.7 %reduce-scatter.9.cloned.1.call-start = ((), (), s32[]{:S(2)}) async-start(), calls=%async_computation.9 | async-start | bytes 5242880 | tf_op jit(solution)/shard_map/reduce_scatter | solution.py:661
  541.4 66.9 %collective-permute-start.33 = (bf16[1024,1536]{1,0:T(8,128)(2,1)}, bf16[1024,1536]{1,0:T(8,128)(2,1)S(1)}, u32[]{:S(2)}, u32[]{:S(2)}) collective-permute-start(bf16[1024,1536]{1,0:T(8,128)(2,1)} %add_convert_fusion.2), channel_id=1, source_target_pairs={{0,4},{4,0},{8,12},{12,8},{16,20},{20,16},{24,28},{28,24},{1,5},{5... | collective-permute-start | bytes 9437192 | tf_op jit(solution)/shard_map/ppermute | solution.py:81
  563.0 51.2 %collective-permute-start.34 = (bf16[1024,3072]{1,0:T(8,128)(2,1)}, bf16[1024,3072]{1,0:T(8,128)(2,1)}, u32[]{:S(2)}, u32[]{:S(2)}) collective-permute-start(bf16[1024,3072]{1,0:T(8,128)(2,1)} %add_convert_fusion), channel_id=1, source_target_pairs={{0,4},{4,0},{8,12},{12,8},{16,20},{20,16},{24,28},{28,24},{1,5},{5... | collective-permute-start | bytes 18874376 | tf_op jit(solution)/shard_map/ppermute | solution.py:81
  619.0 182.3 %reduce-scatter.11.cloned.1.call-start = ((), (), s32[]{:S(2)}) async-start(), calls=%async_computation.10 | async-start | bytes 5242880 | tf_op jit(solution)/shard_map/reduce_scatter | solution.py:661
  620.9 39.4 %collective-permute-start.36 = (bf16[256,1536]{1,0:T(8,128)(2,1)}, bf16[256,1536]{1,0:T(8,128)(2,1)}, u32[]{:S(2)}, u32[]{:S(2)}) collective-permute-start(bf16[256,1536]{1,0:T(8,128)(2,1)} %get-tuple-element.226.refs_3_), channel_id=1, source_target_pairs={{0,16},{4,20},{8,24},{12,28},{16,0},{20,4},{24,8},{28,12},{1,17},{... | collective-permute-start | bytes 2359304 | tf_op jit(solution)/shard_map/ppermute | solution.py:81
  622.3 39.2 %collective-permute-start.35 = (bf16[256,1536]{1,0:T(8,128)(2,1)}, bf16[256,1536]{1,0:T(8,128)(2,1)}, u32[]{:S(2)}, u32[]{:S(2)}) collective-permute-start(bf16[256,1536]{1,0:T(8,128)(2,1)} %get-tuple-element.227.refs_2_), channel_id=1, source_target_pairs={{0,8},{4,12},{8,0},{12,4},{16,24},{20,28},{24,16},{28,20},{1,9},{5... | collective-permute-start | bytes 2359304 | tf_op jit(solution)/shard_map/ppermute | solution.py:81
  623.8 50.5 %collective-permute-start.38 = (bf16[256,3072]{1,0:T(8,128)(2,1)}, bf16[256,3072]{1,0:T(8,128)(2,1)}, u32[]{:S(2)}, u32[]{:S(2)}) collective-permute-start(bf16[256,3072]{1,0:T(8,128)(2,1)} %get-tuple-element.200.refs_5_), channel_id=1, source_target_pairs={{0,16},{4,20},{8,24},{12,28},{16,0},{20,4},{24,8},{28,12},{1,17},{... | collective-permute-start | bytes 4718600 | tf_op jit(solution)/shard_map/ppermute | solution.py:81
  624.3 51.1 %collective-permute-start.37 = (bf16[256,3072]{1,0:T(8,128)(2,1)}, bf16[256,3072]{1,0:T(8,128)(2,1)}, u32[]{:S(2)}, u32[]{:S(2)}) collective-permute-start(bf16[256,3072]{1,0:T(8,128)(2,1)} %get-tuple-element.201.refs_4_), channel_id=1, source_target_pairs={{0,8},{4,12},{8,0},{12,4},{16,24},{20,28},{24,16},{28,20},{1,9},{5... | collective-permute-start | bytes 4718600 | tf_op jit(solution)/shard_map/ppermute | solution.py:81
  658.9 16.5 %collective-permute-start.41 = (f32[2,2560]{1,0:T(2,128)S(1)}, f32[2,2560]{1,0:T(2,128)S(1)}, u32[]{:S(2)}, u32[]{:S(2)}) collective-permute-start(f32[2,2560]{1,0:T(2,128)S(1)} %pad_maximum_fusion.16), channel_id=1, source_target_pairs={{3,0},{7,4},{11,8},{15,12},{19,16},{23,20},{27,24},{31,28}} | collective-permute-start | bytes 61448 | tf_op jit(solution)/shard_map/ppermute | solution.py:164
  663.0 303.3 %all-gather.16.cloned.1.call-start = ((), (), s32[]{:S(2)}) async-start(), calls=%async_computation.12 | async-start | bytes 10485760 | tf_op jit(solution)/shard_map/all_gather | solution.py:701
  779.6 51.1 %collective-permute-start.46 = (bf16[1024,2560]{1,0:T(8,128)(2,1)}, bf16[1024,2560]{1,0:T(8,128)(2,1)}, u32[]{:S(2)}, u32[]{:S(2)}) collective-permute-start(bf16[1024,2560]{1,0:T(8,128)(2,1)} %convolution_convert_fusion.2), channel_id=1, source_target_pairs={{0,4},{4,0},{8,12},{12,8},{16,20},{20,16},{24,28},{28,24},{1,5},{5... | collective-permute-start | bytes 15728648 | tf_op jit(solution)/shard_map/ppermute | solution.py:81
  782.6 380.4 %all-gather.14.cloned.1.call-start = ((), (), s32[]{:S(2)}) async-start(), calls=%async_computation.11 | async-start | bytes 10485760 | tf_op jit(solution)/shard_map/all_gather | solution.py:709
  788.9 63.7 %collective-permute-start.53 = (bf16[1024,2560]{1,0:T(8,128)(2,1)}, bf16[1024,2560]{1,0:T(8,128)(2,1)}, u32[]{:S(2)}, u32[]{:S(2)}) collective-permute-start(bf16[1024,2560]{1,0:T(8,128)(2,1)} %convolution_convert_fusion), channel_id=1, source_target_pairs={{0,4},{4,0},{8,12},{12,8},{16,20},{20,16},{24,28},{28,24},{1,5},{5... | collective-permute-start | bytes 15728648 | tf_op jit(solution)/shard_map/ppermute | solution.py:81
  815.3 30.7 %collective-permute-start.44 = (bf16[256,2560]{1,0:T(8,128)(2,1)}, bf16[256,2560]{1,0:T(8,128)(2,1)}, u32[]{:S(2)}, u32[]{:S(2)}) collective-permute-start(bf16[256,2560]{1,0:T(8,128)(2,1)} %get-tuple-element.91), channel_id=1, source_target_pairs={{0,16},{4,20},{8,24},{12,28},{16,0},{20,4},{24,8},{28,12},{1,17},{... | collective-permute-start | bytes 3932168 | tf_op jit(solution)/shard_map/ppermute | solution.py:81
  816.7 30.5 %collective-permute-start.45 = (bf16[256,2560]{1,0:T(8,128)(2,1)}, bf16[256,2560]{1,0:T(8,128)(2,1)}, u32[]{:S(2)}, u32[]{:S(2)}) collective-permute-start(bf16[256,2560]{1,0:T(8,128)(2,1)} %get-tuple-element.92), channel_id=1, source_target_pairs={{0,8},{4,12},{8,0},{12,4},{16,24},{20,28},{24,16},{28,20},{1,9},{5... | collective-permute-start | bytes 3932168 | tf_op jit(solution)/shard_map/ppermute | solution.py:81
  847.2 29.6 %collective-permute-start.47 = (bf16[256,2560]{1,0:T(8,128)(2,1)}, bf16[256,2560]{1,0:T(8,128)(2,1)}, u32[]{:S(2)}, u32[]{:S(2)}) collective-permute-start(bf16[256,2560]{1,0:T(8,128)(2,1)} %get-tuple-element.94), channel_id=1, source_target_pairs={{0,8},{4,12},{8,0},{12,4},{16,24},{20,28},{24,16},{28,20},{1,9},{5... | collective-permute-start | bytes 3932168 | tf_op jit(solution)/shard_map/ppermute | solution.py:81
  848.7 29.3 %collective-permute-start.48 = (bf16[256,2560]{1,0:T(8,128)(2,1)}, bf16[256,2560]{1,0:T(8,128)(2,1)}, u32[]{:S(2)}, u32[]{:S(2)}) collective-permute-start(bf16[256,2560]{1,0:T(8,128)(2,1)} %get-tuple-element.95), channel_id=1, source_target_pairs={{0,16},{4,20},{8,24},{12,28},{16,0},{20,4},{24,8},{28,12},{1,17},{... | collective-permute-start | bytes 3932168 | tf_op jit(solution)/shard_map/ppermute | solution.py:81
  878.0 17.9 %collective-permute-start.49 = (bf16[128,2560]{1,0:T(8,128)(2,1)}, bf16[128,2560]{1,0:T(8,128)(2,1)S(1)}, u32[]{:S(2)}, u32[]{:S(2)}) collective-permute-start(bf16[128,2560]{1,0:T(8,128)(2,1)} %get-tuple-element.96), channel_id=1, source_target_pairs={{0,8},{4,12},{8,0},{12,4},{16,24},{20,28},{24,16},{28,20},{1,9},{5... | collective-permute-start | bytes 1966088 | tf_op jit(solution)/shard_map/ppermute | solution.py:81
  878.6 18.2 %collective-permute-start.50 = (bf16[128,2560]{1,0:T(8,128)(2,1)}, bf16[128,2560]{1,0:T(8,128)(2,1)}, u32[]{:S(2)}, u32[]{:S(2)}) collective-permute-start(bf16[128,2560]{1,0:T(8,128)(2,1)} %get-tuple-element.97), channel_id=1, source_target_pairs={{0,16},{4,20},{8,24},{12,28},{16,0},{20,4},{24,8},{28,12},{1,17},{... | collective-permute-start | bytes 1966088 | tf_op jit(solution)/shard_map/ppermute | solution.py:81
  882.8 27.2 %collective-permute-start.51 = (bf16[128,2560]{1,0:T(8,128)(2,1)}, bf16[128,2560]{1,0:T(8,128)(2,1)}, u32[]{:S(2)}, u32[]{:S(2)}) collective-permute-start(bf16[128,2560]{1,0:T(8,128)(2,1)} %get-tuple-element.98), channel_id=1, source_target_pairs={{0,8},{4,12},{8,0},{12,4},{16,24},{20,28},{24,16},{28,20},{1,9},{5... | collective-permute-start | bytes 1966088 | tf_op jit(solution)/shard_map/ppermute | solution.py:81
  884.3 26.3 %collective-permute-start.52 = (bf16[128,2560]{1,0:T(8,128)(2,1)}, bf16[128,2560]{1,0:T(8,128)(2,1)}, u32[]{:S(2)}, u32[]{:S(2)}) collective-permute-start(bf16[128,2560]{1,0:T(8,128)(2,1)} %get-tuple-element.99), channel_id=1, source_target_pairs={{0,16},{4,20},{8,24},{12,28},{16,0},{20,4},{24,8},{28,12},{1,17},{... | collective-permute-start | bytes 1966088 | tf_op jit(solution)/shard_map/ppermute | solution.py:81
  885.7 49.0 %collective-permute-start.54 = (bf16[256,2560]{1,0:T(8,128)(2,1)}, bf16[256,2560]{1,0:T(8,128)(2,1)S(1)}, u32[]{:S(2)}, u32[]{:S(2)}) collective-permute-start(bf16[256,2560]{1,0:T(8,128)(2,1)} %get-tuple-element.101), channel_id=1, source_target_pairs={{0,16},{4,20},{8,24},{12,28},{16,0},{20,4},{24,8},{28,12},{1,17},{... | collective-permute-start | bytes 3932168 | tf_op jit(solution)/shard_map/ppermute | solution.py:81
  895.9 38.8 %collective-permute-start.55 = (bf16[256,2560]{1,0:T(8,128)(2,1)}, bf16[256,2560]{1,0:T(8,128)(2,1)S(1)}, u32[]{:S(2)}, u32[]{:S(2)}) collective-permute-start(bf16[256,2560]{1,0:T(8,128)(2,1)} %get-tuple-element.102), channel_id=1, source_target_pairs={{0,8},{4,12},{8,0},{12,4},{16,24},{20,28},{24,16},{28,20},{1,9},{5... | collective-permute-start | bytes 3932168 | tf_op jit(solution)/shard_map/ppermute | solution.py:81
  964.5 32.0 %collective-permute-start.58 = (bf16[3,256,640]{2,1,0:T(8,128)(2,1)S(1)}, bf16[3,256,640]{2,1,0:T(8,128)(2,1)S(1)}, u32[]{:S(2)}, u32[]{:S(2)}) collective-permute-start(bf16[3,256,640]{2,1,0:T(8,128)(2,1)S(1)} %get-tuple-element.233), channel_id=1, source_target_pairs={{0,1},{4,5},{8,9},{12,13},{16,17},{20,21},{24,25},{28,29}} | collective-permute-start | bytes 2949128 | tf_op jit(solution)/shard_map/ppermute | solution.py:191
  1004.9 15.5 %collective-permute-start.67 = (bf16[128,1536]{1,0:T(8,128)(2,1)}, bf16[128,1536]{1,0:T(8,128)(2,1)}, u32[]{:S(2)}, u32[]{:S(2)}) collective-permute-start(bf16[128,1536]{1,0:T(8,128)(2,1)} %get-tuple-element.112), channel_id=1, source_target_pairs={{0,16},{4,20},{8,24},{12,28},{16,0},{20,4},{24,8},{28,12},{1,17},{... | collective-permute-start | bytes 1179656 | tf_op jit(solution)/shard_map/ppermute | solution.py:81
  1006.9 24.3 %collective-permute-start.64 = (bf16[128,3072]{1,0:T(8,128)(2,1)}, bf16[128,3072]{1,0:T(8,128)(2,1)}, u32[]{:S(2)}, u32[]{:S(2)}) collective-permute-start(bf16[128,3072]{1,0:T(8,128)(2,1)} %get-tuple-element.109), channel_id=1, source_target_pairs={{0,8},{4,12},{8,0},{12,4},{16,24},{20,28},{24,16},{28,20},{1,9},{5... | collective-permute-start | bytes 2359304 | tf_op jit(solution)/shard_map/ppermute | solution.py:81
  1008.8 22.4 %collective-permute-start.65 = (bf16[128,3072]{1,0:T(8,128)(2,1)}, bf16[128,3072]{1,0:T(8,128)(2,1)}, u32[]{:S(2)}, u32[]{:S(2)}) collective-permute-start(bf16[128,3072]{1,0:T(8,128)(2,1)} %get-tuple-element.110), channel_id=1, source_target_pairs={{0,16},{4,20},{8,24},{12,28},{16,0},{20,4},{24,8},{28,12},{1,17},{... | collective-permute-start | bytes 2359304 | tf_op jit(solution)/shard_map/ppermute | solution.py:81
  1013.3 22.2 %collective-permute-start.68 = (bf16[4,4,26752]{2,1,0:T(4,128)(2,1)}, bf16[4,4,26752]{2,1,0:T(4,128)(2,1)}, u32[]{:S(2)}, u32[]{:S(2)}) collective-permute-start(bf16[4,4,26752]{2,1,0:T(4,128)(2,1)} %slice.825), channel_id=1, source_target_pairs={{0,16},{4,20},{8,24},{12,28},{16,0},{20,4},{24,8},{28,12},{1,17},{... | collective-permute-start | bytes 2568200 | tf_op jit(solution)/shard_map/ppermute | solution.py:81
  1018.7 22.1 %collective-permute-start.61 = (bf16[3,256,640]{2,1,0:T(8,128)(2,1)}, bf16[3,256,640]{2,1,0:T(8,128)(2,1)}, u32[]{:S(2)}, u32[]{:S(2)}) collective-permute-start(bf16[3,256,640]{2,1,0:T(8,128)(2,1)} %get-tuple-element.228), channel_id=1, source_target_pairs={{2,1},{3,2},{6,5},{7,6},{10,9},{11,10},{14,13},{15,14},{18,17},{19... | collective-permute-start | bytes 2949128 | tf_op jit(solution)/shard_map/ppermute | solution.py:192
  1020.4 40.9 %collective-permute-start.60 = (bf16[3,256,640]{2,1,0:T(8,128)(2,1)}, bf16[3,256,640]{2,1,0:T(8,128)(2,1)}, u32[]{:S(2)}, u32[]{:S(2)}) collective-permute-start(bf16[3,256,640]{2,1,0:T(8,128)(2,1)} %get-tuple-element.229), channel_id=1, source_target_pairs={{0,1},{1,2},{4,5},{5,6},{8,9},{9,10},{12,13},{13,14},{16,17},{17,1... | collective-permute-start | bytes 2949128 | tf_op jit(solution)/shard_map/ppermute | solution.py:191
  1038.7 22.6 %collective-permute-start.69 = (bf16[2,4,26752]{2,1,0:T(4,128)(2,1)S(1)}, bf16[2,4,26752]{2,1,0:T(4,128)(2,1)S(1)}, u32[]{:S(2)}, u32[]{:S(2)}) collective-permute-start(bf16[2,4,26752]{2,1,0:T(4,128)(2,1)S(1)} %slice.827), channel_id=1, source_target_pairs={{0,8},{4,12},{8,0},{12,4},{16,24},{20,28},{24,16},{28,20},{1,9},{5... | collective-permute-start | bytes 1284104 | tf_op jit(solution)/shard_map/ppermute | solution.py:81
  1065.4 42.4 %collective-permute-start.71 = (bf16[26752]{0:T(1024)(128)(2,1)S(1)}, bf16[26752]{0:T(1024)(128)(2,1)S(1)}, u32[]{:S(2)}, u32[]{:S(2)}) collective-permute-start(bf16[26752]{0:T(1024)(128)(2,1)S(1)} %get-tuple-element.187), channel_id=1, source_target_pairs={{0,1},{1,2},{2,3},{3,0},{4,5},{5,6},{6,7},{7,4},{8,9},{9,10},{10,1... | collective-permute-start | bytes 160520 | tf_op jit(solution)/shard_map/ppermute | solution.py:164
  1101.6 39.0 %collective-permute-start.63 = (bf16[3,256,640]{2,1,0:T(8,128)(2,1)}, bf16[3,256,640]{2,1,0:T(8,128)(2,1)S(1)}, u32[]{:S(2)}, u32[]{:S(2)}) collective-permute-start(bf16[3,256,640]{2,1,0:T(8,128)(2,1)} %add_convert_fusion.14), channel_id=1, source_target_pairs={{1,0},{2,1},{3,2},{5,4},{6,5},{7,6},{9,8},{10,9},{11,10},{13,12},{... | collective-permute-start | bytes 2949128 | tf_op jit(solution)/shard_map/ppermute | solution.py:192
  1102.9 47.6 %collective-permute-start.62 = (bf16[3,256,640]{2,1,0:T(8,128)(2,1)}, bf16[3,256,640]{2,1,0:T(8,128)(2,1)S(1)}, u32[]{:S(2)}, u32[]{:S(2)}) collective-permute-start(bf16[3,256,640]{2,1,0:T(8,128)(2,1)} %add_convert_fusion.15), channel_id=1, source_target_pairs={{0,1},{1,2},{2,3},{4,5},{5,6},{6,7},{8,9},{9,10},{10,11},{12,13},{... | collective-permute-start | bytes 2949128 | tf_op jit(solution)/shard_map/ppermute | solution.py:191
  (151 other events, 1204.9 us)
Sparse Core Ops, SparseCore 0:
  12.1 43.3 all-gather.7
  57.6 54.7 all-gather.17
  287.9 80.7 all-gather.9
  370.1 79.2 all-gather.11
  451.6 75.2 reduce-scatter.4
  531.7 75.2 reduce-scatter.6
  619.1 76.5 reduce-scatter.8
  698.1 80.7 reduce-scatter.10
  782.7 147.8 all-gather.15
  966.4 196.5 all-gather.13
